TPU v7x, 32 devices: a whole 2x2x4 slice. The times are simulated.
32 devices in a mesh: dp: 8 (over z, x), space: 4 (over y, core).
Axes of the slice: x: 2, y: 2, z: 4, core: 2. Of those that a mesh axis runs over, the one named last changes fastest.
Arguments:
- volume_in: bfloat16 [8, 4, 16, 64, 128], P('dp', 'space'), may hold values from -6 to 6
- hidden_act: bfloat16 [8, 4, 32, 64, 128], P('dp', 'space'), may hold values from -6 to 6
- out_cot: bfloat16 [8, 4, 32, 64, 128], P('dp', 'space'), may hold values from -6 to 6
- kernel_one: bfloat16 [3, 3, 3, 16, 32], replicated, may hold values from -0.3125 to 0.3125
- kernel_two: bfloat16 [3, 3, 3, 32, 32], replicated, may hold values from -0.21875 to 0.21875
- grad_bucket: float32 [32, 524288], P(('dp', 'space')), may hold values from -1 to 1
Outputs:
- grad_input: bfloat16 [8, 4, 16, 64, 128], P('dp', 'space')
- grad_kernel_one: float32 [3, 3, 3, 16, 32], replicated
- grad_kernel_two: float32 [3, 3, 3, 32, 32], replicated
- bucket_sum: float32 [524288], replicated
All inputs are finite; a program needn't handle non-finite values.
Results may differ from a plain program's by a relative error of at most 0.013.
Values may be sent and summed in bfloat16 or wider, within the bound.
No kernel may reach another device: no remote copies, remote signals or barrier semaphores. Data moves between devices by JAX's collectives and lax.ppermute only.
A program may use at most 128 MiB of HBM per device.

v0:
```python
import math

import jax
import jax.numpy as jnp
from jax import lax
from jax.experimental import pallas as pl
from jax.experimental.pallas import tpu as pltpu
from jax.sharding import Mesh, PartitionSpec as P

SPACE = ("slab", "core")
EVERY = ("dp", "slab", "core")
GROUP = 4
LANES = 128
BF16 = jnp.bfloat16
F32 = jnp.float32


def ceil_to(value, step):
    return -(-value // step) * step


def slid(value, step):
    lane = lax.broadcasted_iota(jnp.int32, value.shape, 1)
    width = value.shape[1]
    keep = lane >= step if step > 0 else lane < width + step
    return jnp.where(keep, pltpu.roll(value, step % width, 1), 0.0)


def beside(window, rows, step, count):
    return jnp.concatenate([window[g * step : g * step + rows] for g in range(count)], axis=1)


def turned(src, flat, dst, offset, pitch, lead):
    chans, length, _ = src.shape

    def stage(c, carry):
        flat[pl.ds(pl.multiple_of(c * length, length), length), :] = src[c].astype(F32)
        return carry

    lax.fori_loop(0, chans, stage, 0, unroll=4)

    def gather(x, carry):
        rows = flat[pl.ds(x, chans, stride=length), :]
        at = pl.multiple_of((x + lead) * pitch + offset, 16)
        dst[pl.ds(at, chans), :] = rows.astype(BF16)
        return carry

    lax.fori_loop(0, length, gather, 0, unroll=4)


def compute_kernel(
    cot_m, cot_0, cot_p, act, vol_m, vol_0, vol_p, w_two, w_one,
    terms, own, up, down,
    flat, cots, acts, vols, pres, acc_two, acc_one,
):
    c1, length, _ = act.shape
    c0 = vol_0.shape[0]
    c2 = cot_0.shape[0]
    wide_two, wide_one = 3 * c2, 3 * c0

    for buffer, rows in ((cots, wide_two), (vols, wide_one), (pres, c1)):
        zeros = jnp.zeros((rows, LANES), BF16)
        buffer[0:rows, :] = zeros
        buffer[(length + 1) * rows : (length + 2) * rows, :] = zeros
    for place, src in enumerate((cot_m, cot_0, cot_p)):
        turned(src, flat, cots, place * c2, wide_two, 1)
    for place, src in enumerate((vol_m, vol_0, vol_p)):
        turned(src, flat, vols, place * c0, wide_one, 1)
    turned(act, flat, acts, 0, c1, 0)
    acc_two[...] = jnp.zeros_like(acc_two)
    acc_one[...] = jnp.zeros_like(acc_one)

    def first(step, carry):
        x = step * GROUP
        window = cots[pl.ds(pl.multiple_of(x * wide_two, 16), (GROUP + 2) * wide_two), :]
        right = beside(window, 3 * wide_two, wide_two, GROUP)
        sums = jnp.dot(w_two[...], right, preferred_element_type=F32)
        field = acts[pl.ds(pl.multiple_of(x * c1, 16), GROUP * c1), :].astype(F32)
        columns = []
        for g in range(GROUP):
            part = sums[:, g * LANES : (g + 1) * LANES]
            grad = slid(part[0:c1], 1) + part[c1 : 2 * c1] + slid(part[2 * c1 : 3 * c1], -1)
            value = field[g * c1 : (g + 1) * c1]
            pre = (grad * jnp.where(value > 0, 1.0, 0.2)).astype(BF16)
            pres[pl.ds(pl.multiple_of((x + g + 1) * c1, 16), c1), :] = pre
            columns.append(
                jnp.concatenate([slid(value, 1), value, slid(value, -1)], axis=0).astype(BF16)
            )
        left = jnp.concatenate(columns, axis=1)
        acc_two[...] += lax.dot_general(
            right, left, (((1,), (1,)), ((), ())), preferred_element_type=F32
        )
        return carry

    lax.fori_loop(0, length // GROUP, first, 0)

    def second(step, carry):
        x = step * GROUP
        window = pres[pl.ds(pl.multiple_of(x * c1, 16), (GROUP + 2) * c1), :]
        sums = jnp.dot(w_one[...], beside(window, 3 * c1, c1, GROUP), preferred_element_type=F32)
        columns = []
        for g in range(GROUP):
            part = sums[:, g * LANES : (g + 1) * LANES]
            at = pl.ds(pl.multiple_of((x + g) * c0, 16), c0)
            for i, out in ((0, up), (1, own), (2, down)):
                b = 3 * i * c0
                grad = (
                    slid(part[b : b + c0], 1)
                    + part[b + c0 : b + 2 * c0]
                    + slid(part[b + 2 * c0 : b + 3 * c0], -1)
                )
                out[at, :] = grad.astype(out.dtype)
            value = window[(g + 1) * c1 : (g + 2) * c1].astype(F32)
            columns.append(
                jnp.concatenate([slid(value, -1), value, slid(value, 1)], axis=0).astype(BF16)
            )
        left = jnp.concatenate(columns, axis=1)
        volume = vols[pl.ds(pl.multiple_of(x * wide_one, 16), (GROUP + 2) * wide_one), :]
        right = beside(volume, 3 * wide_one, wide_one, GROUP)
        acc_one[...] += lax.dot_general(
            right, left, (((1,), (1,)), ((), ())), preferred_element_type=F32
        )
        return carry

    lax.fori_loop(0, length // GROUP, second, 0)

    terms[...] = jnp.zeros_like(terms)
    two = acc_two[...].T
    rows, width = two.shape
    blocks = -(-width // LANES)
    for block in range(blocks):
        part = two[:, block * LANES : min(width, (block + 1) * LANES)]
        terms[block * rows : (block + 1) * rows, 0 : part.shape[1]] = part.astype(terms.dtype)
    one = acc_one[...]
    terms[blocks * rows : blocks * rows + one.shape[0], 0 : one.shape[1]] = one.astype(terms.dtype)


def vmem_call(body, out_shape, scratch=(), cost=None, limit=48 * 2**20):
    spec = pl.BlockSpec(memory_space=pltpu.VMEM)
    return pl.pallas_call(
        body,
        out_shape=out_shape,
        out_specs=jax.tree.map(lambda _: spec, out_shape),
        scratch_shapes=list(scratch),
        compiler_params=pltpu.CompilerParams(vmem_limit_bytes=limit),
        cost_estimate=cost,
    )


def compute(cots, act, vols, kernel_two, kernel_one, rows):
    c1, length, width = act.shape
    c0, c2 = (vols[0].shape[0], cots[0].shape[0])
    w_two = kernel_two[::-1, ::-1, ::-1].transpose(2, 3, 1, 0, 4).reshape(3 * c1, 9 * c2)
    w_one = kernel_one[::-1, ::-1, ::-1].transpose(0, 2, 3, 1, 4).reshape(9 * c0, 3 * c1)
    plane = (length * c0, width)
    flops = 2 * 27 * length * width * c1 * 2 * (c0 + c2)
    return vmem_call(
        compute_kernel,
        (
            jax.ShapeDtypeStruct((rows, LANES), BF16),
            jax.ShapeDtypeStruct(plane, F32),
            jax.ShapeDtypeStruct(plane, BF16),
            jax.ShapeDtypeStruct(plane, BF16),
        ),
        (
            pltpu.VMEM((max(c0, c1, c2) * length, width), F32),
            pltpu.VMEM(((length + 2) * 3 * c2, width), BF16),
            pltpu.VMEM((length * c1, width), BF16),
            pltpu.VMEM(((length + 2) * 3 * c0, width), BF16),
            pltpu.VMEM(((length + 2) * c1, width), BF16),
            pltpu.VMEM((9 * c2, 3 * c1), F32),
            pltpu.VMEM((9 * c0, 3 * c1), F32),
        ),
        pl.CostEstimate(flops=flops, bytes_accessed=5 * 2**20, transcendentals=0),
    )(*cots, act, *vols, w_two, w_one)


def merge_kernel(own, from_below, from_above, out, flat):
    chans, length, _ = out.shape

    def add(step, carry):
        at = pl.ds(pl.multiple_of(step * 64, 64), 64)
        flat[at, :] = own[at, :] + from_below[at, :].astype(F32) + from_above[at, :].astype(F32)
        return carry

    lax.fori_loop(0, own.shape[0] // 64, add, 0, unroll=4)

    def gather(c, carry):
        out[c] = flat[pl.ds(c, length, stride=chans), :].astype(out.dtype)
        return carry

    lax.fori_loop(0, chans, gather, 0, unroll=4)


def merge(own, from_below, from_above, shape):
    return vmem_call(
        merge_kernel,
        jax.ShapeDtypeStruct(shape, BF16),
        (pltpu.VMEM(own.shape, F32),),
        pl.CostEstimate(flops=2 * own.size, bytes_accessed=8 * own.size, transcendentals=0),
    )(own, from_below, from_above)


def share_kernel(scale, bucket, terms, out):
    total = jnp.sum(bucket[...].astype(F32), axis=0).astype(BF16)
    grads = (jnp.sum(terms[...].astype(F32), axis=0) * scale).astype(BF16)
    height = total.shape[0]

    def write(n, carry):
        out[n, 0:height, :] = total
        out[n, height : height + grads.shape[0], :] = grads
        return carry

    lax.fori_loop(0, out.shape[0], write, 0)


def share(bucket, terms, scale, copies):
    rows = bucket.shape[1] + terms.shape[1]
    return vmem_call(
        lambda *refs: share_kernel(scale, *refs),
        jax.ShapeDtypeStruct((copies, rows, LANES), BF16),
        (),
        pl.CostEstimate(flops=bucket.size, bytes_accessed=3 * bucket.size, transcendentals=0),
    )(bucket, terms)


def finish_kernel(sizes, core, mine, other, bucket, out_one, out_two, raw):
    c0, c1, c2 = sizes
    copies, rows, _ = mine.shape
    height = bucket.shape[0] // (2 * copies)
    extra = rows - height
    me = core[0]

    def place(q, carry):
        for source, which in ((mine, me), (other, 1 - me)):
            chunk = 2 * q + which
            bucket[pl.ds(pl.multiple_of(chunk * height, 8), height), :] = source[q, 0:height, :].astype(F32)
            raw[pl.ds(pl.multiple_of(chunk * extra, 8), extra), :] = source[q, height:rows, :].astype(F32)
        return carry

    lax.fori_loop(0, copies, place, 0)
    block = 3 * c1
    first = -(-9 * c2 // LANES) * block
    for i in range(3):
        for j in range(3):
            column = ((2 - j) * 3 + 2 - i) * c2
            whole, lane = (column // LANES, column % LANES)
            out_two[(3 * i + j) * block : (3 * i + j + 1) * block, :] = raw[
                whole * block : (whole + 1) * block, lane : lane + c2
            ]
            row = first + (3 * j + i) * c0
            for k in range(3):
                to = (9 * i + 3 * j + k) * c0
                out_one[to : to + c0, :] = raw[row : row + c0, k * c1 : (k + 1) * c1]


def finish(core, mine, other, length, sizes):
    c0, c1, c2 = sizes
    copies, rows, _ = mine.shape
    extra = rows - length // LANES // (2 * copies)
    spec = pl.BlockSpec(memory_space=pltpu.VMEM)
    return pl.pallas_call(
        lambda *refs: finish_kernel(sizes, *refs),
        out_shape=(
            jax.ShapeDtypeStruct((length // LANES, LANES), F32),
            jax.ShapeDtypeStruct((27 * c0, c1), F32),
            jax.ShapeDtypeStruct((27 * c1, c2), F32),
        ),
        in_specs=[pl.BlockSpec(memory_space=pltpu.SMEM), spec, spec],
        out_specs=(spec, spec, spec),
        scratch_shapes=[pltpu.VMEM((2 * copies * extra, LANES), F32)],
        compiler_params=pltpu.CompilerParams(vmem_limit_bytes=48 * 2**20),
    )(core, mine, other)


def halos(value):
    count = lax.axis_size(SPACE)
    up = [(i, i + 1) for i in range(count - 1)]
    down = [(j, i) for i, j in up]
    return (lax.ppermute(value, SPACE, up), lax.ppermute(value, SPACE, down))


def per_device(volume_in, hidden_act, out_cot, kernel_one, kernel_two, grad_bucket):
    c0, c1, c2 = (volume_in.shape[2], hidden_act.shape[2], out_cot.shape[2])
    devices, copies = (lax.axis_size(EVERY), lax.axis_size(("dp", "slab")))
    cot, vol = (out_cot[0, 0], volume_in[0, 0])
    cot_m, cot_p = halos(cot)
    vol_m, vol_p = halos(vol)
    length = grad_bucket.shape[1]
    parts = grad_bucket.reshape(devices, length // devices // LANES, LANES).astype(BF16)
    parts = lax.all_to_all(parts, EVERY, 0, 0)

    used = -(-9 * c2 // LANES) * 3 * c1 + 9 * c0
    rows = ceil_to(used, 16 * devices)
    terms, own, up, down = compute(
        (cot_m, cot, cot_p), hidden_act[0, 0], (vol_m, vol, vol_p), kernel_two, kernel_one, rows
    )
    terms = lax.all_to_all(terms.reshape(devices, rows // devices, LANES), EVERY, 0, 0)
    count = lax.axis_size(SPACE)
    upward = [(i, i + 1) for i in range(count - 1)]
    from_below = lax.ppermute(up, SPACE, upward)
    from_above = lax.ppermute(down, SPACE, [(j, i) for i, j in upward])
    grad_input = merge(own, from_below, from_above, vol.shape)

    cells = volume_in.shape[3] * volume_in.shape[4] * devices
    shares = share(parts, terms, 1.0 / math.sqrt(cells), copies)
    mine = lax.all_to_all(shares, ("dp", "slab"), 0, 0)
    other = lax.ppermute(mine, "core", [(0, 1), (1, 0)])
    core = lax.axis_index("core").astype(jnp.int32).reshape(1)
    bucket_sum, total_one, total_two = finish(core, mine, other, length, (c0, c1, c2))
    return (
        grad_input[None, None],
        total_one.reshape(3, 3, 3, c0, c1),
        total_two.reshape(3, 3, 3, c1, c2),
        bucket_sum.reshape(length),
    )


def solution(mesh):
    dp, space = (mesh.shape["dp"], mesh.shape["space"])
    split = Mesh(mesh.devices.reshape(dp, space // 2, 2), EVERY)
    volume = P("dp", SPACE, None, None, None)
    in_specs = (volume, volume, volume, P(), P(), P(EVERY, None))
    out_specs = (volume, P(), P(), P())
    return jax.shard_map(
        per_device, mesh=split, in_specs=in_specs, out_specs=out_specs, check_vma=False
    )
```

profile of v0, /device:TPU:1, one launch (start us, length us, event | category | flops | bytes accessed | tf_op | source)
XLA Modules:
  0.0 130.9 jit_solution(1019211316311559213)
XLA Ops:
  0.6 2.0 %collective-permute-start.1 = (bf16[32,64,128]{2,1,0:T(8,128)(2,1)}, bf16[32,64,128]{2,1,0:T(8,128)(2,1)S(1)}, u32[]{:S(2)}, u32[]{:S(2)}) collective-permute-start(bf16[32,64,128]{2,1,0:T(8,128)(2,1)} %bitcast.14), channel_id=1, source_target_pairs={{1,0},{2,1},{3,2},{5,4},{6,5},{7,6},{9,8},{10,9},{11,10},{13,12},{... | collective-permute-start | bytes 1572872 | tf_op jit(solution)/shard_map/ppermute | solution.py:280
  2.6 4.5 %collective-permute-start = (bf16[32,64,128]{2,1,0:T(8,128)(2,1)}, bf16[32,64,128]{2,1,0:T(8,128)(2,1)S(1)}, u32[]{:S(2)}, u32[]{:S(2)}) collective-permute-start(bf16[32,64,128]{2,1,0:T(8,128)(2,1)} %bitcast.15), channel_id=1, source_target_pairs={{0,1},{1,2},{2,3},{4,5},{5,6},{6,7},{8,9},{9,10},{10,11},{12,13},{... | collective-permute-start | bytes 1572872 | tf_op jit(solution)/shard_map/ppermute | solution.py:280
  7.1 1.9 %collective-permute-start.3 = (bf16[16,64,128]{2,1,0:T(8,128)(2,1)}, bf16[16,64,128]{2,1,0:T(8,128)(2,1)S(1)}, u32[]{:S(2)}, u32[]{:S(2)}) collective-permute-start(bf16[16,64,128]{2,1,0:T(8,128)(2,1)} %bitcast.18), channel_id=1, source_target_pairs={{1,0},{2,1},{3,2},{5,4},{6,5},{7,6},{9,8},{10,9},{11,10},{13,12},{... | collective-permute-start | bytes 786440 | tf_op jit(solution)/shard_map/ppermute | solution.py:280
  9.0 3.6 %collective-permute-start.2 = (bf16[16,64,128]{2,1,0:T(8,128)(2,1)}, bf16[16,64,128]{2,1,0:T(8,128)(2,1)S(1)}, u32[]{:S(2)}, u32[]{:S(2)}) collective-permute-start(bf16[16,64,128]{2,1,0:T(8,128)(2,1)} %bitcast.19), channel_id=1, source_target_pairs={{0,1},{1,2},{2,3},{4,5},{5,6},{6,7},{8,9},{9,10},{10,11},{12,13},{... | collective-permute-start | bytes 786440 | tf_op jit(solution)/shard_map/ppermute | solution.py:280
  12.7 0.9 reverse_bitcast_fusion.1
  13.6 0.1 copy.13
  13.7 0.1 reshape.32.w_one
  13.8 1.0 reverse_bitcast_fusion
  14.7 0.2 copy.12
  14.9 0.2 reshape.31.w_two
  15.1 0.0 collective-permute-done.3.vol_p
  15.1 1.2 collective-permute-done.2.vol_m
  16.3 0.0 collective-permute-done.1.cot_p
  16.3 0.0 collective-permute-done.cot_m
  16.3 0.0 copy-start
  16.3 1.0 copy-done
  17.4 0.0 copy-start.1
  17.4 1.0 copy-done.1
  18.4 0.0 copy-start.2
  18.4 0.9 copy-done.2
  19.4 14.8 %shard_map.93 = (bf16[512,128]{1,0:T(8,128)(2,1)}, f32[1024,128]{1,0:T(8,128)S(1)}, bf16[1024,128]{1,0:T(8,128)(2,1)S(1)}, bf16[1024,128]{1,0:T(8,128)(2,1)S(1)}) custom-call(bf16[32,64,128]{2,1,0:T(8,128)(2,1)S(1)} %collective-permute-done.cot_m, bf16[32,64,128]{2,1,0:T(8,128)(2,1)S(1)} %bitcast.16, bf16[32,64,128]{2,1,0:T(8,128)(2,1)S(1)} %collective-permute-done.1.cot_p, ...), custom_call_target="tpu_custom_call" | custom-call | flops 1358954496 | bytes 5242880 | tf_op jit(solution)/shard_map/pallas_call | solution.py:157
  34.2 6.9 %all-to-all-start.1 = ((bf16[32,16,128]{2,1,0:T(8,128)(2,1)}), bf16[32,16,128]{2,1,0:T(8,128)(2,1)S(1)}, u32[]{:S(2)}, u32[]{:S(2)}) async-start(bf16[32,16,128]{2,1,0:T(8,128)(2,1)} %bitcast.7), calls=%async_computation.1 | async-start | bytes 262144 | tf_op jit(solution)/shard_map/all_to_all | solution.py:298
  41.0 22.8 %convert_reduce_fusion = bf16[524288]{0:T(1024)(128)(2,1)S(1)} fusion(f32[1,524288]{1,0:T(1,128)} %param.11), kind=kLoop, calls=%fused_computation | loop fusion | flops 524288 | bytes 3145728 | tf_op jit(solution)/shard_map/convert_element_type | solution.py:290
  63.8 0.0 all-to-all-done.1.refs_1_
  63.9 31.0 %all_to_all.15.refs_0_ = bf16[32,128,128]{2,1,0:T(8,128)(2,1)S(1)} all-to-all(bf16[32,128,128]{2,1,0:T(8,128)(2,1)S(1)} %bitcast.21), channel_id=1, replica_groups=mesh['dp'=8,'slab'=2,'core'=2] {'dp','slab','core'}, dimensions={0} | all-to-all | bytes 2097152 | tf_op jit(solution)/shard_map/all_to_all | solution.py:291
  94.8 0.3 shard_map.95
  95.1 21.4 %all_to_all.16.refs_1_ = bf16[16,144,128]{2,1,0:T(8,128)(2,1)S(1)} all-to-all(bf16[16,144,128]{2,1,0:T(8,128)(2,1)S(1)} %shard_map.95), channel_id=1, replica_groups=mesh['dp'=8,'slab'=2,'core'=2] {'dp','slab'}, dimensions={0} | all-to-all | bytes 1179648 | tf_op jit(solution)/shard_map/all_to_all | solution.py:307
  116.6 1.8 %collective-permute-start.6 = (bf16[16,144,128]{2,1,0:T(8,128)(2,1)S(1)}, bf16[16,144,128]{2,1,0:T(8,128)(2,1)S(1)}, u32[]{:S(2)}, u32[]{:S(2)}) collective-permute-start(bf16[16,144,128]{2,1,0:T(8,128)(2,1)S(1)} %all_to_all.16.refs_1_), channel_id=1, source_target_pairs={{0,1},{1,0},{2,3},{3,2},{4,5},{5,4},{6,7},{7,6},{8,9},{9,8},{10,11... | collective-permute-start | bytes 1769480 | tf_op jit(solution)/shard_map/ppermute | solution.py:308
  118.4 2.1 %collective-permute-start.4 = (bf16[1024,128]{1,0:T(8,128)(2,1)S(1)}, bf16[1024,128]{1,0:T(8,128)(2,1)S(1)}, u32[]{:S(2)}, u32[]{:S(2)}) collective-permute-start(bf16[1024,128]{1,0:T(8,128)(2,1)S(1)} %get-tuple-element.12), channel_id=1, source_target_pairs={{0,1},{1,2},{2,3},{4,5},{5,6},{6,7},{8,9},{9,10},{10,11},{12,13},{... | collective-permute-start | bytes 786440 | tf_op jit(solution)/shard_map/ppermute | solution.py:301
  120.5 2.3 %collective-permute-start.5 = (bf16[1024,128]{1,0:T(8,128)(2,1)S(1)}, bf16[1024,128]{1,0:T(8,128)(2,1)S(1)}, u32[]{:S(2)}, u32[]{:S(2)}) collective-permute-start(bf16[1024,128]{1,0:T(8,128)(2,1)S(1)} %get-tuple-element.13), channel_id=1, source_target_pairs={{1,0},{2,1},{3,2},{5,4},{6,5},{7,6},{9,8},{10,9},{11,10},{13,12},{... | collective-permute-start | bytes 786440 | tf_op jit(solution)/shard_map/ppermute | solution.py:302
  122.8 1.0 collective-permute-done.4.from_below
  123.8 4.4 %collective-permute-done.5.from_above = bf16[1024,128]{1,0:T(8,128)(2,1)S(1)} collective-permute-done((bf16[1024,128]{1,0:T(8,128)(2,1)S(1)}, bf16[1024,128]{1,0:T(8,128)(2,1)S(1)}, u32[]{:S(2)}, u32[]{:S(2)}) %collective-permute-start.5) | collective-permute-done | bytes 262176 | tf_op jit(solution)/shard_map/ppermute | solution.py:302
  128.2 1.0 shard_map.94
  129.2 0.0 collective-permute-done.6.refs_2_
  129.2 1.8 %shard_map.96 = (f32[4096,128]{1,0:T(8,128)}, f32[432,32]{1,0:T(8,128)}, f32[864,32]{1,0:T(8,128)}) custom-call(s32[1]{0:T(128)} %bitcast.6.refs_0_, bf16[16,144,128]{2,1,0:T(8,128)(2,1)S(1)} %all_to_all.16.refs_1_, bf16[16,144,128]{2,1,0:T(8,128)(2,1)S(1)} %collective-permute-done.6.refs_2_), custom_call_target="tpu_custom_call" | custom-call | tf_op jit(solution)/shard_map/pallas_call | solution.py:262
Async XLA Ops:
  0.6 15.7 %collective-permute-start.1 = (bf16[32,64,128]{2,1,0:T(8,128)(2,1)}, bf16[32,64,128]{2,1,0:T(8,128)(2,1)S(1)}, u32[]{:S(2)}, u32[]{:S(2)}) collective-permute-start(bf16[32,64,128]{2,1,0:T(8,128)(2,1)} %bitcast.14), channel_id=1, source_target_pairs={{1,0},{2,1},{3,2},{5,4},{6,5},{7,6},{9,8},{10,9},{11,10},{13,12},{... | collective-permute-start | bytes 1572872 | tf_op jit(solution)/shard_map/ppermute | solution.py:280
  2.6 13.7 %collective-permute-start = (bf16[32,64,128]{2,1,0:T(8,128)(2,1)}, bf16[32,64,128]{2,1,0:T(8,128)(2,1)S(1)}, u32[]{:S(2)}, u32[]{:S(2)}) collective-permute-start(bf16[32,64,128]{2,1,0:T(8,128)(2,1)} %bitcast.15), channel_id=1, source_target_pairs={{0,1},{1,2},{2,3},{4,5},{5,6},{6,7},{8,9},{9,10},{10,11},{12,13},{... | collective-permute-start | bytes 1572872 | tf_op jit(solution)/shard_map/ppermute | solution.py:280
  7.1 8.0 %collective-permute-start.3 = (bf16[16,64,128]{2,1,0:T(8,128)(2,1)}, bf16[16,64,128]{2,1,0:T(8,128)(2,1)S(1)}, u32[]{:S(2)}, u32[]{:S(2)}) collective-permute-start(bf16[16,64,128]{2,1,0:T(8,128)(2,1)} %bitcast.18), channel_id=1, source_target_pairs={{1,0},{2,1},{3,2},{5,4},{6,5},{7,6},{9,8},{10,9},{11,10},{13,12},{... | collective-permute-start | bytes 786440 | tf_op jit(solution)/shard_map/ppermute | solution.py:280
  9.0 7.3 %collective-permute-start.2 = (bf16[16,64,128]{2,1,0:T(8,128)(2,1)}, bf16[16,64,128]{2,1,0:T(8,128)(2,1)S(1)}, u32[]{:S(2)}, u32[]{:S(2)}) collective-permute-start(bf16[16,64,128]{2,1,0:T(8,128)(2,1)} %bitcast.19), channel_id=1, source_target_pairs={{0,1},{1,2},{2,3},{4,5},{5,6},{6,7},{8,9},{9,10},{10,11},{12,13},{... | collective-permute-start | bytes 786440 | tf_op jit(solution)/shard_map/ppermute | solution.py:280
  16.3 1.0 copy-start
  17.4 1.0 copy-start.1
  18.4 0.9 copy-start.2
  34.2 29.7 %all-to-all-start.1 = ((bf16[32,16,128]{2,1,0:T(8,128)(2,1)}), bf16[32,16,128]{2,1,0:T(8,128)(2,1)S(1)}, u32[]{:S(2)}, u32[]{:S(2)}) async-start(bf16[32,16,128]{2,1,0:T(8,128)(2,1)} %bitcast.7), calls=%async_computation.1 | async-start | bytes 262144 | tf_op jit(solution)/shard_map/all_to_all | solution.py:298
  116.6 12.6 %collective-permute-start.6 = (bf16[16,144,128]{2,1,0:T(8,128)(2,1)S(1)}, bf16[16,144,128]{2,1,0:T(8,128)(2,1)S(1)}, u32[]{:S(2)}, u32[]{:S(2)}) collective-permute-start(bf16[16,144,128]{2,1,0:T(8,128)(2,1)S(1)} %all_to_all.16.refs_1_), channel_id=1, source_target_pairs={{0,1},{1,0},{2,3},{3,2},{4,5},{5,4},{6,7},{7,6},{8,9},{9,8},{10,11... | collective-permute-start | bytes 1769480 | tf_op jit(solution)/shard_map/ppermute | solution.py:308
  118.4 5.4 %collective-permute-start.4 = (bf16[1024,128]{1,0:T(8,128)(2,1)S(1)}, bf16[1024,128]{1,0:T(8,128)(2,1)S(1)}, u32[]{:S(2)}, u32[]{:S(2)}) collective-permute-start(bf16[1024,128]{1,0:T(8,128)(2,1)S(1)} %get-tuple-element.12), channel_id=1, source_target_pairs={{0,1},{1,2},{2,3},{4,5},{5,6},{6,7},{8,9},{9,10},{10,11},{12,13},{... | collective-permute-start | bytes 786440 | tf_op jit(solution)/shard_map/ppermute | solution.py:301
  120.5 7.7 %collective-permute-start.5 = (bf16[1024,128]{1,0:T(8,128)(2,1)S(1)}, bf16[1024,128]{1,0:T(8,128)(2,1)S(1)}, u32[]{:S(2)}, u32[]{:S(2)}) collective-permute-start(bf16[1024,128]{1,0:T(8,128)(2,1)S(1)} %get-tuple-element.13), channel_id=1, source_target_pairs={{1,0},{2,1},{3,2},{5,4},{6,5},{7,6},{9,8},{10,9},{11,10},{13,12},{... | collective-permute-start | bytes 786440 | tf_op jit(solution)/shard_map/ppermute | solution.py:302
where the time goes:
time: 131 us
  blocking collectives  52.4 us (40%)
  starting transfers between devices  25.1 us (19%)
  other arithmetic  22.8 us (17%)
  Pallas kernels  17.8 us (14%)
  waiting for transfers between devices  6.67 us (5%)
  local copies, waits for them, and re-layouts  5.41 us (4%)
    all_to_all x1, blocking collectives, per_device(): parts = lax.all_to_all(parts, EVERY, 0, 0)  31 us
    convert_element_type x1, other arithmetic, per_device(): grad_bucket.reshape(devices, length // devices // LANES, LANES).astype(BF16)  22.8 us
    all_to_all x1, blocking collectives, per_device(): mine = lax.all_to_all(shares, ('dp', 'slab'), 0, 0)  21.4 us
    pallas_call x1, Pallas kernels, compute(): vmem_call(compute_kernel, (jax.ShapeDtypeStruct((rows, LANES), BF16), jax...  14.8 us
    ppermute x4, starting transfers between devices, halos(): return (lax.ppermute(value, SPACE, up), lax.ppermute(value, SPACE, down))  12 us
    all_to_all x1, starting transfers between devices, per_device(): lax.all_to_all(terms.reshape(devices, rows // devices, LANES), EVERY, 0, 0)  6.85 us
    ppermute x1, waiting for transfers between devices, per_device(): from_above = lax.ppermute(down, SPACE, [(j, i) for i, j in upward])  4.4 us
    unnamed x6, local copies, waits for them, and re-layouts  3.03 us
  transfers between devices with their start and end apart: 8, of which 3 were waited for; matrix products, arithmetic and copies ran while one was open for 19% of the time, Pallas kernels for 1%

commit v1 on v0

--- a/solution.py
+++ b/solution.py
@@ -48,44 +48,109 @@
     lax.fori_loop(0, length, gather, 0, unroll=4)
 
 
+def pack_kernel(cot, vol, out, flat):
+    c2, length, width = cot.shape
+    pitch = c2 + vol.shape[0]
+    zeros = jnp.zeros((pitch, width), BF16)
+    out[0:pitch, :] = zeros
+    out[(length + 1) * pitch : (length + 2) * pitch, :] = zeros
+    turned(cot, flat, out, 0, pitch, 1)
+    turned(vol, flat, out, c2, pitch, 1)
+
+
+def pack(cot, vol):
+    c2, length, width = cot.shape
+    pitch = c2 + vol.shape[0]
+    return vmem_call(
+        pack_kernel,
+        jax.ShapeDtypeStruct(((length + 2) * pitch, width), BF16),
+        (pltpu.VMEM((max(c2, vol.shape[0]) * length, width), F32),),
+        pl.CostEstimate(flops=0, bytes_accessed=4 * cot.size, transcendentals=0),
+    )(cot, vol)
+
+
+def slide_kernel(act, out, flat, rows):
+    c1, length, _ = act.shape
+    turned(act, flat, rows, 0, c1, 0)
+
+    def slide(x, carry):
+        value = rows[pl.ds(pl.multiple_of(x * c1, 16), c1), :].astype(F32)
+        stack = jnp.concatenate([slid(value, 1), value, slid(value, -1)], axis=0)
+        out[pl.ds(pl.multiple_of(x * 3 * c1, 16), 3 * c1), :] = stack.astype(BF16)
+        return carry
+
+    lax.fori_loop(0, length, slide, 0, unroll=4)
+
+
+def slide(act):
+    c1, length, width = act.shape
+    return vmem_call(
+        slide_kernel,
+        jax.ShapeDtypeStruct((length * 3 * c1, width), BF16),
+        (
+            pltpu.VMEM((c1 * length, width), F32),
+            pltpu.VMEM((c1 * length, width), BF16),
+        ),
+        pl.CostEstimate(flops=0, bytes_accessed=8 * act.size, transcendentals=0),
+    )(act)
+
+
+def cast_kernel(src, out):
+    out[...] = src[...].reshape(out.shape).astype(out.dtype)
+
+
+def cast(value, devices):
+    rows = value.shape[0] // devices
+    steps = 4
+    return pl.pallas_call(
+        cast_kernel,
+        grid=(steps,),
+        out_shape=jax.ShapeDtypeStruct((devices, rows, LANES), BF16),
+        in_specs=[pl.BlockSpec((value.shape[0] // steps, LANES), lambda n: (n, 0))],
+        out_specs=pl.BlockSpec((devices // steps, rows, LANES), lambda n: (n, 0, 0)),
+        cost_estimate=pl.CostEstimate(flops=0, bytes_accessed=6 * value.size, transcendentals=0),
+    )(value)
+
+
 def compute_kernel(
-    cot_m, cot_0, cot_p, act, vol_m, vol_0, vol_p, w_two, w_one,
+    pack_m, pack_0, pack_p, acts, w_two, w_one,
     terms, own, up, down,
-    flat, cots, acts, vols, pres, acc_two, acc_one,
+    pres, acc_two, acc_one,
 ):
-    c1, length, _ = act.shape
-    c0 = vol_0.shape[0]
-    c2 = cot_0.shape[0]
-    wide_two, wide_one = 3 * c2, 3 * c0
-
-    for buffer, rows in ((cots, wide_two), (vols, wide_one), (pres, c1)):
-        zeros = jnp.zeros((rows, LANES), BF16)
-        buffer[0:rows, :] = zeros
-        buffer[(length + 1) * rows : (length + 2) * rows, :] = zeros
-    for place, src in enumerate((cot_m, cot_0, cot_p)):
-        turned(src, flat, cots, place * c2, wide_two, 1)
-    for place, src in enumerate((vol_m, vol_0, vol_p)):
-        turned(src, flat, vols, place * c0, wide_one, 1)
-    turned(act, flat, acts, 0, c1, 0)
+    length = acts.shape[0] // w_two.shape[0]
+    c1 = w_two.shape[0] // 3
+    c2 = w_two.shape[1] // 9
+    c0 = w_one.shape[0] // 9
+    pitch = c0 + c2
+    packs = (pack_m, pack_0, pack_p)
+
+    pres[0:c1, :] = jnp.zeros((c1, LANES), BF16)
+    pres[(length + 1) * c1 : (length + 2) * c1, :] = jnp.zeros((c1, LANES), BF16)
     acc_two[...] = jnp.zeros_like(acc_two)
     acc_one[...] = jnp.zeros_like(acc_one)
 
+    def windows(x, offset, count):
+        rows = [
+            [p[pl.ds(pl.multiple_of((x + n) * pitch + offset, 16), count), :] for p in packs]
+            for n in range(GROUP + 2)
+        ]
+        return jnp.concatenate(
+            [jnp.concatenate(sum(rows[g : g + 3], []), axis=0) for g in range(GROUP)], axis=1
+        )
+
     def first(step, carry):
         x = step * GROUP
-        window = cots[pl.ds(pl.multiple_of(x * wide_two, 16), (GROUP + 2) * wide_two), :]
-        right = beside(window, 3 * wide_two, wide_two, GROUP)
+        right = windows(x, 0, c2)
         sums = jnp.dot(w_two[...], right, preferred_element_type=F32)
-        field = acts[pl.ds(pl.multiple_of(x * c1, 16), GROUP * c1), :].astype(F32)
         columns = []
         for g in range(GROUP):
             part = sums[:, g * LANES : (g + 1) * LANES]
             grad = slid(part[0:c1], 1) + part[c1 : 2 * c1] + slid(part[2 * c1 : 3 * c1], -1)
-            value = field[g * c1 : (g + 1) * c1]
+            stack = acts[pl.ds(pl.multiple_of((x + g) * 3 * c1, 16), 3 * c1), :]
+            value = stack[c1 : 2 * c1].astype(F32)
             pre = (grad * jnp.where(value > 0, 1.0, 0.2)).astype(BF16)
             pres[pl.ds(pl.multiple_of((x + g + 1) * c1, 16), c1), :] = pre
-            columns.append(
-                jnp.concatenate([slid(value, 1), value, slid(value, -1)], axis=0).astype(BF16)
-            )
+            columns.append(stack)
         left = jnp.concatenate(columns, axis=1)
         acc_two[...] += lax.dot_general(
             right, left, (((1,), (1,)), ((), ())), preferred_element_type=F32
@@ -115,10 +180,8 @@
                 jnp.concatenate([slid(value, -1), value, slid(value, 1)], axis=0).astype(BF16)
             )
         left = jnp.concatenate(columns, axis=1)
-        volume = vols[pl.ds(pl.multiple_of(x * wide_one, 16), (GROUP + 2) * wide_one), :]
-        right = beside(volume, 3 * wide_one, wide_one, GROUP)
         acc_one[...] += lax.dot_general(
-            right, left, (((1,), (1,)), ((), ())), preferred_element_type=F32
+            windows(x, c2, c0), left, (((1,), (1,)), ((), ())), preferred_element_type=F32
         )
         return carry
 
@@ -135,7 +198,7 @@
     terms[blocks * rows : blocks * rows + one.shape[0], 0 : one.shape[1]] = one.astype(terms.dtype)
 
 
-def vmem_call(body, out_shape, scratch=(), cost=None, limit=48 * 2**20):
+def vmem_call(body, out_shape, scratch=(), cost=None, limit=24 * 2**20):
     spec = pl.BlockSpec(memory_space=pltpu.VMEM)
     return pl.pallas_call(
         body,
@@ -147,13 +210,13 @@
     )
 
 
-def compute(cots, act, vols, kernel_two, kernel_one, rows):
-    c1, length, width = act.shape
-    c0, c2 = (vols[0].shape[0], cots[0].shape[0])
+def compute(packs, acts, kernel_two, kernel_one, rows):
+    c0, c1 = kernel_one.shape[3:]
+    c2 = kernel_two.shape[4]
     w_two = kernel_two[::-1, ::-1, ::-1].transpose(2, 3, 1, 0, 4).reshape(3 * c1, 9 * c2)
     w_one = kernel_one[::-1, ::-1, ::-1].transpose(0, 2, 3, 1, 4).reshape(9 * c0, 3 * c1)
+    length, width = (acts.shape[0] // (3 * c1), acts.shape[1])
     plane = (length * c0, width)
-    flops = 2 * 27 * length * width * c1 * 2 * (c0 + c2)
     return vmem_call(
         compute_kernel,
         (
@@ -163,16 +226,12 @@
             jax.ShapeDtypeStruct(plane, BF16),
         ),
         (
-            pltpu.VMEM((max(c0, c1, c2) * length, width), F32),
-            pltpu.VMEM(((length + 2) * 3 * c2, width), BF16),
-            pltpu.VMEM((length * c1, width), BF16),
-            pltpu.VMEM(((length + 2) * 3 * c0, width), BF16),
             pltpu.VMEM(((length + 2) * c1, width), BF16),
             pltpu.VMEM((9 * c2, 3 * c1), F32),
             pltpu.VMEM((9 * c0, 3 * c1), F32),
         ),
-        pl.CostEstimate(flops=flops, bytes_accessed=5 * 2**20, transcendentals=0),
-    )(*cots, act, *vols, w_two, w_one)
+        pl.CostEstimate(flops=10**10, bytes_accessed=40 * 2**20, transcendentals=0),
+    )(*packs, acts, w_two, w_one)
 
 
 def merge_kernel(own, from_below, from_above, out, flat):
@@ -269,7 +328,7 @@
         in_specs=[pl.BlockSpec(memory_space=pltpu.SMEM), spec, spec],
         out_specs=(spec, spec, spec),
         scratch_shapes=[pltpu.VMEM((2 * copies * extra, LANES), F32)],
-        compiler_params=pltpu.CompilerParams(vmem_limit_bytes=48 * 2**20),
+        compiler_params=pltpu.CompilerParams(vmem_limit_bytes=24 * 2**20),
     )(core, mine, other)
 
 
@@ -283,27 +342,29 @@
 def per_device(volume_in, hidden_act, out_cot, kernel_one, kernel_two, grad_bucket):
     c0, c1, c2 = (volume_in.shape[2], hidden_act.shape[2], out_cot.shape[2])
     devices, copies = (lax.axis_size(EVERY), lax.axis_size(("dp", "slab")))
-    cot, vol = (out_cot[0, 0], volume_in[0, 0])
-    cot_m, cot_p = halos(cot)
-    vol_m, vol_p = halos(vol)
     length = grad_bucket.shape[1]
-    parts = grad_bucket.reshape(devices, length // devices // LANES, LANES).astype(BF16)
+    packed = pack(out_cot[0, 0], volume_in[0, 0])
+    below, above = halos(packed)
+    parts = cast(grad_bucket.reshape(length // LANES, LANES), devices)
+    act, parts = lax.optimization_barrier((hidden_act[0, 0], parts))
     parts = lax.all_to_all(parts, EVERY, 0, 0)
 
     used = -(-9 * c2 // LANES) * 3 * c1 + 9 * c0
     rows = ceil_to(used, 16 * devices)
     terms, own, up, down = compute(
-        (cot_m, cot, cot_p), hidden_act[0, 0], (vol_m, vol, vol_p), kernel_two, kernel_one, rows
+        (below, packed, above), slide(act), kernel_two, kernel_one, rows
     )
+    terms, parts = lax.optimization_barrier((terms, parts))
     terms = lax.all_to_all(terms.reshape(devices, rows // devices, LANES), EVERY, 0, 0)
     count = lax.axis_size(SPACE)
     upward = [(i, i + 1) for i in range(count - 1)]
     from_below = lax.ppermute(up, SPACE, upward)
     from_above = lax.ppermute(down, SPACE, [(j, i) for i, j in upward])
-    grad_input = merge(own, from_below, from_above, vol.shape)
+    grad_input = merge(own, from_below, from_above, volume_in.shape[2:])
 
     cells = volume_in.shape[3] * volume_in.shape[4] * devices
     shares = share(parts, terms, 1.0 / math.sqrt(cells), copies)
+    grad_input, shares = lax.optimization_barrier((grad_input, shares))
     mine = lax.all_to_all(shares, ("dp", "slab"), 0, 0)
     other = lax.ppermute(mine, "core", [(0, 1), (1, 0)])
     core = lax.axis_index("core").astype(jnp.int32).reshape(1)

time: 131 us -> 90.9 us (0.69)
  blocking collectives: 52.4 us -> 19.2 us
  other arithmetic: 22.8 us -> 0 us
  waiting for transfers between devices: 6.67 us -> 15 us
  Pallas kernels: 17.8 us -> 21.6 us
  local copies, waits for them, and re-layouts: 5.41 us -> 8.25 us
    all_to_all x1 -> x0, blocking collectives: 31 us -> none  [per_device(): parts = lax.all_to_all(parts, EVERY, 0, 0)]
    convert_element_type x1 -> x0, other arithmetic: 22.8 us -> none  [per_device(): grad_bucket.reshape(devices, length // devices // LANES, LANES).astype(BF16)]
    pallas_call x0 -> x3, Pallas kernels: none -> 7.2 us  [the longest x1 3.66 us: cast(): pl.pallas_call(cast_kernel, grid=(steps,), out_shape=jax.ShapeDtypeStruct...]
    all_to_all x0 -> x1, starting transfers between devices: none -> 7.1 us  [per_device(): parts = lax.all_to_all(parts, EVERY, 0, 0)]
    ppermute x4 -> x2, starting transfers between devices: 12 us -> 5.46 us  [halos(): return (lax.ppermute(value, SPACE, up), lax.ppermute(value, SPACE, down))]
    all_to_all x1, waiting for transfers between devices: 0.01 us -> 6.16 us  [per_device(): lax.all_to_all(terms.reshape(devices, rows // devices, LANES), EVERY, 0, 0)]
    ppermute x4 -> x2, waiting for transfers between devices: 1.24 us -> 7.19 us  [halos(): return (lax.ppermute(value, SPACE, up), lax.ppermute(value, SPACE, down))]
    ppermute x1, waiting for transfers between devices: 4.4 us -> 0.01 us  [per_device(): from_above = lax.ppermute(down, SPACE, [(j, i) for i, j in upward])]
  transfers between devices with their start and end apart: 8 -> 7, of which waited for: 3 -> 4; matrix products, arithmetic and copies ran while one was open for 19% -> 5% of each run, Pallas kernels for 1% -> 18%
where the time goes in v1:
time: 90.9 us; the launch traced here: 90 us
  starting transfers between devices  25.1 us (28%)
  Pallas kernels  21.6 us (24%)
  blocking collectives  19.2 us (21%)
  waiting for transfers between devices  15 us (17%)
  local copies, waits for them, and re-layouts  8.25 us (9%)
    all_to_all x1, blocking collectives, per_device(): mine = lax.all_to_all(shares, ('dp', 'slab'), 0, 0)  19.2 us
    pallas_call x1, Pallas kernels, compute(): vmem_call(compute_kernel, (jax.ShapeDtypeStruct((rows, LANES), BF16), jax...  11.4 us
    ppermute x2, waiting for transfers between devices, halos(): return (lax.ppermute(value, SPACE, up), lax.ppermute(value, SPACE, down))  7.19 us
    all_to_all x1, starting transfers between devices, per_device(): parts = lax.all_to_all(parts, EVERY, 0, 0)  7.1 us
    all_to_all x1, starting transfers between devices, per_device(): lax.all_to_all(terms.reshape(devices, rows // devices, LANES), EVERY, 0, 0)  6.21 us
    all_to_all x1, waiting for transfers between devices, per_device(): lax.all_to_all(terms.reshape(devices, rows // devices, LANES), EVERY, 0, 0)  6.16 us
    ppermute x2, starting transfers between devices, halos(): return (lax.ppermute(value, SPACE, up), lax.ppermute(value, SPACE, down))  5.46 us
    pallas_call x1, Pallas kernels, cast(): pl.pallas_call(cast_kernel, grid=(steps,), out_shape=jax.ShapeDtypeStruct...  3.66 us
  transfers between devices with their start and end apart: 7, of which 4 were waited for; matrix products, arithmetic and copies ran while one was open for 5% of the time, Pallas kernels for 18%

profile of v1, /device:TPU:1, one launch (start us, length us, event | category | flops | bytes accessed | tf_op | source)
XLA Modules:
  0.0 90.0 jit_solution(14375488418202833517)
XLA Ops:
  0.6 0.0 copy-start
  0.6 0.0 copy-start.4
  0.7 3.7 %shard_map.94 = bf16[32,128,128]{2,1,0:T(8,128)(2,1)} custom-call(f32[4096,128]{1,0:T(8,128)} %bitcast.18), custom_call_target="tpu_custom_call" | custom-call | bytes 3145728 | tf_op jit(solution)/shard_map/pallas_call | solution.py:105
  4.3 7.1 %all-to-all-start = ((bf16[32,128,128]{2,1,0:T(8,128)(2,1)}), bf16[32,128,128]{2,1,0:T(8,128)(2,1)S(1)}, u32[]{:S(2)}, u32[]{:S(2)}) async-start(bf16[32,128,128]{2,1,0:T(8,128)(2,1)} %shard_map.94), calls=%async_computation | async-start | bytes 2097152 | tf_op jit(solution)/shard_map/all_to_all | solution.py:350
  11.4 0.0 copy-start.6
  11.4 0.0 copy-done
  11.4 0.0 copy-done.4
  11.4 1.3 %shard_map.93.pack_0 = bf16[3168,128]{1,0:T(8,128)(2,1)S(1)} custom-call(bf16[32,64,128]{2,1,0:T(8,128)(2,1)S(1)} %bitcast.14, bf16[16,64,128]{2,1,0:T(8,128)(2,1)S(1)} %bitcast.16), custom_call_target="tpu_custom_call" | custom-call | bytes 1048576 | tf_op jit(solution)/shard_map/pallas_call | solution.py:64
  12.7 3.5 %collective-permute-start = (bf16[3168,128]{1,0:T(8,128)(2,1)S(1)}, bf16[3168,128]{1,0:T(8,128)(2,1)}, u32[]{:S(2)}, u32[]{:S(2)}) collective-permute-start(bf16[3168,128]{1,0:T(8,128)(2,1)S(1)} %shard_map.93.pack_0), channel_id=1, source_target_pairs={{0,1},{1,2},{2,3},{4,5},{5,6},{6,7},{8,9},{9,10},{10,11},{12,13},{... | collective-permute-start | bytes 2433032 | tf_op jit(solution)/shard_map/ppermute | solution.py:339
  16.3 1.9 %collective-permute-start.1 = (bf16[3168,128]{1,0:T(8,128)(2,1)S(1)}, bf16[3168,128]{1,0:T(8,128)(2,1)}, u32[]{:S(2)}, u32[]{:S(2)}) collective-permute-start(bf16[3168,128]{1,0:T(8,128)(2,1)S(1)} %shard_map.93.pack_0), channel_id=1, source_target_pairs={{1,0},{2,1},{3,2},{5,4},{6,5},{7,6},{9,8},{10,9},{11,10},{13,12},{... | collective-permute-start | bytes 2433032 | tf_op jit(solution)/shard_map/ppermute | solution.py:339
  18.2 0.0 copy-start.3
  18.2 1.0 %copy-done.3 = bf16[1,1,32,64,128]{4,3,2,1,0:T(8,128)(2,1)S(1)} copy-done((bf16[1,1,32,64,128]{4,3,2,1,0:T(8,128)(2,1)S(1)}, bf16[1,1,32,64,128]{4,3,2,1,0:T(8,128)(2,1)}, u32[]{:S(2)}) %copy-start.3) | copy-done | bytes 524312
  19.3 2.2 %shard_map.95.acts = bf16[6144,128]{1,0:T(8,128)(2,1)S(1)} custom-call(bf16[32,64,128]{2,1,0:T(8,128)(2,1)S(1)} %bitcast.15), custom_call_target="tpu_custom_call" | custom-call | bytes 2097152 | tf_op jit(solution)/shard_map/pallas_call | solution.py:87
  21.5 0.0 copy-done.6
  21.6 0.9 copy.12
  22.4 1.2 %reshape.33.w_two = bf16[96,288]{1,0:T(8,128)(2,1)S(1)} reshape(bf16[3,32,3,3,32]{4,3,2,1,0:T(4,128)(2,1)} %copy.12) | data formatting | bytes 110592 | tf_op jit(solution)/shard_map/reshape | solution.py:216
  23.6 0.9 %reverse_bitcast_fusion.1 = bf16[3,3,16,3,32]{4,2,1,3,0:T(8,128)(2,1)S(1)} fusion(bf16[3,3,3,16,32]{4,3,2,1,0:T(8,128)(2,1)} %param.9), kind=kLoop, calls=%fused_computation.1 | loop fusion | bytes 55296 | tf_op jit(solution)/shard_map/transpose | solution.py:217
  24.5 0.7 copy.13
  25.2 1.0 %reshape.34.w_one = bf16[144,96]{1,0:T(8,128)(2,1)S(1)} reshape(bf16[3,3,16,3,32]{4,3,2,1,0:T(4,128)(2,1)} %copy.13) | data formatting | bytes 55296 | tf_op jit(solution)/shard_map/reshape | solution.py:217
  26.3 5.4 %collective-permute-done.pack_m = bf16[3168,128]{1,0:T(8,128)(2,1)} collective-permute-done((bf16[3168,128]{1,0:T(8,128)(2,1)S(1)}, bf16[3168,128]{1,0:T(8,128)(2,1)}, u32[]{:S(2)}, u32[]{:S(2)}) %collective-permute-start) | collective-permute-done | bytes 811040 | tf_op jit(solution)/shard_map/ppermute | solution.py:339
  31.6 1.8 %collective-permute-done.1.pack_p = bf16[3168,128]{1,0:T(8,128)(2,1)} collective-permute-done((bf16[3168,128]{1,0:T(8,128)(2,1)S(1)}, bf16[3168,128]{1,0:T(8,128)(2,1)}, u32[]{:S(2)}, u32[]{:S(2)}) %collective-permute-start.1) | collective-permute-done | bytes 811040 | tf_op jit(solution)/shard_map/ppermute | solution.py:339
  33.5 11.4 %shard_map.96 = (bf16[512,128]{1,0:T(8,128)(2,1)S(1)}, f32[1024,128]{1,0:T(8,128)S(1)}, bf16[1024,128]{1,0:T(8,128)(2,1)}, bf16[1024,128]{1,0:T(8,128)(2,1)}) custom-call(bf16[3168,128]{1,0:T(8,128)(2,1)} %collective-permute-done.pack_m, bf16[3168,128]{1,0:T(8,128)(2,1)S(1)} %shard_map.93.pack_0, bf16[3168,128]{1,0:T(8,128)(2,1)} %collective-permute-done.1.pack_p, ...), custom_call_target="tpu_custom_call" | custom-call | flops 10000000000 | bytes 41943040 | tf_op jit(solution)/shard_map/pallas_call | solution.py:220
  44.8 0.0 copy-start.1
  44.8 0.8 copy-done.1
  45.6 0.0 copy-start.5
  45.6 0.7 copy-done.5
  46.3 2.7 %collective-permute-start.2 = (bf16[1024,128]{1,0:T(8,128)(2,1)}, bf16[1024,128]{1,0:T(8,128)(2,1)S(1)}, u32[]{:S(2)}, u32[]{:S(2)}) collective-permute-start(bf16[1024,128]{1,0:T(8,128)(2,1)} %get-tuple-element.19), channel_id=1, source_target_pairs={{0,1},{1,2},{2,3},{4,5},{5,6},{6,7},{8,9},{9,10},{10,11},{12,13},{... | collective-permute-start | bytes 786440 | tf_op jit(solution)/shard_map/ppermute | solution.py:361
  48.9 1.9 %collective-permute-start.3 = (bf16[1024,128]{1,0:T(8,128)(2,1)}, bf16[1024,128]{1,0:T(8,128)(2,1)S(1)}, u32[]{:S(2)}, u32[]{:S(2)}) collective-permute-start(bf16[1024,128]{1,0:T(8,128)(2,1)} %get-tuple-element.20), channel_id=1, source_target_pairs={{1,0},{2,1},{3,2},{5,4},{6,5},{7,6},{9,8},{10,9},{11,10},{13,12},{... | collective-permute-start | bytes 786440 | tf_op jit(solution)/shard_map/ppermute | solution.py:362
  50.9 0.0 all-to-all-done.refs_0_
  50.9 6.2 %all-to-all-start.1 = ((bf16[32,16,128]{2,1,0:T(8,128)(2,1)}), bf16[32,16,128]{2,1,0:T(8,128)(2,1)S(1)}, u32[]{:S(2)}, u32[]{:S(2)}) async-start(bf16[32,16,128]{2,1,0:T(8,128)(2,1)} %bitcast.17), calls=%async_computation.1 | async-start | bytes 262144 | tf_op jit(solution)/shard_map/all_to_all | solution.py:358
  57.1 0.0 collective-permute-done.2.from_below
  57.1 0.0 collective-permute-done.3.from_above
  57.1 0.0 copy-start.2
  57.1 1.0 %copy-done.2 = f32[1024,128]{1,0:T(8,128)S(1)} copy-done((f32[1024,128]{1,0:T(8,128)S(1)}, f32[1024,128]{1,0:T(8,128)}, u32[]{:S(2)}) %copy-start.2) | copy-done | bytes 524312
  58.1 1.0 %shard_map.97 = bf16[16,64,128]{2,1,0:T(8,128)(2,1)} custom-call(f32[1024,128]{1,0:T(8,128)S(1)} %copy-done.2, bf16[1024,128]{1,0:T(8,128)(2,1)S(1)} %collective-permute-done.2.from_below, bf16[1024,128]{1,0:T(8,128)(2,1)S(1)} %collective-permute-done.3.from_above), custom_call_target="tpu_custom_call" | custom-call | flops 262144 | bytes 1048576 | tf_op jit(solution)/shard_map/pallas_call | solution.py:255
  59.1 6.2 %all-to-all-done.1.refs_1_ = bf16[32,16,128]{2,1,0:T(8,128)(2,1)S(1)} async-done(((bf16[32,16,128]{2,1,0:T(8,128)(2,1)}), bf16[32,16,128]{2,1,0:T(8,128)(2,1)S(1)}, u32[]{:S(2)}, u32[]{:S(2)}) %all-to-all-start.1) | async-done | bytes 131104 | tf_op jit(solution)/shard_map/all_to_all | solution.py:358
  65.3 0.3 shard_map.98
  65.6 19.2 %all_to_all.15.refs_1_ = bf16[16,144,128]{2,1,0:T(8,128)(2,1)S(1)} all-to-all(bf16[16,144,128]{2,1,0:T(8,128)(2,1)S(1)} %shard_map.98), channel_id=1, replica_groups=mesh['dp'=8,'slab'=2,'core'=2] {'dp','slab'}, dimensions={0} | all-to-all | bytes 1179648 | tf_op jit(solution)/shard_map/all_to_all | solution.py:368
  84.8 1.8 %collective-permute-start.4 = (bf16[16,144,128]{2,1,0:T(8,128)(2,1)S(1)}, bf16[16,144,128]{2,1,0:T(8,128)(2,1)S(1)}, u32[]{:S(2)}, u32[]{:S(2)}) collective-permute-start(bf16[16,144,128]{2,1,0:T(8,128)(2,1)S(1)} %all_to_all.15.refs_1_), channel_id=1, source_target_pairs={{0,1},{1,0},{2,3},{3,2},{4,5},{5,4},{6,7},{7,6},{8,9},{9,8},{10,11... | collective-permute-start | bytes 1769480 | tf_op jit(solution)/shard_map/ppermute | solution.py:369
  86.6 1.6 %collective-permute-done.4.refs_2_ = bf16[16,144,128]{2,1,0:T(8,128)(2,1)S(1)} collective-permute-done((bf16[16,144,128]{2,1,0:T(8,128)(2,1)S(1)}, bf16[16,144,128]{2,1,0:T(8,128)(2,1)S(1)}, u32[]{:S(2)}, u32[]{:S(2)}) %collective-permute-start.4) | collective-permute-done | bytes 589856 | tf_op jit(solution)/shard_map/ppermute | solution.py:369
  88.2 1.8 %shard_map.99 = (f32[4096,128]{1,0:T(8,128)}, f32[432,32]{1,0:T(8,128)}, f32[864,32]{1,0:T(8,128)}) custom-call(s32[1]{0:T(128)} %bitcast.8.refs_0_, bf16[16,144,128]{2,1,0:T(8,128)(2,1)S(1)} %all_to_all.15.refs_1_, bf16[16,144,128]{2,1,0:T(8,128)(2,1)S(1)} %collective-permute-done.4.refs_2_), custom_call_target="tpu_custom_call" | custom-call | tf_op jit(solution)/shard_map/pallas_call | solution.py:321
  (1 shorter events, 0.0 us)
Async XLA Ops:
  0.6 10.8 %copy-start = (bf16[1,1,32,64,128]{4,3,2,1,0:T(8,128)(2,1)S(1)}, bf16[1,1,32,64,128]{4,3,2,1,0:T(8,128)(2,1)}, u32[]{:S(2)}) copy-start(bf16[1,1,32,64,128]{4,3,2,1,0:T(8,128)(2,1)} %param.8) | copy-start | bytes 1572868
  0.6 10.8 %copy-start.4 = (bf16[1,1,16,64,128]{4,3,2,1,0:T(8,128)(2,1)S(1)}, bf16[1,1,16,64,128]{4,3,2,1,0:T(8,128)(2,1)}, u32[]{:S(2)}) copy-start(bf16[1,1,16,64,128]{4,3,2,1,0:T(8,128)(2,1)} %param.6) | copy-start | bytes 786436
  4.3 46.6 %all-to-all-start = ((bf16[32,128,128]{2,1,0:T(8,128)(2,1)}), bf16[32,128,128]{2,1,0:T(8,128)(2,1)S(1)}, u32[]{:S(2)}, u32[]{:S(2)}) async-start(bf16[32,128,128]{2,1,0:T(8,128)(2,1)} %shard_map.94), calls=%async_computation | async-start | bytes 2097152 | tf_op jit(solution)/shard_map/all_to_all | solution.py:350
  11.4 10.1 %copy-start.6 = (bf16[3,3,3,32,32]{4,3,2,1,0:T(8,128)(2,1)S(1)}, bf16[3,3,3,32,32]{4,3,2,1,0:T(8,128)(2,1)}, u32[]{:S(2)}) copy-start(bf16[3,3,3,32,32]{4,3,2,1,0:T(8,128)(2,1)} %param.10) | copy-start | bytes 165892
  12.7 18.9 %collective-permute-start = (bf16[3168,128]{1,0:T(8,128)(2,1)S(1)}, bf16[3168,128]{1,0:T(8,128)(2,1)}, u32[]{:S(2)}, u32[]{:S(2)}) collective-permute-start(bf16[3168,128]{1,0:T(8,128)(2,1)S(1)} %shard_map.93.pack_0), channel_id=1, source_target_pairs={{0,1},{1,2},{2,3},{4,5},{5,6},{6,7},{8,9},{9,10},{10,11},{12,13},{... | collective-permute-start | bytes 2433032 | tf_op jit(solution)/shard_map/ppermute | solution.py:339
  16.3 17.2 %collective-permute-start.1 = (bf16[3168,128]{1,0:T(8,128)(2,1)S(1)}, bf16[3168,128]{1,0:T(8,128)(2,1)}, u32[]{:S(2)}, u32[]{:S(2)}) collective-permute-start(bf16[3168,128]{1,0:T(8,128)(2,1)S(1)} %shard_map.93.pack_0), channel_id=1, source_target_pairs={{1,0},{2,1},{3,2},{5,4},{6,5},{7,6},{9,8},{10,9},{11,10},{13,12},{... | collective-permute-start | bytes 2433032 | tf_op jit(solution)/shard_map/ppermute | solution.py:339
  18.2 1.0 %copy-start.3 = (bf16[1,1,32,64,128]{4,3,2,1,0:T(8,128)(2,1)S(1)}, bf16[1,1,32,64,128]{4,3,2,1,0:T(8,128)(2,1)}, u32[]{:S(2)}) copy-start(bf16[1,1,32,64,128]{4,3,2,1,0:T(8,128)(2,1)} %param.7) | copy-start | bytes 1572868
  44.8 0.8 copy-start.1
  45.6 0.7 copy-start.5
  46.3 10.8 %collective-permute-start.2 = (bf16[1024,128]{1,0:T(8,128)(2,1)}, bf16[1024,128]{1,0:T(8,128)(2,1)S(1)}, u32[]{:S(2)}, u32[]{:S(2)}) collective-permute-start(bf16[1024,128]{1,0:T(8,128)(2,1)} %get-tuple-element.19), channel_id=1, source_target_pairs={{0,1},{1,2},{2,3},{4,5},{5,6},{6,7},{8,9},{9,10},{10,11},{12,13},{... | collective-permute-start | bytes 786440 | tf_op jit(solution)/shard_map/ppermute | solution.py:361
  48.9 8.2 %collective-permute-start.3 = (bf16[1024,128]{1,0:T(8,128)(2,1)}, bf16[1024,128]{1,0:T(8,128)(2,1)S(1)}, u32[]{:S(2)}, u32[]{:S(2)}) collective-permute-start(bf16[1024,128]{1,0:T(8,128)(2,1)} %get-tuple-element.20), channel_id=1, source_target_pairs={{1,0},{2,1},{3,2},{5,4},{6,5},{7,6},{9,8},{10,9},{11,10},{13,12},{... | collective-permute-start | bytes 786440 | tf_op jit(solution)/shard_map/ppermute | solution.py:362
  50.9 14.4 %all-to-all-start.1 = ((bf16[32,16,128]{2,1,0:T(8,128)(2,1)}), bf16[32,16,128]{2,1,0:T(8,128)(2,1)S(1)}, u32[]{:S(2)}, u32[]{:S(2)}) async-start(bf16[32,16,128]{2,1,0:T(8,128)(2,1)} %bitcast.17), calls=%async_computation.1 | async-start | bytes 262144 | tf_op jit(solution)/shard_map/all_to_all | solution.py:358
  57.1 1.0 %copy-start.2 = (f32[1024,128]{1,0:T(8,128)S(1)}, f32[1024,128]{1,0:T(8,128)}, u32[]{:S(2)}) copy-start(f32[1024,128]{1,0:T(8,128)} %copy-done.1) | copy-start | bytes 1572868
  84.8 3.4 %collective-permute-start.4 = (bf16[16,144,128]{2,1,0:T(8,128)(2,1)S(1)}, bf16[16,144,128]{2,1,0:T(8,128)(2,1)S(1)}, u32[]{:S(2)}, u32[]{:S(2)}) collective-permute-start(bf16[16,144,128]{2,1,0:T(8,128)(2,1)S(1)} %all_to_all.15.refs_1_), channel_id=1, source_target_pairs={{0,1},{1,0},{2,3},{3,2},{4,5},{5,4},{6,7},{7,6},{8,9},{9,8},{10,11... | collective-permute-start | bytes 1769480 | tf_op jit(solution)/shard_map/ppermute | solution.py:369

commit v2 on v1

--- a/solution.py
+++ b/solution.py
@@ -9,7 +9,7 @@
 
 SPACE = ("slab", "core")
 EVERY = ("dp", "slab", "core")
-GROUP = 4
+GROUP = 8
 LANES = 128
 BF16 = jnp.bfloat16
 F32 = jnp.float32
@@ -69,7 +69,7 @@
     )(cot, vol)
 
 
-def slide_kernel(act, out, flat, rows):
+def slide_kernel(act, two, one, out, w_two, w_one, flat, rows):
     c1, length, _ = act.shape
     turned(act, flat, rows, 0, c1, 0)
 
@@ -81,35 +81,72 @@
 
     lax.fori_loop(0, length, slide, 0, unroll=4)
 
-
-def slide(act):
+    offsets = [(j, i) for j in range(3) for i in range(3)]
+    w_two[...] = jnp.concatenate(
+        [
+            jnp.concatenate([two[2 - i, 2 - j, 2 - k].astype(F32) for k in range(3)], axis=0)
+            for j, i in offsets
+        ],
+        axis=1,
+    ).astype(BF16)
+    w_one[...] = jnp.concatenate(
+        [
+            jnp.concatenate([one[2 - i, 2 - j, k].astype(F32) for i in range(3)], axis=0)
+            for j, k in offsets
+        ],
+        axis=1,
+    ).astype(BF16)
+
+
+def slide(act, kernel_two, kernel_one):
     c1, length, width = act.shape
+    c0, c2 = (kernel_one.shape[3], kernel_two.shape[4])
     return vmem_call(
         slide_kernel,
-        jax.ShapeDtypeStruct((length * 3 * c1, width), BF16),
+        (
+            jax.ShapeDtypeStruct((length * 3 * c1, width), BF16),
+            jax.ShapeDtypeStruct((3 * c1, 9 * c2), BF16),
+            jax.ShapeDtypeStruct((3 * c0, 9 * c1), BF16),
+        ),
         (
             pltpu.VMEM((c1 * length, width), F32),
             pltpu.VMEM((c1 * length, width), BF16),
         ),
         pl.CostEstimate(flops=0, bytes_accessed=8 * act.size, transcendentals=0),
-    )(act)
-
-
-def cast_kernel(src, out):
-    out[...] = src[...].reshape(out.shape).astype(out.dtype)
-
-
-def cast(value, devices):
-    rows = value.shape[0] // devices
-    steps = 4
+    )(act, kernel_two, kernel_one)
+
+
+def cast_kernel(core, src, out):
+    out[...] = src[...].astype(out.dtype)
+
+
+def half_call(body, core, steps, height, which, value, others, cost):
+    block = (height // steps, LANES)
+    plain = pl.BlockSpec(block, lambda n, core: (n, 0))
+    chosen = pl.BlockSpec(block, lambda n, core: (which(core[0]) * steps + n, 0))
     return pl.pallas_call(
-        cast_kernel,
-        grid=(steps,),
-        out_shape=jax.ShapeDtypeStruct((devices, rows, LANES), BF16),
-        in_specs=[pl.BlockSpec((value.shape[0] // steps, LANES), lambda n: (n, 0))],
-        out_specs=pl.BlockSpec((devices // steps, rows, LANES), lambda n: (n, 0, 0)),
-        cost_estimate=pl.CostEstimate(flops=0, bytes_accessed=6 * value.size, transcendentals=0),
-    )(value)
+        body,
+        grid_spec=pltpu.PrefetchScalarGridSpec(
+            num_scalar_prefetch=1,
+            grid=(steps,),
+            in_specs=[chosen] + [plain] * len(others),
+            out_specs=plain,
+        ),
+        out_shape=jax.ShapeDtypeStruct((height, LANES), BF16),
+        cost_estimate=pl.CostEstimate(flops=0, bytes_accessed=cost, transcendentals=0),
+    )(core, value, *others)
+
+
+def add_kernel(core, src, other, out):
+    out[...] = (src[...] + other[...].astype(F32)).astype(out.dtype)
+
+
+def swapped_half(core, value):
+    height = value.shape[0] // 2
+    steps = 2
+    send = half_call(cast_kernel, core, steps, height, lambda c: 1 - c, value, [], 6 * value.size // 2)
+    other = lax.ppermute(send, "core", [(0, 1), (1, 0)])
+    return half_call(add_kernel, core, steps, height, lambda c: c, value, [other], 4 * value.size)
 
 
 def compute_kernel(
@@ -120,12 +157,13 @@
     length = acts.shape[0] // w_two.shape[0]
     c1 = w_two.shape[0] // 3
     c2 = w_two.shape[1] // 9
-    c0 = w_one.shape[0] // 9
+    c0 = w_one.shape[0] // 3
     pitch = c0 + c2
     packs = (pack_m, pack_0, pack_p)
 
-    pres[0:c1, :] = jnp.zeros((c1, LANES), BF16)
-    pres[(length + 1) * c1 : (length + 2) * c1, :] = jnp.zeros((c1, LANES), BF16)
+    stacked = 3 * c1
+    pres[0:stacked, :] = jnp.zeros((stacked, LANES), BF16)
+    pres[(length + 1) * stacked : (length + 2) * stacked, :] = jnp.zeros((stacked, LANES), BF16)
     acc_two[...] = jnp.zeros_like(acc_two)
     acc_one[...] = jnp.zeros_like(acc_one)
 
@@ -146,10 +184,11 @@
         for g in range(GROUP):
             part = sums[:, g * LANES : (g + 1) * LANES]
             grad = slid(part[0:c1], 1) + part[c1 : 2 * c1] + slid(part[2 * c1 : 3 * c1], -1)
-            stack = acts[pl.ds(pl.multiple_of((x + g) * 3 * c1, 16), 3 * c1), :]
+            stack = acts[pl.ds(pl.multiple_of((x + g) * stacked, 16), stacked), :]
             value = stack[c1 : 2 * c1].astype(F32)
-            pre = (grad * jnp.where(value > 0, 1.0, 0.2)).astype(BF16)
-            pres[pl.ds(pl.multiple_of((x + g + 1) * c1, 16), c1), :] = pre
+            pre = (grad * jnp.where(value > 0, 1.0, 0.2)).astype(BF16).astype(F32)
+            moved = jnp.concatenate([slid(pre, -1), pre, slid(pre, 1)], axis=0).astype(BF16)
+            pres[pl.ds(pl.multiple_of((x + g + 1) * stacked, 16), stacked), :] = moved
             columns.append(stack)
         left = jnp.concatenate(columns, axis=1)
         acc_two[...] += lax.dot_general(
@@ -157,35 +196,27 @@
         )
         return carry
 
-    lax.fori_loop(0, length // GROUP, first, 0)
+    lax.fori_loop(0, length // GROUP, first, 0, unroll=2)
 
     def second(step, carry):
         x = step * GROUP
-        window = pres[pl.ds(pl.multiple_of(x * c1, 16), (GROUP + 2) * c1), :]
-        sums = jnp.dot(w_one[...], beside(window, 3 * c1, c1, GROUP), preferred_element_type=F32)
-        columns = []
+        window = pres[pl.ds(pl.multiple_of(x * stacked, 16), (GROUP + 2) * stacked), :]
+        moved = beside(window, 3 * stacked, stacked, GROUP)
+        sums = jnp.dot(w_one[...], moved, preferred_element_type=F32)
         for g in range(GROUP):
             part = sums[:, g * LANES : (g + 1) * LANES]
             at = pl.ds(pl.multiple_of((x + g) * c0, 16), c0)
             for i, out in ((0, up), (1, own), (2, down)):
-                b = 3 * i * c0
-                grad = (
-                    slid(part[b : b + c0], 1)
-                    + part[b + c0 : b + 2 * c0]
-                    + slid(part[b + 2 * c0 : b + 3 * c0], -1)
-                )
-                out[at, :] = grad.astype(out.dtype)
-            value = window[(g + 1) * c1 : (g + 2) * c1].astype(F32)
-            columns.append(
-                jnp.concatenate([slid(value, -1), value, slid(value, 1)], axis=0).astype(BF16)
-            )
-        left = jnp.concatenate(columns, axis=1)
+                out[at, :] = part[i * c0 : (i + 1) * c0].astype(out.dtype)
         acc_one[...] += lax.dot_general(
-            windows(x, c2, c0), left, (((1,), (1,)), ((), ())), preferred_element_type=F32
+            windows(x, c2, c0),
+            moved[stacked : 2 * stacked],
+            (((1,), (1,)), ((), ())),
+            preferred_element_type=F32,
         )
         return carry
 
-    lax.fori_loop(0, length // GROUP, second, 0)
+    lax.fori_loop(0, length // GROUP, second, 0, unroll=2)
 
     terms[...] = jnp.zeros_like(terms)
     two = acc_two[...].T
@@ -210,11 +241,8 @@
     )
 
 
-def compute(packs, acts, kernel_two, kernel_one, rows):
-    c0, c1 = kernel_one.shape[3:]
-    c2 = kernel_two.shape[4]
-    w_two = kernel_two[::-1, ::-1, ::-1].transpose(2, 3, 1, 0, 4).reshape(3 * c1, 9 * c2)
-    w_one = kernel_one[::-1, ::-1, ::-1].transpose(0, 2, 3, 1, 4).reshape(9 * c0, 3 * c1)
+def compute(packs, acts, w_two, w_one, rows):
+    c0, c1, c2 = (w_one.shape[0] // 3, w_two.shape[0] // 3, w_two.shape[1] // 9)
     length, width = (acts.shape[0] // (3 * c1), acts.shape[1])
     plane = (length * c0, width)
     return vmem_call(
@@ -226,7 +254,7 @@
             jax.ShapeDtypeStruct(plane, BF16),
         ),
         (
-            pltpu.VMEM(((length + 2) * c1, width), BF16),
+            pltpu.VMEM(((length + 2) * 3 * c1, width), BF16),
             pltpu.VMEM((9 * c2, 3 * c1), F32),
             pltpu.VMEM((9 * c0, 3 * c1), F32),
         ),
@@ -292,9 +320,10 @@
 
     def place(q, carry):
         for source, which in ((mine, me), (other, 1 - me)):
-            chunk = 2 * q + which
-            bucket[pl.ds(pl.multiple_of(chunk * height, 8), height), :] = source[q, 0:height, :].astype(F32)
-            raw[pl.ds(pl.multiple_of(chunk * extra, 8), extra), :] = source[q, height:rows, :].astype(F32)
+            at = pl.multiple_of((which * copies + q) * height, 8)
+            bucket[pl.ds(at, height), :] = source[q, 0:height, :].astype(F32)
+            at = pl.multiple_of((2 * q + which) * extra, 8)
+            raw[pl.ds(at, extra), :] = source[q, height:rows, :].astype(F32)
         return carry
 
     lax.fori_loop(0, copies, place, 0)
@@ -343,17 +372,17 @@
     c0, c1, c2 = (volume_in.shape[2], hidden_act.shape[2], out_cot.shape[2])
     devices, copies = (lax.axis_size(EVERY), lax.axis_size(("dp", "slab")))
     length = grad_bucket.shape[1]
+    core = lax.axis_index("core").astype(jnp.int32).reshape(1)
     packed = pack(out_cot[0, 0], volume_in[0, 0])
     below, above = halos(packed)
-    parts = cast(grad_bucket.reshape(length // LANES, LANES), devices)
-    act, parts = lax.optimization_barrier((hidden_act[0, 0], parts))
-    parts = lax.all_to_all(parts, EVERY, 0, 0)
+    half = swapped_half(core, grad_bucket.reshape(length // LANES, LANES))
+    acts, w_two, w_one = slide(hidden_act[0, 0], kernel_two, kernel_one)
+    acts, half = lax.optimization_barrier((acts, half))
+    parts = lax.all_to_all(half.reshape(copies, -1, LANES), ("dp", "slab"), 0, 0)
 
     used = -(-9 * c2 // LANES) * 3 * c1 + 9 * c0
     rows = ceil_to(used, 16 * devices)
-    terms, own, up, down = compute(
-        (below, packed, above), slide(act), kernel_two, kernel_one, rows
-    )
+    terms, own, up, down = compute((below, packed, above), acts, w_two, w_one, rows)
     terms, parts = lax.optimization_barrier((terms, parts))
     terms = lax.all_to_all(terms.reshape(devices, rows // devices, LANES), EVERY, 0, 0)
     count = lax.axis_size(SPACE)
@@ -367,7 +396,6 @@
     grad_input, shares = lax.optimization_barrier((grad_input, shares))
     mine = lax.all_to_all(shares, ("dp", "slab"), 0, 0)
     other = lax.ppermute(mine, "core", [(0, 1), (1, 0)])
-    core = lax.axis_index("core").astype(jnp.int32).reshape(1)
     bucket_sum, total_one, total_two = finish(core, mine, other, length, (c0, c1, c2))
     return (
         grad_input[None, None],

time: 90.9 us -> 76.2 us (0.84)
  local copies, waits for them, and re-layouts: 8.25 us -> 2 us
  waiting for transfers between devices: 15 us -> 8.95 us
  Pallas kernels: 21.6 us -> 17.9 us
  starting transfers between devices: 25.1 us -> 26.6 us
    ppermute x2, waiting for transfers between devices: 7.19 us -> 0.01 us  [halos(): return (lax.ppermute(value, SPACE, up), lax.ppermute(value, SPACE, down))]
    pallas_call x1, Pallas kernels: 11.4 us -> 7.19 us  [compute(): vmem_call(compute_kernel, (jax.ShapeDtypeStruct((rows, LANES), BF16), jax...]
    transpose x4 -> x0, local copies, waits for them, and re-layouts: 2.51 us -> none  [the longest x2 1.63 us: compute(): kernel_one[::-1, ::-1, ::-1].transpose(0, 2, 3, 1, 4)]
    reshape x2 -> x0, local copies, waits for them, and re-layouts: 2.21 us -> none  [the longest x1 1.17 us: compute(): kernel_two[::-1, ::-1, ::-1].transpose(2, 3, 1, 0, 4)]
    unnamed x14 -> x10, local copies, waits for them, and re-layouts: 3.53 us -> 2 us
    ppermute x1, starting transfers between devices: 2.66 us -> 3.71 us  [per_device(): from_below = lax.ppermute(up, SPACE, upward)]
    all_to_all x1, waiting for transfers between devices: 6.16 us -> 7.19 us  [per_device(): lax.all_to_all(terms.reshape(devices, rows // devices, LANES), EVERY, 0, 0)]
    ppermute x2, starting transfers between devices: 5.46 us -> 6.46 us  [halos(): return (lax.ppermute(value, SPACE, up), lax.ppermute(value, SPACE, down))]
  transfers between devices with their start and end apart: 7 -> 8, of which waited for: 4 -> 3; matrix products, arithmetic and copies ran while one was open for 5% -> 0% of each run, Pallas kernels for 18% -> 19%
where the time goes in v2:
time: 76.2 us; the launch traced here: 75.4 us
  starting transfers between devices  26.6 us (35%)
  blocking collectives  19.2 us (25%)
  Pallas kernels  17.9 us (23%)
  waiting for transfers between devices  8.95 us (12%)
  local copies, waits for them, and re-layouts  2 us (3%)
  between operations  0.77 us (1%)
    all_to_all x1, blocking collectives, per_device(): mine = lax.all_to_all(shares, ('dp', 'slab'), 0, 0)  19.2 us
    pallas_call x1, Pallas kernels, compute(): vmem_call(compute_kernel, (jax.ShapeDtypeStruct((rows, LANES), BF16), jax...  7.19 us
    all_to_all x1, waiting for transfers between devices, per_device(): lax.all_to_all(terms.reshape(devices, rows // devices, LANES), EVERY, 0, 0)  7.19 us
    all_to_all x1, starting transfers between devices, per_device(): lax.all_to_all(half.reshape(copies, -1, LANES), ('dp', 'slab'), 0, 0)  6.85 us
    ppermute x2, starting transfers between devices, halos(): return (lax.ppermute(value, SPACE, up), lax.ppermute(value, SPACE, down))  6.46 us
    all_to_all x1, starting transfers between devices, per_device(): lax.all_to_all(terms.reshape(devices, rows // devices, LANES), EVERY, 0, 0)  5.84 us
    pallas_call x2, Pallas kernels, half_call(): pl.pallas_call(body, grid_spec=pltpu.PrefetchScalarGridSpec(num_scalar_pr...  4.07 us
    ppermute x1, starting transfers between devices, per_device(): from_below = lax.ppermute(up, SPACE, upward)  3.71 us
  transfers between devices with their start and end apart: 8, of which 3 were waited for; matrix products, arithmetic and copies ran while one was open for 0% of the time, Pallas kernels for 19%

profile of v2, /device:TPU:1, one launch (start us, length us, event | category | flops | bytes accessed | tf_op | source)
XLA Modules:
  0.0 75.4 jit_solution(5063708000485835037)
XLA Ops:
  0.6 0.0 copy-start
  0.6 1.0 %copy-done = bf16[1,1,32,64,128]{4,3,2,1,0:T(8,128)(2,1)S(1)} copy-done((bf16[1,1,32,64,128]{4,3,2,1,0:T(8,128)(2,1)S(1)}, bf16[1,1,32,64,128]{4,3,2,1,0:T(8,128)(2,1)}, u32[]{:S(2)}) %copy-start) | copy-done | bytes 524312
  1.7 0.0 copy-start.2
  1.7 0.9 %copy-done.2 = bf16[1,1,16,64,128]{4,3,2,1,0:T(8,128)(2,1)S(1)} copy-done((bf16[1,1,16,64,128]{4,3,2,1,0:T(8,128)(2,1)S(1)}, bf16[1,1,16,64,128]{4,3,2,1,0:T(8,128)(2,1)}, u32[]{:S(2)}) %copy-start.2) | copy-done | bytes 262168
  2.6 0.0 copy-start.1
  2.6 0.0 copy-start.3
  2.6 0.0 copy-start.4
  2.6 1.3 %shard_map.93.pack_0 = bf16[3168,128]{1,0:T(8,128)(2,1)S(1)} custom-call(bf16[32,64,128]{2,1,0:T(8,128)(2,1)S(1)} %bitcast.11, bf16[16,64,128]{2,1,0:T(8,128)(2,1)S(1)} %bitcast.13), custom_call_target="tpu_custom_call" | custom-call | bytes 1048576 | tf_op jit(solution)/shard_map/pallas_call | solution.py:64
  3.9 2.0 %collective-permute-start.1 = (bf16[3168,128]{1,0:T(8,128)(2,1)S(1)}, bf16[3168,128]{1,0:T(8,128)(2,1)}, u32[]{:S(2)}, u32[]{:S(2)}) collective-permute-start(bf16[3168,128]{1,0:T(8,128)(2,1)S(1)} %shard_map.93.pack_0), channel_id=1, source_target_pairs={{1,0},{2,1},{3,2},{5,4},{6,5},{7,6},{9,8},{10,9},{11,10},{13,12},{... | collective-permute-start | bytes 2433032 | tf_op jit(solution)/shard_map/ppermute | solution.py:368
  5.9 4.5 %collective-permute-start = (bf16[3168,128]{1,0:T(8,128)(2,1)S(1)}, bf16[3168,128]{1,0:T(8,128)(2,1)}, u32[]{:S(2)}, u32[]{:S(2)}) collective-permute-start(bf16[3168,128]{1,0:T(8,128)(2,1)S(1)} %shard_map.93.pack_0), channel_id=1, source_target_pairs={{0,1},{1,2},{2,3},{4,5},{5,6},{6,7},{8,9},{9,10},{10,11},{12,13},{... | collective-permute-start | bytes 2433032 | tf_op jit(solution)/shard_map/ppermute | solution.py:368
  10.4 2.0 %shard_map.95 = bf16[2048,128]{1,0:T(8,128)(2,1)} custom-call(s32[1]{0:T(128)} %bitcast.3.core.refs_0_, f32[4096,128]{1,0:T(8,128)} %bitcast.14), custom_call_target="tpu_custom_call" | custom-call | bytes 1572864 | tf_op jit(solution)/shard_map/pallas_call | solution.py:127
  12.4 0.0 collective-permute-start.2
  12.4 0.0 copy-done.1
  12.4 0.0 copy-done.3
  12.4 0.0 copy-done.4
  12.4 2.4 %shard_map.94 = (bf16[6144,128]{1,0:T(8,128)(2,1)S(1)}, bf16[96,288]{1,0:T(8,128)(2,1)S(1)}, bf16[48,288]{1,0:T(8,128)(2,1)S(1)}) custom-call(bf16[32,64,128]{2,1,0:T(8,128)(2,1)S(1)} %bitcast.12, bf16[3,3,3,32,32]{4,3,2,1,0:T(8,128)(2,1)S(1)} %copy-done.3, bf16[3,3,3,16,32]{4,3,2,1,0:T(8,128)(2,1)S(1)} %copy-done.4), custom_call_target="tpu_custom_call" | custom-call | bytes 2097152 | tf_op jit(solution)/shard_map/pallas_call | solution.py:104
  14.8 0.0 collective-permute-done.2.other
  14.8 2.1 %shard_map.96 = bf16[2048,128]{1,0:T(8,128)(2,1)} custom-call(s32[1]{0:T(128)} %bitcast.3.core.refs_0_, f32[4096,128]{1,0:T(8,128)} %bitcast.15, bf16[2048,128]{1,0:T(8,128)(2,1)} %collective-permute-done.2.other), custom_call_target="tpu_custom_call" | custom-call | bytes 2097152 | tf_op jit(solution)/shard_map/pallas_call | solution.py:127
  16.9 6.8 %all-to-all-start = ((bf16[16,128,128]{2,1,0:T(8,128)(2,1)}), bf16[16,128,128]{2,1,0:T(8,128)(2,1)S(1)}, u32[]{:S(2)}, u32[]{:S(2)}) async-start(bf16[16,128,128]{2,1,0:T(8,128)(2,1)} %bitcast.16), calls=%async_computation | async-start | bytes 1048576 | tf_op jit(solution)/shard_map/all_to_all | solution.py:381
  23.8 0.0 collective-permute-done.1.pack_p
  23.8 0.0 collective-permute-done.pack_m
  23.8 7.2 %shard_map.97 = (bf16[512,128]{1,0:T(8,128)(2,1)}, f32[1024,128]{1,0:T(8,128)S(1)}, bf16[1024,128]{1,0:T(8,128)(2,1)}, bf16[1024,128]{1,0:T(8,128)(2,1)}) custom-call(bf16[3168,128]{1,0:T(8,128)(2,1)} %collective-permute-done.pack_m, bf16[3168,128]{1,0:T(8,128)(2,1)S(1)} %shard_map.93.pack_0, bf16[3168,128]{1,0:T(8,128)(2,1)} %collective-permute-done.1.pack_p, ...), custom_call_target="tpu_custom_call" | custom-call | flops 10000000000 | bytes 41943040 | tf_op jit(solution)/shard_map/pallas_call | solution.py:248
  31.0 3.7 %collective-permute-start.3 = (bf16[1024,128]{1,0:T(8,128)(2,1)}, bf16[1024,128]{1,0:T(8,128)(2,1)S(1)}, u32[]{:S(2)}, u32[]{:S(2)}) collective-permute-start(bf16[1024,128]{1,0:T(8,128)(2,1)} %get-tuple-element.25), channel_id=1, source_target_pairs={{0,1},{1,2},{2,3},{4,5},{5,6},{6,7},{8,9},{9,10},{10,11},{12,13},{... | collective-permute-start | bytes 786440 | tf_op jit(solution)/shard_map/ppermute | solution.py:390
  34.7 1.9 %collective-permute-start.4 = (bf16[1024,128]{1,0:T(8,128)(2,1)}, bf16[1024,128]{1,0:T(8,128)(2,1)S(1)}, u32[]{:S(2)}, u32[]{:S(2)}) collective-permute-start(bf16[1024,128]{1,0:T(8,128)(2,1)} %get-tuple-element.26), channel_id=1, source_target_pairs={{1,0},{2,1},{3,2},{5,4},{6,5},{7,6},{9,8},{10,9},{11,10},{13,12},{... | collective-permute-start | bytes 786440 | tf_op jit(solution)/shard_map/ppermute | solution.py:391
  36.6 0.1 all-to-all-done.refs_0_
  36.7 5.8 %all-to-all-start.1 = ((bf16[32,16,128]{2,1,0:T(8,128)(2,1)}), bf16[32,16,128]{2,1,0:T(8,128)(2,1)S(1)}, u32[]{:S(2)}, u32[]{:S(2)}) async-start(bf16[32,16,128]{2,1,0:T(8,128)(2,1)} %bitcast.6), calls=%async_computation.1 | async-start | bytes 262144 | tf_op jit(solution)/shard_map/all_to_all | solution.py:387
  42.6 0.0 collective-permute-done.3.from_below
  42.6 0.0 collective-permute-done.4.from_above
  42.6 1.0 %shard_map.98 = bf16[16,64,128]{2,1,0:T(8,128)(2,1)} custom-call(f32[1024,128]{1,0:T(8,128)S(1)} %get-tuple-element.24.own, bf16[1024,128]{1,0:T(8,128)(2,1)S(1)} %collective-permute-done.3.from_below, bf16[1024,128]{1,0:T(8,128)(2,1)S(1)} %collective-permute-done.4.from_above), custom_call_target="tpu_custom_call" | custom-call | flops 262144 | bytes 1048576 | tf_op jit(solution)/shard_map/pallas_call | solution.py:283
  43.6 7.2 %all-to-all-done.1.refs_1_ = bf16[32,16,128]{2,1,0:T(8,128)(2,1)S(1)} async-done(((bf16[32,16,128]{2,1,0:T(8,128)(2,1)}), bf16[32,16,128]{2,1,0:T(8,128)(2,1)S(1)}, u32[]{:S(2)}, u32[]{:S(2)}) %all-to-all-start.1) | async-done | bytes 131104 | tf_op jit(solution)/shard_map/all_to_all | solution.py:387
  50.8 0.2 shard_map.99
  51.0 19.2 %all_to_all.15.refs_1_ = bf16[16,144,128]{2,1,0:T(8,128)(2,1)S(1)} all-to-all(bf16[16,144,128]{2,1,0:T(8,128)(2,1)S(1)} %shard_map.99), channel_id=1, replica_groups=mesh['dp'=8,'slab'=2,'core'=2] {'dp','slab'}, dimensions={0} | all-to-all | bytes 1179648 | tf_op jit(solution)/shard_map/all_to_all | solution.py:397
  70.2 1.8 %collective-permute-start.5 = (bf16[16,144,128]{2,1,0:T(8,128)(2,1)S(1)}, bf16[16,144,128]{2,1,0:T(8,128)(2,1)S(1)}, u32[]{:S(2)}, u32[]{:S(2)}) collective-permute-start(bf16[16,144,128]{2,1,0:T(8,128)(2,1)S(1)} %all_to_all.15.refs_1_), channel_id=1, source_target_pairs={{0,1},{1,0},{2,3},{3,2},{4,5},{5,4},{6,7},{7,6},{8,9},{9,8},{10,11... | collective-permute-start | bytes 1769480 | tf_op jit(solution)/shard_map/ppermute | solution.py:398
  72.0 1.6 %collective-permute-done.5.refs_2_ = bf16[16,144,128]{2,1,0:T(8,128)(2,1)S(1)} collective-permute-done((bf16[16,144,128]{2,1,0:T(8,128)(2,1)S(1)}, bf16[16,144,128]{2,1,0:T(8,128)(2,1)S(1)}, u32[]{:S(2)}, u32[]{:S(2)}) %collective-permute-start.5) | collective-permute-done | bytes 589856 | tf_op jit(solution)/shard_map/ppermute | solution.py:398
  73.6 1.8 %shard_map.100 = (f32[4096,128]{1,0:T(8,128)}, f32[432,32]{1,0:T(8,128)}, f32[864,32]{1,0:T(8,128)}) custom-call(s32[1]{0:T(128)} %bitcast.3.core.refs_0_, bf16[16,144,128]{2,1,0:T(8,128)(2,1)S(1)} %all_to_all.15.refs_1_, bf16[16,144,128]{2,1,0:T(8,128)(2,1)S(1)} %collective-permute-done.5.refs_2_), custom_call_target="tpu_custom_call" | custom-call | tf_op jit(solution)/shard_map/pallas_call | solution.py:350
Async XLA Ops:
  0.6 1.0 %copy-start = (bf16[1,1,32,64,128]{4,3,2,1,0:T(8,128)(2,1)S(1)}, bf16[1,1,32,64,128]{4,3,2,1,0:T(8,128)(2,1)}, u32[]{:S(2)}) copy-start(bf16[1,1,32,64,128]{4,3,2,1,0:T(8,128)(2,1)} %param.8) | copy-start | bytes 1572868
  1.7 0.9 %copy-start.2 = (bf16[1,1,16,64,128]{4,3,2,1,0:T(8,128)(2,1)S(1)}, bf16[1,1,16,64,128]{4,3,2,1,0:T(8,128)(2,1)}, u32[]{:S(2)}) copy-start(bf16[1,1,16,64,128]{4,3,2,1,0:T(8,128)(2,1)} %param.6) | copy-start | bytes 786436
  2.6 9.7 %copy-start.1 = (bf16[1,1,32,64,128]{4,3,2,1,0:T(8,128)(2,1)S(1)}, bf16[1,1,32,64,128]{4,3,2,1,0:T(8,128)(2,1)}, u32[]{:S(2)}) copy-start(bf16[1,1,32,64,128]{4,3,2,1,0:T(8,128)(2,1)} %param.7) | copy-start | bytes 1572868
  2.6 9.7 %copy-start.3 = (bf16[3,3,3,32,32]{4,3,2,1,0:T(8,128)(2,1)S(1)}, bf16[3,3,3,32,32]{4,3,2,1,0:T(8,128)(2,1)}, u32[]{:S(2)}) copy-start(bf16[3,3,3,32,32]{4,3,2,1,0:T(8,128)(2,1)} %two.1) | copy-start | bytes 165892
  2.6 9.7 %copy-start.4 = (bf16[3,3,3,16,32]{4,3,2,1,0:T(8,128)(2,1)S(1)}, bf16[3,3,3,16,32]{4,3,2,1,0:T(8,128)(2,1)}, u32[]{:S(2)}) copy-start(bf16[3,3,3,16,32]{4,3,2,1,0:T(8,128)(2,1)} %one.1) | copy-start | bytes 82948
  3.9 19.8 %collective-permute-start.1 = (bf16[3168,128]{1,0:T(8,128)(2,1)S(1)}, bf16[3168,128]{1,0:T(8,128)(2,1)}, u32[]{:S(2)}, u32[]{:S(2)}) collective-permute-start(bf16[3168,128]{1,0:T(8,128)(2,1)S(1)} %shard_map.93.pack_0), channel_id=1, source_target_pairs={{1,0},{2,1},{3,2},{5,4},{6,5},{7,6},{9,8},{10,9},{11,10},{13,12},{... | collective-permute-start | bytes 2433032 | tf_op jit(solution)/shard_map/ppermute | solution.py:368
  5.9 17.9 %collective-permute-start = (bf16[3168,128]{1,0:T(8,128)(2,1)S(1)}, bf16[3168,128]{1,0:T(8,128)(2,1)}, u32[]{:S(2)}, u32[]{:S(2)}) collective-permute-start(bf16[3168,128]{1,0:T(8,128)(2,1)S(1)} %shard_map.93.pack_0), channel_id=1, source_target_pairs={{0,1},{1,2},{2,3},{4,5},{5,6},{6,7},{8,9},{9,10},{10,11},{12,13},{... | collective-permute-start | bytes 2433032 | tf_op jit(solution)/shard_map/ppermute | solution.py:368
  12.4 2.4 %collective-permute-start.2 = (bf16[2048,128]{1,0:T(8,128)(2,1)}, bf16[2048,128]{1,0:T(8,128)(2,1)}, u32[]{:S(2)}, u32[]{:S(2)}) collective-permute-start(bf16[2048,128]{1,0:T(8,128)(2,1)} %shard_map.95), channel_id=1, source_target_pairs={{0,1},{1,0},{2,3},{3,2},{4,5},{5,4},{6,7},{7,6},{8,9},{9,8},{10,11... | collective-permute-start | bytes 1572872 | tf_op jit(solution)/shard_map/ppermute | solution.py:148
  16.9 19.8 %all-to-all-start = ((bf16[16,128,128]{2,1,0:T(8,128)(2,1)}), bf16[16,128,128]{2,1,0:T(8,128)(2,1)S(1)}, u32[]{:S(2)}, u32[]{:S(2)}) async-start(bf16[16,128,128]{2,1,0:T(8,128)(2,1)} %bitcast.16), calls=%async_computation | async-start | bytes 1048576 | tf_op jit(solution)/shard_map/all_to_all | solution.py:381
  31.0 11.6 %collective-permute-start.3 = (bf16[1024,128]{1,0:T(8,128)(2,1)}, bf16[1024,128]{1,0:T(8,128)(2,1)S(1)}, u32[]{:S(2)}, u32[]{:S(2)}) collective-permute-start(bf16[1024,128]{1,0:T(8,128)(2,1)} %get-tuple-element.25), channel_id=1, source_target_pairs={{0,1},{1,2},{2,3},{4,5},{5,6},{6,7},{8,9},{9,10},{10,11},{12,13},{... | collective-permute-start | bytes 786440 | tf_op jit(solution)/shard_map/ppermute | solution.py:390
  34.7 7.9 %collective-permute-start.4 = (bf16[1024,128]{1,0:T(8,128)(2,1)}, bf16[1024,128]{1,0:T(8,128)(2,1)S(1)}, u32[]{:S(2)}, u32[]{:S(2)}) collective-permute-start(bf16[1024,128]{1,0:T(8,128)(2,1)} %get-tuple-element.26), channel_id=1, source_target_pairs={{1,0},{2,1},{3,2},{5,4},{6,5},{7,6},{9,8},{10,9},{11,10},{13,12},{... | collective-permute-start | bytes 786440 | tf_op jit(solution)/shard_map/ppermute | solution.py:391
  36.7 14.0 %all-to-all-start.1 = ((bf16[32,16,128]{2,1,0:T(8,128)(2,1)}), bf16[32,16,128]{2,1,0:T(8,128)(2,1)S(1)}, u32[]{:S(2)}, u32[]{:S(2)}) async-start(bf16[32,16,128]{2,1,0:T(8,128)(2,1)} %bitcast.6), calls=%async_computation.1 | async-start | bytes 262144 | tf_op jit(solution)/shard_map/all_to_all | solution.py:387
  70.2 3.4 %collective-permute-start.5 = (bf16[16,144,128]{2,1,0:T(8,128)(2,1)S(1)}, bf16[16,144,128]{2,1,0:T(8,128)(2,1)S(1)}, u32[]{:S(2)}, u32[]{:S(2)}) collective-permute-start(bf16[16,144,128]{2,1,0:T(8,128)(2,1)S(1)} %all_to_all.15.refs_1_), channel_id=1, source_target_pairs={{0,1},{1,0},{2,3},{3,2},{4,5},{5,4},{6,7},{7,6},{8,9},{9,8},{10,11... | collective-permute-start | bytes 1769480 | tf_op jit(solution)/shard_map/ppermute | solution.py:398

commit v3 on v2

--- a/solution.py
+++ b/solution.py
@@ -48,24 +48,41 @@
     lax.fori_loop(0, length, gather, 0, unroll=4)
 
 
-def pack_kernel(cot, vol, out, flat):
-    c2, length, width = cot.shape
-    pitch = c2 + vol.shape[0]
+def pack_kernel(cot, vol, out, fetched, flat, sems):
+    step = vol.shape[0]
+    length, width = vol.shape[1:]
+    pitch = cot.shape[0] + step
+    pieces = [cot.at[pl.ds(n, step)] for n in range(0, cot.shape[0], step)] + [vol]
+    copies = [
+        pltpu.make_async_copy(piece, fetched.at[n], sems.at[n]) for n, piece in enumerate(pieces)
+    ]
+    for copy in copies:
+        copy.start()
     zeros = jnp.zeros((pitch, width), BF16)
     out[0:pitch, :] = zeros
     out[(length + 1) * pitch : (length + 2) * pitch, :] = zeros
-    turned(cot, flat, out, 0, pitch, 1)
-    turned(vol, flat, out, c2, pitch, 1)
+    for n, copy in enumerate(copies):
+        copy.wait()
+        turned(fetched.at[n], flat, out, n * step, pitch, 1)
 
 
 def pack(cot, vol):
     c2, length, width = cot.shape
     pitch = c2 + vol.shape[0]
-    return vmem_call(
+    pieces = pitch // vol.shape[0]
+    source = pl.BlockSpec(memory_space=pltpu.HBM)
+    return pl.pallas_call(
         pack_kernel,
-        jax.ShapeDtypeStruct(((length + 2) * pitch, width), BF16),
-        (pltpu.VMEM((max(c2, vol.shape[0]) * length, width), F32),),
-        pl.CostEstimate(flops=0, bytes_accessed=4 * cot.size, transcendentals=0),
+        out_shape=jax.ShapeDtypeStruct(((length + 2) * pitch, width), BF16),
+        in_specs=[source, source],
+        out_specs=pl.BlockSpec(memory_space=pltpu.VMEM),
+        scratch_shapes=[
+            pltpu.VMEM((pieces,) + vol.shape, BF16),
+            pltpu.VMEM((vol.shape[0] * length, width), F32),
+            pltpu.SemaphoreType.DMA((pieces,)),
+        ],
+        compiler_params=pltpu.CompilerParams(vmem_limit_bytes=24 * 2**20),
+        cost_estimate=pl.CostEstimate(flops=0, bytes_accessed=4 * cot.size, transcendentals=0),
     )(cot, vol)
 
 
@@ -288,45 +305,36 @@
     )(own, from_below, from_above)
 
 
-def share_kernel(scale, bucket, terms, out):
-    total = jnp.sum(bucket[...].astype(F32), axis=0).astype(BF16)
-    grads = (jnp.sum(terms[...].astype(F32), axis=0) * scale).astype(BF16)
-    height = total.shape[0]
+def share_kernel(scale, parts, out):
+    total = (jnp.sum(parts[...].astype(F32), axis=0) * scale).astype(BF16)
 
     def write(n, carry):
-        out[n, 0:height, :] = total
-        out[n, height : height + grads.shape[0], :] = grads
+        out[n] = total
         return carry
 
     lax.fori_loop(0, out.shape[0], write, 0)
 
 
-def share(bucket, terms, scale, copies):
-    rows = bucket.shape[1] + terms.shape[1]
+def share(parts, scale):
     return vmem_call(
         lambda *refs: share_kernel(scale, *refs),
-        jax.ShapeDtypeStruct((copies, rows, LANES), BF16),
+        jax.ShapeDtypeStruct(parts.shape, BF16),
         (),
-        pl.CostEstimate(flops=bucket.size, bytes_accessed=3 * bucket.size, transcendentals=0),
-    )(bucket, terms)
-
-
-def finish_kernel(sizes, core, mine, other, bucket, out_one, out_two, raw):
+        pl.CostEstimate(flops=parts.size, bytes_accessed=4 * parts.size, transcendentals=0),
+    )(parts)
+
+
+def gathered(parts, axes, scale=1.0):
+    return lax.all_to_all(share(parts, scale), axes, 0, 0)
+
+
+def finish_kernel(sizes, core, mine, other, raw_parts, bucket, out_one, out_two, raw):
     c0, c1, c2 = sizes
-    copies, rows, _ = mine.shape
-    height = bucket.shape[0] // (2 * copies)
-    extra = rows - height
+    half = mine.shape[0]
     me = core[0]
-
-    def place(q, carry):
-        for source, which in ((mine, me), (other, 1 - me)):
-            at = pl.multiple_of((which * copies + q) * height, 8)
-            bucket[pl.ds(at, height), :] = source[q, 0:height, :].astype(F32)
-            at = pl.multiple_of((2 * q + which) * extra, 8)
-            raw[pl.ds(at, extra), :] = source[q, height:rows, :].astype(F32)
-        return carry
-
-    lax.fori_loop(0, copies, place, 0)
+    bucket[pl.ds(pl.multiple_of(me * half, 8), half), :] = mine[...].astype(F32)
+    bucket[pl.ds(pl.multiple_of((1 - me) * half, 8), half), :] = other[...].astype(F32)
+    raw[...] = raw_parts[...].astype(F32)
     block = 3 * c1
     first = -(-9 * c2 // LANES) * block
     for i in range(3):
@@ -342,23 +350,21 @@
                 out_one[to : to + c0, :] = raw[row : row + c0, k * c1 : (k + 1) * c1]
 
 
-def finish(core, mine, other, length, sizes):
+def finish(core, mine, other, raw, sizes):
     c0, c1, c2 = sizes
-    copies, rows, _ = mine.shape
-    extra = rows - length // LANES // (2 * copies)
     spec = pl.BlockSpec(memory_space=pltpu.VMEM)
     return pl.pallas_call(
         lambda *refs: finish_kernel(sizes, *refs),
         out_shape=(
-            jax.ShapeDtypeStruct((length // LANES, LANES), F32),
+            jax.ShapeDtypeStruct((2 * mine.shape[0], LANES), F32),
             jax.ShapeDtypeStruct((27 * c0, c1), F32),
             jax.ShapeDtypeStruct((27 * c1, c2), F32),
         ),
-        in_specs=[pl.BlockSpec(memory_space=pltpu.SMEM), spec, spec],
+        in_specs=[pl.BlockSpec(memory_space=pltpu.SMEM), spec, spec, spec],
         out_specs=(spec, spec, spec),
-        scratch_shapes=[pltpu.VMEM((2 * copies * extra, LANES), F32)],
+        scratch_shapes=[pltpu.VMEM(raw.shape, F32)],
         compiler_params=pltpu.CompilerParams(vmem_limit_bytes=24 * 2**20),
-    )(core, mine, other)
+    )(core, mine, other, raw)
 
 
 def halos(value):
@@ -376,27 +382,27 @@
     packed = pack(out_cot[0, 0], volume_in[0, 0])
     below, above = halos(packed)
     half = swapped_half(core, grad_bucket.reshape(length // LANES, LANES))
-    acts, w_two, w_one = slide(hidden_act[0, 0], kernel_two, kernel_one)
-    acts, half = lax.optimization_barrier((acts, half))
+    act, half = lax.optimization_barrier((hidden_act[0, 0], half))
     parts = lax.all_to_all(half.reshape(copies, -1, LANES), ("dp", "slab"), 0, 0)
+    mine = gathered(parts, ("dp", "slab")).reshape(-1, LANES)
 
     used = -(-9 * c2 // LANES) * 3 * c1 + 9 * c0
     rows = ceil_to(used, 16 * devices)
+    acts, w_two, w_one = slide(act, kernel_two, kernel_one)
     terms, own, up, down = compute((below, packed, above), acts, w_two, w_one, rows)
-    terms, parts = lax.optimization_barrier((terms, parts))
     terms = lax.all_to_all(terms.reshape(devices, rows // devices, LANES), EVERY, 0, 0)
+    cells = volume_in.shape[3] * volume_in.shape[4] * devices
+    raw = gathered(terms, EVERY, 1.0 / math.sqrt(cells)).reshape(-1, LANES)
+
     count = lax.axis_size(SPACE)
     upward = [(i, i + 1) for i in range(count - 1)]
     from_below = lax.ppermute(up, SPACE, upward)
     from_above = lax.ppermute(down, SPACE, [(j, i) for i, j in upward])
     grad_input = merge(own, from_below, from_above, volume_in.shape[2:])
 
-    cells = volume_in.shape[3] * volume_in.shape[4] * devices
-    shares = share(parts, terms, 1.0 / math.sqrt(cells), copies)
-    grad_input, shares = lax.optimization_barrier((grad_input, shares))
-    mine = lax.all_to_all(shares, ("dp", "slab"), 0, 0)
+    mine, grad_input = lax.optimization_barrier((mine, grad_input))
     other = lax.ppermute(mine, "core", [(0, 1), (1, 0)])
-    bucket_sum, total_one, total_two = finish(core, mine, other, length, (c0, c1, c2))
+    bucket_sum, total_one, total_two = finish(core, mine, other, raw, (c0, c1, c2))
     return (
         grad_input[None, None],
         total_one.reshape(3, 3, 3, c0, c1),

time: 76.2 us -> 80.6 us (1.058)
  blocking collectives: 19.2 us -> 22.8 us
    all_to_all x1, waiting for transfers between devices: 7.19 us -> 0.01 us  [gathered(): return lax.all_to_all(share(parts, scale), axes, 0, 0)]
    ppermute x1, waiting for transfers between devices: 0.01 us -> 3.72 us  [per_device(): from_above = lax.ppermute(down, SPACE, [(j, i) for i, j in upward])]
    all_to_all x1 -> x2, blocking collectives: 19.2 us -> 22.8 us  [the longest x1 12.8 us: per_device(): lax.all_to_all(terms.reshape(devices, rows // devices, LANES), EVERY, 0, 0)]
    ppermute x1, waiting for transfers between devices: 0.01 us -> 2.06 us  [swapped_half(): other = lax.ppermute(send, 'core', [(0, 1), (1, 0)])]
    ppermute x1, waiting for transfers between devices: 0.01 us -> 2.04 us  [per_device(): from_below = lax.ppermute(up, SPACE, upward)]
    ppermute x1, starting transfers between devices: 1.78 us -> 0.01 us  [per_device(): other = lax.ppermute(mine, 'core', [(0, 1), (1, 0)])]
    ppermute x1, waiting for transfers between devices: 1.63 us -> 0.01 us  [per_device(): other = lax.ppermute(mine, 'core', [(0, 1), (1, 0)])]
    ppermute x1, starting transfers between devices: 3.71 us -> 5.16 us  [per_device(): from_below = lax.ppermute(up, SPACE, upward)]
  transfers between devices with their start and end apart: 8 -> 8, of which waited for: 3 -> 4; matrix products, arithmetic and copies ran while one was open for 0% -> 0% of each run, Pallas kernels for 19% -> 16%
where the time goes in v3:
time: 80.6 us; the launch traced here: 79.9 us
  starting transfers between devices  26.7 us (33%)
  blocking collectives  22.8 us (28%)
  Pallas kernels  18.3 us (23%)
  waiting for transfers between devices  9.33 us (12%)
  local copies, waits for them, and re-layouts  1.95 us (2%)
    all_to_all x1, blocking collectives, per_device(): lax.all_to_all(terms.reshape(devices, rows // devices, LANES), EVERY, 0, 0)  12.8 us
    all_to_all x1, blocking collectives, gathered(): return lax.all_to_all(share(parts, scale), axes, 0, 0)  10 us
    all_to_all x1, starting transfers between devices, per_device(): lax.all_to_all(half.reshape(copies, -1, LANES), ('dp', 'slab'), 0, 0)  7.86 us
    pallas_call x1, Pallas kernels, compute(): vmem_call(compute_kernel, (jax.ShapeDtypeStruct((rows, LANES), BF16), jax...  6.56 us
    ppermute x2, starting transfers between devices, halos(): return (lax.ppermute(value, SPACE, up), lax.ppermute(value, SPACE, down))  6.01 us
    all_to_all x1, starting transfers between devices, gathered(): return lax.all_to_all(share(parts, scale), axes, 0, 0)  5.69 us
    ppermute x1, starting transfers between devices, per_device(): from_below = lax.ppermute(up, SPACE, upward)  5.16 us
    pallas_call x2, Pallas kernels, half_call(): pl.pallas_call(body, grid_spec=pltpu.PrefetchScalarGridSpec(num_scalar_pr...  4.05 us
  transfers between devices with their start and end apart: 8, of which 4 were waited for; matrix products, arithmetic and copies ran while one was open for 0% of the time, Pallas kernels for 16%

profile of v3, /device:TPU:1, one launch (start us, length us, event | category | flops | bytes accessed | tf_op | source)
XLA Modules:
  0.0 79.9 jit_solution(5362812497306562420)
XLA Ops:
  0.6 1.9 %shard_map.93 = bf16[2048,128]{1,0:T(8,128)(2,1)} custom-call(s32[1]{0:T(128)} %bitcast.1.core.refs_0_, f32[4096,128]{1,0:T(8,128)} %bitcast.20), custom_call_target="tpu_custom_call" | custom-call | bytes 1572864 | tf_op jit(solution)/shard_map/pallas_call | solution.py:144
  2.6 0.0 copy-start
  2.6 0.0 copy-start.2
  2.6 0.1 collective-permute-start
  2.6 2.1 %collective-permute-done.other = bf16[2048,128]{1,0:T(8,128)(2,1)S(1)} collective-permute-done((bf16[2048,128]{1,0:T(8,128)(2,1)}, bf16[2048,128]{1,0:T(8,128)(2,1)S(1)}, u32[]{:S(2)}, u32[]{:S(2)}) %collective-permute-start) | collective-permute-done | bytes 524320 | tf_op jit(solution)/shard_map/ppermute | solution.py:165
  4.7 0.0 copy-start.7
  4.7 0.8 copy-done.7
  5.5 2.1 %shard_map.94 = bf16[2048,128]{1,0:T(8,128)(2,1)} custom-call(s32[1]{0:T(128)} %bitcast.1.core.refs_0_, f32[4096,128]{1,0:T(8,128)} %bitcast.21, bf16[2048,128]{1,0:T(8,128)(2,1)} %copy-done.7), custom_call_target="tpu_custom_call" | custom-call | bytes 2097152 | tf_op jit(solution)/shard_map/pallas_call | solution.py:144
  7.6 0.0 copy-start.1
  7.6 0.0 copy-start.3
  7.6 0.0 copy-start.4
  7.6 7.9 %all-to-all-start = ((bf16[16,128,128]{2,1,0:T(8,128)(2,1)}), bf16[16,128,128]{2,1,0:T(8,128)(2,1)S(1)}, u32[]{:S(2)}, u32[]{:S(2)}) async-start(bf16[16,128,128]{2,1,0:T(8,128)(2,1)} %bitcast.22), calls=%async_computation | async-start | bytes 1048576 | tf_op jit(solution)/shard_map/all_to_all | solution.py:386
  15.5 0.0 copy-done
  15.5 0.0 copy-done.2
  15.5 1.5 %shard_map.96.pack_0 = bf16[3168,128]{1,0:T(8,128)(2,1)S(1)} custom-call(bf16[32,64,128]{2,1,0:T(8,128)(2,1)S(1)} %bitcast.15, bf16[16,64,128]{2,1,0:T(8,128)(2,1)S(1)} %bitcast.18), custom_call_target="tpu_custom_call" | custom-call | bytes 1048576 | tf_op jit(solution)/shard_map/pallas_call | solution.py:74
  17.0 2.6 %collective-permute-start.2 = (bf16[3168,128]{1,0:T(8,128)(2,1)S(1)}, bf16[3168,128]{1,0:T(8,128)(2,1)}, u32[]{:S(2)}, u32[]{:S(2)}) collective-permute-start(bf16[3168,128]{1,0:T(8,128)(2,1)S(1)} %shard_map.96.pack_0), channel_id=1, source_target_pairs={{1,0},{2,1},{3,2},{5,4},{6,5},{7,6},{9,8},{10,9},{11,10},{13,12},{... | collective-permute-start | bytes 2433032 | tf_op jit(solution)/shard_map/ppermute | solution.py:374
  19.6 3.4 %collective-permute-start.1 = (bf16[3168,128]{1,0:T(8,128)(2,1)S(1)}, bf16[3168,128]{1,0:T(8,128)(2,1)}, u32[]{:S(2)}, u32[]{:S(2)}) collective-permute-start(bf16[3168,128]{1,0:T(8,128)(2,1)S(1)} %shard_map.96.pack_0), channel_id=1, source_target_pairs={{0,1},{1,2},{2,3},{4,5},{5,6},{6,7},{8,9},{9,10},{10,11},{12,13},{... | collective-permute-start | bytes 2433032 | tf_op jit(solution)/shard_map/ppermute | solution.py:374
  23.0 0.0 copy-done.1
  23.1 0.0 copy-done.3
  23.1 0.0 copy-done.4
  23.1 2.4 %shard_map.97 = (bf16[6144,128]{1,0:T(8,128)(2,1)S(1)}, bf16[96,288]{1,0:T(8,128)(2,1)S(1)}, bf16[48,288]{1,0:T(8,128)(2,1)S(1)}) custom-call(bf16[32,64,128]{2,1,0:T(8,128)(2,1)S(1)} %bitcast.17, bf16[3,3,3,32,32]{4,3,2,1,0:T(8,128)(2,1)S(1)} %copy-done.3, bf16[3,3,3,16,32]{4,3,2,1,0:T(8,128)(2,1)S(1)} %copy-done.4), custom_call_target="tpu_custom_call" | custom-call | bytes 2097152 | tf_op jit(solution)/shard_map/pallas_call | solution.py:121
  25.5 0.0 copy-start.5
  25.5 1.1 %copy-done.5 = bf16[6144,128]{1,0:T(8,128)(2,1)} copy-done((bf16[6144,128]{1,0:T(8,128)(2,1)}, bf16[6144,128]{1,0:T(8,128)(2,1)S(1)}, u32[]{:S(2)}) %copy-start.5) | copy-done | bytes 1572888
  26.6 1.5 %all-to-all-done.refs_0_ = bf16[16,128,128]{2,1,0:T(8,128)(2,1)S(1)} async-done(((bf16[16,128,128]{2,1,0:T(8,128)(2,1)}), bf16[16,128,128]{2,1,0:T(8,128)(2,1)S(1)}, u32[]{:S(2)}, u32[]{:S(2)}) %all-to-all-start) | async-done | bytes 524320 | tf_op jit(solution)/shard_map/all_to_all | solution.py:386
  28.1 0.0 copy-start.6
  28.1 1.0 %shard_map.95 = bf16[16,128,128]{2,1,0:T(8,128)(2,1)} custom-call(bf16[16,128,128]{2,1,0:T(8,128)(2,1)S(1)} %all-to-all-done.refs_0_), custom_call_target="tpu_custom_call" | custom-call | flops 262144 | bytes 1048576 | tf_op jit(solution)/shard_map/pallas_call | solution.py:319
  29.1 5.7 %all-to-all-start.1 = ((bf16[16,128,128]{2,1,0:T(8,128)(2,1)}), bf16[16,128,128]{2,1,0:T(8,128)(2,1)S(1)}, u32[]{:S(2)}, u32[]{:S(2)}) async-start(bf16[16,128,128]{2,1,0:T(8,128)(2,1)} %shard_map.95), calls=%async_computation.1 | async-start | bytes 1048576 | tf_op jit(solution)/shard_map/all_to_all | solution.py:328
  34.8 0.0 collective-permute-done.2.pack_p
  34.8 0.0 collective-permute-done.1.pack_m
  34.8 0.0 copy-done.6
  34.8 6.6 %shard_map.98 = (bf16[512,128]{1,0:T(8,128)(2,1)S(1)}, f32[1024,128]{1,0:T(8,128)S(1)}, bf16[1024,128]{1,0:T(8,128)(2,1)S(1)}, bf16[1024,128]{1,0:T(8,128)(2,1)S(1)}) custom-call(bf16[3168,128]{1,0:T(8,128)(2,1)} %collective-permute-done.1.pack_m, bf16[3168,128]{1,0:T(8,128)(2,1)S(1)} %shard_map.96.pack_0, bf16[3168,128]{1,0:T(8,128)(2,1)} %collective-permute-done.2.pack_p, ...), custom_call_target="tpu_custom_call" | custom-call | flops 10000000000 | bytes 41943040 | tf_op jit(solution)/shard_map/pallas_call | solution.py:265
  41.4 5.2 %collective-permute-start.3 = (bf16[1024,128]{1,0:T(8,128)(2,1)S(1)}, bf16[1024,128]{1,0:T(8,128)(2,1)S(1)}, u32[]{:S(2)}, u32[]{:S(2)}) collective-permute-start(bf16[1024,128]{1,0:T(8,128)(2,1)S(1)} %get-tuple-element.24), channel_id=1, source_target_pairs={{0,1},{1,2},{2,3},{4,5},{5,6},{6,7},{8,9},{9,10},{10,11},{12,13},{... | collective-permute-start | bytes 786440 | tf_op jit(solution)/shard_map/ppermute | solution.py:399
  46.5 1.9 %collective-permute-start.4 = (bf16[1024,128]{1,0:T(8,128)(2,1)S(1)}, bf16[1024,128]{1,0:T(8,128)(2,1)S(1)}, u32[]{:S(2)}, u32[]{:S(2)}) collective-permute-start(bf16[1024,128]{1,0:T(8,128)(2,1)S(1)} %get-tuple-element.25), channel_id=1, source_target_pairs={{1,0},{2,1},{3,2},{5,4},{6,5},{7,6},{9,8},{10,9},{11,10},{13,12},{... | collective-permute-start | bytes 786440 | tf_op jit(solution)/shard_map/ppermute | solution.py:400
  48.5 2.0 %collective-permute-done.3.from_below = bf16[1024,128]{1,0:T(8,128)(2,1)S(1)} collective-permute-done((bf16[1024,128]{1,0:T(8,128)(2,1)S(1)}, bf16[1024,128]{1,0:T(8,128)(2,1)S(1)}, u32[]{:S(2)}, u32[]{:S(2)}) %collective-permute-start.3) | collective-permute-done | bytes 262176 | tf_op jit(solution)/shard_map/ppermute | solution.py:399
  50.5 3.7 %collective-permute-done.4.from_above = bf16[1024,128]{1,0:T(8,128)(2,1)S(1)} collective-permute-done((bf16[1024,128]{1,0:T(8,128)(2,1)S(1)}, bf16[1024,128]{1,0:T(8,128)(2,1)S(1)}, u32[]{:S(2)}, u32[]{:S(2)}) %collective-permute-start.4) | collective-permute-done | bytes 262176 | tf_op jit(solution)/shard_map/ppermute | solution.py:400
  54.2 1.0 %shard_map.99 = bf16[16,64,128]{2,1,0:T(8,128)(2,1)} custom-call(f32[1024,128]{1,0:T(8,128)S(1)} %get-tuple-element.23.own, bf16[1024,128]{1,0:T(8,128)(2,1)S(1)} %collective-permute-done.3.from_below, bf16[1024,128]{1,0:T(8,128)(2,1)S(1)} %collective-permute-done.4.from_above), custom_call_target="tpu_custom_call" | custom-call | flops 262144 | bytes 1048576 | tf_op jit(solution)/shard_map/pallas_call | solution.py:300
  55.2 0.0 all-to-all-done.1
  55.2 0.0 collective-permute-start.5
  55.2 12.8 %all_to_all.20.refs_0_ = bf16[32,16,128]{2,1,0:T(8,128)(2,1)S(1)} all-to-all(bf16[32,16,128]{2,1,0:T(8,128)(2,1)S(1)} %bitcast.19), channel_id=1, replica_groups=mesh['dp'=8,'slab'=2,'core'=2] {'dp','slab','core'}, dimensions={0} | all-to-all | bytes 262144 | tf_op jit(solution)/shard_map/all_to_all | solution.py:393
  68.0 0.2 shard_map.100
  68.2 10.0 %all_to_all.21 = bf16[32,16,128]{2,1,0:T(8,128)(2,1)S(1)} all-to-all(bf16[32,16,128]{2,1,0:T(8,128)(2,1)S(1)} %shard_map.100), channel_id=1, replica_groups=mesh['dp'=8,'slab'=2,'core'=2] {'dp','slab','core'}, dimensions={0} | all-to-all | bytes 262144 | tf_op jit(solution)/shard_map/all_to_all | solution.py:328
  78.2 0.0 collective-permute-done.5.refs_2_
  78.2 1.7 %shard_map.101 = (f32[4096,128]{1,0:T(8,128)}, f32[432,32]{1,0:T(8,128)}, f32[864,32]{1,0:T(8,128)}) custom-call(s32[1]{0:T(128)} %bitcast.1.core.refs_0_, bf16[2048,128]{1,0:T(8,128)(2,1)S(1)} %bitcast.14, bf16[2048,128]{1,0:T(8,128)(2,1)S(1)} %collective-permute-done.5.refs_2_, bf16[512,128]{1,0:T(8,128)(2,1)S(1)} %bitcast.16), custom_call_target="tpu_custom_call" | custom-call | tf_op jit(solution)/shard_map/pallas_call | solution.py:356
Async XLA Ops:
  2.6 12.9 %copy-start = (bf16[1,1,32,64,128]{4,3,2,1,0:T(8,128)(2,1)S(1)}, bf16[1,1,32,64,128]{4,3,2,1,0:T(8,128)(2,1)}, u32[]{:S(2)}) copy-start(bf16[1,1,32,64,128]{4,3,2,1,0:T(8,128)(2,1)} %param.8) | copy-start | bytes 1572868
  2.6 12.9 %copy-start.2 = (bf16[1,1,16,64,128]{4,3,2,1,0:T(8,128)(2,1)S(1)}, bf16[1,1,16,64,128]{4,3,2,1,0:T(8,128)(2,1)}, u32[]{:S(2)}) copy-start(bf16[1,1,16,64,128]{4,3,2,1,0:T(8,128)(2,1)} %param.6) | copy-start | bytes 786436
  2.6 2.1 %collective-permute-start = (bf16[2048,128]{1,0:T(8,128)(2,1)}, bf16[2048,128]{1,0:T(8,128)(2,1)S(1)}, u32[]{:S(2)}, u32[]{:S(2)}) collective-permute-start(bf16[2048,128]{1,0:T(8,128)(2,1)} %shard_map.93), channel_id=1, source_target_pairs={{0,1},{1,0},{2,3},{3,2},{4,5},{5,4},{6,7},{7,6},{8,9},{9,8},{10,11... | collective-permute-start | bytes 1572872 | tf_op jit(solution)/shard_map/ppermute | solution.py:165
  4.7 0.8 copy-start.7
  7.6 15.4 %copy-start.1 = (bf16[1,1,32,64,128]{4,3,2,1,0:T(8,128)(2,1)S(1)}, bf16[1,1,32,64,128]{4,3,2,1,0:T(8,128)(2,1)}, u32[]{:S(2)}) copy-start(bf16[1,1,32,64,128]{4,3,2,1,0:T(8,128)(2,1)} %param.7) | copy-start | bytes 1572868
  7.6 15.5 %copy-start.3 = (bf16[3,3,3,32,32]{4,3,2,1,0:T(8,128)(2,1)S(1)}, bf16[3,3,3,32,32]{4,3,2,1,0:T(8,128)(2,1)}, u32[]{:S(2)}) copy-start(bf16[3,3,3,32,32]{4,3,2,1,0:T(8,128)(2,1)} %two.1) | copy-start | bytes 165892
  7.6 15.5 %copy-start.4 = (bf16[3,3,3,16,32]{4,3,2,1,0:T(8,128)(2,1)S(1)}, bf16[3,3,3,16,32]{4,3,2,1,0:T(8,128)(2,1)}, u32[]{:S(2)}) copy-start(bf16[3,3,3,16,32]{4,3,2,1,0:T(8,128)(2,1)} %one.1) | copy-start | bytes 82948
  7.6 20.5 %all-to-all-start = ((bf16[16,128,128]{2,1,0:T(8,128)(2,1)}), bf16[16,128,128]{2,1,0:T(8,128)(2,1)S(1)}, u32[]{:S(2)}, u32[]{:S(2)}) async-start(bf16[16,128,128]{2,1,0:T(8,128)(2,1)} %bitcast.22), calls=%async_computation | async-start | bytes 1048576 | tf_op jit(solution)/shard_map/all_to_all | solution.py:386
  17.0 17.8 %collective-permute-start.2 = (bf16[3168,128]{1,0:T(8,128)(2,1)S(1)}, bf16[3168,128]{1,0:T(8,128)(2,1)}, u32[]{:S(2)}, u32[]{:S(2)}) collective-permute-start(bf16[3168,128]{1,0:T(8,128)(2,1)S(1)} %shard_map.96.pack_0), channel_id=1, source_target_pairs={{1,0},{2,1},{3,2},{5,4},{6,5},{7,6},{9,8},{10,9},{11,10},{13,12},{... | collective-permute-start | bytes 2433032 | tf_op jit(solution)/shard_map/ppermute | solution.py:374
  19.6 15.2 %collective-permute-start.1 = (bf16[3168,128]{1,0:T(8,128)(2,1)S(1)}, bf16[3168,128]{1,0:T(8,128)(2,1)}, u32[]{:S(2)}, u32[]{:S(2)}) collective-permute-start(bf16[3168,128]{1,0:T(8,128)(2,1)S(1)} %shard_map.96.pack_0), channel_id=1, source_target_pairs={{0,1},{1,2},{2,3},{4,5},{5,6},{6,7},{8,9},{9,10},{10,11},{12,13},{... | collective-permute-start | bytes 2433032 | tf_op jit(solution)/shard_map/ppermute | solution.py:374
  25.5 1.1 %copy-start.5 = (bf16[6144,128]{1,0:T(8,128)(2,1)}, bf16[6144,128]{1,0:T(8,128)(2,1)S(1)}, u32[]{:S(2)}) copy-start(bf16[6144,128]{1,0:T(8,128)(2,1)S(1)} %get-tuple-element.20.acts) | copy-start | bytes 4718596
  28.1 6.7 %copy-start.6 = (bf16[6144,128]{1,0:T(8,128)(2,1)S(1)}, bf16[6144,128]{1,0:T(8,128)(2,1)}, u32[]{:S(2)}) copy-start(bf16[6144,128]{1,0:T(8,128)(2,1)} %copy-done.5) | copy-start | bytes 4718596
  29.1 26.1 %all-to-all-start.1 = ((bf16[16,128,128]{2,1,0:T(8,128)(2,1)}), bf16[16,128,128]{2,1,0:T(8,128)(2,1)S(1)}, u32[]{:S(2)}, u32[]{:S(2)}) async-start(bf16[16,128,128]{2,1,0:T(8,128)(2,1)} %shard_map.95), calls=%async_computation.1 | async-start | bytes 1048576 | tf_op jit(solution)/shard_map/all_to_all | solution.py:328
  41.4 9.1 %collective-permute-start.3 = (bf16[1024,128]{1,0:T(8,128)(2,1)S(1)}, bf16[1024,128]{1,0:T(8,128)(2,1)S(1)}, u32[]{:S(2)}, u32[]{:S(2)}) collective-permute-start(bf16[1024,128]{1,0:T(8,128)(2,1)S(1)} %get-tuple-element.24), channel_id=1, source_target_pairs={{0,1},{1,2},{2,3},{4,5},{5,6},{6,7},{8,9},{9,10},{10,11},{12,13},{... | collective-permute-start | bytes 786440 | tf_op jit(solution)/shard_map/ppermute | solution.py:399
  46.5 7.7 %collective-permute-start.4 = (bf16[1024,128]{1,0:T(8,128)(2,1)S(1)}, bf16[1024,128]{1,0:T(8,128)(2,1)S(1)}, u32[]{:S(2)}, u32[]{:S(2)}) collective-permute-start(bf16[1024,128]{1,0:T(8,128)(2,1)S(1)} %get-tuple-element.25), channel_id=1, source_target_pairs={{1,0},{2,1},{3,2},{5,4},{6,5},{7,6},{9,8},{10,9},{11,10},{13,12},{... | collective-permute-start | bytes 786440 | tf_op jit(solution)/shard_map/ppermute | solution.py:400
  55.2 23.0 %collective-permute-start.5 = (bf16[2048,128]{1,0:T(8,128)(2,1)S(1)}, bf16[2048,128]{1,0:T(8,128)(2,1)S(1)}, u32[]{:S(2)}, u32[]{:S(2)}) collective-permute-start(bf16[2048,128]{1,0:T(8,128)(2,1)S(1)} %bitcast.13), channel_id=1, source_target_pairs={{0,1},{1,0},{2,3},{3,2},{4,5},{5,4},{6,7},{7,6},{8,9},{9,8},{10,11... | collective-permute-start | bytes 1572872 | tf_op jit(solution)/shard_map/ppermute | solution.py:404

commit v4 on v3

--- a/solution.py
+++ b/solution.py
@@ -81,24 +81,64 @@
             pltpu.VMEM((vol.shape[0] * length, width), F32),
             pltpu.SemaphoreType.DMA((pieces,)),
         ],
-        compiler_params=pltpu.CompilerParams(vmem_limit_bytes=24 * 2**20),
         cost_estimate=pl.CostEstimate(flops=0, bytes_accessed=4 * cot.size, transcendentals=0),
     )(cot, vol)
 
 
-def slide_kernel(act, two, one, out, w_two, w_one, flat, rows):
+def fetched_chunks(src, start, buffer, sems):
+    count = sems.shape[0]
+    step = buffer.shape[0] // count
+    copies = []
+    for n in range(count):
+        at = pl.ds(pl.multiple_of(start + n * step, 8), step)
+        copies.append(
+            pltpu.make_async_copy(src.at[at], buffer.at[pl.ds(n * step, step)], sems.at[n])
+        )
+        copies[-1].start()
+    return [(pl.ds(n * step, step), copy) for n, copy in enumerate(copies)]
+
+
+def cast_kernel(core, src, out, buffer, sems):
+    for rows, copy in fetched_chunks(src, (1 - core[0]) * out.shape[0], buffer, sems):
+        copy.wait()
+        out[rows, :] = buffer[rows, :].astype(out.dtype)
+
+
+def add_kernel(core, src, other, out, buffer, more, sems, more_sems):
+    chunks = fetched_chunks(src, core[0] * out.shape[0], buffer, sems)
+    for (rows, copy), (_, second) in zip(chunks, fetched_chunks(other, 0, more, more_sems)):
+        copy.wait()
+        second.wait()
+        out[rows, :] = (buffer[rows, :] + more[rows, :].astype(F32)).astype(out.dtype)
+
+
+def half_call(body, core, value, others, chunks=8):
+    half = (value.shape[0] // 2, LANES)
+    source = pl.BlockSpec(memory_space=pltpu.HBM)
+    return pl.pallas_call(
+        body,
+        out_shape=jax.ShapeDtypeStruct(half, BF16),
+        in_specs=[pl.BlockSpec(memory_space=pltpu.SMEM)] + [source] * (1 + len(others)),
+        out_specs=pl.BlockSpec(memory_space=pltpu.VMEM),
+        scratch_shapes=[pltpu.VMEM(half, F32)]
+        + [pltpu.VMEM(half, BF16) for _ in others]
+        + [pltpu.SemaphoreType.DMA((chunks,)) for _ in range(1 + len(others))],
+        cost_estimate=pl.CostEstimate(flops=0, bytes_accessed=6 * value.size, transcendentals=0),
+    )(core, value, *others)
+
+
+def compute_kernel(
+    pack_m, pack_0, pack_p, act, two, one,
+    terms, own, up, down,
+    flat, acts, pres, w_two, w_one, acc_two, acc_one,
+):
     c1, length, _ = act.shape
-    turned(act, flat, rows, 0, c1, 0)
-
-    def slide(x, carry):
-        value = rows[pl.ds(pl.multiple_of(x * c1, 16), c1), :].astype(F32)
-        stack = jnp.concatenate([slid(value, 1), value, slid(value, -1)], axis=0)
-        out[pl.ds(pl.multiple_of(x * 3 * c1, 16), 3 * c1), :] = stack.astype(BF16)
-        return carry
-
-    lax.fori_loop(0, length, slide, 0, unroll=4)
-
-    offsets = [(j, i) for j in range(3) for i in range(3)]
+    c2, c0 = (two.shape[4], one.shape[3])
+    pitch = c0 + c2
+    packs = (pack_m, pack_0, pack_p)
+
+    turned(act, flat, acts, 0, c1, 0)
+    offsets = [(m, n) for m in range(3) for n in range(3)]
     w_two[...] = jnp.concatenate(
         [
             jnp.concatenate([two[2 - i, 2 - j, 2 - k].astype(F32) for k in range(3)], axis=0)
@@ -113,71 +153,6 @@
         ],
         axis=1,
     ).astype(BF16)
-
-
-def slide(act, kernel_two, kernel_one):
-    c1, length, width = act.shape
-    c0, c2 = (kernel_one.shape[3], kernel_two.shape[4])
-    return vmem_call(
-        slide_kernel,
-        (
-            jax.ShapeDtypeStruct((length * 3 * c1, width), BF16),
-            jax.ShapeDtypeStruct((3 * c1, 9 * c2), BF16),
-            jax.ShapeDtypeStruct((3 * c0, 9 * c1), BF16),
-        ),
-        (
-            pltpu.VMEM((c1 * length, width), F32),
-            pltpu.VMEM((c1 * length, width), BF16),
-        ),
-        pl.CostEstimate(flops=0, bytes_accessed=8 * act.size, transcendentals=0),
-    )(act, kernel_two, kernel_one)
-
-
-def cast_kernel(core, src, out):
-    out[...] = src[...].astype(out.dtype)
-
-
-def half_call(body, core, steps, height, which, value, others, cost):
-    block = (height // steps, LANES)
-    plain = pl.BlockSpec(block, lambda n, core: (n, 0))
-    chosen = pl.BlockSpec(block, lambda n, core: (which(core[0]) * steps + n, 0))
-    return pl.pallas_call(
-        body,
-        grid_spec=pltpu.PrefetchScalarGridSpec(
-            num_scalar_prefetch=1,
-            grid=(steps,),
-            in_specs=[chosen] + [plain] * len(others),
-            out_specs=plain,
-        ),
-        out_shape=jax.ShapeDtypeStruct((height, LANES), BF16),
-        cost_estimate=pl.CostEstimate(flops=0, bytes_accessed=cost, transcendentals=0),
-    )(core, value, *others)
-
-
-def add_kernel(core, src, other, out):
-    out[...] = (src[...] + other[...].astype(F32)).astype(out.dtype)
-
-
-def swapped_half(core, value):
-    height = value.shape[0] // 2
-    steps = 2
-    send = half_call(cast_kernel, core, steps, height, lambda c: 1 - c, value, [], 6 * value.size // 2)
-    other = lax.ppermute(send, "core", [(0, 1), (1, 0)])
-    return half_call(add_kernel, core, steps, height, lambda c: c, value, [other], 4 * value.size)
-
-
-def compute_kernel(
-    pack_m, pack_0, pack_p, acts, w_two, w_one,
-    terms, own, up, down,
-    pres, acc_two, acc_one,
-):
-    length = acts.shape[0] // w_two.shape[0]
-    c1 = w_two.shape[0] // 3
-    c2 = w_two.shape[1] // 9
-    c0 = w_one.shape[0] // 3
-    pitch = c0 + c2
-    packs = (pack_m, pack_0, pack_p)
-
     stacked = 3 * c1
     pres[0:stacked, :] = jnp.zeros((stacked, LANES), BF16)
     pres[(length + 1) * stacked : (length + 2) * stacked, :] = jnp.zeros((stacked, LANES), BF16)
@@ -201,12 +176,12 @@
         for g in range(GROUP):
             part = sums[:, g * LANES : (g + 1) * LANES]
             grad = slid(part[0:c1], 1) + part[c1 : 2 * c1] + slid(part[2 * c1 : 3 * c1], -1)
-            stack = acts[pl.ds(pl.multiple_of((x + g) * stacked, 16), stacked), :]
-            value = stack[c1 : 2 * c1].astype(F32)
+            value = acts[pl.ds(pl.multiple_of((x + g) * c1, 16), c1), :].astype(F32)
             pre = (grad * jnp.where(value > 0, 1.0, 0.2)).astype(BF16).astype(F32)
             moved = jnp.concatenate([slid(pre, -1), pre, slid(pre, 1)], axis=0).astype(BF16)
             pres[pl.ds(pl.multiple_of((x + g + 1) * stacked, 16), stacked), :] = moved
-            columns.append(stack)
+            stack = jnp.concatenate([slid(value, 1), value, slid(value, -1)], axis=0)
+            columns.append(stack.astype(BF16))
         left = jnp.concatenate(columns, axis=1)
         acc_two[...] += lax.dot_general(
             right, left, (((1,), (1,)), ((), ())), preferred_element_type=F32
@@ -258,9 +233,9 @@
     )
 
 
-def compute(packs, acts, w_two, w_one, rows):
-    c0, c1, c2 = (w_one.shape[0] // 3, w_two.shape[0] // 3, w_two.shape[1] // 9)
-    length, width = (acts.shape[0] // (3 * c1), acts.shape[1])
+def compute(packs, act, kernel_two, kernel_one, rows):
+    c1, length, width = act.shape
+    c0, c2 = (kernel_one.shape[3], kernel_two.shape[4])
     plane = (length * c0, width)
     return vmem_call(
         compute_kernel,
@@ -271,12 +246,16 @@
             jax.ShapeDtypeStruct(plane, BF16),
         ),
         (
+            pltpu.VMEM((c1 * length, width), F32),
+            pltpu.VMEM((c1 * length, width), BF16),
             pltpu.VMEM(((length + 2) * 3 * c1, width), BF16),
+            pltpu.VMEM((3 * c1, 9 * c2), BF16),
+            pltpu.VMEM((3 * c0, 9 * c1), BF16),
             pltpu.VMEM((9 * c2, 3 * c1), F32),
             pltpu.VMEM((9 * c0, 3 * c1), F32),
         ),
         pl.CostEstimate(flops=10**10, bytes_accessed=40 * 2**20, transcendentals=0),
-    )(*packs, acts, w_two, w_one)
+    )(*packs, act, kernel_two, kernel_one)
 
 
 def merge_kernel(own, from_below, from_above, out, flat):
@@ -305,36 +284,63 @@
     )(own, from_below, from_above)
 
 
-def share_kernel(scale, parts, out):
-    total = (jnp.sum(parts[...].astype(F32), axis=0) * scale).astype(BF16)
+def share_kernel(scale, bucket, terms, out):
+    total = jnp.sum(bucket[...].astype(F32), axis=0).astype(BF16)
+    grads = (jnp.sum(terms[...].astype(F32), axis=0) * scale).astype(BF16)
+    height = total.shape[0]
 
     def write(n, carry):
-        out[n] = total
+        out[n, 0:height, :] = total
+        out[n, height : height + grads.shape[0], :] = grads
         return carry
 
     lax.fori_loop(0, out.shape[0], write, 0)
 
 
-def share(parts, scale):
+def share(bucket, terms, scale, copies):
+    rows = bucket.shape[1] + terms.shape[1]
     return vmem_call(
         lambda *refs: share_kernel(scale, *refs),
-        jax.ShapeDtypeStruct(parts.shape, BF16),
+        jax.ShapeDtypeStruct((copies, rows, LANES), BF16),
         (),
-        pl.CostEstimate(flops=parts.size, bytes_accessed=4 * parts.size, transcendentals=0),
-    )(parts)
-
-
-def gathered(parts, axes, scale=1.0):
-    return lax.all_to_all(share(parts, scale), axes, 0, 0)
-
-
-def finish_kernel(sizes, core, mine, other, raw_parts, bucket, out_one, out_two, raw):
+        pl.CostEstimate(flops=bucket.size, bytes_accessed=3 * bucket.size, transcendentals=0),
+    )(bucket, terms)
+
+
+def place(source, height, which, bucket, buffer, sems):
+    copies, count = (source.shape[0], sems.shape[0])
+    size = copies * height
+    step = copies // count
+    sent = []
+    for n in range(count):
+        for q in range(n * step, (n + 1) * step):
+            buffer[q * height : (q + 1) * height, :] = source[q, 0:height, :].astype(F32)
+        rows = pl.ds(n * step * height, step * height)
+        at = pl.ds(pl.multiple_of(which * size + n * step * height, 8), step * height)
+        sent.append(pltpu.make_async_copy(buffer.at[rows], bucket.at[at], sems.at[n]))
+        sent[-1].start()
+    return sent
+
+
+def start_kernel(height, core, mine, bucket, buffer, sems):
+    for copy in place(mine, height, core[0], bucket, buffer, sems):
+        copy.wait()
+
+
+def finish_kernel(sizes, height, core, mine, other, partial, bucket, out_one, out_two, raw, buffer, sems):
     c0, c1, c2 = sizes
-    half = mine.shape[0]
+    copies, rows, _ = mine.shape
+    extra = rows - height
     me = core[0]
-    bucket[pl.ds(pl.multiple_of(me * half, 8), half), :] = mine[...].astype(F32)
-    bucket[pl.ds(pl.multiple_of((1 - me) * half, 8), half), :] = other[...].astype(F32)
-    raw[...] = raw_parts[...].astype(F32)
+    sent = place(other, height, 1 - me, bucket, buffer, sems)
+
+    def unpack(q, carry):
+        for source, which in ((mine, me), (other, 1 - me)):
+            at = pl.multiple_of((2 * q + which) * extra, 8)
+            raw[pl.ds(at, extra), :] = source[q, height:rows, :].astype(F32)
+        return carry
+
+    lax.fori_loop(0, copies, unpack, 0)
     block = 3 * c1
     first = -(-9 * c2 // LANES) * block
     for i in range(3):
@@ -348,23 +354,44 @@
             for k in range(3):
                 to = (9 * i + 3 * j + k) * c0
                 out_one[to : to + c0, :] = raw[row : row + c0, k * c1 : (k + 1) * c1]
-
-
-def finish(core, mine, other, raw, sizes):
+    for copy in sent:
+        copy.wait()
+
+
+def finish(core, mine, other, length, sizes):
     c0, c1, c2 = sizes
+    copies, rows, _ = mine.shape
+    height = length // LANES // (2 * copies)
     spec = pl.BlockSpec(memory_space=pltpu.VMEM)
+    scalar, remote = (pl.BlockSpec(memory_space=pltpu.SMEM), pl.BlockSpec(memory_space=pltpu.HBM))
+    whole = jax.ShapeDtypeStruct((length // LANES, LANES), F32)
+    chunks = 4
+    scratch = [
+        pltpu.VMEM((copies * height, LANES), F32),
+        pltpu.SemaphoreType.DMA((chunks,)),
+    ]
+    params = pltpu.CompilerParams(vmem_limit_bytes=24 * 2**20)
+    partial = pl.pallas_call(
+        lambda *refs: start_kernel(height, *refs),
+        out_shape=whole,
+        in_specs=[scalar, spec],
+        out_specs=remote,
+        scratch_shapes=scratch,
+        compiler_params=params,
+    )(core, mine)
     return pl.pallas_call(
-        lambda *refs: finish_kernel(sizes, *refs),
+        lambda *refs: finish_kernel(sizes, height, *refs),
         out_shape=(
-            jax.ShapeDtypeStruct((2 * mine.shape[0], LANES), F32),
+            whole,
             jax.ShapeDtypeStruct((27 * c0, c1), F32),
             jax.ShapeDtypeStruct((27 * c1, c2), F32),
         ),
-        in_specs=[pl.BlockSpec(memory_space=pltpu.SMEM), spec, spec, spec],
-        out_specs=(spec, spec, spec),
-        scratch_shapes=[pltpu.VMEM(raw.shape, F32)],
-        compiler_params=pltpu.CompilerParams(vmem_limit_bytes=24 * 2**20),
-    )(core, mine, other, raw)
+        in_specs=[scalar, spec, spec, remote],
+        out_specs=(remote, spec, spec),
+        scratch_shapes=[pltpu.VMEM((2 * copies * (rows - height), LANES), F32)] + scratch,
+        input_output_aliases={3: 0},
+        compiler_params=params,
+    )(core, mine, other, partial)
 
 
 def halos(value):
@@ -379,30 +406,35 @@
     devices, copies = (lax.axis_size(EVERY), lax.axis_size(("dp", "slab")))
     length = grad_bucket.shape[1]
     core = lax.axis_index("core").astype(jnp.int32).reshape(1)
-    packed = pack(out_cot[0, 0], volume_in[0, 0])
+    swap = [(0, 1), (1, 0)]
+    bucket = grad_bucket.reshape(length // LANES, LANES)
+    send = half_call(cast_kernel, core, bucket, [])
+    cot, vol, send = lax.optimization_barrier((out_cot[0, 0], volume_in[0, 0], send))
+    packed = pack(cot, vol)
+    other, packed = lax.optimization_barrier((lax.ppermute(send, "core", swap), packed))
     below, above = halos(packed)
-    half = swapped_half(core, grad_bucket.reshape(length // LANES, LANES))
+    half = half_call(add_kernel, core, bucket, [other])
     act, half = lax.optimization_barrier((hidden_act[0, 0], half))
     parts = lax.all_to_all(half.reshape(copies, -1, LANES), ("dp", "slab"), 0, 0)
-    mine = gathered(parts, ("dp", "slab")).reshape(-1, LANES)
 
     used = -(-9 * c2 // LANES) * 3 * c1 + 9 * c0
     rows = ceil_to(used, 16 * devices)
-    acts, w_two, w_one = slide(act, kernel_two, kernel_one)
-    terms, own, up, down = compute((below, packed, above), acts, w_two, w_one, rows)
+    terms, own, up, down = compute((below, packed, above), act, kernel_two, kernel_one, rows)
+    terms, parts = lax.optimization_barrier((terms, parts))
     terms = lax.all_to_all(terms.reshape(devices, rows // devices, LANES), EVERY, 0, 0)
     cells = volume_in.shape[3] * volume_in.shape[4] * devices
-    raw = gathered(terms, EVERY, 1.0 / math.sqrt(cells)).reshape(-1, LANES)
-
+    shares = share(parts, terms, 1.0 / math.sqrt(cells), copies)
+
+    up, down, shares = lax.optimization_barrier((up, down, shares))
+    mine = lax.all_to_all(shares, ("dp", "slab"), 0, 0)
     count = lax.axis_size(SPACE)
     upward = [(i, i + 1) for i in range(count - 1)]
     from_below = lax.ppermute(up, SPACE, upward)
     from_above = lax.ppermute(down, SPACE, [(j, i) for i, j in upward])
     grad_input = merge(own, from_below, from_above, volume_in.shape[2:])
-
     mine, grad_input = lax.optimization_barrier((mine, grad_input))
-    other = lax.ppermute(mine, "core", [(0, 1), (1, 0)])
-    bucket_sum, total_one, total_two = finish(core, mine, other, raw, (c0, c1, c2))
+    other = lax.ppermute(mine, "core", swap)
+    bucket_sum, total_one, total_two = finish(core, mine, other, length, (c0, c1, c2))
     return (
         grad_input[None, None],
         total_one.reshape(3, 3, 3, c0, c1),

time: 80.6 us -> 75 us (0.931)
  blocking collectives: 22.8 us -> 14.5 us
  waiting for transfers between devices: 9.33 us -> 13.3 us
  starting transfers between devices: 26.7 us -> 23.3 us
  Pallas kernels: 18.3 us -> 19.9 us
    all_to_all x1 -> x0, blocking collectives: 10 us -> none  [gathered(): return lax.all_to_all(share(parts, scale), axes, 0, 0)]
    ppermute x1, waiting for transfers between devices: 2.04 us -> 4.64 us  [per_device(): from_below = lax.ppermute(up, SPACE, upward)]
    all_to_all x1, starting transfers between devices: 5.69 us -> 3.58 us  [per_device(): mine = lax.all_to_all(shares, ('dp', 'slab'), 0, 0)]
    pallas_call x1, Pallas kernels: 1.51 us -> 3.31 us  [pack(): pl.pallas_call(pack_kernel, out_shape=jax.ShapeDtypeStruct(((length + 2)...]
    all_to_all x1, blocking collectives: 12.8 us -> 14.5 us  [per_device(): lax.all_to_all(terms.reshape(devices, rows // devices, LANES), EVERY, 0, 0)]
    all_to_all x1, starting transfers between devices: 7.86 us -> 6.23 us  [per_device(): lax.all_to_all(half.reshape(copies, -1, LANES), ('dp', 'slab'), 0, 0)]
    ppermute x1, starting transfers between devices: 5.16 us -> 3.61 us  [per_device(): from_below = lax.ppermute(up, SPACE, upward)]
    ppermute x2, waiting for transfers between devices: 2.07 us -> 0.61 us  [the longest x1 0.61 us: per_device(): other = lax.ppermute(mine, 'core', swap)]
  transfers between devices with their start and end apart: 8 -> 8, of which waited for: 4 -> 5; matrix products, arithmetic and copies ran while one was open for 0% -> 0% of each run, Pallas kernels for 16% -> 20%
where the time goes in v4:
time: 75 us; the launch traced here: 74.1 us
  starting transfers between devices  23.3 us (31%)
  Pallas kernels  19.9 us (27%)
  blocking collectives  14.5 us (19%)
  waiting for transfers between devices  13.3 us (18%)
  local copies, waits for them, and re-layouts  2.32 us (3%)
  between operations  0.81 us (1%)
    all_to_all x1, blocking collectives, per_device(): lax.all_to_all(terms.reshape(devices, rows // devices, LANES), EVERY, 0, 0)  14.5 us
    pallas_call x1, Pallas kernels, compute(): vmem_call(compute_kernel, (jax.ShapeDtypeStruct((rows, LANES), BF16), jax...  7.21 us
    ppermute x2, starting transfers between devices, halos(): return (lax.ppermute(value, SPACE, up), lax.ppermute(value, SPACE, down))  6.55 us
    all_to_all x1, starting transfers between devices, per_device(): lax.all_to_all(half.reshape(copies, -1, LANES), ('dp', 'slab'), 0, 0)  6.23 us
    ppermute x1, waiting for transfers between devices, per_device(): from_below = lax.ppermute(up, SPACE, upward)  4.64 us
    pallas_call x2, Pallas kernels, half_call(): pl.pallas_call(body, out_shape=jax.ShapeDtypeStruct(half, BF16), in_specs...  4.53 us
    ppermute x1, waiting for transfers between devices, per_device(): from_above = lax.ppermute(down, SPACE, [(j, i) for i, j in upward])  4.43 us
    ppermute x1, starting transfers between devices, per_device(): from_below = lax.ppermute(up, SPACE, upward)  3.61 us
  transfers between devices with their start and end apart: 8, of which 5 were waited for; matrix products, arithmetic and copies ran while one was open for 0% of the time, Pallas kernels for 20%

profile of v4, /device:TPU:1, one launch (start us, length us, event | category | flops | bytes accessed | tf_op | source)
XLA Modules:
  0.0 74.1 jit_solution(6669588298326841093)
XLA Ops:
  0.6 2.2 %shard_map.93 = bf16[2048,128]{1,0:T(8,128)(2,1)} custom-call(s32[1]{0:T(128)} %bitcast.2.core.refs_0_, f32[4096,128]{1,0:T(8,128)} %bitcast.13), custom_call_target="tpu_custom_call" | custom-call | bytes 3145728 | tf_op jit(solution)/shard_map/pallas_call | solution.py:118
  2.8 0.1 collective-permute-start
  2.9 3.3 %shard_map.94.pack_0 = bf16[3168,128]{1,0:T(8,128)(2,1)} custom-call(bf16[32,64,128]{2,1,0:T(8,128)(2,1)} %bitcast.17, bf16[16,64,128]{2,1,0:T(8,128)(2,1)} %bitcast.18), custom_call_target="tpu_custom_call" | custom-call | bytes 1048576 | tf_op jit(solution)/shard_map/pallas_call | solution.py:74
  6.2 0.0 copy-start
  6.2 0.0 copy-start.1
  6.3 0.0 copy-start.6
  6.3 0.0 collective-permute-done.other
  6.3 0.0 copy-start.8
  6.3 2.5 %collective-permute-start.2 = (bf16[3168,128]{1,0:T(8,128)(2,1)}, bf16[3168,128]{1,0:T(8,128)(2,1)S(1)}, u32[]{:S(2)}, u32[]{:S(2)}) collective-permute-start(bf16[3168,128]{1,0:T(8,128)(2,1)} %shard_map.94.pack_0), channel_id=1, source_target_pairs={{1,0},{2,1},{3,2},{5,4},{6,5},{7,6},{9,8},{10,9},{11,10},{13,12},{... | collective-permute-start | bytes 2433032 | tf_op jit(solution)/shard_map/ppermute | solution.py:401
  8.8 4.1 %collective-permute-start.1 = (bf16[3168,128]{1,0:T(8,128)(2,1)}, bf16[3168,128]{1,0:T(8,128)(2,1)}, u32[]{:S(2)}, u32[]{:S(2)}) collective-permute-start(bf16[3168,128]{1,0:T(8,128)(2,1)} %shard_map.94.pack_0), channel_id=1, source_target_pairs={{0,1},{1,2},{2,3},{4,5},{5,6},{6,7},{8,9},{9,10},{10,11},{12,13},{... | collective-permute-start | bytes 2433032 | tf_op jit(solution)/shard_map/ppermute | solution.py:401
  12.9 0.0 copy-done.8
  12.9 2.4 %shard_map.95 = bf16[2048,128]{1,0:T(8,128)(2,1)} custom-call(s32[1]{0:T(128)} %bitcast.2.core.refs_0_, f32[4096,128]{1,0:T(8,128)} %bitcast.14, bf16[2048,128]{1,0:T(8,128)(2,1)} %copy-done.8), custom_call_target="tpu_custom_call" | custom-call | bytes 3145728 | tf_op jit(solution)/shard_map/pallas_call | solution.py:118
  15.3 6.2 %all-to-all-start = ((bf16[16,128,128]{2,1,0:T(8,128)(2,1)}), bf16[16,128,128]{2,1,0:T(8,128)(2,1)S(1)}, u32[]{:S(2)}, u32[]{:S(2)}) async-start(bf16[16,128,128]{2,1,0:T(8,128)(2,1)} %bitcast.16), calls=%async_computation | async-start | bytes 1048576 | tf_op jit(solution)/shard_map/all_to_all | solution.py:418
  21.5 0.0 collective-permute-done.2.pack_p
  21.5 0.8 %collective-permute-done.1.pack_m = bf16[3168,128]{1,0:T(8,128)(2,1)} collective-permute-done((bf16[3168,128]{1,0:T(8,128)(2,1)}, bf16[3168,128]{1,0:T(8,128)(2,1)}, u32[]{:S(2)}, u32[]{:S(2)}) %collective-permute-start.1) | collective-permute-done | bytes 811040 | tf_op jit(solution)/shard_map/ppermute | solution.py:401
  22.4 0.0 copy-done
  22.4 0.0 copy-done.1
  22.4 0.0 copy-done.6
  22.4 0.0 copy-start.7
  22.4 0.9 %copy-done.7 = bf16[3,3,3,16,32]{4,3,2,1,0:T(8,128)(2,1)S(1)} copy-done((bf16[3,3,3,16,32]{4,3,2,1,0:T(8,128)(2,1)S(1)}, bf16[3,3,3,16,32]{4,3,2,1,0:T(8,128)(2,1)}, u32[]{:S(2)}) %copy-start.7) | copy-done | bytes 27672
  23.3 7.2 %shard_map.96 = (bf16[512,128]{1,0:T(8,128)(2,1)S(1)}, f32[1024,128]{1,0:T(8,128)S(1)}, bf16[1024,128]{1,0:T(8,128)(2,1)S(1)}, bf16[1024,128]{1,0:T(8,128)(2,1)S(1)}) custom-call(bf16[3168,128]{1,0:T(8,128)(2,1)} %collective-permute-done.1.pack_m, bf16[3168,128]{1,0:T(8,128)(2,1)S(1)} %copy-done, bf16[3168,128]{1,0:T(8,128)(2,1)S(1)} %collective-permute-done.2.pack_p, ...), custom_call_target="tpu_custom_call" | custom-call | flops 10000000000 | bytes 41943040 | tf_op jit(solution)/shard_map/pallas_call | solution.py:240
  30.5 0.0 copy-start.2
  30.5 0.7 copy-done.2
  31.2 0.0 copy-start.4
  31.2 0.7 copy-done.4
  31.9 2.8 %all-to-all-done.refs_0_ = bf16[16,128,128]{2,1,0:T(8,128)(2,1)S(1)} async-done(((bf16[16,128,128]{2,1,0:T(8,128)(2,1)}), bf16[16,128,128]{2,1,0:T(8,128)(2,1)S(1)}, u32[]{:S(2)}, u32[]{:S(2)}) %all-to-all-start) | async-done | bytes 524320 | tf_op jit(solution)/shard_map/all_to_all | solution.py:418
  34.6 0.0 copy-start.5
  34.6 0.0 copy-start.3
  34.6 14.5 %all_to_all.15.refs_1_ = bf16[32,16,128]{2,1,0:T(8,128)(2,1)S(1)} all-to-all(bf16[32,16,128]{2,1,0:T(8,128)(2,1)S(1)} %bitcast.11), channel_id=1, replica_groups=mesh['dp'=8,'slab'=2,'core'=2] {'dp','slab','core'}, dimensions={0} | all-to-all | bytes 262144 | tf_op jit(solution)/shard_map/all_to_all | solution.py:424
  49.2 1.0 %shard_map.97 = bf16[16,144,128]{2,1,0:T(8,128)(2,1)} custom-call(bf16[16,128,128]{2,1,0:T(8,128)(2,1)S(1)} %all-to-all-done.refs_0_, bf16[32,16,128]{2,1,0:T(8,128)(2,1)S(1)} %all_to_all.15.refs_1_), custom_call_target="tpu_custom_call" | custom-call | flops 262144 | bytes 786432 | tf_op jit(solution)/shard_map/pallas_call | solution.py:302
  50.2 3.6 %all-to-all-start.2 = ((bf16[16,144,128]{2,1,0:T(8,128)(2,1)}), bf16[16,144,128]{2,1,0:T(8,128)(2,1)S(1)}, u32[]{:S(2)}, u32[]{:S(2)}) async-start(bf16[16,144,128]{2,1,0:T(8,128)(2,1)} %shard_map.97), calls=%async_computation.2 | async-start | bytes 1179648 | tf_op jit(solution)/shard_map/all_to_all | solution.py:429
  53.8 0.0 copy-done.5
  53.8 3.6 %collective-permute-start.3 = (bf16[1024,128]{1,0:T(8,128)(2,1)S(1)}, bf16[1024,128]{1,0:T(8,128)(2,1)S(1)}, u32[]{:S(2)}, u32[]{:S(2)}) collective-permute-start(bf16[1024,128]{1,0:T(8,128)(2,1)S(1)} %copy-done.5), channel_id=1, source_target_pairs={{0,1},{1,2},{2,3},{4,5},{5,6},{6,7},{8,9},{9,10},{10,11},{12,13},{... | collective-permute-start | bytes 786440 | tf_op jit(solution)/shard_map/ppermute | solution.py:432
  57.4 0.0 copy-done.3
  57.4 1.9 %collective-permute-start.4 = (bf16[1024,128]{1,0:T(8,128)(2,1)S(1)}, bf16[1024,128]{1,0:T(8,128)(2,1)S(1)}, u32[]{:S(2)}, u32[]{:S(2)}) collective-permute-start(bf16[1024,128]{1,0:T(8,128)(2,1)S(1)} %copy-done.3), channel_id=1, source_target_pairs={{1,0},{2,1},{3,2},{5,4},{6,5},{7,6},{9,8},{10,9},{11,10},{13,12},{... | collective-permute-start | bytes 786440 | tf_op jit(solution)/shard_map/ppermute | solution.py:433
  59.4 4.6 %collective-permute-done.3.from_below = bf16[1024,128]{1,0:T(8,128)(2,1)S(1)} collective-permute-done((bf16[1024,128]{1,0:T(8,128)(2,1)S(1)}, bf16[1024,128]{1,0:T(8,128)(2,1)S(1)}, u32[]{:S(2)}, u32[]{:S(2)}) %collective-permute-start.3) | collective-permute-done | bytes 262176 | tf_op jit(solution)/shard_map/ppermute | solution.py:432
  64.0 4.4 %collective-permute-done.4.from_above = bf16[1024,128]{1,0:T(8,128)(2,1)S(1)} collective-permute-done((bf16[1024,128]{1,0:T(8,128)(2,1)S(1)}, bf16[1024,128]{1,0:T(8,128)(2,1)S(1)}, u32[]{:S(2)}, u32[]{:S(2)}) %collective-permute-start.4) | collective-permute-done | bytes 262176 | tf_op jit(solution)/shard_map/ppermute | solution.py:433
  68.4 1.0 %shard_map.98 = bf16[16,64,128]{2,1,0:T(8,128)(2,1)} custom-call(f32[1024,128]{1,0:T(8,128)S(1)} %get-tuple-element.38.own, bf16[1024,128]{1,0:T(8,128)(2,1)S(1)} %collective-permute-done.3.from_below, bf16[1024,128]{1,0:T(8,128)(2,1)S(1)} %collective-permute-done.4.from_above), custom_call_target="tpu_custom_call" | custom-call | flops 262144 | bytes 1048576 | tf_op jit(solution)/shard_map/pallas_call | solution.py:279
  69.4 0.0 all-to-all-done.2.refs_1_
  69.4 1.2 %collective-permute-start.5 = (bf16[16,144,128]{2,1,0:T(8,128)(2,1)S(1)}, bf16[16,144,128]{2,1,0:T(8,128)(2,1)S(1)}, u32[]{:S(2)}, u32[]{:S(2)}) collective-permute-start(bf16[16,144,128]{2,1,0:T(8,128)(2,1)S(1)} %all-to-all-done.2.refs_1_), channel_id=1, source_target_pairs={{0,1},{1,0},{2,3},{3,2},{4,5},{5,4},{6,7},{7,6},{8,9},{9,8},{10,11... | collective-permute-start | bytes 1769480 | tf_op jit(solution)/shard_map/ppermute | solution.py:436
  70.6 1.0 %shard_map.99.refs_3_ = f32[4096,128]{1,0:T(8,128)} custom-call(s32[1]{0:T(128)} %bitcast.2.core.refs_0_, bf16[16,144,128]{2,1,0:T(8,128)(2,1)S(1)} %all-to-all-done.2.refs_1_), custom_call_target="tpu_custom_call" | custom-call | tf_op jit(solution)/shard_map/pallas_call | solution.py:374
  71.7 0.6 collective-permute-done.5.refs_2_
  72.3 1.8 %shard_map.100 = (f32[4096,128]{1,0:T(8,128)}, f32[432,32]{1,0:T(8,128)}, f32[864,32]{1,0:T(8,128)}) custom-call(s32[1]{0:T(128)} %bitcast.2.core.refs_0_, bf16[16,144,128]{2,1,0:T(8,128)(2,1)S(1)} %all-to-all-done.2.refs_1_, bf16[16,144,128]{2,1,0:T(8,128)(2,1)S(1)} %collective-permute-done.5.refs_2_, ...), custom_call_target="tpu_custom_call", output_to_operand_aliasing={{0}: (3, {})} | custom-call | tf_op jit(solution)/shard_map/pallas_call | solution.py:382
Async XLA Ops:
  2.8 3.5 %collective-permute-start = (bf16[2048,128]{1,0:T(8,128)(2,1)}, bf16[2048,128]{1,0:T(8,128)(2,1)S(1)}, u32[]{:S(2)}, u32[]{:S(2)}) collective-permute-start(bf16[2048,128]{1,0:T(8,128)(2,1)} %shard_map.93), channel_id=1, source_target_pairs={{0,1},{1,0},{2,3},{3,2},{4,5},{5,4},{6,7},{7,6},{8,9},{9,8},{10,11... | collective-permute-start | bytes 1572872 | tf_op jit(solution)/shard_map/ppermute | solution.py:414
  6.2 16.1 %copy-start = (bf16[3168,128]{1,0:T(8,128)(2,1)S(1)}, bf16[3168,128]{1,0:T(8,128)(2,1)}, u32[]{:S(2)}) copy-start(bf16[3168,128]{1,0:T(8,128)(2,1)} %shard_map.94.pack_0) | copy-start | bytes 2433028
  6.2 16.1 %copy-start.1 = (bf16[1,1,32,64,128]{4,3,2,1,0:T(8,128)(2,1)S(1)}, bf16[1,1,32,64,128]{4,3,2,1,0:T(8,128)(2,1)}, u32[]{:S(2)}) copy-start(bf16[1,1,32,64,128]{4,3,2,1,0:T(8,128)(2,1)} %param.7) | copy-start | bytes 1572868
  6.3 16.1 %copy-start.6 = (bf16[3,3,3,32,32]{4,3,2,1,0:T(8,128)(2,1)S(1)}, bf16[3,3,3,32,32]{4,3,2,1,0:T(8,128)(2,1)}, u32[]{:S(2)}) copy-start(bf16[3,3,3,32,32]{4,3,2,1,0:T(8,128)(2,1)} %two.1) | copy-start | bytes 165892
  6.3 6.6 %copy-start.8 = (bf16[2048,128]{1,0:T(8,128)(2,1)}, bf16[2048,128]{1,0:T(8,128)(2,1)S(1)}, u32[]{:S(2)}) copy-start(bf16[2048,128]{1,0:T(8,128)(2,1)S(1)} %collective-permute-done.other) | copy-start | bytes 1572868
  6.3 15.2 %collective-permute-start.2 = (bf16[3168,128]{1,0:T(8,128)(2,1)}, bf16[3168,128]{1,0:T(8,128)(2,1)S(1)}, u32[]{:S(2)}, u32[]{:S(2)}) collective-permute-start(bf16[3168,128]{1,0:T(8,128)(2,1)} %shard_map.94.pack_0), channel_id=1, source_target_pairs={{1,0},{2,1},{3,2},{5,4},{6,5},{7,6},{9,8},{10,9},{11,10},{13,12},{... | collective-permute-start | bytes 2433032 | tf_op jit(solution)/shard_map/ppermute | solution.py:401
  8.8 13.6 %collective-permute-start.1 = (bf16[3168,128]{1,0:T(8,128)(2,1)}, bf16[3168,128]{1,0:T(8,128)(2,1)}, u32[]{:S(2)}, u32[]{:S(2)}) collective-permute-start(bf16[3168,128]{1,0:T(8,128)(2,1)} %shard_map.94.pack_0), channel_id=1, source_target_pairs={{0,1},{1,2},{2,3},{4,5},{5,6},{6,7},{8,9},{9,10},{10,11},{12,13},{... | collective-permute-start | bytes 2433032 | tf_op jit(solution)/shard_map/ppermute | solution.py:401
  15.3 19.4 %all-to-all-start = ((bf16[16,128,128]{2,1,0:T(8,128)(2,1)}), bf16[16,128,128]{2,1,0:T(8,128)(2,1)S(1)}, u32[]{:S(2)}, u32[]{:S(2)}) async-start(bf16[16,128,128]{2,1,0:T(8,128)(2,1)} %bitcast.16), calls=%async_computation | async-start | bytes 1048576 | tf_op jit(solution)/shard_map/all_to_all | solution.py:418
  22.4 0.9 %copy-start.7 = (bf16[3,3,3,16,32]{4,3,2,1,0:T(8,128)(2,1)S(1)}, bf16[3,3,3,16,32]{4,3,2,1,0:T(8,128)(2,1)}, u32[]{:S(2)}) copy-start(bf16[3,3,3,16,32]{4,3,2,1,0:T(8,128)(2,1)} %one.1) | copy-start | bytes 82948
  30.5 0.7 copy-start.2
  31.2 0.7 copy-start.4
  34.6 19.2 %copy-start.5 = (bf16[1024,128]{1,0:T(8,128)(2,1)S(1)}, bf16[1024,128]{1,0:T(8,128)(2,1)}, u32[]{:S(2)}) copy-start(bf16[1024,128]{1,0:T(8,128)(2,1)} %copy-done.4) | copy-start | bytes 786436
  34.6 22.8 %copy-start.3 = (bf16[1024,128]{1,0:T(8,128)(2,1)S(1)}, bf16[1024,128]{1,0:T(8,128)(2,1)}, u32[]{:S(2)}) copy-start(bf16[1024,128]{1,0:T(8,128)(2,1)} %copy-done.2) | copy-start | bytes 786436
  50.2 19.2 %all-to-all-start.2 = ((bf16[16,144,128]{2,1,0:T(8,128)(2,1)}), bf16[16,144,128]{2,1,0:T(8,128)(2,1)S(1)}, u32[]{:S(2)}, u32[]{:S(2)}) async-start(bf16[16,144,128]{2,1,0:T(8,128)(2,1)} %shard_map.97), calls=%async_computation.2 | async-start | bytes 1179648 | tf_op jit(solution)/shard_map/all_to_all | solution.py:429
  53.8 10.2 %collective-permute-start.3 = (bf16[1024,128]{1,0:T(8,128)(2,1)S(1)}, bf16[1024,128]{1,0:T(8,128)(2,1)S(1)}, u32[]{:S(2)}, u32[]{:S(2)}) collective-permute-start(bf16[1024,128]{1,0:T(8,128)(2,1)S(1)} %copy-done.5), channel_id=1, source_target_pairs={{0,1},{1,2},{2,3},{4,5},{5,6},{6,7},{8,9},{9,10},{10,11},{12,13},{... | collective-permute-start | bytes 786440 | tf_op jit(solution)/shard_map/ppermute | solution.py:432
  57.4 11.0 %collective-permute-start.4 = (bf16[1024,128]{1,0:T(8,128)(2,1)S(1)}, bf16[1024,128]{1,0:T(8,128)(2,1)S(1)}, u32[]{:S(2)}, u32[]{:S(2)}) collective-permute-start(bf16[1024,128]{1,0:T(8,128)(2,1)S(1)} %copy-done.3), channel_id=1, source_target_pairs={{1,0},{2,1},{3,2},{5,4},{6,5},{7,6},{9,8},{10,9},{11,10},{13,12},{... | collective-permute-start | bytes 786440 | tf_op jit(solution)/shard_map/ppermute | solution.py:433
  69.4 2.9 %collective-permute-start.5 = (bf16[16,144,128]{2,1,0:T(8,128)(2,1)S(1)}, bf16[16,144,128]{2,1,0:T(8,128)(2,1)S(1)}, u32[]{:S(2)}, u32[]{:S(2)}) collective-permute-start(bf16[16,144,128]{2,1,0:T(8,128)(2,1)S(1)} %all-to-all-done.2.refs_1_), channel_id=1, source_target_pairs={{0,1},{1,0},{2,3},{3,2},{4,5},{5,4},{6,7},{7,6},{8,9},{9,8},{10,11... | collective-permute-start | bytes 1769480 | tf_op jit(solution)/shard_map/ppermute | solution.py:436

commit v5 on v4

--- a/solution.py
+++ b/solution.py
@@ -7,8 +7,8 @@
 from jax.experimental.pallas import tpu as pltpu
 from jax.sharding import Mesh, PartitionSpec as P
 
-SPACE = ("slab", "core")
-EVERY = ("dp", "slab", "core")
+SPACE = ("y", "core")
+EVERY = ("z", "x", "y", "core")
 GROUP = 8
 LANES = 128
 BF16 = jnp.bfloat16
@@ -81,6 +81,7 @@
             pltpu.VMEM((vol.shape[0] * length, width), F32),
             pltpu.SemaphoreType.DMA((pieces,)),
         ],
+        compiler_params=pltpu.CompilerParams(vmem_limit_bytes=24 * 2**20),
         cost_estimate=pl.CostEstimate(flops=0, bytes_accessed=4 * cot.size, transcendentals=0),
     )(cot, vol)
 
@@ -98,39 +99,81 @@
     return [(pl.ds(n * step, step), copy) for n, copy in enumerate(copies)]
 
 
-def cast_kernel(core, src, out, buffer, sems):
-    for rows, copy in fetched_chunks(src, (1 - core[0]) * out.shape[0], buffer, sems):
+def cast_kernel(src, out, buffer, sems):
+    start = (1 - lax.axis_index("core")) * out.shape[0]
+    for rows, copy in fetched_chunks(src, start, buffer, sems):
         copy.wait()
         out[rows, :] = buffer[rows, :].astype(out.dtype)
 
 
-def add_kernel(core, src, other, out, buffer, more, sems, more_sems):
-    chunks = fetched_chunks(src, core[0] * out.shape[0], buffer, sems)
-    for (rows, copy), (_, second) in zip(chunks, fetched_chunks(other, 0, more, more_sems)):
-        copy.wait()
-        second.wait()
-        out[rows, :] = (buffer[rows, :] + more[rows, :].astype(F32)).astype(out.dtype)
-
-
-def half_call(body, core, value, others, chunks=8):
+def cast(value, chunks=8):
     half = (value.shape[0] // 2, LANES)
-    source = pl.BlockSpec(memory_space=pltpu.HBM)
     return pl.pallas_call(
-        body,
+        cast_kernel,
         out_shape=jax.ShapeDtypeStruct(half, BF16),
-        in_specs=[pl.BlockSpec(memory_space=pltpu.SMEM)] + [source] * (1 + len(others)),
+        in_specs=[pl.BlockSpec(memory_space=pltpu.HBM)],
         out_specs=pl.BlockSpec(memory_space=pltpu.VMEM),
-        scratch_shapes=[pltpu.VMEM(half, F32)]
-        + [pltpu.VMEM(half, BF16) for _ in others]
-        + [pltpu.SemaphoreType.DMA((chunks,)) for _ in range(1 + len(others))],
+        scratch_shapes=[pltpu.VMEM(half, F32), pltpu.SemaphoreType.DMA((chunks,))],
         cost_estimate=pl.CostEstimate(flops=0, bytes_accessed=6 * value.size, transcendentals=0),
-    )(core, value, *others)
+    )(value)
+
+
+def add_kernel(src, other, out):
+    rows = out.shape[0]
+    step = rows // 8
+    start = lax.axis_index("core") * rows
+
+    def add(n, carry):
+        at = pl.ds(pl.multiple_of(n * step, 16), step)
+        own = src[pl.ds(pl.multiple_of(start + n * step, 16), step), :]
+        out[at, :] = (own + other[at, :].astype(F32)).astype(out.dtype)
+        return carry
+
+    lax.fori_loop(0, 8, add, 0)
+
+
+def add(value, other):
+    return vmem_call(
+        add_kernel,
+        jax.ShapeDtypeStruct(other.shape, BF16),
+        (),
+        pl.CostEstimate(flops=0, bytes_accessed=4 * value.size, transcendentals=0),
+    )(value, other)
+
+
+def bit(axis, distance):
+    return lax.rem(lax.axis_index(axis) // distance, 2)
+
+
+def split_to(total, mine, send, keep):
+    half = total.shape[0] // 2
+    keep[...] = total[pl.ds(pl.multiple_of(mine * half, 16), half), :]
+    send[...] = total[pl.ds(pl.multiple_of((1 - mine) * half, 16), half), :].astype(send.dtype)
+
+
+def halve_kernel(axis, distance, keep, other, send_out, keep_out, total):
+    total[...] = keep[...] + other[...].astype(F32)
+    split_to(total, bit(axis, distance), send_out, keep_out)
+
+
+def halve(keep, other, axis, distance):
+    half = (keep.shape[0] // 2, LANES)
+    return vmem_call(
+        lambda *refs: halve_kernel(axis, distance, *refs),
+        (jax.ShapeDtypeStruct(half, BF16), jax.ShapeDtypeStruct(half, F32)),
+        (pltpu.VMEM(keep.shape, F32),),
+        pl.CostEstimate(flops=0, bytes_accessed=8 * keep.size, transcendentals=0),
+    )(keep, other)
+
+
+def exchanged(value, axis, distance):
+    return lax.ppermute(value, axis, [(i, i ^ distance) for i in range(lax.axis_size(axis))])
 
 
 def compute_kernel(
     pack_m, pack_0, pack_p, act, two, one,
-    terms, own, up, down,
-    flat, acts, pres, w_two, w_one, acc_two, acc_one,
+    send, keep, own, up, down,
+    terms, flat, acts, pres, w_two, w_one, acc_two, acc_one,
 ):
     c1, length, _ = act.shape
     c2, c0 = (two.shape[4], one.shape[3])
@@ -216,9 +259,10 @@
     blocks = -(-width // LANES)
     for block in range(blocks):
         part = two[:, block * LANES : min(width, (block + 1) * LANES)]
-        terms[block * rows : (block + 1) * rows, 0 : part.shape[1]] = part.astype(terms.dtype)
+        terms[block * rows : (block + 1) * rows, 0 : part.shape[1]] = part
     one = acc_one[...]
-    terms[blocks * rows : blocks * rows + one.shape[0], 0 : one.shape[1]] = one.astype(terms.dtype)
+    terms[blocks * rows : blocks * rows + one.shape[0], 0 : one.shape[1]] = one
+    split_to(terms, bit("core", 1), send, keep)
 
 
 def vmem_call(body, out_shape, scratch=(), cost=None, limit=24 * 2**20):
@@ -240,12 +284,14 @@
     return vmem_call(
         compute_kernel,
         (
-            jax.ShapeDtypeStruct((rows, LANES), BF16),
+            jax.ShapeDtypeStruct((rows // 2, LANES), BF16),
+            jax.ShapeDtypeStruct((rows // 2, LANES), F32),
             jax.ShapeDtypeStruct(plane, F32),
             jax.ShapeDtypeStruct(plane, BF16),
             jax.ShapeDtypeStruct(plane, BF16),
         ),
         (
+            pltpu.VMEM((rows, LANES), F32),
             pltpu.VMEM((c1 * length, width), F32),
             pltpu.VMEM((c1 * length, width), BF16),
             pltpu.VMEM(((length + 2) * 3 * c1, width), BF16),
@@ -284,9 +330,9 @@
     )(own, from_below, from_above)
 
 
-def share_kernel(scale, bucket, terms, out):
-    total = jnp.sum(bucket[...].astype(F32), axis=0).astype(BF16)
-    grads = (jnp.sum(terms[...].astype(F32), axis=0) * scale).astype(BF16)
+def share_kernel(parts, keep, other, out):
+    total = jnp.sum(parts[...].astype(F32), axis=0).astype(BF16)
+    grads = (keep[...] + other[...].astype(F32)).astype(BF16)
     height = total.shape[0]
 
     def write(n, carry):
@@ -297,50 +343,72 @@
     lax.fori_loop(0, out.shape[0], write, 0)
 
 
-def share(bucket, terms, scale, copies):
-    rows = bucket.shape[1] + terms.shape[1]
+def share(parts, keep, other, copies):
+    rows = parts.shape[1] + keep.shape[0]
     return vmem_call(
-        lambda *refs: share_kernel(scale, *refs),
+        share_kernel,
         jax.ShapeDtypeStruct((copies, rows, LANES), BF16),
         (),
-        pl.CostEstimate(flops=bucket.size, bytes_accessed=3 * bucket.size, transcendentals=0),
-    )(bucket, terms)
-
-
-def place(source, height, which, bucket, buffer, sems):
-    copies, count = (source.shape[0], sems.shape[0])
-    size = copies * height
-    step = copies // count
+        pl.CostEstimate(flops=parts.size, bytes_accessed=3 * parts.size, transcendentals=0),
+    )(parts, keep, other)
+
+
+def column_kernel(scale, height, column, out):
+    along, rows, _ = column.shape
+    grads = jnp.sum(column[:, height:rows, :].astype(F32), axis=0) * scale
+    grads = grads.astype(BF16)
+
+    def write(n, carry):
+        for m in range(along):
+            out[n, m * height : (m + 1) * height, :] = column[m, 0:height, :]
+        out[n, along * height : along * height + rows - height, :] = grads
+        return carry
+
+    lax.fori_loop(0, out.shape[0], write, 0)
+
+
+def column_share(column, height, scale, copies):
+    along, rows, _ = column.shape
+    return vmem_call(
+        lambda *refs: column_kernel(scale, height, *refs),
+        jax.ShapeDtypeStruct((copies, along * height + rows - height, LANES), BF16),
+        (),
+        pl.CostEstimate(flops=0, bytes_accessed=4 * column.size, transcendentals=0),
+    )(column)
+
+
+def place(source, height, along, which, bucket, buffer, sems):
+    count = source.shape[0]
     sent = []
-    for n in range(count):
-        for q in range(n * step, (n + 1) * step):
-            buffer[q * height : (q + 1) * height, :] = source[q, 0:height, :].astype(F32)
-        rows = pl.ds(n * step * height, step * height)
-        at = pl.ds(pl.multiple_of(which * size + n * step * height, 8), step * height)
-        sent.append(pltpu.make_async_copy(buffer.at[rows], bucket.at[at], sems.at[n]))
+    for z in range(along):
+        for n in range(count):
+            rows = slice((z * count + n) * height, (z * count + n + 1) * height)
+            buffer[rows, :] = source[n, z * height : (z + 1) * height, :].astype(F32)
+        rows = pl.ds(z * count * height, count * height)
+        at = pl.ds(pl.multiple_of((which * along + z) * count * height, 8), count * height)
+        sent.append(pltpu.make_async_copy(buffer.at[rows], bucket.at[at], sems.at[z]))
         sent[-1].start()
     return sent
 
 
-def start_kernel(height, core, mine, bucket, buffer, sems):
-    for copy in place(mine, height, core[0], bucket, buffer, sems):
+def start_kernel(height, along, mine, bucket, buffer, sems):
+    for copy in place(mine, height, along, lax.axis_index("core"), bucket, buffer, sems):
         copy.wait()
 
 
-def finish_kernel(sizes, height, core, mine, other, partial, bucket, out_one, out_two, raw, buffer, sems):
+def finish_kernel(sizes, height, along, across, mine, other, partial, bucket, out_one, out_two, raw, buffer, sems):
     c0, c1, c2 = sizes
-    copies, rows, _ = mine.shape
-    extra = rows - height
-    me = core[0]
-    sent = place(other, height, 1 - me, bucket, buffer, sems)
-
-    def unpack(q, carry):
-        for source, which in ((mine, me), (other, 1 - me)):
-            at = pl.multiple_of((2 * q + which) * extra, 8)
-            raw[pl.ds(at, extra), :] = source[q, height:rows, :].astype(F32)
-        return carry
-
-    lax.fori_loop(0, copies, unpack, 0)
+    count, rows, _ = mine.shape
+    extra = rows - along * height
+    me = lax.axis_index("core")
+    sent = place(other, height, along, 1 - me, bucket, buffer, sems)
+
+    nx, ny = across
+    for x in range(nx):
+        for y in range(ny):
+            for source, which in ((mine, me), (other, 1 - me)):
+                at = pl.multiple_of((which * count + y * nx + x) * extra, 8)
+                raw[pl.ds(at, extra), :] = source[x * ny + y, along * height : rows, :].astype(F32)
     block = 3 * c1
     first = -(-9 * c2 // LANES) * block
     for i in range(3):
@@ -358,40 +426,38 @@
         copy.wait()
 
 
-def finish(core, mine, other, length, sizes):
+def finish(mine, other, length, along, across, sizes):
     c0, c1, c2 = sizes
-    copies, rows, _ = mine.shape
-    height = length // LANES // (2 * copies)
-    spec = pl.BlockSpec(memory_space=pltpu.VMEM)
-    scalar, remote = (pl.BlockSpec(memory_space=pltpu.SMEM), pl.BlockSpec(memory_space=pltpu.HBM))
+    count, rows, _ = mine.shape
+    height = length // LANES // (2 * along * count)
+    spec, remote = (pl.BlockSpec(memory_space=pltpu.VMEM), pl.BlockSpec(memory_space=pltpu.HBM))
     whole = jax.ShapeDtypeStruct((length // LANES, LANES), F32)
-    chunks = 4
     scratch = [
-        pltpu.VMEM((copies * height, LANES), F32),
-        pltpu.SemaphoreType.DMA((chunks,)),
+        pltpu.VMEM((along * count * height, LANES), F32),
+        pltpu.SemaphoreType.DMA((along,)),
     ]
     params = pltpu.CompilerParams(vmem_limit_bytes=24 * 2**20)
     partial = pl.pallas_call(
-        lambda *refs: start_kernel(height, *refs),
+        lambda *refs: start_kernel(height, along, *refs),
         out_shape=whole,
-        in_specs=[scalar, spec],
+        in_specs=[spec],
         out_specs=remote,
         scratch_shapes=scratch,
         compiler_params=params,
-    )(core, mine)
+    )(mine)
     return pl.pallas_call(
-        lambda *refs: finish_kernel(sizes, height, *refs),
+        lambda *refs: finish_kernel(sizes, height, along, across, *refs),
         out_shape=(
             whole,
             jax.ShapeDtypeStruct((27 * c0, c1), F32),
             jax.ShapeDtypeStruct((27 * c1, c2), F32),
         ),
-        in_specs=[scalar, spec, spec, remote],
+        in_specs=[spec, spec, remote],
         out_specs=(remote, spec, spec),
-        scratch_shapes=[pltpu.VMEM((2 * copies * (rows - height), LANES), F32)] + scratch,
-        input_output_aliases={3: 0},
+        scratch_shapes=[pltpu.VMEM((2 * count * (rows - along * height), LANES), F32)] + scratch,
+        input_output_aliases={2: 0},
         compiler_params=params,
-    )(core, mine, other, partial)
+    )(mine, other, partial)
 
 
 def halos(value):
@@ -403,38 +469,44 @@
 
 def per_device(volume_in, hidden_act, out_cot, kernel_one, kernel_two, grad_bucket):
     c0, c1, c2 = (volume_in.shape[2], hidden_act.shape[2], out_cot.shape[2])
-    devices, copies = (lax.axis_size(EVERY), lax.axis_size(("dp", "slab")))
+    devices, planar = (lax.axis_size(EVERY), lax.axis_size(("x", "y")))
+    along, across = (lax.axis_size("z"), (lax.axis_size("x"), lax.axis_size("y")))
     length = grad_bucket.shape[1]
-    core = lax.axis_index("core").astype(jnp.int32).reshape(1)
-    swap = [(0, 1), (1, 0)]
     bucket = grad_bucket.reshape(length // LANES, LANES)
-    send = half_call(cast_kernel, core, bucket, [])
+    send = cast(bucket)
     cot, vol, send = lax.optimization_barrier((out_cot[0, 0], volume_in[0, 0], send))
     packed = pack(cot, vol)
-    other, packed = lax.optimization_barrier((lax.ppermute(send, "core", swap), packed))
+    other, packed = lax.optimization_barrier((exchanged(send, "core", 1), packed))
     below, above = halos(packed)
-    half = half_call(add_kernel, core, bucket, [other])
+    half = add(bucket, other)
     act, half = lax.optimization_barrier((hidden_act[0, 0], half))
-    parts = lax.all_to_all(half.reshape(copies, -1, LANES), ("dp", "slab"), 0, 0)
+    parts = lax.all_to_all(half.reshape(along * planar, -1, LANES), ("z", "x", "y"), 0, 0)
 
     used = -(-9 * c2 // LANES) * 3 * c1 + 9 * c0
-    rows = ceil_to(used, 16 * devices)
-    terms, own, up, down = compute((below, packed, above), act, kernel_two, kernel_one, rows)
-    terms, parts = lax.optimization_barrier((terms, parts))
-    terms = lax.all_to_all(terms.reshape(devices, rows // devices, LANES), EVERY, 0, 0)
+    rows = ceil_to(used, 16 * 2 * planar)
+    send, keep, own, up, down = compute((below, packed, above), act, kernel_two, kernel_one, rows)
+    other = exchanged(send, "core", 1)
+    for axis in ("y", "x"):
+        distance = lax.axis_size(axis) // 2
+        while distance >= 1:
+            send, keep = halve(keep, other, axis, distance)
+            other = exchanged(send, axis, distance)
+            distance //= 2
+    shares = share(parts, keep, other, along)
+
+    up, down, shares = lax.optimization_barrier((up, down, shares))
+    column = lax.all_to_all(shares, "z", 0, 0)
     cells = volume_in.shape[3] * volume_in.shape[4] * devices
-    shares = share(parts, terms, 1.0 / math.sqrt(cells), copies)
-
-    up, down, shares = lax.optimization_barrier((up, down, shares))
-    mine = lax.all_to_all(shares, ("dp", "slab"), 0, 0)
+    shares = column_share(column, parts.shape[1], 1.0 / math.sqrt(cells), planar)
+    mine = lax.all_to_all(shares, ("x", "y"), 0, 0)
     count = lax.axis_size(SPACE)
     upward = [(i, i + 1) for i in range(count - 1)]
     from_below = lax.ppermute(up, SPACE, upward)
     from_above = lax.ppermute(down, SPACE, [(j, i) for i, j in upward])
     grad_input = merge(own, from_below, from_above, volume_in.shape[2:])
     mine, grad_input = lax.optimization_barrier((mine, grad_input))
-    other = lax.ppermute(mine, "core", swap)
-    bucket_sum, total_one, total_two = finish(core, mine, other, length, (c0, c1, c2))
+    other = exchanged(mine, "core", 1)
+    bucket_sum, total_one, total_two = finish(mine, other, length, along, across, (c0, c1, c2))
     return (
         grad_input[None, None],
         total_one.reshape(3, 3, 3, c0, c1),
@@ -445,8 +517,8 @@
 
 def solution(mesh):
     dp, space = (mesh.shape["dp"], mesh.shape["space"])
-    split = Mesh(mesh.devices.reshape(dp, space // 2, 2), EVERY)
-    volume = P("dp", SPACE, None, None, None)
+    split = Mesh(mesh.devices.reshape(dp // 2, 2, space // 2, 2), EVERY)
+    volume = P(("z", "x"), SPACE, None, None, None)
     in_specs = (volume, volume, volume, P(), P(), P(EVERY, None))
     out_specs = (volume, P(), P(), P())
     return jax.shard_map(

time: 75 us -> 76.4 us (1.019)
  starting transfers between devices: 23.3 us -> 31.9 us
  blocking collectives: 14.5 us -> 11.5 us
  Pallas kernels: 19.9 us -> 17.3 us
  waiting for transfers between devices: 13.3 us -> 12.4 us
    ppermute x2 -> x5, starting transfers between devices: 1.36 us -> 5.68 us  [exchanged(): lax.ppermute(value, axis, [(i, i ^ distance) for i in range(lax.axis_size...]
    ppermute x1, starting transfers between devices: 3.61 us -> 7.89 us  [per_device(): from_below = lax.ppermute(up, SPACE, upward)]
    ppermute x2 -> x5, waiting for transfers between devices: 0.61 us -> 4.67 us  [exchanged(): lax.ppermute(value, axis, [(i, i ^ distance) for i in range(lax.axis_size...]
    ppermute x1, waiting for transfers between devices: 4.64 us -> 1.41 us  [per_device(): from_below = lax.ppermute(up, SPACE, upward)]
    all_to_all x1, blocking collectives: 14.5 us -> 11.5 us  [per_device(): column = lax.all_to_all(shares, 'z', 0, 0)]
    all_to_all x2, waiting for transfers between devices: 2.76 us -> 0.01 us  [the longest x1 0.01 us: per_device(): lax.all_to_all(half.reshape(along * planar, -1, LANES), ('z', 'x', 'y'),...]
    pallas_call x1, Pallas kernels: 3.31 us -> 1.5 us  [pack(): pl.pallas_call(pack_kernel, out_shape=jax.ShapeDtypeStruct(((length + 2)...]
    ppermute x2, waiting for transfers between devices: 0.84 us -> 2.01 us  [halos(): return (lax.ppermute(value, SPACE, up), lax.ppermute(value, SPACE, down))]
  transfers between devices with their start and end apart: 8 -> 11, of which waited for: 5 -> 8; matrix products, arithmetic and copies ran while one was open for 0% -> 0% of each run, Pallas kernels for 20% -> 16%
where the time goes in v5:
time: 76.4 us; the launch traced here: 75.8 us
  starting transfers between devices  31.9 us (42%)
  Pallas kernels  17.3 us (23%)
  waiting for transfers between devices  12.4 us (16%)
  blocking collectives  11.5 us (15%)
  local copies, waits for them, and re-layouts  1.91 us (2%)
  between operations  0.78 us (1%)
    all_to_all x1, blocking collectives, per_device(): column = lax.all_to_all(shares, 'z', 0, 0)  11.5 us
    ppermute x1, starting transfers between devices, per_device(): from_below = lax.ppermute(up, SPACE, upward)  7.89 us
    pallas_call x1, Pallas kernels, compute(): vmem_call(compute_kernel, (jax.ShapeDtypeStruct((rows // 2, LANES), BF16)...  7.55 us
    ppermute x2, starting transfers between devices, halos(): return (lax.ppermute(value, SPACE, up), lax.ppermute(value, SPACE, down))  6.56 us
    all_to_all x1, starting transfers between devices, per_device(): lax.all_to_all(half.reshape(along * planar, -1, LANES), ('z', 'x', 'y'),...  6.22 us
    ppermute x5, starting transfers between devices, exchanged(): lax.ppermute(value, axis, [(i, i ^ distance) for i in range(lax.axis_size...  5.68 us
    ppermute x5, waiting for transfers between devices, exchanged(): lax.ppermute(value, axis, [(i, i ^ distance) for i in range(lax.axis_size...  4.67 us
    ppermute x1, waiting for transfers between devices, per_device(): from_above = lax.ppermute(down, SPACE, [(j, i) for i, j in upward])  4.36 us
  transfers between devices with their start and end apart: 11, of which 8 were waited for; matrix products, arithmetic and copies ran while one was open for 0% of the time, Pallas kernels for 16%

profile of v5, /device:TPU:1, one launch (start us, length us, event | category | flops | bytes accessed | tf_op | source)
XLA Modules:
  0.0 75.8 jit_solution(9273965377031788537)
XLA Ops:
  0.6 0.0 copy-start.1
  0.6 0.0 copy-start
  0.7 2.3 %shard_map.93 = bf16[2048,128]{1,0:T(8,128)(2,1)} custom-call(f32[4096,128]{1,0:T(8,128)} %bitcast.9), custom_call_target="tpu_custom_call" | custom-call | bytes 3145728 | tf_op jit(solution)/shard_map/pallas_call | solution.py:111
  3.0 0.1 collective-permute-start
  3.1 0.0 copy-done.1
  3.1 0.0 copy-start.2
  3.1 0.9 %copy-done.2 = bf16[1,1,16,64,128]{4,3,2,1,0:T(8,128)(2,1)S(1)} copy-done((bf16[1,1,16,64,128]{4,3,2,1,0:T(8,128)(2,1)S(1)}, bf16[1,1,16,64,128]{4,3,2,1,0:T(8,128)(2,1)}, u32[]{:S(2)}) %copy-start.2) | copy-done | bytes 262168
  4.0 1.5 %shard_map.94.pack_0 = bf16[3168,128]{1,0:T(8,128)(2,1)S(1)} custom-call(bf16[32,64,128]{2,1,0:T(8,128)(2,1)S(1)} %bitcast.11, bf16[16,64,128]{2,1,0:T(8,128)(2,1)S(1)} %bitcast.12), custom_call_target="tpu_custom_call" | custom-call | bytes 1048576 | tf_op jit(solution)/shard_map/pallas_call | solution.py:74
  5.5 0.0 copy-start.3
  5.6 0.0 copy-start.5
  5.6 0.0 collective-permute-done.other
  5.6 2.5 %collective-permute-start.2 = (bf16[3168,128]{1,0:T(8,128)(2,1)S(1)}, bf16[3168,128]{1,0:T(8,128)(2,1)}, u32[]{:S(2)}, u32[]{:S(2)}) collective-permute-start(bf16[3168,128]{1,0:T(8,128)(2,1)S(1)} %shard_map.94.pack_0), channel_id=1, source_target_pairs={{1,0},{2,1},{3,2},{5,4},{6,5},{7,6},{9,8},{10,9},{11,10},{13,12},{... | collective-permute-start | bytes 2433032 | tf_op jit(solution)/shard_map/ppermute | solution.py:467
  8.1 4.1 %collective-permute-start.1 = (bf16[3168,128]{1,0:T(8,128)(2,1)S(1)}, bf16[3168,128]{1,0:T(8,128)(2,1)}, u32[]{:S(2)}, u32[]{:S(2)}) collective-permute-start(bf16[3168,128]{1,0:T(8,128)(2,1)S(1)} %shard_map.94.pack_0), channel_id=1, source_target_pairs={{0,1},{1,2},{2,3},{4,5},{5,6},{6,7},{8,9},{9,10},{10,11},{12,13},{... | collective-permute-start | bytes 2433032 | tf_op jit(solution)/shard_map/ppermute | solution.py:467
  12.2 0.0 copy-done
  12.2 0.9 %shard_map.95 = bf16[2048,128]{1,0:T(8,128)(2,1)} custom-call(f32[4096,128]{1,0:T(8,128)S(1)} %bitcast.10, bf16[2048,128]{1,0:T(8,128)(2,1)S(1)} %collective-permute-done.other), custom_call_target="tpu_custom_call" | custom-call | bytes 2097152 | tf_op jit(solution)/shard_map/pallas_call | solution.py:136
  13.1 6.2 %all-to-all-start = ((bf16[16,128,128]{2,1,0:T(8,128)(2,1)}), bf16[16,128,128]{2,1,0:T(8,128)(2,1)S(1)}, u32[]{:S(2)}, u32[]{:S(2)}) async-start(bf16[16,128,128]{2,1,0:T(8,128)(2,1)} %bitcast.4), calls=%async_computation | async-start | bytes 1048576 | tf_op jit(solution)/shard_map/all_to_all | solution.py:483
  19.3 0.9 %collective-permute-done.2.pack_p = bf16[3168,128]{1,0:T(8,128)(2,1)} collective-permute-done((bf16[3168,128]{1,0:T(8,128)(2,1)S(1)}, bf16[3168,128]{1,0:T(8,128)(2,1)}, u32[]{:S(2)}, u32[]{:S(2)}) %collective-permute-start.2) | collective-permute-done | bytes 811040 | tf_op jit(solution)/shard_map/ppermute | solution.py:467
  20.3 1.1 %collective-permute-done.1.pack_m = bf16[3168,128]{1,0:T(8,128)(2,1)} collective-permute-done((bf16[3168,128]{1,0:T(8,128)(2,1)S(1)}, bf16[3168,128]{1,0:T(8,128)(2,1)}, u32[]{:S(2)}, u32[]{:S(2)}) %collective-permute-start.1) | collective-permute-done | bytes 811040 | tf_op jit(solution)/shard_map/ppermute | solution.py:467
  21.3 0.0 copy-done.3
  21.3 0.0 copy-done.5
  21.3 0.0 copy-start.4
  21.3 0.9 %copy-done.4 = bf16[3,3,3,32,32]{4,3,2,1,0:T(8,128)(2,1)S(1)} copy-done((bf16[3,3,3,32,32]{4,3,2,1,0:T(8,128)(2,1)S(1)}, bf16[3,3,3,32,32]{4,3,2,1,0:T(8,128)(2,1)}, u32[]{:S(2)}) %copy-start.4) | copy-done | bytes 55320
  22.3 7.5 %shard_map.96 = (bf16[256,128]{1,0:T(8,128)(2,1)S(1)}, f32[256,128]{1,0:T(8,128)S(1)}, f32[1024,128]{1,0:T(8,128)S(1)}, bf16[1024,128]{1,0:T(8,128)(2,1)S(1)}, bf16[1024,128]{1,0:T(8,128)(2,1)S(1)}) custom-call(bf16[3168,128]{1,0:T(8,128)(2,1)} %collective-permute-done.1.pack_m, bf16[3168,128]{1,0:T(8,128)(2,1)S(1)} %shard_map.94.pack_0, ...), custom_call_target="tpu_custom_call" | custom-call | flops 10000000000 | bytes 41943040 | tf_op jit(solution)/shard_map/pallas_call | solution.py:284
  29.8 0.1 collective-permute-start.3
  29.9 1.2 %collective-permute-done.3.refs_1_ = bf16[256,128]{1,0:T(8,128)(2,1)S(1)} collective-permute-done((bf16[256,128]{1,0:T(8,128)(2,1)S(1)}, bf16[256,128]{1,0:T(8,128)(2,1)S(1)}, u32[]{:S(2)}, u32[]{:S(2)}) %collective-permute-start.3) | collective-permute-done | bytes 65568 | tf_op jit(solution)/shard_map/ppermute | solution.py:170
  31.2 2.6 %collective-permute-start.4 = (bf16[128,128]{1,0:T(8,128)(2,1)S(1)}, bf16[128,128]{1,0:T(8,128)(2,1)S(1)}, u32[]{:S(2)}, u32[]{:S(2)}) collective-permute-start(bf16[128,128]{1,0:T(8,128)(2,1)S(1)} %get-tuple-element.40), channel_id=1, source_target_pairs={{0,2},{2,0},{1,3},{3,1},{4,6},{6,4},{5,7},{7,5},{8,10},{10,8},{9,1... | collective-permute-start | bytes 98312 | tf_op jit(solution)/shard_map/ppermute | solution.py:170
  33.7 1.3 %collective-permute-done.4.refs_1_ = bf16[128,128]{1,0:T(8,128)(2,1)S(1)} collective-permute-done((bf16[128,128]{1,0:T(8,128)(2,1)S(1)}, bf16[128,128]{1,0:T(8,128)(2,1)S(1)}, u32[]{:S(2)}, u32[]{:S(2)}) %collective-permute-start.4) | collective-permute-done | bytes 32800 | tf_op jit(solution)/shard_map/ppermute | solution.py:170
  35.1 2.9 %collective-permute-start.5 = (bf16[64,128]{1,0:T(8,128)(2,1)S(1)}, bf16[64,128]{1,0:T(8,128)(2,1)S(1)}, u32[]{:S(2)}, u32[]{:S(2)}) collective-permute-start(bf16[64,128]{1,0:T(8,128)(2,1)S(1)} %get-tuple-element.42), channel_id=1, source_target_pairs={{0,4},{4,0},{1,5},{5,1},{2,6},{6,2},{3,7},{7,3},{8,12},{12,8},{9,1... | collective-permute-start | bytes 49160 | tf_op jit(solution)/shard_map/ppermute | solution.py:170
  38.0 1.1 %collective-permute-done.5.other = bf16[64,128]{1,0:T(8,128)(2,1)S(1)} collective-permute-done((bf16[64,128]{1,0:T(8,128)(2,1)S(1)}, bf16[64,128]{1,0:T(8,128)(2,1)S(1)}, u32[]{:S(2)}, u32[]{:S(2)}) %collective-permute-start.5) | collective-permute-done | bytes 16416 | tf_op jit(solution)/shard_map/ppermute | solution.py:170
  39.1 0.0 all-to-all-done.parts
  39.1 0.1 shard_map.99
  39.2 11.5 %all_to_all.15.refs_0_ = bf16[4,192,128]{2,1,0:T(8,128)(2,1)S(1)} all-to-all(bf16[4,192,128]{2,1,0:T(8,128)(2,1)S(1)} %shard_map.99), channel_id=1, replica_groups=mesh['z'=4,'x'=2,'y'=2,'core'=2] {'z'}, dimensions={0} | all-to-all | bytes 393216 | tf_op jit(solution)/shard_map/all_to_all | solution.py:498
  50.8 0.9 %shard_map.100 = bf16[4,576,128]{2,1,0:T(8,128)(2,1)} custom-call(bf16[4,192,128]{2,1,0:T(8,128)(2,1)S(1)} %all_to_all.15.refs_0_), custom_call_target="tpu_custom_call" | custom-call | bytes 393216 | tf_op jit(solution)/shard_map/pallas_call | solution.py:372
  51.7 3.6 %all-to-all-start.2 = ((bf16[4,576,128]{2,1,0:T(8,128)(2,1)}), bf16[4,576,128]{2,1,0:T(8,128)(2,1)S(1)}, u32[]{:S(2)}, u32[]{:S(2)}) async-start(bf16[4,576,128]{2,1,0:T(8,128)(2,1)} %shard_map.100), calls=%async_computation.2 | async-start | bytes 1179648 | tf_op jit(solution)/shard_map/all_to_all | solution.py:501
  55.3 7.9 %collective-permute-start.6 = (bf16[1024,128]{1,0:T(8,128)(2,1)S(1)}, bf16[1024,128]{1,0:T(8,128)(2,1)S(1)}, u32[]{:S(2)}, u32[]{:S(2)}) collective-permute-start(bf16[1024,128]{1,0:T(8,128)(2,1)S(1)} %get-tuple-element.45), channel_id=1, source_target_pairs={{0,1},{1,2},{2,3},{4,5},{5,6},{6,7},{8,9},{9,10},{10,11},{12,13},{... | collective-permute-start | bytes 786440 | tf_op jit(solution)/shard_map/ppermute | solution.py:504
  63.2 1.9 %collective-permute-start.7 = (bf16[1024,128]{1,0:T(8,128)(2,1)S(1)}, bf16[1024,128]{1,0:T(8,128)(2,1)S(1)}, u32[]{:S(2)}, u32[]{:S(2)}) collective-permute-start(bf16[1024,128]{1,0:T(8,128)(2,1)S(1)} %get-tuple-element.46), channel_id=1, source_target_pairs={{1,0},{2,1},{3,2},{5,4},{6,5},{7,6},{9,8},{10,9},{11,10},{13,12},{... | collective-permute-start | bytes 786440 | tf_op jit(solution)/shard_map/ppermute | solution.py:505
  65.1 1.4 %collective-permute-done.6.from_below = bf16[1024,128]{1,0:T(8,128)(2,1)S(1)} collective-permute-done((bf16[1024,128]{1,0:T(8,128)(2,1)S(1)}, bf16[1024,128]{1,0:T(8,128)(2,1)S(1)}, u32[]{:S(2)}, u32[]{:S(2)}) %collective-permute-start.6) | collective-permute-done | bytes 262176 | tf_op jit(solution)/shard_map/ppermute | solution.py:504
  66.5 4.4 %collective-permute-done.7.from_above = bf16[1024,128]{1,0:T(8,128)(2,1)S(1)} collective-permute-done((bf16[1024,128]{1,0:T(8,128)(2,1)S(1)}, bf16[1024,128]{1,0:T(8,128)(2,1)S(1)}, u32[]{:S(2)}, u32[]{:S(2)}) %collective-permute-start.7) | collective-permute-done | bytes 262176 | tf_op jit(solution)/shard_map/ppermute | solution.py:505
  70.9 1.0 %shard_map.101 = bf16[16,64,128]{2,1,0:T(8,128)(2,1)} custom-call(f32[1024,128]{1,0:T(8,128)S(1)} %get-tuple-element.44.own, bf16[1024,128]{1,0:T(8,128)(2,1)S(1)} %collective-permute-done.6.from_below, bf16[1024,128]{1,0:T(8,128)(2,1)S(1)} %collective-permute-done.7.from_above), custom_call_target="tpu_custom_call" | custom-call | flops 262144 | bytes 1048576 | tf_op jit(solution)/shard_map/pallas_call | solution.py:325
  71.9 0.0 all-to-all-done.2.refs_0_
  71.9 0.0 collective-permute-start.8
  71.9 1.0 %shard_map.102.refs_2_ = f32[4096,128]{1,0:T(8,128)} custom-call(bf16[4,576,128]{2,1,0:T(8,128)(2,1)S(1)} %all-to-all-done.2.refs_0_), custom_call_target="tpu_custom_call" | custom-call | tf_op jit(solution)/shard_map/pallas_call | solution.py:440
  72.9 1.0 %collective-permute-done.8.refs_1_ = bf16[4,576,128]{2,1,0:T(8,128)(2,1)S(1)} collective-permute-done((bf16[4,576,128]{2,1,0:T(8,128)(2,1)S(1)}, bf16[4,576,128]{2,1,0:T(8,128)(2,1)S(1)}, u32[]{:S(2)}, u32[]{:S(2)}) %collective-permute-start.8) | collective-permute-done | bytes 589856 | tf_op jit(solution)/shard_map/ppermute | solution.py:170
  73.9 2.0 %shard_map.103 = (f32[4096,128]{1,0:T(8,128)}, f32[432,32]{1,0:T(8,128)}, f32[864,32]{1,0:T(8,128)}) custom-call(bf16[4,576,128]{2,1,0:T(8,128)(2,1)S(1)} %all-to-all-done.2.refs_0_, bf16[4,576,128]{2,1,0:T(8,128)(2,1)S(1)} %collective-permute-done.8.refs_1_, f32[4096,128]{1,0:T(8,128)} %shard_map.102.refs_2_), custom_call_target="tpu_custom_call", output_to_operand_aliasing={{0}: (2, {})} | custom-call | tf_op jit(solution)/shard_map/pallas_call | solution.py:448
  (2 shorter events, 0.0 us)
Async XLA Ops:
  0.6 2.5 %copy-start.1 = (bf16[1,1,32,64,128]{4,3,2,1,0:T(8,128)(2,1)S(1)}, bf16[1,1,32,64,128]{4,3,2,1,0:T(8,128)(2,1)}, u32[]{:S(2)}) copy-start(bf16[1,1,32,64,128]{4,3,2,1,0:T(8,128)(2,1)} %param.8) | copy-start | bytes 1572868
  0.6 11.5 %copy-start = (f32[1,524288]{1,0:T(1,128)S(1)}, f32[1,524288]{1,0:T(1,128)}, u32[]{:S(2)}) copy-start(f32[1,524288]{1,0:T(1,128)} %param.11) | copy-start | bytes 6291460
  3.0 2.6 %collective-permute-start = (bf16[2048,128]{1,0:T(8,128)(2,1)}, bf16[2048,128]{1,0:T(8,128)(2,1)S(1)}, u32[]{:S(2)}, u32[]{:S(2)}) collective-permute-start(bf16[2048,128]{1,0:T(8,128)(2,1)} %shard_map.93), channel_id=1, source_target_pairs={{0,1},{1,0},{2,3},{3,2},{4,5},{5,4},{6,7},{7,6},{8,9},{9,8},{10,11... | collective-permute-start | bytes 1572872 | tf_op jit(solution)/shard_map/ppermute | solution.py:170
  3.1 1.0 %copy-start.2 = (bf16[1,1,16,64,128]{4,3,2,1,0:T(8,128)(2,1)S(1)}, bf16[1,1,16,64,128]{4,3,2,1,0:T(8,128)(2,1)}, u32[]{:S(2)}) copy-start(bf16[1,1,16,64,128]{4,3,2,1,0:T(8,128)(2,1)} %param.6) | copy-start | bytes 786436
  5.5 15.8 %copy-start.3 = (bf16[1,1,32,64,128]{4,3,2,1,0:T(8,128)(2,1)S(1)}, bf16[1,1,32,64,128]{4,3,2,1,0:T(8,128)(2,1)}, u32[]{:S(2)}) copy-start(bf16[1,1,32,64,128]{4,3,2,1,0:T(8,128)(2,1)} %param.7) | copy-start | bytes 1572868
  5.6 15.8 %copy-start.5 = (bf16[3,3,3,16,32]{4,3,2,1,0:T(8,128)(2,1)S(1)}, bf16[3,3,3,16,32]{4,3,2,1,0:T(8,128)(2,1)}, u32[]{:S(2)}) copy-start(bf16[3,3,3,16,32]{4,3,2,1,0:T(8,128)(2,1)} %one.1) | copy-start | bytes 82948
  5.6 14.7 %collective-permute-start.2 = (bf16[3168,128]{1,0:T(8,128)(2,1)S(1)}, bf16[3168,128]{1,0:T(8,128)(2,1)}, u32[]{:S(2)}, u32[]{:S(2)}) collective-permute-start(bf16[3168,128]{1,0:T(8,128)(2,1)S(1)} %shard_map.94.pack_0), channel_id=1, source_target_pairs={{1,0},{2,1},{3,2},{5,4},{6,5},{7,6},{9,8},{10,9},{11,10},{13,12},{... | collective-permute-start | bytes 2433032 | tf_op jit(solution)/shard_map/ppermute | solution.py:467
  8.1 13.2 %collective-permute-start.1 = (bf16[3168,128]{1,0:T(8,128)(2,1)S(1)}, bf16[3168,128]{1,0:T(8,128)(2,1)}, u32[]{:S(2)}, u32[]{:S(2)}) collective-permute-start(bf16[3168,128]{1,0:T(8,128)(2,1)S(1)} %shard_map.94.pack_0), channel_id=1, source_target_pairs={{0,1},{1,2},{2,3},{4,5},{5,6},{6,7},{8,9},{9,10},{10,11},{12,13},{... | collective-permute-start | bytes 2433032 | tf_op jit(solution)/shard_map/ppermute | solution.py:467
  13.1 26.0 %all-to-all-start = ((bf16[16,128,128]{2,1,0:T(8,128)(2,1)}), bf16[16,128,128]{2,1,0:T(8,128)(2,1)S(1)}, u32[]{:S(2)}, u32[]{:S(2)}) async-start(bf16[16,128,128]{2,1,0:T(8,128)(2,1)} %bitcast.4), calls=%async_computation | async-start | bytes 1048576 | tf_op jit(solution)/shard_map/all_to_all | solution.py:483
  21.3 0.9 %copy-start.4 = (bf16[3,3,3,32,32]{4,3,2,1,0:T(8,128)(2,1)S(1)}, bf16[3,3,3,32,32]{4,3,2,1,0:T(8,128)(2,1)}, u32[]{:S(2)}) copy-start(bf16[3,3,3,32,32]{4,3,2,1,0:T(8,128)(2,1)} %two.1) | copy-start | bytes 165892
  29.8 1.3 %collective-permute-start.3 = (bf16[256,128]{1,0:T(8,128)(2,1)S(1)}, bf16[256,128]{1,0:T(8,128)(2,1)S(1)}, u32[]{:S(2)}, u32[]{:S(2)}) collective-permute-start(bf16[256,128]{1,0:T(8,128)(2,1)S(1)} %get-tuple-element.38), channel_id=1, source_target_pairs={{0,1},{1,0},{2,3},{3,2},{4,5},{5,4},{6,7},{7,6},{8,9},{9,8},{10,11... | collective-permute-start | bytes 196616 | tf_op jit(solution)/shard_map/ppermute | solution.py:170
  31.2 3.9 %collective-permute-start.4 = (bf16[128,128]{1,0:T(8,128)(2,1)S(1)}, bf16[128,128]{1,0:T(8,128)(2,1)S(1)}, u32[]{:S(2)}, u32[]{:S(2)}) collective-permute-start(bf16[128,128]{1,0:T(8,128)(2,1)S(1)} %get-tuple-element.40), channel_id=1, source_target_pairs={{0,2},{2,0},{1,3},{3,1},{4,6},{6,4},{5,7},{7,5},{8,10},{10,8},{9,1... | collective-permute-start | bytes 98312 | tf_op jit(solution)/shard_map/ppermute | solution.py:170
  35.1 4.0 %collective-permute-start.5 = (bf16[64,128]{1,0:T(8,128)(2,1)S(1)}, bf16[64,128]{1,0:T(8,128)(2,1)S(1)}, u32[]{:S(2)}, u32[]{:S(2)}) collective-permute-start(bf16[64,128]{1,0:T(8,128)(2,1)S(1)} %get-tuple-element.42), channel_id=1, source_target_pairs={{0,4},{4,0},{1,5},{5,1},{2,6},{6,2},{3,7},{7,3},{8,12},{12,8},{9,1... | collective-permute-start | bytes 49160 | tf_op jit(solution)/shard_map/ppermute | solution.py:170
  51.7 20.2 %all-to-all-start.2 = ((bf16[4,576,128]{2,1,0:T(8,128)(2,1)}), bf16[4,576,128]{2,1,0:T(8,128)(2,1)S(1)}, u32[]{:S(2)}, u32[]{:S(2)}) async-start(bf16[4,576,128]{2,1,0:T(8,128)(2,1)} %shard_map.100), calls=%async_computation.2 | async-start | bytes 1179648 | tf_op jit(solution)/shard_map/all_to_all | solution.py:501
  55.3 11.2 %collective-permute-start.6 = (bf16[1024,128]{1,0:T(8,128)(2,1)S(1)}, bf16[1024,128]{1,0:T(8,128)(2,1)S(1)}, u32[]{:S(2)}, u32[]{:S(2)}) collective-permute-start(bf16[1024,128]{1,0:T(8,128)(2,1)S(1)} %get-tuple-element.45), channel_id=1, source_target_pairs={{0,1},{1,2},{2,3},{4,5},{5,6},{6,7},{8,9},{9,10},{10,11},{12,13},{... | collective-permute-start | bytes 786440 | tf_op jit(solution)/shard_map/ppermute | solution.py:504
  63.2 7.7 %collective-permute-start.7 = (bf16[1024,128]{1,0:T(8,128)(2,1)S(1)}, bf16[1024,128]{1,0:T(8,128)(2,1)S(1)}, u32[]{:S(2)}, u32[]{:S(2)}) collective-permute-start(bf16[1024,128]{1,0:T(8,128)(2,1)S(1)} %get-tuple-element.46), channel_id=1, source_target_pairs={{1,0},{2,1},{3,2},{5,4},{6,5},{7,6},{9,8},{10,9},{11,10},{13,12},{... | collective-permute-start | bytes 786440 | tf_op jit(solution)/shard_map/ppermute | solution.py:505
  71.9 2.0 %collective-permute-start.8 = (bf16[4,576,128]{2,1,0:T(8,128)(2,1)S(1)}, bf16[4,576,128]{2,1,0:T(8,128)(2,1)S(1)}, u32[]{:S(2)}, u32[]{:S(2)}) collective-permute-start(bf16[4,576,128]{2,1,0:T(8,128)(2,1)S(1)} %all-to-all-done.2.refs_0_), channel_id=1, source_target_pairs={{0,1},{1,0},{2,3},{3,2},{4,5},{5,4},{6,7},{7,6},{8,9},{9,8},{10,11... | collective-permute-start | bytes 1769480 | tf_op jit(solution)/shard_map/ppermute | solution.py:170

commit v6 on v4

--- a/solution.py
+++ b/solution.py
@@ -8,6 +8,7 @@
 from jax.sharding import Mesh, PartitionSpec as P
 
 SPACE = ("slab", "core")
+SAME = ("dp", "slab")
 EVERY = ("dp", "slab", "core")
 GROUP = 8
 LANES = 128
@@ -81,6 +82,7 @@
             pltpu.VMEM((vol.shape[0] * length, width), F32),
             pltpu.SemaphoreType.DMA((pieces,)),
         ],
+        compiler_params=pltpu.CompilerParams(vmem_limit_bytes=24 * 2**20),
         cost_estimate=pl.CostEstimate(flops=0, bytes_accessed=4 * cot.size, transcendentals=0),
     )(cot, vol)
 
@@ -98,39 +100,75 @@
     return [(pl.ds(n * step, step), copy) for n, copy in enumerate(copies)]
 
 
-def cast_kernel(core, src, out, buffer, sems):
-    for rows, copy in fetched_chunks(src, (1 - core[0]) * out.shape[0], buffer, sems):
+def cast_kernel(src, out, buffer, sems):
+    start = (1 - lax.axis_index("core")) * out.shape[0]
+    for rows, copy in fetched_chunks(src, start, buffer, sems):
         copy.wait()
         out[rows, :] = buffer[rows, :].astype(out.dtype)
 
 
-def add_kernel(core, src, other, out, buffer, more, sems, more_sems):
-    chunks = fetched_chunks(src, core[0] * out.shape[0], buffer, sems)
-    for (rows, copy), (_, second) in zip(chunks, fetched_chunks(other, 0, more, more_sems)):
-        copy.wait()
-        second.wait()
-        out[rows, :] = (buffer[rows, :] + more[rows, :].astype(F32)).astype(out.dtype)
-
-
-def half_call(body, core, value, others, chunks=8):
+def cast(value, chunks=8):
     half = (value.shape[0] // 2, LANES)
-    source = pl.BlockSpec(memory_space=pltpu.HBM)
     return pl.pallas_call(
-        body,
+        cast_kernel,
         out_shape=jax.ShapeDtypeStruct(half, BF16),
-        in_specs=[pl.BlockSpec(memory_space=pltpu.SMEM)] + [source] * (1 + len(others)),
+        in_specs=[pl.BlockSpec(memory_space=pltpu.HBM)],
         out_specs=pl.BlockSpec(memory_space=pltpu.VMEM),
-        scratch_shapes=[pltpu.VMEM(half, F32)]
-        + [pltpu.VMEM(half, BF16) for _ in others]
-        + [pltpu.SemaphoreType.DMA((chunks,)) for _ in range(1 + len(others))],
+        scratch_shapes=[pltpu.VMEM(half, F32), pltpu.SemaphoreType.DMA((chunks,))],
         cost_estimate=pl.CostEstimate(flops=0, bytes_accessed=6 * value.size, transcendentals=0),
-    )(core, value, *others)
+    )(value)
+
+
+def add_kernel(src, other, out):
+    rows = out.shape[0]
+    step = rows // 8
+    start = lax.axis_index("core") * rows
+
+    def add(n, carry):
+        at = pl.ds(pl.multiple_of(n * step, 16), step)
+        own = src[pl.ds(pl.multiple_of(start + n * step, 16), step), :]
+        out[at, :] = (own + other[at, :].astype(F32)).astype(out.dtype)
+        return carry
+
+    lax.fori_loop(0, 8, add, 0)
+
+
+def add(value, other):
+    return vmem_call(
+        add_kernel,
+        jax.ShapeDtypeStruct(other.shape, BF16),
+        (),
+        pl.CostEstimate(flops=0, bytes_accessed=4 * value.size, transcendentals=0),
+    )(value, other)
+
+
+def split_to(total, mine, send, keep):
+    half = total.shape[0] // 2
+    keep[...] = total[pl.ds(pl.multiple_of(mine * half, 16), half), :]
+    send[...] = total[pl.ds(pl.multiple_of((1 - mine) * half, 16), half), :].astype(send.dtype)
+
+
+def pair_kernel(keep, other, out):
+    out[...] = (keep[...] + other[...].astype(F32)).astype(out.dtype)
+
+
+def pair_sum(keep, other):
+    return vmem_call(
+        pair_kernel,
+        jax.ShapeDtypeStruct(other.shape, BF16),
+        (),
+        pl.CostEstimate(flops=0, bytes_accessed=8 * keep.size, transcendentals=0),
+    )(keep, other)
+
+
+def swapped(value):
+    return lax.ppermute(value, "core", [(0, 1), (1, 0)])
 
 
 def compute_kernel(
     pack_m, pack_0, pack_p, act, two, one,
-    terms, own, up, down,
-    flat, acts, pres, w_two, w_one, acc_two, acc_one,
+    send, keep, own, up, down,
+    terms, flat, acts, pres, w_two, w_one, acc_two, acc_one,
 ):
     c1, length, _ = act.shape
     c2, c0 = (two.shape[4], one.shape[3])
@@ -216,9 +254,10 @@
     blocks = -(-width // LANES)
     for block in range(blocks):
         part = two[:, block * LANES : min(width, (block + 1) * LANES)]
-        terms[block * rows : (block + 1) * rows, 0 : part.shape[1]] = part.astype(terms.dtype)
+        terms[block * rows : (block + 1) * rows, 0 : part.shape[1]] = part
     one = acc_one[...]
-    terms[blocks * rows : blocks * rows + one.shape[0], 0 : one.shape[1]] = one.astype(terms.dtype)
+    terms[blocks * rows : blocks * rows + one.shape[0], 0 : one.shape[1]] = one
+    split_to(terms, lax.axis_index("core"), send, keep)
 
 
 def vmem_call(body, out_shape, scratch=(), cost=None, limit=24 * 2**20):
@@ -240,12 +279,14 @@
     return vmem_call(
         compute_kernel,
         (
-            jax.ShapeDtypeStruct((rows, LANES), BF16),
+            jax.ShapeDtypeStruct((rows // 2, LANES), BF16),
+            jax.ShapeDtypeStruct((rows // 2, LANES), F32),
             jax.ShapeDtypeStruct(plane, F32),
             jax.ShapeDtypeStruct(plane, BF16),
             jax.ShapeDtypeStruct(plane, BF16),
         ),
         (
+            pltpu.VMEM((rows, LANES), F32),
             pltpu.VMEM((c1 * length, width), F32),
             pltpu.VMEM((c1 * length, width), BF16),
             pltpu.VMEM(((length + 2) * 3 * c1, width), BF16),
@@ -322,21 +363,21 @@
     return sent
 
 
-def start_kernel(height, core, mine, bucket, buffer, sems):
-    for copy in place(mine, height, core[0], bucket, buffer, sems):
+def start_kernel(height, mine, bucket, buffer, sems):
+    for copy in place(mine, height, lax.axis_index("core"), bucket, buffer, sems):
         copy.wait()
 
 
-def finish_kernel(sizes, height, core, mine, other, partial, bucket, out_one, out_two, raw, buffer, sems):
+def finish_kernel(sizes, height, mine, other, partial, bucket, out_one, out_two, raw, buffer, sems):
     c0, c1, c2 = sizes
     copies, rows, _ = mine.shape
     extra = rows - height
-    me = core[0]
+    me = lax.axis_index("core")
     sent = place(other, height, 1 - me, bucket, buffer, sems)
 
     def unpack(q, carry):
         for source, which in ((mine, me), (other, 1 - me)):
-            at = pl.multiple_of((2 * q + which) * extra, 8)
+            at = pl.multiple_of((which * copies + q) * extra, 8)
             raw[pl.ds(at, extra), :] = source[q, height:rows, :].astype(F32)
         return carry
 
@@ -358,12 +399,12 @@
         copy.wait()
 
 
-def finish(core, mine, other, length, sizes):
+def finish(mine, other, length, sizes):
     c0, c1, c2 = sizes
     copies, rows, _ = mine.shape
     height = length // LANES // (2 * copies)
     spec = pl.BlockSpec(memory_space=pltpu.VMEM)
-    scalar, remote = (pl.BlockSpec(memory_space=pltpu.SMEM), pl.BlockSpec(memory_space=pltpu.HBM))
+    remote = pl.BlockSpec(memory_space=pltpu.HBM)
     whole = jax.ShapeDtypeStruct((length // LANES, LANES), F32)
     chunks = 4
     scratch = [
@@ -374,11 +415,11 @@
     partial = pl.pallas_call(
         lambda *refs: start_kernel(height, *refs),
         out_shape=whole,
-        in_specs=[scalar, spec],
+        in_specs=[spec],
         out_specs=remote,
         scratch_shapes=scratch,
         compiler_params=params,
-    )(core, mine)
+    )(mine)
     return pl.pallas_call(
         lambda *refs: finish_kernel(sizes, height, *refs),
         out_shape=(
@@ -386,12 +427,12 @@
             jax.ShapeDtypeStruct((27 * c0, c1), F32),
             jax.ShapeDtypeStruct((27 * c1, c2), F32),
         ),
-        in_specs=[scalar, spec, spec, remote],
+        in_specs=[spec, spec, remote],
         out_specs=(remote, spec, spec),
         scratch_shapes=[pltpu.VMEM((2 * copies * (rows - height), LANES), F32)] + scratch,
-        input_output_aliases={3: 0},
+        input_output_aliases={2: 0},
         compiler_params=params,
-    )(core, mine, other, partial)
+    )(mine, other, partial)
 
 
 def halos(value):
@@ -403,38 +444,36 @@
 
 def per_device(volume_in, hidden_act, out_cot, kernel_one, kernel_two, grad_bucket):
     c0, c1, c2 = (volume_in.shape[2], hidden_act.shape[2], out_cot.shape[2])
-    devices, copies = (lax.axis_size(EVERY), lax.axis_size(("dp", "slab")))
+    devices, copies = (lax.axis_size(EVERY), lax.axis_size(SAME))
     length = grad_bucket.shape[1]
-    core = lax.axis_index("core").astype(jnp.int32).reshape(1)
-    swap = [(0, 1), (1, 0)]
     bucket = grad_bucket.reshape(length // LANES, LANES)
-    send = half_call(cast_kernel, core, bucket, [])
+    send = cast(bucket)
     cot, vol, send = lax.optimization_barrier((out_cot[0, 0], volume_in[0, 0], send))
     packed = pack(cot, vol)
-    other, packed = lax.optimization_barrier((lax.ppermute(send, "core", swap), packed))
+    other, packed = lax.optimization_barrier((swapped(send), packed))
     below, above = halos(packed)
-    half = half_call(add_kernel, core, bucket, [other])
+    half = add(bucket, other)
     act, half = lax.optimization_barrier((hidden_act[0, 0], half))
-    parts = lax.all_to_all(half.reshape(copies, -1, LANES), ("dp", "slab"), 0, 0)
+    parts = lax.all_to_all(half.reshape(copies, -1, LANES), SAME, 0, 0)
 
     used = -(-9 * c2 // LANES) * 3 * c1 + 9 * c0
     rows = ceil_to(used, 16 * devices)
-    terms, own, up, down = compute((below, packed, above), act, kernel_two, kernel_one, rows)
+    send, keep, own, up, down = compute((below, packed, above), act, kernel_two, kernel_one, rows)
+    terms = pair_sum(keep, swapped(send))
     terms, parts = lax.optimization_barrier((terms, parts))
-    terms = lax.all_to_all(terms.reshape(devices, rows // devices, LANES), EVERY, 0, 0)
+    terms = lax.all_to_all(terms.reshape(copies, -1, LANES), SAME, 0, 0)
     cells = volume_in.shape[3] * volume_in.shape[4] * devices
     shares = share(parts, terms, 1.0 / math.sqrt(cells), copies)
 
     up, down, shares = lax.optimization_barrier((up, down, shares))
-    mine = lax.all_to_all(shares, ("dp", "slab"), 0, 0)
+    mine = lax.all_to_all(shares, SAME, 0, 0)
     count = lax.axis_size(SPACE)
     upward = [(i, i + 1) for i in range(count - 1)]
     from_below = lax.ppermute(up, SPACE, upward)
     from_above = lax.ppermute(down, SPACE, [(j, i) for i, j in upward])
     grad_input = merge(own, from_below, from_above, volume_in.shape[2:])
     mine, grad_input = lax.optimization_barrier((mine, grad_input))
-    other = lax.ppermute(mine, "core", swap)
-    bucket_sum, total_one, total_two = finish(core, mine, other, length, (c0, c1, c2))
+    bucket_sum, total_one, total_two = finish(mine, swapped(mine), length, (c0, c1, c2))
     return (
         grad_input[None, None],
         total_one.reshape(3, 3, 3, c0, c1),

time: 75 us -> 74.3 us (level)
  Pallas kernels: 19.9 us -> 17.1 us
  blocking collectives: 14.5 us -> 16.5 us
  starting transfers between devices: 23.3 us -> 25.1 us
  waiting for transfers between devices: 13.3 us -> 12 us
    all_to_all x2, waiting for transfers between devices: 2.76 us -> 0.47 us  [the longest x1 0.47 us: per_device(): parts = lax.all_to_all(half.reshape(copies, -1, LANES), SAME, 0, 0)]
    all_to_all x1, blocking collectives: 14.5 us -> 16.5 us  [per_device(): terms = lax.all_to_all(terms.reshape(copies, -1, LANES), SAME, 0, 0)]
    pallas_call x1, Pallas kernels: 3.31 us -> 1.5 us  [pack(): pl.pallas_call(pack_kernel, out_shape=jax.ShapeDtypeStruct(((length + 2)...]
    ppermute x1, starting transfers between devices: 3.61 us -> 4.99 us  [per_device(): from_below = lax.ppermute(up, SPACE, upward)]
    ppermute x2 -> x3, waiting for transfers between devices: 0.61 us -> 1.85 us  [swapped(): return lax.ppermute(value, 'core', [(0, 1), (1, 0)])]
    ppermute x2, waiting for transfers between devices: 0.84 us -> 2.01 us  [halos(): return (lax.ppermute(value, SPACE, up), lax.ppermute(value, SPACE, down))]
    pallas_call x3 -> x4, Pallas kernels: 11.7 us -> 10.8 us  [the longest x1 7.55 us: compute(): vmem_call(compute_kernel, (jax.ShapeDtypeStruct((rows // 2, LANES), BF16)...]
    ppermute x1, waiting for transfers between devices: 4.64 us -> 3.74 us  [per_device(): from_below = lax.ppermute(up, SPACE, upward)]
  transfers between devices with their start and end apart: 8 -> 9, of which waited for: 5 -> 7; matrix products, arithmetic and copies ran while one was open for 0% -> 0% of each run, Pallas kernels for 20% -> 16%
where the time goes in v6:
time: 74.3 us; the launch traced here: 73.5 us
  starting transfers between devices  25.1 us (34%)
  Pallas kernels  17.1 us (23%)
  blocking collectives  16.5 us (22%)
  waiting for transfers between devices  12 us (16%)
  local copies, waits for them, and re-layouts  1.91 us (3%)
  between operations  0.77 us (1%)
    all_to_all x1, blocking collectives, per_device(): terms = lax.all_to_all(terms.reshape(copies, -1, LANES), SAME, 0, 0)  16.5 us
    pallas_call x1, Pallas kernels, compute(): vmem_call(compute_kernel, (jax.ShapeDtypeStruct((rows // 2, LANES), BF16)...  7.55 us
    ppermute x2, starting transfers between devices, halos(): return (lax.ppermute(value, SPACE, up), lax.ppermute(value, SPACE, down))  6.56 us
    all_to_all x1, starting transfers between devices, per_device(): parts = lax.all_to_all(half.reshape(copies, -1, LANES), SAME, 0, 0)  6.22 us
    ppermute x1, starting transfers between devices, per_device(): from_below = lax.ppermute(up, SPACE, upward)  4.99 us
    ppermute x1, waiting for transfers between devices, per_device(): from_above = lax.ppermute(down, SPACE, [(j, i) for i, j in upward])  3.9 us
    ppermute x1, waiting for transfers between devices, per_device(): from_below = lax.ppermute(up, SPACE, upward)  3.74 us
    all_to_all x1, starting transfers between devices, per_device(): mine = lax.all_to_all(shares, SAME, 0, 0)  3.58 us
  transfers between devices with their start and end apart: 9, of which 7 were waited for; matrix products, arithmetic and copies ran while one was open for 0% of the time, Pallas kernels for 16%

profile of v6, /device:TPU:1, one launch (start us, length us, event | category | flops | bytes accessed | tf_op | source)
XLA Modules:
  0.0 73.5 jit_solution(11951536646087347456)
XLA Ops:
  0.6 0.0 copy-start.1
  0.6 0.0 copy-start
  0.7 2.3 %shard_map.93 = bf16[2048,128]{1,0:T(8,128)(2,1)} custom-call(f32[4096,128]{1,0:T(8,128)} %bitcast.10), custom_call_target="tpu_custom_call" | custom-call | bytes 3145728 | tf_op jit(solution)/shard_map/pallas_call | solution.py:112
  3.0 0.1 collective-permute-start
  3.1 0.0 copy-done.1
  3.1 0.0 copy-start.2
  3.1 0.9 %copy-done.2 = bf16[1,1,16,64,128]{4,3,2,1,0:T(8,128)(2,1)S(1)} copy-done((bf16[1,1,16,64,128]{4,3,2,1,0:T(8,128)(2,1)S(1)}, bf16[1,1,16,64,128]{4,3,2,1,0:T(8,128)(2,1)}, u32[]{:S(2)}) %copy-start.2) | copy-done | bytes 262168
  4.0 1.5 %shard_map.94.pack_0 = bf16[3168,128]{1,0:T(8,128)(2,1)S(1)} custom-call(bf16[32,64,128]{2,1,0:T(8,128)(2,1)S(1)} %bitcast.12, bf16[16,64,128]{2,1,0:T(8,128)(2,1)S(1)} %bitcast.13), custom_call_target="tpu_custom_call" | custom-call | bytes 1048576 | tf_op jit(solution)/shard_map/pallas_call | solution.py:75
  5.5 0.0 copy-start.3
  5.6 0.0 copy-start.5
  5.6 0.0 collective-permute-done.other
  5.6 2.5 %collective-permute-start.2 = (bf16[3168,128]{1,0:T(8,128)(2,1)S(1)}, bf16[3168,128]{1,0:T(8,128)(2,1)}, u32[]{:S(2)}, u32[]{:S(2)}) collective-permute-start(bf16[3168,128]{1,0:T(8,128)(2,1)S(1)} %shard_map.94.pack_0), channel_id=1, source_target_pairs={{1,0},{2,1},{3,2},{5,4},{6,5},{7,6},{9,8},{10,9},{11,10},{13,12},{... | collective-permute-start | bytes 2433032 | tf_op jit(solution)/shard_map/ppermute | solution.py:442
  8.1 4.1 %collective-permute-start.1 = (bf16[3168,128]{1,0:T(8,128)(2,1)S(1)}, bf16[3168,128]{1,0:T(8,128)(2,1)}, u32[]{:S(2)}, u32[]{:S(2)}) collective-permute-start(bf16[3168,128]{1,0:T(8,128)(2,1)S(1)} %shard_map.94.pack_0), channel_id=1, source_target_pairs={{0,1},{1,2},{2,3},{4,5},{5,6},{6,7},{8,9},{9,10},{10,11},{12,13},{... | collective-permute-start | bytes 2433032 | tf_op jit(solution)/shard_map/ppermute | solution.py:442
  12.2 0.0 copy-done
  12.2 0.9 %shard_map.95 = bf16[2048,128]{1,0:T(8,128)(2,1)} custom-call(f32[4096,128]{1,0:T(8,128)S(1)} %bitcast.11, bf16[2048,128]{1,0:T(8,128)(2,1)S(1)} %collective-permute-done.other), custom_call_target="tpu_custom_call" | custom-call | bytes 2097152 | tf_op jit(solution)/shard_map/pallas_call | solution.py:137
  13.1 6.2 %all-to-all-start = ((bf16[16,128,128]{2,1,0:T(8,128)(2,1)}), bf16[16,128,128]{2,1,0:T(8,128)(2,1)S(1)}, u32[]{:S(2)}, u32[]{:S(2)}) async-start(bf16[16,128,128]{2,1,0:T(8,128)(2,1)} %bitcast.4), calls=%async_computation | async-start | bytes 1048576 | tf_op jit(solution)/shard_map/all_to_all | solution.py:457
  19.3 0.9 %collective-permute-done.2.pack_p = bf16[3168,128]{1,0:T(8,128)(2,1)} collective-permute-done((bf16[3168,128]{1,0:T(8,128)(2,1)S(1)}, bf16[3168,128]{1,0:T(8,128)(2,1)}, u32[]{:S(2)}, u32[]{:S(2)}) %collective-permute-start.2) | collective-permute-done | bytes 811040 | tf_op jit(solution)/shard_map/ppermute | solution.py:442
  20.3 1.1 %collective-permute-done.1.pack_m = bf16[3168,128]{1,0:T(8,128)(2,1)} collective-permute-done((bf16[3168,128]{1,0:T(8,128)(2,1)S(1)}, bf16[3168,128]{1,0:T(8,128)(2,1)}, u32[]{:S(2)}, u32[]{:S(2)}) %collective-permute-start.1) | collective-permute-done | bytes 811040 | tf_op jit(solution)/shard_map/ppermute | solution.py:442
  21.3 0.0 copy-done.3
  21.3 0.0 copy-done.5
  21.3 0.0 copy-start.4
  21.3 0.9 %copy-done.4 = bf16[3,3,3,32,32]{4,3,2,1,0:T(8,128)(2,1)S(1)} copy-done((bf16[3,3,3,32,32]{4,3,2,1,0:T(8,128)(2,1)S(1)}, bf16[3,3,3,32,32]{4,3,2,1,0:T(8,128)(2,1)}, u32[]{:S(2)}) %copy-start.4) | copy-done | bytes 55320
  22.3 7.5 %shard_map.96 = (bf16[256,128]{1,0:T(8,128)(2,1)S(1)}, f32[256,128]{1,0:T(8,128)S(1)}, f32[1024,128]{1,0:T(8,128)S(1)}, bf16[1024,128]{1,0:T(8,128)(2,1)S(1)}, bf16[1024,128]{1,0:T(8,128)(2,1)S(1)}) custom-call(bf16[3168,128]{1,0:T(8,128)(2,1)} %collective-permute-done.1.pack_m, bf16[3168,128]{1,0:T(8,128)(2,1)S(1)} %shard_map.94.pack_0, ...), custom_call_target="tpu_custom_call" | custom-call | flops 10000000000 | bytes 41943040 | tf_op jit(solution)/shard_map/pallas_call | solution.py:279
  29.8 0.1 collective-permute-start.3
  29.9 1.2 %collective-permute-done.3.other = bf16[256,128]{1,0:T(8,128)(2,1)S(1)} collective-permute-done((bf16[256,128]{1,0:T(8,128)(2,1)S(1)}, bf16[256,128]{1,0:T(8,128)(2,1)S(1)}, u32[]{:S(2)}, u32[]{:S(2)}) %collective-permute-start.3) | collective-permute-done | bytes 65568 | tf_op jit(solution)/shard_map/ppermute | solution.py:165
  31.2 0.5 all-to-all-done.refs_0_
  31.6 16.5 %all_to_all.15.refs_1_ = bf16[16,16,128]{2,1,0:T(8,128)(2,1)S(1)} all-to-all(bf16[16,16,128]{2,1,0:T(8,128)(2,1)S(1)} %bitcast.14), channel_id=1, replica_groups=mesh['dp'=8,'slab'=2,'core'=2] {'dp','slab'}, dimensions={0} | all-to-all | bytes 131072 | tf_op jit(solution)/shard_map/all_to_all | solution.py:464
  48.2 1.0 %shard_map.98 = bf16[16,144,128]{2,1,0:T(8,128)(2,1)} custom-call(bf16[16,128,128]{2,1,0:T(8,128)(2,1)S(1)} %all-to-all-done.refs_0_, bf16[16,16,128]{2,1,0:T(8,128)(2,1)S(1)} %all_to_all.15.refs_1_), custom_call_target="tpu_custom_call" | custom-call | flops 262144 | bytes 786432 | tf_op jit(solution)/shard_map/pallas_call | solution.py:343
  49.2 3.6 %all-to-all-start.2 = ((bf16[16,144,128]{2,1,0:T(8,128)(2,1)}), bf16[16,144,128]{2,1,0:T(8,128)(2,1)S(1)}, u32[]{:S(2)}, u32[]{:S(2)}) async-start(bf16[16,144,128]{2,1,0:T(8,128)(2,1)} %shard_map.98), calls=%async_computation.2 | async-start | bytes 1179648 | tf_op jit(solution)/shard_map/all_to_all | solution.py:469
  52.8 5.0 %collective-permute-start.4 = (bf16[1024,128]{1,0:T(8,128)(2,1)S(1)}, bf16[1024,128]{1,0:T(8,128)(2,1)S(1)}, u32[]{:S(2)}, u32[]{:S(2)}) collective-permute-start(bf16[1024,128]{1,0:T(8,128)(2,1)S(1)} %get-tuple-element.41), channel_id=1, source_target_pairs={{0,1},{1,2},{2,3},{4,5},{5,6},{6,7},{8,9},{9,10},{10,11},{12,13},{... | collective-permute-start | bytes 786440 | tf_op jit(solution)/shard_map/ppermute | solution.py:472
  57.8 1.9 %collective-permute-start.5 = (bf16[1024,128]{1,0:T(8,128)(2,1)S(1)}, bf16[1024,128]{1,0:T(8,128)(2,1)S(1)}, u32[]{:S(2)}, u32[]{:S(2)}) collective-permute-start(bf16[1024,128]{1,0:T(8,128)(2,1)S(1)} %get-tuple-element.42), channel_id=1, source_target_pairs={{1,0},{2,1},{3,2},{5,4},{6,5},{7,6},{9,8},{10,9},{11,10},{13,12},{... | collective-permute-start | bytes 786440 | tf_op jit(solution)/shard_map/ppermute | solution.py:473
  59.7 3.7 %collective-permute-done.4.from_below = bf16[1024,128]{1,0:T(8,128)(2,1)S(1)} collective-permute-done((bf16[1024,128]{1,0:T(8,128)(2,1)S(1)}, bf16[1024,128]{1,0:T(8,128)(2,1)S(1)}, u32[]{:S(2)}, u32[]{:S(2)}) %collective-permute-start.4) | collective-permute-done | bytes 262176 | tf_op jit(solution)/shard_map/ppermute | solution.py:472
  63.4 3.9 %collective-permute-done.5.from_above = bf16[1024,128]{1,0:T(8,128)(2,1)S(1)} collective-permute-done((bf16[1024,128]{1,0:T(8,128)(2,1)S(1)}, bf16[1024,128]{1,0:T(8,128)(2,1)S(1)}, u32[]{:S(2)}, u32[]{:S(2)}) %collective-permute-start.5) | collective-permute-done | bytes 262176 | tf_op jit(solution)/shard_map/ppermute | solution.py:473
  67.3 1.0 %shard_map.99 = bf16[16,64,128]{2,1,0:T(8,128)(2,1)} custom-call(f32[1024,128]{1,0:T(8,128)S(1)} %get-tuple-element.40.own, bf16[1024,128]{1,0:T(8,128)(2,1)S(1)} %collective-permute-done.4.from_below, bf16[1024,128]{1,0:T(8,128)(2,1)S(1)} %collective-permute-done.5.from_above), custom_call_target="tpu_custom_call" | custom-call | flops 262144 | bytes 1048576 | tf_op jit(solution)/shard_map/pallas_call | solution.py:320
  68.3 0.0 all-to-all-done.2.refs_0_
  68.3 1.7 %collective-permute-start.6 = (bf16[16,144,128]{2,1,0:T(8,128)(2,1)S(1)}, bf16[16,144,128]{2,1,0:T(8,128)(2,1)S(1)}, u32[]{:S(2)}, u32[]{:S(2)}) collective-permute-start(bf16[16,144,128]{2,1,0:T(8,128)(2,1)S(1)} %all-to-all-done.2.refs_0_), channel_id=1, source_target_pairs={{0,1},{1,0},{2,3},{3,2},{4,5},{5,4},{6,7},{7,6},{8,9},{9,8},{10,11... | collective-permute-start | bytes 1769480 | tf_op jit(solution)/shard_map/ppermute | solution.py:165
  70.0 1.0 %shard_map.100.refs_2_ = f32[4096,128]{1,0:T(8,128)} custom-call(bf16[16,144,128]{2,1,0:T(8,128)(2,1)S(1)} %all-to-all-done.2.refs_0_), custom_call_target="tpu_custom_call" | custom-call | tf_op jit(solution)/shard_map/pallas_call | solution.py:415
  71.0 0.6 collective-permute-done.6.refs_1_
  71.6 1.8 %shard_map.101 = (f32[4096,128]{1,0:T(8,128)}, f32[432,32]{1,0:T(8,128)}, f32[864,32]{1,0:T(8,128)}) custom-call(bf16[16,144,128]{2,1,0:T(8,128)(2,1)S(1)} %all-to-all-done.2.refs_0_, bf16[16,144,128]{2,1,0:T(8,128)(2,1)S(1)} %collective-permute-done.6.refs_1_, f32[4096,128]{1,0:T(8,128)} %shard_map.100.refs_2_), custom_call_target="tpu_custom_call", output_to_operand_aliasing={{0}: (2, {})} | custom-call | tf_op jit(solution)/shard_map/pallas_call | solution.py:423
  (1 shorter events, 0.0 us)
Async XLA Ops:
  0.6 2.5 %copy-start.1 = (bf16[1,1,32,64,128]{4,3,2,1,0:T(8,128)(2,1)S(1)}, bf16[1,1,32,64,128]{4,3,2,1,0:T(8,128)(2,1)}, u32[]{:S(2)}) copy-start(bf16[1,1,32,64,128]{4,3,2,1,0:T(8,128)(2,1)} %param.8) | copy-start | bytes 1572868
  0.6 11.5 %copy-start = (f32[1,524288]{1,0:T(1,128)S(1)}, f32[1,524288]{1,0:T(1,128)}, u32[]{:S(2)}) copy-start(f32[1,524288]{1,0:T(1,128)} %param.11) | copy-start | bytes 6291460
  3.0 2.6 %collective-permute-start = (bf16[2048,128]{1,0:T(8,128)(2,1)}, bf16[2048,128]{1,0:T(8,128)(2,1)S(1)}, u32[]{:S(2)}, u32[]{:S(2)}) collective-permute-start(bf16[2048,128]{1,0:T(8,128)(2,1)} %shard_map.93), channel_id=1, source_target_pairs={{0,1},{1,0},{2,3},{3,2},{4,5},{5,4},{6,7},{7,6},{8,9},{9,8},{10,11... | collective-permute-start | bytes 1572872 | tf_op jit(solution)/shard_map/ppermute | solution.py:165
  3.1 1.0 %copy-start.2 = (bf16[1,1,16,64,128]{4,3,2,1,0:T(8,128)(2,1)S(1)}, bf16[1,1,16,64,128]{4,3,2,1,0:T(8,128)(2,1)}, u32[]{:S(2)}) copy-start(bf16[1,1,16,64,128]{4,3,2,1,0:T(8,128)(2,1)} %param.6) | copy-start | bytes 786436
  5.5 15.8 %copy-start.3 = (bf16[1,1,32,64,128]{4,3,2,1,0:T(8,128)(2,1)S(1)}, bf16[1,1,32,64,128]{4,3,2,1,0:T(8,128)(2,1)}, u32[]{:S(2)}) copy-start(bf16[1,1,32,64,128]{4,3,2,1,0:T(8,128)(2,1)} %param.7) | copy-start | bytes 1572868
  5.6 15.8 %copy-start.5 = (bf16[3,3,3,16,32]{4,3,2,1,0:T(8,128)(2,1)S(1)}, bf16[3,3,3,16,32]{4,3,2,1,0:T(8,128)(2,1)}, u32[]{:S(2)}) copy-start(bf16[3,3,3,16,32]{4,3,2,1,0:T(8,128)(2,1)} %one.1) | copy-start | bytes 82948
  5.6 14.7 %collective-permute-start.2 = (bf16[3168,128]{1,0:T(8,128)(2,1)S(1)}, bf16[3168,128]{1,0:T(8,128)(2,1)}, u32[]{:S(2)}, u32[]{:S(2)}) collective-permute-start(bf16[3168,128]{1,0:T(8,128)(2,1)S(1)} %shard_map.94.pack_0), channel_id=1, source_target_pairs={{1,0},{2,1},{3,2},{5,4},{6,5},{7,6},{9,8},{10,9},{11,10},{13,12},{... | collective-permute-start | bytes 2433032 | tf_op jit(solution)/shard_map/ppermute | solution.py:442
  8.1 13.2 %collective-permute-start.1 = (bf16[3168,128]{1,0:T(8,128)(2,1)S(1)}, bf16[3168,128]{1,0:T(8,128)(2,1)}, u32[]{:S(2)}, u32[]{:S(2)}) collective-permute-start(bf16[3168,128]{1,0:T(8,128)(2,1)S(1)} %shard_map.94.pack_0), channel_id=1, source_target_pairs={{0,1},{1,2},{2,3},{4,5},{5,6},{6,7},{8,9},{9,10},{10,11},{12,13},{... | collective-permute-start | bytes 2433032 | tf_op jit(solution)/shard_map/ppermute | solution.py:442
  13.1 18.5 %all-to-all-start = ((bf16[16,128,128]{2,1,0:T(8,128)(2,1)}), bf16[16,128,128]{2,1,0:T(8,128)(2,1)S(1)}, u32[]{:S(2)}, u32[]{:S(2)}) async-start(bf16[16,128,128]{2,1,0:T(8,128)(2,1)} %bitcast.4), calls=%async_computation | async-start | bytes 1048576 | tf_op jit(solution)/shard_map/all_to_all | solution.py:457
  21.3 0.9 %copy-start.4 = (bf16[3,3,3,32,32]{4,3,2,1,0:T(8,128)(2,1)S(1)}, bf16[3,3,3,32,32]{4,3,2,1,0:T(8,128)(2,1)}, u32[]{:S(2)}) copy-start(bf16[3,3,3,32,32]{4,3,2,1,0:T(8,128)(2,1)} %two.1) | copy-start | bytes 165892
  29.8 1.3 %collective-permute-start.3 = (bf16[256,128]{1,0:T(8,128)(2,1)S(1)}, bf16[256,128]{1,0:T(8,128)(2,1)S(1)}, u32[]{:S(2)}, u32[]{:S(2)}) collective-permute-start(bf16[256,128]{1,0:T(8,128)(2,1)S(1)} %get-tuple-element.35), channel_id=1, source_target_pairs={{0,1},{1,0},{2,3},{3,2},{4,5},{5,4},{6,7},{7,6},{8,9},{9,8},{10,11... | collective-permute-start | bytes 196616 | tf_op jit(solution)/shard_map/ppermute | solution.py:165
  49.2 19.1 %all-to-all-start.2 = ((bf16[16,144,128]{2,1,0:T(8,128)(2,1)}), bf16[16,144,128]{2,1,0:T(8,128)(2,1)S(1)}, u32[]{:S(2)}, u32[]{:S(2)}) async-start(bf16[16,144,128]{2,1,0:T(8,128)(2,1)} %shard_map.98), calls=%async_computation.2 | async-start | bytes 1179648 | tf_op jit(solution)/shard_map/all_to_all | solution.py:469
  52.8 10.7 %collective-permute-start.4 = (bf16[1024,128]{1,0:T(8,128)(2,1)S(1)}, bf16[1024,128]{1,0:T(8,128)(2,1)S(1)}, u32[]{:S(2)}, u32[]{:S(2)}) collective-permute-start(bf16[1024,128]{1,0:T(8,128)(2,1)S(1)} %get-tuple-element.41), channel_id=1, source_target_pairs={{0,1},{1,2},{2,3},{4,5},{5,6},{6,7},{8,9},{9,10},{10,11},{12,13},{... | collective-permute-start | bytes 786440 | tf_op jit(solution)/shard_map/ppermute | solution.py:472
  57.8 9.6 %collective-permute-start.5 = (bf16[1024,128]{1,0:T(8,128)(2,1)S(1)}, bf16[1024,128]{1,0:T(8,128)(2,1)S(1)}, u32[]{:S(2)}, u32[]{:S(2)}) collective-permute-start(bf16[1024,128]{1,0:T(8,128)(2,1)S(1)} %get-tuple-element.42), channel_id=1, source_target_pairs={{1,0},{2,1},{3,2},{5,4},{6,5},{7,6},{9,8},{10,9},{11,10},{13,12},{... | collective-permute-start | bytes 786440 | tf_op jit(solution)/shard_map/ppermute | solution.py:473
  68.3 3.3 %collective-permute-start.6 = (bf16[16,144,128]{2,1,0:T(8,128)(2,1)S(1)}, bf16[16,144,128]{2,1,0:T(8,128)(2,1)S(1)}, u32[]{:S(2)}, u32[]{:S(2)}) collective-permute-start(bf16[16,144,128]{2,1,0:T(8,128)(2,1)S(1)} %all-to-all-done.2.refs_0_), channel_id=1, source_target_pairs={{0,1},{1,0},{2,3},{3,2},{4,5},{5,4},{6,7},{7,6},{8,9},{9,8},{10,11... | collective-permute-start | bytes 1769480 | tf_op jit(solution)/shard_map/ppermute | solution.py:165

commit v7 on v6

--- a/solution.py
+++ b/solution.py
@@ -82,7 +82,6 @@
             pltpu.VMEM((vol.shape[0] * length, width), F32),
             pltpu.SemaphoreType.DMA((pieces,)),
         ],
-        compiler_params=pltpu.CompilerParams(vmem_limit_bytes=24 * 2**20),
         cost_estimate=pl.CostEstimate(flops=0, bytes_accessed=4 * cot.size, transcendentals=0),
     )(cot, vol)
 
@@ -119,46 +118,41 @@
     )(value)
 
 
-def add_kernel(src, other, out):
-    rows = out.shape[0]
-    step = rows // 8
-    start = lax.axis_index("core") * rows
-
-    def add(n, carry):
-        at = pl.ds(pl.multiple_of(n * step, 16), step)
-        own = src[pl.ds(pl.multiple_of(start + n * step, 16), step), :]
-        out[at, :] = (own + other[at, :].astype(F32)).astype(out.dtype)
-        return carry
-
-    lax.fori_loop(0, 8, add, 0)
-
-
-def add(value, other):
+def fetch_kernel(src, out, sems):
+    for _, copy in fetched_chunks(src, lax.axis_index("core") * out.shape[0], out, sems):
+        copy.wait()
+
+
+def fetch(value, chunks=4):
+    half = (value.shape[0] // 2, LANES)
+    return pl.pallas_call(
+        fetch_kernel,
+        out_shape=jax.ShapeDtypeStruct(half, F32),
+        in_specs=[pl.BlockSpec(memory_space=pltpu.HBM)],
+        out_specs=pl.BlockSpec(memory_space=pltpu.VMEM),
+        scratch_shapes=[pltpu.SemaphoreType.DMA((chunks,))],
+        compiler_params=pltpu.CompilerParams(vmem_limit_bytes=61 * 2**20),
+        cost_estimate=pl.CostEstimate(flops=0, bytes_accessed=4 * value.size, transcendentals=0),
+    )(value)
+
+
+def add_kernel(own, other, out):
+    out[...] = (own[...] + other[...].astype(F32)).astype(out.dtype)
+
+
+def add(own, other):
     return vmem_call(
         add_kernel,
         jax.ShapeDtypeStruct(other.shape, BF16),
         (),
-        pl.CostEstimate(flops=0, bytes_accessed=4 * value.size, transcendentals=0),
-    )(value, other)
+        pl.CostEstimate(flops=0, bytes_accessed=8 * own.size, transcendentals=0),
+    )(own, other)
 
 
 def split_to(total, mine, send, keep):
     half = total.shape[0] // 2
     keep[...] = total[pl.ds(pl.multiple_of(mine * half, 16), half), :]
     send[...] = total[pl.ds(pl.multiple_of((1 - mine) * half, 16), half), :].astype(send.dtype)
-
-
-def pair_kernel(keep, other, out):
-    out[...] = (keep[...] + other[...].astype(F32)).astype(out.dtype)
-
-
-def pair_sum(keep, other):
-    return vmem_call(
-        pair_kernel,
-        jax.ShapeDtypeStruct(other.shape, BF16),
-        (),
-        pl.CostEstimate(flops=0, bytes_accessed=8 * keep.size, transcendentals=0),
-    )(keep, other)
 
 
 def swapped(value):
@@ -368,7 +362,11 @@
         copy.wait()
 
 
-def finish_kernel(sizes, height, mine, other, partial, bucket, out_one, out_two, raw, buffer, sems):
+def finish_kernel(
+    sizes, height, mine, other, partial,
+    bucket, out_one, out_two,
+    raw, one, two, out_sems, buffer, sems,
+):
     c0, c1, c2 = sizes
     copies, rows, _ = mine.shape
     extra = rows - height
@@ -381,20 +379,28 @@
             raw[pl.ds(at, extra), :] = source[q, height:rows, :].astype(F32)
         return carry
 
-    lax.fori_loop(0, copies, unpack, 0)
+    lax.fori_loop(0, copies, unpack, 0, unroll=4)
     block = 3 * c1
     first = -(-9 * c2 // LANES) * block
     for i in range(3):
         for j in range(3):
             column = ((2 - j) * 3 + 2 - i) * c2
             whole, lane = (column // LANES, column % LANES)
-            out_two[(3 * i + j) * block : (3 * i + j + 1) * block, :] = raw[
+            two[(3 * i + j) * block : (3 * i + j + 1) * block, :] = raw[
                 whole * block : (whole + 1) * block, lane : lane + c2
             ]
+        at = pl.ds(3 * i * block, 3 * block)
+        sent.append(pltpu.make_async_copy(two.at[at], out_two.at[at], out_sems.at[i]))
+        sent[-1].start()
+    for i in range(3):
+        for j in range(3):
             row = first + (3 * j + i) * c0
             for k in range(3):
                 to = (9 * i + 3 * j + k) * c0
-                out_one[to : to + c0, :] = raw[row : row + c0, k * c1 : (k + 1) * c1]
+                one[to : to + c0, :] = raw[row : row + c0, k * c1 : (k + 1) * c1]
+        at = pl.ds(9 * i * c0, 9 * c0)
+        sent.append(pltpu.make_async_copy(one.at[at], out_one.at[at], out_sems.at[3 + i]))
+        sent[-1].start()
     for copy in sent:
         copy.wait()
 
@@ -428,8 +434,14 @@
             jax.ShapeDtypeStruct((27 * c1, c2), F32),
         ),
         in_specs=[spec, spec, remote],
-        out_specs=(remote, spec, spec),
-        scratch_shapes=[pltpu.VMEM((2 * copies * (rows - height), LANES), F32)] + scratch,
+        out_specs=(remote, remote, remote),
+        scratch_shapes=[
+            pltpu.VMEM((2 * copies * (rows - height), LANES), F32),
+            pltpu.VMEM((27 * c0, c1), F32),
+            pltpu.VMEM((27 * c1, c2), F32),
+            pltpu.SemaphoreType.DMA((6,)),
+        ]
+        + scratch,
         input_output_aliases={2: 0},
         compiler_params=params,
     )(mine, other, partial)
@@ -447,19 +459,18 @@
     devices, copies = (lax.axis_size(EVERY), lax.axis_size(SAME))
     length = grad_bucket.shape[1]
     bucket = grad_bucket.reshape(length // LANES, LANES)
-    send = cast(bucket)
-    cot, vol, send = lax.optimization_barrier((out_cot[0, 0], volume_in[0, 0], send))
-    packed = pack(cot, vol)
-    other, packed = lax.optimization_barrier((swapped(send), packed))
+    packed = pack(out_cot[0, 0], volume_in[0, 0])
+    packed, bucket = lax.optimization_barrier((packed, bucket))
     below, above = halos(packed)
-    half = add(bucket, other)
+    send, bucket = lax.optimization_barrier((cast(bucket), bucket))
+    half = add(fetch(bucket), swapped(send))
     act, half = lax.optimization_barrier((hidden_act[0, 0], half))
     parts = lax.all_to_all(half.reshape(copies, -1, LANES), SAME, 0, 0)
 
     used = -(-9 * c2 // LANES) * 3 * c1 + 9 * c0
     rows = ceil_to(used, 16 * devices)
     send, keep, own, up, down = compute((below, packed, above), act, kernel_two, kernel_one, rows)
-    terms = pair_sum(keep, swapped(send))
+    terms = add(keep, swapped(send))
     terms, parts = lax.optimization_barrier((terms, parts))
     terms = lax.all_to_all(terms.reshape(copies, -1, LANES), SAME, 0, 0)
     cells = volume_in.shape[3] * volume_in.shape[4] * devices

time: 74.3 us -> 73.6 us (level)
  blocking collectives: 16.5 us -> 11.9 us
  local copies, waits for them, and re-layouts: 1.91 us -> 5.5 us
  waiting for transfers between devices: 12 us -> 9.55 us
  Pallas kernels: 17.1 us -> 19 us
  starting transfers between devices: 25.1 us -> 25.9 us
    all_to_all x1, blocking collectives: 16.5 us -> 11.9 us  [per_device(): terms = lax.all_to_all(terms.reshape(copies, -1, LANES), SAME, 0, 0)]
    unnamed x12 -> x18, local copies, waits for them, and re-layouts: 1.91 us -> 5.5 us
    pallas_call x1, Pallas kernels: 0.01 us -> 2.2 us  [fetch(): pl.pallas_call(fetch_kernel, out_shape=jax.ShapeDtypeStruct(half, F32), i...]
    ppermute x2, waiting for transfers between devices: 2.01 us -> 0.01 us  [halos(): return (lax.ppermute(value, SPACE, up), lax.ppermute(value, SPACE, down))]
    pallas_call x1, Pallas kernels: 1.5 us -> 3.32 us  [pack(): pl.pallas_call(pack_kernel, out_shape=jax.ShapeDtypeStruct(((length + 2)...]
    pallas_call x1, Pallas kernels: 7.55 us -> 6.14 us  [compute(): vmem_call(compute_kernel, (jax.ShapeDtypeStruct((rows // 2, LANES), BF16)...]
    ppermute x1, starting transfers between devices: 4.99 us -> 5.9 us  [per_device(): from_below = lax.ppermute(up, SPACE, upward)]
  transfers between devices with their start and end apart: 9 -> 9, of which waited for: 7 -> 5; matrix products, arithmetic and copies ran while one was open for 0% -> 0% of each run, Pallas kernels for 16% -> 18%
where the time goes in v7:
time: 73.6 us; the launch traced here: 72.6 us
  starting transfers between devices  25.9 us (35%)
  Pallas kernels  19 us (26%)
  blocking collectives  11.9 us (16%)
  waiting for transfers between devices  9.55 us (13%)
  local copies, waits for them, and re-layouts  5.5 us (7%)
  between operations  0.81 us (1%)
    all_to_all x1, blocking collectives, per_device(): terms = lax.all_to_all(terms.reshape(copies, -1, LANES), SAME, 0, 0)  11.9 us
    ppermute x2, starting transfers between devices, halos(): return (lax.ppermute(value, SPACE, up), lax.ppermute(value, SPACE, down))  6.46 us
    pallas_call x1, Pallas kernels, compute(): vmem_call(compute_kernel, (jax.ShapeDtypeStruct((rows // 2, LANES), BF16)...  6.14 us
    all_to_all x1, starting transfers between devices, per_device(): parts = lax.all_to_all(half.reshape(copies, -1, LANES), SAME, 0, 0)  5.98 us
    ppermute x1, starting transfers between devices, per_device(): from_below = lax.ppermute(up, SPACE, upward)  5.9 us
    unnamed x18, local copies, waits for them, and re-layouts  5.5 us
    ppermute x1, waiting for transfers between devices, per_device(): from_above = lax.ppermute(down, SPACE, [(j, i) for i, j in upward])  3.85 us
    all_to_all x1, starting transfers between devices, per_device(): mine = lax.all_to_all(shares, SAME, 0, 0)  3.58 us
  transfers between devices with their start and end apart: 9, of which 5 were waited for; matrix products, arithmetic and copies ran while one was open for 0% of the time, Pallas kernels for 18%

profile of v7, /device:TPU:1, one launch (start us, length us, event | category | flops | bytes accessed | tf_op | source)
XLA Modules:
  0.0 72.6 jit_solution(4947158384314931275)
XLA Ops:
  0.6 3.3 %shard_map.93.pack_0 = bf16[3168,128]{1,0:T(8,128)(2,1)} custom-call(bf16[32,64,128]{2,1,0:T(8,128)(2,1)} %bitcast.15, bf16[16,64,128]{2,1,0:T(8,128)(2,1)} %bitcast.16), custom_call_target="tpu_custom_call" | custom-call | bytes 1048576 | tf_op jit(solution)/shard_map/pallas_call | solution.py:75
  4.0 2.0 %collective-permute-start.1 = (bf16[3168,128]{1,0:T(8,128)(2,1)}, bf16[3168,128]{1,0:T(8,128)(2,1)S(1)}, u32[]{:S(2)}, u32[]{:S(2)}) collective-permute-start(bf16[3168,128]{1,0:T(8,128)(2,1)} %shard_map.93.pack_0), channel_id=1, source_target_pairs={{1,0},{2,1},{3,2},{5,4},{6,5},{7,6},{9,8},{10,9},{11,10},{13,12},{... | collective-permute-start | bytes 2433032 | tf_op jit(solution)/shard_map/ppermute | solution.py:454
  5.9 4.5 %collective-permute-start = (bf16[3168,128]{1,0:T(8,128)(2,1)}, bf16[3168,128]{1,0:T(8,128)(2,1)S(1)}, u32[]{:S(2)}, u32[]{:S(2)}) collective-permute-start(bf16[3168,128]{1,0:T(8,128)(2,1)} %shard_map.93.pack_0), channel_id=1, source_target_pairs={{0,1},{1,2},{2,3},{4,5},{5,6},{6,7},{8,9},{9,10},{10,11},{12,13},{... | collective-permute-start | bytes 2433032 | tf_op jit(solution)/shard_map/ppermute | solution.py:454
  10.4 2.2 %shard_map.94 = bf16[2048,128]{1,0:T(8,128)(2,1)} custom-call(f32[4096,128]{1,0:T(8,128)} %bitcast.12), custom_call_target="tpu_custom_call" | custom-call | bytes 3145728 | tf_op jit(solution)/shard_map/pallas_call | solution.py:111
  12.6 0.1 collective-permute-start.2
  12.7 2.2 %shard_map.95.own = f32[2048,128]{1,0:T(8,128)} custom-call(f32[4096,128]{1,0:T(8,128)} %bitcast.13), custom_call_target="tpu_custom_call" | custom-call | bytes 2097152 | tf_op jit(solution)/shard_map/pallas_call | solution.py:128
  14.9 0.0 collective-permute-done.2.other
  14.9 0.0 copy-start
  14.9 1.2 %copy-done = f32[2048,128]{1,0:T(8,128)S(1)} copy-done((f32[2048,128]{1,0:T(8,128)S(1)}, f32[2048,128]{1,0:T(8,128)}, u32[]{:S(2)}) %copy-start) | copy-done | bytes 1048600
  16.1 0.0 copy-start.1
  16.1 0.9 %shard_map.96 = bf16[2048,128]{1,0:T(8,128)(2,1)} custom-call(f32[2048,128]{1,0:T(8,128)S(1)} %copy-done, bf16[2048,128]{1,0:T(8,128)(2,1)S(1)} %collective-permute-done.2.other), custom_call_target="tpu_custom_call" | custom-call | bytes 2097152 | tf_op jit(solution)/shard_map/pallas_call | solution.py:144
  17.0 6.0 %all-to-all-start = ((bf16[16,128,128]{2,1,0:T(8,128)(2,1)}), bf16[16,128,128]{2,1,0:T(8,128)(2,1)S(1)}, u32[]{:S(2)}, u32[]{:S(2)}) async-start(bf16[16,128,128]{2,1,0:T(8,128)(2,1)} %bitcast.4), calls=%async_computation | async-start | bytes 1048576 | tf_op jit(solution)/shard_map/all_to_all | solution.py:468
  23.0 0.0 collective-permute-done.1.pack_p
  23.0 0.0 collective-permute-done.pack_m
  23.0 0.0 copy-done.1
  23.0 0.0 copy-start.2
  23.1 1.0 %copy-done.2 = bf16[1,1,32,64,128]{4,3,2,1,0:T(8,128)(2,1)S(1)} copy-done((bf16[1,1,32,64,128]{4,3,2,1,0:T(8,128)(2,1)S(1)}, bf16[1,1,32,64,128]{4,3,2,1,0:T(8,128)(2,1)}, u32[]{:S(2)}) %copy-start.2) | copy-done | bytes 524312
  24.1 0.0 copy-start.7
  24.1 0.9 %copy-done.7 = bf16[3,3,3,32,32]{4,3,2,1,0:T(8,128)(2,1)S(1)} copy-done((bf16[3,3,3,32,32]{4,3,2,1,0:T(8,128)(2,1)S(1)}, bf16[3,3,3,32,32]{4,3,2,1,0:T(8,128)(2,1)}, u32[]{:S(2)}) %copy-start.7) | copy-done | bytes 55320
  25.0 0.0 copy-start.8
  25.0 0.9 %copy-done.8 = bf16[3,3,3,16,32]{4,3,2,1,0:T(8,128)(2,1)S(1)} copy-done((bf16[3,3,3,16,32]{4,3,2,1,0:T(8,128)(2,1)S(1)}, bf16[3,3,3,16,32]{4,3,2,1,0:T(8,128)(2,1)}, u32[]{:S(2)}) %copy-start.8) | copy-done | bytes 27672
  25.9 6.1 %shard_map.97 = (bf16[256,128]{1,0:T(8,128)(2,1)S(1)}, f32[256,128]{1,0:T(8,128)S(1)}, f32[1024,128]{1,0:T(8,128)S(1)}, bf16[1024,128]{1,0:T(8,128)(2,1)S(1)}, bf16[1024,128]{1,0:T(8,128)(2,1)S(1)}) custom-call(bf16[3168,128]{1,0:T(8,128)(2,1)S(1)} %collective-permute-done.pack_m, bf16[3168,128]{1,0:T(8,128)(2,1)S(1)} %copy-done.1, ...), custom_call_target="tpu_custom_call" | custom-call | flops 10000000000 | bytes 41943040 | tf_op jit(solution)/shard_map/pallas_call | solution.py:273
  32.1 0.0 copy-start.3
  32.1 0.7 copy-done.3
  32.8 0.0 copy-start.5
  32.8 0.7 copy-done.5
  33.5 0.0 copy-start.6
  33.5 0.0 copy-start.4
  33.5 0.4 collective-permute-start.3
  33.9 0.9 %collective-permute-done.3.other = bf16[256,128]{1,0:T(8,128)(2,1)S(1)} collective-permute-done((bf16[256,128]{1,0:T(8,128)(2,1)S(1)}, bf16[256,128]{1,0:T(8,128)(2,1)S(1)}, u32[]{:S(2)}, u32[]{:S(2)}) %collective-permute-start.3) | collective-permute-done | bytes 65568 | tf_op jit(solution)/shard_map/ppermute | solution.py:159
  34.8 1.0 %all-to-all-done.refs_0_ = bf16[16,128,128]{2,1,0:T(8,128)(2,1)S(1)} async-done(((bf16[16,128,128]{2,1,0:T(8,128)(2,1)}), bf16[16,128,128]{2,1,0:T(8,128)(2,1)S(1)}, u32[]{:S(2)}, u32[]{:S(2)}) %all-to-all-start) | async-done | bytes 524320 | tf_op jit(solution)/shard_map/all_to_all | solution.py:468
  35.9 11.9 %all_to_all.15.refs_1_ = bf16[16,16,128]{2,1,0:T(8,128)(2,1)S(1)} all-to-all(bf16[16,16,128]{2,1,0:T(8,128)(2,1)S(1)} %bitcast.10), channel_id=1, replica_groups=mesh['dp'=8,'slab'=2,'core'=2] {'dp','slab'}, dimensions={0} | all-to-all | bytes 131072 | tf_op jit(solution)/shard_map/all_to_all | solution.py:475
  47.7 1.0 %shard_map.99 = bf16[16,144,128]{2,1,0:T(8,128)(2,1)} custom-call(bf16[16,128,128]{2,1,0:T(8,128)(2,1)S(1)} %all-to-all-done.refs_0_, bf16[16,16,128]{2,1,0:T(8,128)(2,1)S(1)} %all_to_all.15.refs_1_), custom_call_target="tpu_custom_call" | custom-call | flops 262144 | bytes 786432 | tf_op jit(solution)/shard_map/pallas_call | solution.py:337
  48.7 3.6 %all-to-all-start.2 = ((bf16[16,144,128]{2,1,0:T(8,128)(2,1)}), bf16[16,144,128]{2,1,0:T(8,128)(2,1)S(1)}, u32[]{:S(2)}, u32[]{:S(2)}) async-start(bf16[16,144,128]{2,1,0:T(8,128)(2,1)} %shard_map.99), calls=%async_computation.2 | async-start | bytes 1179648 | tf_op jit(solution)/shard_map/all_to_all | solution.py:480
  52.3 0.0 copy-done.6
  52.4 5.9 %collective-permute-start.4 = (bf16[1024,128]{1,0:T(8,128)(2,1)S(1)}, bf16[1024,128]{1,0:T(8,128)(2,1)S(1)}, u32[]{:S(2)}, u32[]{:S(2)}) collective-permute-start(bf16[1024,128]{1,0:T(8,128)(2,1)S(1)} %copy-done.6), channel_id=1, source_target_pairs={{0,1},{1,2},{2,3},{4,5},{5,6},{6,7},{8,9},{9,10},{10,11},{12,13},{... | collective-permute-start | bytes 786440 | tf_op jit(solution)/shard_map/ppermute | solution.py:483
  58.3 0.0 copy-done.4
  58.3 1.9 %collective-permute-start.5 = (bf16[1024,128]{1,0:T(8,128)(2,1)S(1)}, bf16[1024,128]{1,0:T(8,128)(2,1)S(1)}, u32[]{:S(2)}, u32[]{:S(2)}) collective-permute-start(bf16[1024,128]{1,0:T(8,128)(2,1)S(1)} %copy-done.4), channel_id=1, source_target_pairs={{1,0},{2,1},{3,2},{5,4},{6,5},{7,6},{9,8},{10,9},{11,10},{13,12},{... | collective-permute-start | bytes 786440 | tf_op jit(solution)/shard_map/ppermute | solution.py:484
  60.2 3.1 %collective-permute-done.4.from_below = bf16[1024,128]{1,0:T(8,128)(2,1)S(1)} collective-permute-done((bf16[1024,128]{1,0:T(8,128)(2,1)S(1)}, bf16[1024,128]{1,0:T(8,128)(2,1)S(1)}, u32[]{:S(2)}, u32[]{:S(2)}) %collective-permute-start.4) | collective-permute-done | bytes 262176 | tf_op jit(solution)/shard_map/ppermute | solution.py:483
  63.3 3.9 %collective-permute-done.5.from_above = bf16[1024,128]{1,0:T(8,128)(2,1)S(1)} collective-permute-done((bf16[1024,128]{1,0:T(8,128)(2,1)S(1)}, bf16[1024,128]{1,0:T(8,128)(2,1)S(1)}, u32[]{:S(2)}, u32[]{:S(2)}) %collective-permute-start.5) | collective-permute-done | bytes 262176 | tf_op jit(solution)/shard_map/ppermute | solution.py:484
  67.2 1.0 %shard_map.100 = bf16[16,64,128]{2,1,0:T(8,128)(2,1)} custom-call(f32[1024,128]{1,0:T(8,128)S(1)} %get-tuple-element.38.own, bf16[1024,128]{1,0:T(8,128)(2,1)S(1)} %collective-permute-done.4.from_below, bf16[1024,128]{1,0:T(8,128)(2,1)S(1)} %collective-permute-done.5.from_above), custom_call_target="tpu_custom_call" | custom-call | flops 262144 | bytes 1048576 | tf_op jit(solution)/shard_map/pallas_call | solution.py:314
  68.2 0.0 all-to-all-done.2.refs_0_
  68.2 1.5 %collective-permute-start.6 = (bf16[16,144,128]{2,1,0:T(8,128)(2,1)S(1)}, bf16[16,144,128]{2,1,0:T(8,128)(2,1)S(1)}, u32[]{:S(2)}, u32[]{:S(2)}) collective-permute-start(bf16[16,144,128]{2,1,0:T(8,128)(2,1)S(1)} %all-to-all-done.2.refs_0_), channel_id=1, source_target_pairs={{0,1},{1,0},{2,3},{3,2},{4,5},{5,4},{6,7},{7,6},{8,9},{9,8},{10,11... | collective-permute-start | bytes 1769480 | tf_op jit(solution)/shard_map/ppermute | solution.py:159
  69.7 1.0 %shard_map.101.refs_2_ = f32[4096,128]{1,0:T(8,128)} custom-call(bf16[16,144,128]{2,1,0:T(8,128)(2,1)S(1)} %all-to-all-done.2.refs_0_), custom_call_target="tpu_custom_call" | custom-call | tf_op jit(solution)/shard_map/pallas_call | solution.py:421
  70.7 0.6 collective-permute-done.6.refs_1_
  71.3 1.3 %shard_map.102 = (f32[4096,128]{1,0:T(8,128)}, f32[432,32]{1,0:T(8,128)}, f32[864,32]{1,0:T(8,128)}) custom-call(bf16[16,144,128]{2,1,0:T(8,128)(2,1)S(1)} %all-to-all-done.2.refs_0_, bf16[16,144,128]{2,1,0:T(8,128)(2,1)S(1)} %collective-permute-done.6.refs_1_, f32[4096,128]{1,0:T(8,128)} %shard_map.101.refs_2_), custom_call_target="tpu_custom_call", output_to_operand_aliasing={{0}: (2, {})} | custom-call | tf_op jit(solution)/shard_map/pallas_call | solution.py:429
  (1 shorter events, 0.0 us)
Async XLA Ops:
  4.0 19.1 %collective-permute-start.1 = (bf16[3168,128]{1,0:T(8,128)(2,1)}, bf16[3168,128]{1,0:T(8,128)(2,1)S(1)}, u32[]{:S(2)}, u32[]{:S(2)}) collective-permute-start(bf16[3168,128]{1,0:T(8,128)(2,1)} %shard_map.93.pack_0), channel_id=1, source_target_pairs={{1,0},{2,1},{3,2},{5,4},{6,5},{7,6},{9,8},{10,9},{11,10},{13,12},{... | collective-permute-start | bytes 2433032 | tf_op jit(solution)/shard_map/ppermute | solution.py:454
  5.9 17.1 %collective-permute-start = (bf16[3168,128]{1,0:T(8,128)(2,1)}, bf16[3168,128]{1,0:T(8,128)(2,1)S(1)}, u32[]{:S(2)}, u32[]{:S(2)}) collective-permute-start(bf16[3168,128]{1,0:T(8,128)(2,1)} %shard_map.93.pack_0), channel_id=1, source_target_pairs={{0,1},{1,2},{2,3},{4,5},{5,6},{6,7},{8,9},{9,10},{10,11},{12,13},{... | collective-permute-start | bytes 2433032 | tf_op jit(solution)/shard_map/ppermute | solution.py:454
  12.6 2.3 %collective-permute-start.2 = (bf16[2048,128]{1,0:T(8,128)(2,1)}, bf16[2048,128]{1,0:T(8,128)(2,1)S(1)}, u32[]{:S(2)}, u32[]{:S(2)}) collective-permute-start(bf16[2048,128]{1,0:T(8,128)(2,1)} %shard_map.94), channel_id=1, source_target_pairs={{0,1},{1,0},{2,3},{3,2},{4,5},{5,4},{6,7},{7,6},{8,9},{9,8},{10,11... | collective-permute-start | bytes 1572872 | tf_op jit(solution)/shard_map/ppermute | solution.py:159
  14.9 1.2 %copy-start = (f32[2048,128]{1,0:T(8,128)S(1)}, f32[2048,128]{1,0:T(8,128)}, u32[]{:S(2)}) copy-start(f32[2048,128]{1,0:T(8,128)} %shard_map.95.own) | copy-start | bytes 3145732
  16.1 6.9 %copy-start.1 = (bf16[3168,128]{1,0:T(8,128)(2,1)S(1)}, bf16[3168,128]{1,0:T(8,128)(2,1)}, u32[]{:S(2)}) copy-start(bf16[3168,128]{1,0:T(8,128)(2,1)} %shard_map.93.pack_0) | copy-start | bytes 2433028
  17.0 18.8 %all-to-all-start = ((bf16[16,128,128]{2,1,0:T(8,128)(2,1)}), bf16[16,128,128]{2,1,0:T(8,128)(2,1)S(1)}, u32[]{:S(2)}, u32[]{:S(2)}) async-start(bf16[16,128,128]{2,1,0:T(8,128)(2,1)} %bitcast.4), calls=%async_computation | async-start | bytes 1048576 | tf_op jit(solution)/shard_map/all_to_all | solution.py:468
  23.0 1.0 %copy-start.2 = (bf16[1,1,32,64,128]{4,3,2,1,0:T(8,128)(2,1)S(1)}, bf16[1,1,32,64,128]{4,3,2,1,0:T(8,128)(2,1)}, u32[]{:S(2)}) copy-start(bf16[1,1,32,64,128]{4,3,2,1,0:T(8,128)(2,1)} %param.7) | copy-start | bytes 1572868
  24.1 0.9 %copy-start.7 = (bf16[3,3,3,32,32]{4,3,2,1,0:T(8,128)(2,1)S(1)}, bf16[3,3,3,32,32]{4,3,2,1,0:T(8,128)(2,1)}, u32[]{:S(2)}) copy-start(bf16[3,3,3,32,32]{4,3,2,1,0:T(8,128)(2,1)} %two.1) | copy-start | bytes 165892
  25.0 0.9 %copy-start.8 = (bf16[3,3,3,16,32]{4,3,2,1,0:T(8,128)(2,1)S(1)}, bf16[3,3,3,16,32]{4,3,2,1,0:T(8,128)(2,1)}, u32[]{:S(2)}) copy-start(bf16[3,3,3,16,32]{4,3,2,1,0:T(8,128)(2,1)} %one.1) | copy-start | bytes 82948
  32.1 0.7 copy-start.3
  32.8 0.7 copy-start.5
  33.5 18.9 %copy-start.6 = (bf16[1024,128]{1,0:T(8,128)(2,1)S(1)}, bf16[1024,128]{1,0:T(8,128)(2,1)}, u32[]{:S(2)}) copy-start(bf16[1024,128]{1,0:T(8,128)(2,1)} %copy-done.5) | copy-start | bytes 786436
  33.5 24.8 %copy-start.4 = (bf16[1024,128]{1,0:T(8,128)(2,1)S(1)}, bf16[1024,128]{1,0:T(8,128)(2,1)}, u32[]{:S(2)}) copy-start(bf16[1024,128]{1,0:T(8,128)(2,1)} %copy-done.3) | copy-start | bytes 786436
  33.5 1.3 %collective-permute-start.3 = (bf16[256,128]{1,0:T(8,128)(2,1)S(1)}, bf16[256,128]{1,0:T(8,128)(2,1)S(1)}, u32[]{:S(2)}, u32[]{:S(2)}) collective-permute-start(bf16[256,128]{1,0:T(8,128)(2,1)S(1)} %get-tuple-element.33), channel_id=1, source_target_pairs={{0,1},{1,0},{2,3},{3,2},{4,5},{5,4},{6,7},{7,6},{8,9},{9,8},{10,11... | collective-permute-start | bytes 196616 | tf_op jit(solution)/shard_map/ppermute | solution.py:159
  48.7 19.4 %all-to-all-start.2 = ((bf16[16,144,128]{2,1,0:T(8,128)(2,1)}), bf16[16,144,128]{2,1,0:T(8,128)(2,1)S(1)}, u32[]{:S(2)}, u32[]{:S(2)}) async-start(bf16[16,144,128]{2,1,0:T(8,128)(2,1)} %shard_map.99), calls=%async_computation.2 | async-start | bytes 1179648 | tf_op jit(solution)/shard_map/all_to_all | solution.py:480
  52.4 11.0 %collective-permute-start.4 = (bf16[1024,128]{1,0:T(8,128)(2,1)S(1)}, bf16[1024,128]{1,0:T(8,128)(2,1)S(1)}, u32[]{:S(2)}, u32[]{:S(2)}) collective-permute-start(bf16[1024,128]{1,0:T(8,128)(2,1)S(1)} %copy-done.6), channel_id=1, source_target_pairs={{0,1},{1,2},{2,3},{4,5},{5,6},{6,7},{8,9},{9,10},{10,11},{12,13},{... | collective-permute-start | bytes 786440 | tf_op jit(solution)/shard_map/ppermute | solution.py:483
  58.3 8.9 %collective-permute-start.5 = (bf16[1024,128]{1,0:T(8,128)(2,1)S(1)}, bf16[1024,128]{1,0:T(8,128)(2,1)S(1)}, u32[]{:S(2)}, u32[]{:S(2)}) collective-permute-start(bf16[1024,128]{1,0:T(8,128)(2,1)S(1)} %copy-done.4), channel_id=1, source_target_pairs={{1,0},{2,1},{3,2},{5,4},{6,5},{7,6},{9,8},{10,9},{11,10},{13,12},{... | collective-permute-start | bytes 786440 | tf_op jit(solution)/shard_map/ppermute | solution.py:484
  68.2 3.2 %collective-permute-start.6 = (bf16[16,144,128]{2,1,0:T(8,128)(2,1)S(1)}, bf16[16,144,128]{2,1,0:T(8,128)(2,1)S(1)}, u32[]{:S(2)}, u32[]{:S(2)}) collective-permute-start(bf16[16,144,128]{2,1,0:T(8,128)(2,1)S(1)} %all-to-all-done.2.refs_0_), channel_id=1, source_target_pairs={{0,1},{1,0},{2,3},{3,2},{4,5},{5,4},{6,7},{7,6},{8,9},{9,8},{10,11... | collective-permute-start | bytes 1769480 | tf_op jit(solution)/shard_map/ppermute | solution.py:159

commit v8 on v7

--- a/solution.py
+++ b/solution.py
@@ -49,104 +49,76 @@
     lax.fori_loop(0, length, gather, 0, unroll=4)
 
 
-def pack_kernel(cot, vol, out, fetched, flat, sems):
-    step = vol.shape[0]
-    length, width = vol.shape[1:]
-    pitch = cot.shape[0] + step
-    pieces = [cot.at[pl.ds(n, step)] for n in range(0, cot.shape[0], step)] + [vol]
-    copies = [
-        pltpu.make_async_copy(piece, fetched.at[n], sems.at[n]) for n, piece in enumerate(pieces)
-    ]
-    for copy in copies:
-        copy.start()
+def pack_kernel(cot, vol, out, flat):
+    c2, length, width = cot.shape
+    pitch = c2 + vol.shape[0]
     zeros = jnp.zeros((pitch, width), BF16)
     out[0:pitch, :] = zeros
     out[(length + 1) * pitch : (length + 2) * pitch, :] = zeros
-    for n, copy in enumerate(copies):
-        copy.wait()
-        turned(fetched.at[n], flat, out, n * step, pitch, 1)
+    turned(cot, flat, out, 0, pitch, 1)
+    turned(vol, flat, out, c2, pitch, 1)
 
 
 def pack(cot, vol):
     c2, length, width = cot.shape
     pitch = c2 + vol.shape[0]
-    pieces = pitch // vol.shape[0]
-    source = pl.BlockSpec(memory_space=pltpu.HBM)
-    return pl.pallas_call(
+    return vmem_call(
         pack_kernel,
-        out_shape=jax.ShapeDtypeStruct(((length + 2) * pitch, width), BF16),
-        in_specs=[source, source],
-        out_specs=pl.BlockSpec(memory_space=pltpu.VMEM),
-        scratch_shapes=[
-            pltpu.VMEM((pieces,) + vol.shape, BF16),
-            pltpu.VMEM((vol.shape[0] * length, width), F32),
-            pltpu.SemaphoreType.DMA((pieces,)),
-        ],
-        cost_estimate=pl.CostEstimate(flops=0, bytes_accessed=4 * cot.size, transcendentals=0),
+        jax.ShapeDtypeStruct(((length + 2) * pitch, width), BF16),
+        (pltpu.VMEM((max(c2, vol.shape[0]) * length, width), F32),),
+        pl.CostEstimate(flops=0, bytes_accessed=32 * cot.size, transcendentals=0),
     )(cot, vol)
 
 
-def fetched_chunks(src, start, buffer, sems):
-    count = sems.shape[0]
-    step = buffer.shape[0] // count
-    copies = []
-    for n in range(count):
-        at = pl.ds(pl.multiple_of(start + n * step, 8), step)
-        copies.append(
-            pltpu.make_async_copy(src.at[at], buffer.at[pl.ds(n * step, step)], sems.at[n])
-        )
-        copies[-1].start()
-    return [(pl.ds(n * step, step), copy) for n, copy in enumerate(copies)]
-
-
-def cast_kernel(src, out, buffer, sems):
-    start = (1 - lax.axis_index("core")) * out.shape[0]
-    for rows, copy in fetched_chunks(src, start, buffer, sems):
-        copy.wait()
-        out[rows, :] = buffer[rows, :].astype(out.dtype)
-
-
-def cast(value, chunks=8):
-    half = (value.shape[0] // 2, LANES)
-    return pl.pallas_call(
+def in_steps(body, rows, count=8):
+    step = rows // count
+
+    def one(n, carry):
+        body(n * step, step)
+        return carry
+
+    lax.fori_loop(0, count, one, 0)
+
+
+def cast_kernel(src, out):
+    rows = out.shape[0]
+    start = (1 - lax.axis_index("core")) * rows
+
+    def cast(at, step):
+        value = src[pl.ds(pl.multiple_of(start + at, 16), step), :]
+        out[pl.ds(pl.multiple_of(at, 16), step), :] = value.astype(out.dtype)
+
+    in_steps(cast, rows)
+
+
+def cast(value):
+    return vmem_call(
         cast_kernel,
-        out_shape=jax.ShapeDtypeStruct(half, BF16),
-        in_specs=[pl.BlockSpec(memory_space=pltpu.HBM)],
-        out_specs=pl.BlockSpec(memory_space=pltpu.VMEM),
-        scratch_shapes=[pltpu.VMEM(half, F32), pltpu.SemaphoreType.DMA((chunks,))],
-        cost_estimate=pl.CostEstimate(flops=0, bytes_accessed=6 * value.size, transcendentals=0),
+        jax.ShapeDtypeStruct((value.shape[0] // 2, LANES), BF16),
+        (),
+        pl.CostEstimate(flops=0, bytes_accessed=4 * value.size, transcendentals=0),
     )(value)
 
 
-def fetch_kernel(src, out, sems):
-    for _, copy in fetched_chunks(src, lax.axis_index("core") * out.shape[0], out, sems):
-        copy.wait()
-
-
-def fetch(value, chunks=4):
-    half = (value.shape[0] // 2, LANES)
-    return pl.pallas_call(
-        fetch_kernel,
-        out_shape=jax.ShapeDtypeStruct(half, F32),
-        in_specs=[pl.BlockSpec(memory_space=pltpu.HBM)],
-        out_specs=pl.BlockSpec(memory_space=pltpu.VMEM),
-        scratch_shapes=[pltpu.SemaphoreType.DMA((chunks,))],
-        compiler_params=pltpu.CompilerParams(vmem_limit_bytes=61 * 2**20),
-        cost_estimate=pl.CostEstimate(flops=0, bytes_accessed=4 * value.size, transcendentals=0),
-    )(value)
-
-
-def add_kernel(own, other, out):
-    out[...] = (own[...] + other[...].astype(F32)).astype(out.dtype)
-
-
-def add(own, other):
+def add_kernel(src, other, out):
+    rows = out.shape[0]
+    start = lax.axis_index("core") * rows if src.shape[0] > rows else 0
+
+    def add(at, step):
+        value = src[pl.ds(pl.multiple_of(start + at, 16), step), :]
+        at = pl.ds(pl.multiple_of(at, 16), step)
+        out[at, :] = (value + other[at, :].astype(F32)).astype(out.dtype)
+
+    in_steps(add, rows)
+
+
+def add(value, other):
     return vmem_call(
         add_kernel,
         jax.ShapeDtypeStruct(other.shape, BF16),
         (),
-        pl.CostEstimate(flops=0, bytes_accessed=8 * own.size, transcendentals=0),
-    )(own, other)
+        pl.CostEstimate(flops=0, bytes_accessed=4 * value.size, transcendentals=0),
+    )(value, other)
 
 
 def split_to(total, mine, send, keep):
@@ -462,8 +434,7 @@
     packed = pack(out_cot[0, 0], volume_in[0, 0])
     packed, bucket = lax.optimization_barrier((packed, bucket))
     below, above = halos(packed)
-    send, bucket = lax.optimization_barrier((cast(bucket), bucket))
-    half = add(fetch(bucket), swapped(send))
+    half = add(bucket, swapped(cast(bucket)))
     act, half = lax.optimization_barrier((hidden_act[0, 0], half))
     parts = lax.all_to_all(half.reshape(copies, -1, LANES), SAME, 0, 0)
 

time: 73.6 us -> 71.3 us (0.969)
  Pallas kernels: 19 us -> 12.7 us
  local copies, waits for them, and re-layouts: 5.5 us -> 7.85 us
  waiting for transfers between devices: 9.55 us -> 11.3 us
    pallas_call x3 -> x2, Pallas kernels: 7.7 us -> 1.36 us  [the longest x1 1.29 us: pack(): vmem_call(pack_kernel, jax.ShapeDtypeStruct(((length + 2) * pitch, width)...]
    unnamed x18 -> x20, local copies, waits for them, and re-layouts: 5.5 us -> 7.85 us
    ppermute x3, waiting for transfers between devices: 1.52 us -> 3.41 us  [swapped(): return lax.ppermute(value, 'core', [(0, 1), (1, 0)])]
  transfers between devices with their start and end apart: 9 -> 9, of which waited for: 5 -> 6; matrix products, arithmetic and copies ran while one was open for 0% -> 0% of each run, Pallas kernels for 18% -> 13%
where the time goes in v8:
time: 71.3 us; the launch traced here: 70.4 us
  starting transfers between devices  25.4 us (36%)
  Pallas kernels  12.7 us (18%)
  blocking collectives  12.3 us (17%)
  waiting for transfers between devices  11.3 us (16%)
  local copies, waits for them, and re-layouts  7.85 us (11%)
  between operations  0.79 us (1%)
    all_to_all x1, blocking collectives, per_device(): terms = lax.all_to_all(terms.reshape(copies, -1, LANES), SAME, 0, 0)  12.3 us
    unnamed x20, local copies, waits for them, and re-layouts  7.85 us
    ppermute x2, starting transfers between devices, halos(): return (lax.ppermute(value, SPACE, up), lax.ppermute(value, SPACE, down))  6.46 us
    pallas_call x1, Pallas kernels, compute(): vmem_call(compute_kernel, (jax.ShapeDtypeStruct((rows // 2, LANES), BF16)...  6.15 us
    ppermute x1, starting transfers between devices, per_device(): from_below = lax.ppermute(up, SPACE, upward)  5.73 us
    all_to_all x1, starting transfers between devices, per_device(): parts = lax.all_to_all(half.reshape(copies, -1, LANES), SAME, 0, 0)  5.63 us
    ppermute x1, waiting for transfers between devices, per_device(): from_above = lax.ppermute(down, SPACE, [(j, i) for i, j in upward])  3.9 us
    all_to_all x1, starting transfers between devices, per_device(): mine = lax.all_to_all(shares, SAME, 0, 0)  3.58 us
  transfers between devices with their start and end apart: 9, of which 6 were waited for; matrix products, arithmetic and copies ran while one was open for 0% of the time, Pallas kernels for 13%

profile of v8, /device:TPU:1, one launch (start us, length us, event | category | flops | bytes accessed | tf_op | source)
XLA Modules:
  0.0 70.4 jit_solution(12166723793822679324)
XLA Ops:
  0.6 0.0 copy-start.1
  0.6 1.0 %copy-done.1 = bf16[1,1,32,64,128]{4,3,2,1,0:T(8,128)(2,1)S(1)} copy-done((bf16[1,1,32,64,128]{4,3,2,1,0:T(8,128)(2,1)S(1)}, bf16[1,1,32,64,128]{4,3,2,1,0:T(8,128)(2,1)}, u32[]{:S(2)}) %copy-start.1) | copy-done | bytes 524312
  1.7 0.0 copy-start.2
  1.7 0.9 %copy-done.2 = bf16[1,1,16,64,128]{4,3,2,1,0:T(8,128)(2,1)S(1)} copy-done((bf16[1,1,16,64,128]{4,3,2,1,0:T(8,128)(2,1)S(1)}, bf16[1,1,16,64,128]{4,3,2,1,0:T(8,128)(2,1)}, u32[]{:S(2)}) %copy-start.2) | copy-done | bytes 262168
  2.6 1.3 %shard_map.93.pack_0 = bf16[3168,128]{1,0:T(8,128)(2,1)S(1)} custom-call(bf16[32,64,128]{2,1,0:T(8,128)(2,1)S(1)} %bitcast.12, bf16[16,64,128]{2,1,0:T(8,128)(2,1)S(1)} %bitcast.13), custom_call_target="tpu_custom_call" | custom-call | bytes 8388608 | tf_op jit(solution)/shard_map/pallas_call | solution.py:65
  3.9 2.0 %collective-permute-start.1 = (bf16[3168,128]{1,0:T(8,128)(2,1)S(1)}, bf16[3168,128]{1,0:T(8,128)(2,1)S(1)}, u32[]{:S(2)}, u32[]{:S(2)}) collective-permute-start(bf16[3168,128]{1,0:T(8,128)(2,1)S(1)} %shard_map.93.pack_0), channel_id=1, source_target_pairs={{1,0},{2,1},{3,2},{5,4},{6,5},{7,6},{9,8},{10,9},{11,10},{13,12},{... | collective-permute-start | bytes 2433032 | tf_op jit(solution)/shard_map/ppermute | solution.py:426
  5.9 4.5 %collective-permute-start = (bf16[3168,128]{1,0:T(8,128)(2,1)S(1)}, bf16[3168,128]{1,0:T(8,128)(2,1)S(1)}, u32[]{:S(2)}, u32[]{:S(2)}) collective-permute-start(bf16[3168,128]{1,0:T(8,128)(2,1)S(1)} %shard_map.93.pack_0), channel_id=1, source_target_pairs={{0,1},{1,2},{2,3},{4,5},{5,6},{6,7},{8,9},{9,10},{10,11},{12,13},{... | collective-permute-start | bytes 2433032 | tf_op jit(solution)/shard_map/ppermute | solution.py:426
  10.4 0.0 copy-start
  10.4 1.6 %copy-done = f32[1,524288]{1,0:T(1,128)S(1)} copy-done((f32[1,524288]{1,0:T(1,128)S(1)}, f32[1,524288]{1,0:T(1,128)}, u32[]{:S(2)}) %copy-start) | copy-done | bytes 2097176
  12.0 0.1 shard_map.94
  12.1 0.1 collective-permute-start.2
  12.1 1.9 %collective-permute-done.2.other = bf16[2048,128]{1,0:T(8,128)(2,1)S(1)} collective-permute-done((bf16[2048,128]{1,0:T(8,128)(2,1)S(1)}, bf16[2048,128]{1,0:T(8,128)(2,1)S(1)}, u32[]{:S(2)}, u32[]{:S(2)}) %collective-permute-start.2) | collective-permute-done | bytes 524320 | tf_op jit(solution)/shard_map/ppermute | solution.py:131
  14.0 0.9 %shard_map.95 = bf16[2048,128]{1,0:T(8,128)(2,1)} custom-call(f32[4096,128]{1,0:T(8,128)S(1)} %bitcast.11, bf16[2048,128]{1,0:T(8,128)(2,1)S(1)} %collective-permute-done.2.other), custom_call_target="tpu_custom_call" | custom-call | bytes 2097152 | tf_op jit(solution)/shard_map/pallas_call | solution.py:116
  15.0 5.6 %all-to-all-start = ((bf16[16,128,128]{2,1,0:T(8,128)(2,1)}), bf16[16,128,128]{2,1,0:T(8,128)(2,1)S(1)}, u32[]{:S(2)}, u32[]{:S(2)}) async-start(bf16[16,128,128]{2,1,0:T(8,128)(2,1)} %bitcast.4), calls=%async_computation | async-start | bytes 1048576 | tf_op jit(solution)/shard_map/all_to_all | solution.py:439
  20.6 0.0 collective-permute-done.1.pack_p
  20.6 0.0 collective-permute-done.pack_m
  20.6 0.0 copy-start.3
  20.6 1.0 %copy-done.3 = bf16[1,1,32,64,128]{4,3,2,1,0:T(8,128)(2,1)S(1)} copy-done((bf16[1,1,32,64,128]{4,3,2,1,0:T(8,128)(2,1)S(1)}, bf16[1,1,32,64,128]{4,3,2,1,0:T(8,128)(2,1)}, u32[]{:S(2)}) %copy-start.3) | copy-done | bytes 524312
  21.7 0.0 copy-start.8
  21.7 0.9 %copy-done.8 = bf16[3,3,3,32,32]{4,3,2,1,0:T(8,128)(2,1)S(1)} copy-done((bf16[3,3,3,32,32]{4,3,2,1,0:T(8,128)(2,1)S(1)}, bf16[3,3,3,32,32]{4,3,2,1,0:T(8,128)(2,1)}, u32[]{:S(2)}) %copy-start.8) | copy-done | bytes 55320
  22.6 0.0 copy-start.9
  22.6 0.9 %copy-done.9 = bf16[3,3,3,16,32]{4,3,2,1,0:T(8,128)(2,1)S(1)} copy-done((bf16[3,3,3,16,32]{4,3,2,1,0:T(8,128)(2,1)S(1)}, bf16[3,3,3,16,32]{4,3,2,1,0:T(8,128)(2,1)}, u32[]{:S(2)}) %copy-start.9) | copy-done | bytes 27672
  23.5 6.2 %shard_map.96 = (bf16[256,128]{1,0:T(8,128)(2,1)S(1)}, f32[256,128]{1,0:T(8,128)S(1)}, f32[1024,128]{1,0:T(8,128)S(1)}, bf16[1024,128]{1,0:T(8,128)(2,1)S(1)}, bf16[1024,128]{1,0:T(8,128)(2,1)S(1)}) custom-call(bf16[3168,128]{1,0:T(8,128)(2,1)S(1)} %collective-permute-done.pack_m, bf16[3168,128]{1,0:T(8,128)(2,1)S(1)} %shard_map.93.pack_0, ...), custom_call_target="tpu_custom_call" | custom-call | flops 10000000000 | bytes 41943040 | tf_op jit(solution)/shard_map/pallas_call | solution.py:245
  29.7 0.0 copy-start.4
  29.7 0.7 copy-done.4
  30.4 0.0 copy-start.6
  30.4 0.7 copy-done.6
  31.1 0.0 copy-start.7
  31.1 0.0 copy-start.5
  31.1 0.7 collective-permute-start.3
  31.7 0.9 %collective-permute-done.3.other = bf16[256,128]{1,0:T(8,128)(2,1)S(1)} collective-permute-done((bf16[256,128]{1,0:T(8,128)(2,1)S(1)}, bf16[256,128]{1,0:T(8,128)(2,1)S(1)}, u32[]{:S(2)}, u32[]{:S(2)}) %collective-permute-start.3) | collective-permute-done | bytes 65568 | tf_op jit(solution)/shard_map/ppermute | solution.py:131
  32.7 0.5 all-to-all-done.refs_0_
  33.2 12.3 %all_to_all.15.refs_1_ = bf16[16,16,128]{2,1,0:T(8,128)(2,1)S(1)} all-to-all(bf16[16,16,128]{2,1,0:T(8,128)(2,1)S(1)} %bitcast.14), channel_id=1, replica_groups=mesh['dp'=8,'slab'=2,'core'=2] {'dp','slab'}, dimensions={0} | all-to-all | bytes 131072 | tf_op jit(solution)/shard_map/all_to_all | solution.py:446
  45.5 1.0 %shard_map.98 = bf16[16,144,128]{2,1,0:T(8,128)(2,1)} custom-call(bf16[16,128,128]{2,1,0:T(8,128)(2,1)S(1)} %all-to-all-done.refs_0_, bf16[16,16,128]{2,1,0:T(8,128)(2,1)S(1)} %all_to_all.15.refs_1_), custom_call_target="tpu_custom_call" | custom-call | flops 262144 | bytes 786432 | tf_op jit(solution)/shard_map/pallas_call | solution.py:309
  46.5 3.6 %all-to-all-start.2 = ((bf16[16,144,128]{2,1,0:T(8,128)(2,1)}), bf16[16,144,128]{2,1,0:T(8,128)(2,1)S(1)}, u32[]{:S(2)}, u32[]{:S(2)}) async-start(bf16[16,144,128]{2,1,0:T(8,128)(2,1)} %shard_map.98), calls=%async_computation.2 | async-start | bytes 1179648 | tf_op jit(solution)/shard_map/all_to_all | solution.py:451
  50.1 0.0 copy-done.7
  50.1 5.7 %collective-permute-start.4 = (bf16[1024,128]{1,0:T(8,128)(2,1)S(1)}, bf16[1024,128]{1,0:T(8,128)(2,1)S(1)}, u32[]{:S(2)}, u32[]{:S(2)}) collective-permute-start(bf16[1024,128]{1,0:T(8,128)(2,1)S(1)} %copy-done.7), channel_id=1, source_target_pairs={{0,1},{1,2},{2,3},{4,5},{5,6},{6,7},{8,9},{9,10},{10,11},{12,13},{... | collective-permute-start | bytes 786440 | tf_op jit(solution)/shard_map/ppermute | solution.py:454
  55.8 0.0 copy-done.5
  55.9 1.9 %collective-permute-start.5 = (bf16[1024,128]{1,0:T(8,128)(2,1)S(1)}, bf16[1024,128]{1,0:T(8,128)(2,1)S(1)}, u32[]{:S(2)}, u32[]{:S(2)}) collective-permute-start(bf16[1024,128]{1,0:T(8,128)(2,1)S(1)} %copy-done.5), channel_id=1, source_target_pairs={{1,0},{2,1},{3,2},{5,4},{6,5},{7,6},{9,8},{10,9},{11,10},{13,12},{... | collective-permute-start | bytes 786440 | tf_op jit(solution)/shard_map/ppermute | solution.py:455
  57.8 3.4 %collective-permute-done.4.from_below = bf16[1024,128]{1,0:T(8,128)(2,1)S(1)} collective-permute-done((bf16[1024,128]{1,0:T(8,128)(2,1)S(1)}, bf16[1024,128]{1,0:T(8,128)(2,1)S(1)}, u32[]{:S(2)}, u32[]{:S(2)}) %collective-permute-start.4) | collective-permute-done | bytes 262176 | tf_op jit(solution)/shard_map/ppermute | solution.py:454
  61.2 3.9 %collective-permute-done.5.from_above = bf16[1024,128]{1,0:T(8,128)(2,1)S(1)} collective-permute-done((bf16[1024,128]{1,0:T(8,128)(2,1)S(1)}, bf16[1024,128]{1,0:T(8,128)(2,1)S(1)}, u32[]{:S(2)}, u32[]{:S(2)}) %collective-permute-start.5) | collective-permute-done | bytes 262176 | tf_op jit(solution)/shard_map/ppermute | solution.py:455
  65.1 1.0 %shard_map.99 = bf16[16,64,128]{2,1,0:T(8,128)(2,1)} custom-call(f32[1024,128]{1,0:T(8,128)S(1)} %get-tuple-element.34.own, bf16[1024,128]{1,0:T(8,128)(2,1)S(1)} %collective-permute-done.4.from_below, bf16[1024,128]{1,0:T(8,128)(2,1)S(1)} %collective-permute-done.5.from_above), custom_call_target="tpu_custom_call" | custom-call | flops 262144 | bytes 1048576 | tf_op jit(solution)/shard_map/pallas_call | solution.py:286
  66.1 0.0 all-to-all-done.2.refs_0_
  66.1 1.4 %collective-permute-start.6 = (bf16[16,144,128]{2,1,0:T(8,128)(2,1)S(1)}, bf16[16,144,128]{2,1,0:T(8,128)(2,1)S(1)}, u32[]{:S(2)}, u32[]{:S(2)}) collective-permute-start(bf16[16,144,128]{2,1,0:T(8,128)(2,1)S(1)} %all-to-all-done.2.refs_0_), channel_id=1, source_target_pairs={{0,1},{1,0},{2,3},{3,2},{4,5},{5,4},{6,7},{7,6},{8,9},{9,8},{10,11... | collective-permute-start | bytes 1769480 | tf_op jit(solution)/shard_map/ppermute | solution.py:131
  67.5 1.0 %shard_map.100.refs_2_ = f32[4096,128]{1,0:T(8,128)} custom-call(bf16[16,144,128]{2,1,0:T(8,128)(2,1)S(1)} %all-to-all-done.2.refs_0_), custom_call_target="tpu_custom_call" | custom-call | tf_op jit(solution)/shard_map/pallas_call | solution.py:393
  68.5 0.6 collective-permute-done.6.refs_1_
  69.1 1.3 %shard_map.101 = (f32[4096,128]{1,0:T(8,128)}, f32[432,32]{1,0:T(8,128)}, f32[864,32]{1,0:T(8,128)}) custom-call(bf16[16,144,128]{2,1,0:T(8,128)(2,1)S(1)} %all-to-all-done.2.refs_0_, bf16[16,144,128]{2,1,0:T(8,128)(2,1)S(1)} %collective-permute-done.6.refs_1_, f32[4096,128]{1,0:T(8,128)} %shard_map.100.refs_2_), custom_call_target="tpu_custom_call", output_to_operand_aliasing={{0}: (2, {})} | custom-call | tf_op jit(solution)/shard_map/pallas_call | solution.py:401
  (1 shorter events, 0.0 us)
Async XLA Ops:
  0.6 1.0 %copy-start.1 = (bf16[1,1,32,64,128]{4,3,2,1,0:T(8,128)(2,1)S(1)}, bf16[1,1,32,64,128]{4,3,2,1,0:T(8,128)(2,1)}, u32[]{:S(2)}) copy-start(bf16[1,1,32,64,128]{4,3,2,1,0:T(8,128)(2,1)} %param.8) | copy-start | bytes 1572868
  1.7 0.9 %copy-start.2 = (bf16[1,1,16,64,128]{4,3,2,1,0:T(8,128)(2,1)S(1)}, bf16[1,1,16,64,128]{4,3,2,1,0:T(8,128)(2,1)}, u32[]{:S(2)}) copy-start(bf16[1,1,16,64,128]{4,3,2,1,0:T(8,128)(2,1)} %param.6) | copy-start | bytes 786436
  3.9 16.7 %collective-permute-start.1 = (bf16[3168,128]{1,0:T(8,128)(2,1)S(1)}, bf16[3168,128]{1,0:T(8,128)(2,1)S(1)}, u32[]{:S(2)}, u32[]{:S(2)}) collective-permute-start(bf16[3168,128]{1,0:T(8,128)(2,1)S(1)} %shard_map.93.pack_0), channel_id=1, source_target_pairs={{1,0},{2,1},{3,2},{5,4},{6,5},{7,6},{9,8},{10,9},{11,10},{13,12},{... | collective-permute-start | bytes 2433032 | tf_op jit(solution)/shard_map/ppermute | solution.py:426
  5.9 14.7 %collective-permute-start = (bf16[3168,128]{1,0:T(8,128)(2,1)S(1)}, bf16[3168,128]{1,0:T(8,128)(2,1)S(1)}, u32[]{:S(2)}, u32[]{:S(2)}) collective-permute-start(bf16[3168,128]{1,0:T(8,128)(2,1)S(1)} %shard_map.93.pack_0), channel_id=1, source_target_pairs={{0,1},{1,2},{2,3},{4,5},{5,6},{6,7},{8,9},{9,10},{10,11},{12,13},{... | collective-permute-start | bytes 2433032 | tf_op jit(solution)/shard_map/ppermute | solution.py:426
  10.4 1.6 %copy-start = (f32[1,524288]{1,0:T(1,128)S(1)}, f32[1,524288]{1,0:T(1,128)}, u32[]{:S(2)}) copy-start(f32[1,524288]{1,0:T(1,128)} %param.11) | copy-start | bytes 6291460
  12.1 2.0 %collective-permute-start.2 = (bf16[2048,128]{1,0:T(8,128)(2,1)S(1)}, bf16[2048,128]{1,0:T(8,128)(2,1)S(1)}, u32[]{:S(2)}, u32[]{:S(2)}) collective-permute-start(bf16[2048,128]{1,0:T(8,128)(2,1)S(1)} %shard_map.94), channel_id=1, source_target_pairs={{0,1},{1,0},{2,3},{3,2},{4,5},{5,4},{6,7},{7,6},{8,9},{9,8},{10,11... | collective-permute-start | bytes 1572872 | tf_op jit(solution)/shard_map/ppermute | solution.py:131
  15.0 18.3 %all-to-all-start = ((bf16[16,128,128]{2,1,0:T(8,128)(2,1)}), bf16[16,128,128]{2,1,0:T(8,128)(2,1)S(1)}, u32[]{:S(2)}, u32[]{:S(2)}) async-start(bf16[16,128,128]{2,1,0:T(8,128)(2,1)} %bitcast.4), calls=%async_computation | async-start | bytes 1048576 | tf_op jit(solution)/shard_map/all_to_all | solution.py:439
  20.6 1.0 %copy-start.3 = (bf16[1,1,32,64,128]{4,3,2,1,0:T(8,128)(2,1)S(1)}, bf16[1,1,32,64,128]{4,3,2,1,0:T(8,128)(2,1)}, u32[]{:S(2)}) copy-start(bf16[1,1,32,64,128]{4,3,2,1,0:T(8,128)(2,1)} %param.7) | copy-start | bytes 1572868
  21.7 0.9 %copy-start.8 = (bf16[3,3,3,32,32]{4,3,2,1,0:T(8,128)(2,1)S(1)}, bf16[3,3,3,32,32]{4,3,2,1,0:T(8,128)(2,1)}, u32[]{:S(2)}) copy-start(bf16[3,3,3,32,32]{4,3,2,1,0:T(8,128)(2,1)} %two.1) | copy-start | bytes 165892
  22.6 0.9 %copy-start.9 = (bf16[3,3,3,16,32]{4,3,2,1,0:T(8,128)(2,1)S(1)}, bf16[3,3,3,16,32]{4,3,2,1,0:T(8,128)(2,1)}, u32[]{:S(2)}) copy-start(bf16[3,3,3,16,32]{4,3,2,1,0:T(8,128)(2,1)} %one.1) | copy-start | bytes 82948
  29.7 0.7 %copy-start.4 = (bf16[1024,128]{1,0:T(8,128)(2,1)}, bf16[1024,128]{1,0:T(8,128)(2,1)S(1)}, u32[]{:S(2)}) copy-start(bf16[1024,128]{1,0:T(8,128)(2,1)S(1)} %get-tuple-element.36) | copy-start | bytes 786436
  30.4 0.7 copy-start.6
  31.1 19.0 %copy-start.7 = (bf16[1024,128]{1,0:T(8,128)(2,1)S(1)}, bf16[1024,128]{1,0:T(8,128)(2,1)}, u32[]{:S(2)}) copy-start(bf16[1024,128]{1,0:T(8,128)(2,1)} %copy-done.6) | copy-start | bytes 786436
  31.1 24.8 %copy-start.5 = (bf16[1024,128]{1,0:T(8,128)(2,1)S(1)}, bf16[1024,128]{1,0:T(8,128)(2,1)}, u32[]{:S(2)}) copy-start(bf16[1024,128]{1,0:T(8,128)(2,1)} %copy-done.4) | copy-start | bytes 786436
  31.1 1.6 %collective-permute-start.3 = (bf16[256,128]{1,0:T(8,128)(2,1)S(1)}, bf16[256,128]{1,0:T(8,128)(2,1)S(1)}, u32[]{:S(2)}, u32[]{:S(2)}) collective-permute-start(bf16[256,128]{1,0:T(8,128)(2,1)S(1)} %get-tuple-element.29), channel_id=1, source_target_pairs={{0,1},{1,0},{2,3},{3,2},{4,5},{5,4},{6,7},{7,6},{8,9},{9,8},{10,11... | collective-permute-start | bytes 196616 | tf_op jit(solution)/shard_map/ppermute | solution.py:131
  46.5 19.6 %all-to-all-start.2 = ((bf16[16,144,128]{2,1,0:T(8,128)(2,1)}), bf16[16,144,128]{2,1,0:T(8,128)(2,1)S(1)}, u32[]{:S(2)}, u32[]{:S(2)}) async-start(bf16[16,144,128]{2,1,0:T(8,128)(2,1)} %shard_map.98), calls=%async_computation.2 | async-start | bytes 1179648 | tf_op jit(solution)/shard_map/all_to_all | solution.py:451
  50.1 11.1 %collective-permute-start.4 = (bf16[1024,128]{1,0:T(8,128)(2,1)S(1)}, bf16[1024,128]{1,0:T(8,128)(2,1)S(1)}, u32[]{:S(2)}, u32[]{:S(2)}) collective-permute-start(bf16[1024,128]{1,0:T(8,128)(2,1)S(1)} %copy-done.7), channel_id=1, source_target_pairs={{0,1},{1,2},{2,3},{4,5},{5,6},{6,7},{8,9},{9,10},{10,11},{12,13},{... | collective-permute-start | bytes 786440 | tf_op jit(solution)/shard_map/ppermute | solution.py:454
  55.9 9.2 %collective-permute-start.5 = (bf16[1024,128]{1,0:T(8,128)(2,1)S(1)}, bf16[1024,128]{1,0:T(8,128)(2,1)S(1)}, u32[]{:S(2)}, u32[]{:S(2)}) collective-permute-start(bf16[1024,128]{1,0:T(8,128)(2,1)S(1)} %copy-done.5), channel_id=1, source_target_pairs={{1,0},{2,1},{3,2},{5,4},{6,5},{7,6},{9,8},{10,9},{11,10},{13,12},{... | collective-permute-start | bytes 786440 | tf_op jit(solution)/shard_map/ppermute | solution.py:455
  66.1 3.0 %collective-permute-start.6 = (bf16[16,144,128]{2,1,0:T(8,128)(2,1)S(1)}, bf16[16,144,128]{2,1,0:T(8,128)(2,1)S(1)}, u32[]{:S(2)}, u32[]{:S(2)}) collective-permute-start(bf16[16,144,128]{2,1,0:T(8,128)(2,1)S(1)} %all-to-all-done.2.refs_0_), channel_id=1, source_target_pairs={{0,1},{1,0},{2,3},{3,2},{4,5},{5,4},{6,7},{7,6},{8,9},{9,8},{10,11... | collective-permute-start | bytes 1769480 | tf_op jit(solution)/shard_map/ppermute | solution.py:131

commit v9 on v8

--- a/solution.py
+++ b/solution.py
@@ -80,7 +80,7 @@
     lax.fori_loop(0, count, one, 0)
 
 
-def cast_kernel(src, out):
+def cast_kernel(src, after, out):
     rows = out.shape[0]
     start = (1 - lax.axis_index("core")) * rows
 
@@ -91,13 +91,16 @@
     in_steps(cast, rows)
 
 
-def cast(value):
-    return vmem_call(
+def cast(value, after):
+    spec = pl.BlockSpec(memory_space=pltpu.VMEM)
+    return pl.pallas_call(
         cast_kernel,
-        jax.ShapeDtypeStruct((value.shape[0] // 2, LANES), BF16),
-        (),
-        pl.CostEstimate(flops=0, bytes_accessed=4 * value.size, transcendentals=0),
-    )(value)
+        out_shape=jax.ShapeDtypeStruct((value.shape[0] // 2, LANES), BF16),
+        in_specs=[spec, pl.BlockSpec(memory_space=pl.ANY)],
+        out_specs=spec,
+        compiler_params=pltpu.CompilerParams(vmem_limit_bytes=24 * 2**20),
+        cost_estimate=pl.CostEstimate(flops=0, bytes_accessed=4 * value.size, transcendentals=0),
+    )(value, after)
 
 
 def add_kernel(src, other, out):
@@ -432,9 +435,9 @@
     length = grad_bucket.shape[1]
     bucket = grad_bucket.reshape(length // LANES, LANES)
     packed = pack(out_cot[0, 0], volume_in[0, 0])
-    packed, bucket = lax.optimization_barrier((packed, bucket))
+    packed, send = lax.optimization_barrier((packed, cast(bucket, packed)))
     below, above = halos(packed)
-    half = add(bucket, swapped(cast(bucket)))
+    half = add(bucket, swapped(send))
     act, half = lax.optimization_barrier((hidden_act[0, 0], half))
     parts = lax.all_to_all(half.reshape(copies, -1, LANES), SAME, 0, 0)
 

time: 71.3 us -> 72.7 us (1.020)
    all_to_all x1, starting transfers between devices: 5.63 us -> 6.57 us  [per_device(): parts = lax.all_to_all(half.reshape(copies, -1, LANES), SAME, 0, 0)]
    ppermute x1, waiting for transfers between devices: 3.4 us -> 4.24 us  [per_device(): from_below = lax.ppermute(up, SPACE, upward)]
    unnamed x20 -> x22, local copies, waits for them, and re-layouts: 7.85 us -> 7.85 us
where the time goes in v9:
time: 72.7 us; the launch traced here: 71.8 us
  starting transfers between devices  26 us (36%)
  Pallas kernels  12.8 us (18%)
  blocking collectives  12.4 us (17%)
  waiting for transfers between devices  11.9 us (16%)
  local copies, waits for them, and re-layouts  7.85 us (11%)
  between operations  0.79 us (1%)
    all_to_all x1, blocking collectives, per_device(): terms = lax.all_to_all(terms.reshape(copies, -1, LANES), SAME, 0, 0)  12.4 us
    unnamed x22, local copies, waits for them, and re-layouts  7.85 us
    ppermute x2, starting transfers between devices, halos(): return (lax.ppermute(value, SPACE, up), lax.ppermute(value, SPACE, down))  6.59 us
    all_to_all x1, starting transfers between devices, per_device(): parts = lax.all_to_all(half.reshape(copies, -1, LANES), SAME, 0, 0)  6.57 us
    pallas_call x1, Pallas kernels, compute(): vmem_call(compute_kernel, (jax.ShapeDtypeStruct((rows // 2, LANES), BF16)...  6.15 us
    ppermute x1, starting transfers between devices, per_device(): from_below = lax.ppermute(up, SPACE, upward)  5.43 us
    ppermute x1, waiting for transfers between devices, per_device(): from_below = lax.ppermute(up, SPACE, upward)  4.24 us
    all_to_all x1, starting transfers between devices, per_device(): mine = lax.all_to_all(shares, SAME, 0, 0)  3.58 us
  transfers between devices with their start and end apart: 9, of which 6 were waited for; matrix products, arithmetic and copies ran while one was open for 0% of the time, Pallas kernels for 13%

profile of v9, /device:TPU:1, one launch (start us, length us, event | category | flops | bytes accessed | tf_op | source)
XLA Modules:
  0.0 71.8 jit_solution(5521294456310272019)
XLA Ops:
  0.6 0.0 copy-start.2
  0.6 1.0 %copy-done.2 = bf16[1,1,32,64,128]{4,3,2,1,0:T(8,128)(2,1)S(1)} copy-done((bf16[1,1,32,64,128]{4,3,2,1,0:T(8,128)(2,1)S(1)}, bf16[1,1,32,64,128]{4,3,2,1,0:T(8,128)(2,1)}, u32[]{:S(2)}) %copy-start.2) | copy-done | bytes 524312
  1.7 0.0 copy-start.3
  1.7 0.9 %copy-done.3 = bf16[1,1,16,64,128]{4,3,2,1,0:T(8,128)(2,1)S(1)} copy-done((bf16[1,1,16,64,128]{4,3,2,1,0:T(8,128)(2,1)S(1)}, bf16[1,1,16,64,128]{4,3,2,1,0:T(8,128)(2,1)}, u32[]{:S(2)}) %copy-start.3) | copy-done | bytes 262168
  2.6 1.3 %shard_map.93.after.pack_0 = bf16[3168,128]{1,0:T(8,128)(2,1)S(1)} custom-call(bf16[32,64,128]{2,1,0:T(8,128)(2,1)S(1)} %bitcast.12, bf16[16,64,128]{2,1,0:T(8,128)(2,1)S(1)} %bitcast.13), custom_call_target="tpu_custom_call" | custom-call | bytes 8388608 | tf_op jit(solution)/shard_map/pallas_call | solution.py:65
  3.9 0.0 copy-start
  3.9 1.6 %copy-done = f32[1,524288]{1,0:T(1,128)S(1)} copy-done((f32[1,524288]{1,0:T(1,128)S(1)}, f32[1,524288]{1,0:T(1,128)}, u32[]{:S(2)}) %copy-start) | copy-done | bytes 2097176
  5.5 0.0 copy-start.1
  5.5 0.1 shard_map.94
  5.6 2.1 %collective-permute-start.1 = (bf16[3168,128]{1,0:T(8,128)(2,1)S(1)}, bf16[3168,128]{1,0:T(8,128)(2,1)S(1)}, u32[]{:S(2)}, u32[]{:S(2)}) collective-permute-start(bf16[3168,128]{1,0:T(8,128)(2,1)S(1)} %shard_map.93.after.pack_0), channel_id=1, source_target_pairs={{1,0},{2,1},{3,2},{5,4},{6,5},{7,6},{9,8},{10,9},{11,10},{13,12},{... | collective-permute-start | bytes 2433032 | tf_op jit(solution)/shard_map/ppermute | solution.py:429
  7.7 4.5 %collective-permute-start = (bf16[3168,128]{1,0:T(8,128)(2,1)S(1)}, bf16[3168,128]{1,0:T(8,128)(2,1)S(1)}, u32[]{:S(2)}, u32[]{:S(2)}) collective-permute-start(bf16[3168,128]{1,0:T(8,128)(2,1)S(1)} %shard_map.93.after.pack_0), channel_id=1, source_target_pairs={{0,1},{1,2},{2,3},{4,5},{5,6},{6,7},{8,9},{9,10},{10,11},{12,13},{... | collective-permute-start | bytes 2433032 | tf_op jit(solution)/shard_map/ppermute | solution.py:429
  12.2 0.1 collective-permute-start.2
  12.3 1.9 %collective-permute-done.2.other = bf16[2048,128]{1,0:T(8,128)(2,1)S(1)} collective-permute-done((bf16[2048,128]{1,0:T(8,128)(2,1)S(1)}, bf16[2048,128]{1,0:T(8,128)(2,1)S(1)}, u32[]{:S(2)}, u32[]{:S(2)}) %collective-permute-start.2) | collective-permute-done | bytes 524320 | tf_op jit(solution)/shard_map/ppermute | solution.py:134
  14.2 0.0 copy-done.1
  14.2 1.0 %shard_map.95 = bf16[2048,128]{1,0:T(8,128)(2,1)} custom-call(f32[4096,128]{1,0:T(8,128)S(1)} %bitcast.11, bf16[2048,128]{1,0:T(8,128)(2,1)S(1)} %collective-permute-done.2.other), custom_call_target="tpu_custom_call" | custom-call | bytes 2097152 | tf_op jit(solution)/shard_map/pallas_call | solution.py:119
  15.1 6.6 %all-to-all-start = ((bf16[16,128,128]{2,1,0:T(8,128)(2,1)}), bf16[16,128,128]{2,1,0:T(8,128)(2,1)S(1)}, u32[]{:S(2)}, u32[]{:S(2)}) async-start(bf16[16,128,128]{2,1,0:T(8,128)(2,1)} %bitcast.4), calls=%async_computation | async-start | bytes 1048576 | tf_op jit(solution)/shard_map/all_to_all | solution.py:442
  21.7 0.0 collective-permute-done.1.pack_p
  21.7 0.0 collective-permute-done.pack_m
  21.7 0.0 copy-start.4
  21.7 1.0 %copy-done.4 = bf16[1,1,32,64,128]{4,3,2,1,0:T(8,128)(2,1)S(1)} copy-done((bf16[1,1,32,64,128]{4,3,2,1,0:T(8,128)(2,1)S(1)}, bf16[1,1,32,64,128]{4,3,2,1,0:T(8,128)(2,1)}, u32[]{:S(2)}) %copy-start.4) | copy-done | bytes 524312
  22.8 0.0 copy-start.9
  22.8 0.9 %copy-done.9 = bf16[3,3,3,32,32]{4,3,2,1,0:T(8,128)(2,1)S(1)} copy-done((bf16[3,3,3,32,32]{4,3,2,1,0:T(8,128)(2,1)S(1)}, bf16[3,3,3,32,32]{4,3,2,1,0:T(8,128)(2,1)}, u32[]{:S(2)}) %copy-start.9) | copy-done | bytes 55320
  23.7 0.0 copy-start.10
  23.7 0.9 %copy-done.10 = bf16[3,3,3,16,32]{4,3,2,1,0:T(8,128)(2,1)S(1)} copy-done((bf16[3,3,3,16,32]{4,3,2,1,0:T(8,128)(2,1)S(1)}, bf16[3,3,3,16,32]{4,3,2,1,0:T(8,128)(2,1)}, u32[]{:S(2)}) %copy-start.10) | copy-done | bytes 27672
  24.6 6.2 %shard_map.96 = (bf16[256,128]{1,0:T(8,128)(2,1)S(1)}, f32[256,128]{1,0:T(8,128)S(1)}, f32[1024,128]{1,0:T(8,128)S(1)}, bf16[1024,128]{1,0:T(8,128)(2,1)S(1)}, bf16[1024,128]{1,0:T(8,128)(2,1)S(1)}) custom-call(bf16[3168,128]{1,0:T(8,128)(2,1)S(1)} %collective-permute-done.pack_m, bf16[3168,128]{1,0:T(8,128)(2,1)S(1)} %shard_map.93.after.pack_0, ...), custom_call_target="tpu_custom_call" | custom-call | flops 10000000000 | bytes 41943040 | tf_op jit(solution)/shard_map/pallas_call | solution.py:248
  30.8 0.0 copy-start.5
  30.8 0.7 copy-done.5
  31.5 0.0 copy-start.7
  31.5 0.7 copy-done.7
  32.2 0.0 copy-start.8
  32.2 0.0 copy-start.6
  32.2 0.4 collective-permute-start.3
  32.6 0.9 %collective-permute-done.3.other = bf16[256,128]{1,0:T(8,128)(2,1)S(1)} collective-permute-done((bf16[256,128]{1,0:T(8,128)(2,1)S(1)}, bf16[256,128]{1,0:T(8,128)(2,1)S(1)}, u32[]{:S(2)}, u32[]{:S(2)}) %collective-permute-start.3) | collective-permute-done | bytes 65568 | tf_op jit(solution)/shard_map/ppermute | solution.py:134
  33.6 1.0 %all-to-all-done.refs_0_ = bf16[16,128,128]{2,1,0:T(8,128)(2,1)S(1)} async-done(((bf16[16,128,128]{2,1,0:T(8,128)(2,1)}), bf16[16,128,128]{2,1,0:T(8,128)(2,1)S(1)}, u32[]{:S(2)}, u32[]{:S(2)}) %all-to-all-start) | async-done | bytes 524320 | tf_op jit(solution)/shard_map/all_to_all | solution.py:442
  34.5 12.4 %all_to_all.15.refs_1_ = bf16[16,16,128]{2,1,0:T(8,128)(2,1)S(1)} all-to-all(bf16[16,16,128]{2,1,0:T(8,128)(2,1)S(1)} %bitcast.14), channel_id=1, replica_groups=mesh['dp'=8,'slab'=2,'core'=2] {'dp','slab'}, dimensions={0} | all-to-all | bytes 131072 | tf_op jit(solution)/shard_map/all_to_all | solution.py:449
  46.9 1.0 %shard_map.98 = bf16[16,144,128]{2,1,0:T(8,128)(2,1)} custom-call(bf16[16,128,128]{2,1,0:T(8,128)(2,1)S(1)} %all-to-all-done.refs_0_, bf16[16,16,128]{2,1,0:T(8,128)(2,1)S(1)} %all_to_all.15.refs_1_), custom_call_target="tpu_custom_call" | custom-call | flops 262144 | bytes 786432 | tf_op jit(solution)/shard_map/pallas_call | solution.py:312
  47.9 3.6 %all-to-all-start.2 = ((bf16[16,144,128]{2,1,0:T(8,128)(2,1)}), bf16[16,144,128]{2,1,0:T(8,128)(2,1)S(1)}, u32[]{:S(2)}, u32[]{:S(2)}) async-start(bf16[16,144,128]{2,1,0:T(8,128)(2,1)} %shard_map.98), calls=%async_computation.2 | async-start | bytes 1179648 | tf_op jit(solution)/shard_map/all_to_all | solution.py:454
  51.5 0.0 copy-done.8
  51.5 5.4 %collective-permute-start.4 = (bf16[1024,128]{1,0:T(8,128)(2,1)S(1)}, bf16[1024,128]{1,0:T(8,128)(2,1)S(1)}, u32[]{:S(2)}, u32[]{:S(2)}) collective-permute-start(bf16[1024,128]{1,0:T(8,128)(2,1)S(1)} %copy-done.8), channel_id=1, source_target_pairs={{0,1},{1,2},{2,3},{4,5},{5,6},{6,7},{8,9},{9,10},{10,11},{12,13},{... | collective-permute-start | bytes 786440 | tf_op jit(solution)/shard_map/ppermute | solution.py:457
  57.0 0.0 copy-done.6
  57.0 1.9 %collective-permute-start.5 = (bf16[1024,128]{1,0:T(8,128)(2,1)S(1)}, bf16[1024,128]{1,0:T(8,128)(2,1)S(1)}, u32[]{:S(2)}, u32[]{:S(2)}) collective-permute-start(bf16[1024,128]{1,0:T(8,128)(2,1)S(1)} %copy-done.6), channel_id=1, source_target_pairs={{1,0},{2,1},{3,2},{5,4},{6,5},{7,6},{9,8},{10,9},{11,10},{13,12},{... | collective-permute-start | bytes 786440 | tf_op jit(solution)/shard_map/ppermute | solution.py:458
  58.9 4.2 %collective-permute-done.4.from_below = bf16[1024,128]{1,0:T(8,128)(2,1)S(1)} collective-permute-done((bf16[1024,128]{1,0:T(8,128)(2,1)S(1)}, bf16[1024,128]{1,0:T(8,128)(2,1)S(1)}, u32[]{:S(2)}, u32[]{:S(2)}) %collective-permute-start.4) | collective-permute-done | bytes 262176 | tf_op jit(solution)/shard_map/ppermute | solution.py:457
  63.1 3.3 %collective-permute-done.5.from_above = bf16[1024,128]{1,0:T(8,128)(2,1)S(1)} collective-permute-done((bf16[1024,128]{1,0:T(8,128)(2,1)S(1)}, bf16[1024,128]{1,0:T(8,128)(2,1)S(1)}, u32[]{:S(2)}, u32[]{:S(2)}) %collective-permute-start.5) | collective-permute-done | bytes 262176 | tf_op jit(solution)/shard_map/ppermute | solution.py:458
  66.5 1.0 %shard_map.99 = bf16[16,64,128]{2,1,0:T(8,128)(2,1)} custom-call(f32[1024,128]{1,0:T(8,128)S(1)} %get-tuple-element.34.own, bf16[1024,128]{1,0:T(8,128)(2,1)S(1)} %collective-permute-done.4.from_below, bf16[1024,128]{1,0:T(8,128)(2,1)S(1)} %collective-permute-done.5.from_above), custom_call_target="tpu_custom_call" | custom-call | flops 262144 | bytes 1048576 | tf_op jit(solution)/shard_map/pallas_call | solution.py:289
  67.4 0.0 all-to-all-done.2.refs_0_
  67.4 1.4 %collective-permute-start.6 = (bf16[16,144,128]{2,1,0:T(8,128)(2,1)S(1)}, bf16[16,144,128]{2,1,0:T(8,128)(2,1)S(1)}, u32[]{:S(2)}, u32[]{:S(2)}) collective-permute-start(bf16[16,144,128]{2,1,0:T(8,128)(2,1)S(1)} %all-to-all-done.2.refs_0_), channel_id=1, source_target_pairs={{0,1},{1,0},{2,3},{3,2},{4,5},{5,4},{6,7},{7,6},{8,9},{9,8},{10,11... | collective-permute-start | bytes 1769480 | tf_op jit(solution)/shard_map/ppermute | solution.py:134
  68.9 1.0 %shard_map.100.refs_2_ = f32[4096,128]{1,0:T(8,128)} custom-call(bf16[16,144,128]{2,1,0:T(8,128)(2,1)S(1)} %all-to-all-done.2.refs_0_), custom_call_target="tpu_custom_call" | custom-call | tf_op jit(solution)/shard_map/pallas_call | solution.py:396
  69.9 0.6 collective-permute-done.6.refs_1_
  70.5 1.3 %shard_map.101 = (f32[4096,128]{1,0:T(8,128)}, f32[432,32]{1,0:T(8,128)}, f32[864,32]{1,0:T(8,128)}) custom-call(bf16[16,144,128]{2,1,0:T(8,128)(2,1)S(1)} %all-to-all-done.2.refs_0_, bf16[16,144,128]{2,1,0:T(8,128)(2,1)S(1)} %collective-permute-done.6.refs_1_, f32[4096,128]{1,0:T(8,128)} %shard_map.100.refs_2_), custom_call_target="tpu_custom_call", output_to_operand_aliasing={{0}: (2, {})} | custom-call | tf_op jit(solution)/shard_map/pallas_call | solution.py:404
  (1 shorter events, 0.0 us)
Async XLA Ops:
  0.6 1.0 %copy-start.2 = (bf16[1,1,32,64,128]{4,3,2,1,0:T(8,128)(2,1)S(1)}, bf16[1,1,32,64,128]{4,3,2,1,0:T(8,128)(2,1)}, u32[]{:S(2)}) copy-start(bf16[1,1,32,64,128]{4,3,2,1,0:T(8,128)(2,1)} %param.8) | copy-start | bytes 1572868
  1.7 0.9 %copy-start.3 = (bf16[1,1,16,64,128]{4,3,2,1,0:T(8,128)(2,1)S(1)}, bf16[1,1,16,64,128]{4,3,2,1,0:T(8,128)(2,1)}, u32[]{:S(2)}) copy-start(bf16[1,1,16,64,128]{4,3,2,1,0:T(8,128)(2,1)} %param.6) | copy-start | bytes 786436
  3.9 1.6 %copy-start = (f32[1,524288]{1,0:T(1,128)S(1)}, f32[1,524288]{1,0:T(1,128)}, u32[]{:S(2)}) copy-start(f32[1,524288]{1,0:T(1,128)} %param.11) | copy-start | bytes 6291460
  5.5 8.7 %copy-start.1 = (f32[1,524288]{1,0:T(1,128)S(1)}, f32[1,524288]{1,0:T(1,128)}, u32[]{:S(2)}) copy-start(f32[1,524288]{1,0:T(1,128)} %param.11) | copy-start | bytes 6291460
  5.6 16.1 %collective-permute-start.1 = (bf16[3168,128]{1,0:T(8,128)(2,1)S(1)}, bf16[3168,128]{1,0:T(8,128)(2,1)S(1)}, u32[]{:S(2)}, u32[]{:S(2)}) collective-permute-start(bf16[3168,128]{1,0:T(8,128)(2,1)S(1)} %shard_map.93.after.pack_0), channel_id=1, source_target_pairs={{1,0},{2,1},{3,2},{5,4},{6,5},{7,6},{9,8},{10,9},{11,10},{13,12},{... | collective-permute-start | bytes 2433032 | tf_op jit(solution)/shard_map/ppermute | solution.py:429
  7.7 14.0 %collective-permute-start = (bf16[3168,128]{1,0:T(8,128)(2,1)S(1)}, bf16[3168,128]{1,0:T(8,128)(2,1)S(1)}, u32[]{:S(2)}, u32[]{:S(2)}) collective-permute-start(bf16[3168,128]{1,0:T(8,128)(2,1)S(1)} %shard_map.93.after.pack_0), channel_id=1, source_target_pairs={{0,1},{1,2},{2,3},{4,5},{5,6},{6,7},{8,9},{9,10},{10,11},{12,13},{... | collective-permute-start | bytes 2433032 | tf_op jit(solution)/shard_map/ppermute | solution.py:429
  12.2 2.0 %collective-permute-start.2 = (bf16[2048,128]{1,0:T(8,128)(2,1)S(1)}, bf16[2048,128]{1,0:T(8,128)(2,1)S(1)}, u32[]{:S(2)}, u32[]{:S(2)}) collective-permute-start(bf16[2048,128]{1,0:T(8,128)(2,1)S(1)} %shard_map.94), channel_id=1, source_target_pairs={{0,1},{1,0},{2,3},{3,2},{4,5},{5,4},{6,7},{7,6},{8,9},{9,8},{10,11... | collective-permute-start | bytes 1572872 | tf_op jit(solution)/shard_map/ppermute | solution.py:134
  15.1 19.4 %all-to-all-start = ((bf16[16,128,128]{2,1,0:T(8,128)(2,1)}), bf16[16,128,128]{2,1,0:T(8,128)(2,1)S(1)}, u32[]{:S(2)}, u32[]{:S(2)}) async-start(bf16[16,128,128]{2,1,0:T(8,128)(2,1)} %bitcast.4), calls=%async_computation | async-start | bytes 1048576 | tf_op jit(solution)/shard_map/all_to_all | solution.py:442
  21.7 1.0 %copy-start.4 = (bf16[1,1,32,64,128]{4,3,2,1,0:T(8,128)(2,1)S(1)}, bf16[1,1,32,64,128]{4,3,2,1,0:T(8,128)(2,1)}, u32[]{:S(2)}) copy-start(bf16[1,1,32,64,128]{4,3,2,1,0:T(8,128)(2,1)} %param.7) | copy-start | bytes 1572868
  22.8 0.9 %copy-start.9 = (bf16[3,3,3,32,32]{4,3,2,1,0:T(8,128)(2,1)S(1)}, bf16[3,3,3,32,32]{4,3,2,1,0:T(8,128)(2,1)}, u32[]{:S(2)}) copy-start(bf16[3,3,3,32,32]{4,3,2,1,0:T(8,128)(2,1)} %two.1) | copy-start | bytes 165892
  23.7 0.9 %copy-start.10 = (bf16[3,3,3,16,32]{4,3,2,1,0:T(8,128)(2,1)S(1)}, bf16[3,3,3,16,32]{4,3,2,1,0:T(8,128)(2,1)}, u32[]{:S(2)}) copy-start(bf16[3,3,3,16,32]{4,3,2,1,0:T(8,128)(2,1)} %one.1) | copy-start | bytes 82948
  30.8 0.7 copy-start.5
  31.5 0.7 copy-start.7
  32.2 19.3 %copy-start.8 = (bf16[1024,128]{1,0:T(8,128)(2,1)S(1)}, bf16[1024,128]{1,0:T(8,128)(2,1)}, u32[]{:S(2)}) copy-start(bf16[1024,128]{1,0:T(8,128)(2,1)} %copy-done.7) | copy-start | bytes 786436
  32.2 24.8 %copy-start.6 = (bf16[1024,128]{1,0:T(8,128)(2,1)S(1)}, bf16[1024,128]{1,0:T(8,128)(2,1)}, u32[]{:S(2)}) copy-start(bf16[1024,128]{1,0:T(8,128)(2,1)} %copy-done.5) | copy-start | bytes 786436
  32.2 1.3 %collective-permute-start.3 = (bf16[256,128]{1,0:T(8,128)(2,1)S(1)}, bf16[256,128]{1,0:T(8,128)(2,1)S(1)}, u32[]{:S(2)}, u32[]{:S(2)}) collective-permute-start(bf16[256,128]{1,0:T(8,128)(2,1)S(1)} %get-tuple-element.29), channel_id=1, source_target_pairs={{0,1},{1,0},{2,3},{3,2},{4,5},{5,4},{6,7},{7,6},{8,9},{9,8},{10,11... | collective-permute-start | bytes 196616 | tf_op jit(solution)/shard_map/ppermute | solution.py:134
  47.9 19.5 %all-to-all-start.2 = ((bf16[16,144,128]{2,1,0:T(8,128)(2,1)}), bf16[16,144,128]{2,1,0:T(8,128)(2,1)S(1)}, u32[]{:S(2)}, u32[]{:S(2)}) async-start(bf16[16,144,128]{2,1,0:T(8,128)(2,1)} %shard_map.98), calls=%async_computation.2 | async-start | bytes 1179648 | tf_op jit(solution)/shard_map/all_to_all | solution.py:454
  51.5 11.6 %collective-permute-start.4 = (bf16[1024,128]{1,0:T(8,128)(2,1)S(1)}, bf16[1024,128]{1,0:T(8,128)(2,1)S(1)}, u32[]{:S(2)}, u32[]{:S(2)}) collective-permute-start(bf16[1024,128]{1,0:T(8,128)(2,1)S(1)} %copy-done.8), channel_id=1, source_target_pairs={{0,1},{1,2},{2,3},{4,5},{5,6},{6,7},{8,9},{9,10},{10,11},{12,13},{... | collective-permute-start | bytes 786440 | tf_op jit(solution)/shard_map/ppermute | solution.py:457
  57.0 9.5 %collective-permute-start.5 = (bf16[1024,128]{1,0:T(8,128)(2,1)S(1)}, bf16[1024,128]{1,0:T(8,128)(2,1)S(1)}, u32[]{:S(2)}, u32[]{:S(2)}) collective-permute-start(bf16[1024,128]{1,0:T(8,128)(2,1)S(1)} %copy-done.6), channel_id=1, source_target_pairs={{1,0},{2,1},{3,2},{5,4},{6,5},{7,6},{9,8},{10,9},{11,10},{13,12},{... | collective-permute-start | bytes 786440 | tf_op jit(solution)/shard_map/ppermute | solution.py:458
  67.4 3.1 %collective-permute-start.6 = (bf16[16,144,128]{2,1,0:T(8,128)(2,1)S(1)}, bf16[16,144,128]{2,1,0:T(8,128)(2,1)S(1)}, u32[]{:S(2)}, u32[]{:S(2)}) collective-permute-start(bf16[16,144,128]{2,1,0:T(8,128)(2,1)S(1)} %all-to-all-done.2.refs_0_), channel_id=1, source_target_pairs={{0,1},{1,0},{2,3},{3,2},{4,5},{5,4},{6,7},{7,6},{8,9},{9,8},{10,11... | collective-permute-start | bytes 1769480 | tf_op jit(solution)/shard_map/ppermute | solution.py:134

commit v10 on v9

--- a/solution.py
+++ b/solution.py
@@ -7,9 +7,10 @@
 from jax.experimental.pallas import tpu as pltpu
 from jax.sharding import Mesh, PartitionSpec as P
 
-SPACE = ("slab", "core")
-SAME = ("dp", "slab")
-EVERY = ("dp", "slab", "core")
+SPACE = ("y", "core")
+COLUMN = ("z", "y")
+SAME = ("x", "z", "y")
+EVERY = ("z", "x", "y", "core")
 GROUP = 8
 LANES = 128
 BF16 = jnp.bfloat16
@@ -103,25 +104,51 @@
     )(value, after)
 
 
-def add_kernel(src, other, out):
-    rows = out.shape[0]
-    start = lax.axis_index("core") * rows if src.shape[0] > rows else 0
+def add_kernel(src, other, send, keep):
+    half, rows = (other.shape[0], send.shape[0])
+    start = lax.axis_index("core") * half
+    mine = lax.axis_index("x") * rows
+    theirs = rows - mine
+
+    def total(at, step):
+        value = src[pl.ds(pl.multiple_of(start + at, 16), step), :]
+        return value + other[pl.ds(pl.multiple_of(at, 16), step), :].astype(F32)
 
     def add(at, step):
-        value = src[pl.ds(pl.multiple_of(start + at, 16), step), :]
-        at = pl.ds(pl.multiple_of(at, 16), step)
-        out[at, :] = (value + other[at, :].astype(F32)).astype(out.dtype)
+        to = pl.ds(pl.multiple_of(at, 16), step)
+        send[to, :] = total(theirs + at, step).astype(send.dtype)
+        keep[to, :] = total(mine + at, step)
 
     in_steps(add, rows)
 
 
 def add(value, other):
+    rows = other.shape[0] // 2
     return vmem_call(
         add_kernel,
-        jax.ShapeDtypeStruct(other.shape, BF16),
+        (jax.ShapeDtypeStruct((rows, LANES), BF16), jax.ShapeDtypeStruct((rows, LANES), F32)),
         (),
         pl.CostEstimate(flops=0, bytes_accessed=4 * value.size, transcendentals=0),
     )(value, other)
+
+
+def combine_kernel(keep, other, terms, more, out):
+    height, extra = (keep.shape[0] // out.shape[0], terms.shape[0] // out.shape[0])
+    for n in range(out.shape[0]):
+        at = slice(n * height, (n + 1) * height)
+        out[n, 0:height, :] = (keep[at, :] + other[at, :].astype(F32)).astype(out.dtype)
+        at = slice(n * extra, (n + 1) * extra)
+        out[n, height : height + extra, :] = (terms[at, :] + more[at, :].astype(F32)).astype(out.dtype)
+
+
+def combine(keep, other, terms, more, parts):
+    rows = (keep.shape[0] + terms.shape[0]) // parts
+    return vmem_call(
+        combine_kernel,
+        jax.ShapeDtypeStruct((parts, rows, LANES), BF16),
+        (),
+        pl.CostEstimate(flops=0, bytes_accessed=8 * keep.size, transcendentals=0),
+    )(keep, other, terms, more)
 
 
 def split_to(total, mine, send, keep):
@@ -130,8 +157,8 @@
     send[...] = total[pl.ds(pl.multiple_of((1 - mine) * half, 16), half), :].astype(send.dtype)
 
 
-def swapped(value):
-    return lax.ppermute(value, "core", [(0, 1), (1, 0)])
+def swapped(value, axis="core"):
+    return lax.ppermute(value, axis, [(0, 1), (1, 0)])
 
 
 def compute_kernel(
@@ -294,27 +321,26 @@
     )(own, from_below, from_above)
 
 
-def share_kernel(scale, bucket, terms, out):
-    total = jnp.sum(bucket[...].astype(F32), axis=0).astype(BF16)
-    grads = (jnp.sum(terms[...].astype(F32), axis=0) * scale).astype(BF16)
-    height = total.shape[0]
+def share_kernel(scale, height, parts, out):
+    total = jnp.sum(parts[:, 0:height, :].astype(F32), axis=0).astype(BF16)
+    rows = parts.shape[1]
+    grads = (jnp.sum(parts[:, height:rows, :].astype(F32), axis=0) * scale).astype(BF16)
 
     def write(n, carry):
         out[n, 0:height, :] = total
-        out[n, height : height + grads.shape[0], :] = grads
+        out[n, height:rows, :] = grads
         return carry
 
     lax.fori_loop(0, out.shape[0], write, 0)
 
 
-def share(bucket, terms, scale, copies):
-    rows = bucket.shape[1] + terms.shape[1]
+def share(parts, height, scale, copies):
     return vmem_call(
-        lambda *refs: share_kernel(scale, *refs),
-        jax.ShapeDtypeStruct((copies, rows, LANES), BF16),
+        lambda *refs: share_kernel(scale, height, *refs),
+        jax.ShapeDtypeStruct((copies,) + parts.shape[1:], BF16),
         (),
-        pl.CostEstimate(flops=bucket.size, bytes_accessed=3 * bucket.size, transcendentals=0),
-    )(bucket, terms)
+        pl.CostEstimate(flops=parts.size, bytes_accessed=6 * parts.size, transcendentals=0),
+    )(parts)
 
 
 def place(source, height, which, bucket, buffer, sems):
@@ -348,13 +374,12 @@
     me = lax.axis_index("core")
     sent = place(other, height, 1 - me, bucket, buffer, sems)
 
-    def unpack(q, carry):
+    column = copies // 2
+    for q in range(column):
         for source, which in ((mine, me), (other, 1 - me)):
-            at = pl.multiple_of((which * copies + q) * extra, 8)
-            raw[pl.ds(at, extra), :] = source[q, height:rows, :].astype(F32)
-        return carry
-
-    lax.fori_loop(0, copies, unpack, 0, unroll=4)
+            at = pl.multiple_of((which * column + q) * extra, 8)
+            near = source[q, height:rows, :].astype(F32)
+            raw[pl.ds(at, extra), :] = near + source[column + q, height:rows, :].astype(F32)
     block = 3 * c1
     first = -(-9 * c2 // LANES) * block
     for i in range(3):
@@ -411,7 +436,7 @@
         in_specs=[spec, spec, remote],
         out_specs=(remote, remote, remote),
         scratch_shapes=[
-            pltpu.VMEM((2 * copies * (rows - height), LANES), F32),
+            pltpu.VMEM((copies * (rows - height), LANES), F32),
             pltpu.VMEM((27 * c0, c1), F32),
             pltpu.VMEM((27 * c1, c2), F32),
             pltpu.SemaphoreType.DMA((6,)),
@@ -431,24 +456,23 @@
 
 def per_device(volume_in, hidden_act, out_cot, kernel_one, kernel_two, grad_bucket):
     c0, c1, c2 = (volume_in.shape[2], hidden_act.shape[2], out_cot.shape[2])
-    devices, copies = (lax.axis_size(EVERY), lax.axis_size(SAME))
+    devices, copies, column = (lax.axis_size(EVERY), lax.axis_size(SAME), lax.axis_size(COLUMN))
     length = grad_bucket.shape[1]
     bucket = grad_bucket.reshape(length // LANES, LANES)
     packed = pack(out_cot[0, 0], volume_in[0, 0])
-    packed, send = lax.optimization_barrier((packed, cast(bucket, packed)))
     below, above = halos(packed)
-    half = add(bucket, swapped(send))
-    act, half = lax.optimization_barrier((hidden_act[0, 0], half))
-    parts = lax.all_to_all(half.reshape(copies, -1, LANES), SAME, 0, 0)
+    send, near = add(bucket, swapped(cast(bucket, packed)))
+    act, send, near = lax.optimization_barrier((hidden_act[0, 0], send, near))
+    far = swapped(send, "x")
 
     used = -(-9 * c2 // LANES) * 3 * c1 + 9 * c0
-    rows = ceil_to(used, 16 * devices)
+    rows = ceil_to(used, 16 * 2 * column)
     send, keep, own, up, down = compute((below, packed, above), act, kernel_two, kernel_one, rows)
-    terms = add(keep, swapped(send))
-    terms, parts = lax.optimization_barrier((terms, parts))
-    terms = lax.all_to_all(terms.reshape(copies, -1, LANES), SAME, 0, 0)
+    parts = combine(near, far, keep, swapped(send), column)
+    parts = lax.all_to_all(parts, COLUMN, 0, 0)
     cells = volume_in.shape[3] * volume_in.shape[4] * devices
-    shares = share(parts, terms, 1.0 / math.sqrt(cells), copies)
+    height = length // LANES // devices
+    shares = share(parts, height, 1.0 / math.sqrt(cells), copies)
 
     up, down, shares = lax.optimization_barrier((up, down, shares))
     mine = lax.all_to_all(shares, SAME, 0, 0)
@@ -469,8 +493,8 @@
 
 def solution(mesh):
     dp, space = (mesh.shape["dp"], mesh.shape["space"])
-    split = Mesh(mesh.devices.reshape(dp, space // 2, 2), EVERY)
-    volume = P("dp", SPACE, None, None, None)
+    split = Mesh(mesh.devices.reshape(dp // 2, 2, space // 2, 2), EVERY)
+    volume = P(("z", "x"), SPACE, None, None, None)
     in_specs = (volume, volume, volume, P(), P(), P(EVERY, None))
     out_specs = (volume, P(), P(), P())
     return jax.shard_map(

time: 72.7 us -> 71.9 us (0.989)
  waiting for transfers between devices: 11.9 us -> 16.9 us
  local copies, waits for them, and re-layouts: 7.85 us -> 3.59 us
  starting transfers between devices: 26 us -> 21.9 us
  blocking collectives: 12.4 us -> 16 us
  Pallas kernels: 12.8 us -> 12 us
    all_to_all x1 -> x0, starting transfers between devices: 6.57 us -> none  [per_device(): parts = lax.all_to_all(half.reshape(copies, -1, LANES), SAME, 0, 0)]
    unnamed x22 -> x14, local copies, waits for them, and re-layouts: 7.85 us -> 3.59 us
    ppermute x2, waiting for transfers between devices: 0.01 us -> 4.05 us  [halos(): return (lax.ppermute(value, SPACE, up), lax.ppermute(value, SPACE, down))]
    all_to_all x1, blocking collectives: 12.4 us -> 16 us  [per_device(): parts = lax.all_to_all(parts, COLUMN, 0, 0)]
    ppermute x3 -> x4, starting transfers between devices: 1.93 us -> 3.8 us  [swapped(): return lax.ppermute(value, axis, [(0, 1), (1, 0)])]
    all_to_all x1, starting transfers between devices: 3.58 us -> 5.26 us  [per_device(): mine = lax.all_to_all(shares, SAME, 0, 0)]
    all_to_all x1 -> x0, waiting for transfers between devices: 0.97 us -> none  [per_device(): parts = lax.all_to_all(half.reshape(copies, -1, LANES), SAME, 0, 0)]
    ppermute x1, starting transfers between devices: 5.43 us -> 4.46 us  [per_device(): from_below = lax.ppermute(up, SPACE, upward)]
  transfers between devices with their start and end apart: 9 -> 9, of which waited for: 6 -> 8; matrix products, arithmetic and copies ran while one was open for 0% -> 0% of each run, Pallas kernels for 13% -> 12%
where the time goes in v10:
time: 71.9 us; the launch traced here: 71.2 us
  starting transfers between devices  21.9 us (30%)
  waiting for transfers between devices  16.9 us (24%)
  blocking collectives  16 us (22%)
  Pallas kernels  12 us (17%)
  local copies, waits for them, and re-layouts  3.59 us (5%)
  between operations  0.77 us (1%)
    all_to_all x1, blocking collectives, per_device(): parts = lax.all_to_all(parts, COLUMN, 0, 0)  16 us
    ppermute x2, starting transfers between devices, halos(): return (lax.ppermute(value, SPACE, up), lax.ppermute(value, SPACE, down))  6.46 us
    pallas_call x1, Pallas kernels, compute(): vmem_call(compute_kernel, (jax.ShapeDtypeStruct((rows // 2, LANES), BF16)...  6.12 us
    all_to_all x1, starting transfers between devices, per_device(): mine = lax.all_to_all(shares, SAME, 0, 0)  5.26 us
    ppermute x1, starting transfers between devices, per_device(): from_below = lax.ppermute(up, SPACE, upward)  4.46 us
    ppermute x1, waiting for transfers between devices, per_device(): from_above = lax.ppermute(down, SPACE, [(j, i) for i, j in upward])  4.27 us
    ppermute x1, waiting for transfers between devices, per_device(): from_below = lax.ppermute(up, SPACE, upward)  4.14 us
    ppermute x2, waiting for transfers between devices, halos(): return (lax.ppermute(value, SPACE, up), lax.ppermute(value, SPACE, down))  4.05 us
  transfers between devices with their start and end apart: 9, of which 8 were waited for; matrix products, arithmetic and copies ran while one was open for 0% of the time, Pallas kernels for 12%

profile of v10, /device:TPU:1, one launch (start us, length us, event | category | flops | bytes accessed | tf_op | source)
XLA Modules:
  0.0 71.2 jit_solution(16328554451647145600)
XLA Ops:
  0.6 0.0 copy-start.2
  0.6 1.0 %copy-done.2 = bf16[1,1,32,64,128]{4,3,2,1,0:T(8,128)(2,1)S(1)} copy-done((bf16[1,1,32,64,128]{4,3,2,1,0:T(8,128)(2,1)S(1)}, bf16[1,1,32,64,128]{4,3,2,1,0:T(8,128)(2,1)}, u32[]{:S(2)}) %copy-start.2) | copy-done | bytes 524312
  1.7 0.0 copy-start.3
  1.7 0.9 %copy-done.3 = bf16[1,1,16,64,128]{4,3,2,1,0:T(8,128)(2,1)S(1)} copy-done((bf16[1,1,16,64,128]{4,3,2,1,0:T(8,128)(2,1)S(1)}, bf16[1,1,16,64,128]{4,3,2,1,0:T(8,128)(2,1)}, u32[]{:S(2)}) %copy-start.3) | copy-done | bytes 262168
  2.6 1.3 %shard_map.93.after.pack_0 = bf16[3168,128]{1,0:T(8,128)(2,1)S(1)} custom-call(bf16[32,64,128]{2,1,0:T(8,128)(2,1)S(1)} %bitcast.10, bf16[16,64,128]{2,1,0:T(8,128)(2,1)S(1)} %bitcast.11), custom_call_target="tpu_custom_call" | custom-call | bytes 8388608 | tf_op jit(solution)/shard_map/pallas_call | solution.py:66
  3.9 2.0 %collective-permute-start.1 = (bf16[3168,128]{1,0:T(8,128)(2,1)S(1)}, bf16[3168,128]{1,0:T(8,128)(2,1)S(1)}, u32[]{:S(2)}, u32[]{:S(2)}) collective-permute-start(bf16[3168,128]{1,0:T(8,128)(2,1)S(1)} %shard_map.93.after.pack_0), channel_id=1, source_target_pairs={{1,0},{2,1},{3,2},{5,4},{6,5},{7,6},{9,8},{10,9},{11,10},{13,12},{... | collective-permute-start | bytes 2433032 | tf_op jit(solution)/shard_map/ppermute | solution.py:454
  5.9 4.5 %collective-permute-start = (bf16[3168,128]{1,0:T(8,128)(2,1)S(1)}, bf16[3168,128]{1,0:T(8,128)(2,1)S(1)}, u32[]{:S(2)}, u32[]{:S(2)}) collective-permute-start(bf16[3168,128]{1,0:T(8,128)(2,1)S(1)} %shard_map.93.after.pack_0), channel_id=1, source_target_pairs={{0,1},{1,2},{2,3},{4,5},{5,6},{6,7},{8,9},{9,10},{10,11},{12,13},{... | collective-permute-start | bytes 2433032 | tf_op jit(solution)/shard_map/ppermute | solution.py:454
  10.4 0.0 copy-start
  10.4 1.6 %copy-done = f32[1,524288]{1,0:T(1,128)S(1)} copy-done((f32[1,524288]{1,0:T(1,128)S(1)}, f32[1,524288]{1,0:T(1,128)}, u32[]{:S(2)}) %copy-start) | copy-done | bytes 2097176
  12.0 0.0 copy-start.1
  12.0 0.1 shard_map.94
  12.1 0.0 copy-start.4
  12.1 0.0 copy-start.5
  12.1 0.0 copy-start.6
  12.1 0.1 collective-permute-start.2
  12.2 1.9 %collective-permute-done.2.other = bf16[2048,128]{1,0:T(8,128)(2,1)S(1)} collective-permute-done((bf16[2048,128]{1,0:T(8,128)(2,1)S(1)}, bf16[2048,128]{1,0:T(8,128)(2,1)S(1)}, u32[]{:S(2)}, u32[]{:S(2)}) %collective-permute-start.2) | collective-permute-done | bytes 524320 | tf_op jit(solution)/shard_map/ppermute | solution.py:161
  14.1 0.0 copy-done.1
  14.1 0.2 shard_map.95
  14.2 1.3 %collective-permute-start.3 = (bf16[1024,128]{1,0:T(8,128)(2,1)S(1)}, bf16[1024,128]{1,0:T(8,128)(2,1)S(1)}, u32[]{:S(2)}, u32[]{:S(2)}) collective-permute-start(bf16[1024,128]{1,0:T(8,128)(2,1)S(1)} %get-tuple-element.28), channel_id=1, source_target_pairs={{0,4},{4,0},{1,5},{5,1},{2,6},{6,2},{3,7},{7,3},{8,12},{12,8},{9,1... | collective-permute-start | bytes 786440 | tf_op jit(solution)/shard_map/ppermute | solution.py:161
  15.5 3.2 %collective-permute-done.1.pack_p = bf16[3168,128]{1,0:T(8,128)(2,1)S(1)} collective-permute-done((bf16[3168,128]{1,0:T(8,128)(2,1)S(1)}, bf16[3168,128]{1,0:T(8,128)(2,1)S(1)}, u32[]{:S(2)}, u32[]{:S(2)}) %collective-permute-start.1) | collective-permute-done | bytes 811040 | tf_op jit(solution)/shard_map/ppermute | solution.py:454
  18.7 0.9 %collective-permute-done.pack_m = bf16[3168,128]{1,0:T(8,128)(2,1)S(1)} collective-permute-done((bf16[3168,128]{1,0:T(8,128)(2,1)S(1)}, bf16[3168,128]{1,0:T(8,128)(2,1)S(1)}, u32[]{:S(2)}, u32[]{:S(2)}) %collective-permute-start) | collective-permute-done | bytes 811040 | tf_op jit(solution)/shard_map/ppermute | solution.py:454
  19.6 0.0 copy-done.4
  19.6 0.0 copy-done.5
  19.6 0.0 copy-done.6
  19.6 6.1 %shard_map.96 = (bf16[256,128]{1,0:T(8,128)(2,1)S(1)}, f32[256,128]{1,0:T(8,128)S(1)}, f32[1024,128]{1,0:T(8,128)S(1)}, bf16[1024,128]{1,0:T(8,128)(2,1)S(1)}, bf16[1024,128]{1,0:T(8,128)(2,1)S(1)}) custom-call(bf16[3168,128]{1,0:T(8,128)(2,1)S(1)} %collective-permute-done.pack_m, bf16[3168,128]{1,0:T(8,128)(2,1)S(1)} %shard_map.93.after.pack_0, ...), custom_call_target="tpu_custom_call" | custom-call | flops 10000000000 | bytes 41943040 | tf_op jit(solution)/shard_map/pallas_call | solution.py:275
  25.7 0.1 collective-permute-start.4
  25.8 0.0 collective-permute-done.3.other
  25.8 1.2 %collective-permute-done.4.more = bf16[256,128]{1,0:T(8,128)(2,1)S(1)} collective-permute-done((bf16[256,128]{1,0:T(8,128)(2,1)S(1)}, bf16[256,128]{1,0:T(8,128)(2,1)S(1)}, u32[]{:S(2)}, u32[]{:S(2)}) %collective-permute-start.4) | collective-permute-done | bytes 65568 | tf_op jit(solution)/shard_map/ppermute | solution.py:161
  27.0 0.1 shard_map.97
  27.1 16.0 %all_to_all.10.refs_0_ = bf16[8,160,128]{2,1,0:T(8,128)(2,1)S(1)} all-to-all(bf16[8,160,128]{2,1,0:T(8,128)(2,1)S(1)} %shard_map.97), channel_id=1, replica_groups=mesh['z'=4,'x'=2,'y'=2,'core'=2] {'z','y'}, dimensions={0} | all-to-all | bytes 655360 | tf_op jit(solution)/shard_map/all_to_all | solution.py:472
  43.0 1.0 %shard_map.98 = bf16[16,160,128]{2,1,0:T(8,128)(2,1)} custom-call(bf16[8,160,128]{2,1,0:T(8,128)(2,1)S(1)} %all_to_all.10.refs_0_), custom_call_target="tpu_custom_call" | custom-call | flops 163840 | bytes 983040 | tf_op jit(solution)/shard_map/pallas_call | solution.py:338
  44.0 5.3 %all-to-all-start.1 = ((bf16[16,160,128]{2,1,0:T(8,128)(2,1)}), bf16[16,160,128]{2,1,0:T(8,128)(2,1)S(1)}, u32[]{:S(2)}, u32[]{:S(2)}) async-start(bf16[16,160,128]{2,1,0:T(8,128)(2,1)} %shard_map.98), calls=%async_computation.1 | async-start | bytes 1310720 | tf_op jit(solution)/shard_map/all_to_all | solution.py:478
  49.3 4.5 %collective-permute-start.5 = (bf16[1024,128]{1,0:T(8,128)(2,1)S(1)}, bf16[1024,128]{1,0:T(8,128)(2,1)S(1)}, u32[]{:S(2)}, u32[]{:S(2)}) collective-permute-start(bf16[1024,128]{1,0:T(8,128)(2,1)S(1)} %get-tuple-element.33), channel_id=1, source_target_pairs={{0,1},{1,2},{2,3},{4,5},{5,6},{6,7},{8,9},{9,10},{10,11},{12,13},{... | collective-permute-start | bytes 786440 | tf_op jit(solution)/shard_map/ppermute | solution.py:481
  53.8 1.9 %collective-permute-start.6 = (bf16[1024,128]{1,0:T(8,128)(2,1)S(1)}, bf16[1024,128]{1,0:T(8,128)(2,1)S(1)}, u32[]{:S(2)}, u32[]{:S(2)}) collective-permute-start(bf16[1024,128]{1,0:T(8,128)(2,1)S(1)} %get-tuple-element.34), channel_id=1, source_target_pairs={{1,0},{2,1},{3,2},{5,4},{6,5},{7,6},{9,8},{10,9},{11,10},{13,12},{... | collective-permute-start | bytes 786440 | tf_op jit(solution)/shard_map/ppermute | solution.py:482
  55.7 4.1 %collective-permute-done.5.from_below = bf16[1024,128]{1,0:T(8,128)(2,1)S(1)} collective-permute-done((bf16[1024,128]{1,0:T(8,128)(2,1)S(1)}, bf16[1024,128]{1,0:T(8,128)(2,1)S(1)}, u32[]{:S(2)}, u32[]{:S(2)}) %collective-permute-start.5) | collective-permute-done | bytes 262176 | tf_op jit(solution)/shard_map/ppermute | solution.py:481
  59.8 4.3 %collective-permute-done.6.from_above = bf16[1024,128]{1,0:T(8,128)(2,1)S(1)} collective-permute-done((bf16[1024,128]{1,0:T(8,128)(2,1)S(1)}, bf16[1024,128]{1,0:T(8,128)(2,1)S(1)}, u32[]{:S(2)}, u32[]{:S(2)}) %collective-permute-start.6) | collective-permute-done | bytes 262176 | tf_op jit(solution)/shard_map/ppermute | solution.py:482
  64.1 1.0 %shard_map.99 = bf16[16,64,128]{2,1,0:T(8,128)(2,1)} custom-call(f32[1024,128]{1,0:T(8,128)S(1)} %get-tuple-element.32.own, bf16[1024,128]{1,0:T(8,128)(2,1)S(1)} %collective-permute-done.5.from_below, bf16[1024,128]{1,0:T(8,128)(2,1)S(1)} %collective-permute-done.6.from_above), custom_call_target="tpu_custom_call" | custom-call | flops 262144 | bytes 1048576 | tf_op jit(solution)/shard_map/pallas_call | solution.py:316
  65.1 0.6 all-to-all-done.1.refs_0_
  65.7 2.4 %collective-permute-start.7 = (bf16[16,160,128]{2,1,0:T(8,128)(2,1)S(1)}, bf16[16,160,128]{2,1,0:T(8,128)(2,1)S(1)}, u32[]{:S(2)}, u32[]{:S(2)}) collective-permute-start(bf16[16,160,128]{2,1,0:T(8,128)(2,1)S(1)} %all-to-all-done.1.refs_0_), channel_id=1, source_target_pairs={{0,1},{1,0},{2,3},{3,2},{4,5},{5,4},{6,7},{7,6},{8,9},{9,8},{10,11... | collective-permute-start | bytes 1966088 | tf_op jit(solution)/shard_map/ppermute | solution.py:161
  68.0 1.0 %shard_map.100.refs_2_ = f32[4096,128]{1,0:T(8,128)} custom-call(bf16[16,160,128]{2,1,0:T(8,128)(2,1)S(1)} %all-to-all-done.1.refs_0_), custom_call_target="tpu_custom_call" | custom-call | tf_op jit(solution)/shard_map/pallas_call | solution.py:421
  69.1 0.7 collective-permute-done.7.refs_1_
  69.8 1.4 %shard_map.101 = (f32[4096,128]{1,0:T(8,128)}, f32[432,32]{1,0:T(8,128)}, f32[864,32]{1,0:T(8,128)}) custom-call(bf16[16,160,128]{2,1,0:T(8,128)(2,1)S(1)} %all-to-all-done.1.refs_0_, bf16[16,160,128]{2,1,0:T(8,128)(2,1)S(1)} %collective-permute-done.7.refs_1_, f32[4096,128]{1,0:T(8,128)} %shard_map.100.refs_2_), custom_call_target="tpu_custom_call", output_to_operand_aliasing={{0}: (2, {})} | custom-call | tf_op jit(solution)/shard_map/pallas_call | solution.py:429
Async XLA Ops:
  0.6 1.0 %copy-start.2 = (bf16[1,1,32,64,128]{4,3,2,1,0:T(8,128)(2,1)S(1)}, bf16[1,1,32,64,128]{4,3,2,1,0:T(8,128)(2,1)}, u32[]{:S(2)}) copy-start(bf16[1,1,32,64,128]{4,3,2,1,0:T(8,128)(2,1)} %param.8) | copy-start | bytes 1572868
  1.7 0.9 %copy-start.3 = (bf16[1,1,16,64,128]{4,3,2,1,0:T(8,128)(2,1)S(1)}, bf16[1,1,16,64,128]{4,3,2,1,0:T(8,128)(2,1)}, u32[]{:S(2)}) copy-start(bf16[1,1,16,64,128]{4,3,2,1,0:T(8,128)(2,1)} %param.6) | copy-start | bytes 786436
  3.9 14.8 %collective-permute-start.1 = (bf16[3168,128]{1,0:T(8,128)(2,1)S(1)}, bf16[3168,128]{1,0:T(8,128)(2,1)S(1)}, u32[]{:S(2)}, u32[]{:S(2)}) collective-permute-start(bf16[3168,128]{1,0:T(8,128)(2,1)S(1)} %shard_map.93.after.pack_0), channel_id=1, source_target_pairs={{1,0},{2,1},{3,2},{5,4},{6,5},{7,6},{9,8},{10,9},{11,10},{13,12},{... | collective-permute-start | bytes 2433032 | tf_op jit(solution)/shard_map/ppermute | solution.py:454
  5.9 13.7 %collective-permute-start = (bf16[3168,128]{1,0:T(8,128)(2,1)S(1)}, bf16[3168,128]{1,0:T(8,128)(2,1)S(1)}, u32[]{:S(2)}, u32[]{:S(2)}) collective-permute-start(bf16[3168,128]{1,0:T(8,128)(2,1)S(1)} %shard_map.93.after.pack_0), channel_id=1, source_target_pairs={{0,1},{1,2},{2,3},{4,5},{5,6},{6,7},{8,9},{9,10},{10,11},{12,13},{... | collective-permute-start | bytes 2433032 | tf_op jit(solution)/shard_map/ppermute | solution.py:454
  10.4 1.6 %copy-start = (f32[1,524288]{1,0:T(1,128)S(1)}, f32[1,524288]{1,0:T(1,128)}, u32[]{:S(2)}) copy-start(f32[1,524288]{1,0:T(1,128)} %param.11) | copy-start | bytes 6291460
  12.0 2.1 %copy-start.1 = (f32[1,524288]{1,0:T(1,128)S(1)}, f32[1,524288]{1,0:T(1,128)}, u32[]{:S(2)}) copy-start(f32[1,524288]{1,0:T(1,128)} %param.11) | copy-start | bytes 6291460
  12.1 7.5 %copy-start.4 = (bf16[1,1,32,64,128]{4,3,2,1,0:T(8,128)(2,1)S(1)}, bf16[1,1,32,64,128]{4,3,2,1,0:T(8,128)(2,1)}, u32[]{:S(2)}) copy-start(bf16[1,1,32,64,128]{4,3,2,1,0:T(8,128)(2,1)} %param.7) | copy-start | bytes 1572868
  12.1 7.5 %copy-start.5 = (bf16[3,3,3,32,32]{4,3,2,1,0:T(8,128)(2,1)S(1)}, bf16[3,3,3,32,32]{4,3,2,1,0:T(8,128)(2,1)}, u32[]{:S(2)}) copy-start(bf16[3,3,3,32,32]{4,3,2,1,0:T(8,128)(2,1)} %two.1) | copy-start | bytes 165892
  12.1 7.5 %copy-start.6 = (bf16[3,3,3,16,32]{4,3,2,1,0:T(8,128)(2,1)S(1)}, bf16[3,3,3,16,32]{4,3,2,1,0:T(8,128)(2,1)}, u32[]{:S(2)}) copy-start(bf16[3,3,3,16,32]{4,3,2,1,0:T(8,128)(2,1)} %one.1) | copy-start | bytes 82948
  12.1 2.0 %collective-permute-start.2 = (bf16[2048,128]{1,0:T(8,128)(2,1)S(1)}, bf16[2048,128]{1,0:T(8,128)(2,1)S(1)}, u32[]{:S(2)}, u32[]{:S(2)}) collective-permute-start(bf16[2048,128]{1,0:T(8,128)(2,1)S(1)} %shard_map.94), channel_id=1, source_target_pairs={{0,1},{1,0},{2,3},{3,2},{4,5},{5,4},{6,7},{7,6},{8,9},{9,8},{10,11... | collective-permute-start | bytes 1572872 | tf_op jit(solution)/shard_map/ppermute | solution.py:161
  14.2 11.5 %collective-permute-start.3 = (bf16[1024,128]{1,0:T(8,128)(2,1)S(1)}, bf16[1024,128]{1,0:T(8,128)(2,1)S(1)}, u32[]{:S(2)}, u32[]{:S(2)}) collective-permute-start(bf16[1024,128]{1,0:T(8,128)(2,1)S(1)} %get-tuple-element.28), channel_id=1, source_target_pairs={{0,4},{4,0},{1,5},{5,1},{2,6},{6,2},{3,7},{7,3},{8,12},{12,8},{9,1... | collective-permute-start | bytes 786440 | tf_op jit(solution)/shard_map/ppermute | solution.py:161
  25.7 1.3 %collective-permute-start.4 = (bf16[256,128]{1,0:T(8,128)(2,1)S(1)}, bf16[256,128]{1,0:T(8,128)(2,1)S(1)}, u32[]{:S(2)}, u32[]{:S(2)}) collective-permute-start(bf16[256,128]{1,0:T(8,128)(2,1)S(1)} %get-tuple-element.30), channel_id=1, source_target_pairs={{0,1},{1,0},{2,3},{3,2},{4,5},{5,4},{6,7},{7,6},{8,9},{9,8},{10,11... | collective-permute-start | bytes 196616 | tf_op jit(solution)/shard_map/ppermute | solution.py:161
  44.0 21.6 %all-to-all-start.1 = ((bf16[16,160,128]{2,1,0:T(8,128)(2,1)}), bf16[16,160,128]{2,1,0:T(8,128)(2,1)S(1)}, u32[]{:S(2)}, u32[]{:S(2)}) async-start(bf16[16,160,128]{2,1,0:T(8,128)(2,1)} %shard_map.98), calls=%async_computation.1 | async-start | bytes 1310720 | tf_op jit(solution)/shard_map/all_to_all | solution.py:478
  49.3 10.5 %collective-permute-start.5 = (bf16[1024,128]{1,0:T(8,128)(2,1)S(1)}, bf16[1024,128]{1,0:T(8,128)(2,1)S(1)}, u32[]{:S(2)}, u32[]{:S(2)}) collective-permute-start(bf16[1024,128]{1,0:T(8,128)(2,1)S(1)} %get-tuple-element.33), channel_id=1, source_target_pairs={{0,1},{1,2},{2,3},{4,5},{5,6},{6,7},{8,9},{9,10},{10,11},{12,13},{... | collective-permute-start | bytes 786440 | tf_op jit(solution)/shard_map/ppermute | solution.py:481
  53.8 10.3 %collective-permute-start.6 = (bf16[1024,128]{1,0:T(8,128)(2,1)S(1)}, bf16[1024,128]{1,0:T(8,128)(2,1)S(1)}, u32[]{:S(2)}, u32[]{:S(2)}) collective-permute-start(bf16[1024,128]{1,0:T(8,128)(2,1)S(1)} %get-tuple-element.34), channel_id=1, source_target_pairs={{1,0},{2,1},{3,2},{5,4},{6,5},{7,6},{9,8},{10,9},{11,10},{13,12},{... | collective-permute-start | bytes 786440 | tf_op jit(solution)/shard_map/ppermute | solution.py:482
  65.7 4.1 %collective-permute-start.7 = (bf16[16,160,128]{2,1,0:T(8,128)(2,1)S(1)}, bf16[16,160,128]{2,1,0:T(8,128)(2,1)S(1)}, u32[]{:S(2)}, u32[]{:S(2)}) collective-permute-start(bf16[16,160,128]{2,1,0:T(8,128)(2,1)S(1)} %all-to-all-done.1.refs_0_), channel_id=1, source_target_pairs={{0,1},{1,0},{2,3},{3,2},{4,5},{5,4},{6,7},{7,6},{8,9},{9,8},{10,11... | collective-permute-start | bytes 1966088 | tf_op jit(solution)/shard_map/ppermute | solution.py:161

commit v11 on v10

--- a/solution.py
+++ b/solution.py
@@ -162,27 +162,30 @@
 
 
 def compute_kernel(
-    pack_m, pack_0, pack_p, act, two, one,
-    send, keep, own, up, down,
+    pack_in, pack_0, pack_out, act, two, one,
+    send, keep, own, inner, outer,
     terms, flat, acts, pres, w_two, w_one, acc_two, acc_one,
 ):
     c1, length, _ = act.shape
     c2, c0 = (two.shape[4], one.shape[3])
     pitch = c0 + c2
-    packs = (pack_m, pack_0, pack_p)
+    packs = (pack_in, pack_0, pack_out)
+    core = lax.axis_index("core")
+    ahead = [core * n + (1 - core) * (2 - n) for n in range(3)]
+    back = [core * (2 - n) + (1 - core) * n for n in range(3)]
 
     turned(act, flat, acts, 0, c1, 0)
     offsets = [(m, n) for m in range(3) for n in range(3)]
     w_two[...] = jnp.concatenate(
         [
-            jnp.concatenate([two[2 - i, 2 - j, 2 - k].astype(F32) for k in range(3)], axis=0)
-            for j, i in offsets
+            jnp.concatenate([two[back[n], 2 - j, 2 - k].astype(F32) for k in range(3)], axis=0)
+            for j, n in offsets
         ],
         axis=1,
     ).astype(BF16)
     w_one[...] = jnp.concatenate(
         [
-            jnp.concatenate([one[2 - i, 2 - j, k].astype(F32) for i in range(3)], axis=0)
+            jnp.concatenate([one[ahead[n], 2 - j, k].astype(F32) for n in range(3)], axis=0)
             for j, k in offsets
         ],
         axis=1,
@@ -222,7 +225,7 @@
         )
         return carry
 
-    lax.fori_loop(0, length // GROUP, first, 0, unroll=2)
+    lax.fori_loop(0, length // GROUP, first, 0, unroll=4)
 
     def second(step, carry):
         x = step * GROUP
@@ -232,7 +235,7 @@
         for g in range(GROUP):
             part = sums[:, g * LANES : (g + 1) * LANES]
             at = pl.ds(pl.multiple_of((x + g) * c0, 16), c0)
-            for i, out in ((0, up), (1, own), (2, down)):
+            for i, out in ((0, inner), (1, own), (2, outer)):
                 out[at, :] = part[i * c0 : (i + 1) * c0].astype(out.dtype)
         acc_one[...] += lax.dot_general(
             windows(x, c2, c0),
@@ -242,16 +245,21 @@
         )
         return carry
 
-    lax.fori_loop(0, length // GROUP, second, 0, unroll=2)
+    lax.fori_loop(0, length // GROUP, second, 0, unroll=4)
 
     terms[...] = jnp.zeros_like(terms)
-    two = acc_two[...].T
+
+    def ordered(acc, count):
+        blocks = [pl.multiple_of((3 * j + n) * count, 16) for j in range(3) for n in ahead]
+        return jnp.concatenate([acc[pl.ds(at, count), :] for at in blocks], axis=0)
+
+    two = ordered(acc_two, c2).T
     rows, width = two.shape
     blocks = -(-width // LANES)
     for block in range(blocks):
         part = two[:, block * LANES : min(width, (block + 1) * LANES)]
         terms[block * rows : (block + 1) * rows, 0 : part.shape[1]] = part
-    one = acc_one[...]
+    one = ordered(acc_one, c0)
     terms[blocks * rows : blocks * rows + one.shape[0], 0 : one.shape[1]] = one
     split_to(terms, lax.axis_index("core"), send, keep)
 
@@ -295,12 +303,12 @@
     )(*packs, act, kernel_two, kernel_one)
 
 
-def merge_kernel(own, from_below, from_above, out, flat):
+def merge_kernel(own, first, second, out, flat):
     chans, length, _ = out.shape
 
     def add(step, carry):
         at = pl.ds(pl.multiple_of(step * 64, 64), 64)
-        flat[at, :] = own[at, :] + from_below[at, :].astype(F32) + from_above[at, :].astype(F32)
+        flat[at, :] = own[at, :] + first[at, :].astype(F32) + second[at, :].astype(F32)
         return carry
 
     lax.fori_loop(0, own.shape[0] // 64, add, 0, unroll=4)
@@ -312,13 +320,13 @@
     lax.fori_loop(0, chans, gather, 0, unroll=4)
 
 
-def merge(own, from_below, from_above, shape):
+def merge(own, first, second, shape):
     return vmem_call(
         merge_kernel,
         jax.ShapeDtypeStruct(shape, BF16),
         (pltpu.VMEM(own.shape, F32),),
         pl.CostEstimate(flops=2 * own.size, bytes_accessed=8 * own.size, transcendentals=0),
-    )(own, from_below, from_above)
+    )(own, first, second)
 
 
 def share_kernel(scale, height, parts, out):
@@ -447,11 +455,9 @@
     )(mine, other, partial)
 
 
-def halos(value):
-    count = lax.axis_size(SPACE)
-    up = [(i, i + 1) for i in range(count - 1)]
-    down = [(j, i) for i, j in up]
-    return (lax.ppermute(value, SPACE, up), lax.ppermute(value, SPACE, down))
+def crossed(value):
+    pairs = [(n, n + 1) for n in range(1, lax.axis_size(SPACE) - 1, 2)]
+    return lax.ppermute(value, SPACE, pairs + [(m, n) for n, m in pairs])
 
 
 def per_device(volume_in, hidden_act, out_cot, kernel_one, kernel_two, grad_bucket):
@@ -460,28 +466,26 @@
     length = grad_bucket.shape[1]
     bucket = grad_bucket.reshape(length // LANES, LANES)
     packed = pack(out_cot[0, 0], volume_in[0, 0])
-    below, above = halos(packed)
+    outer, inner = (crossed(packed), swapped(packed))
     send, near = add(bucket, swapped(cast(bucket, packed)))
     act, send, near = lax.optimization_barrier((hidden_act[0, 0], send, near))
     far = swapped(send, "x")
 
     used = -(-9 * c2 // LANES) * 3 * c1 + 9 * c0
     rows = ceil_to(used, 16 * 2 * column)
-    send, keep, own, up, down = compute((below, packed, above), act, kernel_two, kernel_one, rows)
+    send, keep, own, inner, outer = compute(
+        (inner, packed, outer), act, kernel_two, kernel_one, rows
+    )
     parts = combine(near, far, keep, swapped(send), column)
+    parts, inner, outer = lax.optimization_barrier((parts, inner, outer))
     parts = lax.all_to_all(parts, COLUMN, 0, 0)
+    grad_input = merge(own, swapped(inner), crossed(outer), volume_in.shape[2:])
+    parts, grad_input = lax.optimization_barrier((parts, grad_input))
     cells = volume_in.shape[3] * volume_in.shape[4] * devices
     height = length // LANES // devices
     shares = share(parts, height, 1.0 / math.sqrt(cells), copies)
 
-    up, down, shares = lax.optimization_barrier((up, down, shares))
     mine = lax.all_to_all(shares, SAME, 0, 0)
-    count = lax.axis_size(SPACE)
-    upward = [(i, i + 1) for i in range(count - 1)]
-    from_below = lax.ppermute(up, SPACE, upward)
-    from_above = lax.ppermute(down, SPACE, [(j, i) for i, j in upward])
-    grad_input = merge(own, from_below, from_above, volume_in.shape[2:])
-    mine, grad_input = lax.optimization_barrier((mine, grad_input))
     bucket_sum, total_one, total_two = finish(mine, swapped(mine), length, (c0, c1, c2))
     return (
         grad_input[None, None],

time: 71.9 us -> 71.4 us (level)
  blocking collectives: 16 us -> 22.7 us
  starting transfers between devices: 21.9 us -> 18.4 us
  waiting for transfers between devices: 16.9 us -> 13.9 us
    all_to_all x1, blocking collectives: 16 us -> 22.7 us  [per_device(): mine = lax.all_to_all(shares, SAME, 0, 0)]
    ppermute x4 -> x2, starting transfers between devices: 12.8 us -> 8.06 us  [crossed(): return lax.ppermute(value, SPACE, pairs + [(m, n) for n, m in pairs])]
    ppermute x4 -> x2, waiting for transfers between devices: 12.5 us -> 10.4 us  [crossed(): return lax.ppermute(value, SPACE, pairs + [(m, n) for n, m in pairs])]
    ppermute x4 -> x6, starting transfers between devices: 3.8 us -> 4.77 us  [swapped(): return lax.ppermute(value, axis, [(0, 1), (1, 0)])]
    pallas_call x1, Pallas kernels: 0.97 us -> 0.13 us  [share(): vmem_call(lambda *refs: share_kernel(scale, height, *refs), jax.ShapeDtyp...]
    pallas_call x1, Pallas kernels: 0.06 us -> 0.78 us  [combine(): vmem_call(combine_kernel, jax.ShapeDtypeStruct((parts, rows, LANES), BF16...]
    ppermute x4 -> x6, waiting for transfers between devices: 3.83 us -> 3.48 us  [swapped(): return lax.ppermute(value, axis, [(0, 1), (1, 0)])]
  transfers between devices with their start and end apart: 9 -> 9, of which waited for: 8 -> 5; matrix products, arithmetic and copies ran while one was open for 0% -> 0% of each run, Pallas kernels for 12% -> 11%
where the time goes in v11:
time: 71.4 us; the launch traced here: 70.7 us
  blocking collectives  22.7 us (32%)
  starting transfers between devices  18.4 us (26%)
  waiting for transfers between devices  13.9 us (19%)
  Pallas kernels  11.4 us (16%)
  local copies, waits for them, and re-layouts  3.59 us (5%)
  between operations  0.77 us (1%)
    all_to_all x1, blocking collectives, per_device(): mine = lax.all_to_all(shares, SAME, 0, 0)  22.7 us
    ppermute x2, waiting for transfers between devices, crossed(): return lax.ppermute(value, SPACE, pairs + [(m, n) for n, m in pairs])  10.4 us
    ppermute x2, starting transfers between devices, crossed(): return lax.ppermute(value, SPACE, pairs + [(m, n) for n, m in pairs])  8.06 us
    pallas_call x1, Pallas kernels, compute(): vmem_call(compute_kernel, (jax.ShapeDtypeStruct((rows // 2, LANES), BF16)...  5.57 us
    all_to_all x1, starting transfers between devices, per_device(): parts = lax.all_to_all(parts, COLUMN, 0, 0)  5.52 us
    ppermute x6, starting transfers between devices, swapped(): return lax.ppermute(value, axis, [(0, 1), (1, 0)])  4.77 us
    unnamed x14, local copies, waits for them, and re-layouts  3.59 us
    ppermute x6, waiting for transfers between devices, swapped(): return lax.ppermute(value, axis, [(0, 1), (1, 0)])  3.48 us
  transfers between devices with their start and end apart: 9, of which 5 were waited for; matrix products, arithmetic and copies ran while one was open for 0% of the time, Pallas kernels for 11%

profile of v11, /device:TPU:1, one launch (start us, length us, event | category | flops | bytes accessed | tf_op | source)
XLA Modules:
  0.0 70.7 jit_solution(12009616502038896917)
XLA Ops:
  0.6 0.0 copy-start.2
  0.6 1.0 %copy-done.2 = bf16[1,1,32,64,128]{4,3,2,1,0:T(8,128)(2,1)S(1)} copy-done((bf16[1,1,32,64,128]{4,3,2,1,0:T(8,128)(2,1)S(1)}, bf16[1,1,32,64,128]{4,3,2,1,0:T(8,128)(2,1)}, u32[]{:S(2)}) %copy-start.2) | copy-done | bytes 524312
  1.7 0.0 copy-start.3
  1.7 0.9 %copy-done.3 = bf16[1,1,16,64,128]{4,3,2,1,0:T(8,128)(2,1)S(1)} copy-done((bf16[1,1,16,64,128]{4,3,2,1,0:T(8,128)(2,1)S(1)}, bf16[1,1,16,64,128]{4,3,2,1,0:T(8,128)(2,1)}, u32[]{:S(2)}) %copy-start.3) | copy-done | bytes 262168
  2.6 1.3 %shard_map.93.after.pack_0 = bf16[3168,128]{1,0:T(8,128)(2,1)S(1)} custom-call(bf16[32,64,128]{2,1,0:T(8,128)(2,1)S(1)} %bitcast.10, bf16[16,64,128]{2,1,0:T(8,128)(2,1)S(1)} %bitcast.11), custom_call_target="tpu_custom_call" | custom-call | bytes 8388608 | tf_op jit(solution)/shard_map/pallas_call | solution.py:66
  3.9 4.5 %collective-permute-start.3 = (bf16[3168,128]{1,0:T(8,128)(2,1)S(1)}, bf16[3168,128]{1,0:T(8,128)(2,1)S(1)}, u32[]{:S(2)}, u32[]{:S(2)}) collective-permute-start(bf16[3168,128]{1,0:T(8,128)(2,1)S(1)} %shard_map.93.after.pack_0), channel_id=1, source_target_pairs={{1,2},{2,1},{5,6},{6,5},{9,10},{10,9},{13,14},{14,13},{17,18},{18,... | collective-permute-start | bytes 2433032 | tf_op jit(solution)/shard_map/ppermute | solution.py:460
  8.5 0.1 collective-permute-start.2
  8.5 0.0 copy-start
  8.6 1.6 %copy-done = f32[1,524288]{1,0:T(1,128)S(1)} copy-done((f32[1,524288]{1,0:T(1,128)S(1)}, f32[1,524288]{1,0:T(1,128)}, u32[]{:S(2)}) %copy-start) | copy-done | bytes 2097176
  10.1 0.0 copy-start.1
  10.1 0.1 shard_map.94
  10.2 0.0 copy-start.4
  10.2 0.0 copy-start.5
  10.2 0.0 copy-start.6
  10.3 0.6 collective-permute-start
  10.8 1.5 %collective-permute-done.other = bf16[2048,128]{1,0:T(8,128)(2,1)S(1)} collective-permute-done((bf16[2048,128]{1,0:T(8,128)(2,1)S(1)}, bf16[2048,128]{1,0:T(8,128)(2,1)S(1)}, u32[]{:S(2)}, u32[]{:S(2)}) %collective-permute-start) | collective-permute-done | bytes 524320 | tf_op jit(solution)/shard_map/ppermute | solution.py:161
  12.4 0.0 copy-done.1
  12.4 0.2 shard_map.95
  12.5 1.3 %collective-permute-start.1 = (bf16[1024,128]{1,0:T(8,128)(2,1)S(1)}, bf16[1024,128]{1,0:T(8,128)(2,1)S(1)}, u32[]{:S(2)}, u32[]{:S(2)}) collective-permute-start(bf16[1024,128]{1,0:T(8,128)(2,1)S(1)} %get-tuple-element.25), channel_id=1, source_target_pairs={{0,4},{4,0},{1,5},{5,1},{2,6},{6,2},{3,7},{7,3},{8,12},{12,8},{9,1... | collective-permute-start | bytes 786440 | tf_op jit(solution)/shard_map/ppermute | solution.py:161
  13.8 4.9 %collective-permute-done.3.pack_out = bf16[3168,128]{1,0:T(8,128)(2,1)S(1)} collective-permute-done((bf16[3168,128]{1,0:T(8,128)(2,1)S(1)}, bf16[3168,128]{1,0:T(8,128)(2,1)S(1)}, u32[]{:S(2)}, u32[]{:S(2)}) %collective-permute-start.3) | collective-permute-done | bytes 811040 | tf_op jit(solution)/shard_map/ppermute | solution.py:460
  18.7 0.0 collective-permute-done.2.pack_in
  18.7 0.0 copy-done.4
  18.7 0.0 copy-done.5
  18.7 0.0 copy-done.6
  18.7 5.6 %shard_map.96 = (bf16[256,128]{1,0:T(8,128)(2,1)S(1)}, f32[256,128]{1,0:T(8,128)S(1)}, f32[1024,128]{1,0:T(8,128)S(1)}, bf16[1024,128]{1,0:T(8,128)(2,1)S(1)}, bf16[1024,128]{1,0:T(8,128)(2,1)S(1)}) custom-call(bf16[3168,128]{1,0:T(8,128)(2,1)S(1)} %collective-permute-done.2.pack_in, bf16[3168,128]{1,0:T(8,128)(2,1)S(1)} %shard_map.93.after.pack_0, ...), custom_call_target="tpu_custom_call" | custom-call | flops 10000000000 | bytes 41943040 | tf_op jit(solution)/shard_map/pallas_call | solution.py:283
  24.3 0.1 collective-permute-start.4
  24.4 0.0 collective-permute-done.1.other
  24.4 1.2 %collective-permute-done.4.more = bf16[256,128]{1,0:T(8,128)(2,1)S(1)} collective-permute-done((bf16[256,128]{1,0:T(8,128)(2,1)S(1)}, bf16[256,128]{1,0:T(8,128)(2,1)S(1)}, u32[]{:S(2)}, u32[]{:S(2)}) %collective-permute-start.4) | collective-permute-done | bytes 65568 | tf_op jit(solution)/shard_map/ppermute | solution.py:161
  25.6 0.8 %shard_map.97 = bf16[8,160,128]{2,1,0:T(8,128)(2,1)} custom-call(f32[1024,128]{1,0:T(8,128)S(1)} %get-tuple-element.24.keep, bf16[1024,128]{1,0:T(8,128)(2,1)S(1)} %collective-permute-done.1.other, f32[256,128]{1,0:T(8,128)S(1)} %get-tuple-element.27.terms, bf16[256,128]{1,0:T(8,128)(2,1)S(1)} %collective-permute-done.4.more), custom_call_target="tpu_custom_call" | custom-call | bytes 1048576 | tf_op jit(solution)/shard_map/pallas_call | solution.py:146
  26.4 5.5 %all-to-all-start = ((bf16[8,160,128]{2,1,0:T(8,128)(2,1)}), bf16[8,160,128]{2,1,0:T(8,128)(2,1)S(1)}, u32[]{:S(2)}, u32[]{:S(2)}) async-start(bf16[8,160,128]{2,1,0:T(8,128)(2,1)} %shard_map.97), calls=%async_computation | async-start | bytes 655360 | tf_op jit(solution)/shard_map/all_to_all | solution.py:481
  31.9 0.6 collective-permute-start.5
  32.5 3.5 %collective-permute-start.6 = (bf16[1024,128]{1,0:T(8,128)(2,1)S(1)}, bf16[1024,128]{1,0:T(8,128)(2,1)S(1)}, u32[]{:S(2)}, u32[]{:S(2)}) collective-permute-start(bf16[1024,128]{1,0:T(8,128)(2,1)S(1)} %get-tuple-element.34), channel_id=1, source_target_pairs={{1,2},{2,1},{5,6},{6,5},{9,10},{10,9},{13,14},{14,13},{17,18},{18,... | collective-permute-start | bytes 786440 | tf_op jit(solution)/shard_map/ppermute | solution.py:460
  36.1 0.0 collective-permute-done.5.first
  36.1 5.5 %collective-permute-done.6.second = bf16[1024,128]{1,0:T(8,128)(2,1)S(1)} collective-permute-done((bf16[1024,128]{1,0:T(8,128)(2,1)S(1)}, bf16[1024,128]{1,0:T(8,128)(2,1)S(1)}, u32[]{:S(2)}, u32[]{:S(2)}) %collective-permute-start.6) | collective-permute-done | bytes 262176 | tf_op jit(solution)/shard_map/ppermute | solution.py:460
  41.6 1.0 %shard_map.98 = bf16[16,64,128]{2,1,0:T(8,128)(2,1)} custom-call(f32[1024,128]{1,0:T(8,128)S(1)} %get-tuple-element.32.own, bf16[1024,128]{1,0:T(8,128)(2,1)S(1)} %collective-permute-done.5.first, bf16[1024,128]{1,0:T(8,128)(2,1)S(1)} %collective-permute-done.6.second), custom_call_target="tpu_custom_call" | custom-call | flops 262144 | bytes 1048576 | tf_op jit(solution)/shard_map/pallas_call | solution.py:324
  42.6 0.0 all-to-all-done.refs_0_
  42.6 0.1 shard_map.99
  42.7 22.7 %all_to_all.10.refs_0_ = bf16[16,160,128]{2,1,0:T(8,128)(2,1)S(1)} all-to-all(bf16[16,160,128]{2,1,0:T(8,128)(2,1)S(1)} %shard_map.99), channel_id=1, replica_groups=mesh['z'=4,'x'=2,'y'=2,'core'=2] {'x','z','y'}, dimensions={0} | all-to-all | bytes 1310720 | tf_op jit(solution)/shard_map/all_to_all | solution.py:488
  65.4 2.2 %collective-permute-start.7 = (bf16[16,160,128]{2,1,0:T(8,128)(2,1)S(1)}, bf16[16,160,128]{2,1,0:T(8,128)(2,1)S(1)}, u32[]{:S(2)}, u32[]{:S(2)}) collective-permute-start(bf16[16,160,128]{2,1,0:T(8,128)(2,1)S(1)} %all_to_all.10.refs_0_), channel_id=1, source_target_pairs={{0,1},{1,0},{2,3},{3,2},{4,5},{5,4},{6,7},{7,6},{8,9},{9,8},{10,11... | collective-permute-start | bytes 1966088 | tf_op jit(solution)/shard_map/ppermute | solution.py:161
  67.5 1.0 %shard_map.100.refs_2_ = f32[4096,128]{1,0:T(8,128)} custom-call(bf16[16,160,128]{2,1,0:T(8,128)(2,1)S(1)} %all_to_all.10.refs_0_), custom_call_target="tpu_custom_call" | custom-call | tf_op jit(solution)/shard_map/pallas_call | solution.py:429
  68.6 0.7 collective-permute-done.7.refs_1_
  69.3 1.4 %shard_map.101 = (f32[4096,128]{1,0:T(8,128)}, f32[432,32]{1,0:T(8,128)}, f32[864,32]{1,0:T(8,128)}) custom-call(bf16[16,160,128]{2,1,0:T(8,128)(2,1)S(1)} %all_to_all.10.refs_0_, bf16[16,160,128]{2,1,0:T(8,128)(2,1)S(1)} %collective-permute-done.7.refs_1_, f32[4096,128]{1,0:T(8,128)} %shard_map.100.refs_2_), custom_call_target="tpu_custom_call", output_to_operand_aliasing={{0}: (2, {})} | custom-call | tf_op jit(solution)/shard_map/pallas_call | solution.py:437
Async XLA Ops:
  0.6 1.0 %copy-start.2 = (bf16[1,1,32,64,128]{4,3,2,1,0:T(8,128)(2,1)S(1)}, bf16[1,1,32,64,128]{4,3,2,1,0:T(8,128)(2,1)}, u32[]{:S(2)}) copy-start(bf16[1,1,32,64,128]{4,3,2,1,0:T(8,128)(2,1)} %param.8) | copy-start | bytes 1572868
  1.7 0.9 %copy-start.3 = (bf16[1,1,16,64,128]{4,3,2,1,0:T(8,128)(2,1)S(1)}, bf16[1,1,16,64,128]{4,3,2,1,0:T(8,128)(2,1)}, u32[]{:S(2)}) copy-start(bf16[1,1,16,64,128]{4,3,2,1,0:T(8,128)(2,1)} %param.6) | copy-start | bytes 786436
  3.9 14.8 %collective-permute-start.3 = (bf16[3168,128]{1,0:T(8,128)(2,1)S(1)}, bf16[3168,128]{1,0:T(8,128)(2,1)S(1)}, u32[]{:S(2)}, u32[]{:S(2)}) collective-permute-start(bf16[3168,128]{1,0:T(8,128)(2,1)S(1)} %shard_map.93.after.pack_0), channel_id=1, source_target_pairs={{1,2},{2,1},{5,6},{6,5},{9,10},{10,9},{13,14},{14,13},{17,18},{18,... | collective-permute-start | bytes 2433032 | tf_op jit(solution)/shard_map/ppermute | solution.py:460
  8.5 10.2 %collective-permute-start.2 = (bf16[3168,128]{1,0:T(8,128)(2,1)S(1)}, bf16[3168,128]{1,0:T(8,128)(2,1)S(1)}, u32[]{:S(2)}, u32[]{:S(2)}) collective-permute-start(bf16[3168,128]{1,0:T(8,128)(2,1)S(1)} %shard_map.93.after.pack_0), channel_id=1, source_target_pairs={{0,1},{1,0},{2,3},{3,2},{4,5},{5,4},{6,7},{7,6},{8,9},{9,8},{10,11... | collective-permute-start | bytes 2433032 | tf_op jit(solution)/shard_map/ppermute | solution.py:161
  8.5 1.6 %copy-start = (f32[1,524288]{1,0:T(1,128)S(1)}, f32[1,524288]{1,0:T(1,128)}, u32[]{:S(2)}) copy-start(f32[1,524288]{1,0:T(1,128)} %param.11) | copy-start | bytes 6291460
  10.1 2.2 %copy-start.1 = (f32[1,524288]{1,0:T(1,128)S(1)}, f32[1,524288]{1,0:T(1,128)}, u32[]{:S(2)}) copy-start(f32[1,524288]{1,0:T(1,128)} %param.11) | copy-start | bytes 6291460
  10.2 8.5 %copy-start.4 = (bf16[1,1,32,64,128]{4,3,2,1,0:T(8,128)(2,1)S(1)}, bf16[1,1,32,64,128]{4,3,2,1,0:T(8,128)(2,1)}, u32[]{:S(2)}) copy-start(bf16[1,1,32,64,128]{4,3,2,1,0:T(8,128)(2,1)} %param.7) | copy-start | bytes 1572868
  10.2 8.5 %copy-start.5 = (bf16[3,3,3,32,32]{4,3,2,1,0:T(8,128)(2,1)S(1)}, bf16[3,3,3,32,32]{4,3,2,1,0:T(8,128)(2,1)}, u32[]{:S(2)}) copy-start(bf16[3,3,3,32,32]{4,3,2,1,0:T(8,128)(2,1)} %two.1) | copy-start | bytes 165892
  10.2 8.5 %copy-start.6 = (bf16[3,3,3,16,32]{4,3,2,1,0:T(8,128)(2,1)S(1)}, bf16[3,3,3,16,32]{4,3,2,1,0:T(8,128)(2,1)}, u32[]{:S(2)}) copy-start(bf16[3,3,3,16,32]{4,3,2,1,0:T(8,128)(2,1)} %one.1) | copy-start | bytes 82948
  10.3 2.1 %collective-permute-start = (bf16[2048,128]{1,0:T(8,128)(2,1)S(1)}, bf16[2048,128]{1,0:T(8,128)(2,1)S(1)}, u32[]{:S(2)}, u32[]{:S(2)}) collective-permute-start(bf16[2048,128]{1,0:T(8,128)(2,1)S(1)} %shard_map.94), channel_id=1, source_target_pairs={{0,1},{1,0},{2,3},{3,2},{4,5},{5,4},{6,7},{7,6},{8,9},{9,8},{10,11... | collective-permute-start | bytes 1572872 | tf_op jit(solution)/shard_map/ppermute | solution.py:161
  12.5 11.8 %collective-permute-start.1 = (bf16[1024,128]{1,0:T(8,128)(2,1)S(1)}, bf16[1024,128]{1,0:T(8,128)(2,1)S(1)}, u32[]{:S(2)}, u32[]{:S(2)}) collective-permute-start(bf16[1024,128]{1,0:T(8,128)(2,1)S(1)} %get-tuple-element.25), channel_id=1, source_target_pairs={{0,4},{4,0},{1,5},{5,1},{2,6},{6,2},{3,7},{7,3},{8,12},{12,8},{9,1... | collective-permute-start | bytes 786440 | tf_op jit(solution)/shard_map/ppermute | solution.py:161
  24.3 1.3 %collective-permute-start.4 = (bf16[256,128]{1,0:T(8,128)(2,1)S(1)}, bf16[256,128]{1,0:T(8,128)(2,1)S(1)}, u32[]{:S(2)}, u32[]{:S(2)}) collective-permute-start(bf16[256,128]{1,0:T(8,128)(2,1)S(1)} %get-tuple-element.28), channel_id=1, source_target_pairs={{0,1},{1,0},{2,3},{3,2},{4,5},{5,4},{6,7},{7,6},{8,9},{9,8},{10,11... | collective-permute-start | bytes 196616 | tf_op jit(solution)/shard_map/ppermute | solution.py:161
  26.4 16.2 %all-to-all-start = ((bf16[8,160,128]{2,1,0:T(8,128)(2,1)}), bf16[8,160,128]{2,1,0:T(8,128)(2,1)S(1)}, u32[]{:S(2)}, u32[]{:S(2)}) async-start(bf16[8,160,128]{2,1,0:T(8,128)(2,1)} %shard_map.97), calls=%async_computation | async-start | bytes 655360 | tf_op jit(solution)/shard_map/all_to_all | solution.py:481
  31.9 4.2 %collective-permute-start.5 = (bf16[1024,128]{1,0:T(8,128)(2,1)S(1)}, bf16[1024,128]{1,0:T(8,128)(2,1)S(1)}, u32[]{:S(2)}, u32[]{:S(2)}) collective-permute-start(bf16[1024,128]{1,0:T(8,128)(2,1)S(1)} %get-tuple-element.33), channel_id=1, source_target_pairs={{0,1},{1,0},{2,3},{3,2},{4,5},{5,4},{6,7},{7,6},{8,9},{9,8},{10,11... | collective-permute-start | bytes 786440 | tf_op jit(solution)/shard_map/ppermute | solution.py:161
  32.5 9.1 %collective-permute-start.6 = (bf16[1024,128]{1,0:T(8,128)(2,1)S(1)}, bf16[1024,128]{1,0:T(8,128)(2,1)S(1)}, u32[]{:S(2)}, u32[]{:S(2)}) collective-permute-start(bf16[1024,128]{1,0:T(8,128)(2,1)S(1)} %get-tuple-element.34), channel_id=1, source_target_pairs={{1,2},{2,1},{5,6},{6,5},{9,10},{10,9},{13,14},{14,13},{17,18},{18,... | collective-permute-start | bytes 786440 | tf_op jit(solution)/shard_map/ppermute | solution.py:460
  65.4 3.9 %collective-permute-start.7 = (bf16[16,160,128]{2,1,0:T(8,128)(2,1)S(1)}, bf16[16,160,128]{2,1,0:T(8,128)(2,1)S(1)}, u32[]{:S(2)}, u32[]{:S(2)}) collective-permute-start(bf16[16,160,128]{2,1,0:T(8,128)(2,1)S(1)} %all_to_all.10.refs_0_), channel_id=1, source_target_pairs={{0,1},{1,0},{2,3},{3,2},{4,5},{5,4},{6,7},{7,6},{8,9},{9,8},{10,11... | collective-permute-start | bytes 1966088 | tf_op jit(solution)/shard_map/ppermute | solution.py:161

commit v12 on v11

--- a/solution.py
+++ b/solution.py
@@ -50,25 +50,22 @@
     lax.fori_loop(0, length, gather, 0, unroll=4)
 
 
-def pack_kernel(cot, vol, out, flat):
-    c2, length, width = cot.shape
-    pitch = c2 + vol.shape[0]
-    zeros = jnp.zeros((pitch, width), BF16)
-    out[0:pitch, :] = zeros
-    out[(length + 1) * pitch : (length + 2) * pitch, :] = zeros
-    turned(cot, flat, out, 0, pitch, 1)
-    turned(vol, flat, out, c2, pitch, 1)
-
-
-def pack(cot, vol):
-    c2, length, width = cot.shape
-    pitch = c2 + vol.shape[0]
+def pack_kernel(field, out, flat):
+    chans, length, width = field.shape
+    zeros = jnp.zeros((chans, width), BF16)
+    out[0:chans, :] = zeros
+    out[(length + 1) * chans : (length + 2) * chans, :] = zeros
+    turned(field, flat, out, 0, chans, 1)
+
+
+def pack(field):
+    chans, length, width = field.shape
     return vmem_call(
         pack_kernel,
-        jax.ShapeDtypeStruct(((length + 2) * pitch, width), BF16),
-        (pltpu.VMEM((max(c2, vol.shape[0]) * length, width), F32),),
-        pl.CostEstimate(flops=0, bytes_accessed=32 * cot.size, transcendentals=0),
-    )(cot, vol)
+        jax.ShapeDtypeStruct(((length + 2) * chans, width), BF16),
+        (pltpu.VMEM((chans * length, width), F32),),
+        pl.CostEstimate(flops=0, bytes_accessed=16 * field.size, transcendentals=0),
+    )(field)
 
 
 def in_steps(body, rows, count=8):
@@ -161,53 +158,56 @@
     return lax.ppermute(value, axis, [(0, 1), (1, 0)])
 
 
-def compute_kernel(
-    pack_in, pack_0, pack_out, act, two, one,
-    send, keep, own, inner, outer,
-    terms, flat, acts, pres, w_two, w_one, acc_two, acc_one,
-):
-    c1, length, _ = act.shape
-    c2, c0 = (two.shape[4], one.shape[3])
-    pitch = c0 + c2
-    packs = (pack_in, pack_0, pack_out)
+def plane_order():
     core = lax.axis_index("core")
     ahead = [core * n + (1 - core) * (2 - n) for n in range(3)]
     back = [core * (2 - n) + (1 - core) * n for n in range(3)]
-
+    return (ahead, back)
+
+
+def windows(packs, x, count):
+    rows = [
+        [p[pl.ds(pl.multiple_of((x + n) * count, 16), count), :] for p in packs]
+        for n in range(GROUP + 2)
+    ]
+    return jnp.concatenate(
+        [jnp.concatenate(sum(rows[g : g + 3], []), axis=0) for g in range(GROUP)], axis=1
+    )
+
+
+def ordered(acc, count, ahead):
+    blocks = [pl.multiple_of((3 * j + n) * count, 16) for j in range(3) for n in ahead]
+    return jnp.concatenate([acc[pl.ds(at, count), :] for at in blocks], axis=0)
+
+
+def across_lanes(first, second):
+    return lax.dot_general(
+        first, second, (((1,), (1,)), ((), ())), preferred_element_type=F32
+    )
+
+
+def first_kernel(pack_in, pack_0, pack_out, act, two, pres, terms, flat, acts, w_two, acc):
+    c1, length, _ = act.shape
+    c2 = two.shape[4]
+    packs = (pack_in, pack_0, pack_out)
+    ahead, back = plane_order()
     turned(act, flat, acts, 0, c1, 0)
-    offsets = [(m, n) for m in range(3) for n in range(3)]
     w_two[...] = jnp.concatenate(
         [
             jnp.concatenate([two[back[n], 2 - j, 2 - k].astype(F32) for k in range(3)], axis=0)
-            for j, n in offsets
-        ],
-        axis=1,
-    ).astype(BF16)
-    w_one[...] = jnp.concatenate(
-        [
-            jnp.concatenate([one[ahead[n], 2 - j, k].astype(F32) for n in range(3)], axis=0)
-            for j, k in offsets
+            for j in range(3)
+            for n in range(3)
         ],
         axis=1,
     ).astype(BF16)
     stacked = 3 * c1
     pres[0:stacked, :] = jnp.zeros((stacked, LANES), BF16)
     pres[(length + 1) * stacked : (length + 2) * stacked, :] = jnp.zeros((stacked, LANES), BF16)
-    acc_two[...] = jnp.zeros_like(acc_two)
-    acc_one[...] = jnp.zeros_like(acc_one)
-
-    def windows(x, offset, count):
-        rows = [
-            [p[pl.ds(pl.multiple_of((x + n) * pitch + offset, 16), count), :] for p in packs]
-            for n in range(GROUP + 2)
-        ]
-        return jnp.concatenate(
-            [jnp.concatenate(sum(rows[g : g + 3], []), axis=0) for g in range(GROUP)], axis=1
-        )
-
-    def first(step, carry):
+    acc[...] = jnp.zeros_like(acc)
+
+    def body(step, carry):
         x = step * GROUP
-        right = windows(x, 0, c2)
+        right = windows(packs, x, c2)
         sums = jnp.dot(w_two[...], right, preferred_element_type=F32)
         columns = []
         for g in range(GROUP):
@@ -219,15 +219,40 @@
             pres[pl.ds(pl.multiple_of((x + g + 1) * stacked, 16), stacked), :] = moved
             stack = jnp.concatenate([slid(value, 1), value, slid(value, -1)], axis=0)
             columns.append(stack.astype(BF16))
-        left = jnp.concatenate(columns, axis=1)
-        acc_two[...] += lax.dot_general(
-            right, left, (((1,), (1,)), ((), ())), preferred_element_type=F32
-        )
-        return carry
-
-    lax.fori_loop(0, length // GROUP, first, 0, unroll=4)
-
-    def second(step, carry):
+        acc[...] += across_lanes(right, jnp.concatenate(columns, axis=1))
+        return carry
+
+    lax.fori_loop(0, length // GROUP, body, 0, unroll=4)
+
+    terms[...] = jnp.zeros_like(terms)
+    total = ordered(acc, c2, ahead).T
+    rows, width = total.shape
+    for block in range(-(-width // LANES)):
+        part = total[:, block * LANES : min(width, (block + 1) * LANES)]
+        terms[block * rows : (block + 1) * rows, 0 : part.shape[1]] = part
+
+
+def second_kernel(
+    pack_in, pack_0, pack_out, pres, one, before,
+    send, keep, own, inner, outer,
+    w_one, acc, terms,
+):
+    c0, c1 = one.shape[3:]
+    packs = (pack_in, pack_0, pack_out)
+    ahead, _ = plane_order()
+    stacked = 3 * c1
+    length = pres.shape[0] // stacked - 2
+    w_one[...] = jnp.concatenate(
+        [
+            jnp.concatenate([one[ahead[n], 2 - j, k].astype(F32) for n in range(3)], axis=0)
+            for j in range(3)
+            for k in range(3)
+        ],
+        axis=1,
+    ).astype(BF16)
+    acc[...] = jnp.zeros_like(acc)
+
+    def body(step, carry):
         x = step * GROUP
         window = pres[pl.ds(pl.multiple_of(x * stacked, 16), (GROUP + 2) * stacked), :]
         moved = beside(window, 3 * stacked, stacked, GROUP)
@@ -237,30 +262,16 @@
             at = pl.ds(pl.multiple_of((x + g) * c0, 16), c0)
             for i, out in ((0, inner), (1, own), (2, outer)):
                 out[at, :] = part[i * c0 : (i + 1) * c0].astype(out.dtype)
-        acc_one[...] += lax.dot_general(
-            windows(x, c2, c0),
-            moved[stacked : 2 * stacked],
-            (((1,), (1,)), ((), ())),
-            preferred_element_type=F32,
-        )
-        return carry
-
-    lax.fori_loop(0, length // GROUP, second, 0, unroll=4)
-
-    terms[...] = jnp.zeros_like(terms)
-
-    def ordered(acc, count):
-        blocks = [pl.multiple_of((3 * j + n) * count, 16) for j in range(3) for n in ahead]
-        return jnp.concatenate([acc[pl.ds(at, count), :] for at in blocks], axis=0)
-
-    two = ordered(acc_two, c2).T
-    rows, width = two.shape
-    blocks = -(-width // LANES)
-    for block in range(blocks):
-        part = two[:, block * LANES : min(width, (block + 1) * LANES)]
-        terms[block * rows : (block + 1) * rows, 0 : part.shape[1]] = part
-    one = ordered(acc_one, c0)
-    terms[blocks * rows : blocks * rows + one.shape[0], 0 : one.shape[1]] = one
+        acc[...] += across_lanes(windows(packs, x, c0), moved[stacked : 2 * stacked])
+        return carry
+
+    lax.fori_loop(0, length // GROUP, body, 0, unroll=4)
+
+    used = before.shape[0]
+    terms[0:used, :] = before[...]
+    terms[used:, :] = jnp.zeros((terms.shape[0] - used, LANES), F32)
+    total = ordered(acc, c0, ahead)
+    terms[used : used + total.shape[0], 0 : total.shape[1]] = total
     split_to(terms, lax.axis_index("core"), send, keep)
 
 
@@ -276,12 +287,31 @@
     )
 
 
-def compute(packs, act, kernel_two, kernel_one, rows):
+def first_part(packs, act, kernel_two):
     c1, length, width = act.shape
-    c0, c2 = (kernel_one.shape[3], kernel_two.shape[4])
+    c2 = kernel_two.shape[4]
+    return vmem_call(
+        first_kernel,
+        (
+            jax.ShapeDtypeStruct(((length + 2) * 3 * c1, width), BF16),
+            jax.ShapeDtypeStruct((-(-9 * c2 // LANES) * 3 * c1, LANES), F32),
+        ),
+        (
+            pltpu.VMEM((c1 * length, width), F32),
+            pltpu.VMEM((c1 * length, width), BF16),
+            pltpu.VMEM((3 * c1, 9 * c2), BF16),
+            pltpu.VMEM((9 * c2, 3 * c1), F32),
+        ),
+        pl.CostEstimate(flops=10**9, bytes_accessed=20 * 2**20, transcendentals=0),
+    )(*packs, act, kernel_two)
+
+
+def second_part(packs, pres, kernel_one, terms, rows):
+    c0, c1 = kernel_one.shape[3:]
+    length, width = (pres.shape[0] // (3 * c1) - 2, pres.shape[1])
     plane = (length * c0, width)
     return vmem_call(
-        compute_kernel,
+        second_kernel,
         (
             jax.ShapeDtypeStruct((rows // 2, LANES), BF16),
             jax.ShapeDtypeStruct((rows // 2, LANES), F32),
@@ -290,17 +320,12 @@
             jax.ShapeDtypeStruct(plane, BF16),
         ),
         (
+            pltpu.VMEM((3 * c0, 9 * c1), BF16),
+            pltpu.VMEM((9 * c0, 3 * c1), F32),
             pltpu.VMEM((rows, LANES), F32),
-            pltpu.VMEM((c1 * length, width), F32),
-            pltpu.VMEM((c1 * length, width), BF16),
-            pltpu.VMEM(((length + 2) * 3 * c1, width), BF16),
-            pltpu.VMEM((3 * c1, 9 * c2), BF16),
-            pltpu.VMEM((3 * c0, 9 * c1), BF16),
-            pltpu.VMEM((9 * c2, 3 * c1), F32),
-            pltpu.VMEM((9 * c0, 3 * c1), F32),
         ),
-        pl.CostEstimate(flops=10**10, bytes_accessed=40 * 2**20, transcendentals=0),
-    )(*packs, act, kernel_two, kernel_one)
+        pl.CostEstimate(flops=10**9, bytes_accessed=10 * 2**20, transcendentals=0),
+    )(*packs, pres, kernel_one, terms)
 
 
 def merge_kernel(own, first, second, out, flat):
@@ -465,17 +490,18 @@
     devices, copies, column = (lax.axis_size(EVERY), lax.axis_size(SAME), lax.axis_size(COLUMN))
     length = grad_bucket.shape[1]
     bucket = grad_bucket.reshape(length // LANES, LANES)
-    packed = pack(out_cot[0, 0], volume_in[0, 0])
-    outer, inner = (crossed(packed), swapped(packed))
-    send, near = add(bucket, swapped(cast(bucket, packed)))
+    cot = pack(out_cot[0, 0])
+    cots = (swapped(cot), cot, crossed(cot))
+    vol = pack(volume_in[0, 0])
+    vols = (swapped(vol), vol, crossed(vol))
+    send, near = add(bucket, swapped(cast(bucket, cot)))
     act, send, near = lax.optimization_barrier((hidden_act[0, 0], send, near))
     far = swapped(send, "x")
 
     used = -(-9 * c2 // LANES) * 3 * c1 + 9 * c0
     rows = ceil_to(used, 16 * 2 * column)
-    send, keep, own, inner, outer = compute(
-        (inner, packed, outer), act, kernel_two, kernel_one, rows
-    )
+    pres, terms = first_part(cots, act, kernel_two)
+    send, keep, own, inner, outer = second_part(vols, pres, kernel_one, terms, rows)
     parts = combine(near, far, keep, swapped(send), column)
     parts, inner, outer = lax.optimization_barrier((parts, inner, outer))
     parts = lax.all_to_all(parts, COLUMN, 0, 0)

time: 71.4 us -> 67.1 us (0.940)
  waiting for transfers between devices: 13.9 us -> 8.5 us
  starting transfers between devices: 18.4 us -> 20.4 us
  local copies, waits for them, and re-layouts: 3.59 us -> 2.65 us
    ppermute x2 -> x3, waiting for transfers between devices: 10.4 us -> 6.54 us  [crossed(): return lax.ppermute(value, SPACE, pairs + [(m, n) for n, m in pairs])]
    ppermute x2 -> x3, starting transfers between devices: 8.06 us -> 9.98 us  [crossed(): return lax.ppermute(value, SPACE, pairs + [(m, n) for n, m in pairs])]
    ppermute x6 -> x7, waiting for transfers between devices: 3.48 us -> 1.96 us  [swapped(): return lax.ppermute(value, axis, [(0, 1), (1, 0)])]
    unnamed x14, local copies, waits for them, and re-layouts: 3.59 us -> 2.65 us
    ppermute x6 -> x7, starting transfers between devices: 4.77 us -> 4.84 us  [swapped(): return lax.ppermute(value, axis, [(0, 1), (1, 0)])]
    pallas_call x2 -> x4, Pallas kernels: 6.86 us -> 6.82 us  [the longest x1 3.58 us: first_part(): vmem_call(first_kernel, (jax.ShapeDtypeStruct(((length + 2) * 3 * c1, wid...]
  transfers between devices with their start and end apart: 9 -> 11, of which waited for: 5 -> 5; matrix products, arithmetic and copies ran while one was open for 0% -> 0% of each run, Pallas kernels for 11% -> 12%
where the time goes in v12:
time: 67.1 us; the launch traced here: 66.4 us
  blocking collectives  22.6 us (34%)
  starting transfers between devices  20.4 us (30%)
  Pallas kernels  11.4 us (17%)
  waiting for transfers between devices  8.5 us (13%)
  local copies, waits for them, and re-layouts  2.65 us (4%)
  between operations  0.81 us (1%)
    all_to_all x1, blocking collectives, per_device(): mine = lax.all_to_all(shares, SAME, 0, 0)  22.6 us
    ppermute x3, starting transfers between devices, crossed(): return lax.ppermute(value, SPACE, pairs + [(m, n) for n, m in pairs])  9.98 us
    ppermute x3, waiting for transfers between devices, crossed(): return lax.ppermute(value, SPACE, pairs + [(m, n) for n, m in pairs])  6.54 us
    all_to_all x1, starting transfers between devices, per_device(): parts = lax.all_to_all(parts, COLUMN, 0, 0)  5.58 us
    ppermute x7, starting transfers between devices, swapped(): return lax.ppermute(value, axis, [(0, 1), (1, 0)])  4.84 us
    pallas_call x1, Pallas kernels, first_part(): vmem_call(first_kernel, (jax.ShapeDtypeStruct(((length + 2) * 3 * c1, wid...  3.58 us
    unnamed x14, local copies, waits for them, and re-layouts  2.65 us
    pallas_call x1, Pallas kernels, second_part(): vmem_call(second_kernel, (jax.ShapeDtypeStruct((rows // 2, LANES), BF16),...  1.98 us
  transfers between devices with their start and end apart: 11, of which 5 were waited for; matrix products, arithmetic and copies ran while one was open for 0% of the time, Pallas kernels for 12%

profile of v12, /device:TPU:1, one launch (start us, length us, event | category | flops | bytes accessed | tf_op | source)
XLA Modules:
  0.0 66.4 jit_solution(8307171873309690335)
XLA Ops:
  0.6 0.0 copy-start.2
  0.6 1.0 %copy-done.2 = bf16[1,1,32,64,128]{4,3,2,1,0:T(8,128)(2,1)S(1)} copy-done((bf16[1,1,32,64,128]{4,3,2,1,0:T(8,128)(2,1)S(1)}, bf16[1,1,32,64,128]{4,3,2,1,0:T(8,128)(2,1)}, u32[]{:S(2)}) %copy-start.2) | copy-done | bytes 524312
  1.7 0.0 copy-start.3
  1.7 0.8 %shard_map.93.after.pack_0 = bf16[2112,128]{1,0:T(8,128)(2,1)S(1)} custom-call(bf16[32,64,128]{2,1,0:T(8,128)(2,1)S(1)} %bitcast.10), custom_call_target="tpu_custom_call" | custom-call | bytes 4194304 | tf_op jit(solution)/shard_map/pallas_call | solution.py:63
  2.5 4.5 %collective-permute-start.5 = (bf16[2112,128]{1,0:T(8,128)(2,1)S(1)}, bf16[2112,128]{1,0:T(8,128)(2,1)S(1)}, u32[]{:S(2)}, u32[]{:S(2)}) collective-permute-start(bf16[2112,128]{1,0:T(8,128)(2,1)S(1)} %shard_map.93.after.pack_0), channel_id=1, source_target_pairs={{1,2},{2,1},{5,6},{6,5},{9,10},{10,9},{13,14},{14,13},{17,18},{18,... | collective-permute-start | bytes 1622024 | tf_op jit(solution)/shard_map/ppermute | solution.py:485
  7.0 0.1 collective-permute-start.4
  7.1 0.0 copy-start
  7.1 1.6 %copy-done = f32[1,524288]{1,0:T(1,128)S(1)} copy-done((f32[1,524288]{1,0:T(1,128)S(1)}, f32[1,524288]{1,0:T(1,128)}, u32[]{:S(2)}) %copy-start) | copy-done | bytes 2097176
  8.7 0.0 copy-start.1
  8.7 0.1 shard_map.94
  8.8 0.0 copy-start.4
  8.8 0.0 copy-start.5
  8.8 0.6 collective-permute-start
  9.4 0.0 copy-done.3
  9.4 0.5 shard_map.96.pack_0
  9.8 1.9 %collective-permute-start.3 = (bf16[1056,128]{1,0:T(8,128)(2,1)S(1)}, bf16[1056,128]{1,0:T(8,128)(2,1)S(1)}, u32[]{:S(2)}, u32[]{:S(2)}) collective-permute-start(bf16[1056,128]{1,0:T(8,128)(2,1)S(1)} %shard_map.96.pack_0), channel_id=1, source_target_pairs={{1,2},{2,1},{5,6},{6,5},{9,10},{10,9},{13,14},{14,13},{17,18},{18,... | collective-permute-start | bytes 811016 | tf_op jit(solution)/shard_map/ppermute | solution.py:485
  11.8 0.1 collective-permute-start.2
  11.8 0.0 collective-permute-done.other
  11.9 0.0 copy-done.1
  11.9 0.2 shard_map.95
  12.0 0.0 copy-start.6
  12.0 1.3 %collective-permute-start.1 = (bf16[1024,128]{1,0:T(8,128)(2,1)S(1)}, bf16[1024,128]{1,0:T(8,128)(2,1)S(1)}, u32[]{:S(2)}, u32[]{:S(2)}) collective-permute-start(bf16[1024,128]{1,0:T(8,128)(2,1)S(1)} %get-tuple-element.27), channel_id=1, source_target_pairs={{0,4},{4,0},{1,5},{5,1},{2,6},{6,2},{3,7},{7,3},{8,12},{12,8},{9,1... | collective-permute-start | bytes 786440 | tf_op jit(solution)/shard_map/ppermute | solution.py:158
  13.3 0.7 %collective-permute-done.5.pack_out = bf16[2112,128]{1,0:T(8,128)(2,1)S(1)} collective-permute-done((bf16[2112,128]{1,0:T(8,128)(2,1)S(1)}, bf16[2112,128]{1,0:T(8,128)(2,1)S(1)}, u32[]{:S(2)}, u32[]{:S(2)}) %collective-permute-start.5) | collective-permute-done | bytes 540704 | tf_op jit(solution)/shard_map/ppermute | solution.py:485
  14.1 0.0 collective-permute-done.4.pack_in
  14.1 0.0 copy-done.4
  14.1 0.0 copy-done.5
  14.1 3.6 %shard_map.97 = (bf16[6336,128]{1,0:T(8,128)(2,1)S(1)}, f32[288,128]{1,0:T(8,128)S(1)}) custom-call(bf16[2112,128]{1,0:T(8,128)(2,1)S(1)} %collective-permute-done.4.pack_in, bf16[2112,128]{1,0:T(8,128)(2,1)S(1)} %shard_map.93.after.pack_0, bf16[2112,128]{1,0:T(8,128)(2,1)S(1)} %collective-permute-done.5.pack_out, bf16[32,64,128]{2,1,0:T(8,128)(2,1)S(1)} %bitcast.12, ...), custom_call_target="tpu_custom_call" | custom-call | flops 1000000000 | bytes 20971520 | tf_op jit(solution)/shard_map/pallas_call | solution.py:293
  17.6 0.3 collective-permute-done.3.pack_out
  17.9 0.0 collective-permute-done.2.pack_in
  17.9 0.0 copy-done.6
  17.9 2.0 %shard_map.98 = (bf16[256,128]{1,0:T(8,128)(2,1)S(1)}, f32[256,128]{1,0:T(8,128)S(1)}, f32[1024,128]{1,0:T(8,128)S(1)}, bf16[1024,128]{1,0:T(8,128)(2,1)S(1)}, bf16[1024,128]{1,0:T(8,128)(2,1)S(1)}) custom-call(bf16[1056,128]{1,0:T(8,128)(2,1)S(1)} %collective-permute-done.2.pack_in, bf16[1056,128]{1,0:T(8,128)(2,1)S(1)} %shard_map.96.pack_0, ...), custom_call_target="tpu_custom_call" | custom-call | flops 1000000000 | bytes 10485760 | tf_op jit(solution)/shard_map/pallas_call | solution.py:313
  19.9 0.1 collective-permute-start.6
  20.0 1.2 %collective-permute-done.6.more = bf16[256,128]{1,0:T(8,128)(2,1)S(1)} collective-permute-done((bf16[256,128]{1,0:T(8,128)(2,1)S(1)}, bf16[256,128]{1,0:T(8,128)(2,1)S(1)}, u32[]{:S(2)}, u32[]{:S(2)}) %collective-permute-start.6) | collective-permute-done | bytes 65568 | tf_op jit(solution)/shard_map/ppermute | solution.py:158
  21.2 0.0 collective-permute-done.1.other
  21.2 0.8 %shard_map.99 = bf16[8,160,128]{2,1,0:T(8,128)(2,1)} custom-call(f32[1024,128]{1,0:T(8,128)S(1)} %get-tuple-element.26.keep, bf16[1024,128]{1,0:T(8,128)(2,1)S(1)} %collective-permute-done.1.other, f32[256,128]{1,0:T(8,128)S(1)} %get-tuple-element.31.terms, bf16[256,128]{1,0:T(8,128)(2,1)S(1)} %collective-permute-done.6.more), custom_call_target="tpu_custom_call" | custom-call | bytes 1048576 | tf_op jit(solution)/shard_map/pallas_call | solution.py:143
  22.0 5.6 %all-to-all-start = ((bf16[8,160,128]{2,1,0:T(8,128)(2,1)}), bf16[8,160,128]{2,1,0:T(8,128)(2,1)S(1)}, u32[]{:S(2)}, u32[]{:S(2)}) async-start(bf16[8,160,128]{2,1,0:T(8,128)(2,1)} %shard_map.99), calls=%async_computation | async-start | bytes 655360 | tf_op jit(solution)/shard_map/all_to_all | solution.py:507
  27.6 0.6 collective-permute-start.7
  28.3 3.5 %collective-permute-start.8 = (bf16[1024,128]{1,0:T(8,128)(2,1)S(1)}, bf16[1024,128]{1,0:T(8,128)(2,1)S(1)}, u32[]{:S(2)}, u32[]{:S(2)}) collective-permute-start(bf16[1024,128]{1,0:T(8,128)(2,1)S(1)} %get-tuple-element.38), channel_id=1, source_target_pairs={{1,2},{2,1},{5,6},{6,5},{9,10},{10,9},{13,14},{14,13},{17,18},{18,... | collective-permute-start | bytes 786440 | tf_op jit(solution)/shard_map/ppermute | solution.py:485
  31.8 0.0 collective-permute-done.7.first
  31.8 5.5 %collective-permute-done.8.second = bf16[1024,128]{1,0:T(8,128)(2,1)S(1)} collective-permute-done((bf16[1024,128]{1,0:T(8,128)(2,1)S(1)}, bf16[1024,128]{1,0:T(8,128)(2,1)S(1)}, u32[]{:S(2)}, u32[]{:S(2)}) %collective-permute-start.8) | collective-permute-done | bytes 262176 | tf_op jit(solution)/shard_map/ppermute | solution.py:485
  37.3 1.0 %shard_map.100 = bf16[16,64,128]{2,1,0:T(8,128)(2,1)} custom-call(f32[1024,128]{1,0:T(8,128)S(1)} %get-tuple-element.36.own, bf16[1024,128]{1,0:T(8,128)(2,1)S(1)} %collective-permute-done.7.first, bf16[1024,128]{1,0:T(8,128)(2,1)S(1)} %collective-permute-done.8.second), custom_call_target="tpu_custom_call" | custom-call | flops 262144 | bytes 1048576 | tf_op jit(solution)/shard_map/pallas_call | solution.py:349
  38.3 0.0 all-to-all-done.refs_0_
  38.3 0.1 shard_map.101
  38.4 22.6 %all_to_all.10.refs_0_ = bf16[16,160,128]{2,1,0:T(8,128)(2,1)S(1)} all-to-all(bf16[16,160,128]{2,1,0:T(8,128)(2,1)S(1)} %shard_map.101), channel_id=1, replica_groups=mesh['z'=4,'x'=2,'y'=2,'core'=2] {'x','z','y'}, dimensions={0} | all-to-all | bytes 1310720 | tf_op jit(solution)/shard_map/all_to_all | solution.py:514
  61.1 2.2 %collective-permute-start.9 = (bf16[16,160,128]{2,1,0:T(8,128)(2,1)S(1)}, bf16[16,160,128]{2,1,0:T(8,128)(2,1)S(1)}, u32[]{:S(2)}, u32[]{:S(2)}) collective-permute-start(bf16[16,160,128]{2,1,0:T(8,128)(2,1)S(1)} %all_to_all.10.refs_0_), channel_id=1, source_target_pairs={{0,1},{1,0},{2,3},{3,2},{4,5},{5,4},{6,7},{7,6},{8,9},{9,8},{10,11... | collective-permute-start | bytes 1966088 | tf_op jit(solution)/shard_map/ppermute | solution.py:158
  63.2 1.0 %shard_map.102.refs_2_ = f32[4096,128]{1,0:T(8,128)} custom-call(bf16[16,160,128]{2,1,0:T(8,128)(2,1)S(1)} %all_to_all.10.refs_0_), custom_call_target="tpu_custom_call" | custom-call | tf_op jit(solution)/shard_map/pallas_call | solution.py:454
  64.3 0.7 %collective-permute-done.9.refs_1_ = bf16[16,160,128]{2,1,0:T(8,128)(2,1)S(1)} collective-permute-done((bf16[16,160,128]{2,1,0:T(8,128)(2,1)S(1)}, bf16[16,160,128]{2,1,0:T(8,128)(2,1)S(1)}, u32[]{:S(2)}, u32[]{:S(2)}) %collective-permute-start.9) | collective-permute-done | bytes 655392 | tf_op jit(solution)/shard_map/ppermute | solution.py:158
  65.0 1.4 %shard_map.103 = (f32[4096,128]{1,0:T(8,128)}, f32[432,32]{1,0:T(8,128)}, f32[864,32]{1,0:T(8,128)}) custom-call(bf16[16,160,128]{2,1,0:T(8,128)(2,1)S(1)} %all_to_all.10.refs_0_, bf16[16,160,128]{2,1,0:T(8,128)(2,1)S(1)} %collective-permute-done.9.refs_1_, f32[4096,128]{1,0:T(8,128)} %shard_map.102.refs_2_), custom_call_target="tpu_custom_call", output_to_operand_aliasing={{0}: (2, {})} | custom-call | tf_op jit(solution)/shard_map/pallas_call | solution.py:462
Async XLA Ops:
  0.6 1.0 %copy-start.2 = (bf16[1,1,32,64,128]{4,3,2,1,0:T(8,128)(2,1)S(1)}, bf16[1,1,32,64,128]{4,3,2,1,0:T(8,128)(2,1)}, u32[]{:S(2)}) copy-start(bf16[1,1,32,64,128]{4,3,2,1,0:T(8,128)(2,1)} %param.8) | copy-start | bytes 1572868
  1.7 7.7 %copy-start.3 = (bf16[1,1,16,64,128]{4,3,2,1,0:T(8,128)(2,1)S(1)}, bf16[1,1,16,64,128]{4,3,2,1,0:T(8,128)(2,1)}, u32[]{:S(2)}) copy-start(bf16[1,1,16,64,128]{4,3,2,1,0:T(8,128)(2,1)} %param.6) | copy-start | bytes 786436
  2.5 11.6 %collective-permute-start.5 = (bf16[2112,128]{1,0:T(8,128)(2,1)S(1)}, bf16[2112,128]{1,0:T(8,128)(2,1)S(1)}, u32[]{:S(2)}, u32[]{:S(2)}) collective-permute-start(bf16[2112,128]{1,0:T(8,128)(2,1)S(1)} %shard_map.93.after.pack_0), channel_id=1, source_target_pairs={{1,2},{2,1},{5,6},{6,5},{9,10},{10,9},{13,14},{14,13},{17,18},{18,... | collective-permute-start | bytes 1622024 | tf_op jit(solution)/shard_map/ppermute | solution.py:485
  7.0 7.0 %collective-permute-start.4 = (bf16[2112,128]{1,0:T(8,128)(2,1)S(1)}, bf16[2112,128]{1,0:T(8,128)(2,1)S(1)}, u32[]{:S(2)}, u32[]{:S(2)}) collective-permute-start(bf16[2112,128]{1,0:T(8,128)(2,1)S(1)} %shard_map.93.after.pack_0), channel_id=1, source_target_pairs={{0,1},{1,0},{2,3},{3,2},{4,5},{5,4},{6,7},{7,6},{8,9},{9,8},{10,11... | collective-permute-start | bytes 1622024 | tf_op jit(solution)/shard_map/ppermute | solution.py:158
  7.1 1.6 %copy-start = (f32[1,524288]{1,0:T(1,128)S(1)}, f32[1,524288]{1,0:T(1,128)}, u32[]{:S(2)}) copy-start(f32[1,524288]{1,0:T(1,128)} %param.11) | copy-start | bytes 6291460
  8.7 3.2 %copy-start.1 = (f32[1,524288]{1,0:T(1,128)S(1)}, f32[1,524288]{1,0:T(1,128)}, u32[]{:S(2)}) copy-start(f32[1,524288]{1,0:T(1,128)} %param.11) | copy-start | bytes 6291460
  8.8 5.3 %copy-start.4 = (bf16[1,1,32,64,128]{4,3,2,1,0:T(8,128)(2,1)S(1)}, bf16[1,1,32,64,128]{4,3,2,1,0:T(8,128)(2,1)}, u32[]{:S(2)}) copy-start(bf16[1,1,32,64,128]{4,3,2,1,0:T(8,128)(2,1)} %param.7) | copy-start | bytes 1572868
  8.8 5.3 %copy-start.5 = (bf16[3,3,3,32,32]{4,3,2,1,0:T(8,128)(2,1)S(1)}, bf16[3,3,3,32,32]{4,3,2,1,0:T(8,128)(2,1)}, u32[]{:S(2)}) copy-start(bf16[3,3,3,32,32]{4,3,2,1,0:T(8,128)(2,1)} %two.1) | copy-start | bytes 165892
  8.8 3.0 %collective-permute-start = (bf16[2048,128]{1,0:T(8,128)(2,1)S(1)}, bf16[2048,128]{1,0:T(8,128)(2,1)S(1)}, u32[]{:S(2)}, u32[]{:S(2)}) collective-permute-start(bf16[2048,128]{1,0:T(8,128)(2,1)S(1)} %shard_map.94), channel_id=1, source_target_pairs={{0,1},{1,0},{2,3},{3,2},{4,5},{5,4},{6,7},{7,6},{8,9},{9,8},{10,11... | collective-permute-start | bytes 1572872 | tf_op jit(solution)/shard_map/ppermute | solution.py:158
  9.8 8.1 %collective-permute-start.3 = (bf16[1056,128]{1,0:T(8,128)(2,1)S(1)}, bf16[1056,128]{1,0:T(8,128)(2,1)S(1)}, u32[]{:S(2)}, u32[]{:S(2)}) collective-permute-start(bf16[1056,128]{1,0:T(8,128)(2,1)S(1)} %shard_map.96.pack_0), channel_id=1, source_target_pairs={{1,2},{2,1},{5,6},{6,5},{9,10},{10,9},{13,14},{14,13},{17,18},{18,... | collective-permute-start | bytes 811016 | tf_op jit(solution)/shard_map/ppermute | solution.py:485
  11.8 6.1 %collective-permute-start.2 = (bf16[1056,128]{1,0:T(8,128)(2,1)S(1)}, bf16[1056,128]{1,0:T(8,128)(2,1)S(1)}, u32[]{:S(2)}, u32[]{:S(2)}) collective-permute-start(bf16[1056,128]{1,0:T(8,128)(2,1)S(1)} %shard_map.96.pack_0), channel_id=1, source_target_pairs={{0,1},{1,0},{2,3},{3,2},{4,5},{5,4},{6,7},{7,6},{8,9},{9,8},{10,11... | collective-permute-start | bytes 811016 | tf_op jit(solution)/shard_map/ppermute | solution.py:158
  12.0 5.9 %copy-start.6 = (bf16[3,3,3,16,32]{4,3,2,1,0:T(8,128)(2,1)S(1)}, bf16[3,3,3,16,32]{4,3,2,1,0:T(8,128)(2,1)}, u32[]{:S(2)}) copy-start(bf16[3,3,3,16,32]{4,3,2,1,0:T(8,128)(2,1)} %one.1) | copy-start | bytes 82948
  12.0 9.2 %collective-permute-start.1 = (bf16[1024,128]{1,0:T(8,128)(2,1)S(1)}, bf16[1024,128]{1,0:T(8,128)(2,1)S(1)}, u32[]{:S(2)}, u32[]{:S(2)}) collective-permute-start(bf16[1024,128]{1,0:T(8,128)(2,1)S(1)} %get-tuple-element.27), channel_id=1, source_target_pairs={{0,4},{4,0},{1,5},{5,1},{2,6},{6,2},{3,7},{7,3},{8,12},{12,8},{9,1... | collective-permute-start | bytes 786440 | tf_op jit(solution)/shard_map/ppermute | solution.py:158
  19.9 1.3 %collective-permute-start.6 = (bf16[256,128]{1,0:T(8,128)(2,1)S(1)}, bf16[256,128]{1,0:T(8,128)(2,1)S(1)}, u32[]{:S(2)}, u32[]{:S(2)}) collective-permute-start(bf16[256,128]{1,0:T(8,128)(2,1)S(1)} %get-tuple-element.32), channel_id=1, source_target_pairs={{0,1},{1,0},{2,3},{3,2},{4,5},{5,4},{6,7},{7,6},{8,9},{9,8},{10,11... | collective-permute-start | bytes 196616 | tf_op jit(solution)/shard_map/ppermute | solution.py:158
  22.0 16.3 %all-to-all-start = ((bf16[8,160,128]{2,1,0:T(8,128)(2,1)}), bf16[8,160,128]{2,1,0:T(8,128)(2,1)S(1)}, u32[]{:S(2)}, u32[]{:S(2)}) async-start(bf16[8,160,128]{2,1,0:T(8,128)(2,1)} %shard_map.99), calls=%async_computation | async-start | bytes 655360 | tf_op jit(solution)/shard_map/all_to_all | solution.py:507
  27.6 4.2 %collective-permute-start.7 = (bf16[1024,128]{1,0:T(8,128)(2,1)S(1)}, bf16[1024,128]{1,0:T(8,128)(2,1)S(1)}, u32[]{:S(2)}, u32[]{:S(2)}) collective-permute-start(bf16[1024,128]{1,0:T(8,128)(2,1)S(1)} %get-tuple-element.37), channel_id=1, source_target_pairs={{0,1},{1,0},{2,3},{3,2},{4,5},{5,4},{6,7},{7,6},{8,9},{9,8},{10,11... | collective-permute-start | bytes 786440 | tf_op jit(solution)/shard_map/ppermute | solution.py:158
  28.3 9.1 %collective-permute-start.8 = (bf16[1024,128]{1,0:T(8,128)(2,1)S(1)}, bf16[1024,128]{1,0:T(8,128)(2,1)S(1)}, u32[]{:S(2)}, u32[]{:S(2)}) collective-permute-start(bf16[1024,128]{1,0:T(8,128)(2,1)S(1)} %get-tuple-element.38), channel_id=1, source_target_pairs={{1,2},{2,1},{5,6},{6,5},{9,10},{10,9},{13,14},{14,13},{17,18},{18,... | collective-permute-start | bytes 786440 | tf_op jit(solution)/shard_map/ppermute | solution.py:485
  61.1 3.9 %collective-permute-start.9 = (bf16[16,160,128]{2,1,0:T(8,128)(2,1)S(1)}, bf16[16,160,128]{2,1,0:T(8,128)(2,1)S(1)}, u32[]{:S(2)}, u32[]{:S(2)}) collective-permute-start(bf16[16,160,128]{2,1,0:T(8,128)(2,1)S(1)} %all_to_all.10.refs_0_), channel_id=1, source_target_pairs={{0,1},{1,0},{2,3},{3,2},{4,5},{5,4},{6,7},{7,6},{8,9},{9,8},{10,11... | collective-permute-start | bytes 1966088 | tf_op jit(solution)/shard_map/ppermute | solution.py:158

commit v13 on v12

--- a/solution.py
+++ b/solution.py
@@ -8,7 +8,6 @@
 from jax.sharding import Mesh, PartitionSpec as P
 
 SPACE = ("y", "core")
-COLUMN = ("z", "y")
 SAME = ("x", "z", "y")
 EVERY = ("z", "x", "y", "core")
 GROUP = 8
@@ -130,16 +129,21 @@
 
 
 def combine_kernel(keep, other, terms, more, out):
-    height, extra = (keep.shape[0] // out.shape[0], terms.shape[0] // out.shape[0])
-    for n in range(out.shape[0]):
-        at = slice(n * height, (n + 1) * height)
-        out[n, 0:height, :] = (keep[at, :] + other[at, :].astype(F32)).astype(out.dtype)
-        at = slice(n * extra, (n + 1) * extra)
-        out[n, height : height + extra, :] = (terms[at, :] + more[at, :].astype(F32)).astype(out.dtype)
+    parts, rows, _ = out.shape
+    height, extra = (keep.shape[0] // parts, terms.shape[0] // parts)
+    padded = rows - extra
+    total = keep[...] + other[...].astype(F32)
+    grads = terms[...] + more[...].astype(F32)
+    for n in range(parts):
+        value = total[n * height : (n + 1) * height]
+        if padded > height:
+            value = jnp.concatenate([value, jnp.zeros((padded - height, LANES), F32)], axis=0)
+        out[n, 0:padded, :] = value.astype(out.dtype)
+        out[n, padded:rows, :] = grads[n * extra : (n + 1) * extra].astype(out.dtype)
 
 
 def combine(keep, other, terms, more, parts):
-    rows = (keep.shape[0] + terms.shape[0]) // parts
+    rows = ceil_to(keep.shape[0] // parts, 16) + terms.shape[0] // parts
     return vmem_call(
         combine_kernel,
         jax.ShapeDtypeStruct((parts, rows, LANES), BF16),
@@ -186,12 +190,9 @@
     )
 
 
-def first_kernel(pack_in, pack_0, pack_out, act, two, pres, terms, flat, acts, w_two, acc):
-    c1, length, _ = act.shape
-    c2 = two.shape[4]
-    packs = (pack_in, pack_0, pack_out)
+def prepare_kernel(act, two, one, acts, w_two, w_one, flat):
     ahead, back = plane_order()
-    turned(act, flat, acts, 0, c1, 0)
+    turned(act, flat, acts, 0, act.shape[0], 0)
     w_two[...] = jnp.concatenate(
         [
             jnp.concatenate([two[back[n], 2 - j, 2 - k].astype(F32) for k in range(3)], axis=0)
@@ -200,6 +201,36 @@
         ],
         axis=1,
     ).astype(BF16)
+    w_one[...] = jnp.concatenate(
+        [
+            jnp.concatenate([one[ahead[n], 2 - j, k].astype(F32) for n in range(3)], axis=0)
+            for j in range(3)
+            for k in range(3)
+        ],
+        axis=1,
+    ).astype(BF16)
+
+
+def prepare(act, kernel_two, kernel_one):
+    c1, length, width = act.shape
+    c0, c2 = (kernel_one.shape[3], kernel_two.shape[4])
+    return vmem_call(
+        prepare_kernel,
+        (
+            jax.ShapeDtypeStruct((length * c1, width), BF16),
+            jax.ShapeDtypeStruct((3 * c1, 9 * c2), BF16),
+            jax.ShapeDtypeStruct((3 * c0, 9 * c1), BF16),
+        ),
+        (pltpu.VMEM((c1 * length, width), F32),),
+        pl.CostEstimate(flops=0, bytes_accessed=16 * act.size, transcendentals=0),
+    )(act, kernel_two, kernel_one)
+
+
+def first_kernel(pack_in, pack_0, pack_out, acts, w_two, pres, terms, acc):
+    c1, c2 = (w_two.shape[0] // 3, w_two.shape[1] // 9)
+    length = acts.shape[0] // c1
+    packs = (pack_in, pack_0, pack_out)
+    ahead, _ = plane_order()
     stacked = 3 * c1
     pres[0:stacked, :] = jnp.zeros((stacked, LANES), BF16)
     pres[(length + 1) * stacked : (length + 2) * stacked, :] = jnp.zeros((stacked, LANES), BF16)
@@ -233,23 +264,15 @@
 
 
 def second_kernel(
-    pack_in, pack_0, pack_out, pres, one, before,
+    pack_in, pack_0, pack_out, pres, w_one, before,
     send, keep, own, inner, outer,
-    w_one, acc, terms,
+    acc, terms,
 ):
-    c0, c1 = one.shape[3:]
+    c0, c1 = (w_one.shape[0] // 3, w_one.shape[1] // 9)
     packs = (pack_in, pack_0, pack_out)
     ahead, _ = plane_order()
     stacked = 3 * c1
     length = pres.shape[0] // stacked - 2
-    w_one[...] = jnp.concatenate(
-        [
-            jnp.concatenate([one[ahead[n], 2 - j, k].astype(F32) for n in range(3)], axis=0)
-            for j in range(3)
-            for k in range(3)
-        ],
-        axis=1,
-    ).astype(BF16)
     acc[...] = jnp.zeros_like(acc)
 
     def body(step, carry):
@@ -287,27 +310,22 @@
     )
 
 
-def first_part(packs, act, kernel_two):
-    c1, length, width = act.shape
-    c2 = kernel_two.shape[4]
+def first_part(packs, acts, w_two):
+    c1, c2, width = (w_two.shape[0] // 3, w_two.shape[1] // 9, acts.shape[1])
+    length = acts.shape[0] // c1
     return vmem_call(
         first_kernel,
         (
             jax.ShapeDtypeStruct(((length + 2) * 3 * c1, width), BF16),
             jax.ShapeDtypeStruct((-(-9 * c2 // LANES) * 3 * c1, LANES), F32),
         ),
-        (
-            pltpu.VMEM((c1 * length, width), F32),
-            pltpu.VMEM((c1 * length, width), BF16),
-            pltpu.VMEM((3 * c1, 9 * c2), BF16),
-            pltpu.VMEM((9 * c2, 3 * c1), F32),
-        ),
+        (pltpu.VMEM((9 * c2, 3 * c1), F32),),
         pl.CostEstimate(flops=10**9, bytes_accessed=20 * 2**20, transcendentals=0),
-    )(*packs, act, kernel_two)
-
-
-def second_part(packs, pres, kernel_one, terms, rows):
-    c0, c1 = kernel_one.shape[3:]
+    )(*packs, acts, w_two)
+
+
+def second_part(packs, pres, w_one, terms, rows):
+    c0, c1 = (w_one.shape[0] // 3, w_one.shape[1] // 9)
     length, width = (pres.shape[0] // (3 * c1) - 2, pres.shape[1])
     plane = (length * c0, width)
     return vmem_call(
@@ -320,12 +338,11 @@
             jax.ShapeDtypeStruct(plane, BF16),
         ),
         (
-            pltpu.VMEM((3 * c0, 9 * c1), BF16),
             pltpu.VMEM((9 * c0, 3 * c1), F32),
             pltpu.VMEM((rows, LANES), F32),
         ),
         pl.CostEstimate(flops=10**9, bytes_accessed=10 * 2**20, transcendentals=0),
-    )(*packs, pres, kernel_one, terms)
+    )(*packs, pres, w_one, terms)
 
 
 def merge_kernel(own, first, second, out, flat):
@@ -354,65 +371,69 @@
     )(own, first, second)
 
 
-def share_kernel(scale, height, parts, out):
-    total = jnp.sum(parts[:, 0:height, :].astype(F32), axis=0).astype(BF16)
-    rows = parts.shape[1]
-    grads = (jnp.sum(parts[:, height:rows, :].astype(F32), axis=0) * scale).astype(BF16)
+def share_kernel(scale, parts, out):
+    copies, rows, _ = parts.shape
+    padded = out.shape[1] - rows
+    near = jnp.sum(parts[0 : copies // 2, 0:padded, :].astype(F32), axis=0).astype(BF16)
+    far = jnp.sum(parts[copies // 2 :, 0:padded, :].astype(F32), axis=0).astype(BF16)
+    grads = (jnp.sum(parts[:, padded:rows, :].astype(F32), axis=0) * scale).astype(BF16)
 
     def write(n, carry):
-        out[n, 0:height, :] = total
-        out[n, height:rows, :] = grads
-        return carry
-
-    lax.fori_loop(0, out.shape[0], write, 0)
-
-
-def share(parts, height, scale, copies):
-    return vmem_call(
-        lambda *refs: share_kernel(scale, height, *refs),
-        jax.ShapeDtypeStruct((copies,) + parts.shape[1:], BF16),
+        out[n, 0:padded, :] = near
+        out[n, padded : 2 * padded, :] = far
+        out[n, 2 * padded :, :] = grads
+        return carry
+
+    lax.fori_loop(0, copies, write, 0)
+
+
+def share(parts, extra, scale):
+    copies, rows, _ = parts.shape
+    return vmem_call(
+        lambda *refs: share_kernel(scale, *refs),
+        jax.ShapeDtypeStruct((copies, 2 * rows - extra, LANES), BF16),
         (),
         pl.CostEstimate(flops=parts.size, bytes_accessed=6 * parts.size, transcendentals=0),
     )(parts)
 
 
-def place(source, height, which, bucket, buffer, sems):
+def place(source, height, padded, which, bucket, buffer, sems):
     copies, count = (source.shape[0], sems.shape[0])
-    size = copies * height
-    step = copies // count
+    step = 2 * copies // count
     sent = []
     for n in range(count):
-        for q in range(n * step, (n + 1) * step):
-            buffer[q * height : (q + 1) * height, :] = source[q, 0:height, :].astype(F32)
+        for m in range(n * step, (n + 1) * step):
+            half, q = (m // copies, m % copies)
+            value = source[q, half * padded : (half + 1) * padded, :].astype(F32)
+            buffer[m * height : (m + 1) * height, :] = value[0:height]
         rows = pl.ds(n * step * height, step * height)
-        at = pl.ds(pl.multiple_of(which * size + n * step * height, 8), step * height)
+        at = (which * count + n) * step * height
+        at = pl.ds(pl.multiple_of(at, 8), step * height)
         sent.append(pltpu.make_async_copy(buffer.at[rows], bucket.at[at], sems.at[n]))
         sent[-1].start()
     return sent
 
 
-def start_kernel(height, mine, bucket, buffer, sems):
-    for copy in place(mine, height, lax.axis_index("core"), bucket, buffer, sems):
+def start_kernel(height, padded, mine, bucket, buffer, sems):
+    for copy in place(mine, height, padded, lax.axis_index("core"), bucket, buffer, sems):
         copy.wait()
 
 
 def finish_kernel(
-    sizes, height, mine, other, partial,
+    sizes, height, padded, mine, other, partial,
     bucket, out_one, out_two,
     raw, one, two, out_sems, buffer, sems,
 ):
     c0, c1, c2 = sizes
     copies, rows, _ = mine.shape
-    extra = rows - height
+    extra = rows - 2 * padded
     me = lax.axis_index("core")
-    sent = place(other, height, 1 - me, bucket, buffer, sems)
-
-    column = copies // 2
-    for q in range(column):
+    sent = place(other, height, padded, 1 - me, bucket, buffer, sems)
+
+    for q in range(copies):
         for source, which in ((mine, me), (other, 1 - me)):
-            at = pl.multiple_of((which * column + q) * extra, 8)
-            near = source[q, height:rows, :].astype(F32)
-            raw[pl.ds(at, extra), :] = near + source[column + q, height:rows, :].astype(F32)
+            at = pl.multiple_of((which * copies + q) * extra, 8)
+            raw[pl.ds(at, extra), :] = source[q, 2 * padded : rows, :].astype(F32)
     block = 3 * c1
     first = -(-9 * c2 // LANES) * block
     for i in range(3):
@@ -441,18 +462,19 @@
 def finish(mine, other, length, sizes):
     c0, c1, c2 = sizes
     copies, rows, _ = mine.shape
-    height = length // LANES // (2 * copies)
+    height = length // LANES // (4 * copies)
+    padded = ceil_to(height, 16)
     spec = pl.BlockSpec(memory_space=pltpu.VMEM)
     remote = pl.BlockSpec(memory_space=pltpu.HBM)
     whole = jax.ShapeDtypeStruct((length // LANES, LANES), F32)
     chunks = 4
     scratch = [
-        pltpu.VMEM((copies * height, LANES), F32),
+        pltpu.VMEM((2 * copies * height, LANES), F32),
         pltpu.SemaphoreType.DMA((chunks,)),
     ]
     params = pltpu.CompilerParams(vmem_limit_bytes=24 * 2**20)
     partial = pl.pallas_call(
-        lambda *refs: start_kernel(height, *refs),
+        lambda *refs: start_kernel(height, padded, *refs),
         out_shape=whole,
         in_specs=[spec],
         out_specs=remote,
@@ -460,7 +482,7 @@
         compiler_params=params,
     )(mine)
     return pl.pallas_call(
-        lambda *refs: finish_kernel(sizes, height, *refs),
+        lambda *refs: finish_kernel(sizes, height, padded, *refs),
         out_shape=(
             whole,
             jax.ShapeDtypeStruct((27 * c0, c1), F32),
@@ -469,7 +491,7 @@
         in_specs=[spec, spec, remote],
         out_specs=(remote, remote, remote),
         scratch_shapes=[
-            pltpu.VMEM((copies * (rows - height), LANES), F32),
+            pltpu.VMEM((2 * copies * (rows - 2 * padded), LANES), F32),
             pltpu.VMEM((27 * c0, c1), F32),
             pltpu.VMEM((27 * c1, c2), F32),
             pltpu.SemaphoreType.DMA((6,)),
@@ -487,7 +509,7 @@
 
 def per_device(volume_in, hidden_act, out_cot, kernel_one, kernel_two, grad_bucket):
     c0, c1, c2 = (volume_in.shape[2], hidden_act.shape[2], out_cot.shape[2])
-    devices, copies, column = (lax.axis_size(EVERY), lax.axis_size(SAME), lax.axis_size(COLUMN))
+    devices, copies = (lax.axis_size(EVERY), lax.axis_size(SAME))
     length = grad_bucket.shape[1]
     bucket = grad_bucket.reshape(length // LANES, LANES)
     cot = pack(out_cot[0, 0])
@@ -499,17 +521,17 @@
     far = swapped(send, "x")
 
     used = -(-9 * c2 // LANES) * 3 * c1 + 9 * c0
-    rows = ceil_to(used, 16 * 2 * column)
-    pres, terms = first_part(cots, act, kernel_two)
-    send, keep, own, inner, outer = second_part(vols, pres, kernel_one, terms, rows)
-    parts = combine(near, far, keep, swapped(send), column)
+    rows = ceil_to(used, 16 * devices)
+    acts, w_two, w_one = prepare(act, kernel_two, kernel_one)
+    pres, terms = first_part(cots, acts, w_two)
+    send, keep, own, inner, outer = second_part(vols, pres, w_one, terms, rows)
+    parts = combine(near, far, keep, swapped(send), copies)
     parts, inner, outer = lax.optimization_barrier((parts, inner, outer))
-    parts = lax.all_to_all(parts, COLUMN, 0, 0)
+    parts = lax.all_to_all(parts, SAME, 0, 0)
     grad_input = merge(own, swapped(inner), crossed(outer), volume_in.shape[2:])
     parts, grad_input = lax.optimization_barrier((parts, grad_input))
     cells = volume_in.shape[3] * volume_in.shape[4] * devices
-    height = length // LANES // devices
-    shares = share(parts, height, 1.0 / math.sqrt(cells), copies)
+    shares = share(parts, rows // devices, 1.0 / math.sqrt(cells))
 
     mine = lax.all_to_all(shares, SAME, 0, 0)
     bucket_sum, total_one, total_two = finish(mine, swapped(mine), length, (c0, c1, c2))

time: 67.1 us -> 66.8 us (level)
  blocking collectives: 22.6 us -> 21.3 us
    all_to_all x1, blocking collectives: 22.6 us -> 21.3 us  [per_device(): mine = lax.all_to_all(shares, SAME, 0, 0)]
    pallas_call x3 -> x4, Pallas kernels: 2.55 us -> 3.44 us  [the longest x1 1.37 us: finish(): pl.pallas_call(lambda *refs: finish_kernel(sizes, height, padded, *refs),...]
    pallas_call x1, Pallas kernels: 3.58 us -> 2.7 us  [first_part(): vmem_call(first_kernel, (jax.ShapeDtypeStruct(((length + 2) * 3 * c1, wid...]
    ppermute x3, waiting for transfers between devices: 6.54 us -> 7.27 us  [crossed(): return lax.ppermute(value, SPACE, pairs + [(m, n) for n, m in pairs])]
  transfers between devices with their start and end apart: 11 -> 11, of which waited for: 5 -> 4; matrix products, arithmetic and copies ran while one was open for 0% -> 0% of each run, Pallas kernels for 12% -> 12%
where the time goes in v13:
time: 66.8 us; the launch traced here: 66.1 us
  blocking collectives  21.3 us (32%)
  starting transfers between devices  20.9 us (31%)
  Pallas kernels  11.3 us (17%)
  waiting for transfers between devices  9.14 us (14%)
  local copies, waits for them, and re-layouts  2.65 us (4%)
  between operations  0.84 us (1%)
    all_to_all x1, blocking collectives, per_device(): mine = lax.all_to_all(shares, SAME, 0, 0)  21.3 us
    ppermute x3, starting transfers between devices, crossed(): return lax.ppermute(value, SPACE, pairs + [(m, n) for n, m in pairs])  9.84 us
    ppermute x3, waiting for transfers between devices, crossed(): return lax.ppermute(value, SPACE, pairs + [(m, n) for n, m in pairs])  7.27 us
    all_to_all x1, starting transfers between devices, per_device(): parts = lax.all_to_all(parts, SAME, 0, 0)  5.98 us
    ppermute x7, starting transfers between devices, swapped(): return lax.ppermute(value, axis, [(0, 1), (1, 0)])  5.07 us
    pallas_call x1, Pallas kernels, first_part(): vmem_call(first_kernel, (jax.ShapeDtypeStruct(((length + 2) * 3 * c1, wid...  2.7 us
    unnamed x14, local copies, waits for them, and re-layouts  2.65 us
    pallas_call x1, Pallas kernels, second_part(): vmem_call(second_kernel, (jax.ShapeDtypeStruct((rows // 2, LANES), BF16),...  1.91 us
  transfers between devices with their start and end apart: 11, of which 4 were waited for; matrix products, arithmetic and copies ran while one was open for 0% of the time, Pallas kernels for 12%

profile of v13, /device:TPU:1, one launch (start us, length us, event | category | flops | bytes accessed | tf_op | source)
XLA Modules:
  0.0 66.1 jit_solution(16906704850880604740)
XLA Ops:
  0.6 0.0 copy-start.2
  0.6 1.0 %copy-done.2 = bf16[1,1,32,64,128]{4,3,2,1,0:T(8,128)(2,1)S(1)} copy-done((bf16[1,1,32,64,128]{4,3,2,1,0:T(8,128)(2,1)S(1)}, bf16[1,1,32,64,128]{4,3,2,1,0:T(8,128)(2,1)}, u32[]{:S(2)}) %copy-start.2) | copy-done | bytes 524312
  1.7 0.0 copy-start.4
  1.7 0.8 %shard_map.93.after.pack_0 = bf16[2112,128]{1,0:T(8,128)(2,1)S(1)} custom-call(bf16[32,64,128]{2,1,0:T(8,128)(2,1)S(1)} %bitcast.10), custom_call_target="tpu_custom_call" | custom-call | bytes 4194304 | tf_op jit(solution)/shard_map/pallas_call | solution.py:62
  2.5 4.5 %collective-permute-start.5 = (bf16[2112,128]{1,0:T(8,128)(2,1)S(1)}, bf16[2112,128]{1,0:T(8,128)(2,1)S(1)}, u32[]{:S(2)}, u32[]{:S(2)}) collective-permute-start(bf16[2112,128]{1,0:T(8,128)(2,1)S(1)} %shard_map.93.after.pack_0), channel_id=1, source_target_pairs={{1,2},{2,1},{5,6},{6,5},{9,10},{10,9},{13,14},{14,13},{17,18},{18,... | collective-permute-start | bytes 1622024 | tf_op jit(solution)/shard_map/ppermute | solution.py:507
  7.0 0.1 collective-permute-start.4
  7.1 0.0 copy-start
  7.1 1.6 %copy-done = f32[1,524288]{1,0:T(1,128)S(1)} copy-done((f32[1,524288]{1,0:T(1,128)S(1)}, f32[1,524288]{1,0:T(1,128)}, u32[]{:S(2)}) %copy-start) | copy-done | bytes 2097176
  8.7 0.0 copy-start.1
  8.7 0.1 shard_map.94
  8.8 0.0 copy-start.3
  8.8 0.0 copy-start.5
  8.8 0.0 copy-start.6
  8.8 0.6 collective-permute-start
  9.4 0.0 copy-done.4
  9.4 0.5 shard_map.96.pack_0
  9.9 1.9 %collective-permute-start.3 = (bf16[1056,128]{1,0:T(8,128)(2,1)S(1)}, bf16[1056,128]{1,0:T(8,128)(2,1)S(1)}, u32[]{:S(2)}, u32[]{:S(2)}) collective-permute-start(bf16[1056,128]{1,0:T(8,128)(2,1)S(1)} %shard_map.96.pack_0), channel_id=1, source_target_pairs={{1,2},{2,1},{5,6},{6,5},{9,10},{10,9},{13,14},{14,13},{17,18},{18,... | collective-permute-start | bytes 811016 | tf_op jit(solution)/shard_map/ppermute | solution.py:507
  11.8 0.1 collective-permute-start.2
  11.9 0.0 collective-permute-done.other
  11.9 0.0 copy-done.1
  11.9 0.2 shard_map.95
  12.0 1.3 %collective-permute-start.1 = (bf16[1024,128]{1,0:T(8,128)(2,1)S(1)}, bf16[1024,128]{1,0:T(8,128)(2,1)S(1)}, u32[]{:S(2)}, u32[]{:S(2)}) collective-permute-start(bf16[1024,128]{1,0:T(8,128)(2,1)S(1)} %get-tuple-element.30), channel_id=1, source_target_pairs={{0,4},{4,0},{1,5},{5,1},{2,6},{6,2},{3,7},{7,3},{8,12},{12,8},{9,1... | collective-permute-start | bytes 786440 | tf_op jit(solution)/shard_map/ppermute | solution.py:162
  13.3 0.0 copy-done.3
  13.3 0.0 copy-done.5
  13.3 0.0 copy-done.6
  13.3 0.9 %shard_map.97 = (bf16[2048,128]{1,0:T(8,128)(2,1)S(1)}, bf16[96,288]{1,0:T(8,128)(2,1)S(1)}, bf16[48,288]{1,0:T(8,128)(2,1)S(1)}) custom-call(bf16[32,64,128]{2,1,0:T(8,128)(2,1)S(1)} %bitcast.11, bf16[3,3,3,32,32]{4,3,2,1,0:T(8,128)(2,1)S(1)} %copy-done.5, bf16[3,3,3,16,32]{4,3,2,1,0:T(8,128)(2,1)S(1)} %copy-done.6), custom_call_target="tpu_custom_call" | custom-call | bytes 4194304 | tf_op jit(solution)/shard_map/pallas_call | solution.py:217
  14.3 0.0 collective-permute-done.5.pack_out
  14.3 0.0 collective-permute-done.4.pack_in
  14.3 2.7 %shard_map.98 = (bf16[6336,128]{1,0:T(8,128)(2,1)S(1)}, f32[288,128]{1,0:T(8,128)S(1)}) custom-call(bf16[2112,128]{1,0:T(8,128)(2,1)S(1)} %collective-permute-done.4.pack_in, bf16[2112,128]{1,0:T(8,128)(2,1)S(1)} %shard_map.93.after.pack_0, bf16[2112,128]{1,0:T(8,128)(2,1)S(1)} %collective-permute-done.5.pack_out, ...), custom_call_target="tpu_custom_call" | custom-call | flops 1000000000 | bytes 20971520 | tf_op jit(solution)/shard_map/pallas_call | solution.py:316
  17.0 0.9 %collective-permute-done.3.pack_out = bf16[1056,128]{1,0:T(8,128)(2,1)S(1)} collective-permute-done((bf16[1056,128]{1,0:T(8,128)(2,1)S(1)}, bf16[1056,128]{1,0:T(8,128)(2,1)S(1)}, u32[]{:S(2)}, u32[]{:S(2)}) %collective-permute-start.3) | collective-permute-done | bytes 270368 | tf_op jit(solution)/shard_map/ppermute | solution.py:507
  17.9 0.0 collective-permute-done.2.pack_in
  17.9 1.9 %shard_map.99 = (bf16[256,128]{1,0:T(8,128)(2,1)S(1)}, f32[256,128]{1,0:T(8,128)S(1)}, f32[1024,128]{1,0:T(8,128)S(1)}, bf16[1024,128]{1,0:T(8,128)(2,1)S(1)}, bf16[1024,128]{1,0:T(8,128)(2,1)S(1)}) custom-call(bf16[1056,128]{1,0:T(8,128)(2,1)S(1)} %collective-permute-done.2.pack_in, bf16[1056,128]{1,0:T(8,128)(2,1)S(1)} %shard_map.96.pack_0, ...), custom_call_target="tpu_custom_call" | custom-call | flops 1000000000 | bytes 10485760 | tf_op jit(solution)/shard_map/pallas_call | solution.py:331
  19.9 0.1 collective-permute-start.6
  19.9 1.2 %collective-permute-done.6.more = bf16[256,128]{1,0:T(8,128)(2,1)S(1)} collective-permute-done((bf16[256,128]{1,0:T(8,128)(2,1)S(1)}, bf16[256,128]{1,0:T(8,128)(2,1)S(1)}, u32[]{:S(2)}, u32[]{:S(2)}) %collective-permute-start.6) | collective-permute-done | bytes 65568 | tf_op jit(solution)/shard_map/ppermute | solution.py:162
  21.2 0.0 collective-permute-done.1.other
  21.2 0.8 %shard_map.100 = bf16[16,80,128]{2,1,0:T(8,128)(2,1)} custom-call(f32[1024,128]{1,0:T(8,128)S(1)} %get-tuple-element.29.keep, bf16[1024,128]{1,0:T(8,128)(2,1)S(1)} %collective-permute-done.1.other, f32[256,128]{1,0:T(8,128)S(1)} %get-tuple-element.37.terms, bf16[256,128]{1,0:T(8,128)(2,1)S(1)} %collective-permute-done.6.more), custom_call_target="tpu_custom_call" | custom-call | bytes 1048576 | tf_op jit(solution)/shard_map/pallas_call | solution.py:147
  22.0 6.0 %all-to-all-start = ((bf16[16,80,128]{2,1,0:T(8,128)(2,1)}), bf16[16,80,128]{2,1,0:T(8,128)(2,1)S(1)}, u32[]{:S(2)}, u32[]{:S(2)}) async-start(bf16[16,80,128]{2,1,0:T(8,128)(2,1)} %shard_map.100), calls=%async_computation | async-start | bytes 655360 | tf_op jit(solution)/shard_map/all_to_all | solution.py:530
  28.0 1.2 %collective-permute-start.7 = (bf16[1024,128]{1,0:T(8,128)(2,1)S(1)}, bf16[1024,128]{1,0:T(8,128)(2,1)S(1)}, u32[]{:S(2)}, u32[]{:S(2)}) collective-permute-start(bf16[1024,128]{1,0:T(8,128)(2,1)S(1)} %get-tuple-element.43), channel_id=1, source_target_pairs={{0,1},{1,0},{2,3},{3,2},{4,5},{5,4},{6,7},{7,6},{8,9},{9,8},{10,11... | collective-permute-start | bytes 786440 | tf_op jit(solution)/shard_map/ppermute | solution.py:162
  29.1 3.4 %collective-permute-start.8 = (bf16[1024,128]{1,0:T(8,128)(2,1)S(1)}, bf16[1024,128]{1,0:T(8,128)(2,1)S(1)}, u32[]{:S(2)}, u32[]{:S(2)}) collective-permute-start(bf16[1024,128]{1,0:T(8,128)(2,1)S(1)} %get-tuple-element.44), channel_id=1, source_target_pairs={{1,2},{2,1},{5,6},{6,5},{9,10},{10,9},{13,14},{14,13},{17,18},{18,... | collective-permute-start | bytes 786440 | tf_op jit(solution)/shard_map/ppermute | solution.py:507
  32.5 0.0 collective-permute-done.7.first
  32.5 6.3 %collective-permute-done.8.second = bf16[1024,128]{1,0:T(8,128)(2,1)S(1)} collective-permute-done((bf16[1024,128]{1,0:T(8,128)(2,1)S(1)}, bf16[1024,128]{1,0:T(8,128)(2,1)S(1)}, u32[]{:S(2)}, u32[]{:S(2)}) %collective-permute-start.8) | collective-permute-done | bytes 262176 | tf_op jit(solution)/shard_map/ppermute | solution.py:507
  38.9 1.0 %shard_map.101 = bf16[16,64,128]{2,1,0:T(8,128)(2,1)} custom-call(f32[1024,128]{1,0:T(8,128)S(1)} %get-tuple-element.42.own, bf16[1024,128]{1,0:T(8,128)(2,1)S(1)} %collective-permute-done.7.first, bf16[1024,128]{1,0:T(8,128)(2,1)S(1)} %collective-permute-done.8.second), custom_call_target="tpu_custom_call" | custom-call | flops 262144 | bytes 1048576 | tf_op jit(solution)/shard_map/pallas_call | solution.py:366
  39.8 0.0 all-to-all-done.refs_0_
  39.8 0.1 shard_map.102
  40.0 21.3 %all_to_all.10.refs_0_ = bf16[16,144,128]{2,1,0:T(8,128)(2,1)S(1)} all-to-all(bf16[16,144,128]{2,1,0:T(8,128)(2,1)S(1)} %shard_map.102), channel_id=1, replica_groups=mesh['z'=4,'x'=2,'y'=2,'core'=2] {'x','z','y'}, dimensions={0} | all-to-all | bytes 1179648 | tf_op jit(solution)/shard_map/all_to_all | solution.py:536
  61.3 1.8 %collective-permute-start.9 = (bf16[16,144,128]{2,1,0:T(8,128)(2,1)S(1)}, bf16[16,144,128]{2,1,0:T(8,128)(2,1)S(1)}, u32[]{:S(2)}, u32[]{:S(2)}) collective-permute-start(bf16[16,144,128]{2,1,0:T(8,128)(2,1)S(1)} %all_to_all.10.refs_0_), channel_id=1, source_target_pairs={{0,1},{1,0},{2,3},{3,2},{4,5},{5,4},{6,7},{7,6},{8,9},{9,8},{10,11... | collective-permute-start | bytes 1769480 | tf_op jit(solution)/shard_map/ppermute | solution.py:162
  63.1 1.0 %shard_map.103.refs_2_ = f32[4096,128]{1,0:T(8,128)} custom-call(bf16[16,144,128]{2,1,0:T(8,128)(2,1)S(1)} %all_to_all.10.refs_0_), custom_call_target="tpu_custom_call" | custom-call | tf_op jit(solution)/shard_map/pallas_call | solution.py:476
  64.1 0.6 collective-permute-done.9.refs_1_
  64.7 1.4 %shard_map.104 = (f32[4096,128]{1,0:T(8,128)}, f32[432,32]{1,0:T(8,128)}, f32[864,32]{1,0:T(8,128)}) custom-call(bf16[16,144,128]{2,1,0:T(8,128)(2,1)S(1)} %all_to_all.10.refs_0_, bf16[16,144,128]{2,1,0:T(8,128)(2,1)S(1)} %collective-permute-done.9.refs_1_, f32[4096,128]{1,0:T(8,128)} %shard_map.103.refs_2_), custom_call_target="tpu_custom_call", output_to_operand_aliasing={{0}: (2, {})} | custom-call | tf_op jit(solution)/shard_map/pallas_call | solution.py:484
Async XLA Ops:
  0.6 1.0 %copy-start.2 = (bf16[1,1,32,64,128]{4,3,2,1,0:T(8,128)(2,1)S(1)}, bf16[1,1,32,64,128]{4,3,2,1,0:T(8,128)(2,1)}, u32[]{:S(2)}) copy-start(bf16[1,1,32,64,128]{4,3,2,1,0:T(8,128)(2,1)} %param.8) | copy-start | bytes 1572868
  1.7 7.7 %copy-start.4 = (bf16[1,1,16,64,128]{4,3,2,1,0:T(8,128)(2,1)S(1)}, bf16[1,1,16,64,128]{4,3,2,1,0:T(8,128)(2,1)}, u32[]{:S(2)}) copy-start(bf16[1,1,16,64,128]{4,3,2,1,0:T(8,128)(2,1)} %param.6) | copy-start | bytes 786436
  2.5 11.8 %collective-permute-start.5 = (bf16[2112,128]{1,0:T(8,128)(2,1)S(1)}, bf16[2112,128]{1,0:T(8,128)(2,1)S(1)}, u32[]{:S(2)}, u32[]{:S(2)}) collective-permute-start(bf16[2112,128]{1,0:T(8,128)(2,1)S(1)} %shard_map.93.after.pack_0), channel_id=1, source_target_pairs={{1,2},{2,1},{5,6},{6,5},{9,10},{10,9},{13,14},{14,13},{17,18},{18,... | collective-permute-start | bytes 1622024 | tf_op jit(solution)/shard_map/ppermute | solution.py:507
  7.0 7.2 %collective-permute-start.4 = (bf16[2112,128]{1,0:T(8,128)(2,1)S(1)}, bf16[2112,128]{1,0:T(8,128)(2,1)S(1)}, u32[]{:S(2)}, u32[]{:S(2)}) collective-permute-start(bf16[2112,128]{1,0:T(8,128)(2,1)S(1)} %shard_map.93.after.pack_0), channel_id=1, source_target_pairs={{0,1},{1,0},{2,3},{3,2},{4,5},{5,4},{6,7},{7,6},{8,9},{9,8},{10,11... | collective-permute-start | bytes 1622024 | tf_op jit(solution)/shard_map/ppermute | solution.py:162
  7.1 1.6 %copy-start = (f32[1,524288]{1,0:T(1,128)S(1)}, f32[1,524288]{1,0:T(1,128)}, u32[]{:S(2)}) copy-start(f32[1,524288]{1,0:T(1,128)} %param.11) | copy-start | bytes 6291460
  8.7 3.2 %copy-start.1 = (f32[1,524288]{1,0:T(1,128)S(1)}, f32[1,524288]{1,0:T(1,128)}, u32[]{:S(2)}) copy-start(f32[1,524288]{1,0:T(1,128)} %param.11) | copy-start | bytes 6291460
  8.8 4.5 %copy-start.3 = (bf16[1,1,32,64,128]{4,3,2,1,0:T(8,128)(2,1)S(1)}, bf16[1,1,32,64,128]{4,3,2,1,0:T(8,128)(2,1)}, u32[]{:S(2)}) copy-start(bf16[1,1,32,64,128]{4,3,2,1,0:T(8,128)(2,1)} %param.7) | copy-start | bytes 1572868
  8.8 4.5 %copy-start.5 = (bf16[3,3,3,32,32]{4,3,2,1,0:T(8,128)(2,1)S(1)}, bf16[3,3,3,32,32]{4,3,2,1,0:T(8,128)(2,1)}, u32[]{:S(2)}) copy-start(bf16[3,3,3,32,32]{4,3,2,1,0:T(8,128)(2,1)} %two.1) | copy-start | bytes 165892
  8.8 4.5 %copy-start.6 = (bf16[3,3,3,16,32]{4,3,2,1,0:T(8,128)(2,1)S(1)}, bf16[3,3,3,16,32]{4,3,2,1,0:T(8,128)(2,1)}, u32[]{:S(2)}) copy-start(bf16[3,3,3,16,32]{4,3,2,1,0:T(8,128)(2,1)} %one.1) | copy-start | bytes 82948
  8.8 3.0 %collective-permute-start = (bf16[2048,128]{1,0:T(8,128)(2,1)S(1)}, bf16[2048,128]{1,0:T(8,128)(2,1)S(1)}, u32[]{:S(2)}, u32[]{:S(2)}) collective-permute-start(bf16[2048,128]{1,0:T(8,128)(2,1)S(1)} %shard_map.94), channel_id=1, source_target_pairs={{0,1},{1,0},{2,3},{3,2},{4,5},{5,4},{6,7},{7,6},{8,9},{9,8},{10,11... | collective-permute-start | bytes 1572872 | tf_op jit(solution)/shard_map/ppermute | solution.py:162
  9.9 8.1 %collective-permute-start.3 = (bf16[1056,128]{1,0:T(8,128)(2,1)S(1)}, bf16[1056,128]{1,0:T(8,128)(2,1)S(1)}, u32[]{:S(2)}, u32[]{:S(2)}) collective-permute-start(bf16[1056,128]{1,0:T(8,128)(2,1)S(1)} %shard_map.96.pack_0), channel_id=1, source_target_pairs={{1,2},{2,1},{5,6},{6,5},{9,10},{10,9},{13,14},{14,13},{17,18},{18,... | collective-permute-start | bytes 811016 | tf_op jit(solution)/shard_map/ppermute | solution.py:507
  11.8 6.1 %collective-permute-start.2 = (bf16[1056,128]{1,0:T(8,128)(2,1)S(1)}, bf16[1056,128]{1,0:T(8,128)(2,1)S(1)}, u32[]{:S(2)}, u32[]{:S(2)}) collective-permute-start(bf16[1056,128]{1,0:T(8,128)(2,1)S(1)} %shard_map.96.pack_0), channel_id=1, source_target_pairs={{0,1},{1,0},{2,3},{3,2},{4,5},{5,4},{6,7},{7,6},{8,9},{9,8},{10,11... | collective-permute-start | bytes 811016 | tf_op jit(solution)/shard_map/ppermute | solution.py:162
  12.0 9.1 %collective-permute-start.1 = (bf16[1024,128]{1,0:T(8,128)(2,1)S(1)}, bf16[1024,128]{1,0:T(8,128)(2,1)S(1)}, u32[]{:S(2)}, u32[]{:S(2)}) collective-permute-start(bf16[1024,128]{1,0:T(8,128)(2,1)S(1)} %get-tuple-element.30), channel_id=1, source_target_pairs={{0,4},{4,0},{1,5},{5,1},{2,6},{6,2},{3,7},{7,3},{8,12},{12,8},{9,1... | collective-permute-start | bytes 786440 | tf_op jit(solution)/shard_map/ppermute | solution.py:162
  19.9 1.3 %collective-permute-start.6 = (bf16[256,128]{1,0:T(8,128)(2,1)S(1)}, bf16[256,128]{1,0:T(8,128)(2,1)S(1)}, u32[]{:S(2)}, u32[]{:S(2)}) collective-permute-start(bf16[256,128]{1,0:T(8,128)(2,1)S(1)} %get-tuple-element.38), channel_id=1, source_target_pairs={{0,1},{1,0},{2,3},{3,2},{4,5},{5,4},{6,7},{7,6},{8,9},{9,8},{10,11... | collective-permute-start | bytes 196616 | tf_op jit(solution)/shard_map/ppermute | solution.py:162
  22.0 17.9 %all-to-all-start = ((bf16[16,80,128]{2,1,0:T(8,128)(2,1)}), bf16[16,80,128]{2,1,0:T(8,128)(2,1)S(1)}, u32[]{:S(2)}, u32[]{:S(2)}) async-start(bf16[16,80,128]{2,1,0:T(8,128)(2,1)} %shard_map.100), calls=%async_computation | async-start | bytes 655360 | tf_op jit(solution)/shard_map/all_to_all | solution.py:530
  28.0 4.6 %collective-permute-start.7 = (bf16[1024,128]{1,0:T(8,128)(2,1)S(1)}, bf16[1024,128]{1,0:T(8,128)(2,1)S(1)}, u32[]{:S(2)}, u32[]{:S(2)}) collective-permute-start(bf16[1024,128]{1,0:T(8,128)(2,1)S(1)} %get-tuple-element.43), channel_id=1, source_target_pairs={{0,1},{1,0},{2,3},{3,2},{4,5},{5,4},{6,7},{7,6},{8,9},{9,8},{10,11... | collective-permute-start | bytes 786440 | tf_op jit(solution)/shard_map/ppermute | solution.py:162
  29.1 9.7 %collective-permute-start.8 = (bf16[1024,128]{1,0:T(8,128)(2,1)S(1)}, bf16[1024,128]{1,0:T(8,128)(2,1)S(1)}, u32[]{:S(2)}, u32[]{:S(2)}) collective-permute-start(bf16[1024,128]{1,0:T(8,128)(2,1)S(1)} %get-tuple-element.44), channel_id=1, source_target_pairs={{1,2},{2,1},{5,6},{6,5},{9,10},{10,9},{13,14},{14,13},{17,18},{18,... | collective-permute-start | bytes 786440 | tf_op jit(solution)/shard_map/ppermute | solution.py:507
  61.3 3.5 %collective-permute-start.9 = (bf16[16,144,128]{2,1,0:T(8,128)(2,1)S(1)}, bf16[16,144,128]{2,1,0:T(8,128)(2,1)S(1)}, u32[]{:S(2)}, u32[]{:S(2)}) collective-permute-start(bf16[16,144,128]{2,1,0:T(8,128)(2,1)S(1)} %all_to_all.10.refs_0_), channel_id=1, source_target_pairs={{0,1},{1,0},{2,3},{3,2},{4,5},{5,4},{6,7},{7,6},{8,9},{9,8},{10,11... | collective-permute-start | bytes 1769480 | tf_op jit(solution)/shard_map/ppermute | solution.py:162

commit v14 on v13

--- a/solution.py
+++ b/solution.py
@@ -253,7 +253,7 @@
         acc[...] += across_lanes(right, jnp.concatenate(columns, axis=1))
         return carry
 
-    lax.fori_loop(0, length // GROUP, body, 0, unroll=4)
+    lax.fori_loop(0, length // GROUP, body, 0, unroll=True)
 
     terms[...] = jnp.zeros_like(terms)
     total = ordered(acc, c2, ahead).T
@@ -263,17 +263,34 @@
         terms[block * rows : (block + 1) * rows, 0 : part.shape[1]] = part
 
 
-def second_kernel(
-    pack_in, pack_0, pack_out, pres, w_one, before,
-    send, keep, own, inner, outer,
-    acc, terms,
-):
-    c0, c1 = (w_one.shape[0] // 3, w_one.shape[1] // 9)
+def gradient_kernel(pack_in, pack_0, pack_out, pres, before, send, keep, acc, terms):
+    c0, stacked = (acc.shape[0] // 9, acc.shape[1])
     packs = (pack_in, pack_0, pack_out)
     ahead, _ = plane_order()
-    stacked = 3 * c1
     length = pres.shape[0] // stacked - 2
     acc[...] = jnp.zeros_like(acc)
+
+    def body(step, carry):
+        x = step * GROUP
+        rows = [
+            pres[pl.ds(pl.multiple_of((x + g + 1) * stacked, 16), stacked), :] for g in range(GROUP)
+        ]
+        acc[...] += across_lanes(windows(packs, x, c0), jnp.concatenate(rows, axis=1))
+        return carry
+
+    lax.fori_loop(0, length // GROUP, body, 0, unroll=True)
+
+    used = before.shape[0]
+    terms[0:used, :] = before[...]
+    terms[used:, :] = jnp.zeros((terms.shape[0] - used, LANES), F32)
+    total = ordered(acc, c0, ahead)
+    terms[used : used + total.shape[0], 0 : total.shape[1]] = total
+    split_to(terms, lax.axis_index("core"), send, keep)
+
+
+def input_kernel(pres, w_one, own, inner, outer):
+    c0, stacked = (w_one.shape[0] // 3, w_one.shape[1] // 3)
+    length = pres.shape[0] // stacked - 2
 
     def body(step, carry):
         x = step * GROUP
@@ -285,17 +302,9 @@
             at = pl.ds(pl.multiple_of((x + g) * c0, 16), c0)
             for i, out in ((0, inner), (1, own), (2, outer)):
                 out[at, :] = part[i * c0 : (i + 1) * c0].astype(out.dtype)
-        acc[...] += across_lanes(windows(packs, x, c0), moved[stacked : 2 * stacked])
-        return carry
-
-    lax.fori_loop(0, length // GROUP, body, 0, unroll=4)
-
-    used = before.shape[0]
-    terms[0:used, :] = before[...]
-    terms[used:, :] = jnp.zeros((terms.shape[0] - used, LANES), F32)
-    total = ordered(acc, c0, ahead)
-    terms[used : used + total.shape[0], 0 : total.shape[1]] = total
-    split_to(terms, lax.axis_index("core"), send, keep)
+        return carry
+
+    lax.fori_loop(0, length // GROUP, body, 0, unroll=True)
 
 
 def vmem_call(body, out_shape, scratch=(), cost=None, limit=24 * 2**20):
@@ -324,25 +333,33 @@
     )(*packs, acts, w_two)
 
 
-def second_part(packs, pres, w_one, terms, rows):
-    c0, c1 = (w_one.shape[0] // 3, w_one.shape[1] // 9)
-    length, width = (pres.shape[0] // (3 * c1) - 2, pres.shape[1])
-    plane = (length * c0, width)
-    return vmem_call(
-        second_kernel,
+def gradient_part(packs, pres, terms, rows, c1):
+    width = pres.shape[1]
+    c0 = packs[0].shape[0] // (pres.shape[0] // (3 * c1))
+    return vmem_call(
+        gradient_kernel,
         (
             jax.ShapeDtypeStruct((rows // 2, LANES), BF16),
             jax.ShapeDtypeStruct((rows // 2, LANES), F32),
+        ),
+        (pltpu.VMEM((9 * c0, 3 * c1), F32), pltpu.VMEM((rows, width), F32)),
+        pl.CostEstimate(flops=10**9, bytes_accessed=5 * 2**20, transcendentals=0),
+    )(*packs, pres, terms)
+
+
+def input_part(pres, w_one):
+    c0, stacked = (w_one.shape[0] // 3, w_one.shape[1] // 3)
+    plane = ((pres.shape[0] // stacked - 2) * c0, pres.shape[1])
+    return vmem_call(
+        input_kernel,
+        (
             jax.ShapeDtypeStruct(plane, F32),
             jax.ShapeDtypeStruct(plane, BF16),
             jax.ShapeDtypeStruct(plane, BF16),
         ),
-        (
-            pltpu.VMEM((9 * c0, 3 * c1), F32),
-            pltpu.VMEM((rows, LANES), F32),
-        ),
-        pl.CostEstimate(flops=10**9, bytes_accessed=10 * 2**20, transcendentals=0),
-    )(*packs, pres, w_one, terms)
+        (),
+        pl.CostEstimate(flops=10**9, bytes_accessed=5 * 2**20, transcendentals=0),
+    )(pres, w_one)
 
 
 def merge_kernel(own, first, second, out, flat):
@@ -524,16 +541,18 @@
     rows = ceil_to(used, 16 * devices)
     acts, w_two, w_one = prepare(act, kernel_two, kernel_one)
     pres, terms = first_part(cots, acts, w_two)
-    send, keep, own, inner, outer = second_part(vols, pres, w_one, terms, rows)
+    send, keep = gradient_part(vols, pres, terms, rows, c1)
+    own, inner, outer = input_part(pres, w_one)
     parts = combine(near, far, keep, swapped(send), copies)
     parts, inner, outer = lax.optimization_barrier((parts, inner, outer))
     parts = lax.all_to_all(parts, SAME, 0, 0)
-    grad_input = merge(own, swapped(inner), crossed(outer), volume_in.shape[2:])
-    parts, grad_input = lax.optimization_barrier((parts, grad_input))
+    parts, inner, outer = lax.optimization_barrier((parts, swapped(inner), crossed(outer)))
     cells = volume_in.shape[3] * volume_in.shape[4] * devices
     shares = share(parts, rows // devices, 1.0 / math.sqrt(cells))
 
     mine = lax.all_to_all(shares, SAME, 0, 0)
+    mine, own = lax.optimization_barrier((mine, own))
+    grad_input = merge(own, inner, outer, volume_in.shape[2:])
     bucket_sum, total_one, total_two = finish(mine, swapped(mine), length, (c0, c1, c2))
     return (
         grad_input[None, None],

time: 66.8 us -> 65.9 us (0.987)
  waiting for transfers between devices: 9.14 us -> 7.61 us
  starting transfers between devices: 20.9 us -> 22 us
    ppermute x7, waiting for transfers between devices: 1.86 us -> 0.2 us  [swapped(): return lax.ppermute(value, axis, [(0, 1), (1, 0)])]
    all_to_all x1, starting transfers between devices: 5.98 us -> 7.09 us  [per_device(): parts = lax.all_to_all(parts, SAME, 0, 0)]
    pallas_call x1 -> x2, Pallas kernels: 1.91 us -> 1.87 us  [the longest x1 1.05 us: input_part(): vmem_call(input_kernel, (jax.ShapeDtypeStruct(plane, F32), jax.ShapeDtype...]
  transfers between devices with their start and end apart: 11 -> 11, of which waited for: 4 -> 3; matrix products, arithmetic and copies ran while one was open for 0% -> 0% of each run, Pallas kernels for 12% -> 12%
where the time goes in v14:
time: 65.9 us; the launch traced here: 65.5 us
  starting transfers between devices  22 us (33%)
  blocking collectives  21.3 us (32%)
  Pallas kernels  11.1 us (17%)
  waiting for transfers between devices  7.61 us (12%)
  local copies, waits for them, and re-layouts  2.65 us (4%)
  between operations  0.84 us (1%)
    all_to_all x1, blocking collectives, per_device(): mine = lax.all_to_all(shares, SAME, 0, 0)  21.3 us
    ppermute x3, starting transfers between devices, crossed(): return lax.ppermute(value, SPACE, pairs + [(m, n) for n, m in pairs])  9.84 us
    ppermute x3, waiting for transfers between devices, crossed(): return lax.ppermute(value, SPACE, pairs + [(m, n) for n, m in pairs])  7.41 us
    all_to_all x1, starting transfers between devices, per_device(): parts = lax.all_to_all(parts, SAME, 0, 0)  7.09 us
    ppermute x7, starting transfers between devices, swapped(): return lax.ppermute(value, axis, [(0, 1), (1, 0)])  5.07 us
    unnamed x14, local copies, waits for them, and re-layouts  2.65 us
    pallas_call x1, Pallas kernels, first_part(): vmem_call(first_kernel, (jax.ShapeDtypeStruct(((length + 2) * 3 * c1, wid...  2.57 us
    pallas_call x1, Pallas kernels, finish(): pl.pallas_call(lambda *refs: finish_kernel(sizes, height, padded, *refs),...  1.38 us
  transfers between devices with their start and end apart: 11, of which 3 were waited for; matrix products, arithmetic and copies ran while one was open for 0% of the time, Pallas kernels for 12%

profile of v14, /device:TPU:1, one launch (start us, length us, event | category | flops | bytes accessed | tf_op | source)
XLA Modules:
  0.0 65.5 jit_solution(13979208917219763888)
XLA Ops:
  0.6 0.0 copy-start.2
  0.6 1.0 %copy-done.2 = bf16[1,1,32,64,128]{4,3,2,1,0:T(8,128)(2,1)S(1)} copy-done((bf16[1,1,32,64,128]{4,3,2,1,0:T(8,128)(2,1)S(1)}, bf16[1,1,32,64,128]{4,3,2,1,0:T(8,128)(2,1)}, u32[]{:S(2)}) %copy-start.2) | copy-done | bytes 524312
  1.7 0.0 copy-start.4
  1.7 0.8 %shard_map.93.after.pack_0 = bf16[2112,128]{1,0:T(8,128)(2,1)S(1)} custom-call(bf16[32,64,128]{2,1,0:T(8,128)(2,1)S(1)} %bitcast.10), custom_call_target="tpu_custom_call" | custom-call | bytes 4194304 | tf_op jit(solution)/shard_map/pallas_call | solution.py:62
  2.5 4.5 %collective-permute-start.5 = (bf16[2112,128]{1,0:T(8,128)(2,1)S(1)}, bf16[2112,128]{1,0:T(8,128)(2,1)S(1)}, u32[]{:S(2)}, u32[]{:S(2)}) collective-permute-start(bf16[2112,128]{1,0:T(8,128)(2,1)S(1)} %shard_map.93.after.pack_0), channel_id=1, source_target_pairs={{1,2},{2,1},{5,6},{6,5},{9,10},{10,9},{13,14},{14,13},{17,18},{18,... | collective-permute-start | bytes 1622024 | tf_op jit(solution)/shard_map/ppermute | solution.py:524
  7.0 0.1 collective-permute-start.4
  7.1 0.0 copy-start
  7.1 1.6 %copy-done = f32[1,524288]{1,0:T(1,128)S(1)} copy-done((f32[1,524288]{1,0:T(1,128)S(1)}, f32[1,524288]{1,0:T(1,128)}, u32[]{:S(2)}) %copy-start) | copy-done | bytes 2097176
  8.7 0.0 copy-start.1
  8.7 0.1 shard_map.94
  8.8 0.0 copy-start.3
  8.8 0.0 copy-start.5
  8.8 0.0 copy-start.6
  8.8 0.6 collective-permute-start
  9.4 0.0 copy-done.4
  9.4 0.5 shard_map.96.pack_0
  9.9 1.9 %collective-permute-start.3 = (bf16[1056,128]{1,0:T(8,128)(2,1)S(1)}, bf16[1056,128]{1,0:T(8,128)(2,1)S(1)}, u32[]{:S(2)}, u32[]{:S(2)}) collective-permute-start(bf16[1056,128]{1,0:T(8,128)(2,1)S(1)} %shard_map.96.pack_0), channel_id=1, source_target_pairs={{1,2},{2,1},{5,6},{6,5},{9,10},{10,9},{13,14},{14,13},{17,18},{18,... | collective-permute-start | bytes 811016 | tf_op jit(solution)/shard_map/ppermute | solution.py:524
  11.8 0.1 collective-permute-start.2
  11.9 0.0 collective-permute-done.other
  11.9 0.0 copy-done.1
  11.9 0.2 shard_map.95
  12.0 1.3 %collective-permute-start.1 = (bf16[1024,128]{1,0:T(8,128)(2,1)S(1)}, bf16[1024,128]{1,0:T(8,128)(2,1)S(1)}, u32[]{:S(2)}, u32[]{:S(2)}) collective-permute-start(bf16[1024,128]{1,0:T(8,128)(2,1)S(1)} %get-tuple-element.33), channel_id=1, source_target_pairs={{0,4},{4,0},{1,5},{5,1},{2,6},{6,2},{3,7},{7,3},{8,12},{12,8},{9,1... | collective-permute-start | bytes 786440 | tf_op jit(solution)/shard_map/ppermute | solution.py:162
  13.3 0.0 copy-done.3
  13.3 0.0 copy-done.5
  13.3 0.0 copy-done.6
  13.3 0.9 %shard_map.97 = (bf16[2048,128]{1,0:T(8,128)(2,1)S(1)}, bf16[96,288]{1,0:T(8,128)(2,1)S(1)}, bf16[48,288]{1,0:T(8,128)(2,1)S(1)}) custom-call(bf16[32,64,128]{2,1,0:T(8,128)(2,1)S(1)} %bitcast.11, bf16[3,3,3,32,32]{4,3,2,1,0:T(8,128)(2,1)S(1)} %copy-done.5, bf16[3,3,3,16,32]{4,3,2,1,0:T(8,128)(2,1)S(1)} %copy-done.6), custom_call_target="tpu_custom_call" | custom-call | bytes 4194304 | tf_op jit(solution)/shard_map/pallas_call | solution.py:217
  14.3 0.0 collective-permute-done.5.pack_out
  14.3 0.0 collective-permute-done.4.pack_in
  14.3 2.6 %shard_map.98 = (bf16[6336,128]{1,0:T(8,128)(2,1)S(1)}, f32[288,128]{1,0:T(8,128)S(1)}) custom-call(bf16[2112,128]{1,0:T(8,128)(2,1)S(1)} %collective-permute-done.4.pack_in, bf16[2112,128]{1,0:T(8,128)(2,1)S(1)} %shard_map.93.after.pack_0, bf16[2112,128]{1,0:T(8,128)(2,1)S(1)} %collective-permute-done.5.pack_out, ...), custom_call_target="tpu_custom_call" | custom-call | flops 1000000000 | bytes 20971520 | tf_op jit(solution)/shard_map/pallas_call | solution.py:325
  16.8 1.1 %collective-permute-done.3.pack_out = bf16[1056,128]{1,0:T(8,128)(2,1)S(1)} collective-permute-done((bf16[1056,128]{1,0:T(8,128)(2,1)S(1)}, bf16[1056,128]{1,0:T(8,128)(2,1)S(1)}, u32[]{:S(2)}, u32[]{:S(2)}) %collective-permute-start.3) | collective-permute-done | bytes 270368 | tf_op jit(solution)/shard_map/ppermute | solution.py:524
  17.9 0.0 collective-permute-done.2.pack_in
  17.9 0.8 %shard_map.99 = (bf16[256,128]{1,0:T(8,128)(2,1)S(1)}, f32[256,128]{1,0:T(8,128)S(1)}) custom-call(bf16[1056,128]{1,0:T(8,128)(2,1)S(1)} %collective-permute-done.2.pack_in, bf16[1056,128]{1,0:T(8,128)(2,1)S(1)} %shard_map.96.pack_0, bf16[1056,128]{1,0:T(8,128)(2,1)S(1)} %collective-permute-done.3.pack_out, bf16[6336,128]{1,0:T(8,128)(2,1)S(1)} %get-tuple-element.37.pres, ...), custom_call_target="tpu_custom_call" | custom-call | flops 1000000000 | bytes 5242880 | tf_op jit(solution)/shard_map/pallas_call | solution.py:339
  18.7 0.1 collective-permute-start.6
  18.8 1.1 %shard_map.101 = (f32[1024,128]{1,0:T(8,128)S(1)}, bf16[1024,128]{1,0:T(8,128)(2,1)S(1)}, bf16[1024,128]{1,0:T(8,128)(2,1)S(1)}) custom-call(bf16[6336,128]{1,0:T(8,128)(2,1)S(1)} %get-tuple-element.37.pres, bf16[48,288]{1,0:T(8,128)(2,1)S(1)} %get-tuple-element.41.w_one), custom_call_target="tpu_custom_call" | custom-call | flops 1000000000 | bytes 5242880 | tf_op jit(solution)/shard_map/pallas_call | solution.py:353
  19.9 0.2 collective-permute-done.6.more
  20.1 0.0 collective-permute-done.1.other
  20.1 0.8 %shard_map.100 = bf16[16,80,128]{2,1,0:T(8,128)(2,1)} custom-call(f32[1024,128]{1,0:T(8,128)S(1)} %get-tuple-element.32.keep, bf16[1024,128]{1,0:T(8,128)(2,1)S(1)} %collective-permute-done.1.other, f32[256,128]{1,0:T(8,128)S(1)} %get-tuple-element.39.terms, bf16[256,128]{1,0:T(8,128)(2,1)S(1)} %collective-permute-done.6.more), custom_call_target="tpu_custom_call" | custom-call | bytes 1048576 | tf_op jit(solution)/shard_map/pallas_call | solution.py:147
  20.9 7.1 %all-to-all-start = ((bf16[16,80,128]{2,1,0:T(8,128)(2,1)}), bf16[16,80,128]{2,1,0:T(8,128)(2,1)S(1)}, u32[]{:S(2)}, u32[]{:S(2)}) async-start(bf16[16,80,128]{2,1,0:T(8,128)(2,1)} %shard_map.100), calls=%async_computation | async-start | bytes 655360 | tf_op jit(solution)/shard_map/all_to_all | solution.py:548
  28.0 1.2 %collective-permute-start.7 = (bf16[1024,128]{1,0:T(8,128)(2,1)S(1)}, bf16[1024,128]{1,0:T(8,128)(2,1)S(1)}, u32[]{:S(2)}, u32[]{:S(2)}) collective-permute-start(bf16[1024,128]{1,0:T(8,128)(2,1)S(1)} %get-tuple-element.45), channel_id=1, source_target_pairs={{0,1},{1,0},{2,3},{3,2},{4,5},{5,4},{6,7},{7,6},{8,9},{9,8},{10,11... | collective-permute-start | bytes 786440 | tf_op jit(solution)/shard_map/ppermute | solution.py:162
  29.1 3.4 %collective-permute-start.8 = (bf16[1024,128]{1,0:T(8,128)(2,1)S(1)}, bf16[1024,128]{1,0:T(8,128)(2,1)S(1)}, u32[]{:S(2)}, u32[]{:S(2)}) collective-permute-start(bf16[1024,128]{1,0:T(8,128)(2,1)S(1)} %get-tuple-element.46), channel_id=1, source_target_pairs={{1,2},{2,1},{5,6},{6,5},{9,10},{10,9},{13,14},{14,13},{17,18},{18,... | collective-permute-start | bytes 786440 | tf_op jit(solution)/shard_map/ppermute | solution.py:524
  32.5 0.0 collective-permute-done.7.first
  32.5 6.3 %collective-permute-done.8.second = bf16[1024,128]{1,0:T(8,128)(2,1)S(1)} collective-permute-done((bf16[1024,128]{1,0:T(8,128)(2,1)S(1)}, bf16[1024,128]{1,0:T(8,128)(2,1)S(1)}, u32[]{:S(2)}, u32[]{:S(2)}) %collective-permute-start.8) | collective-permute-done | bytes 262176 | tf_op jit(solution)/shard_map/ppermute | solution.py:524
  38.9 0.0 all-to-all-done.refs_0_
  38.9 0.1 shard_map.102
  39.0 21.3 %all_to_all.10.refs_0_ = bf16[16,144,128]{2,1,0:T(8,128)(2,1)S(1)} all-to-all(bf16[16,144,128]{2,1,0:T(8,128)(2,1)S(1)} %shard_map.102), channel_id=1, replica_groups=mesh['z'=4,'x'=2,'y'=2,'core'=2] {'x','z','y'}, dimensions={0} | all-to-all | bytes 1179648 | tf_op jit(solution)/shard_map/all_to_all | solution.py:553
  60.3 1.8 %collective-permute-start.9 = (bf16[16,144,128]{2,1,0:T(8,128)(2,1)S(1)}, bf16[16,144,128]{2,1,0:T(8,128)(2,1)S(1)}, u32[]{:S(2)}, u32[]{:S(2)}) collective-permute-start(bf16[16,144,128]{2,1,0:T(8,128)(2,1)S(1)} %all_to_all.10.refs_0_), channel_id=1, source_target_pairs={{0,1},{1,0},{2,3},{3,2},{4,5},{5,4},{6,7},{7,6},{8,9},{9,8},{10,11... | collective-permute-start | bytes 1769480 | tf_op jit(solution)/shard_map/ppermute | solution.py:162
  62.1 1.0 %shard_map.103 = bf16[16,64,128]{2,1,0:T(8,128)(2,1)} custom-call(f32[1024,128]{1,0:T(8,128)S(1)} %get-tuple-element.49.own, bf16[1024,128]{1,0:T(8,128)(2,1)S(1)} %collective-permute-done.7.first, bf16[1024,128]{1,0:T(8,128)(2,1)S(1)} %collective-permute-done.8.second), custom_call_target="tpu_custom_call" | custom-call | flops 262144 | bytes 1048576 | tf_op jit(solution)/shard_map/pallas_call | solution.py:383
  63.1 1.0 %shard_map.104.refs_2_ = f32[4096,128]{1,0:T(8,128)} custom-call(bf16[16,144,128]{2,1,0:T(8,128)(2,1)S(1)} %all_to_all.10.refs_0_), custom_call_target="tpu_custom_call" | custom-call | tf_op jit(solution)/shard_map/pallas_call | solution.py:493
  64.1 0.0 collective-permute-done.9.refs_1_
  64.1 1.4 %shard_map.105 = (f32[4096,128]{1,0:T(8,128)}, f32[432,32]{1,0:T(8,128)}, f32[864,32]{1,0:T(8,128)}) custom-call(bf16[16,144,128]{2,1,0:T(8,128)(2,1)S(1)} %all_to_all.10.refs_0_, bf16[16,144,128]{2,1,0:T(8,128)(2,1)S(1)} %collective-permute-done.9.refs_1_, f32[4096,128]{1,0:T(8,128)} %shard_map.104.refs_2_), custom_call_target="tpu_custom_call", output_to_operand_aliasing={{0}: (2, {})} | custom-call | tf_op jit(solution)/shard_map/pallas_call | solution.py:501
Async XLA Ops:
  0.6 1.0 %copy-start.2 = (bf16[1,1,32,64,128]{4,3,2,1,0:T(8,128)(2,1)S(1)}, bf16[1,1,32,64,128]{4,3,2,1,0:T(8,128)(2,1)}, u32[]{:S(2)}) copy-start(bf16[1,1,32,64,128]{4,3,2,1,0:T(8,128)(2,1)} %param.8) | copy-start | bytes 1572868
  1.7 7.7 %copy-start.4 = (bf16[1,1,16,64,128]{4,3,2,1,0:T(8,128)(2,1)S(1)}, bf16[1,1,16,64,128]{4,3,2,1,0:T(8,128)(2,1)}, u32[]{:S(2)}) copy-start(bf16[1,1,16,64,128]{4,3,2,1,0:T(8,128)(2,1)} %param.6) | copy-start | bytes 786436
  2.5 11.8 %collective-permute-start.5 = (bf16[2112,128]{1,0:T(8,128)(2,1)S(1)}, bf16[2112,128]{1,0:T(8,128)(2,1)S(1)}, u32[]{:S(2)}, u32[]{:S(2)}) collective-permute-start(bf16[2112,128]{1,0:T(8,128)(2,1)S(1)} %shard_map.93.after.pack_0), channel_id=1, source_target_pairs={{1,2},{2,1},{5,6},{6,5},{9,10},{10,9},{13,14},{14,13},{17,18},{18,... | collective-permute-start | bytes 1622024 | tf_op jit(solution)/shard_map/ppermute | solution.py:524
  7.0 7.2 %collective-permute-start.4 = (bf16[2112,128]{1,0:T(8,128)(2,1)S(1)}, bf16[2112,128]{1,0:T(8,128)(2,1)S(1)}, u32[]{:S(2)}, u32[]{:S(2)}) collective-permute-start(bf16[2112,128]{1,0:T(8,128)(2,1)S(1)} %shard_map.93.after.pack_0), channel_id=1, source_target_pairs={{0,1},{1,0},{2,3},{3,2},{4,5},{5,4},{6,7},{7,6},{8,9},{9,8},{10,11... | collective-permute-start | bytes 1622024 | tf_op jit(solution)/shard_map/ppermute | solution.py:162
  7.1 1.6 %copy-start = (f32[1,524288]{1,0:T(1,128)S(1)}, f32[1,524288]{1,0:T(1,128)}, u32[]{:S(2)}) copy-start(f32[1,524288]{1,0:T(1,128)} %param.11) | copy-start | bytes 6291460
  8.7 3.2 %copy-start.1 = (f32[1,524288]{1,0:T(1,128)S(1)}, f32[1,524288]{1,0:T(1,128)}, u32[]{:S(2)}) copy-start(f32[1,524288]{1,0:T(1,128)} %param.11) | copy-start | bytes 6291460
  8.8 4.5 %copy-start.3 = (bf16[1,1,32,64,128]{4,3,2,1,0:T(8,128)(2,1)S(1)}, bf16[1,1,32,64,128]{4,3,2,1,0:T(8,128)(2,1)}, u32[]{:S(2)}) copy-start(bf16[1,1,32,64,128]{4,3,2,1,0:T(8,128)(2,1)} %param.7) | copy-start | bytes 1572868
  8.8 4.5 %copy-start.5 = (bf16[3,3,3,32,32]{4,3,2,1,0:T(8,128)(2,1)S(1)}, bf16[3,3,3,32,32]{4,3,2,1,0:T(8,128)(2,1)}, u32[]{:S(2)}) copy-start(bf16[3,3,3,32,32]{4,3,2,1,0:T(8,128)(2,1)} %two.1) | copy-start | bytes 165892
  8.8 4.5 %copy-start.6 = (bf16[3,3,3,16,32]{4,3,2,1,0:T(8,128)(2,1)S(1)}, bf16[3,3,3,16,32]{4,3,2,1,0:T(8,128)(2,1)}, u32[]{:S(2)}) copy-start(bf16[3,3,3,16,32]{4,3,2,1,0:T(8,128)(2,1)} %one.1) | copy-start | bytes 82948
  8.8 3.0 %collective-permute-start = (bf16[2048,128]{1,0:T(8,128)(2,1)S(1)}, bf16[2048,128]{1,0:T(8,128)(2,1)S(1)}, u32[]{:S(2)}, u32[]{:S(2)}) collective-permute-start(bf16[2048,128]{1,0:T(8,128)(2,1)S(1)} %shard_map.94), channel_id=1, source_target_pairs={{0,1},{1,0},{2,3},{3,2},{4,5},{5,4},{6,7},{7,6},{8,9},{9,8},{10,11... | collective-permute-start | bytes 1572872 | tf_op jit(solution)/shard_map/ppermute | solution.py:162
  9.9 8.1 %collective-permute-start.3 = (bf16[1056,128]{1,0:T(8,128)(2,1)S(1)}, bf16[1056,128]{1,0:T(8,128)(2,1)S(1)}, u32[]{:S(2)}, u32[]{:S(2)}) collective-permute-start(bf16[1056,128]{1,0:T(8,128)(2,1)S(1)} %shard_map.96.pack_0), channel_id=1, source_target_pairs={{1,2},{2,1},{5,6},{6,5},{9,10},{10,9},{13,14},{14,13},{17,18},{18,... | collective-permute-start | bytes 811016 | tf_op jit(solution)/shard_map/ppermute | solution.py:524
  11.8 6.1 %collective-permute-start.2 = (bf16[1056,128]{1,0:T(8,128)(2,1)S(1)}, bf16[1056,128]{1,0:T(8,128)(2,1)S(1)}, u32[]{:S(2)}, u32[]{:S(2)}) collective-permute-start(bf16[1056,128]{1,0:T(8,128)(2,1)S(1)} %shard_map.96.pack_0), channel_id=1, source_target_pairs={{0,1},{1,0},{2,3},{3,2},{4,5},{5,4},{6,7},{7,6},{8,9},{9,8},{10,11... | collective-permute-start | bytes 811016 | tf_op jit(solution)/shard_map/ppermute | solution.py:162
  12.0 8.0 %collective-permute-start.1 = (bf16[1024,128]{1,0:T(8,128)(2,1)S(1)}, bf16[1024,128]{1,0:T(8,128)(2,1)S(1)}, u32[]{:S(2)}, u32[]{:S(2)}) collective-permute-start(bf16[1024,128]{1,0:T(8,128)(2,1)S(1)} %get-tuple-element.33), channel_id=1, source_target_pairs={{0,4},{4,0},{1,5},{5,1},{2,6},{6,2},{3,7},{7,3},{8,12},{12,8},{9,1... | collective-permute-start | bytes 786440 | tf_op jit(solution)/shard_map/ppermute | solution.py:162
  18.7 1.3 %collective-permute-start.6 = (bf16[256,128]{1,0:T(8,128)(2,1)S(1)}, bf16[256,128]{1,0:T(8,128)(2,1)S(1)}, u32[]{:S(2)}, u32[]{:S(2)}) collective-permute-start(bf16[256,128]{1,0:T(8,128)(2,1)S(1)} %get-tuple-element.40), channel_id=1, source_target_pairs={{0,1},{1,0},{2,3},{3,2},{4,5},{5,4},{6,7},{7,6},{8,9},{9,8},{10,11... | collective-permute-start | bytes 196616 | tf_op jit(solution)/shard_map/ppermute | solution.py:162
  20.9 18.0 %all-to-all-start = ((bf16[16,80,128]{2,1,0:T(8,128)(2,1)}), bf16[16,80,128]{2,1,0:T(8,128)(2,1)S(1)}, u32[]{:S(2)}, u32[]{:S(2)}) async-start(bf16[16,80,128]{2,1,0:T(8,128)(2,1)} %shard_map.100), calls=%async_computation | async-start | bytes 655360 | tf_op jit(solution)/shard_map/all_to_all | solution.py:548
  28.0 4.6 %collective-permute-start.7 = (bf16[1024,128]{1,0:T(8,128)(2,1)S(1)}, bf16[1024,128]{1,0:T(8,128)(2,1)S(1)}, u32[]{:S(2)}, u32[]{:S(2)}) collective-permute-start(bf16[1024,128]{1,0:T(8,128)(2,1)S(1)} %get-tuple-element.45), channel_id=1, source_target_pairs={{0,1},{1,0},{2,3},{3,2},{4,5},{5,4},{6,7},{7,6},{8,9},{9,8},{10,11... | collective-permute-start | bytes 786440 | tf_op jit(solution)/shard_map/ppermute | solution.py:162
  29.1 9.7 %collective-permute-start.8 = (bf16[1024,128]{1,0:T(8,128)(2,1)S(1)}, bf16[1024,128]{1,0:T(8,128)(2,1)S(1)}, u32[]{:S(2)}, u32[]{:S(2)}) collective-permute-start(bf16[1024,128]{1,0:T(8,128)(2,1)S(1)} %get-tuple-element.46), channel_id=1, source_target_pairs={{1,2},{2,1},{5,6},{6,5},{9,10},{10,9},{13,14},{14,13},{17,18},{18,... | collective-permute-start | bytes 786440 | tf_op jit(solution)/shard_map/ppermute | solution.py:524
  60.3 3.8 %collective-permute-start.9 = (bf16[16,144,128]{2,1,0:T(8,128)(2,1)S(1)}, bf16[16,144,128]{2,1,0:T(8,128)(2,1)S(1)}, u32[]{:S(2)}, u32[]{:S(2)}) collective-permute-start(bf16[16,144,128]{2,1,0:T(8,128)(2,1)S(1)} %all_to_all.10.refs_0_), channel_id=1, source_target_pairs={{0,1},{1,0},{2,3},{3,2},{4,5},{5,4},{6,7},{7,6},{8,9},{9,8},{10,11... | collective-permute-start | bytes 1769480 | tf_op jit(solution)/shard_map/ppermute | solution.py:162

commit v15 on v14

--- a/solution.py
+++ b/solution.py
@@ -49,7 +49,8 @@
     lax.fori_loop(0, length, gather, 0, unroll=4)
 
 
-def pack_kernel(field, out, flat):
+def pack_kernel(field, *refs):
+    out, flat = refs[-2:]
     chans, length, width = field.shape
     zeros = jnp.zeros((chans, width), BF16)
     out[0:chans, :] = zeros
@@ -57,14 +58,20 @@
     turned(field, flat, out, 0, chans, 1)
 
 
-def pack(field):
+def pack(field, after, weight):
     chans, length, width = field.shape
-    return vmem_call(
+    spec = pl.BlockSpec(memory_space=pltpu.VMEM)
+    return pl.pallas_call(
         pack_kernel,
-        jax.ShapeDtypeStruct(((length + 2) * chans, width), BF16),
-        (pltpu.VMEM((chans * length, width), F32),),
-        pl.CostEstimate(flops=0, bytes_accessed=16 * field.size, transcendentals=0),
-    )(field)
+        out_shape=jax.ShapeDtypeStruct(((length + 2) * chans, width), BF16),
+        in_specs=[spec] + [pl.BlockSpec(memory_space=pl.ANY) for _ in after],
+        out_specs=spec,
+        scratch_shapes=[pltpu.VMEM((chans * length, width), F32)],
+        compiler_params=pltpu.CompilerParams(vmem_limit_bytes=24 * 2**20),
+        cost_estimate=pl.CostEstimate(
+            flops=0, bytes_accessed=weight * field.size, transcendentals=0
+        ),
+    )(field, *after)
 
 
 def in_steps(body, rows, count=8):
@@ -77,38 +84,14 @@
     lax.fori_loop(0, count, one, 0)
 
 
-def cast_kernel(src, after, out):
-    rows = out.shape[0]
-    start = (1 - lax.axis_index("core")) * rows
-
-    def cast(at, step):
-        value = src[pl.ds(pl.multiple_of(start + at, 16), step), :]
-        out[pl.ds(pl.multiple_of(at, 16), step), :] = value.astype(out.dtype)
-
-    in_steps(cast, rows)
-
-
-def cast(value, after):
-    spec = pl.BlockSpec(memory_space=pltpu.VMEM)
-    return pl.pallas_call(
-        cast_kernel,
-        out_shape=jax.ShapeDtypeStruct((value.shape[0] // 2, LANES), BF16),
-        in_specs=[spec, pl.BlockSpec(memory_space=pl.ANY)],
-        out_specs=spec,
-        compiler_params=pltpu.CompilerParams(vmem_limit_bytes=24 * 2**20),
-        cost_estimate=pl.CostEstimate(flops=0, bytes_accessed=4 * value.size, transcendentals=0),
-    )(value, after)
-
-
-def add_kernel(src, other, send, keep):
-    half, rows = (other.shape[0], send.shape[0])
-    start = lax.axis_index("core") * half
+def add_kernel(own, other, send, keep):
+    rows = send.shape[0]
     mine = lax.axis_index("x") * rows
     theirs = rows - mine
 
     def total(at, step):
-        value = src[pl.ds(pl.multiple_of(start + at, 16), step), :]
-        return value + other[pl.ds(pl.multiple_of(at, 16), step), :].astype(F32)
+        at = pl.ds(pl.multiple_of(at, 16), step)
+        return own[at, :] + other[at, :].astype(F32)
 
     def add(at, step):
         to = pl.ds(pl.multiple_of(at, 16), step)
@@ -118,14 +101,14 @@
     in_steps(add, rows)
 
 
-def add(value, other):
+def add(own, other):
     rows = other.shape[0] // 2
     return vmem_call(
         add_kernel,
         (jax.ShapeDtypeStruct((rows, LANES), BF16), jax.ShapeDtypeStruct((rows, LANES), F32)),
         (),
-        pl.CostEstimate(flops=0, bytes_accessed=4 * value.size, transcendentals=0),
-    )(value, other)
+        pl.CostEstimate(flops=0, bytes_accessed=8 * own.size, transcendentals=0),
+    )(own, other)
 
 
 def combine_kernel(keep, other, terms, more, out):
@@ -529,11 +512,15 @@
     devices, copies = (lax.axis_size(EVERY), lax.axis_size(SAME))
     length = grad_bucket.shape[1]
     bucket = grad_bucket.reshape(length // LANES, LANES)
-    cot = pack(out_cot[0, 0])
+    cot = pack(out_cot[0, 0], [], 256)
     cots = (swapped(cot), cot, crossed(cot))
-    vol = pack(volume_in[0, 0])
+    vol = pack(volume_in[0, 0], [cot], 16)
     vols = (swapped(vol), vol, crossed(vol))
-    send, near = add(bucket, swapped(cast(bucket, cot)))
+    bucket, cot = lax.optimization_barrier((bucket, cot))
+    core, half = (lax.axis_index("core"), bucket.shape[0] // 2)
+    send = lax.dynamic_slice_in_dim(bucket, (1 - core) * half, half).astype(BF16)
+    near = lax.dynamic_slice_in_dim(bucket, core * half, half)
+    send, near = add(near, swapped(send))
     act, send, near = lax.optimization_barrier((hidden_act[0, 0], send, near))
     far = swapped(send, "x")
 

time: 65.9 us -> 67.6 us (1.026)
  Pallas kernels: 11.1 us -> 14 us
  waiting for transfers between devices: 7.61 us -> 6.57 us
  starting transfers between devices: 22 us -> 21.3 us
    pallas_call x1, Pallas kernels: 2.57 us -> 3.77 us  [first_part(): vmem_call(first_kernel, (jax.ShapeDtypeStruct(((length + 2) * 3 * c1, wid...]
    pallas_call x1, Pallas kernels: 0.81 us -> 1.84 us  [gradient_part(): vmem_call(gradient_kernel, (jax.ShapeDtypeStruct((rows // 2, LANES), BF16...]
    all_to_all x1, starting transfers between devices: 7.09 us -> 6.08 us  [per_device(): parts = lax.all_to_all(parts, SAME, 0, 0)]
    ppermute x3, waiting for transfers between devices: 7.41 us -> 6.54 us  [crossed(): return lax.ppermute(value, SPACE, pairs + [(m, n) for n, m in pairs])]
    convert_element_type x0 -> x1, local copies, waits for them, and re-layouts: none -> 0.85 us  [per_device(): lax.dynamic_slice_in_dim(bucket, (1 - core) * half, half).astype(BF16)]
    pallas_call x1, Pallas kernels: 1.05 us -> 1.74 us  [input_part(): vmem_call(input_kernel, (jax.ShapeDtypeStruct(plane, F32), jax.ShapeDtype...]
  transfers between devices with their start and end apart: 11 -> 11, of which waited for: 3 -> 1; matrix products, arithmetic and copies ran while one was open for 0% -> 1% of each run, Pallas kernels for 12% -> 16%
where the time goes in v15:
time: 67.6 us; the launch traced here: 67.1 us
  starting transfers between devices  21.3 us (32%)
  blocking collectives  21.3 us (32%)
  Pallas kernels  14 us (21%)
  waiting for transfers between devices  6.57 us (10%)
  local copies, waits for them, and re-layouts  3.09 us (5%)
  between operations  0.86 us (1%)
    all_to_all x1, blocking collectives, per_device(): mine = lax.all_to_all(shares, SAME, 0, 0)  21.3 us
    ppermute x3, starting transfers between devices, crossed(): return lax.ppermute(value, SPACE, pairs + [(m, n) for n, m in pairs])  9.97 us
    ppermute x3, waiting for transfers between devices, crossed(): return lax.ppermute(value, SPACE, pairs + [(m, n) for n, m in pairs])  6.54 us
    all_to_all x1, starting transfers between devices, per_device(): parts = lax.all_to_all(parts, SAME, 0, 0)  6.08 us
    ppermute x7, starting transfers between devices, swapped(): return lax.ppermute(value, axis, [(0, 1), (1, 0)])  5.29 us
    pallas_call x1, Pallas kernels, first_part(): vmem_call(first_kernel, (jax.ShapeDtypeStruct(((length + 2) * 3 * c1, wid...  3.77 us
    unnamed x14, local copies, waits for them, and re-layouts  2.16 us
    pallas_call x1, Pallas kernels, gradient_part(): vmem_call(gradient_kernel, (jax.ShapeDtypeStruct((rows // 2, LANES), BF16...  1.84 us
  transfers between devices with their start and end apart: 11, of which 1 were waited for; matrix products, arithmetic and copies ran while one was open for 1% of the time, Pallas kernels for 16%

profile of v15, /device:TPU:1, one launch (start us, length us, event | category | flops | bytes accessed | tf_op | source)
XLA Modules:
  0.0 67.1 jit_solution(13056194484154978745)
XLA Ops:
  0.6 0.0 copy-start
  0.6 0.0 copy-start.1
  0.7 1.2 %copy-done.1 = bf16[1,1,32,64,128]{4,3,2,1,0:T(8,128)(2,1)S(1)} copy-done((bf16[1,1,32,64,128]{4,3,2,1,0:T(8,128)(2,1)S(1)}, bf16[1,1,32,64,128]{4,3,2,1,0:T(8,128)(2,1)}, u32[]{:S(2)}) %copy-start.1) | copy-done | bytes 524312
  1.8 0.8 %shard_map.93.refs_0_.pack_0 = bf16[2112,128]{1,0:T(8,128)(2,1)S(1)} custom-call(bf16[32,64,128]{2,1,0:T(8,128)(2,1)S(1)} %bitcast.10), custom_call_target="tpu_custom_call" | custom-call | bytes 67108864 | tf_op jit(solution)/shard_map/pallas_call | solution.py:64
  2.6 4.5 %collective-permute-start.5 = (bf16[2112,128]{1,0:T(8,128)(2,1)S(1)}, bf16[2112,128]{1,0:T(8,128)(2,1)}, u32[]{:S(2)}, u32[]{:S(2)}) collective-permute-start(bf16[2112,128]{1,0:T(8,128)(2,1)S(1)} %shard_map.93.refs_0_.pack_0), channel_id=1, source_target_pairs={{1,2},{2,1},{5,6},{6,5},{9,10},{10,9},{13,14},{14,13},{17,18},{18,... | collective-permute-start | bytes 1622024 | tf_op jit(solution)/shard_map/ppermute | solution.py:507
  7.2 0.1 collective-permute-start.4
  7.3 0.0 copy-done
  7.3 0.9 %dynamic-slice_convert_fusion = bf16[2048,128]{1,0:T(8,128)(2,1)} fusion(f32[4096,128]{1,0:T(8,128)S(1)} %bitcast.8, s32[]{:T(128)S(6)} %select_n.7), kind=kLoop, calls=%fused_computation | loop fusion | bytes 1048580 | tf_op jit(solution)/shard_map/convert_element_type | solution.py:521
  8.1 0.5 collective-permute-start
  8.6 0.0 copy-start.3
  8.6 0.9 %copy-done.3 = bf16[1,1,16,64,128]{4,3,2,1,0:T(8,128)(2,1)S(1)} copy-done((bf16[1,1,16,64,128]{4,3,2,1,0:T(8,128)(2,1)S(1)}, bf16[1,1,16,64,128]{4,3,2,1,0:T(8,128)(2,1)}, u32[]{:S(2)}) %copy-start.3) | copy-done | bytes 262168
  9.6 0.5 shard_map.95.pack_0
  10.0 0.0 copy-start.5
  10.0 2.1 %collective-permute-start.3 = (bf16[1056,128]{1,0:T(8,128)(2,1)S(1)}, bf16[1056,128]{1,0:T(8,128)(2,1)}, u32[]{:S(2)}, u32[]{:S(2)}) collective-permute-start(bf16[1056,128]{1,0:T(8,128)(2,1)S(1)} %shard_map.95.pack_0), channel_id=1, source_target_pairs={{1,2},{2,1},{5,6},{6,5},{9,10},{10,9},{13,14},{14,13},{17,18},{18,... | collective-permute-start | bytes 811016 | tf_op jit(solution)/shard_map/ppermute | solution.py:507
  12.1 0.1 collective-permute-start.2
  12.2 0.0 copy-start.2
  12.2 0.0 copy-start.4
  12.2 0.1 constant_dynamic-slice_fusion.own
  12.3 0.0 collective-permute-done.other
  12.3 0.2 shard_map.94
  12.5 1.3 %collective-permute-start.1 = (bf16[1024,128]{1,0:T(8,128)(2,1)S(1)}, bf16[1024,128]{1,0:T(8,128)(2,1)S(1)}, u32[]{:S(2)}, u32[]{:S(2)}) collective-permute-start(bf16[1024,128]{1,0:T(8,128)(2,1)S(1)} %get-tuple-element.35), channel_id=1, source_target_pairs={{0,4},{4,0},{1,5},{5,1},{2,6},{6,2},{3,7},{7,3},{8,12},{12,8},{9,1... | collective-permute-start | bytes 786440 | tf_op jit(solution)/shard_map/ppermute | solution.py:145
  13.7 0.0 copy-done.5
  13.7 0.0 copy-done.2
  13.7 0.0 copy-done.4
  13.7 0.9 %shard_map.96 = (bf16[2048,128]{1,0:T(8,128)(2,1)S(1)}, bf16[96,288]{1,0:T(8,128)(2,1)S(1)}, bf16[48,288]{1,0:T(8,128)(2,1)S(1)}) custom-call(bf16[32,64,128]{2,1,0:T(8,128)(2,1)S(1)} %bitcast.11, bf16[3,3,3,32,32]{4,3,2,1,0:T(8,128)(2,1)S(1)} %copy-done.4, bf16[3,3,3,16,32]{4,3,2,1,0:T(8,128)(2,1)S(1)} %copy-done.5), custom_call_target="tpu_custom_call" | custom-call | bytes 4194304 | tf_op jit(solution)/shard_map/pallas_call | solution.py:200
  14.7 0.0 collective-permute-done.5.pack_out
  14.7 0.0 collective-permute-done.4.pack_in
  14.7 3.8 %shard_map.97 = (bf16[6336,128]{1,0:T(8,128)(2,1)S(1)}, f32[288,128]{1,0:T(8,128)S(1)}) custom-call(bf16[2112,128]{1,0:T(8,128)(2,1)} %collective-permute-done.4.pack_in, bf16[2112,128]{1,0:T(8,128)(2,1)S(1)} %shard_map.93.refs_0_.pack_0, bf16[2112,128]{1,0:T(8,128)(2,1)} %collective-permute-done.5.pack_out, bf16[2048,128]{1,0:T(8,128)(2,1)S(1)} %get-tuple-element.37.acts, ...), custom_call_target="tpu_custom_call" | custom-call | flops 1000000000 | bytes 20971520 | tf_op jit(solution)/shard_map/pallas_call | solution.py:308
  18.5 0.0 collective-permute-done.3.pack_out
  18.5 0.0 collective-permute-done.2.pack_in
  18.5 1.8 %shard_map.98 = (bf16[256,128]{1,0:T(8,128)(2,1)S(1)}, f32[256,128]{1,0:T(8,128)S(1)}) custom-call(bf16[1056,128]{1,0:T(8,128)(2,1)} %collective-permute-done.2.pack_in, bf16[1056,128]{1,0:T(8,128)(2,1)S(1)} %shard_map.95.pack_0, bf16[1056,128]{1,0:T(8,128)(2,1)} %collective-permute-done.3.pack_out, bf16[6336,128]{1,0:T(8,128)(2,1)S(1)} %get-tuple-element.39.pres, ...), custom_call_target="tpu_custom_call" | custom-call | flops 1000000000 | bytes 5242880 | tf_op jit(solution)/shard_map/pallas_call | solution.py:322
  20.3 0.8 %collective-permute-start.6 = (bf16[256,128]{1,0:T(8,128)(2,1)S(1)}, bf16[256,128]{1,0:T(8,128)(2,1)S(1)}, u32[]{:S(2)}, u32[]{:S(2)}) collective-permute-start(bf16[256,128]{1,0:T(8,128)(2,1)S(1)} %get-tuple-element.42), channel_id=1, source_target_pairs={{0,1},{1,0},{2,3},{3,2},{4,5},{5,4},{6,7},{7,6},{8,9},{9,8},{10,11... | collective-permute-start | bytes 196616 | tf_op jit(solution)/shard_map/ppermute | solution.py:145
  21.1 1.7 %shard_map.100 = (f32[1024,128]{1,0:T(8,128)S(1)}, bf16[1024,128]{1,0:T(8,128)(2,1)}, bf16[1024,128]{1,0:T(8,128)(2,1)S(1)}) custom-call(bf16[6336,128]{1,0:T(8,128)(2,1)S(1)} %get-tuple-element.39.pres, bf16[48,288]{1,0:T(8,128)(2,1)S(1)} %get-tuple-element.43.w_one), custom_call_target="tpu_custom_call" | custom-call | flops 1000000000 | bytes 5242880 | tf_op jit(solution)/shard_map/pallas_call | solution.py:336
  22.9 0.0 copy-start.6
  22.9 0.0 collective-permute-done.6.more
  22.9 0.0 collective-permute-done.1.other
  22.9 0.8 %shard_map.99 = bf16[16,80,128]{2,1,0:T(8,128)(2,1)} custom-call(f32[1024,128]{1,0:T(8,128)S(1)} %get-tuple-element.34.keep, bf16[1024,128]{1,0:T(8,128)(2,1)S(1)} %collective-permute-done.1.other, f32[256,128]{1,0:T(8,128)S(1)} %get-tuple-element.41.terms, bf16[256,128]{1,0:T(8,128)(2,1)S(1)} %collective-permute-done.6.more), custom_call_target="tpu_custom_call" | custom-call | bytes 1048576 | tf_op jit(solution)/shard_map/pallas_call | solution.py:130
  23.7 0.0 copy-done.6
  23.7 6.1 %all-to-all-start = ((bf16[16,80,128]{2,1,0:T(8,128)(2,1)}), bf16[16,80,128]{2,1,0:T(8,128)(2,1)S(1)}, u32[]{:S(2)}, u32[]{:S(2)}) async-start(bf16[16,80,128]{2,1,0:T(8,128)(2,1)} %shard_map.99), calls=%async_computation | async-start | bytes 655360 | tf_op jit(solution)/shard_map/all_to_all | solution.py:535
  29.8 0.7 %collective-permute-start.7 = (bf16[1024,128]{1,0:T(8,128)(2,1)}, bf16[1024,128]{1,0:T(8,128)(2,1)S(1)}, u32[]{:S(2)}, u32[]{:S(2)}) collective-permute-start(bf16[1024,128]{1,0:T(8,128)(2,1)} %get-tuple-element.47), channel_id=1, source_target_pairs={{0,1},{1,0},{2,3},{3,2},{4,5},{5,4},{6,7},{7,6},{8,9},{9,8},{10,11... | collective-permute-start | bytes 786440 | tf_op jit(solution)/shard_map/ppermute | solution.py:145
  30.5 3.4 %collective-permute-start.8 = (bf16[1024,128]{1,0:T(8,128)(2,1)}, bf16[1024,128]{1,0:T(8,128)(2,1)S(1)}, u32[]{:S(2)}, u32[]{:S(2)}) collective-permute-start(bf16[1024,128]{1,0:T(8,128)(2,1)} %copy-done.6), channel_id=1, source_target_pairs={{1,2},{2,1},{5,6},{6,5},{9,10},{10,9},{13,14},{14,13},{17,18},{18,... | collective-permute-start | bytes 786440 | tf_op jit(solution)/shard_map/ppermute | solution.py:507
  33.9 0.0 collective-permute-done.7.first
  33.9 6.5 %collective-permute-done.8.second = bf16[1024,128]{1,0:T(8,128)(2,1)S(1)} collective-permute-done((bf16[1024,128]{1,0:T(8,128)(2,1)}, bf16[1024,128]{1,0:T(8,128)(2,1)S(1)}, u32[]{:S(2)}, u32[]{:S(2)}) %collective-permute-start.8) | collective-permute-done | bytes 262176 | tf_op jit(solution)/shard_map/ppermute | solution.py:507
  40.5 0.0 all-to-all-done.refs_0_
  40.5 0.1 shard_map.101
  40.6 21.3 %all_to_all.10.refs_0_ = bf16[16,144,128]{2,1,0:T(8,128)(2,1)S(1)} all-to-all(bf16[16,144,128]{2,1,0:T(8,128)(2,1)S(1)} %shard_map.101), channel_id=1, replica_groups=mesh['z'=4,'x'=2,'y'=2,'core'=2] {'x','z','y'}, dimensions={0} | all-to-all | bytes 1179648 | tf_op jit(solution)/shard_map/all_to_all | solution.py:540
  61.9 1.9 %collective-permute-start.9 = (bf16[16,144,128]{2,1,0:T(8,128)(2,1)S(1)}, bf16[16,144,128]{2,1,0:T(8,128)(2,1)S(1)}, u32[]{:S(2)}, u32[]{:S(2)}) collective-permute-start(bf16[16,144,128]{2,1,0:T(8,128)(2,1)S(1)} %all_to_all.10.refs_0_), channel_id=1, source_target_pairs={{0,1},{1,0},{2,3},{3,2},{4,5},{5,4},{6,7},{7,6},{8,9},{9,8},{10,11... | collective-permute-start | bytes 1769480 | tf_op jit(solution)/shard_map/ppermute | solution.py:145
  63.8 1.0 %shard_map.102 = bf16[16,64,128]{2,1,0:T(8,128)(2,1)} custom-call(f32[1024,128]{1,0:T(8,128)S(1)} %get-tuple-element.51.own, bf16[1024,128]{1,0:T(8,128)(2,1)S(1)} %collective-permute-done.7.first, bf16[1024,128]{1,0:T(8,128)(2,1)S(1)} %collective-permute-done.8.second), custom_call_target="tpu_custom_call" | custom-call | flops 262144 | bytes 1048576 | tf_op jit(solution)/shard_map/pallas_call | solution.py:366
  64.7 1.0 %shard_map.103.refs_2_ = f32[4096,128]{1,0:T(8,128)} custom-call(bf16[16,144,128]{2,1,0:T(8,128)(2,1)S(1)} %all_to_all.10.refs_0_), custom_call_target="tpu_custom_call" | custom-call | tf_op jit(solution)/shard_map/pallas_call | solution.py:476
  65.7 0.0 collective-permute-done.9.refs_1_
  65.8 1.4 %shard_map.104 = (f32[4096,128]{1,0:T(8,128)}, f32[432,32]{1,0:T(8,128)}, f32[864,32]{1,0:T(8,128)}) custom-call(bf16[16,144,128]{2,1,0:T(8,128)(2,1)S(1)} %all_to_all.10.refs_0_, bf16[16,144,128]{2,1,0:T(8,128)(2,1)S(1)} %collective-permute-done.9.refs_1_, f32[4096,128]{1,0:T(8,128)} %shard_map.103.refs_2_), custom_call_target="tpu_custom_call", output_to_operand_aliasing={{0}: (2, {})} | custom-call | tf_op jit(solution)/shard_map/pallas_call | solution.py:484
Async XLA Ops:
  0.6 6.6 %copy-start = (f32[1,524288]{1,0:T(1,128)S(1)}, f32[1,524288]{1,0:T(1,128)}, u32[]{:S(2)}) copy-start(f32[1,524288]{1,0:T(1,128)} %param.11) | copy-start | bytes 6291460
  0.6 1.2 %copy-start.1 = (bf16[1,1,32,64,128]{4,3,2,1,0:T(8,128)(2,1)S(1)}, bf16[1,1,32,64,128]{4,3,2,1,0:T(8,128)(2,1)}, u32[]{:S(2)}) copy-start(bf16[1,1,32,64,128]{4,3,2,1,0:T(8,128)(2,1)} %param.8) | copy-start | bytes 1572868
  2.6 12.0 %collective-permute-start.5 = (bf16[2112,128]{1,0:T(8,128)(2,1)S(1)}, bf16[2112,128]{1,0:T(8,128)(2,1)}, u32[]{:S(2)}, u32[]{:S(2)}) collective-permute-start(bf16[2112,128]{1,0:T(8,128)(2,1)S(1)} %shard_map.93.refs_0_.pack_0), channel_id=1, source_target_pairs={{1,2},{2,1},{5,6},{6,5},{9,10},{10,9},{13,14},{14,13},{17,18},{18,... | collective-permute-start | bytes 1622024 | tf_op jit(solution)/shard_map/ppermute | solution.py:507
  7.2 7.5 %collective-permute-start.4 = (bf16[2112,128]{1,0:T(8,128)(2,1)S(1)}, bf16[2112,128]{1,0:T(8,128)(2,1)}, u32[]{:S(2)}, u32[]{:S(2)}) collective-permute-start(bf16[2112,128]{1,0:T(8,128)(2,1)S(1)} %shard_map.93.refs_0_.pack_0), channel_id=1, source_target_pairs={{0,1},{1,0},{2,3},{3,2},{4,5},{5,4},{6,7},{7,6},{8,9},{9,8},{10,11... | collective-permute-start | bytes 1622024 | tf_op jit(solution)/shard_map/ppermute | solution.py:145
  8.1 4.2 %collective-permute-start = (bf16[2048,128]{1,0:T(8,128)(2,1)}, bf16[2048,128]{1,0:T(8,128)(2,1)S(1)}, u32[]{:S(2)}, u32[]{:S(2)}) collective-permute-start(bf16[2048,128]{1,0:T(8,128)(2,1)} %dynamic-slice_convert_fusion), channel_id=1, source_target_pairs={{0,1},{1,0},{2,3},{3,2},{4,5},{5,4},{6,7},{7,6},{8,9},{9,8},{10,11... | collective-permute-start | bytes 1572872 | tf_op jit(solution)/shard_map/ppermute | solution.py:145
  8.6 0.9 %copy-start.3 = (bf16[1,1,16,64,128]{4,3,2,1,0:T(8,128)(2,1)S(1)}, bf16[1,1,16,64,128]{4,3,2,1,0:T(8,128)(2,1)}, u32[]{:S(2)}) copy-start(bf16[1,1,16,64,128]{4,3,2,1,0:T(8,128)(2,1)} %param.6) | copy-start | bytes 786436
  10.0 3.7 %copy-start.5 = (bf16[3,3,3,16,32]{4,3,2,1,0:T(8,128)(2,1)S(1)}, bf16[3,3,3,16,32]{4,3,2,1,0:T(8,128)(2,1)}, u32[]{:S(2)}) copy-start(bf16[3,3,3,16,32]{4,3,2,1,0:T(8,128)(2,1)} %one.1) | copy-start | bytes 82948
  10.0 8.4 %collective-permute-start.3 = (bf16[1056,128]{1,0:T(8,128)(2,1)S(1)}, bf16[1056,128]{1,0:T(8,128)(2,1)}, u32[]{:S(2)}, u32[]{:S(2)}) collective-permute-start(bf16[1056,128]{1,0:T(8,128)(2,1)S(1)} %shard_map.95.pack_0), channel_id=1, source_target_pairs={{1,2},{2,1},{5,6},{6,5},{9,10},{10,9},{13,14},{14,13},{17,18},{18,... | collective-permute-start | bytes 811016 | tf_op jit(solution)/shard_map/ppermute | solution.py:507
  12.1 6.4 %collective-permute-start.2 = (bf16[1056,128]{1,0:T(8,128)(2,1)S(1)}, bf16[1056,128]{1,0:T(8,128)(2,1)}, u32[]{:S(2)}, u32[]{:S(2)}) collective-permute-start(bf16[1056,128]{1,0:T(8,128)(2,1)S(1)} %shard_map.95.pack_0), channel_id=1, source_target_pairs={{0,1},{1,0},{2,3},{3,2},{4,5},{5,4},{6,7},{7,6},{8,9},{9,8},{10,11... | collective-permute-start | bytes 811016 | tf_op jit(solution)/shard_map/ppermute | solution.py:145
  12.2 1.6 %copy-start.2 = (bf16[1,1,32,64,128]{4,3,2,1,0:T(8,128)(2,1)S(1)}, bf16[1,1,32,64,128]{4,3,2,1,0:T(8,128)(2,1)}, u32[]{:S(2)}) copy-start(bf16[1,1,32,64,128]{4,3,2,1,0:T(8,128)(2,1)} %param.7) | copy-start | bytes 1572868
  12.2 1.5 %copy-start.4 = (bf16[3,3,3,32,32]{4,3,2,1,0:T(8,128)(2,1)S(1)}, bf16[3,3,3,32,32]{4,3,2,1,0:T(8,128)(2,1)}, u32[]{:S(2)}) copy-start(bf16[3,3,3,32,32]{4,3,2,1,0:T(8,128)(2,1)} %two.1) | copy-start | bytes 165892
  12.5 10.4 %collective-permute-start.1 = (bf16[1024,128]{1,0:T(8,128)(2,1)S(1)}, bf16[1024,128]{1,0:T(8,128)(2,1)S(1)}, u32[]{:S(2)}, u32[]{:S(2)}) collective-permute-start(bf16[1024,128]{1,0:T(8,128)(2,1)S(1)} %get-tuple-element.35), channel_id=1, source_target_pairs={{0,4},{4,0},{1,5},{5,1},{2,6},{6,2},{3,7},{7,3},{8,12},{12,8},{9,1... | collective-permute-start | bytes 786440 | tf_op jit(solution)/shard_map/ppermute | solution.py:145
  20.3 2.5 %collective-permute-start.6 = (bf16[256,128]{1,0:T(8,128)(2,1)S(1)}, bf16[256,128]{1,0:T(8,128)(2,1)S(1)}, u32[]{:S(2)}, u32[]{:S(2)}) collective-permute-start(bf16[256,128]{1,0:T(8,128)(2,1)S(1)} %get-tuple-element.42), channel_id=1, source_target_pairs={{0,1},{1,0},{2,3},{3,2},{4,5},{5,4},{6,7},{7,6},{8,9},{9,8},{10,11... | collective-permute-start | bytes 196616 | tf_op jit(solution)/shard_map/ppermute | solution.py:145
  22.9 0.8 %copy-start.6 = (bf16[1024,128]{1,0:T(8,128)(2,1)}, bf16[1024,128]{1,0:T(8,128)(2,1)S(1)}, u32[]{:S(2)}) copy-start(bf16[1024,128]{1,0:T(8,128)(2,1)S(1)} %get-tuple-element.48) | copy-start | bytes 786436
  23.7 16.8 %all-to-all-start = ((bf16[16,80,128]{2,1,0:T(8,128)(2,1)}), bf16[16,80,128]{2,1,0:T(8,128)(2,1)S(1)}, u32[]{:S(2)}, u32[]{:S(2)}) async-start(bf16[16,80,128]{2,1,0:T(8,128)(2,1)} %shard_map.99), calls=%async_computation | async-start | bytes 655360 | tf_op jit(solution)/shard_map/all_to_all | solution.py:535
  29.8 4.1 %collective-permute-start.7 = (bf16[1024,128]{1,0:T(8,128)(2,1)}, bf16[1024,128]{1,0:T(8,128)(2,1)S(1)}, u32[]{:S(2)}, u32[]{:S(2)}) collective-permute-start(bf16[1024,128]{1,0:T(8,128)(2,1)} %get-tuple-element.47), channel_id=1, source_target_pairs={{0,1},{1,0},{2,3},{3,2},{4,5},{5,4},{6,7},{7,6},{8,9},{9,8},{10,11... | collective-permute-start | bytes 786440 | tf_op jit(solution)/shard_map/ppermute | solution.py:145
  30.5 9.9 %collective-permute-start.8 = (bf16[1024,128]{1,0:T(8,128)(2,1)}, bf16[1024,128]{1,0:T(8,128)(2,1)S(1)}, u32[]{:S(2)}, u32[]{:S(2)}) collective-permute-start(bf16[1024,128]{1,0:T(8,128)(2,1)} %copy-done.6), channel_id=1, source_target_pairs={{1,2},{2,1},{5,6},{6,5},{9,10},{10,9},{13,14},{14,13},{17,18},{18,... | collective-permute-start | bytes 786440 | tf_op jit(solution)/shard_map/ppermute | solution.py:507
  61.9 3.8 %collective-permute-start.9 = (bf16[16,144,128]{2,1,0:T(8,128)(2,1)S(1)}, bf16[16,144,128]{2,1,0:T(8,128)(2,1)S(1)}, u32[]{:S(2)}, u32[]{:S(2)}) collective-permute-start(bf16[16,144,128]{2,1,0:T(8,128)(2,1)S(1)} %all_to_all.10.refs_0_), channel_id=1, source_target_pairs={{0,1},{1,0},{2,3},{3,2},{4,5},{5,4},{6,7},{7,6},{8,9},{9,8},{10,11... | collective-permute-start | bytes 1769480 | tf_op jit(solution)/shard_map/ppermute | solution.py:145

commit v16 on v15

--- a/solution.py
+++ b/solution.py
@@ -513,13 +513,14 @@
     length = grad_bucket.shape[1]
     bucket = grad_bucket.reshape(length // LANES, LANES)
     cot = pack(out_cot[0, 0], [], 256)
-    cots = (swapped(cot), cot, crossed(cot))
-    vol = pack(volume_in[0, 0], [cot], 16)
-    vols = (swapped(vol), vol, crossed(vol))
     bucket, cot = lax.optimization_barrier((bucket, cot))
     core, half = (lax.axis_index("core"), bucket.shape[0] // 2)
     send = lax.dynamic_slice_in_dim(bucket, (1 - core) * half, half).astype(BF16)
     near = lax.dynamic_slice_in_dim(bucket, core * half, half)
+    cot, send, near = lax.optimization_barrier((cot, send, near))
+    cots = (swapped(cot), cot, crossed(cot))
+    vol = pack(volume_in[0, 0], [cot], 16)
+    vols = (swapped(vol), vol, crossed(vol))
     send, near = add(near, swapped(send))
     act, send, near = lax.optimization_barrier((hidden_act[0, 0], send, near))
     far = swapped(send, "x")

time: 67.6 us -> 65.6 us (0.970)
  Pallas kernels: 14 us -> 11.7 us
  waiting for transfers between devices: 6.57 us -> 8.81 us
  local copies, waits for them, and re-layouts: 3.09 us -> 1.36 us
    ppermute x3, waiting for transfers between devices: 6.54 us -> 8.79 us  [crossed(): return lax.ppermute(value, SPACE, pairs + [(m, n) for n, m in pairs])]
    pallas_call x1, Pallas kernels: 3.77 us -> 2.55 us  [first_part(): vmem_call(first_kernel, (jax.ShapeDtypeStruct(((length + 2) * 3 * c1, wid...]
    ppermute x7, starting transfers between devices: 5.29 us -> 4.2 us  [swapped(): return lax.ppermute(value, axis, [(0, 1), (1, 0)])]
    pallas_call x1, Pallas kernels: 1.84 us -> 0.81 us  [gradient_part(): vmem_call(gradient_kernel, (jax.ShapeDtypeStruct((rows // 2, LANES), BF16...]
    unnamed x14, local copies, waits for them, and re-layouts: 2.16 us -> 1.22 us
    all_to_all x1, starting transfers between devices: 6.08 us -> 6.88 us  [per_device(): parts = lax.all_to_all(parts, SAME, 0, 0)]
    convert_element_type x1, local copies, waits for them, and re-layouts: 0.85 us -> 0.06 us  [per_device(): lax.dynamic_slice_in_dim(bucket, (1 - core) * half, half).astype(BF16)]
  transfers between devices with their start and end apart: 11 -> 11, of which waited for: 1 -> 3; matrix products, arithmetic and copies ran while one was open for 1% -> 0% of each run, Pallas kernels for 16% -> 13%
where the time goes in v16:
time: 65.6 us; the launch traced here: 65.3 us
  blocking collectives  21.5 us (33%)
  starting transfers between devices  21.1 us (32%)
  Pallas kernels  11.7 us (18%)
  waiting for transfers between devices  8.81 us (13%)
  local copies, waits for them, and re-layouts  1.36 us (2%)
  between operations  0.84 us (1%)
    all_to_all x1, blocking collectives, per_device(): mine = lax.all_to_all(shares, SAME, 0, 0)  21.5 us
    ppermute x3, starting transfers between devices, crossed(): return lax.ppermute(value, SPACE, pairs + [(m, n) for n, m in pairs])  9.97 us
    ppermute x3, waiting for transfers between devices, crossed(): return lax.ppermute(value, SPACE, pairs + [(m, n) for n, m in pairs])  8.79 us
    all_to_all x1, starting transfers between devices, per_device(): parts = lax.all_to_all(parts, SAME, 0, 0)  6.88 us
    ppermute x7, starting transfers between devices, swapped(): return lax.ppermute(value, axis, [(0, 1), (1, 0)])  4.2 us
    pallas_call x1, Pallas kernels, first_part(): vmem_call(first_kernel, (jax.ShapeDtypeStruct(((length + 2) * 3 * c1, wid...  2.55 us
    pallas_call x1, Pallas kernels, input_part(): vmem_call(input_kernel, (jax.ShapeDtypeStruct(plane, F32), jax.ShapeDtype...  1.75 us
    pallas_call x1, Pallas kernels, finish(): pl.pallas_call(lambda *refs: finish_kernel(sizes, height, padded, *refs),...  1.38 us
  transfers between devices with their start and end apart: 11, of which 3 were waited for; matrix products, arithmetic and copies ran while one was open for 0% of the time, Pallas kernels for 13%

profile of v16, /device:TPU:1, one launch (start us, length us, event | category | flops | bytes accessed | tf_op | source)
XLA Modules:
  0.0 65.3 jit_solution(4980690179627335258)
XLA Ops:
  0.6 0.0 copy-start
  0.7 0.0 copy-start.1
  0.7 1.2 %copy-done.1 = bf16[1,1,32,64,128]{4,3,2,1,0:T(8,128)(2,1)S(1)} copy-done((bf16[1,1,32,64,128]{4,3,2,1,0:T(8,128)(2,1)S(1)}, bf16[1,1,32,64,128]{4,3,2,1,0:T(8,128)(2,1)}, u32[]{:S(2)}) %copy-start.1) | copy-done | bytes 524312
  1.8 0.0 copy-start.3
  1.8 0.8 %shard_map.93.refs_0_.pack_0 = bf16[2112,128]{1,0:T(8,128)(2,1)S(1)} custom-call(bf16[32,64,128]{2,1,0:T(8,128)(2,1)S(1)} %bitcast.10), custom_call_target="tpu_custom_call" | custom-call | bytes 67108864 | tf_op jit(solution)/shard_map/pallas_call | solution.py:64
  2.6 0.0 copy-done
  2.7 0.1 dynamic-slice_convert_fusion
  2.7 0.0 copy-start.2
  2.7 0.0 copy-start.4
  2.8 0.0 copy-start.5
  2.8 0.1 constant_dynamic-slice_fusion.own
  2.9 4.7 %collective-permute-start.5 = (bf16[2112,128]{1,0:T(8,128)(2,1)S(1)}, bf16[2112,128]{1,0:T(8,128)(2,1)S(1)}, u32[]{:S(2)}, u32[]{:S(2)}) collective-permute-start(bf16[2112,128]{1,0:T(8,128)(2,1)S(1)} %shard_map.93.refs_0_.pack_0), channel_id=1, source_target_pairs={{1,2},{2,1},{5,6},{6,5},{9,10},{10,9},{13,14},{14,13},{17,18},{18,... | collective-permute-start | bytes 1622024 | tf_op jit(solution)/shard_map/ppermute | solution.py:507
  7.5 0.1 collective-permute-start.4
  7.6 0.5 collective-permute-start
  8.1 0.0 copy-done.3
  8.1 0.5 shard_map.95.pack_0
  8.6 1.9 %collective-permute-start.3 = (bf16[1056,128]{1,0:T(8,128)(2,1)S(1)}, bf16[1056,128]{1,0:T(8,128)(2,1)S(1)}, u32[]{:S(2)}, u32[]{:S(2)}) collective-permute-start(bf16[1056,128]{1,0:T(8,128)(2,1)S(1)} %shard_map.95.pack_0), channel_id=1, source_target_pairs={{1,2},{2,1},{5,6},{6,5},{9,10},{10,9},{13,14},{14,13},{17,18},{18,... | collective-permute-start | bytes 811016 | tf_op jit(solution)/shard_map/ppermute | solution.py:507
  10.5 0.1 collective-permute-start.2
  10.6 0.0 collective-permute-done.other
  10.6 0.1 shard_map.94
  10.7 1.3 %collective-permute-start.1 = (bf16[1024,128]{1,0:T(8,128)(2,1)S(1)}, bf16[1024,128]{1,0:T(8,128)(2,1)S(1)}, u32[]{:S(2)}, u32[]{:S(2)}) collective-permute-start(bf16[1024,128]{1,0:T(8,128)(2,1)S(1)} %get-tuple-element.42), channel_id=1, source_target_pairs={{0,4},{4,0},{1,5},{5,1},{2,6},{6,2},{3,7},{7,3},{8,12},{12,8},{9,1... | collective-permute-start | bytes 786440 | tf_op jit(solution)/shard_map/ppermute | solution.py:145
  12.0 0.0 copy-done.2
  12.0 0.0 copy-done.4
  12.0 0.0 copy-done.5
  12.0 0.9 %shard_map.96 = (bf16[2048,128]{1,0:T(8,128)(2,1)S(1)}, bf16[96,288]{1,0:T(8,128)(2,1)S(1)}, bf16[48,288]{1,0:T(8,128)(2,1)S(1)}) custom-call(bf16[32,64,128]{2,1,0:T(8,128)(2,1)S(1)} %bitcast.11, bf16[3,3,3,32,32]{4,3,2,1,0:T(8,128)(2,1)S(1)} %copy-done.4, bf16[3,3,3,16,32]{4,3,2,1,0:T(8,128)(2,1)S(1)} %copy-done.5), custom_call_target="tpu_custom_call" | custom-call | bytes 4194304 | tf_op jit(solution)/shard_map/pallas_call | solution.py:200
  12.9 1.9 %collective-permute-done.5.pack_out = bf16[2112,128]{1,0:T(8,128)(2,1)S(1)} collective-permute-done((bf16[2112,128]{1,0:T(8,128)(2,1)S(1)}, bf16[2112,128]{1,0:T(8,128)(2,1)S(1)}, u32[]{:S(2)}, u32[]{:S(2)}) %collective-permute-start.5) | collective-permute-done | bytes 540704 | tf_op jit(solution)/shard_map/ppermute | solution.py:507
  14.8 0.0 collective-permute-done.4.pack_in
  14.9 2.5 %shard_map.97 = (bf16[6336,128]{1,0:T(8,128)(2,1)S(1)}, f32[288,128]{1,0:T(8,128)S(1)}) custom-call(bf16[2112,128]{1,0:T(8,128)(2,1)S(1)} %collective-permute-done.4.pack_in, bf16[2112,128]{1,0:T(8,128)(2,1)S(1)} %shard_map.93.refs_0_.pack_0, bf16[2112,128]{1,0:T(8,128)(2,1)S(1)} %collective-permute-done.5.pack_out, ...), custom_call_target="tpu_custom_call" | custom-call | flops 1000000000 | bytes 20971520 | tf_op jit(solution)/shard_map/pallas_call | solution.py:308
  17.4 0.3 collective-permute-done.3.pack_out
  17.7 0.0 collective-permute-done.2.pack_in
  17.7 0.8 %shard_map.98 = (bf16[256,128]{1,0:T(8,128)(2,1)S(1)}, f32[256,128]{1,0:T(8,128)S(1)}) custom-call(bf16[1056,128]{1,0:T(8,128)(2,1)S(1)} %collective-permute-done.2.pack_in, bf16[1056,128]{1,0:T(8,128)(2,1)S(1)} %shard_map.95.pack_0, bf16[1056,128]{1,0:T(8,128)(2,1)S(1)} %collective-permute-done.3.pack_out, bf16[6336,128]{1,0:T(8,128)(2,1)S(1)} %get-tuple-element.47.pres, ...), custom_call_target="tpu_custom_call" | custom-call | flops 1000000000 | bytes 5242880 | tf_op jit(solution)/shard_map/pallas_call | solution.py:322
  18.6 0.1 collective-permute-start.6
  18.6 1.7 %shard_map.100 = (f32[1024,128]{1,0:T(8,128)S(1)}, bf16[1024,128]{1,0:T(8,128)(2,1)}, bf16[1024,128]{1,0:T(8,128)(2,1)S(1)}) custom-call(bf16[6336,128]{1,0:T(8,128)(2,1)S(1)} %get-tuple-element.47.pres, bf16[48,288]{1,0:T(8,128)(2,1)S(1)} %get-tuple-element.51.w_one), custom_call_target="tpu_custom_call" | custom-call | flops 1000000000 | bytes 5242880 | tf_op jit(solution)/shard_map/pallas_call | solution.py:336
  20.4 0.0 copy-start.6
  20.4 0.0 collective-permute-done.6.more
  20.4 0.0 collective-permute-done.1.other
  20.4 0.8 %shard_map.99 = bf16[16,80,128]{2,1,0:T(8,128)(2,1)} custom-call(f32[1024,128]{1,0:T(8,128)S(1)} %get-tuple-element.41.keep, bf16[1024,128]{1,0:T(8,128)(2,1)S(1)} %collective-permute-done.1.other, f32[256,128]{1,0:T(8,128)S(1)} %get-tuple-element.49.terms, bf16[256,128]{1,0:T(8,128)(2,1)S(1)} %collective-permute-done.6.more), custom_call_target="tpu_custom_call" | custom-call | bytes 1048576 | tf_op jit(solution)/shard_map/pallas_call | solution.py:130
  21.2 0.0 copy-done.6
  21.2 6.9 %all-to-all-start = ((bf16[16,80,128]{2,1,0:T(8,128)(2,1)}), bf16[16,80,128]{2,1,0:T(8,128)(2,1)S(1)}, u32[]{:S(2)}, u32[]{:S(2)}) async-start(bf16[16,80,128]{2,1,0:T(8,128)(2,1)} %shard_map.99), calls=%async_computation | async-start | bytes 655360 | tf_op jit(solution)/shard_map/all_to_all | solution.py:536
  28.1 0.4 collective-permute-start.7
  28.5 3.4 %collective-permute-start.8 = (bf16[1024,128]{1,0:T(8,128)(2,1)}, bf16[1024,128]{1,0:T(8,128)(2,1)S(1)}, u32[]{:S(2)}, u32[]{:S(2)}) collective-permute-start(bf16[1024,128]{1,0:T(8,128)(2,1)} %copy-done.6), channel_id=1, source_target_pairs={{1,2},{2,1},{5,6},{6,5},{9,10},{10,9},{13,14},{14,13},{17,18},{18,... | collective-permute-start | bytes 786440 | tf_op jit(solution)/shard_map/ppermute | solution.py:507
  31.9 0.0 collective-permute-done.7.first
  31.9 6.5 %collective-permute-done.8.second = bf16[1024,128]{1,0:T(8,128)(2,1)S(1)} collective-permute-done((bf16[1024,128]{1,0:T(8,128)(2,1)}, bf16[1024,128]{1,0:T(8,128)(2,1)S(1)}, u32[]{:S(2)}, u32[]{:S(2)}) %collective-permute-start.8) | collective-permute-done | bytes 262176 | tf_op jit(solution)/shard_map/ppermute | solution.py:507
  38.4 0.0 all-to-all-done.refs_0_
  38.4 0.1 shard_map.101
  38.5 21.5 %all_to_all.10.refs_0_ = bf16[16,144,128]{2,1,0:T(8,128)(2,1)S(1)} all-to-all(bf16[16,144,128]{2,1,0:T(8,128)(2,1)S(1)} %shard_map.101), channel_id=1, replica_groups=mesh['z'=4,'x'=2,'y'=2,'core'=2] {'x','z','y'}, dimensions={0} | all-to-all | bytes 1179648 | tf_op jit(solution)/shard_map/all_to_all | solution.py:541
  60.1 1.9 %collective-permute-start.9 = (bf16[16,144,128]{2,1,0:T(8,128)(2,1)S(1)}, bf16[16,144,128]{2,1,0:T(8,128)(2,1)S(1)}, u32[]{:S(2)}, u32[]{:S(2)}) collective-permute-start(bf16[16,144,128]{2,1,0:T(8,128)(2,1)S(1)} %all_to_all.10.refs_0_), channel_id=1, source_target_pairs={{0,1},{1,0},{2,3},{3,2},{4,5},{5,4},{6,7},{7,6},{8,9},{9,8},{10,11... | collective-permute-start | bytes 1769480 | tf_op jit(solution)/shard_map/ppermute | solution.py:145
  61.9 1.0 %shard_map.102 = bf16[16,64,128]{2,1,0:T(8,128)(2,1)} custom-call(f32[1024,128]{1,0:T(8,128)S(1)} %get-tuple-element.59.own, bf16[1024,128]{1,0:T(8,128)(2,1)S(1)} %collective-permute-done.7.first, bf16[1024,128]{1,0:T(8,128)(2,1)S(1)} %collective-permute-done.8.second), custom_call_target="tpu_custom_call" | custom-call | flops 262144 | bytes 1048576 | tf_op jit(solution)/shard_map/pallas_call | solution.py:366
  62.9 1.0 %shard_map.103.refs_2_ = f32[4096,128]{1,0:T(8,128)} custom-call(bf16[16,144,128]{2,1,0:T(8,128)(2,1)S(1)} %all_to_all.10.refs_0_), custom_call_target="tpu_custom_call" | custom-call | tf_op jit(solution)/shard_map/pallas_call | solution.py:476
  63.9 0.0 collective-permute-done.9.refs_1_
  63.9 1.4 %shard_map.104 = (f32[4096,128]{1,0:T(8,128)}, f32[432,32]{1,0:T(8,128)}, f32[864,32]{1,0:T(8,128)}) custom-call(bf16[16,144,128]{2,1,0:T(8,128)(2,1)S(1)} %all_to_all.10.refs_0_, bf16[16,144,128]{2,1,0:T(8,128)(2,1)S(1)} %collective-permute-done.9.refs_1_, f32[4096,128]{1,0:T(8,128)} %shard_map.103.refs_2_), custom_call_target="tpu_custom_call", output_to_operand_aliasing={{0}: (2, {})} | custom-call | tf_op jit(solution)/shard_map/pallas_call | solution.py:484
Async XLA Ops:
  0.6 2.0 %copy-start = (f32[1,524288]{1,0:T(1,128)S(1)}, f32[1,524288]{1,0:T(1,128)}, u32[]{:S(2)}) copy-start(f32[1,524288]{1,0:T(1,128)} %param.11) | copy-start | bytes 6291460
  0.7 1.2 %copy-start.1 = (bf16[1,1,32,64,128]{4,3,2,1,0:T(8,128)(2,1)S(1)}, bf16[1,1,32,64,128]{4,3,2,1,0:T(8,128)(2,1)}, u32[]{:S(2)}) copy-start(bf16[1,1,32,64,128]{4,3,2,1,0:T(8,128)(2,1)} %param.8) | copy-start | bytes 1572868
  1.8 6.3 %copy-start.3 = (bf16[1,1,16,64,128]{4,3,2,1,0:T(8,128)(2,1)S(1)}, bf16[1,1,16,64,128]{4,3,2,1,0:T(8,128)(2,1)}, u32[]{:S(2)}) copy-start(bf16[1,1,16,64,128]{4,3,2,1,0:T(8,128)(2,1)} %param.6) | copy-start | bytes 786436
  2.7 9.3 %copy-start.2 = (bf16[1,1,32,64,128]{4,3,2,1,0:T(8,128)(2,1)S(1)}, bf16[1,1,32,64,128]{4,3,2,1,0:T(8,128)(2,1)}, u32[]{:S(2)}) copy-start(bf16[1,1,32,64,128]{4,3,2,1,0:T(8,128)(2,1)} %param.7) | copy-start | bytes 1572868
  2.7 9.3 %copy-start.4 = (bf16[3,3,3,32,32]{4,3,2,1,0:T(8,128)(2,1)S(1)}, bf16[3,3,3,32,32]{4,3,2,1,0:T(8,128)(2,1)}, u32[]{:S(2)}) copy-start(bf16[3,3,3,32,32]{4,3,2,1,0:T(8,128)(2,1)} %two.1) | copy-start | bytes 165892
  2.8 9.3 %copy-start.5 = (bf16[3,3,3,16,32]{4,3,2,1,0:T(8,128)(2,1)S(1)}, bf16[3,3,3,16,32]{4,3,2,1,0:T(8,128)(2,1)}, u32[]{:S(2)}) copy-start(bf16[3,3,3,16,32]{4,3,2,1,0:T(8,128)(2,1)} %one.1) | copy-start | bytes 82948
  2.9 12.0 %collective-permute-start.5 = (bf16[2112,128]{1,0:T(8,128)(2,1)S(1)}, bf16[2112,128]{1,0:T(8,128)(2,1)S(1)}, u32[]{:S(2)}, u32[]{:S(2)}) collective-permute-start(bf16[2112,128]{1,0:T(8,128)(2,1)S(1)} %shard_map.93.refs_0_.pack_0), channel_id=1, source_target_pairs={{1,2},{2,1},{5,6},{6,5},{9,10},{10,9},{13,14},{14,13},{17,18},{18,... | collective-permute-start | bytes 1622024 | tf_op jit(solution)/shard_map/ppermute | solution.py:507
  7.5 7.3 %collective-permute-start.4 = (bf16[2112,128]{1,0:T(8,128)(2,1)S(1)}, bf16[2112,128]{1,0:T(8,128)(2,1)S(1)}, u32[]{:S(2)}, u32[]{:S(2)}) collective-permute-start(bf16[2112,128]{1,0:T(8,128)(2,1)S(1)} %shard_map.93.refs_0_.pack_0), channel_id=1, source_target_pairs={{0,1},{1,0},{2,3},{3,2},{4,5},{5,4},{6,7},{7,6},{8,9},{9,8},{10,11... | collective-permute-start | bytes 1622024 | tf_op jit(solution)/shard_map/ppermute | solution.py:145
  7.6 3.0 %collective-permute-start = (bf16[2048,128]{1,0:T(8,128)(2,1)S(1)}, bf16[2048,128]{1,0:T(8,128)(2,1)S(1)}, u32[]{:S(2)}, u32[]{:S(2)}) collective-permute-start(bf16[2048,128]{1,0:T(8,128)(2,1)S(1)} %dynamic-slice_convert_fusion), channel_id=1, source_target_pairs={{0,1},{1,0},{2,3},{3,2},{4,5},{5,4},{6,7},{7,6},{8,9},{9,8},{10,11... | collective-permute-start | bytes 1572872 | tf_op jit(solution)/shard_map/ppermute | solution.py:145
  8.6 9.2 %collective-permute-start.3 = (bf16[1056,128]{1,0:T(8,128)(2,1)S(1)}, bf16[1056,128]{1,0:T(8,128)(2,1)S(1)}, u32[]{:S(2)}, u32[]{:S(2)}) collective-permute-start(bf16[1056,128]{1,0:T(8,128)(2,1)S(1)} %shard_map.95.pack_0), channel_id=1, source_target_pairs={{1,2},{2,1},{5,6},{6,5},{9,10},{10,9},{13,14},{14,13},{17,18},{18,... | collective-permute-start | bytes 811016 | tf_op jit(solution)/shard_map/ppermute | solution.py:507
  10.5 7.2 %collective-permute-start.2 = (bf16[1056,128]{1,0:T(8,128)(2,1)S(1)}, bf16[1056,128]{1,0:T(8,128)(2,1)S(1)}, u32[]{:S(2)}, u32[]{:S(2)}) collective-permute-start(bf16[1056,128]{1,0:T(8,128)(2,1)S(1)} %shard_map.95.pack_0), channel_id=1, source_target_pairs={{0,1},{1,0},{2,3},{3,2},{4,5},{5,4},{6,7},{7,6},{8,9},{9,8},{10,11... | collective-permute-start | bytes 811016 | tf_op jit(solution)/shard_map/ppermute | solution.py:145
  10.7 9.7 %collective-permute-start.1 = (bf16[1024,128]{1,0:T(8,128)(2,1)S(1)}, bf16[1024,128]{1,0:T(8,128)(2,1)S(1)}, u32[]{:S(2)}, u32[]{:S(2)}) collective-permute-start(bf16[1024,128]{1,0:T(8,128)(2,1)S(1)} %get-tuple-element.42), channel_id=1, source_target_pairs={{0,4},{4,0},{1,5},{5,1},{2,6},{6,2},{3,7},{7,3},{8,12},{12,8},{9,1... | collective-permute-start | bytes 786440 | tf_op jit(solution)/shard_map/ppermute | solution.py:145
  18.6 1.8 %collective-permute-start.6 = (bf16[256,128]{1,0:T(8,128)(2,1)S(1)}, bf16[256,128]{1,0:T(8,128)(2,1)S(1)}, u32[]{:S(2)}, u32[]{:S(2)}) collective-permute-start(bf16[256,128]{1,0:T(8,128)(2,1)S(1)} %get-tuple-element.50), channel_id=1, source_target_pairs={{0,1},{1,0},{2,3},{3,2},{4,5},{5,4},{6,7},{7,6},{8,9},{9,8},{10,11... | collective-permute-start | bytes 196616 | tf_op jit(solution)/shard_map/ppermute | solution.py:145
  20.4 0.8 %copy-start.6 = (bf16[1024,128]{1,0:T(8,128)(2,1)}, bf16[1024,128]{1,0:T(8,128)(2,1)S(1)}, u32[]{:S(2)}) copy-start(bf16[1024,128]{1,0:T(8,128)(2,1)S(1)} %get-tuple-element.56) | copy-start | bytes 786436
  21.2 17.2 %all-to-all-start = ((bf16[16,80,128]{2,1,0:T(8,128)(2,1)}), bf16[16,80,128]{2,1,0:T(8,128)(2,1)S(1)}, u32[]{:S(2)}, u32[]{:S(2)}) async-start(bf16[16,80,128]{2,1,0:T(8,128)(2,1)} %shard_map.99), calls=%async_computation | async-start | bytes 655360 | tf_op jit(solution)/shard_map/all_to_all | solution.py:536
  28.1 3.8 %collective-permute-start.7 = (bf16[1024,128]{1,0:T(8,128)(2,1)}, bf16[1024,128]{1,0:T(8,128)(2,1)S(1)}, u32[]{:S(2)}, u32[]{:S(2)}) collective-permute-start(bf16[1024,128]{1,0:T(8,128)(2,1)} %get-tuple-element.55), channel_id=1, source_target_pairs={{0,1},{1,0},{2,3},{3,2},{4,5},{5,4},{6,7},{7,6},{8,9},{9,8},{10,11... | collective-permute-start | bytes 786440 | tf_op jit(solution)/shard_map/ppermute | solution.py:145
  28.5 9.9 %collective-permute-start.8 = (bf16[1024,128]{1,0:T(8,128)(2,1)}, bf16[1024,128]{1,0:T(8,128)(2,1)S(1)}, u32[]{:S(2)}, u32[]{:S(2)}) collective-permute-start(bf16[1024,128]{1,0:T(8,128)(2,1)} %copy-done.6), channel_id=1, source_target_pairs={{1,2},{2,1},{5,6},{6,5},{9,10},{10,9},{13,14},{14,13},{17,18},{18,... | collective-permute-start | bytes 786440 | tf_op jit(solution)/shard_map/ppermute | solution.py:507
  60.1 3.8 %collective-permute-start.9 = (bf16[16,144,128]{2,1,0:T(8,128)(2,1)S(1)}, bf16[16,144,128]{2,1,0:T(8,128)(2,1)S(1)}, u32[]{:S(2)}, u32[]{:S(2)}) collective-permute-start(bf16[16,144,128]{2,1,0:T(8,128)(2,1)S(1)} %all_to_all.10.refs_0_), channel_id=1, source_target_pairs={{0,1},{1,0},{2,3},{3,2},{4,5},{5,4},{6,7},{7,6},{8,9},{9,8},{10,11... | collective-permute-start | bytes 1769480 | tf_op jit(solution)/shard_map/ppermute | solution.py:145

commit v17 on v16

--- a/solution.py
+++ b/solution.py
@@ -534,12 +534,13 @@
     parts = combine(near, far, keep, swapped(send), copies)
     parts, inner, outer = lax.optimization_barrier((parts, inner, outer))
     parts = lax.all_to_all(parts, SAME, 0, 0)
-    parts, inner, outer = lax.optimization_barrier((parts, swapped(inner), crossed(outer)))
     cells = volume_in.shape[3] * volume_in.shape[4] * devices
     shares = share(parts, rows // devices, 1.0 / math.sqrt(cells))
 
+    shares, inner, outer = lax.optimization_barrier((shares, inner, outer))
     mine = lax.all_to_all(shares, SAME, 0, 0)
-    mine, own = lax.optimization_barrier((mine, own))
+    inner, outer = (swapped(inner), crossed(outer))
+    mine, own, inner, outer = lax.optimization_barrier((mine, own, inner, outer))
     grad_input = merge(own, inner, outer, volume_in.shape[2:])
     bucket_sum, total_one, total_two = finish(mine, swapped(mine), length, (c0, c1, c2))
     return (

time: 65.6 us -> 63.9 us (0.974)
  blocking collectives: 21.5 us -> 16.4 us
  waiting for transfers between devices: 8.81 us -> 11.7 us
  local copies, waits for them, and re-layouts: 1.36 us -> 3.02 us
  starting transfers between devices: 21.1 us -> 20.4 us
    all_to_all x1, blocking collectives: 21.5 us -> 16.4 us  [per_device(): parts = lax.all_to_all(parts, SAME, 0, 0)]
    all_to_all x1, starting transfers between devices: 6.88 us -> 4.25 us  [per_device(): mine = lax.all_to_all(shares, SAME, 0, 0)]
    all_to_all x1, waiting for transfers between devices: 0.01 us -> 2.42 us  [per_device(): mine = lax.all_to_all(shares, SAME, 0, 0)]
    ppermute x7, starting transfers between devices: 4.2 us -> 6.32 us  [swapped(): return lax.ppermute(value, axis, [(0, 1), (1, 0)])]
    unnamed x14 -> x20, local copies, waits for them, and re-layouts: 1.22 us -> 2.88 us
    pallas_call x1, Pallas kernels: 0.13 us -> 0.95 us  [share(): vmem_call(lambda *refs: share_kernel(scale, *refs), jax.ShapeDtypeStruct(...]
    pallas_call x1, Pallas kernels: 0.8 us -> 0.08 us  [combine(): vmem_call(combine_kernel, jax.ShapeDtypeStruct((parts, rows, LANES), BF16...]
    pallas_call x1, Pallas kernels: 1.75 us -> 1.05 us  [input_part(): vmem_call(input_kernel, (jax.ShapeDtypeStruct(plane, F32), jax.ShapeDtype...]
  transfers between devices with their start and end apart: 11 -> 11, of which waited for: 3 -> 5; matrix products, arithmetic and copies ran while one was open for 0% -> 0% of each run, Pallas kernels for 13% -> 12%
where the time goes in v17:
time: 63.9 us; the launch traced here: 63.6 us
  starting transfers between devices  20.4 us (32%)
  blocking collectives  16.4 us (26%)
  waiting for transfers between devices  11.7 us (18%)
  Pallas kernels  11.1 us (17%)
  local copies, waits for them, and re-layouts  3.02 us (5%)
  between operations  0.86 us (1%)
    all_to_all x1, blocking collectives, per_device(): parts = lax.all_to_all(parts, SAME, 0, 0)  16.4 us
    ppermute x3, starting transfers between devices, crossed(): return lax.ppermute(value, SPACE, pairs + [(m, n) for n, m in pairs])  9.85 us
    ppermute x3, waiting for transfers between devices, crossed(): return lax.ppermute(value, SPACE, pairs + [(m, n) for n, m in pairs])  9.13 us
    ppermute x7, starting transfers between devices, swapped(): return lax.ppermute(value, axis, [(0, 1), (1, 0)])  6.32 us
    all_to_all x1, starting transfers between devices, per_device(): mine = lax.all_to_all(shares, SAME, 0, 0)  4.25 us
    unnamed x20, local copies, waits for them, and re-layouts  2.88 us
    pallas_call x1, Pallas kernels, first_part(): vmem_call(first_kernel, (jax.ShapeDtypeStruct(((length + 2) * 3 * c1, wid...  2.55 us
    all_to_all x1, waiting for transfers between devices, per_device(): mine = lax.all_to_all(shares, SAME, 0, 0)  2.42 us
  transfers between devices with their start and end apart: 11, of which 5 were waited for; matrix products, arithmetic and copies ran while one was open for 0% of the time, Pallas kernels for 12%

profile of v17, /device:TPU:1, one launch (start us, length us, event | category | flops | bytes accessed | tf_op | source)
XLA Modules:
  0.0 63.6 jit_solution(5621779648310340318)
XLA Ops:
  0.6 0.0 copy-start
  0.7 0.0 copy-start.1
  0.7 1.2 %copy-done.1 = bf16[1,1,32,64,128]{4,3,2,1,0:T(8,128)(2,1)S(1)} copy-done((bf16[1,1,32,64,128]{4,3,2,1,0:T(8,128)(2,1)S(1)}, bf16[1,1,32,64,128]{4,3,2,1,0:T(8,128)(2,1)}, u32[]{:S(2)}) %copy-start.1) | copy-done | bytes 524312
  1.8 0.0 copy-start.5
  1.8 0.8 %shard_map.93.refs_0_.pack_0 = bf16[2112,128]{1,0:T(8,128)(2,1)S(1)} custom-call(bf16[32,64,128]{2,1,0:T(8,128)(2,1)S(1)} %bitcast.10), custom_call_target="tpu_custom_call" | custom-call | bytes 67108864 | tf_op jit(solution)/shard_map/pallas_call | solution.py:64
  2.6 0.0 copy-done
  2.7 0.1 dynamic-slice_convert_fusion
  2.7 0.0 copy-start.2
  2.7 0.0 copy-start.6
  2.8 0.0 copy-start.7
  2.8 0.1 constant_dynamic-slice_fusion.own
  2.9 4.7 %collective-permute-start.5 = (bf16[2112,128]{1,0:T(8,128)(2,1)S(1)}, bf16[2112,128]{1,0:T(8,128)(2,1)S(1)}, u32[]{:S(2)}, u32[]{:S(2)}) collective-permute-start(bf16[2112,128]{1,0:T(8,128)(2,1)S(1)} %shard_map.93.refs_0_.pack_0), channel_id=1, source_target_pairs={{1,2},{2,1},{5,6},{6,5},{9,10},{10,9},{13,14},{14,13},{17,18},{18,... | collective-permute-start | bytes 1622024 | tf_op jit(solution)/shard_map/ppermute | solution.py:507
  7.5 0.1 collective-permute-start.4
  7.6 0.5 collective-permute-start
  8.1 0.0 copy-done.5
  8.1 0.5 shard_map.95.pack_0
  8.6 1.9 %collective-permute-start.3 = (bf16[1056,128]{1,0:T(8,128)(2,1)S(1)}, bf16[1056,128]{1,0:T(8,128)(2,1)S(1)}, u32[]{:S(2)}, u32[]{:S(2)}) collective-permute-start(bf16[1056,128]{1,0:T(8,128)(2,1)S(1)} %shard_map.95.pack_0), channel_id=1, source_target_pairs={{1,2},{2,1},{5,6},{6,5},{9,10},{10,9},{13,14},{14,13},{17,18},{18,... | collective-permute-start | bytes 811016 | tf_op jit(solution)/shard_map/ppermute | solution.py:507
  10.5 0.1 collective-permute-start.2
  10.6 0.0 collective-permute-done.other
  10.6 0.1 shard_map.94
  10.7 1.3 %collective-permute-start.1 = (bf16[1024,128]{1,0:T(8,128)(2,1)S(1)}, bf16[1024,128]{1,0:T(8,128)(2,1)S(1)}, u32[]{:S(2)}, u32[]{:S(2)}) collective-permute-start(bf16[1024,128]{1,0:T(8,128)(2,1)S(1)} %get-tuple-element.44), channel_id=1, source_target_pairs={{0,4},{4,0},{1,5},{5,1},{2,6},{6,2},{3,7},{7,3},{8,12},{12,8},{9,1... | collective-permute-start | bytes 786440 | tf_op jit(solution)/shard_map/ppermute | solution.py:145
  12.0 0.0 copy-done.2
  12.0 0.0 copy-done.6
  12.0 0.0 copy-done.7
  12.0 0.9 %shard_map.96 = (bf16[2048,128]{1,0:T(8,128)(2,1)S(1)}, bf16[96,288]{1,0:T(8,128)(2,1)S(1)}, bf16[48,288]{1,0:T(8,128)(2,1)S(1)}) custom-call(bf16[32,64,128]{2,1,0:T(8,128)(2,1)S(1)} %bitcast.11, bf16[3,3,3,32,32]{4,3,2,1,0:T(8,128)(2,1)S(1)} %copy-done.6, bf16[3,3,3,16,32]{4,3,2,1,0:T(8,128)(2,1)S(1)} %copy-done.7), custom_call_target="tpu_custom_call" | custom-call | bytes 4194304 | tf_op jit(solution)/shard_map/pallas_call | solution.py:200
  12.9 1.9 %collective-permute-done.5.pack_out = bf16[2112,128]{1,0:T(8,128)(2,1)S(1)} collective-permute-done((bf16[2112,128]{1,0:T(8,128)(2,1)S(1)}, bf16[2112,128]{1,0:T(8,128)(2,1)S(1)}, u32[]{:S(2)}, u32[]{:S(2)}) %collective-permute-start.5) | collective-permute-done | bytes 540704 | tf_op jit(solution)/shard_map/ppermute | solution.py:507
  14.8 0.0 collective-permute-done.4.pack_in
  14.9 2.5 %shard_map.97 = (bf16[6336,128]{1,0:T(8,128)(2,1)S(1)}, f32[288,128]{1,0:T(8,128)S(1)}) custom-call(bf16[2112,128]{1,0:T(8,128)(2,1)S(1)} %collective-permute-done.4.pack_in, bf16[2112,128]{1,0:T(8,128)(2,1)S(1)} %shard_map.93.refs_0_.pack_0, bf16[2112,128]{1,0:T(8,128)(2,1)S(1)} %collective-permute-done.5.pack_out, ...), custom_call_target="tpu_custom_call" | custom-call | flops 1000000000 | bytes 20971520 | tf_op jit(solution)/shard_map/pallas_call | solution.py:308
  17.4 0.3 collective-permute-done.3.pack_out
  17.7 0.0 collective-permute-done.2.pack_in
  17.7 0.8 %shard_map.98 = (bf16[256,128]{1,0:T(8,128)(2,1)S(1)}, f32[256,128]{1,0:T(8,128)S(1)}) custom-call(bf16[1056,128]{1,0:T(8,128)(2,1)S(1)} %collective-permute-done.2.pack_in, bf16[1056,128]{1,0:T(8,128)(2,1)S(1)} %shard_map.95.pack_0, bf16[1056,128]{1,0:T(8,128)(2,1)S(1)} %collective-permute-done.3.pack_out, bf16[6336,128]{1,0:T(8,128)(2,1)S(1)} %get-tuple-element.49.pres, ...), custom_call_target="tpu_custom_call" | custom-call | flops 1000000000 | bytes 5242880 | tf_op jit(solution)/shard_map/pallas_call | solution.py:322
  18.6 0.1 collective-permute-start.6
  18.6 1.1 %shard_map.100 = (f32[1024,128]{1,0:T(8,128)S(1)}, bf16[1024,128]{1,0:T(8,128)(2,1)S(1)}, bf16[1024,128]{1,0:T(8,128)(2,1)S(1)}) custom-call(bf16[6336,128]{1,0:T(8,128)(2,1)S(1)} %get-tuple-element.49.pres, bf16[48,288]{1,0:T(8,128)(2,1)S(1)} %get-tuple-element.53.w_one), custom_call_target="tpu_custom_call" | custom-call | flops 1000000000 | bytes 5242880 | tf_op jit(solution)/shard_map/pallas_call | solution.py:336
  19.7 0.0 copy-start.8
  19.7 0.0 copy-start.9
  19.7 0.2 collective-permute-done.6.more
  19.9 0.0 collective-permute-done.1.other
  19.9 0.1 shard_map.99
  20.0 16.4 %all_to_all.10.refs_0_ = bf16[16,80,128]{2,1,0:T(8,128)(2,1)S(1)} all-to-all(bf16[16,80,128]{2,1,0:T(8,128)(2,1)S(1)} %shard_map.99), channel_id=1, replica_groups=mesh['z'=4,'x'=2,'y'=2,'core'=2] {'x','z','y'}, dimensions={0} | all-to-all | bytes 655360 | tf_op jit(solution)/shard_map/all_to_all | solution.py:536
  36.4 0.0 copy-done.8
  36.4 0.0 copy-done.9
  36.4 1.0 %shard_map.101 = bf16[16,144,128]{2,1,0:T(8,128)(2,1)} custom-call(bf16[16,80,128]{2,1,0:T(8,128)(2,1)S(1)} %all_to_all.10.refs_0_), custom_call_target="tpu_custom_call" | custom-call | flops 163840 | bytes 983040 | tf_op jit(solution)/shard_map/pallas_call | solution.py:392
  37.4 4.3 %all-to-all-start.1 = ((bf16[16,144,128]{2,1,0:T(8,128)(2,1)}), bf16[16,144,128]{2,1,0:T(8,128)(2,1)S(1)}, u32[]{:S(2)}, u32[]{:S(2)}) async-start(bf16[16,144,128]{2,1,0:T(8,128)(2,1)} %shard_map.101), calls=%async_computation.1 | async-start | bytes 1179648 | tf_op jit(solution)/shard_map/all_to_all | solution.py:541
  41.6 1.8 %collective-permute-start.7 = (bf16[1024,128]{1,0:T(8,128)(2,1)}, bf16[1024,128]{1,0:T(8,128)(2,1)S(1)}, u32[]{:S(2)}, u32[]{:S(2)}) collective-permute-start(bf16[1024,128]{1,0:T(8,128)(2,1)} %copy-done.9), channel_id=1, source_target_pairs={{0,1},{1,0},{2,3},{3,2},{4,5},{5,4},{6,7},{7,6},{8,9},{9,8},{10,11... | collective-permute-start | bytes 786440 | tf_op jit(solution)/shard_map/ppermute | solution.py:145
  43.4 3.3 %collective-permute-start.8 = (bf16[1024,128]{1,0:T(8,128)(2,1)}, bf16[1024,128]{1,0:T(8,128)(2,1)S(1)}, u32[]{:S(2)}, u32[]{:S(2)}) collective-permute-start(bf16[1024,128]{1,0:T(8,128)(2,1)} %copy-done.8), channel_id=1, source_target_pairs={{1,2},{2,1},{5,6},{6,5},{9,10},{10,9},{13,14},{14,13},{17,18},{18,... | collective-permute-start | bytes 786440 | tf_op jit(solution)/shard_map/ppermute | solution.py:507
  46.7 0.0 collective-permute-done.7.first
  46.7 6.9 %collective-permute-done.8.second = bf16[1024,128]{1,0:T(8,128)(2,1)S(1)} collective-permute-done((bf16[1024,128]{1,0:T(8,128)(2,1)}, bf16[1024,128]{1,0:T(8,128)(2,1)S(1)}, u32[]{:S(2)}, u32[]{:S(2)}) %collective-permute-start.8) | collective-permute-done | bytes 262176 | tf_op jit(solution)/shard_map/ppermute | solution.py:507
  53.6 0.0 copy-start.3
  53.6 0.7 %copy-done.3 = bf16[1024,128]{1,0:T(8,128)(2,1)} copy-done((bf16[1024,128]{1,0:T(8,128)(2,1)}, bf16[1024,128]{1,0:T(8,128)(2,1)S(1)}, u32[]{:S(2)}) %copy-start.3) | copy-done | bytes 262168
  54.3 2.4 %all-to-all-done.1.refs_0_ = bf16[16,144,128]{2,1,0:T(8,128)(2,1)S(1)} async-done(((bf16[16,144,128]{2,1,0:T(8,128)(2,1)}), bf16[16,144,128]{2,1,0:T(8,128)(2,1)S(1)}, u32[]{:S(2)}, u32[]{:S(2)}) %all-to-all-start.1) | async-done | bytes 589856 | tf_op jit(solution)/shard_map/all_to_all | solution.py:541
  56.7 2.6 %collective-permute-start.9 = (bf16[16,144,128]{2,1,0:T(8,128)(2,1)S(1)}, bf16[16,144,128]{2,1,0:T(8,128)(2,1)S(1)}, u32[]{:S(2)}, u32[]{:S(2)}) collective-permute-start(bf16[16,144,128]{2,1,0:T(8,128)(2,1)S(1)} %all-to-all-done.1.refs_0_), channel_id=1, source_target_pairs={{0,1},{1,0},{2,3},{3,2},{4,5},{5,4},{6,7},{7,6},{8,9},{9,8},{10,11... | collective-permute-start | bytes 1769480 | tf_op jit(solution)/shard_map/ppermute | solution.py:145
  59.2 0.0 copy-start.4
  59.2 0.9 %copy-done.4 = bf16[1024,128]{1,0:T(8,128)(2,1)S(1)} copy-done((bf16[1024,128]{1,0:T(8,128)(2,1)S(1)}, bf16[1024,128]{1,0:T(8,128)(2,1)}, u32[]{:S(2)}) %copy-start.4) | copy-done | bytes 262168
  60.2 1.0 %shard_map.102 = bf16[16,64,128]{2,1,0:T(8,128)(2,1)} custom-call(f32[1024,128]{1,0:T(8,128)S(1)} %get-tuple-element.63.own, bf16[1024,128]{1,0:T(8,128)(2,1)S(1)} %collective-permute-done.7.first, bf16[1024,128]{1,0:T(8,128)(2,1)S(1)} %copy-done.4), custom_call_target="tpu_custom_call" | custom-call | flops 262144 | bytes 1048576 | tf_op jit(solution)/shard_map/pallas_call | solution.py:366
  61.1 1.0 %shard_map.103.refs_2_ = f32[4096,128]{1,0:T(8,128)} custom-call(bf16[16,144,128]{2,1,0:T(8,128)(2,1)S(1)} %all-to-all-done.1.refs_0_), custom_call_target="tpu_custom_call" | custom-call | tf_op jit(solution)/shard_map/pallas_call | solution.py:476
  62.2 0.0 collective-permute-done.9.refs_1_
  62.2 1.4 %shard_map.104 = (f32[4096,128]{1,0:T(8,128)}, f32[432,32]{1,0:T(8,128)}, f32[864,32]{1,0:T(8,128)}) custom-call(bf16[16,144,128]{2,1,0:T(8,128)(2,1)S(1)} %all-to-all-done.1.refs_0_, bf16[16,144,128]{2,1,0:T(8,128)(2,1)S(1)} %collective-permute-done.9.refs_1_, f32[4096,128]{1,0:T(8,128)} %shard_map.103.refs_2_), custom_call_target="tpu_custom_call", output_to_operand_aliasing={{0}: (2, {})} | custom-call | tf_op jit(solution)/shard_map/pallas_call | solution.py:484
Async XLA Ops:
  0.6 2.0 %copy-start = (f32[1,524288]{1,0:T(1,128)S(1)}, f32[1,524288]{1,0:T(1,128)}, u32[]{:S(2)}) copy-start(f32[1,524288]{1,0:T(1,128)} %param.11) | copy-start | bytes 6291460
  0.7 1.2 %copy-start.1 = (bf16[1,1,32,64,128]{4,3,2,1,0:T(8,128)(2,1)S(1)}, bf16[1,1,32,64,128]{4,3,2,1,0:T(8,128)(2,1)}, u32[]{:S(2)}) copy-start(bf16[1,1,32,64,128]{4,3,2,1,0:T(8,128)(2,1)} %param.8) | copy-start | bytes 1572868
  1.8 6.3 %copy-start.5 = (bf16[1,1,16,64,128]{4,3,2,1,0:T(8,128)(2,1)S(1)}, bf16[1,1,16,64,128]{4,3,2,1,0:T(8,128)(2,1)}, u32[]{:S(2)}) copy-start(bf16[1,1,16,64,128]{4,3,2,1,0:T(8,128)(2,1)} %param.6) | copy-start | bytes 786436
  2.7 9.3 %copy-start.2 = (bf16[1,1,32,64,128]{4,3,2,1,0:T(8,128)(2,1)S(1)}, bf16[1,1,32,64,128]{4,3,2,1,0:T(8,128)(2,1)}, u32[]{:S(2)}) copy-start(bf16[1,1,32,64,128]{4,3,2,1,0:T(8,128)(2,1)} %param.7) | copy-start | bytes 1572868
  2.7 9.3 %copy-start.6 = (bf16[3,3,3,32,32]{4,3,2,1,0:T(8,128)(2,1)S(1)}, bf16[3,3,3,32,32]{4,3,2,1,0:T(8,128)(2,1)}, u32[]{:S(2)}) copy-start(bf16[3,3,3,32,32]{4,3,2,1,0:T(8,128)(2,1)} %two.1) | copy-start | bytes 165892
  2.8 9.3 %copy-start.7 = (bf16[3,3,3,16,32]{4,3,2,1,0:T(8,128)(2,1)S(1)}, bf16[3,3,3,16,32]{4,3,2,1,0:T(8,128)(2,1)}, u32[]{:S(2)}) copy-start(bf16[3,3,3,16,32]{4,3,2,1,0:T(8,128)(2,1)} %one.1) | copy-start | bytes 82948
  2.9 12.0 %collective-permute-start.5 = (bf16[2112,128]{1,0:T(8,128)(2,1)S(1)}, bf16[2112,128]{1,0:T(8,128)(2,1)S(1)}, u32[]{:S(2)}, u32[]{:S(2)}) collective-permute-start(bf16[2112,128]{1,0:T(8,128)(2,1)S(1)} %shard_map.93.refs_0_.pack_0), channel_id=1, source_target_pairs={{1,2},{2,1},{5,6},{6,5},{9,10},{10,9},{13,14},{14,13},{17,18},{18,... | collective-permute-start | bytes 1622024 | tf_op jit(solution)/shard_map/ppermute | solution.py:507
  7.5 7.3 %collective-permute-start.4 = (bf16[2112,128]{1,0:T(8,128)(2,1)S(1)}, bf16[2112,128]{1,0:T(8,128)(2,1)S(1)}, u32[]{:S(2)}, u32[]{:S(2)}) collective-permute-start(bf16[2112,128]{1,0:T(8,128)(2,1)S(1)} %shard_map.93.refs_0_.pack_0), channel_id=1, source_target_pairs={{0,1},{1,0},{2,3},{3,2},{4,5},{5,4},{6,7},{7,6},{8,9},{9,8},{10,11... | collective-permute-start | bytes 1622024 | tf_op jit(solution)/shard_map/ppermute | solution.py:145
  7.6 3.0 %collective-permute-start = (bf16[2048,128]{1,0:T(8,128)(2,1)S(1)}, bf16[2048,128]{1,0:T(8,128)(2,1)S(1)}, u32[]{:S(2)}, u32[]{:S(2)}) collective-permute-start(bf16[2048,128]{1,0:T(8,128)(2,1)S(1)} %dynamic-slice_convert_fusion), channel_id=1, source_target_pairs={{0,1},{1,0},{2,3},{3,2},{4,5},{5,4},{6,7},{7,6},{8,9},{9,8},{10,11... | collective-permute-start | bytes 1572872 | tf_op jit(solution)/shard_map/ppermute | solution.py:145
  8.6 9.2 %collective-permute-start.3 = (bf16[1056,128]{1,0:T(8,128)(2,1)S(1)}, bf16[1056,128]{1,0:T(8,128)(2,1)S(1)}, u32[]{:S(2)}, u32[]{:S(2)}) collective-permute-start(bf16[1056,128]{1,0:T(8,128)(2,1)S(1)} %shard_map.95.pack_0), channel_id=1, source_target_pairs={{1,2},{2,1},{5,6},{6,5},{9,10},{10,9},{13,14},{14,13},{17,18},{18,... | collective-permute-start | bytes 811016 | tf_op jit(solution)/shard_map/ppermute | solution.py:507
  10.5 7.2 %collective-permute-start.2 = (bf16[1056,128]{1,0:T(8,128)(2,1)S(1)}, bf16[1056,128]{1,0:T(8,128)(2,1)S(1)}, u32[]{:S(2)}, u32[]{:S(2)}) collective-permute-start(bf16[1056,128]{1,0:T(8,128)(2,1)S(1)} %shard_map.95.pack_0), channel_id=1, source_target_pairs={{0,1},{1,0},{2,3},{3,2},{4,5},{5,4},{6,7},{7,6},{8,9},{9,8},{10,11... | collective-permute-start | bytes 811016 | tf_op jit(solution)/shard_map/ppermute | solution.py:145
  10.7 9.2 %collective-permute-start.1 = (bf16[1024,128]{1,0:T(8,128)(2,1)S(1)}, bf16[1024,128]{1,0:T(8,128)(2,1)S(1)}, u32[]{:S(2)}, u32[]{:S(2)}) collective-permute-start(bf16[1024,128]{1,0:T(8,128)(2,1)S(1)} %get-tuple-element.44), channel_id=1, source_target_pairs={{0,4},{4,0},{1,5},{5,1},{2,6},{6,2},{3,7},{7,3},{8,12},{12,8},{9,1... | collective-permute-start | bytes 786440 | tf_op jit(solution)/shard_map/ppermute | solution.py:145
  18.6 1.3 %collective-permute-start.6 = (bf16[256,128]{1,0:T(8,128)(2,1)S(1)}, bf16[256,128]{1,0:T(8,128)(2,1)S(1)}, u32[]{:S(2)}, u32[]{:S(2)}) collective-permute-start(bf16[256,128]{1,0:T(8,128)(2,1)S(1)} %get-tuple-element.52), channel_id=1, source_target_pairs={{0,1},{1,0},{2,3},{3,2},{4,5},{5,4},{6,7},{7,6},{8,9},{9,8},{10,11... | collective-permute-start | bytes 196616 | tf_op jit(solution)/shard_map/ppermute | solution.py:145
  19.7 16.7 %copy-start.8 = (bf16[1024,128]{1,0:T(8,128)(2,1)}, bf16[1024,128]{1,0:T(8,128)(2,1)S(1)}, u32[]{:S(2)}) copy-start(bf16[1024,128]{1,0:T(8,128)(2,1)S(1)} %get-tuple-element.62) | copy-start | bytes 786436
  19.7 16.7 %copy-start.9 = (bf16[1024,128]{1,0:T(8,128)(2,1)}, bf16[1024,128]{1,0:T(8,128)(2,1)S(1)}, u32[]{:S(2)}) copy-start(bf16[1024,128]{1,0:T(8,128)(2,1)S(1)} %get-tuple-element.61) | copy-start | bytes 786436
  37.4 19.3 %all-to-all-start.1 = ((bf16[16,144,128]{2,1,0:T(8,128)(2,1)}), bf16[16,144,128]{2,1,0:T(8,128)(2,1)S(1)}, u32[]{:S(2)}, u32[]{:S(2)}) async-start(bf16[16,144,128]{2,1,0:T(8,128)(2,1)} %shard_map.101), calls=%async_computation.1 | async-start | bytes 1179648 | tf_op jit(solution)/shard_map/all_to_all | solution.py:541
  41.6 5.1 %collective-permute-start.7 = (bf16[1024,128]{1,0:T(8,128)(2,1)}, bf16[1024,128]{1,0:T(8,128)(2,1)S(1)}, u32[]{:S(2)}, u32[]{:S(2)}) collective-permute-start(bf16[1024,128]{1,0:T(8,128)(2,1)} %copy-done.9), channel_id=1, source_target_pairs={{0,1},{1,0},{2,3},{3,2},{4,5},{5,4},{6,7},{7,6},{8,9},{9,8},{10,11... | collective-permute-start | bytes 786440 | tf_op jit(solution)/shard_map/ppermute | solution.py:145
  43.4 10.2 %collective-permute-start.8 = (bf16[1024,128]{1,0:T(8,128)(2,1)}, bf16[1024,128]{1,0:T(8,128)(2,1)S(1)}, u32[]{:S(2)}, u32[]{:S(2)}) collective-permute-start(bf16[1024,128]{1,0:T(8,128)(2,1)} %copy-done.8), channel_id=1, source_target_pairs={{1,2},{2,1},{5,6},{6,5},{9,10},{10,9},{13,14},{14,13},{17,18},{18,... | collective-permute-start | bytes 786440 | tf_op jit(solution)/shard_map/ppermute | solution.py:507
  53.6 0.7 %copy-start.3 = (bf16[1024,128]{1,0:T(8,128)(2,1)}, bf16[1024,128]{1,0:T(8,128)(2,1)S(1)}, u32[]{:S(2)}) copy-start(bf16[1024,128]{1,0:T(8,128)(2,1)S(1)} %collective-permute-done.8.second) | copy-start | bytes 786436
  56.7 5.5 %collective-permute-start.9 = (bf16[16,144,128]{2,1,0:T(8,128)(2,1)S(1)}, bf16[16,144,128]{2,1,0:T(8,128)(2,1)S(1)}, u32[]{:S(2)}, u32[]{:S(2)}) collective-permute-start(bf16[16,144,128]{2,1,0:T(8,128)(2,1)S(1)} %all-to-all-done.1.refs_0_), channel_id=1, source_target_pairs={{0,1},{1,0},{2,3},{3,2},{4,5},{5,4},{6,7},{7,6},{8,9},{9,8},{10,11... | collective-permute-start | bytes 1769480 | tf_op jit(solution)/shard_map/ppermute | solution.py:145
  59.2 0.9 %copy-start.4 = (bf16[1024,128]{1,0:T(8,128)(2,1)S(1)}, bf16[1024,128]{1,0:T(8,128)(2,1)}, u32[]{:S(2)}) copy-start(bf16[1024,128]{1,0:T(8,128)(2,1)} %copy-done.3) | copy-start | bytes 786436

commit v18 on v17

--- a/solution.py
+++ b/solution.py
@@ -31,7 +31,7 @@
     return jnp.concatenate([window[g * step : g * step + rows] for g in range(count)], axis=1)
 
 
-def turned(src, flat, dst, offset, pitch, lead):
+def turned(src, flat, dst):
     chans, length, _ = src.shape
 
     def stage(c, carry):
@@ -42,8 +42,7 @@
 
     def gather(x, carry):
         rows = flat[pl.ds(x, chans, stride=length), :]
-        at = pl.multiple_of((x + lead) * pitch + offset, 16)
-        dst[pl.ds(at, chans), :] = rows.astype(BF16)
+        dst[pl.ds(pl.multiple_of(x * chans, 16), chans), :] = rows.astype(BF16)
         return carry
 
     lax.fori_loop(0, length, gather, 0, unroll=4)
@@ -51,11 +50,7 @@
 
 def pack_kernel(field, *refs):
     out, flat = refs[-2:]
-    chans, length, width = field.shape
-    zeros = jnp.zeros((chans, width), BF16)
-    out[0:chans, :] = zeros
-    out[(length + 1) * chans : (length + 2) * chans, :] = zeros
-    turned(field, flat, out, 0, chans, 1)
+    turned(field, flat, out)
 
 
 def pack(field, after, weight):
@@ -63,7 +58,7 @@
     spec = pl.BlockSpec(memory_space=pltpu.VMEM)
     return pl.pallas_call(
         pack_kernel,
-        out_shape=jax.ShapeDtypeStruct(((length + 2) * chans, width), BF16),
+        out_shape=jax.ShapeDtypeStruct((length * chans, width), BF16),
         in_specs=[spec] + [pl.BlockSpec(memory_space=pl.ANY) for _ in after],
         out_specs=spec,
         scratch_shapes=[pltpu.VMEM((chans * length, width), F32)],
@@ -153,10 +148,14 @@
 
 
 def windows(packs, x, count):
-    rows = [
-        [p[pl.ds(pl.multiple_of((x + n) * count, 16), count), :] for p in packs]
-        for n in range(GROUP + 2)
-    ]
+    length = packs[0].shape[0] // count
+
+    def row(p, n):
+        if 0 <= n < length:
+            return p[n * count : (n + 1) * count, :]
+        return jnp.zeros((count, LANES), BF16)
+
+    rows = [[row(p, x + n - 1) for p in packs] for n in range(GROUP + 2)]
     return jnp.concatenate(
         [jnp.concatenate(sum(rows[g : g + 3], []), axis=0) for g in range(GROUP)], axis=1
     )
@@ -175,7 +174,7 @@
 
 def prepare_kernel(act, two, one, acts, w_two, w_one, flat):
     ahead, back = plane_order()
-    turned(act, flat, acts, 0, act.shape[0], 0)
+    turned(act, flat, acts)
     w_two[...] = jnp.concatenate(
         [
             jnp.concatenate([two[back[n], 2 - j, 2 - k].astype(F32) for k in range(3)], axis=0)
@@ -219,24 +218,20 @@
     pres[(length + 1) * stacked : (length + 2) * stacked, :] = jnp.zeros((stacked, LANES), BF16)
     acc[...] = jnp.zeros_like(acc)
 
-    def body(step, carry):
-        x = step * GROUP
+    for x in range(0, length, GROUP):
         right = windows(packs, x, c2)
         sums = jnp.dot(w_two[...], right, preferred_element_type=F32)
         columns = []
         for g in range(GROUP):
             part = sums[:, g * LANES : (g + 1) * LANES]
             grad = slid(part[0:c1], 1) + part[c1 : 2 * c1] + slid(part[2 * c1 : 3 * c1], -1)
-            value = acts[pl.ds(pl.multiple_of((x + g) * c1, 16), c1), :].astype(F32)
+            value = acts[(x + g) * c1 : (x + g + 1) * c1, :].astype(F32)
             pre = (grad * jnp.where(value > 0, 1.0, 0.2)).astype(BF16).astype(F32)
             moved = jnp.concatenate([slid(pre, -1), pre, slid(pre, 1)], axis=0).astype(BF16)
-            pres[pl.ds(pl.multiple_of((x + g + 1) * stacked, 16), stacked), :] = moved
+            pres[(x + g + 1) * stacked : (x + g + 2) * stacked, :] = moved
             stack = jnp.concatenate([slid(value, 1), value, slid(value, -1)], axis=0)
             columns.append(stack.astype(BF16))
         acc[...] += across_lanes(right, jnp.concatenate(columns, axis=1))
-        return carry
-
-    lax.fori_loop(0, length // GROUP, body, 0, unroll=True)
 
     terms[...] = jnp.zeros_like(terms)
     total = ordered(acc, c2, ahead).T
@@ -253,15 +248,9 @@
     length = pres.shape[0] // stacked - 2
     acc[...] = jnp.zeros_like(acc)
 
-    def body(step, carry):
-        x = step * GROUP
-        rows = [
-            pres[pl.ds(pl.multiple_of((x + g + 1) * stacked, 16), stacked), :] for g in range(GROUP)
-        ]
+    for x in range(0, length, GROUP):
+        rows = [pres[(x + g + 1) * stacked : (x + g + 2) * stacked, :] for g in range(GROUP)]
         acc[...] += across_lanes(windows(packs, x, c0), jnp.concatenate(rows, axis=1))
-        return carry
-
-    lax.fori_loop(0, length // GROUP, body, 0, unroll=True)
 
     used = before.shape[0]
     terms[0:used, :] = before[...]
@@ -275,19 +264,15 @@
     c0, stacked = (w_one.shape[0] // 3, w_one.shape[1] // 3)
     length = pres.shape[0] // stacked - 2
 
-    def body(step, carry):
-        x = step * GROUP
-        window = pres[pl.ds(pl.multiple_of(x * stacked, 16), (GROUP + 2) * stacked), :]
+    for x in range(0, length, GROUP):
+        window = pres[x * stacked : (x + GROUP + 2) * stacked, :]
         moved = beside(window, 3 * stacked, stacked, GROUP)
         sums = jnp.dot(w_one[...], moved, preferred_element_type=F32)
         for g in range(GROUP):
             part = sums[:, g * LANES : (g + 1) * LANES]
-            at = pl.ds(pl.multiple_of((x + g) * c0, 16), c0)
+            at = pl.ds((x + g) * c0, c0)
             for i, out in ((0, inner), (1, own), (2, outer)):
                 out[at, :] = part[i * c0 : (i + 1) * c0].astype(out.dtype)
-        return carry
-
-    lax.fori_loop(0, length // GROUP, body, 0, unroll=True)
 
 
 def vmem_call(body, out_shape, scratch=(), cost=None, limit=24 * 2**20):
@@ -318,7 +303,7 @@
 
 def gradient_part(packs, pres, terms, rows, c1):
     width = pres.shape[1]
-    c0 = packs[0].shape[0] // (pres.shape[0] // (3 * c1))
+    c0 = packs[0].shape[0] // (pres.shape[0] // (3 * c1) - 2)
     return vmem_call(
         gradient_kernel,
         (
@@ -371,29 +356,34 @@
     )(own, first, second)
 
 
-def share_kernel(scale, parts, out):
+def share_kernel(scale, parts, out, buffer, sems):
     copies, rows, _ = parts.shape
     padded = out.shape[1] - rows
-    near = jnp.sum(parts[0 : copies // 2, 0:padded, :].astype(F32), axis=0).astype(BF16)
-    far = jnp.sum(parts[copies // 2 :, 0:padded, :].astype(F32), axis=0).astype(BF16)
-    grads = (jnp.sum(parts[:, padded:rows, :].astype(F32), axis=0) * scale).astype(BF16)
-
-    def write(n, carry):
-        out[n, 0:padded, :] = near
-        out[n, padded : 2 * padded, :] = far
-        out[n, 2 * padded :, :] = grads
-        return carry
-
-    lax.fori_loop(0, copies, write, 0)
+    far = copies // 2
+    buffer[0:padded, :] = jnp.sum(parts[0:far, 0:padded, :].astype(F32), axis=0).astype(BF16)
+    buffer[padded : 2 * padded, :] = jnp.sum(parts[far:, 0:padded, :].astype(F32), axis=0).astype(BF16)
+    grads = jnp.sum(parts[:, padded:rows, :].astype(F32), axis=0) * scale
+    buffer[2 * padded :, :] = grads.astype(BF16)
+    sent = [pltpu.make_async_copy(buffer, out.at[n], sems.at[n]) for n in range(copies)]
+    for copy in sent:
+        copy.start()
+    for copy in sent:
+        copy.wait()
 
 
 def share(parts, extra, scale):
     copies, rows, _ = parts.shape
-    return vmem_call(
+    height = 2 * rows - extra
+    return pl.pallas_call(
         lambda *refs: share_kernel(scale, *refs),
-        jax.ShapeDtypeStruct((copies, 2 * rows - extra, LANES), BF16),
-        (),
-        pl.CostEstimate(flops=parts.size, bytes_accessed=6 * parts.size, transcendentals=0),
+        out_shape=jax.ShapeDtypeStruct((copies, height, LANES), BF16),
+        in_specs=[pl.BlockSpec(memory_space=pltpu.VMEM)],
+        out_specs=pl.BlockSpec(memory_space=pl.ANY),
+        scratch_shapes=[pltpu.VMEM((height, LANES), BF16), pltpu.SemaphoreType.DMA((copies,))],
+        compiler_params=pltpu.CompilerParams(vmem_limit_bytes=24 * 2**20),
+        cost_estimate=pl.CostEstimate(
+            flops=parts.size, bytes_accessed=6 * parts.size, transcendentals=0
+        ),
     )(parts)
 
 
@@ -540,8 +530,8 @@
     shares, inner, outer = lax.optimization_barrier((shares, inner, outer))
     mine = lax.all_to_all(shares, SAME, 0, 0)
     inner, outer = (swapped(inner), crossed(outer))
-    mine, own, inner, outer = lax.optimization_barrier((mine, own, inner, outer))
     grad_input = merge(own, inner, outer, volume_in.shape[2:])
+    mine, grad_input = lax.optimization_barrier((mine, grad_input))
     bucket_sum, total_one, total_two = finish(mine, swapped(mine), length, (c0, c1, c2))
     return (
         grad_input[None, None],

time: 63.9 us -> 63.4 us (level)
  local copies, waits for them, and re-layouts: 3.02 us -> 2.06 us
    unnamed x20 -> x14, local copies, waits for them, and re-layouts: 2.88 us -> 1.92 us
  transfers between devices with their start and end apart: 11 -> 11, of which waited for: 5 -> 5; matrix products, arithmetic and copies ran while one was open for 0% -> 0% of each run, Pallas kernels for 12% -> 13%
where the time goes in v18:
time: 63.4 us; the launch traced here: 62.8 us
  starting transfers between devices  20.3 us (32%)
  blocking collectives  16.7 us (26%)
  waiting for transfers between devices  11.7 us (18%)
  Pallas kernels  11.1 us (18%)
  local copies, waits for them, and re-layouts  2.06 us (3%)
  between operations  0.85 us (1%)
    all_to_all x1, blocking collectives, per_device(): parts = lax.all_to_all(parts, SAME, 0, 0)  16.7 us
    ppermute x3, starting transfers between devices, crossed(): return lax.ppermute(value, SPACE, pairs + [(m, n) for n, m in pairs])  9.81 us
    ppermute x3, waiting for transfers between devices, crossed(): return lax.ppermute(value, SPACE, pairs + [(m, n) for n, m in pairs])  8.79 us
    ppermute x7, starting transfers between devices, swapped(): return lax.ppermute(value, axis, [(0, 1), (1, 0)])  6.4 us
    all_to_all x1, starting transfers between devices, per_device(): mine = lax.all_to_all(shares, SAME, 0, 0)  4.09 us
    pallas_call x1, Pallas kernels, first_part(): vmem_call(first_kernel, (jax.ShapeDtypeStruct(((length + 2) * 3 * c1, wid...  2.53 us
    all_to_all x1, waiting for transfers between devices, per_device(): mine = lax.all_to_all(shares, SAME, 0, 0)  2.28 us
    unnamed x14, local copies, waits for them, and re-layouts  1.92 us
  transfers between devices with their start and end apart: 11, of which 5 were waited for; matrix products, arithmetic and copies ran while one was open for 0% of the time, Pallas kernels for 13%

profile of v18, /device:TPU:1, one launch (start us, length us, event | category | flops | bytes accessed | tf_op | source)
XLA Modules:
  0.0 62.8 jit_solution(5905281953960281027)
XLA Ops:
  0.6 0.0 copy-start
  0.7 0.0 copy-start.1
  0.7 1.2 %copy-done.1 = bf16[1,1,32,64,128]{4,3,2,1,0:T(8,128)(2,1)S(1)} copy-done((bf16[1,1,32,64,128]{4,3,2,1,0:T(8,128)(2,1)S(1)}, bf16[1,1,32,64,128]{4,3,2,1,0:T(8,128)(2,1)}, u32[]{:S(2)}) %copy-start.1) | copy-done | bytes 524312
  1.8 0.0 copy-start.3
  1.8 0.8 %shard_map.93.refs_0_.pack_0 = bf16[2048,128]{1,0:T(8,128)(2,1)S(1)} custom-call(bf16[32,64,128]{2,1,0:T(8,128)(2,1)S(1)} %bitcast.10), custom_call_target="tpu_custom_call" | custom-call | bytes 67108864 | tf_op jit(solution)/shard_map/pallas_call | solution.py:59
  2.6 0.0 copy-done
  2.6 0.1 dynamic-slice_convert_fusion
  2.7 0.0 copy-start.2
  2.7 0.0 copy-start.4
  2.7 0.0 copy-start.5
  2.8 0.1 constant_dynamic-slice_fusion.own
  2.8 0.1 collective-permute-start
  3.0 4.6 %collective-permute-start.5 = (bf16[2048,128]{1,0:T(8,128)(2,1)S(1)}, bf16[2048,128]{1,0:T(8,128)(2,1)S(1)}, u32[]{:S(2)}, u32[]{:S(2)}) collective-permute-start(bf16[2048,128]{1,0:T(8,128)(2,1)S(1)} %shard_map.93.refs_0_.pack_0), channel_id=1, source_target_pairs={{1,2},{2,1},{5,6},{6,5},{9,10},{10,9},{13,14},{14,13},{17,18},{18,... | collective-permute-start | bytes 1572872 | tf_op jit(solution)/shard_map/ppermute | solution.py:497
  7.6 0.1 collective-permute-start.4
  7.7 0.0 copy-done.3
  7.7 0.5 shard_map.95.pack_0
  8.2 1.9 %collective-permute-start.3 = (bf16[1024,128]{1,0:T(8,128)(2,1)S(1)}, bf16[1024,128]{1,0:T(8,128)(2,1)S(1)}, u32[]{:S(2)}, u32[]{:S(2)}) collective-permute-start(bf16[1024,128]{1,0:T(8,128)(2,1)S(1)} %shard_map.95.pack_0), channel_id=1, source_target_pairs={{1,2},{2,1},{5,6},{6,5},{9,10},{10,9},{13,14},{14,13},{17,18},{18,... | collective-permute-start | bytes 786440 | tf_op jit(solution)/shard_map/ppermute | solution.py:497
  10.1 0.1 collective-permute-start.2
  10.2 0.0 collective-permute-done.other
  10.2 0.1 shard_map.94
  10.3 1.7 %collective-permute-start.1 = (bf16[1024,128]{1,0:T(8,128)(2,1)S(1)}, bf16[1024,128]{1,0:T(8,128)(2,1)S(1)}, u32[]{:S(2)}, u32[]{:S(2)}) collective-permute-start(bf16[1024,128]{1,0:T(8,128)(2,1)S(1)} %get-tuple-element.42), channel_id=1, source_target_pairs={{0,4},{4,0},{1,5},{5,1},{2,6},{6,2},{3,7},{7,3},{8,12},{12,8},{9,1... | collective-permute-start | bytes 786440 | tf_op jit(solution)/shard_map/ppermute | solution.py:140
  12.0 0.0 copy-done.2
  12.0 0.0 copy-done.4
  12.0 0.0 copy-done.5
  12.0 0.9 %shard_map.96 = (bf16[2048,128]{1,0:T(8,128)(2,1)S(1)}, bf16[96,288]{1,0:T(8,128)(2,1)S(1)}, bf16[48,288]{1,0:T(8,128)(2,1)S(1)}) custom-call(bf16[32,64,128]{2,1,0:T(8,128)(2,1)S(1)} %bitcast.11, bf16[3,3,3,32,32]{4,3,2,1,0:T(8,128)(2,1)S(1)} %copy-done.4, bf16[3,3,3,16,32]{4,3,2,1,0:T(8,128)(2,1)S(1)} %copy-done.5), custom_call_target="tpu_custom_call" | custom-call | bytes 4194304 | tf_op jit(solution)/shard_map/pallas_call | solution.py:199
  13.0 1.8 %collective-permute-done.5.pack_out = bf16[2048,128]{1,0:T(8,128)(2,1)S(1)} collective-permute-done((bf16[2048,128]{1,0:T(8,128)(2,1)S(1)}, bf16[2048,128]{1,0:T(8,128)(2,1)S(1)}, u32[]{:S(2)}, u32[]{:S(2)}) %collective-permute-start.5) | collective-permute-done | bytes 524320 | tf_op jit(solution)/shard_map/ppermute | solution.py:497
  14.7 0.0 collective-permute-done.4.pack_in
  14.7 2.5 %shard_map.97 = (bf16[6336,128]{1,0:T(8,128)(2,1)S(1)}, f32[288,128]{1,0:T(8,128)S(1)}) custom-call(bf16[2048,128]{1,0:T(8,128)(2,1)S(1)} %collective-permute-done.4.pack_in, bf16[2048,128]{1,0:T(8,128)(2,1)S(1)} %shard_map.93.refs_0_.pack_0, bf16[2048,128]{1,0:T(8,128)(2,1)S(1)} %collective-permute-done.5.pack_out, ...), custom_call_target="tpu_custom_call" | custom-call | flops 1000000000 | bytes 20971520 | tf_op jit(solution)/shard_map/pallas_call | solution.py:293
  17.3 0.3 collective-permute-done.3.pack_out
  17.6 0.0 collective-permute-done.2.pack_in
  17.6 0.8 %shard_map.98 = (bf16[256,128]{1,0:T(8,128)(2,1)S(1)}, f32[256,128]{1,0:T(8,128)S(1)}) custom-call(bf16[1024,128]{1,0:T(8,128)(2,1)S(1)} %collective-permute-done.2.pack_in, bf16[1024,128]{1,0:T(8,128)(2,1)S(1)} %shard_map.95.pack_0, bf16[1024,128]{1,0:T(8,128)(2,1)S(1)} %collective-permute-done.3.pack_out, bf16[6336,128]{1,0:T(8,128)(2,1)S(1)} %get-tuple-element.47.pres, ...), custom_call_target="tpu_custom_call" | custom-call | flops 1000000000 | bytes 5242880 | tf_op jit(solution)/shard_map/pallas_call | solution.py:307
  18.4 0.1 collective-permute-start.6
  18.5 1.1 %shard_map.100 = (f32[1024,128]{1,0:T(8,128)S(1)}, bf16[1024,128]{1,0:T(8,128)(2,1)S(1)}, bf16[1024,128]{1,0:T(8,128)(2,1)S(1)}) custom-call(bf16[6336,128]{1,0:T(8,128)(2,1)S(1)} %get-tuple-element.47.pres, bf16[48,288]{1,0:T(8,128)(2,1)S(1)} %get-tuple-element.51.w_one), custom_call_target="tpu_custom_call" | custom-call | flops 1000000000 | bytes 5242880 | tf_op jit(solution)/shard_map/pallas_call | solution.py:321
  19.5 0.0 copy-start.6
  19.5 0.7 %copy-done.6 = bf16[1024,128]{1,0:T(8,128)(2,1)} copy-done((bf16[1024,128]{1,0:T(8,128)(2,1)}, bf16[1024,128]{1,0:T(8,128)(2,1)S(1)}, u32[]{:S(2)}) %copy-start.6) | copy-done | bytes 262168
  20.2 0.0 collective-permute-done.6.more
  20.2 0.0 collective-permute-done.1.other
  20.2 0.1 shard_map.99
  20.3 16.7 %all_to_all.10.refs_0_ = bf16[16,80,128]{2,1,0:T(8,128)(2,1)S(1)} all-to-all(bf16[16,80,128]{2,1,0:T(8,128)(2,1)S(1)} %shard_map.99), channel_id=1, replica_groups=mesh['z'=4,'x'=2,'y'=2,'core'=2] {'x','z','y'}, dimensions={0} | all-to-all | bytes 655360 | tf_op jit(solution)/shard_map/all_to_all | solution.py:526
  37.0 1.0 %shard_map.101 = bf16[16,144,128]{2,1,0:T(8,128)(2,1)} custom-call(bf16[16,80,128]{2,1,0:T(8,128)(2,1)S(1)} %all_to_all.10.refs_0_), custom_call_target="tpu_custom_call" | custom-call | flops 163840 | bytes 983040 | tf_op jit(solution)/shard_map/pallas_call | solution.py:377
  38.0 4.1 %all-to-all-start.1 = ((bf16[16,144,128]{2,1,0:T(8,128)(2,1)}), bf16[16,144,128]{2,1,0:T(8,128)(2,1)S(1)}, u32[]{:S(2)}, u32[]{:S(2)}) async-start(bf16[16,144,128]{2,1,0:T(8,128)(2,1)} %shard_map.101), calls=%async_computation.1 | async-start | bytes 1179648 | tf_op jit(solution)/shard_map/all_to_all | solution.py:531
  42.1 1.8 %collective-permute-start.7 = (bf16[1024,128]{1,0:T(8,128)(2,1)}, bf16[1024,128]{1,0:T(8,128)(2,1)S(1)}, u32[]{:S(2)}, u32[]{:S(2)}) collective-permute-start(bf16[1024,128]{1,0:T(8,128)(2,1)} %copy-done.6), channel_id=1, source_target_pairs={{0,1},{1,0},{2,3},{3,2},{4,5},{5,4},{6,7},{7,6},{8,9},{9,8},{10,11... | collective-permute-start | bytes 786440 | tf_op jit(solution)/shard_map/ppermute | solution.py:140
  43.9 3.3 %collective-permute-start.8 = (bf16[1024,128]{1,0:T(8,128)(2,1)S(1)}, bf16[1024,128]{1,0:T(8,128)(2,1)S(1)}, u32[]{:S(2)}, u32[]{:S(2)}) collective-permute-start(bf16[1024,128]{1,0:T(8,128)(2,1)S(1)} %get-tuple-element.60), channel_id=1, source_target_pairs={{1,2},{2,1},{5,6},{6,5},{9,10},{10,9},{13,14},{14,13},{17,18},{18,... | collective-permute-start | bytes 786440 | tf_op jit(solution)/shard_map/ppermute | solution.py:497
  47.2 0.0 collective-permute-done.7.first
  47.2 6.8 %collective-permute-done.8.second = bf16[1024,128]{1,0:T(8,128)(2,1)S(1)} collective-permute-done((bf16[1024,128]{1,0:T(8,128)(2,1)S(1)}, bf16[1024,128]{1,0:T(8,128)(2,1)S(1)}, u32[]{:S(2)}, u32[]{:S(2)}) %collective-permute-start.8) | collective-permute-done | bytes 262176 | tf_op jit(solution)/shard_map/ppermute | solution.py:497
  53.9 1.0 %shard_map.102 = bf16[16,64,128]{2,1,0:T(8,128)(2,1)} custom-call(f32[1024,128]{1,0:T(8,128)S(1)} %get-tuple-element.58.own, bf16[1024,128]{1,0:T(8,128)(2,1)S(1)} %collective-permute-done.7.first, bf16[1024,128]{1,0:T(8,128)(2,1)S(1)} %collective-permute-done.8.second), custom_call_target="tpu_custom_call" | custom-call | flops 262144 | bytes 1048576 | tf_op jit(solution)/shard_map/pallas_call | solution.py:351
  54.9 2.3 %all-to-all-done.1.refs_0_ = bf16[16,144,128]{2,1,0:T(8,128)(2,1)S(1)} async-done(((bf16[16,144,128]{2,1,0:T(8,128)(2,1)}), bf16[16,144,128]{2,1,0:T(8,128)(2,1)S(1)}, u32[]{:S(2)}, u32[]{:S(2)}) %all-to-all-start.1) | async-done | bytes 589856 | tf_op jit(solution)/shard_map/all_to_all | solution.py:531
  57.2 2.6 %collective-permute-start.9 = (bf16[16,144,128]{2,1,0:T(8,128)(2,1)S(1)}, bf16[16,144,128]{2,1,0:T(8,128)(2,1)S(1)}, u32[]{:S(2)}, u32[]{:S(2)}) collective-permute-start(bf16[16,144,128]{2,1,0:T(8,128)(2,1)S(1)} %all-to-all-done.1.refs_0_), channel_id=1, source_target_pairs={{0,1},{1,0},{2,3},{3,2},{4,5},{5,4},{6,7},{7,6},{8,9},{9,8},{10,11... | collective-permute-start | bytes 1769480 | tf_op jit(solution)/shard_map/ppermute | solution.py:140
  59.7 1.0 %shard_map.103.refs_2_ = f32[4096,128]{1,0:T(8,128)} custom-call(bf16[16,144,128]{2,1,0:T(8,128)(2,1)S(1)} %all-to-all-done.1.refs_0_), custom_call_target="tpu_custom_call" | custom-call | tf_op jit(solution)/shard_map/pallas_call | solution.py:466
  60.8 0.6 collective-permute-done.9.refs_1_
  61.4 1.4 %shard_map.104 = (f32[4096,128]{1,0:T(8,128)}, f32[432,32]{1,0:T(8,128)}, f32[864,32]{1,0:T(8,128)}) custom-call(bf16[16,144,128]{2,1,0:T(8,128)(2,1)S(1)} %all-to-all-done.1.refs_0_, bf16[16,144,128]{2,1,0:T(8,128)(2,1)S(1)} %collective-permute-done.9.refs_1_, f32[4096,128]{1,0:T(8,128)} %shard_map.103.refs_2_), custom_call_target="tpu_custom_call", output_to_operand_aliasing={{0}: (2, {})} | custom-call | tf_op jit(solution)/shard_map/pallas_call | solution.py:474
Async XLA Ops:
  0.6 2.0 %copy-start = (f32[1,524288]{1,0:T(1,128)S(1)}, f32[1,524288]{1,0:T(1,128)}, u32[]{:S(2)}) copy-start(f32[1,524288]{1,0:T(1,128)} %param.11) | copy-start | bytes 6291460
  0.7 1.2 %copy-start.1 = (bf16[1,1,32,64,128]{4,3,2,1,0:T(8,128)(2,1)S(1)}, bf16[1,1,32,64,128]{4,3,2,1,0:T(8,128)(2,1)}, u32[]{:S(2)}) copy-start(bf16[1,1,32,64,128]{4,3,2,1,0:T(8,128)(2,1)} %param.8) | copy-start | bytes 1572868
  1.8 5.8 %copy-start.3 = (bf16[1,1,16,64,128]{4,3,2,1,0:T(8,128)(2,1)S(1)}, bf16[1,1,16,64,128]{4,3,2,1,0:T(8,128)(2,1)}, u32[]{:S(2)}) copy-start(bf16[1,1,16,64,128]{4,3,2,1,0:T(8,128)(2,1)} %param.6) | copy-start | bytes 786436
  2.7 9.3 %copy-start.2 = (bf16[1,1,32,64,128]{4,3,2,1,0:T(8,128)(2,1)S(1)}, bf16[1,1,32,64,128]{4,3,2,1,0:T(8,128)(2,1)}, u32[]{:S(2)}) copy-start(bf16[1,1,32,64,128]{4,3,2,1,0:T(8,128)(2,1)} %param.7) | copy-start | bytes 1572868
  2.7 9.3 %copy-start.4 = (bf16[3,3,3,32,32]{4,3,2,1,0:T(8,128)(2,1)S(1)}, bf16[3,3,3,32,32]{4,3,2,1,0:T(8,128)(2,1)}, u32[]{:S(2)}) copy-start(bf16[3,3,3,32,32]{4,3,2,1,0:T(8,128)(2,1)} %two.1) | copy-start | bytes 165892
  2.7 9.3 %copy-start.5 = (bf16[3,3,3,16,32]{4,3,2,1,0:T(8,128)(2,1)S(1)}, bf16[3,3,3,16,32]{4,3,2,1,0:T(8,128)(2,1)}, u32[]{:S(2)}) copy-start(bf16[3,3,3,16,32]{4,3,2,1,0:T(8,128)(2,1)} %one.1) | copy-start | bytes 82948
  2.8 7.3 %collective-permute-start = (bf16[2048,128]{1,0:T(8,128)(2,1)S(1)}, bf16[2048,128]{1,0:T(8,128)(2,1)S(1)}, u32[]{:S(2)}, u32[]{:S(2)}) collective-permute-start(bf16[2048,128]{1,0:T(8,128)(2,1)S(1)} %dynamic-slice_convert_fusion), channel_id=1, source_target_pairs={{0,1},{1,0},{2,3},{3,2},{4,5},{5,4},{6,7},{7,6},{8,9},{9,8},{10,11... | collective-permute-start | bytes 1572872 | tf_op jit(solution)/shard_map/ppermute | solution.py:140
  3.0 11.8 %collective-permute-start.5 = (bf16[2048,128]{1,0:T(8,128)(2,1)S(1)}, bf16[2048,128]{1,0:T(8,128)(2,1)S(1)}, u32[]{:S(2)}, u32[]{:S(2)}) collective-permute-start(bf16[2048,128]{1,0:T(8,128)(2,1)S(1)} %shard_map.93.refs_0_.pack_0), channel_id=1, source_target_pairs={{1,2},{2,1},{5,6},{6,5},{9,10},{10,9},{13,14},{14,13},{17,18},{18,... | collective-permute-start | bytes 1572872 | tf_op jit(solution)/shard_map/ppermute | solution.py:497
  7.6 7.1 %collective-permute-start.4 = (bf16[2048,128]{1,0:T(8,128)(2,1)S(1)}, bf16[2048,128]{1,0:T(8,128)(2,1)S(1)}, u32[]{:S(2)}, u32[]{:S(2)}) collective-permute-start(bf16[2048,128]{1,0:T(8,128)(2,1)S(1)} %shard_map.93.refs_0_.pack_0), channel_id=1, source_target_pairs={{0,1},{1,0},{2,3},{3,2},{4,5},{5,4},{6,7},{7,6},{8,9},{9,8},{10,11... | collective-permute-start | bytes 1572872 | tf_op jit(solution)/shard_map/ppermute | solution.py:140
  8.2 9.4 %collective-permute-start.3 = (bf16[1024,128]{1,0:T(8,128)(2,1)S(1)}, bf16[1024,128]{1,0:T(8,128)(2,1)S(1)}, u32[]{:S(2)}, u32[]{:S(2)}) collective-permute-start(bf16[1024,128]{1,0:T(8,128)(2,1)S(1)} %shard_map.95.pack_0), channel_id=1, source_target_pairs={{1,2},{2,1},{5,6},{6,5},{9,10},{10,9},{13,14},{14,13},{17,18},{18,... | collective-permute-start | bytes 786440 | tf_op jit(solution)/shard_map/ppermute | solution.py:497
  10.1 7.5 %collective-permute-start.2 = (bf16[1024,128]{1,0:T(8,128)(2,1)S(1)}, bf16[1024,128]{1,0:T(8,128)(2,1)S(1)}, u32[]{:S(2)}, u32[]{:S(2)}) collective-permute-start(bf16[1024,128]{1,0:T(8,128)(2,1)S(1)} %shard_map.95.pack_0), channel_id=1, source_target_pairs={{0,1},{1,0},{2,3},{3,2},{4,5},{5,4},{6,7},{7,6},{8,9},{9,8},{10,11... | collective-permute-start | bytes 786440 | tf_op jit(solution)/shard_map/ppermute | solution.py:140
  10.3 9.9 %collective-permute-start.1 = (bf16[1024,128]{1,0:T(8,128)(2,1)S(1)}, bf16[1024,128]{1,0:T(8,128)(2,1)S(1)}, u32[]{:S(2)}, u32[]{:S(2)}) collective-permute-start(bf16[1024,128]{1,0:T(8,128)(2,1)S(1)} %get-tuple-element.42), channel_id=1, source_target_pairs={{0,4},{4,0},{1,5},{5,1},{2,6},{6,2},{3,7},{7,3},{8,12},{12,8},{9,1... | collective-permute-start | bytes 786440 | tf_op jit(solution)/shard_map/ppermute | solution.py:140
  18.4 1.8 %collective-permute-start.6 = (bf16[256,128]{1,0:T(8,128)(2,1)S(1)}, bf16[256,128]{1,0:T(8,128)(2,1)S(1)}, u32[]{:S(2)}, u32[]{:S(2)}) collective-permute-start(bf16[256,128]{1,0:T(8,128)(2,1)S(1)} %get-tuple-element.50), channel_id=1, source_target_pairs={{0,1},{1,0},{2,3},{3,2},{4,5},{5,4},{6,7},{7,6},{8,9},{9,8},{10,11... | collective-permute-start | bytes 196616 | tf_op jit(solution)/shard_map/ppermute | solution.py:140
  19.5 0.7 %copy-start.6 = (bf16[1024,128]{1,0:T(8,128)(2,1)}, bf16[1024,128]{1,0:T(8,128)(2,1)S(1)}, u32[]{:S(2)}) copy-start(bf16[1024,128]{1,0:T(8,128)(2,1)S(1)} %get-tuple-element.59) | copy-start | bytes 786436
  38.0 19.2 %all-to-all-start.1 = ((bf16[16,144,128]{2,1,0:T(8,128)(2,1)}), bf16[16,144,128]{2,1,0:T(8,128)(2,1)S(1)}, u32[]{:S(2)}, u32[]{:S(2)}) async-start(bf16[16,144,128]{2,1,0:T(8,128)(2,1)} %shard_map.101), calls=%async_computation.1 | async-start | bytes 1179648 | tf_op jit(solution)/shard_map/all_to_all | solution.py:531
  42.1 5.1 %collective-permute-start.7 = (bf16[1024,128]{1,0:T(8,128)(2,1)}, bf16[1024,128]{1,0:T(8,128)(2,1)S(1)}, u32[]{:S(2)}, u32[]{:S(2)}) collective-permute-start(bf16[1024,128]{1,0:T(8,128)(2,1)} %copy-done.6), channel_id=1, source_target_pairs={{0,1},{1,0},{2,3},{3,2},{4,5},{5,4},{6,7},{7,6},{8,9},{9,8},{10,11... | collective-permute-start | bytes 786440 | tf_op jit(solution)/shard_map/ppermute | solution.py:140
  43.9 10.0 %collective-permute-start.8 = (bf16[1024,128]{1,0:T(8,128)(2,1)S(1)}, bf16[1024,128]{1,0:T(8,128)(2,1)S(1)}, u32[]{:S(2)}, u32[]{:S(2)}) collective-permute-start(bf16[1024,128]{1,0:T(8,128)(2,1)S(1)} %get-tuple-element.60), channel_id=1, source_target_pairs={{1,2},{2,1},{5,6},{6,5},{9,10},{10,9},{13,14},{14,13},{17,18},{18,... | collective-permute-start | bytes 786440 | tf_op jit(solution)/shard_map/ppermute | solution.py:497
  57.2 4.2 %collective-permute-start.9 = (bf16[16,144,128]{2,1,0:T(8,128)(2,1)S(1)}, bf16[16,144,128]{2,1,0:T(8,128)(2,1)S(1)}, u32[]{:S(2)}, u32[]{:S(2)}) collective-permute-start(bf16[16,144,128]{2,1,0:T(8,128)(2,1)S(1)} %all-to-all-done.1.refs_0_), channel_id=1, source_target_pairs={{0,1},{1,0},{2,3},{3,2},{4,5},{5,4},{6,7},{7,6},{8,9},{9,8},{10,11... | collective-permute-start | bytes 1769480 | tf_op jit(solution)/shard_map/ppermute | solution.py:140

commit v19 on v18

--- a/solution.py
+++ b/solution.py
@@ -509,9 +509,9 @@
     near = lax.dynamic_slice_in_dim(bucket, core * half, half)
     cot, send, near = lax.optimization_barrier((cot, send, near))
     cots = (swapped(cot), cot, crossed(cot))
-    vol = pack(volume_in[0, 0], [cot], 16)
+    send, near = add(near, swapped(send))
+    vol = pack(volume_in[0, 0], [send], 16)
     vols = (swapped(vol), vol, crossed(vol))
-    send, near = add(near, swapped(send))
     act, send, near = lax.optimization_barrier((hidden_act[0, 0], send, near))
     far = swapped(send, "x")
 
@@ -519,8 +519,9 @@
     rows = ceil_to(used, 16 * devices)
     acts, w_two, w_one = prepare(act, kernel_two, kernel_one)
     pres, terms = first_part(cots, acts, w_two)
+    own, inner, outer = input_part(pres, w_one)
+    terms, inner = lax.optimization_barrier((terms, inner))
     send, keep = gradient_part(vols, pres, terms, rows, c1)
-    own, inner, outer = input_part(pres, w_one)
     parts = combine(near, far, keep, swapped(send), copies)
     parts, inner, outer = lax.optimization_barrier((parts, inner, outer))
     parts = lax.all_to_all(parts, SAME, 0, 0)

time: 63.4 us -> 64 us (level)
  blocking collectives: 16.7 us -> 15.7 us
  waiting for transfers between devices: 11.7 us -> 12.7 us
  starting transfers between devices: 20.3 us -> 21 us
    ppermute x7, waiting for transfers between devices: 0.63 us -> 1.85 us  [swapped(): return lax.ppermute(value, axis, [(0, 1), (1, 0)])]
    all_to_all x1, blocking collectives: 16.7 us -> 15.7 us  [per_device(): parts = lax.all_to_all(parts, SAME, 0, 0)]
    all_to_all x1, starting transfers between devices: 4.09 us -> 4.77 us  [per_device(): mine = lax.all_to_all(shares, SAME, 0, 0)]
  transfers between devices with their start and end apart: 11 -> 11, of which waited for: 5 -> 5; matrix products, arithmetic and copies ran while one was open for 0% -> 0% of each run, Pallas kernels for 13% -> 12%
where the time goes in v19:
time: 64 us; the launch traced here: 63.4 us
  starting transfers between devices  21 us (33%)
  blocking collectives  15.7 us (25%)
  waiting for transfers between devices  12.7 us (20%)
  Pallas kernels  11.1 us (17%)
  local copies, waits for them, and re-layouts  2.06 us (3%)
  between operations  0.87 us (1%)
    all_to_all x1, blocking collectives, per_device(): parts = lax.all_to_all(parts, SAME, 0, 0)  15.7 us
    ppermute x3, starting transfers between devices, crossed(): return lax.ppermute(value, SPACE, pairs + [(m, n) for n, m in pairs])  9.81 us
    ppermute x3, waiting for transfers between devices, crossed(): return lax.ppermute(value, SPACE, pairs + [(m, n) for n, m in pairs])  8.52 us
    ppermute x7, starting transfers between devices, swapped(): return lax.ppermute(value, axis, [(0, 1), (1, 0)])  6.4 us
    all_to_all x1, starting transfers between devices, per_device(): mine = lax.all_to_all(shares, SAME, 0, 0)  4.77 us
    pallas_call x1, Pallas kernels, first_part(): vmem_call(first_kernel, (jax.ShapeDtypeStruct(((length + 2) * 3 * c1, wid...  2.53 us
    all_to_all x1, waiting for transfers between devices, per_device(): mine = lax.all_to_all(shares, SAME, 0, 0)  2.28 us
    unnamed x14, local copies, waits for them, and re-layouts  1.92 us
  transfers between devices with their start and end apart: 11, of which 5 were waited for; matrix products, arithmetic and copies ran while one was open for 0% of the time, Pallas kernels for 12%

profile of v19, /device:TPU:1, one launch (start us, length us, event | category | flops | bytes accessed | tf_op | source)
XLA Modules:
  0.0 63.4 jit_solution(11382843062759556573)
XLA Ops:
  0.6 0.0 copy-start
  0.7 0.0 copy-start.1
  0.7 1.2 %copy-done.1 = bf16[1,1,32,64,128]{4,3,2,1,0:T(8,128)(2,1)S(1)} copy-done((bf16[1,1,32,64,128]{4,3,2,1,0:T(8,128)(2,1)S(1)}, bf16[1,1,32,64,128]{4,3,2,1,0:T(8,128)(2,1)}, u32[]{:S(2)}) %copy-start.1) | copy-done | bytes 524312
  1.8 0.8 %shard_map.93.pack_0 = bf16[2048,128]{1,0:T(8,128)(2,1)S(1)} custom-call(bf16[32,64,128]{2,1,0:T(8,128)(2,1)S(1)} %bitcast.10), custom_call_target="tpu_custom_call" | custom-call | bytes 67108864 | tf_op jit(solution)/shard_map/pallas_call | solution.py:59
  2.6 0.0 copy-done
  2.6 0.1 dynamic-slice_convert_fusion
  2.7 0.0 copy-start.3
  2.7 0.0 copy-start.2
  2.7 0.0 copy-start.4
  2.8 0.0 copy-start.5
  2.8 0.1 constant_dynamic-slice_fusion.own
  2.9 0.1 collective-permute-start
  3.0 4.6 %collective-permute-start.5 = (bf16[2048,128]{1,0:T(8,128)(2,1)S(1)}, bf16[2048,128]{1,0:T(8,128)(2,1)S(1)}, u32[]{:S(2)}, u32[]{:S(2)}) collective-permute-start(bf16[2048,128]{1,0:T(8,128)(2,1)S(1)} %shard_map.93.pack_0), channel_id=1, source_target_pairs={{1,2},{2,1},{5,6},{6,5},{9,10},{10,9},{13,14},{14,13},{17,18},{18,... | collective-permute-start | bytes 1572872 | tf_op jit(solution)/shard_map/ppermute | solution.py:497
  7.6 0.1 collective-permute-start.4
  7.7 0.0 collective-permute-done.other
  7.7 0.1 shard_map.94
  7.8 0.0 copy-done.3
  7.8 0.5 shard_map.95.pack_0
  8.3 1.9 %collective-permute-start.3 = (bf16[1024,128]{1,0:T(8,128)(2,1)S(1)}, bf16[1024,128]{1,0:T(8,128)(2,1)S(1)}, u32[]{:S(2)}, u32[]{:S(2)}) collective-permute-start(bf16[1024,128]{1,0:T(8,128)(2,1)S(1)} %shard_map.95.pack_0), channel_id=1, source_target_pairs={{1,2},{2,1},{5,6},{6,5},{9,10},{10,9},{13,14},{14,13},{17,18},{18,... | collective-permute-start | bytes 786440 | tf_op jit(solution)/shard_map/ppermute | solution.py:497
  10.2 0.1 collective-permute-start.2
  10.3 1.7 %collective-permute-start.1 = (bf16[1024,128]{1,0:T(8,128)(2,1)S(1)}, bf16[1024,128]{1,0:T(8,128)(2,1)S(1)}, u32[]{:S(2)}, u32[]{:S(2)}) collective-permute-start(bf16[1024,128]{1,0:T(8,128)(2,1)S(1)} %get-tuple-element.44.refs_0_), channel_id=1, source_target_pairs={{0,4},{4,0},{1,5},{5,1},{2,6},{6,2},{3,7},{7,3},{8,12},{12,8},{9,1... | collective-permute-start | bytes 786440 | tf_op jit(solution)/shard_map/ppermute | solution.py:140
  12.0 0.0 copy-done.2
  12.0 0.0 copy-done.4
  12.1 0.0 copy-done.5
  12.1 0.9 %shard_map.96 = (bf16[2048,128]{1,0:T(8,128)(2,1)S(1)}, bf16[96,288]{1,0:T(8,128)(2,1)S(1)}, bf16[48,288]{1,0:T(8,128)(2,1)S(1)}) custom-call(bf16[32,64,128]{2,1,0:T(8,128)(2,1)S(1)} %bitcast.11, bf16[3,3,3,32,32]{4,3,2,1,0:T(8,128)(2,1)S(1)} %copy-done.4, bf16[3,3,3,16,32]{4,3,2,1,0:T(8,128)(2,1)S(1)} %copy-done.5), custom_call_target="tpu_custom_call" | custom-call | bytes 4194304 | tf_op jit(solution)/shard_map/pallas_call | solution.py:199
  13.0 1.8 %collective-permute-done.5.pack_out = bf16[2048,128]{1,0:T(8,128)(2,1)S(1)} collective-permute-done((bf16[2048,128]{1,0:T(8,128)(2,1)S(1)}, bf16[2048,128]{1,0:T(8,128)(2,1)S(1)}, u32[]{:S(2)}, u32[]{:S(2)}) %collective-permute-start.5) | collective-permute-done | bytes 524320 | tf_op jit(solution)/shard_map/ppermute | solution.py:497
  14.8 0.0 collective-permute-done.4.pack_in
  14.8 2.5 %shard_map.97 = (bf16[6336,128]{1,0:T(8,128)(2,1)S(1)}, f32[288,128]{1,0:T(8,128)S(1)}) custom-call(bf16[2048,128]{1,0:T(8,128)(2,1)S(1)} %collective-permute-done.4.pack_in, bf16[2048,128]{1,0:T(8,128)(2,1)S(1)} %shard_map.93.pack_0, bf16[2048,128]{1,0:T(8,128)(2,1)S(1)} %collective-permute-done.5.pack_out, bf16[2048,128]{1,0:T(8,128)(2,1)S(1)} %get-tuple-element.47.acts, ...), custom_call_target="tpu_custom_call" | custom-call | flops 1000000000 | bytes 20971520 | tf_op jit(solution)/shard_map/pallas_call | solution.py:293
  17.3 1.1 %shard_map.98 = (f32[1024,128]{1,0:T(8,128)S(1)}, bf16[1024,128]{1,0:T(8,128)(2,1)S(1)}, bf16[1024,128]{1,0:T(8,128)(2,1)S(1)}) custom-call(bf16[6336,128]{1,0:T(8,128)(2,1)S(1)} %get-tuple-element.49.pres, bf16[48,288]{1,0:T(8,128)(2,1)S(1)} %get-tuple-element.51.w_one), custom_call_target="tpu_custom_call" | custom-call | flops 1000000000 | bytes 5242880 | tf_op jit(solution)/shard_map/pallas_call | solution.py:321
  18.3 0.0 copy-start.6
  18.4 0.7 %copy-done.6 = bf16[1024,128]{1,0:T(8,128)(2,1)} copy-done((bf16[1024,128]{1,0:T(8,128)(2,1)}, bf16[1024,128]{1,0:T(8,128)(2,1)S(1)}, u32[]{:S(2)}) %copy-start.6) | copy-done | bytes 262168
  19.1 0.0 collective-permute-done.3.pack_out
  19.1 0.0 collective-permute-done.2.pack_in
  19.1 0.8 %shard_map.99 = (bf16[256,128]{1,0:T(8,128)(2,1)S(1)}, f32[256,128]{1,0:T(8,128)S(1)}) custom-call(bf16[1024,128]{1,0:T(8,128)(2,1)S(1)} %collective-permute-done.2.pack_in, bf16[1024,128]{1,0:T(8,128)(2,1)S(1)} %shard_map.95.pack_0, bf16[1024,128]{1,0:T(8,128)(2,1)S(1)} %collective-permute-done.3.pack_out, bf16[6336,128]{1,0:T(8,128)(2,1)S(1)} %get-tuple-element.49.pres, ...), custom_call_target="tpu_custom_call" | custom-call | flops 1000000000 | bytes 5242880 | tf_op jit(solution)/shard_map/pallas_call | solution.py:307
  19.9 0.1 collective-permute-start.6
  20.0 0.0 collective-permute-done.1.other
  20.0 1.2 %collective-permute-done.6.more = bf16[256,128]{1,0:T(8,128)(2,1)S(1)} collective-permute-done((bf16[256,128]{1,0:T(8,128)(2,1)S(1)}, bf16[256,128]{1,0:T(8,128)(2,1)S(1)}, u32[]{:S(2)}, u32[]{:S(2)}) %collective-permute-start.6) | collective-permute-done | bytes 65568 | tf_op jit(solution)/shard_map/ppermute | solution.py:140
  21.2 0.1 shard_map.100
  21.3 15.7 %all_to_all.10.refs_0_ = bf16[16,80,128]{2,1,0:T(8,128)(2,1)S(1)} all-to-all(bf16[16,80,128]{2,1,0:T(8,128)(2,1)S(1)} %shard_map.100), channel_id=1, replica_groups=mesh['z'=4,'x'=2,'y'=2,'core'=2] {'x','z','y'}, dimensions={0} | all-to-all | bytes 655360 | tf_op jit(solution)/shard_map/all_to_all | solution.py:527
  37.0 1.0 %shard_map.101 = bf16[16,144,128]{2,1,0:T(8,128)(2,1)} custom-call(bf16[16,80,128]{2,1,0:T(8,128)(2,1)S(1)} %all_to_all.10.refs_0_), custom_call_target="tpu_custom_call" | custom-call | flops 163840 | bytes 983040 | tf_op jit(solution)/shard_map/pallas_call | solution.py:377
  38.0 4.8 %all-to-all-start.1 = ((bf16[16,144,128]{2,1,0:T(8,128)(2,1)}), bf16[16,144,128]{2,1,0:T(8,128)(2,1)S(1)}, u32[]{:S(2)}, u32[]{:S(2)}) async-start(bf16[16,144,128]{2,1,0:T(8,128)(2,1)} %shard_map.101), calls=%async_computation.1 | async-start | bytes 1179648 | tf_op jit(solution)/shard_map/all_to_all | solution.py:532
  42.8 1.8 %collective-permute-start.7 = (bf16[1024,128]{1,0:T(8,128)(2,1)}, bf16[1024,128]{1,0:T(8,128)(2,1)S(1)}, u32[]{:S(2)}, u32[]{:S(2)}) collective-permute-start(bf16[1024,128]{1,0:T(8,128)(2,1)} %copy-done.6), channel_id=1, source_target_pairs={{0,1},{1,0},{2,3},{3,2},{4,5},{5,4},{6,7},{7,6},{8,9},{9,8},{10,11... | collective-permute-start | bytes 786440 | tf_op jit(solution)/shard_map/ppermute | solution.py:140
  44.5 3.3 %collective-permute-start.8 = (bf16[1024,128]{1,0:T(8,128)(2,1)S(1)}, bf16[1024,128]{1,0:T(8,128)(2,1)S(1)}, u32[]{:S(2)}, u32[]{:S(2)}) collective-permute-start(bf16[1024,128]{1,0:T(8,128)(2,1)S(1)} %get-tuple-element.64), channel_id=1, source_target_pairs={{1,2},{2,1},{5,6},{6,5},{9,10},{10,9},{13,14},{14,13},{17,18},{18,... | collective-permute-start | bytes 786440 | tf_op jit(solution)/shard_map/ppermute | solution.py:497
  47.8 0.0 collective-permute-done.7.first
  47.8 6.8 %collective-permute-done.8.second = bf16[1024,128]{1,0:T(8,128)(2,1)S(1)} collective-permute-done((bf16[1024,128]{1,0:T(8,128)(2,1)S(1)}, bf16[1024,128]{1,0:T(8,128)(2,1)S(1)}, u32[]{:S(2)}, u32[]{:S(2)}) %collective-permute-start.8) | collective-permute-done | bytes 262176 | tf_op jit(solution)/shard_map/ppermute | solution.py:497
  54.6 1.0 %shard_map.102 = bf16[16,64,128]{2,1,0:T(8,128)(2,1)} custom-call(f32[1024,128]{1,0:T(8,128)S(1)} %get-tuple-element.62.own, bf16[1024,128]{1,0:T(8,128)(2,1)S(1)} %collective-permute-done.7.first, bf16[1024,128]{1,0:T(8,128)(2,1)S(1)} %collective-permute-done.8.second), custom_call_target="tpu_custom_call" | custom-call | flops 262144 | bytes 1048576 | tf_op jit(solution)/shard_map/pallas_call | solution.py:351
  55.5 2.3 %all-to-all-done.1.refs_0_ = bf16[16,144,128]{2,1,0:T(8,128)(2,1)S(1)} async-done(((bf16[16,144,128]{2,1,0:T(8,128)(2,1)}), bf16[16,144,128]{2,1,0:T(8,128)(2,1)S(1)}, u32[]{:S(2)}, u32[]{:S(2)}) %all-to-all-start.1) | async-done | bytes 589856 | tf_op jit(solution)/shard_map/all_to_all | solution.py:532
  57.8 2.6 %collective-permute-start.9 = (bf16[16,144,128]{2,1,0:T(8,128)(2,1)S(1)}, bf16[16,144,128]{2,1,0:T(8,128)(2,1)S(1)}, u32[]{:S(2)}, u32[]{:S(2)}) collective-permute-start(bf16[16,144,128]{2,1,0:T(8,128)(2,1)S(1)} %all-to-all-done.1.refs_0_), channel_id=1, source_target_pairs={{0,1},{1,0},{2,3},{3,2},{4,5},{5,4},{6,7},{7,6},{8,9},{9,8},{10,11... | collective-permute-start | bytes 1769480 | tf_op jit(solution)/shard_map/ppermute | solution.py:140
  60.4 1.0 %shard_map.103.refs_2_ = f32[4096,128]{1,0:T(8,128)} custom-call(bf16[16,144,128]{2,1,0:T(8,128)(2,1)S(1)} %all-to-all-done.1.refs_0_), custom_call_target="tpu_custom_call" | custom-call | tf_op jit(solution)/shard_map/pallas_call | solution.py:466
  61.4 0.6 collective-permute-done.9.refs_1_
  62.0 1.4 %shard_map.104 = (f32[4096,128]{1,0:T(8,128)}, f32[432,32]{1,0:T(8,128)}, f32[864,32]{1,0:T(8,128)}) custom-call(bf16[16,144,128]{2,1,0:T(8,128)(2,1)S(1)} %all-to-all-done.1.refs_0_, bf16[16,144,128]{2,1,0:T(8,128)(2,1)S(1)} %collective-permute-done.9.refs_1_, f32[4096,128]{1,0:T(8,128)} %shard_map.103.refs_2_), custom_call_target="tpu_custom_call", output_to_operand_aliasing={{0}: (2, {})} | custom-call | tf_op jit(solution)/shard_map/pallas_call | solution.py:474
Async XLA Ops:
  0.6 2.0 %copy-start = (f32[1,524288]{1,0:T(1,128)S(1)}, f32[1,524288]{1,0:T(1,128)}, u32[]{:S(2)}) copy-start(f32[1,524288]{1,0:T(1,128)} %param.11) | copy-start | bytes 6291460
  0.7 1.2 %copy-start.1 = (bf16[1,1,32,64,128]{4,3,2,1,0:T(8,128)(2,1)S(1)}, bf16[1,1,32,64,128]{4,3,2,1,0:T(8,128)(2,1)}, u32[]{:S(2)}) copy-start(bf16[1,1,32,64,128]{4,3,2,1,0:T(8,128)(2,1)} %param.8) | copy-start | bytes 1572868
  2.7 5.1 %copy-start.3 = (bf16[1,1,16,64,128]{4,3,2,1,0:T(8,128)(2,1)S(1)}, bf16[1,1,16,64,128]{4,3,2,1,0:T(8,128)(2,1)}, u32[]{:S(2)}) copy-start(bf16[1,1,16,64,128]{4,3,2,1,0:T(8,128)(2,1)} %param.6) | copy-start | bytes 786436
  2.7 9.3 %copy-start.2 = (bf16[1,1,32,64,128]{4,3,2,1,0:T(8,128)(2,1)S(1)}, bf16[1,1,32,64,128]{4,3,2,1,0:T(8,128)(2,1)}, u32[]{:S(2)}) copy-start(bf16[1,1,32,64,128]{4,3,2,1,0:T(8,128)(2,1)} %param.7) | copy-start | bytes 1572868
  2.7 9.3 %copy-start.4 = (bf16[3,3,3,32,32]{4,3,2,1,0:T(8,128)(2,1)S(1)}, bf16[3,3,3,32,32]{4,3,2,1,0:T(8,128)(2,1)}, u32[]{:S(2)}) copy-start(bf16[3,3,3,32,32]{4,3,2,1,0:T(8,128)(2,1)} %two.1) | copy-start | bytes 165892
  2.8 9.3 %copy-start.5 = (bf16[3,3,3,16,32]{4,3,2,1,0:T(8,128)(2,1)S(1)}, bf16[3,3,3,16,32]{4,3,2,1,0:T(8,128)(2,1)}, u32[]{:S(2)}) copy-start(bf16[3,3,3,16,32]{4,3,2,1,0:T(8,128)(2,1)} %one.1) | copy-start | bytes 82948
  2.9 4.8 %collective-permute-start = (bf16[2048,128]{1,0:T(8,128)(2,1)S(1)}, bf16[2048,128]{1,0:T(8,128)(2,1)S(1)}, u32[]{:S(2)}, u32[]{:S(2)}) collective-permute-start(bf16[2048,128]{1,0:T(8,128)(2,1)S(1)} %dynamic-slice_convert_fusion), channel_id=1, source_target_pairs={{0,1},{1,0},{2,3},{3,2},{4,5},{5,4},{6,7},{7,6},{8,9},{9,8},{10,11... | collective-permute-start | bytes 1572872 | tf_op jit(solution)/shard_map/ppermute | solution.py:140
  3.0 11.8 %collective-permute-start.5 = (bf16[2048,128]{1,0:T(8,128)(2,1)S(1)}, bf16[2048,128]{1,0:T(8,128)(2,1)S(1)}, u32[]{:S(2)}, u32[]{:S(2)}) collective-permute-start(bf16[2048,128]{1,0:T(8,128)(2,1)S(1)} %shard_map.93.pack_0), channel_id=1, source_target_pairs={{1,2},{2,1},{5,6},{6,5},{9,10},{10,9},{13,14},{14,13},{17,18},{18,... | collective-permute-start | bytes 1572872 | tf_op jit(solution)/shard_map/ppermute | solution.py:497
  7.6 7.1 %collective-permute-start.4 = (bf16[2048,128]{1,0:T(8,128)(2,1)S(1)}, bf16[2048,128]{1,0:T(8,128)(2,1)S(1)}, u32[]{:S(2)}, u32[]{:S(2)}) collective-permute-start(bf16[2048,128]{1,0:T(8,128)(2,1)S(1)} %shard_map.93.pack_0), channel_id=1, source_target_pairs={{0,1},{1,0},{2,3},{3,2},{4,5},{5,4},{6,7},{7,6},{8,9},{9,8},{10,11... | collective-permute-start | bytes 1572872 | tf_op jit(solution)/shard_map/ppermute | solution.py:140
  8.3 10.7 %collective-permute-start.3 = (bf16[1024,128]{1,0:T(8,128)(2,1)S(1)}, bf16[1024,128]{1,0:T(8,128)(2,1)S(1)}, u32[]{:S(2)}, u32[]{:S(2)}) collective-permute-start(bf16[1024,128]{1,0:T(8,128)(2,1)S(1)} %shard_map.95.pack_0), channel_id=1, source_target_pairs={{1,2},{2,1},{5,6},{6,5},{9,10},{10,9},{13,14},{14,13},{17,18},{18,... | collective-permute-start | bytes 786440 | tf_op jit(solution)/shard_map/ppermute | solution.py:497
  10.2 8.8 %collective-permute-start.2 = (bf16[1024,128]{1,0:T(8,128)(2,1)S(1)}, bf16[1024,128]{1,0:T(8,128)(2,1)S(1)}, u32[]{:S(2)}, u32[]{:S(2)}) collective-permute-start(bf16[1024,128]{1,0:T(8,128)(2,1)S(1)} %shard_map.95.pack_0), channel_id=1, source_target_pairs={{0,1},{1,0},{2,3},{3,2},{4,5},{5,4},{6,7},{7,6},{8,9},{9,8},{10,11... | collective-permute-start | bytes 786440 | tf_op jit(solution)/shard_map/ppermute | solution.py:140
  10.3 9.6 %collective-permute-start.1 = (bf16[1024,128]{1,0:T(8,128)(2,1)S(1)}, bf16[1024,128]{1,0:T(8,128)(2,1)S(1)}, u32[]{:S(2)}, u32[]{:S(2)}) collective-permute-start(bf16[1024,128]{1,0:T(8,128)(2,1)S(1)} %get-tuple-element.44.refs_0_), channel_id=1, source_target_pairs={{0,4},{4,0},{1,5},{5,1},{2,6},{6,2},{3,7},{7,3},{8,12},{12,8},{9,1... | collective-permute-start | bytes 786440 | tf_op jit(solution)/shard_map/ppermute | solution.py:140
  18.3 0.7 %copy-start.6 = (bf16[1024,128]{1,0:T(8,128)(2,1)}, bf16[1024,128]{1,0:T(8,128)(2,1)S(1)}, u32[]{:S(2)}) copy-start(bf16[1024,128]{1,0:T(8,128)(2,1)S(1)} %get-tuple-element.63) | copy-start | bytes 786436
  19.9 1.3 %collective-permute-start.6 = (bf16[256,128]{1,0:T(8,128)(2,1)S(1)}, bf16[256,128]{1,0:T(8,128)(2,1)S(1)}, u32[]{:S(2)}, u32[]{:S(2)}) collective-permute-start(bf16[256,128]{1,0:T(8,128)(2,1)S(1)} %get-tuple-element.55), channel_id=1, source_target_pairs={{0,1},{1,0},{2,3},{3,2},{4,5},{5,4},{6,7},{7,6},{8,9},{9,8},{10,11... | collective-permute-start | bytes 196616 | tf_op jit(solution)/shard_map/ppermute | solution.py:140
  38.0 19.8 %all-to-all-start.1 = ((bf16[16,144,128]{2,1,0:T(8,128)(2,1)}), bf16[16,144,128]{2,1,0:T(8,128)(2,1)S(1)}, u32[]{:S(2)}, u32[]{:S(2)}) async-start(bf16[16,144,128]{2,1,0:T(8,128)(2,1)} %shard_map.101), calls=%async_computation.1 | async-start | bytes 1179648 | tf_op jit(solution)/shard_map/all_to_all | solution.py:532
  42.8 5.1 %collective-permute-start.7 = (bf16[1024,128]{1,0:T(8,128)(2,1)}, bf16[1024,128]{1,0:T(8,128)(2,1)S(1)}, u32[]{:S(2)}, u32[]{:S(2)}) collective-permute-start(bf16[1024,128]{1,0:T(8,128)(2,1)} %copy-done.6), channel_id=1, source_target_pairs={{0,1},{1,0},{2,3},{3,2},{4,5},{5,4},{6,7},{7,6},{8,9},{9,8},{10,11... | collective-permute-start | bytes 786440 | tf_op jit(solution)/shard_map/ppermute | solution.py:140
  44.5 10.0 %collective-permute-start.8 = (bf16[1024,128]{1,0:T(8,128)(2,1)S(1)}, bf16[1024,128]{1,0:T(8,128)(2,1)S(1)}, u32[]{:S(2)}, u32[]{:S(2)}) collective-permute-start(bf16[1024,128]{1,0:T(8,128)(2,1)S(1)} %get-tuple-element.64), channel_id=1, source_target_pairs={{1,2},{2,1},{5,6},{6,5},{9,10},{10,9},{13,14},{14,13},{17,18},{18,... | collective-permute-start | bytes 786440 | tf_op jit(solution)/shard_map/ppermute | solution.py:497
  57.8 4.2 %collective-permute-start.9 = (bf16[16,144,128]{2,1,0:T(8,128)(2,1)S(1)}, bf16[16,144,128]{2,1,0:T(8,128)(2,1)S(1)}, u32[]{:S(2)}, u32[]{:S(2)}) collective-permute-start(bf16[16,144,128]{2,1,0:T(8,128)(2,1)S(1)} %all-to-all-done.1.refs_0_), channel_id=1, source_target_pairs={{0,1},{1,0},{2,3},{3,2},{4,5},{5,4},{6,7},{7,6},{8,9},{9,8},{10,11... | collective-permute-start | bytes 1769480 | tf_op jit(solution)/shard_map/ppermute | solution.py:140

commit v20 on v18

--- a/solution.py
+++ b/solution.py
@@ -321,7 +321,7 @@
     return vmem_call(
         input_kernel,
         (
-            jax.ShapeDtypeStruct(plane, F32),
+            jax.ShapeDtypeStruct(plane, BF16),
             jax.ShapeDtypeStruct(plane, BF16),
             jax.ShapeDtypeStruct(plane, BF16),
         ),
@@ -335,7 +335,7 @@
 
     def add(step, carry):
         at = pl.ds(pl.multiple_of(step * 64, 64), 64)
-        flat[at, :] = own[at, :] + first[at, :].astype(F32) + second[at, :].astype(F32)
+        flat[at, :] = own[at, :].astype(F32) + first[at, :].astype(F32) + second[at, :].astype(F32)
         return carry
 
     lax.fori_loop(0, own.shape[0] // 64, add, 0, unroll=4)

time: 63.4 us -> 62.7 us (0.989)
  local copies, waits for them, and re-layouts: 2.06 us -> 1.35 us
    unnamed x14 -> x12, local copies, waits for them, and re-layouts: 1.92 us -> 1.21 us
  transfers between devices with their start and end apart: 11 -> 11, of which waited for: 5 -> 6; matrix products, arithmetic and copies ran while one was open for 0% -> 0% of each run, Pallas kernels for 13% -> 13%
where the time goes in v20:
time: 62.7 us; the launch traced here: 62.1 us
  starting transfers between devices  20.5 us (33%)
  blocking collectives  16.4 us (26%)
  waiting for transfers between devices  11.8 us (19%)
  Pallas kernels  11.1 us (18%)
  local copies, waits for them, and re-layouts  1.35 us (2%)
  between operations  0.85 us (1%)
    all_to_all x1, blocking collectives, per_device(): parts = lax.all_to_all(parts, SAME, 0, 0)  16.4 us
    ppermute x3, starting transfers between devices, crossed(): return lax.ppermute(value, SPACE, pairs + [(m, n) for n, m in pairs])  9.81 us
    ppermute x3, waiting for transfers between devices, crossed(): return lax.ppermute(value, SPACE, pairs + [(m, n) for n, m in pairs])  8.75 us
    ppermute x7, starting transfers between devices, swapped(): return lax.ppermute(value, axis, [(0, 1), (1, 0)])  6.4 us
    all_to_all x1, starting transfers between devices, per_device(): mine = lax.all_to_all(shares, SAME, 0, 0)  4.29 us
    pallas_call x1, Pallas kernels, first_part(): vmem_call(first_kernel, (jax.ShapeDtypeStruct(((length + 2) * 3 * c1, wid...  2.57 us
    all_to_all x1, waiting for transfers between devices, per_device(): mine = lax.all_to_all(shares, SAME, 0, 0)  2.27 us
    pallas_call x1, Pallas kernels, finish(): pl.pallas_call(lambda *refs: finish_kernel(sizes, height, padded, *refs),...  1.37 us
  transfers between devices with their start and end apart: 11, of which 6 were waited for; matrix products, arithmetic and copies ran while one was open for 0% of the time, Pallas kernels for 13%

profile of v20, /device:TPU:1, one launch (start us, length us, event | category | flops | bytes accessed | tf_op | source)
XLA Modules:
  0.0 62.1 jit_solution(12199739209406869435)
XLA Ops:
  0.6 0.0 copy-start
  0.7 0.0 copy-start.1
  0.7 1.2 %copy-done.1 = bf16[1,1,32,64,128]{4,3,2,1,0:T(8,128)(2,1)S(1)} copy-done((bf16[1,1,32,64,128]{4,3,2,1,0:T(8,128)(2,1)S(1)}, bf16[1,1,32,64,128]{4,3,2,1,0:T(8,128)(2,1)}, u32[]{:S(2)}) %copy-start.1) | copy-done | bytes 524312
  1.8 0.0 copy-start.3
  1.8 0.8 %shard_map.93.refs_0_.pack_0 = bf16[2048,128]{1,0:T(8,128)(2,1)S(1)} custom-call(bf16[32,64,128]{2,1,0:T(8,128)(2,1)S(1)} %bitcast.10), custom_call_target="tpu_custom_call" | custom-call | bytes 67108864 | tf_op jit(solution)/shard_map/pallas_call | solution.py:59
  2.6 0.0 copy-done
  2.6 0.1 dynamic-slice_convert_fusion
  2.7 0.0 copy-start.2
  2.7 0.0 copy-start.4
  2.7 0.0 copy-start.5
  2.8 0.1 constant_dynamic-slice_fusion.own
  2.8 0.1 collective-permute-start
  3.0 4.6 %collective-permute-start.5 = (bf16[2048,128]{1,0:T(8,128)(2,1)S(1)}, bf16[2048,128]{1,0:T(8,128)(2,1)S(1)}, u32[]{:S(2)}, u32[]{:S(2)}) collective-permute-start(bf16[2048,128]{1,0:T(8,128)(2,1)S(1)} %shard_map.93.refs_0_.pack_0), channel_id=1, source_target_pairs={{1,2},{2,1},{5,6},{6,5},{9,10},{10,9},{13,14},{14,13},{17,18},{18,... | collective-permute-start | bytes 1572872 | tf_op jit(solution)/shard_map/ppermute | solution.py:497
  7.6 0.1 collective-permute-start.4
  7.7 0.0 copy-done.3
  7.7 0.5 shard_map.95.pack_0
  8.2 1.9 %collective-permute-start.3 = (bf16[1024,128]{1,0:T(8,128)(2,1)S(1)}, bf16[1024,128]{1,0:T(8,128)(2,1)S(1)}, u32[]{:S(2)}, u32[]{:S(2)}) collective-permute-start(bf16[1024,128]{1,0:T(8,128)(2,1)S(1)} %shard_map.95.pack_0), channel_id=1, source_target_pairs={{1,2},{2,1},{5,6},{6,5},{9,10},{10,9},{13,14},{14,13},{17,18},{18,... | collective-permute-start | bytes 786440 | tf_op jit(solution)/shard_map/ppermute | solution.py:497
  10.1 0.1 collective-permute-start.2
  10.2 0.0 collective-permute-done.other
  10.2 0.1 shard_map.94
  10.3 1.7 %collective-permute-start.1 = (bf16[1024,128]{1,0:T(8,128)(2,1)S(1)}, bf16[1024,128]{1,0:T(8,128)(2,1)S(1)}, u32[]{:S(2)}, u32[]{:S(2)}) collective-permute-start(bf16[1024,128]{1,0:T(8,128)(2,1)S(1)} %get-tuple-element.42), channel_id=1, source_target_pairs={{0,4},{4,0},{1,5},{5,1},{2,6},{6,2},{3,7},{7,3},{8,12},{12,8},{9,1... | collective-permute-start | bytes 786440 | tf_op jit(solution)/shard_map/ppermute | solution.py:140
  12.0 0.0 copy-done.2
  12.0 0.0 copy-done.4
  12.0 0.0 copy-done.5
  12.0 0.9 %shard_map.96 = (bf16[2048,128]{1,0:T(8,128)(2,1)S(1)}, bf16[96,288]{1,0:T(8,128)(2,1)S(1)}, bf16[48,288]{1,0:T(8,128)(2,1)S(1)}) custom-call(bf16[32,64,128]{2,1,0:T(8,128)(2,1)S(1)} %bitcast.11, bf16[3,3,3,32,32]{4,3,2,1,0:T(8,128)(2,1)S(1)} %copy-done.4, bf16[3,3,3,16,32]{4,3,2,1,0:T(8,128)(2,1)S(1)} %copy-done.5), custom_call_target="tpu_custom_call" | custom-call | bytes 4194304 | tf_op jit(solution)/shard_map/pallas_call | solution.py:199
  13.0 1.8 %collective-permute-done.5.pack_out = bf16[2048,128]{1,0:T(8,128)(2,1)S(1)} collective-permute-done((bf16[2048,128]{1,0:T(8,128)(2,1)S(1)}, bf16[2048,128]{1,0:T(8,128)(2,1)S(1)}, u32[]{:S(2)}, u32[]{:S(2)}) %collective-permute-start.5) | collective-permute-done | bytes 524320 | tf_op jit(solution)/shard_map/ppermute | solution.py:497
  14.7 0.0 collective-permute-done.4.pack_in
  14.7 2.6 %shard_map.97 = (bf16[6336,128]{1,0:T(8,128)(2,1)S(1)}, f32[288,128]{1,0:T(8,128)S(1)}) custom-call(bf16[2048,128]{1,0:T(8,128)(2,1)S(1)} %collective-permute-done.4.pack_in, bf16[2048,128]{1,0:T(8,128)(2,1)S(1)} %shard_map.93.refs_0_.pack_0, bf16[2048,128]{1,0:T(8,128)(2,1)S(1)} %collective-permute-done.5.pack_out, ...), custom_call_target="tpu_custom_call" | custom-call | flops 1000000000 | bytes 20971520 | tf_op jit(solution)/shard_map/pallas_call | solution.py:293
  17.3 0.2 collective-permute-done.3.pack_out
  17.6 0.0 collective-permute-done.2.pack_in
  17.6 0.8 %shard_map.98 = (bf16[256,128]{1,0:T(8,128)(2,1)S(1)}, f32[256,128]{1,0:T(8,128)S(1)}) custom-call(bf16[1024,128]{1,0:T(8,128)(2,1)S(1)} %collective-permute-done.2.pack_in, bf16[1024,128]{1,0:T(8,128)(2,1)S(1)} %shard_map.95.pack_0, bf16[1024,128]{1,0:T(8,128)(2,1)S(1)} %collective-permute-done.3.pack_out, bf16[6336,128]{1,0:T(8,128)(2,1)S(1)} %get-tuple-element.47.pres, ...), custom_call_target="tpu_custom_call" | custom-call | flops 1000000000 | bytes 5242880 | tf_op jit(solution)/shard_map/pallas_call | solution.py:307
  18.4 0.1 collective-permute-start.6
  18.4 1.0 %shard_map.100 = (bf16[1024,128]{1,0:T(8,128)(2,1)S(1)}, bf16[1024,128]{1,0:T(8,128)(2,1)S(1)}, bf16[1024,128]{1,0:T(8,128)(2,1)S(1)}) custom-call(bf16[6336,128]{1,0:T(8,128)(2,1)S(1)} %get-tuple-element.47.pres, bf16[48,288]{1,0:T(8,128)(2,1)S(1)} %get-tuple-element.51.w_one), custom_call_target="tpu_custom_call" | custom-call | flops 1000000000 | bytes 5242880 | tf_op jit(solution)/shard_map/pallas_call | solution.py:321
  19.5 0.2 collective-permute-done.6.more
  19.7 0.0 collective-permute-done.1.other
  19.7 0.1 shard_map.99
  19.8 16.4 %all_to_all.10.refs_0_ = bf16[16,80,128]{2,1,0:T(8,128)(2,1)S(1)} all-to-all(bf16[16,80,128]{2,1,0:T(8,128)(2,1)S(1)} %shard_map.99), channel_id=1, replica_groups=mesh['z'=4,'x'=2,'y'=2,'core'=2] {'x','z','y'}, dimensions={0} | all-to-all | bytes 655360 | tf_op jit(solution)/shard_map/all_to_all | solution.py:526
  36.1 1.0 %shard_map.101 = bf16[16,144,128]{2,1,0:T(8,128)(2,1)} custom-call(bf16[16,80,128]{2,1,0:T(8,128)(2,1)S(1)} %all_to_all.10.refs_0_), custom_call_target="tpu_custom_call" | custom-call | flops 163840 | bytes 983040 | tf_op jit(solution)/shard_map/pallas_call | solution.py:377
  37.1 4.3 %all-to-all-start.1 = ((bf16[16,144,128]{2,1,0:T(8,128)(2,1)}), bf16[16,144,128]{2,1,0:T(8,128)(2,1)S(1)}, u32[]{:S(2)}, u32[]{:S(2)}) async-start(bf16[16,144,128]{2,1,0:T(8,128)(2,1)} %shard_map.101), calls=%async_computation.1 | async-start | bytes 1179648 | tf_op jit(solution)/shard_map/all_to_all | solution.py:531
  41.4 1.8 %collective-permute-start.7 = (bf16[1024,128]{1,0:T(8,128)(2,1)S(1)}, bf16[1024,128]{1,0:T(8,128)(2,1)S(1)}, u32[]{:S(2)}, u32[]{:S(2)}) collective-permute-start(bf16[1024,128]{1,0:T(8,128)(2,1)S(1)} %get-tuple-element.59), channel_id=1, source_target_pairs={{0,1},{1,0},{2,3},{3,2},{4,5},{5,4},{6,7},{7,6},{8,9},{9,8},{10,11... | collective-permute-start | bytes 786440 | tf_op jit(solution)/shard_map/ppermute | solution.py:140
  43.2 3.3 %collective-permute-start.8 = (bf16[1024,128]{1,0:T(8,128)(2,1)S(1)}, bf16[1024,128]{1,0:T(8,128)(2,1)S(1)}, u32[]{:S(2)}, u32[]{:S(2)}) collective-permute-start(bf16[1024,128]{1,0:T(8,128)(2,1)S(1)} %get-tuple-element.60), channel_id=1, source_target_pairs={{1,2},{2,1},{5,6},{6,5},{9,10},{10,9},{13,14},{14,13},{17,18},{18,... | collective-permute-start | bytes 786440 | tf_op jit(solution)/shard_map/ppermute | solution.py:497
  46.5 0.0 collective-permute-done.7.first
  46.5 6.7 %collective-permute-done.8.second = bf16[1024,128]{1,0:T(8,128)(2,1)S(1)} collective-permute-done((bf16[1024,128]{1,0:T(8,128)(2,1)S(1)}, bf16[1024,128]{1,0:T(8,128)(2,1)S(1)}, u32[]{:S(2)}, u32[]{:S(2)}) %collective-permute-start.8) | collective-permute-done | bytes 262176 | tf_op jit(solution)/shard_map/ppermute | solution.py:497
  53.2 1.0 %shard_map.102 = bf16[16,64,128]{2,1,0:T(8,128)(2,1)} custom-call(bf16[1024,128]{1,0:T(8,128)(2,1)S(1)} %get-tuple-element.58.own, bf16[1024,128]{1,0:T(8,128)(2,1)S(1)} %collective-permute-done.7.first, bf16[1024,128]{1,0:T(8,128)(2,1)S(1)} %collective-permute-done.8.second), custom_call_target="tpu_custom_call" | custom-call | flops 262144 | bytes 1048576 | tf_op jit(solution)/shard_map/pallas_call | solution.py:351
  54.2 2.3 %all-to-all-done.1.refs_0_ = bf16[16,144,128]{2,1,0:T(8,128)(2,1)S(1)} async-done(((bf16[16,144,128]{2,1,0:T(8,128)(2,1)}), bf16[16,144,128]{2,1,0:T(8,128)(2,1)S(1)}, u32[]{:S(2)}, u32[]{:S(2)}) %all-to-all-start.1) | async-done | bytes 589856 | tf_op jit(solution)/shard_map/all_to_all | solution.py:531
  56.5 2.6 %collective-permute-start.9 = (bf16[16,144,128]{2,1,0:T(8,128)(2,1)S(1)}, bf16[16,144,128]{2,1,0:T(8,128)(2,1)S(1)}, u32[]{:S(2)}, u32[]{:S(2)}) collective-permute-start(bf16[16,144,128]{2,1,0:T(8,128)(2,1)S(1)} %all-to-all-done.1.refs_0_), channel_id=1, source_target_pairs={{0,1},{1,0},{2,3},{3,2},{4,5},{5,4},{6,7},{7,6},{8,9},{9,8},{10,11... | collective-permute-start | bytes 1769480 | tf_op jit(solution)/shard_map/ppermute | solution.py:140
  59.0 1.0 %shard_map.103.refs_2_ = f32[4096,128]{1,0:T(8,128)} custom-call(bf16[16,144,128]{2,1,0:T(8,128)(2,1)S(1)} %all-to-all-done.1.refs_0_), custom_call_target="tpu_custom_call" | custom-call | tf_op jit(solution)/shard_map/pallas_call | solution.py:466
  60.1 0.6 collective-permute-done.9.refs_1_
  60.7 1.4 %shard_map.104 = (f32[4096,128]{1,0:T(8,128)}, f32[432,32]{1,0:T(8,128)}, f32[864,32]{1,0:T(8,128)}) custom-call(bf16[16,144,128]{2,1,0:T(8,128)(2,1)S(1)} %all-to-all-done.1.refs_0_, bf16[16,144,128]{2,1,0:T(8,128)(2,1)S(1)} %collective-permute-done.9.refs_1_, f32[4096,128]{1,0:T(8,128)} %shard_map.103.refs_2_), custom_call_target="tpu_custom_call", output_to_operand_aliasing={{0}: (2, {})} | custom-call | tf_op jit(solution)/shard_map/pallas_call | solution.py:474
Async XLA Ops:
  0.6 2.0 %copy-start = (f32[1,524288]{1,0:T(1,128)S(1)}, f32[1,524288]{1,0:T(1,128)}, u32[]{:S(2)}) copy-start(f32[1,524288]{1,0:T(1,128)} %param.11) | copy-start | bytes 6291460
  0.7 1.2 %copy-start.1 = (bf16[1,1,32,64,128]{4,3,2,1,0:T(8,128)(2,1)S(1)}, bf16[1,1,32,64,128]{4,3,2,1,0:T(8,128)(2,1)}, u32[]{:S(2)}) copy-start(bf16[1,1,32,64,128]{4,3,2,1,0:T(8,128)(2,1)} %param.8) | copy-start | bytes 1572868
  1.8 5.8 %copy-start.3 = (bf16[1,1,16,64,128]{4,3,2,1,0:T(8,128)(2,1)S(1)}, bf16[1,1,16,64,128]{4,3,2,1,0:T(8,128)(2,1)}, u32[]{:S(2)}) copy-start(bf16[1,1,16,64,128]{4,3,2,1,0:T(8,128)(2,1)} %param.6) | copy-start | bytes 786436
  2.7 9.3 %copy-start.2 = (bf16[1,1,32,64,128]{4,3,2,1,0:T(8,128)(2,1)S(1)}, bf16[1,1,32,64,128]{4,3,2,1,0:T(8,128)(2,1)}, u32[]{:S(2)}) copy-start(bf16[1,1,32,64,128]{4,3,2,1,0:T(8,128)(2,1)} %param.7) | copy-start | bytes 1572868
  2.7 9.3 %copy-start.4 = (bf16[3,3,3,32,32]{4,3,2,1,0:T(8,128)(2,1)S(1)}, bf16[3,3,3,32,32]{4,3,2,1,0:T(8,128)(2,1)}, u32[]{:S(2)}) copy-start(bf16[3,3,3,32,32]{4,3,2,1,0:T(8,128)(2,1)} %two.1) | copy-start | bytes 165892
  2.7 9.3 %copy-start.5 = (bf16[3,3,3,16,32]{4,3,2,1,0:T(8,128)(2,1)S(1)}, bf16[3,3,3,16,32]{4,3,2,1,0:T(8,128)(2,1)}, u32[]{:S(2)}) copy-start(bf16[3,3,3,16,32]{4,3,2,1,0:T(8,128)(2,1)} %one.1) | copy-start | bytes 82948
  2.8 7.3 %collective-permute-start = (bf16[2048,128]{1,0:T(8,128)(2,1)S(1)}, bf16[2048,128]{1,0:T(8,128)(2,1)S(1)}, u32[]{:S(2)}, u32[]{:S(2)}) collective-permute-start(bf16[2048,128]{1,0:T(8,128)(2,1)S(1)} %dynamic-slice_convert_fusion), channel_id=1, source_target_pairs={{0,1},{1,0},{2,3},{3,2},{4,5},{5,4},{6,7},{7,6},{8,9},{9,8},{10,11... | collective-permute-start | bytes 1572872 | tf_op jit(solution)/shard_map/ppermute | solution.py:140
  3.0 11.8 %collective-permute-start.5 = (bf16[2048,128]{1,0:T(8,128)(2,1)S(1)}, bf16[2048,128]{1,0:T(8,128)(2,1)S(1)}, u32[]{:S(2)}, u32[]{:S(2)}) collective-permute-start(bf16[2048,128]{1,0:T(8,128)(2,1)S(1)} %shard_map.93.refs_0_.pack_0), channel_id=1, source_target_pairs={{1,2},{2,1},{5,6},{6,5},{9,10},{10,9},{13,14},{14,13},{17,18},{18,... | collective-permute-start | bytes 1572872 | tf_op jit(solution)/shard_map/ppermute | solution.py:497
  7.6 7.1 %collective-permute-start.4 = (bf16[2048,128]{1,0:T(8,128)(2,1)S(1)}, bf16[2048,128]{1,0:T(8,128)(2,1)S(1)}, u32[]{:S(2)}, u32[]{:S(2)}) collective-permute-start(bf16[2048,128]{1,0:T(8,128)(2,1)S(1)} %shard_map.93.refs_0_.pack_0), channel_id=1, source_target_pairs={{0,1},{1,0},{2,3},{3,2},{4,5},{5,4},{6,7},{7,6},{8,9},{9,8},{10,11... | collective-permute-start | bytes 1572872 | tf_op jit(solution)/shard_map/ppermute | solution.py:140
  8.2 9.4 %collective-permute-start.3 = (bf16[1024,128]{1,0:T(8,128)(2,1)S(1)}, bf16[1024,128]{1,0:T(8,128)(2,1)S(1)}, u32[]{:S(2)}, u32[]{:S(2)}) collective-permute-start(bf16[1024,128]{1,0:T(8,128)(2,1)S(1)} %shard_map.95.pack_0), channel_id=1, source_target_pairs={{1,2},{2,1},{5,6},{6,5},{9,10},{10,9},{13,14},{14,13},{17,18},{18,... | collective-permute-start | bytes 786440 | tf_op jit(solution)/shard_map/ppermute | solution.py:497
  10.1 7.5 %collective-permute-start.2 = (bf16[1024,128]{1,0:T(8,128)(2,1)S(1)}, bf16[1024,128]{1,0:T(8,128)(2,1)S(1)}, u32[]{:S(2)}, u32[]{:S(2)}) collective-permute-start(bf16[1024,128]{1,0:T(8,128)(2,1)S(1)} %shard_map.95.pack_0), channel_id=1, source_target_pairs={{0,1},{1,0},{2,3},{3,2},{4,5},{5,4},{6,7},{7,6},{8,9},{9,8},{10,11... | collective-permute-start | bytes 786440 | tf_op jit(solution)/shard_map/ppermute | solution.py:140
  10.3 9.4 %collective-permute-start.1 = (bf16[1024,128]{1,0:T(8,128)(2,1)S(1)}, bf16[1024,128]{1,0:T(8,128)(2,1)S(1)}, u32[]{:S(2)}, u32[]{:S(2)}) collective-permute-start(bf16[1024,128]{1,0:T(8,128)(2,1)S(1)} %get-tuple-element.42), channel_id=1, source_target_pairs={{0,4},{4,0},{1,5},{5,1},{2,6},{6,2},{3,7},{7,3},{8,12},{12,8},{9,1... | collective-permute-start | bytes 786440 | tf_op jit(solution)/shard_map/ppermute | solution.py:140
  18.4 1.3 %collective-permute-start.6 = (bf16[256,128]{1,0:T(8,128)(2,1)S(1)}, bf16[256,128]{1,0:T(8,128)(2,1)S(1)}, u32[]{:S(2)}, u32[]{:S(2)}) collective-permute-start(bf16[256,128]{1,0:T(8,128)(2,1)S(1)} %get-tuple-element.50), channel_id=1, source_target_pairs={{0,1},{1,0},{2,3},{3,2},{4,5},{5,4},{6,7},{7,6},{8,9},{9,8},{10,11... | collective-permute-start | bytes 196616 | tf_op jit(solution)/shard_map/ppermute | solution.py:140
  37.1 19.4 %all-to-all-start.1 = ((bf16[16,144,128]{2,1,0:T(8,128)(2,1)}), bf16[16,144,128]{2,1,0:T(8,128)(2,1)S(1)}, u32[]{:S(2)}, u32[]{:S(2)}) async-start(bf16[16,144,128]{2,1,0:T(8,128)(2,1)} %shard_map.101), calls=%async_computation.1 | async-start | bytes 1179648 | tf_op jit(solution)/shard_map/all_to_all | solution.py:531
  41.4 5.1 %collective-permute-start.7 = (bf16[1024,128]{1,0:T(8,128)(2,1)S(1)}, bf16[1024,128]{1,0:T(8,128)(2,1)S(1)}, u32[]{:S(2)}, u32[]{:S(2)}) collective-permute-start(bf16[1024,128]{1,0:T(8,128)(2,1)S(1)} %get-tuple-element.59), channel_id=1, source_target_pairs={{0,1},{1,0},{2,3},{3,2},{4,5},{5,4},{6,7},{7,6},{8,9},{9,8},{10,11... | collective-permute-start | bytes 786440 | tf_op jit(solution)/shard_map/ppermute | solution.py:140
  43.2 10.0 %collective-permute-start.8 = (bf16[1024,128]{1,0:T(8,128)(2,1)S(1)}, bf16[1024,128]{1,0:T(8,128)(2,1)S(1)}, u32[]{:S(2)}, u32[]{:S(2)}) collective-permute-start(bf16[1024,128]{1,0:T(8,128)(2,1)S(1)} %get-tuple-element.60), channel_id=1, source_target_pairs={{1,2},{2,1},{5,6},{6,5},{9,10},{10,9},{13,14},{14,13},{17,18},{18,... | collective-permute-start | bytes 786440 | tf_op jit(solution)/shard_map/ppermute | solution.py:497
  56.5 4.2 %collective-permute-start.9 = (bf16[16,144,128]{2,1,0:T(8,128)(2,1)S(1)}, bf16[16,144,128]{2,1,0:T(8,128)(2,1)S(1)}, u32[]{:S(2)}, u32[]{:S(2)}) collective-permute-start(bf16[16,144,128]{2,1,0:T(8,128)(2,1)S(1)} %all-to-all-done.1.refs_0_), channel_id=1, source_target_pairs={{0,1},{1,0},{2,3},{3,2},{4,5},{5,4},{6,7},{7,6},{8,9},{9,8},{10,11... | collective-permute-start | bytes 1769480 | tf_op jit(solution)/shard_map/ppermute | solution.py:140

commit v21 on v20

--- a/solution.py
+++ b/solution.py
@@ -508,7 +508,7 @@
     send = lax.dynamic_slice_in_dim(bucket, (1 - core) * half, half).astype(BF16)
     near = lax.dynamic_slice_in_dim(bucket, core * half, half)
     cot, send, near = lax.optimization_barrier((cot, send, near))
-    cots = (swapped(cot), cot, crossed(cot))
+    cots = (swapped(cot), cot, pack(crossed(out_cot[0, 0]), [], 16))
     vol = pack(volume_in[0, 0], [cot], 16)
     vols = (swapped(vol), vol, crossed(vol))
     send, near = add(near, swapped(send))

time: 62.7 us -> 63.2 us (level)
  Pallas kernels: 11.1 us -> 11.9 us
    pallas_call x2 -> x3, Pallas kernels: 1.25 us -> 2.03 us  [pack(): pl.pallas_call(pack_kernel, out_shape=jax.ShapeDtypeStruct((length * chan...]
    unnamed x12 -> x14, local copies, waits for them, and re-layouts: 1.21 us -> 1.27 us
  transfers between devices with their start and end apart: 11 -> 11, of which waited for: 6 -> 5; matrix products, arithmetic and copies ran while one was open for 0% -> 0% of each run, Pallas kernels for 13% -> 14%
where the time goes in v21:
time: 63.2 us; the launch traced here: 62.6 us
  starting transfers between devices  20.4 us (32%)
  blocking collectives  16.4 us (26%)
  Pallas kernels  11.9 us (19%)
  waiting for transfers between devices  11.5 us (18%)
  local copies, waits for them, and re-layouts  1.41 us (2%)
  between operations  0.88 us (1%)
    all_to_all x1, blocking collectives, per_device(): parts = lax.all_to_all(parts, SAME, 0, 0)  16.4 us
    ppermute x3, starting transfers between devices, crossed(): return lax.ppermute(value, SPACE, pairs + [(m, n) for n, m in pairs])  9.71 us
    ppermute x3, waiting for transfers between devices, crossed(): return lax.ppermute(value, SPACE, pairs + [(m, n) for n, m in pairs])  8.48 us
    ppermute x7, starting transfers between devices, swapped(): return lax.ppermute(value, axis, [(0, 1), (1, 0)])  6.45 us
    all_to_all x1, starting transfers between devices, per_device(): mine = lax.all_to_all(shares, SAME, 0, 0)  4.29 us
    pallas_call x1, Pallas kernels, first_part(): vmem_call(first_kernel, (jax.ShapeDtypeStruct(((length + 2) * 3 * c1, wid...  2.56 us
    all_to_all x1, waiting for transfers between devices, per_device(): mine = lax.all_to_all(shares, SAME, 0, 0)  2.27 us
    pallas_call x3, Pallas kernels, pack(): pl.pallas_call(pack_kernel, out_shape=jax.ShapeDtypeStruct((length * chan...  2.03 us
  transfers between devices with their start and end apart: 11, of which 5 were waited for; matrix products, arithmetic and copies ran while one was open for 0% of the time, Pallas kernels for 14%

profile of v21, /device:TPU:1, one launch (start us, length us, event | category | flops | bytes accessed | tf_op | source)
XLA Modules:
  0.0 62.6 jit_solution(5243524043226218835)
XLA Ops:
  0.6 0.0 copy-start
  0.7 0.0 copy-start.2
  0.7 1.2 %copy-done.2 = bf16[1,1,32,64,128]{4,3,2,1,0:T(8,128)(2,1)S(1)} copy-done((bf16[1,1,32,64,128]{4,3,2,1,0:T(8,128)(2,1)S(1)}, bf16[1,1,32,64,128]{4,3,2,1,0:T(8,128)(2,1)}, u32[]{:S(2)}) %copy-start.2) | copy-done | bytes 524312
  1.8 0.0 copy-start.3
  1.8 0.0 copy-start.4
  1.8 0.8 %shard_map.93.refs_0_.pack_0 = bf16[2048,128]{1,0:T(8,128)(2,1)S(1)} custom-call(bf16[32,64,128]{2,1,0:T(8,128)(2,1)S(1)} %bitcast.11), custom_call_target="tpu_custom_call" | custom-call | bytes 67108864 | tf_op jit(solution)/shard_map/pallas_call | solution.py:59
  2.6 0.0 copy-done
  2.6 0.1 dynamic-slice_convert_fusion
  2.7 0.0 copy-start.1
  2.7 0.0 copy-start.5
  2.7 0.0 copy-start.6
  2.8 0.1 constant_dynamic-slice_fusion.own
  2.8 0.1 collective-permute-start
  3.0 0.1 copy-done.3
  3.0 4.5 %collective-permute-start.5 = (bf16[32,64,128]{2,1,0:T(8,128)(2,1)S(1)}, bf16[32,64,128]{2,1,0:T(8,128)(2,1)S(1)}, u32[]{:S(2)}, u32[]{:S(2)}) collective-permute-start(bf16[32,64,128]{2,1,0:T(8,128)(2,1)S(1)} %bitcast.12), channel_id=1, source_target_pairs={{1,2},{2,1},{5,6},{6,5},{9,10},{10,9},{13,14},{14,13},{17,18},{18,... | collective-permute-start | bytes 1572872 | tf_op jit(solution)/shard_map/ppermute | solution.py:497
  7.6 0.1 collective-permute-start.4
  7.6 0.0 copy-done.4
  7.6 0.5 shard_map.95.pack_0
  8.1 1.9 %collective-permute-start.3 = (bf16[1024,128]{1,0:T(8,128)(2,1)S(1)}, bf16[1024,128]{1,0:T(8,128)(2,1)S(1)}, u32[]{:S(2)}, u32[]{:S(2)}) collective-permute-start(bf16[1024,128]{1,0:T(8,128)(2,1)S(1)} %shard_map.95.pack_0), channel_id=1, source_target_pairs={{1,2},{2,1},{5,6},{6,5},{9,10},{10,9},{13,14},{14,13},{17,18},{18,... | collective-permute-start | bytes 786440 | tf_op jit(solution)/shard_map/ppermute | solution.py:497
  10.0 0.1 collective-permute-start.2
  10.1 0.0 collective-permute-done.other
  10.1 0.1 shard_map.94
  10.3 1.8 %collective-permute-start.1 = (bf16[1024,128]{1,0:T(8,128)(2,1)S(1)}, bf16[1024,128]{1,0:T(8,128)(2,1)S(1)}, u32[]{:S(2)}, u32[]{:S(2)}) collective-permute-start(bf16[1024,128]{1,0:T(8,128)(2,1)S(1)} %get-tuple-element.42), channel_id=1, source_target_pairs={{0,4},{4,0},{1,5},{5,1},{2,6},{6,2},{3,7},{7,3},{8,12},{12,8},{9,1... | collective-permute-start | bytes 786440 | tf_op jit(solution)/shard_map/ppermute | solution.py:140
  12.0 0.0 copy-done.1
  12.0 0.0 copy-done.5
  12.0 0.0 copy-done.6
  12.0 0.9 %shard_map.97 = (bf16[2048,128]{1,0:T(8,128)(2,1)S(1)}, bf16[96,288]{1,0:T(8,128)(2,1)S(1)}, bf16[48,288]{1,0:T(8,128)(2,1)S(1)}) custom-call(bf16[32,64,128]{2,1,0:T(8,128)(2,1)S(1)} %bitcast.10, bf16[3,3,3,32,32]{4,3,2,1,0:T(8,128)(2,1)S(1)} %copy-done.5, bf16[3,3,3,16,32]{4,3,2,1,0:T(8,128)(2,1)S(1)} %copy-done.6), custom_call_target="tpu_custom_call" | custom-call | bytes 4194304 | tf_op jit(solution)/shard_map/pallas_call | solution.py:199
  13.0 1.7 %collective-permute-done.5.field = bf16[32,64,128]{2,1,0:T(8,128)(2,1)S(1)} collective-permute-done((bf16[32,64,128]{2,1,0:T(8,128)(2,1)S(1)}, bf16[32,64,128]{2,1,0:T(8,128)(2,1)S(1)}, u32[]{:S(2)}, u32[]{:S(2)}) %collective-permute-start.5) | collective-permute-done | bytes 524320 | tf_op jit(solution)/shard_map/ppermute | solution.py:497
  14.7 0.8 %shard_map.96.pack_out = bf16[2048,128]{1,0:T(8,128)(2,1)S(1)} custom-call(bf16[32,64,128]{2,1,0:T(8,128)(2,1)S(1)} %collective-permute-done.5.field), custom_call_target="tpu_custom_call" | custom-call | bytes 4194304 | tf_op jit(solution)/shard_map/pallas_call | solution.py:59
  15.5 0.0 collective-permute-done.4.pack_in
  15.5 2.6 %shard_map.98 = (bf16[6336,128]{1,0:T(8,128)(2,1)S(1)}, f32[288,128]{1,0:T(8,128)S(1)}) custom-call(bf16[2048,128]{1,0:T(8,128)(2,1)S(1)} %collective-permute-done.4.pack_in, bf16[2048,128]{1,0:T(8,128)(2,1)S(1)} %shard_map.93.refs_0_.pack_0, bf16[2048,128]{1,0:T(8,128)(2,1)S(1)} %shard_map.96.pack_out, bf16[2048,128]{1,0:T(8,128)(2,1)S(1)} %get-tuple-element.45.acts, ...), custom_call_target="tpu_custom_call" | custom-call | flops 1000000000 | bytes 20971520 | tf_op jit(solution)/shard_map/pallas_call | solution.py:293
  18.1 0.0 collective-permute-done.3.pack_out
  18.1 0.0 collective-permute-done.2.pack_in
  18.1 0.8 %shard_map.99 = (bf16[256,128]{1,0:T(8,128)(2,1)S(1)}, f32[256,128]{1,0:T(8,128)S(1)}) custom-call(bf16[1024,128]{1,0:T(8,128)(2,1)S(1)} %collective-permute-done.2.pack_in, bf16[1024,128]{1,0:T(8,128)(2,1)S(1)} %shard_map.95.pack_0, bf16[1024,128]{1,0:T(8,128)(2,1)S(1)} %collective-permute-done.3.pack_out, bf16[6336,128]{1,0:T(8,128)(2,1)S(1)} %get-tuple-element.47.pres, ...), custom_call_target="tpu_custom_call" | custom-call | flops 1000000000 | bytes 5242880 | tf_op jit(solution)/shard_map/pallas_call | solution.py:307
  18.9 0.1 collective-permute-start.6
  19.0 1.0 %shard_map.101 = (bf16[1024,128]{1,0:T(8,128)(2,1)S(1)}, bf16[1024,128]{1,0:T(8,128)(2,1)S(1)}, bf16[1024,128]{1,0:T(8,128)(2,1)S(1)}) custom-call(bf16[6336,128]{1,0:T(8,128)(2,1)S(1)} %get-tuple-element.47.pres, bf16[48,288]{1,0:T(8,128)(2,1)S(1)} %get-tuple-element.51.w_one), custom_call_target="tpu_custom_call" | custom-call | flops 1000000000 | bytes 5242880 | tf_op jit(solution)/shard_map/pallas_call | solution.py:321
  20.0 0.2 collective-permute-done.6.more
  20.2 0.0 collective-permute-done.1.other
  20.2 0.1 shard_map.100
  20.3 16.4 %all_to_all.10.refs_0_ = bf16[16,80,128]{2,1,0:T(8,128)(2,1)S(1)} all-to-all(bf16[16,80,128]{2,1,0:T(8,128)(2,1)S(1)} %shard_map.100), channel_id=1, replica_groups=mesh['z'=4,'x'=2,'y'=2,'core'=2] {'x','z','y'}, dimensions={0} | all-to-all | bytes 655360 | tf_op jit(solution)/shard_map/all_to_all | solution.py:526
  36.7 1.0 %shard_map.102 = bf16[16,144,128]{2,1,0:T(8,128)(2,1)} custom-call(bf16[16,80,128]{2,1,0:T(8,128)(2,1)S(1)} %all_to_all.10.refs_0_), custom_call_target="tpu_custom_call" | custom-call | flops 163840 | bytes 983040 | tf_op jit(solution)/shard_map/pallas_call | solution.py:377
  37.7 4.3 %all-to-all-start.1 = ((bf16[16,144,128]{2,1,0:T(8,128)(2,1)}), bf16[16,144,128]{2,1,0:T(8,128)(2,1)S(1)}, u32[]{:S(2)}, u32[]{:S(2)}) async-start(bf16[16,144,128]{2,1,0:T(8,128)(2,1)} %shard_map.102), calls=%async_computation.1 | async-start | bytes 1179648 | tf_op jit(solution)/shard_map/all_to_all | solution.py:531
  42.0 1.8 %collective-permute-start.7 = (bf16[1024,128]{1,0:T(8,128)(2,1)S(1)}, bf16[1024,128]{1,0:T(8,128)(2,1)S(1)}, u32[]{:S(2)}, u32[]{:S(2)}) collective-permute-start(bf16[1024,128]{1,0:T(8,128)(2,1)S(1)} %get-tuple-element.59), channel_id=1, source_target_pairs={{0,1},{1,0},{2,3},{3,2},{4,5},{5,4},{6,7},{7,6},{8,9},{9,8},{10,11... | collective-permute-start | bytes 786440 | tf_op jit(solution)/shard_map/ppermute | solution.py:140
  43.7 3.3 %collective-permute-start.8 = (bf16[1024,128]{1,0:T(8,128)(2,1)S(1)}, bf16[1024,128]{1,0:T(8,128)(2,1)S(1)}, u32[]{:S(2)}, u32[]{:S(2)}) collective-permute-start(bf16[1024,128]{1,0:T(8,128)(2,1)S(1)} %get-tuple-element.60), channel_id=1, source_target_pairs={{1,2},{2,1},{5,6},{6,5},{9,10},{10,9},{13,14},{14,13},{17,18},{18,... | collective-permute-start | bytes 786440 | tf_op jit(solution)/shard_map/ppermute | solution.py:497
  47.0 0.0 collective-permute-done.7.first
  47.0 6.7 %collective-permute-done.8.second = bf16[1024,128]{1,0:T(8,128)(2,1)S(1)} collective-permute-done((bf16[1024,128]{1,0:T(8,128)(2,1)S(1)}, bf16[1024,128]{1,0:T(8,128)(2,1)S(1)}, u32[]{:S(2)}, u32[]{:S(2)}) %collective-permute-start.8) | collective-permute-done | bytes 262176 | tf_op jit(solution)/shard_map/ppermute | solution.py:497
  53.8 1.0 %shard_map.103 = bf16[16,64,128]{2,1,0:T(8,128)(2,1)} custom-call(bf16[1024,128]{1,0:T(8,128)(2,1)S(1)} %get-tuple-element.58.own, bf16[1024,128]{1,0:T(8,128)(2,1)S(1)} %collective-permute-done.7.first, bf16[1024,128]{1,0:T(8,128)(2,1)S(1)} %collective-permute-done.8.second), custom_call_target="tpu_custom_call" | custom-call | flops 262144 | bytes 1048576 | tf_op jit(solution)/shard_map/pallas_call | solution.py:351
  54.8 2.3 %all-to-all-done.1.refs_0_ = bf16[16,144,128]{2,1,0:T(8,128)(2,1)S(1)} async-done(((bf16[16,144,128]{2,1,0:T(8,128)(2,1)}), bf16[16,144,128]{2,1,0:T(8,128)(2,1)S(1)}, u32[]{:S(2)}, u32[]{:S(2)}) %all-to-all-start.1) | async-done | bytes 589856 | tf_op jit(solution)/shard_map/all_to_all | solution.py:531
  57.0 2.6 %collective-permute-start.9 = (bf16[16,144,128]{2,1,0:T(8,128)(2,1)S(1)}, bf16[16,144,128]{2,1,0:T(8,128)(2,1)S(1)}, u32[]{:S(2)}, u32[]{:S(2)}) collective-permute-start(bf16[16,144,128]{2,1,0:T(8,128)(2,1)S(1)} %all-to-all-done.1.refs_0_), channel_id=1, source_target_pairs={{0,1},{1,0},{2,3},{3,2},{4,5},{5,4},{6,7},{7,6},{8,9},{9,8},{10,11... | collective-permute-start | bytes 1769480 | tf_op jit(solution)/shard_map/ppermute | solution.py:140
  59.6 1.0 %shard_map.104.refs_2_ = f32[4096,128]{1,0:T(8,128)} custom-call(bf16[16,144,128]{2,1,0:T(8,128)(2,1)S(1)} %all-to-all-done.1.refs_0_), custom_call_target="tpu_custom_call" | custom-call | tf_op jit(solution)/shard_map/pallas_call | solution.py:466
  60.6 0.6 collective-permute-done.9.refs_1_
  61.2 1.4 %shard_map.105 = (f32[4096,128]{1,0:T(8,128)}, f32[432,32]{1,0:T(8,128)}, f32[864,32]{1,0:T(8,128)}) custom-call(bf16[16,144,128]{2,1,0:T(8,128)(2,1)S(1)} %all-to-all-done.1.refs_0_, bf16[16,144,128]{2,1,0:T(8,128)(2,1)S(1)} %collective-permute-done.9.refs_1_, f32[4096,128]{1,0:T(8,128)} %shard_map.104.refs_2_), custom_call_target="tpu_custom_call", output_to_operand_aliasing={{0}: (2, {})} | custom-call | tf_op jit(solution)/shard_map/pallas_call | solution.py:474
Async XLA Ops:
  0.6 2.0 %copy-start = (f32[1,524288]{1,0:T(1,128)S(1)}, f32[1,524288]{1,0:T(1,128)}, u32[]{:S(2)}) copy-start(f32[1,524288]{1,0:T(1,128)} %param.11) | copy-start | bytes 6291460
  0.7 1.2 %copy-start.2 = (bf16[1,1,32,64,128]{4,3,2,1,0:T(8,128)(2,1)S(1)}, bf16[1,1,32,64,128]{4,3,2,1,0:T(8,128)(2,1)}, u32[]{:S(2)}) copy-start(bf16[1,1,32,64,128]{4,3,2,1,0:T(8,128)(2,1)} %param.8) | copy-start | bytes 1572868
  1.8 1.2 %copy-start.3 = (bf16[1,1,32,64,128]{4,3,2,1,0:T(8,128)(2,1)S(1)}, bf16[1,1,32,64,128]{4,3,2,1,0:T(8,128)(2,1)}, u32[]{:S(2)}) copy-start(bf16[1,1,32,64,128]{4,3,2,1,0:T(8,128)(2,1)} %param.8) | copy-start | bytes 1572868
  1.8 5.8 %copy-start.4 = (bf16[1,1,16,64,128]{4,3,2,1,0:T(8,128)(2,1)S(1)}, bf16[1,1,16,64,128]{4,3,2,1,0:T(8,128)(2,1)}, u32[]{:S(2)}) copy-start(bf16[1,1,16,64,128]{4,3,2,1,0:T(8,128)(2,1)} %param.6) | copy-start | bytes 786436
  2.7 9.3 %copy-start.1 = (bf16[1,1,32,64,128]{4,3,2,1,0:T(8,128)(2,1)S(1)}, bf16[1,1,32,64,128]{4,3,2,1,0:T(8,128)(2,1)}, u32[]{:S(2)}) copy-start(bf16[1,1,32,64,128]{4,3,2,1,0:T(8,128)(2,1)} %param.7) | copy-start | bytes 1572868
  2.7 9.3 %copy-start.5 = (bf16[3,3,3,32,32]{4,3,2,1,0:T(8,128)(2,1)S(1)}, bf16[3,3,3,32,32]{4,3,2,1,0:T(8,128)(2,1)}, u32[]{:S(2)}) copy-start(bf16[3,3,3,32,32]{4,3,2,1,0:T(8,128)(2,1)} %two.1) | copy-start | bytes 165892
  2.7 9.3 %copy-start.6 = (bf16[3,3,3,16,32]{4,3,2,1,0:T(8,128)(2,1)S(1)}, bf16[3,3,3,16,32]{4,3,2,1,0:T(8,128)(2,1)}, u32[]{:S(2)}) copy-start(bf16[3,3,3,16,32]{4,3,2,1,0:T(8,128)(2,1)} %one.1) | copy-start | bytes 82948
  2.8 7.3 %collective-permute-start = (bf16[2048,128]{1,0:T(8,128)(2,1)S(1)}, bf16[2048,128]{1,0:T(8,128)(2,1)S(1)}, u32[]{:S(2)}, u32[]{:S(2)}) collective-permute-start(bf16[2048,128]{1,0:T(8,128)(2,1)S(1)} %dynamic-slice_convert_fusion), channel_id=1, source_target_pairs={{0,1},{1,0},{2,3},{3,2},{4,5},{5,4},{6,7},{7,6},{8,9},{9,8},{10,11... | collective-permute-start | bytes 1572872 | tf_op jit(solution)/shard_map/ppermute | solution.py:140
  3.0 11.7 %collective-permute-start.5 = (bf16[32,64,128]{2,1,0:T(8,128)(2,1)S(1)}, bf16[32,64,128]{2,1,0:T(8,128)(2,1)S(1)}, u32[]{:S(2)}, u32[]{:S(2)}) collective-permute-start(bf16[32,64,128]{2,1,0:T(8,128)(2,1)S(1)} %bitcast.12), channel_id=1, source_target_pairs={{1,2},{2,1},{5,6},{6,5},{9,10},{10,9},{13,14},{14,13},{17,18},{18,... | collective-permute-start | bytes 1572872 | tf_op jit(solution)/shard_map/ppermute | solution.py:497
  7.6 7.9 %collective-permute-start.4 = (bf16[2048,128]{1,0:T(8,128)(2,1)S(1)}, bf16[2048,128]{1,0:T(8,128)(2,1)S(1)}, u32[]{:S(2)}, u32[]{:S(2)}) collective-permute-start(bf16[2048,128]{1,0:T(8,128)(2,1)S(1)} %shard_map.93.refs_0_.pack_0), channel_id=1, source_target_pairs={{0,1},{1,0},{2,3},{3,2},{4,5},{5,4},{6,7},{7,6},{8,9},{9,8},{10,11... | collective-permute-start | bytes 1572872 | tf_op jit(solution)/shard_map/ppermute | solution.py:140
  8.1 10.0 %collective-permute-start.3 = (bf16[1024,128]{1,0:T(8,128)(2,1)S(1)}, bf16[1024,128]{1,0:T(8,128)(2,1)S(1)}, u32[]{:S(2)}, u32[]{:S(2)}) collective-permute-start(bf16[1024,128]{1,0:T(8,128)(2,1)S(1)} %shard_map.95.pack_0), channel_id=1, source_target_pairs={{1,2},{2,1},{5,6},{6,5},{9,10},{10,9},{13,14},{14,13},{17,18},{18,... | collective-permute-start | bytes 786440 | tf_op jit(solution)/shard_map/ppermute | solution.py:497
  10.0 8.0 %collective-permute-start.2 = (bf16[1024,128]{1,0:T(8,128)(2,1)S(1)}, bf16[1024,128]{1,0:T(8,128)(2,1)S(1)}, u32[]{:S(2)}, u32[]{:S(2)}) collective-permute-start(bf16[1024,128]{1,0:T(8,128)(2,1)S(1)} %shard_map.95.pack_0), channel_id=1, source_target_pairs={{0,1},{1,0},{2,3},{3,2},{4,5},{5,4},{6,7},{7,6},{8,9},{9,8},{10,11... | collective-permute-start | bytes 786440 | tf_op jit(solution)/shard_map/ppermute | solution.py:140
  10.3 10.0 %collective-permute-start.1 = (bf16[1024,128]{1,0:T(8,128)(2,1)S(1)}, bf16[1024,128]{1,0:T(8,128)(2,1)S(1)}, u32[]{:S(2)}, u32[]{:S(2)}) collective-permute-start(bf16[1024,128]{1,0:T(8,128)(2,1)S(1)} %get-tuple-element.42), channel_id=1, source_target_pairs={{0,4},{4,0},{1,5},{5,1},{2,6},{6,2},{3,7},{7,3},{8,12},{12,8},{9,1... | collective-permute-start | bytes 786440 | tf_op jit(solution)/shard_map/ppermute | solution.py:140
  18.9 1.3 %collective-permute-start.6 = (bf16[256,128]{1,0:T(8,128)(2,1)S(1)}, bf16[256,128]{1,0:T(8,128)(2,1)S(1)}, u32[]{:S(2)}, u32[]{:S(2)}) collective-permute-start(bf16[256,128]{1,0:T(8,128)(2,1)S(1)} %get-tuple-element.50), channel_id=1, source_target_pairs={{0,1},{1,0},{2,3},{3,2},{4,5},{5,4},{6,7},{7,6},{8,9},{9,8},{10,11... | collective-permute-start | bytes 196616 | tf_op jit(solution)/shard_map/ppermute | solution.py:140
  37.7 19.4 %all-to-all-start.1 = ((bf16[16,144,128]{2,1,0:T(8,128)(2,1)}), bf16[16,144,128]{2,1,0:T(8,128)(2,1)S(1)}, u32[]{:S(2)}, u32[]{:S(2)}) async-start(bf16[16,144,128]{2,1,0:T(8,128)(2,1)} %shard_map.102), calls=%async_computation.1 | async-start | bytes 1179648 | tf_op jit(solution)/shard_map/all_to_all | solution.py:531
  42.0 5.1 %collective-permute-start.7 = (bf16[1024,128]{1,0:T(8,128)(2,1)S(1)}, bf16[1024,128]{1,0:T(8,128)(2,1)S(1)}, u32[]{:S(2)}, u32[]{:S(2)}) collective-permute-start(bf16[1024,128]{1,0:T(8,128)(2,1)S(1)} %get-tuple-element.59), channel_id=1, source_target_pairs={{0,1},{1,0},{2,3},{3,2},{4,5},{5,4},{6,7},{7,6},{8,9},{9,8},{10,11... | collective-permute-start | bytes 786440 | tf_op jit(solution)/shard_map/ppermute | solution.py:140
  43.7 10.0 %collective-permute-start.8 = (bf16[1024,128]{1,0:T(8,128)(2,1)S(1)}, bf16[1024,128]{1,0:T(8,128)(2,1)S(1)}, u32[]{:S(2)}, u32[]{:S(2)}) collective-permute-start(bf16[1024,128]{1,0:T(8,128)(2,1)S(1)} %get-tuple-element.60), channel_id=1, source_target_pairs={{1,2},{2,1},{5,6},{6,5},{9,10},{10,9},{13,14},{14,13},{17,18},{18,... | collective-permute-start | bytes 786440 | tf_op jit(solution)/shard_map/ppermute | solution.py:497
  57.0 4.2 %collective-permute-start.9 = (bf16[16,144,128]{2,1,0:T(8,128)(2,1)S(1)}, bf16[16,144,128]{2,1,0:T(8,128)(2,1)S(1)}, u32[]{:S(2)}, u32[]{:S(2)}) collective-permute-start(bf16[16,144,128]{2,1,0:T(8,128)(2,1)S(1)} %all-to-all-done.1.refs_0_), channel_id=1, source_target_pairs={{0,1},{1,0},{2,3},{3,2},{4,5},{5,4},{6,7},{7,6},{8,9},{9,8},{10,11... | collective-permute-start | bytes 1769480 | tf_op jit(solution)/shard_map/ppermute | solution.py:140

commit v22 on v20

--- a/solution.py
+++ b/solution.py
@@ -10,7 +10,7 @@
 SPACE = ("y", "core")
 SAME = ("x", "z", "y")
 EVERY = ("z", "x", "y", "core")
-GROUP = 8
+GROUP = 16
 LANES = 128
 BF16 = jnp.bfloat16
 F32 = jnp.float32
@@ -38,14 +38,14 @@
         flat[pl.ds(pl.multiple_of(c * length, length), length), :] = src[c].astype(F32)
         return carry
 
-    lax.fori_loop(0, chans, stage, 0, unroll=4)
+    lax.fori_loop(0, chans, stage, 0, unroll=8)
 
     def gather(x, carry):
         rows = flat[pl.ds(x, chans, stride=length), :]
         dst[pl.ds(pl.multiple_of(x * chans, 16), chans), :] = rows.astype(BF16)
         return carry
 
-    lax.fori_loop(0, length, gather, 0, unroll=4)
+    lax.fori_loop(0, length, gather, 0, unroll=8)
 
 
 def pack_kernel(field, *refs):
@@ -338,13 +338,13 @@
         flat[at, :] = own[at, :].astype(F32) + first[at, :].astype(F32) + second[at, :].astype(F32)
         return carry
 
-    lax.fori_loop(0, own.shape[0] // 64, add, 0, unroll=4)
+    lax.fori_loop(0, own.shape[0] // 64, add, 0, unroll=8)
 
     def gather(c, carry):
         out[c] = flat[pl.ds(c, length, stride=chans), :].astype(out.dtype)
         return carry
 
-    lax.fori_loop(0, chans, gather, 0, unroll=4)
+    lax.fori_loop(0, chans, gather, 0, unroll=8)
 
 
 def merge(own, first, second, shape):

time: 62.7 us -> 62.6 us (level)
  no operation moved by 1% of the time
where the time goes in v22:
time: 62.6 us; the launch traced here: 62 us
  starting transfers between devices  20.5 us (33%)
  blocking collectives  16.4 us (26%)
  waiting for transfers between devices  11.9 us (19%)
  Pallas kernels  10.9 us (17%)
  local copies, waits for them, and re-layouts  1.35 us (2%)
  between operations  0.85 us (1%)
    all_to_all x1, blocking collectives, per_device(): parts = lax.all_to_all(parts, SAME, 0, 0)  16.4 us
    ppermute x3, starting transfers between devices, crossed(): return lax.ppermute(value, SPACE, pairs + [(m, n) for n, m in pairs])  9.81 us
    ppermute x3, waiting for transfers between devices, crossed(): return lax.ppermute(value, SPACE, pairs + [(m, n) for n, m in pairs])  8.84 us
    ppermute x7, starting transfers between devices, swapped(): return lax.ppermute(value, axis, [(0, 1), (1, 0)])  6.4 us
    all_to_all x1, starting transfers between devices, per_device(): mine = lax.all_to_all(shares, SAME, 0, 0)  4.29 us
    pallas_call x1, Pallas kernels, first_part(): vmem_call(first_kernel, (jax.ShapeDtypeStruct(((length + 2) * 3 * c1, wid...  2.62 us
    all_to_all x1, waiting for transfers between devices, per_device(): mine = lax.all_to_all(shares, SAME, 0, 0)  2.29 us
    pallas_call x1, Pallas kernels, finish(): pl.pallas_call(lambda *refs: finish_kernel(sizes, height, padded, *refs),...  1.37 us
  transfers between devices with their start and end apart: 11, of which 6 were waited for; matrix products, arithmetic and copies ran while one was open for 0% of the time, Pallas kernels for 13%

profile of v22, /device:TPU:1, one launch (start us, length us, event | category | flops | bytes accessed | tf_op | source)
XLA Modules:
  0.0 62.0 jit_solution(6477704859591883989)
XLA Ops:
  0.6 0.0 copy-start
  0.7 0.0 copy-start.1
  0.7 1.2 %copy-done.1 = bf16[1,1,32,64,128]{4,3,2,1,0:T(8,128)(2,1)S(1)} copy-done((bf16[1,1,32,64,128]{4,3,2,1,0:T(8,128)(2,1)S(1)}, bf16[1,1,32,64,128]{4,3,2,1,0:T(8,128)(2,1)}, u32[]{:S(2)}) %copy-start.1) | copy-done | bytes 524312
  1.8 0.0 copy-start.3
  1.8 0.7 %shard_map.93.refs_0_.pack_0 = bf16[2048,128]{1,0:T(8,128)(2,1)S(1)} custom-call(bf16[32,64,128]{2,1,0:T(8,128)(2,1)S(1)} %bitcast.10), custom_call_target="tpu_custom_call" | custom-call | bytes 67108864 | tf_op jit(solution)/shard_map/pallas_call | solution.py:59
  2.6 0.0 copy-done
  2.6 0.1 dynamic-slice_convert_fusion
  2.6 0.0 copy-start.2
  2.6 0.0 copy-start.4
  2.7 0.0 copy-start.5
  2.7 0.1 constant_dynamic-slice_fusion.own
  2.8 0.1 collective-permute-start
  2.9 4.6 %collective-permute-start.5 = (bf16[2048,128]{1,0:T(8,128)(2,1)S(1)}, bf16[2048,128]{1,0:T(8,128)(2,1)S(1)}, u32[]{:S(2)}, u32[]{:S(2)}) collective-permute-start(bf16[2048,128]{1,0:T(8,128)(2,1)S(1)} %shard_map.93.refs_0_.pack_0), channel_id=1, source_target_pairs={{1,2},{2,1},{5,6},{6,5},{9,10},{10,9},{13,14},{14,13},{17,18},{18,... | collective-permute-start | bytes 1572872 | tf_op jit(solution)/shard_map/ppermute | solution.py:497
  7.5 0.1 collective-permute-start.4
  7.6 0.0 copy-done.3
  7.6 0.4 shard_map.95.pack_0
  8.0 1.9 %collective-permute-start.3 = (bf16[1024,128]{1,0:T(8,128)(2,1)S(1)}, bf16[1024,128]{1,0:T(8,128)(2,1)S(1)}, u32[]{:S(2)}, u32[]{:S(2)}) collective-permute-start(bf16[1024,128]{1,0:T(8,128)(2,1)S(1)} %shard_map.95.pack_0), channel_id=1, source_target_pairs={{1,2},{2,1},{5,6},{6,5},{9,10},{10,9},{13,14},{14,13},{17,18},{18,... | collective-permute-start | bytes 786440 | tf_op jit(solution)/shard_map/ppermute | solution.py:497
  9.9 0.1 collective-permute-start.2
  10.0 0.0 collective-permute-done.other
  10.0 0.1 shard_map.94
  10.2 1.7 %collective-permute-start.1 = (bf16[1024,128]{1,0:T(8,128)(2,1)S(1)}, bf16[1024,128]{1,0:T(8,128)(2,1)S(1)}, u32[]{:S(2)}, u32[]{:S(2)}) collective-permute-start(bf16[1024,128]{1,0:T(8,128)(2,1)S(1)} %get-tuple-element.42), channel_id=1, source_target_pairs={{0,4},{4,0},{1,5},{5,1},{2,6},{6,2},{3,7},{7,3},{8,12},{12,8},{9,1... | collective-permute-start | bytes 786440 | tf_op jit(solution)/shard_map/ppermute | solution.py:140
  11.9 0.0 copy-done.2
  11.9 0.0 copy-done.4
  11.9 0.0 copy-done.5
  11.9 0.8 %shard_map.96 = (bf16[2048,128]{1,0:T(8,128)(2,1)S(1)}, bf16[96,288]{1,0:T(8,128)(2,1)S(1)}, bf16[48,288]{1,0:T(8,128)(2,1)S(1)}) custom-call(bf16[32,64,128]{2,1,0:T(8,128)(2,1)S(1)} %bitcast.11, bf16[3,3,3,32,32]{4,3,2,1,0:T(8,128)(2,1)S(1)} %copy-done.4, bf16[3,3,3,16,32]{4,3,2,1,0:T(8,128)(2,1)S(1)} %copy-done.5), custom_call_target="tpu_custom_call" | custom-call | bytes 4194304 | tf_op jit(solution)/shard_map/pallas_call | solution.py:199
  12.7 1.9 %collective-permute-done.5.pack_out = bf16[2048,128]{1,0:T(8,128)(2,1)S(1)} collective-permute-done((bf16[2048,128]{1,0:T(8,128)(2,1)S(1)}, bf16[2048,128]{1,0:T(8,128)(2,1)S(1)}, u32[]{:S(2)}, u32[]{:S(2)}) %collective-permute-start.5) | collective-permute-done | bytes 524320 | tf_op jit(solution)/shard_map/ppermute | solution.py:497
  14.7 0.0 collective-permute-done.4.pack_in
  14.7 2.6 %shard_map.97 = (bf16[6336,128]{1,0:T(8,128)(2,1)S(1)}, f32[288,128]{1,0:T(8,128)S(1)}) custom-call(bf16[2048,128]{1,0:T(8,128)(2,1)S(1)} %collective-permute-done.4.pack_in, bf16[2048,128]{1,0:T(8,128)(2,1)S(1)} %shard_map.93.refs_0_.pack_0, bf16[2048,128]{1,0:T(8,128)(2,1)S(1)} %collective-permute-done.5.pack_out, ...), custom_call_target="tpu_custom_call" | custom-call | flops 1000000000 | bytes 20971520 | tf_op jit(solution)/shard_map/pallas_call | solution.py:293
  17.3 0.2 collective-permute-done.3.pack_out
  17.5 0.0 collective-permute-done.2.pack_in
  17.5 0.8 %shard_map.98 = (bf16[256,128]{1,0:T(8,128)(2,1)S(1)}, f32[256,128]{1,0:T(8,128)S(1)}) custom-call(bf16[1024,128]{1,0:T(8,128)(2,1)S(1)} %collective-permute-done.2.pack_in, bf16[1024,128]{1,0:T(8,128)(2,1)S(1)} %shard_map.95.pack_0, bf16[1024,128]{1,0:T(8,128)(2,1)S(1)} %collective-permute-done.3.pack_out, bf16[6336,128]{1,0:T(8,128)(2,1)S(1)} %get-tuple-element.47.pres, ...), custom_call_target="tpu_custom_call" | custom-call | flops 1000000000 | bytes 5242880 | tf_op jit(solution)/shard_map/pallas_call | solution.py:307
  18.3 0.1 collective-permute-start.6
  18.4 1.0 %shard_map.100 = (bf16[1024,128]{1,0:T(8,128)(2,1)S(1)}, bf16[1024,128]{1,0:T(8,128)(2,1)S(1)}, bf16[1024,128]{1,0:T(8,128)(2,1)S(1)}) custom-call(bf16[6336,128]{1,0:T(8,128)(2,1)S(1)} %get-tuple-element.47.pres, bf16[48,288]{1,0:T(8,128)(2,1)S(1)} %get-tuple-element.51.w_one), custom_call_target="tpu_custom_call" | custom-call | flops 1000000000 | bytes 5242880 | tf_op jit(solution)/shard_map/pallas_call | solution.py:321
  19.4 0.2 collective-permute-done.6.more
  19.6 0.0 collective-permute-done.1.other
  19.6 0.1 shard_map.99
  19.7 16.4 %all_to_all.10.refs_0_ = bf16[16,80,128]{2,1,0:T(8,128)(2,1)S(1)} all-to-all(bf16[16,80,128]{2,1,0:T(8,128)(2,1)S(1)} %shard_map.99), channel_id=1, replica_groups=mesh['z'=4,'x'=2,'y'=2,'core'=2] {'x','z','y'}, dimensions={0} | all-to-all | bytes 655360 | tf_op jit(solution)/shard_map/all_to_all | solution.py:526
  36.1 1.0 %shard_map.101 = bf16[16,144,128]{2,1,0:T(8,128)(2,1)} custom-call(bf16[16,80,128]{2,1,0:T(8,128)(2,1)S(1)} %all_to_all.10.refs_0_), custom_call_target="tpu_custom_call" | custom-call | flops 163840 | bytes 983040 | tf_op jit(solution)/shard_map/pallas_call | solution.py:377
  37.1 4.3 %all-to-all-start.1 = ((bf16[16,144,128]{2,1,0:T(8,128)(2,1)}), bf16[16,144,128]{2,1,0:T(8,128)(2,1)S(1)}, u32[]{:S(2)}, u32[]{:S(2)}) async-start(bf16[16,144,128]{2,1,0:T(8,128)(2,1)} %shard_map.101), calls=%async_computation.1 | async-start | bytes 1179648 | tf_op jit(solution)/shard_map/all_to_all | solution.py:531
  41.4 1.8 %collective-permute-start.7 = (bf16[1024,128]{1,0:T(8,128)(2,1)S(1)}, bf16[1024,128]{1,0:T(8,128)(2,1)S(1)}, u32[]{:S(2)}, u32[]{:S(2)}) collective-permute-start(bf16[1024,128]{1,0:T(8,128)(2,1)S(1)} %get-tuple-element.59), channel_id=1, source_target_pairs={{0,1},{1,0},{2,3},{3,2},{4,5},{5,4},{6,7},{7,6},{8,9},{9,8},{10,11... | collective-permute-start | bytes 786440 | tf_op jit(solution)/shard_map/ppermute | solution.py:140
  43.1 3.3 %collective-permute-start.8 = (bf16[1024,128]{1,0:T(8,128)(2,1)S(1)}, bf16[1024,128]{1,0:T(8,128)(2,1)S(1)}, u32[]{:S(2)}, u32[]{:S(2)}) collective-permute-start(bf16[1024,128]{1,0:T(8,128)(2,1)S(1)} %get-tuple-element.60), channel_id=1, source_target_pairs={{1,2},{2,1},{5,6},{6,5},{9,10},{10,9},{13,14},{14,13},{17,18},{18,... | collective-permute-start | bytes 786440 | tf_op jit(solution)/shard_map/ppermute | solution.py:497
  46.4 0.0 collective-permute-done.7.first
  46.4 6.7 %collective-permute-done.8.second = bf16[1024,128]{1,0:T(8,128)(2,1)S(1)} collective-permute-done((bf16[1024,128]{1,0:T(8,128)(2,1)S(1)}, bf16[1024,128]{1,0:T(8,128)(2,1)S(1)}, u32[]{:S(2)}, u32[]{:S(2)}) %collective-permute-start.8) | collective-permute-done | bytes 262176 | tf_op jit(solution)/shard_map/ppermute | solution.py:497
  53.2 1.0 %shard_map.102 = bf16[16,64,128]{2,1,0:T(8,128)(2,1)} custom-call(bf16[1024,128]{1,0:T(8,128)(2,1)S(1)} %get-tuple-element.58.own, bf16[1024,128]{1,0:T(8,128)(2,1)S(1)} %collective-permute-done.7.first, bf16[1024,128]{1,0:T(8,128)(2,1)S(1)} %collective-permute-done.8.second), custom_call_target="tpu_custom_call" | custom-call | flops 262144 | bytes 1048576 | tf_op jit(solution)/shard_map/pallas_call | solution.py:351
  54.1 2.3 %all-to-all-done.1.refs_0_ = bf16[16,144,128]{2,1,0:T(8,128)(2,1)S(1)} async-done(((bf16[16,144,128]{2,1,0:T(8,128)(2,1)}), bf16[16,144,128]{2,1,0:T(8,128)(2,1)S(1)}, u32[]{:S(2)}, u32[]{:S(2)}) %all-to-all-start.1) | async-done | bytes 589856 | tf_op jit(solution)/shard_map/all_to_all | solution.py:531
  56.4 2.6 %collective-permute-start.9 = (bf16[16,144,128]{2,1,0:T(8,128)(2,1)S(1)}, bf16[16,144,128]{2,1,0:T(8,128)(2,1)S(1)}, u32[]{:S(2)}, u32[]{:S(2)}) collective-permute-start(bf16[16,144,128]{2,1,0:T(8,128)(2,1)S(1)} %all-to-all-done.1.refs_0_), channel_id=1, source_target_pairs={{0,1},{1,0},{2,3},{3,2},{4,5},{5,4},{6,7},{7,6},{8,9},{9,8},{10,11... | collective-permute-start | bytes 1769480 | tf_op jit(solution)/shard_map/ppermute | solution.py:140
  59.0 1.0 %shard_map.103.refs_2_ = f32[4096,128]{1,0:T(8,128)} custom-call(bf16[16,144,128]{2,1,0:T(8,128)(2,1)S(1)} %all-to-all-done.1.refs_0_), custom_call_target="tpu_custom_call" | custom-call | tf_op jit(solution)/shard_map/pallas_call | solution.py:466
  60.0 0.6 collective-permute-done.9.refs_1_
  60.6 1.4 %shard_map.104 = (f32[4096,128]{1,0:T(8,128)}, f32[432,32]{1,0:T(8,128)}, f32[864,32]{1,0:T(8,128)}) custom-call(bf16[16,144,128]{2,1,0:T(8,128)(2,1)S(1)} %all-to-all-done.1.refs_0_, bf16[16,144,128]{2,1,0:T(8,128)(2,1)S(1)} %collective-permute-done.9.refs_1_, f32[4096,128]{1,0:T(8,128)} %shard_map.103.refs_2_), custom_call_target="tpu_custom_call", output_to_operand_aliasing={{0}: (2, {})} | custom-call | tf_op jit(solution)/shard_map/pallas_call | solution.py:474
Async XLA Ops:
  0.6 1.9 %copy-start = (f32[1,524288]{1,0:T(1,128)S(1)}, f32[1,524288]{1,0:T(1,128)}, u32[]{:S(2)}) copy-start(f32[1,524288]{1,0:T(1,128)} %param.11) | copy-start | bytes 6291460
  0.7 1.2 %copy-start.1 = (bf16[1,1,32,64,128]{4,3,2,1,0:T(8,128)(2,1)S(1)}, bf16[1,1,32,64,128]{4,3,2,1,0:T(8,128)(2,1)}, u32[]{:S(2)}) copy-start(bf16[1,1,32,64,128]{4,3,2,1,0:T(8,128)(2,1)} %param.8) | copy-start | bytes 1572868
  1.8 5.8 %copy-start.3 = (bf16[1,1,16,64,128]{4,3,2,1,0:T(8,128)(2,1)S(1)}, bf16[1,1,16,64,128]{4,3,2,1,0:T(8,128)(2,1)}, u32[]{:S(2)}) copy-start(bf16[1,1,16,64,128]{4,3,2,1,0:T(8,128)(2,1)} %param.6) | copy-start | bytes 786436
  2.6 9.3 %copy-start.2 = (bf16[1,1,32,64,128]{4,3,2,1,0:T(8,128)(2,1)S(1)}, bf16[1,1,32,64,128]{4,3,2,1,0:T(8,128)(2,1)}, u32[]{:S(2)}) copy-start(bf16[1,1,32,64,128]{4,3,2,1,0:T(8,128)(2,1)} %param.7) | copy-start | bytes 1572868
  2.6 9.2 %copy-start.4 = (bf16[3,3,3,32,32]{4,3,2,1,0:T(8,128)(2,1)S(1)}, bf16[3,3,3,32,32]{4,3,2,1,0:T(8,128)(2,1)}, u32[]{:S(2)}) copy-start(bf16[3,3,3,32,32]{4,3,2,1,0:T(8,128)(2,1)} %two.1) | copy-start | bytes 165892
  2.7 9.2 %copy-start.5 = (bf16[3,3,3,16,32]{4,3,2,1,0:T(8,128)(2,1)S(1)}, bf16[3,3,3,16,32]{4,3,2,1,0:T(8,128)(2,1)}, u32[]{:S(2)}) copy-start(bf16[3,3,3,16,32]{4,3,2,1,0:T(8,128)(2,1)} %one.1) | copy-start | bytes 82948
  2.8 7.3 %collective-permute-start = (bf16[2048,128]{1,0:T(8,128)(2,1)S(1)}, bf16[2048,128]{1,0:T(8,128)(2,1)S(1)}, u32[]{:S(2)}, u32[]{:S(2)}) collective-permute-start(bf16[2048,128]{1,0:T(8,128)(2,1)S(1)} %dynamic-slice_convert_fusion), channel_id=1, source_target_pairs={{0,1},{1,0},{2,3},{3,2},{4,5},{5,4},{6,7},{7,6},{8,9},{9,8},{10,11... | collective-permute-start | bytes 1572872 | tf_op jit(solution)/shard_map/ppermute | solution.py:140
  2.9 11.8 %collective-permute-start.5 = (bf16[2048,128]{1,0:T(8,128)(2,1)S(1)}, bf16[2048,128]{1,0:T(8,128)(2,1)S(1)}, u32[]{:S(2)}, u32[]{:S(2)}) collective-permute-start(bf16[2048,128]{1,0:T(8,128)(2,1)S(1)} %shard_map.93.refs_0_.pack_0), channel_id=1, source_target_pairs={{1,2},{2,1},{5,6},{6,5},{9,10},{10,9},{13,14},{14,13},{17,18},{18,... | collective-permute-start | bytes 1572872 | tf_op jit(solution)/shard_map/ppermute | solution.py:497
  7.5 7.1 %collective-permute-start.4 = (bf16[2048,128]{1,0:T(8,128)(2,1)S(1)}, bf16[2048,128]{1,0:T(8,128)(2,1)S(1)}, u32[]{:S(2)}, u32[]{:S(2)}) collective-permute-start(bf16[2048,128]{1,0:T(8,128)(2,1)S(1)} %shard_map.93.refs_0_.pack_0), channel_id=1, source_target_pairs={{0,1},{1,0},{2,3},{3,2},{4,5},{5,4},{6,7},{7,6},{8,9},{9,8},{10,11... | collective-permute-start | bytes 1572872 | tf_op jit(solution)/shard_map/ppermute | solution.py:140
  8.0 9.5 %collective-permute-start.3 = (bf16[1024,128]{1,0:T(8,128)(2,1)S(1)}, bf16[1024,128]{1,0:T(8,128)(2,1)S(1)}, u32[]{:S(2)}, u32[]{:S(2)}) collective-permute-start(bf16[1024,128]{1,0:T(8,128)(2,1)S(1)} %shard_map.95.pack_0), channel_id=1, source_target_pairs={{1,2},{2,1},{5,6},{6,5},{9,10},{10,9},{13,14},{14,13},{17,18},{18,... | collective-permute-start | bytes 786440 | tf_op jit(solution)/shard_map/ppermute | solution.py:497
  9.9 7.5 %collective-permute-start.2 = (bf16[1024,128]{1,0:T(8,128)(2,1)S(1)}, bf16[1024,128]{1,0:T(8,128)(2,1)S(1)}, u32[]{:S(2)}, u32[]{:S(2)}) collective-permute-start(bf16[1024,128]{1,0:T(8,128)(2,1)S(1)} %shard_map.95.pack_0), channel_id=1, source_target_pairs={{0,1},{1,0},{2,3},{3,2},{4,5},{5,4},{6,7},{7,6},{8,9},{9,8},{10,11... | collective-permute-start | bytes 786440 | tf_op jit(solution)/shard_map/ppermute | solution.py:140
  10.2 9.4 %collective-permute-start.1 = (bf16[1024,128]{1,0:T(8,128)(2,1)S(1)}, bf16[1024,128]{1,0:T(8,128)(2,1)S(1)}, u32[]{:S(2)}, u32[]{:S(2)}) collective-permute-start(bf16[1024,128]{1,0:T(8,128)(2,1)S(1)} %get-tuple-element.42), channel_id=1, source_target_pairs={{0,4},{4,0},{1,5},{5,1},{2,6},{6,2},{3,7},{7,3},{8,12},{12,8},{9,1... | collective-permute-start | bytes 786440 | tf_op jit(solution)/shard_map/ppermute | solution.py:140
  18.3 1.3 %collective-permute-start.6 = (bf16[256,128]{1,0:T(8,128)(2,1)S(1)}, bf16[256,128]{1,0:T(8,128)(2,1)S(1)}, u32[]{:S(2)}, u32[]{:S(2)}) collective-permute-start(bf16[256,128]{1,0:T(8,128)(2,1)S(1)} %get-tuple-element.50), channel_id=1, source_target_pairs={{0,1},{1,0},{2,3},{3,2},{4,5},{5,4},{6,7},{7,6},{8,9},{9,8},{10,11... | collective-permute-start | bytes 196616 | tf_op jit(solution)/shard_map/ppermute | solution.py:140
  37.1 19.4 %all-to-all-start.1 = ((bf16[16,144,128]{2,1,0:T(8,128)(2,1)}), bf16[16,144,128]{2,1,0:T(8,128)(2,1)S(1)}, u32[]{:S(2)}, u32[]{:S(2)}) async-start(bf16[16,144,128]{2,1,0:T(8,128)(2,1)} %shard_map.101), calls=%async_computation.1 | async-start | bytes 1179648 | tf_op jit(solution)/shard_map/all_to_all | solution.py:531
  41.4 5.1 %collective-permute-start.7 = (bf16[1024,128]{1,0:T(8,128)(2,1)S(1)}, bf16[1024,128]{1,0:T(8,128)(2,1)S(1)}, u32[]{:S(2)}, u32[]{:S(2)}) collective-permute-start(bf16[1024,128]{1,0:T(8,128)(2,1)S(1)} %get-tuple-element.59), channel_id=1, source_target_pairs={{0,1},{1,0},{2,3},{3,2},{4,5},{5,4},{6,7},{7,6},{8,9},{9,8},{10,11... | collective-permute-start | bytes 786440 | tf_op jit(solution)/shard_map/ppermute | solution.py:140
  43.1 10.0 %collective-permute-start.8 = (bf16[1024,128]{1,0:T(8,128)(2,1)S(1)}, bf16[1024,128]{1,0:T(8,128)(2,1)S(1)}, u32[]{:S(2)}, u32[]{:S(2)}) collective-permute-start(bf16[1024,128]{1,0:T(8,128)(2,1)S(1)} %get-tuple-element.60), channel_id=1, source_target_pairs={{1,2},{2,1},{5,6},{6,5},{9,10},{10,9},{13,14},{14,13},{17,18},{18,... | collective-permute-start | bytes 786440 | tf_op jit(solution)/shard_map/ppermute | solution.py:497
  56.4 4.2 %collective-permute-start.9 = (bf16[16,144,128]{2,1,0:T(8,128)(2,1)S(1)}, bf16[16,144,128]{2,1,0:T(8,128)(2,1)S(1)}, u32[]{:S(2)}, u32[]{:S(2)}) collective-permute-start(bf16[16,144,128]{2,1,0:T(8,128)(2,1)S(1)} %all-to-all-done.1.refs_0_), channel_id=1, source_target_pairs={{0,1},{1,0},{2,3},{3,2},{4,5},{5,4},{6,7},{7,6},{8,9},{9,8},{10,11... | collective-permute-start | bytes 1769480 | tf_op jit(solution)/shard_map/ppermute | solution.py:140

commit v23 on v20

--- a/solution.py
+++ b/solution.py
@@ -8,7 +8,7 @@
 from jax.sharding import Mesh, PartitionSpec as P
 
 SPACE = ("y", "core")
-SAME = ("x", "z", "y")
+SAME = ("x", "y", "z")
 EVERY = ("z", "x", "y", "core")
 GROUP = 8
 LANES = 128

time: 62.7 us -> 64.2 us (1.024)
  waiting for transfers between devices: 11.8 us -> 13.4 us
  starting transfers between devices: 20.5 us -> 19.1 us
  blocking collectives: 16.4 us -> 17.6 us
    all_to_all x1, waiting for transfers between devices: 2.27 us -> 3.63 us  [per_device(): mine = lax.all_to_all(shares, SAME, 0, 0)]
    all_to_all x1, blocking collectives: 16.4 us -> 17.6 us  [per_device(): parts = lax.all_to_all(parts, SAME, 0, 0)]
    all_to_all x1, starting transfers between devices: 4.29 us -> 3.6 us  [per_device(): mine = lax.all_to_all(shares, SAME, 0, 0)]
    ppermute x7, starting transfers between devices: 6.4 us -> 5.71 us  [swapped(): return lax.ppermute(value, axis, [(0, 1), (1, 0)])]
  transfers between devices with their start and end apart: 11 -> 11, of which waited for: 6 -> 6; matrix products, arithmetic and copies ran while one was open for 0% -> 0% of each run, Pallas kernels for 13% -> 12%
where the time goes in v23:
time: 64.2 us; the launch traced here: 63.5 us
  starting transfers between devices  19.1 us (30%)
  blocking collectives  17.6 us (27%)
  waiting for transfers between devices  13.4 us (21%)
  Pallas kernels  11.1 us (17%)
  local copies, waits for them, and re-layouts  1.35 us (2%)
  between operations  0.85 us (1%)
    all_to_all x1, blocking collectives, per_device(): parts = lax.all_to_all(parts, SAME, 0, 0)  17.6 us
    ppermute x3, starting transfers between devices, crossed(): return lax.ppermute(value, SPACE, pairs + [(m, n) for n, m in pairs])  9.83 us
    ppermute x3, waiting for transfers between devices, crossed(): return lax.ppermute(value, SPACE, pairs + [(m, n) for n, m in pairs])  8.97 us
    ppermute x7, starting transfers between devices, swapped(): return lax.ppermute(value, axis, [(0, 1), (1, 0)])  5.71 us
    all_to_all x1, waiting for transfers between devices, per_device(): mine = lax.all_to_all(shares, SAME, 0, 0)  3.63 us
    all_to_all x1, starting transfers between devices, per_device(): mine = lax.all_to_all(shares, SAME, 0, 0)  3.6 us
    pallas_call x1, Pallas kernels, first_part(): vmem_call(first_kernel, (jax.ShapeDtypeStruct(((length + 2) * 3 * c1, wid...  2.57 us
    pallas_call x1, Pallas kernels, finish(): pl.pallas_call(lambda *refs: finish_kernel(sizes, height, padded, *refs),...  1.37 us
  transfers between devices with their start and end apart: 11, of which 6 were waited for; matrix products, arithmetic and copies ran while one was open for 0% of the time, Pallas kernels for 12%

profile of v23, /device:TPU:1, one launch (start us, length us, event | category | flops | bytes accessed | tf_op | source)
XLA Modules:
  0.0 63.5 jit_solution(1451684978525075291)
XLA Ops:
  0.6 0.0 copy-start
  0.7 0.0 copy-start.1
  0.7 1.2 %copy-done.1 = bf16[1,1,32,64,128]{4,3,2,1,0:T(8,128)(2,1)S(1)} copy-done((bf16[1,1,32,64,128]{4,3,2,1,0:T(8,128)(2,1)S(1)}, bf16[1,1,32,64,128]{4,3,2,1,0:T(8,128)(2,1)}, u32[]{:S(2)}) %copy-start.1) | copy-done | bytes 524312
  1.8 0.0 copy-start.3
  1.8 0.8 %shard_map.93.refs_0_.pack_0 = bf16[2048,128]{1,0:T(8,128)(2,1)S(1)} custom-call(bf16[32,64,128]{2,1,0:T(8,128)(2,1)S(1)} %bitcast.10), custom_call_target="tpu_custom_call" | custom-call | bytes 67108864 | tf_op jit(solution)/shard_map/pallas_call | solution.py:59
  2.6 0.0 copy-done
  2.6 0.1 dynamic-slice_convert_fusion
  2.7 0.0 copy-start.2
  2.7 0.0 copy-start.4
  2.7 0.0 copy-start.5
  2.8 0.1 constant_dynamic-slice_fusion.own
  2.8 0.1 collective-permute-start
  3.0 4.6 %collective-permute-start.5 = (bf16[2048,128]{1,0:T(8,128)(2,1)S(1)}, bf16[2048,128]{1,0:T(8,128)(2,1)S(1)}, u32[]{:S(2)}, u32[]{:S(2)}) collective-permute-start(bf16[2048,128]{1,0:T(8,128)(2,1)S(1)} %shard_map.93.refs_0_.pack_0), channel_id=1, source_target_pairs={{1,2},{2,1},{5,6},{6,5},{9,10},{10,9},{13,14},{14,13},{17,18},{18,... | collective-permute-start | bytes 1572872 | tf_op jit(solution)/shard_map/ppermute | solution.py:497
  7.6 0.1 collective-permute-start.4
  7.7 0.0 copy-done.3
  7.7 0.5 shard_map.95.pack_0
  8.2 1.9 %collective-permute-start.3 = (bf16[1024,128]{1,0:T(8,128)(2,1)S(1)}, bf16[1024,128]{1,0:T(8,128)(2,1)S(1)}, u32[]{:S(2)}, u32[]{:S(2)}) collective-permute-start(bf16[1024,128]{1,0:T(8,128)(2,1)S(1)} %shard_map.95.pack_0), channel_id=1, source_target_pairs={{1,2},{2,1},{5,6},{6,5},{9,10},{10,9},{13,14},{14,13},{17,18},{18,... | collective-permute-start | bytes 786440 | tf_op jit(solution)/shard_map/ppermute | solution.py:497
  10.1 0.1 collective-permute-start.2
  10.2 0.0 collective-permute-done.other
  10.2 0.1 shard_map.94
  10.3 1.7 %collective-permute-start.1 = (bf16[1024,128]{1,0:T(8,128)(2,1)S(1)}, bf16[1024,128]{1,0:T(8,128)(2,1)S(1)}, u32[]{:S(2)}, u32[]{:S(2)}) collective-permute-start(bf16[1024,128]{1,0:T(8,128)(2,1)S(1)} %get-tuple-element.42), channel_id=1, source_target_pairs={{0,4},{4,0},{1,5},{5,1},{2,6},{6,2},{3,7},{7,3},{8,12},{12,8},{9,1... | collective-permute-start | bytes 786440 | tf_op jit(solution)/shard_map/ppermute | solution.py:140
  12.0 0.0 copy-done.2
  12.0 0.0 copy-done.4
  12.0 0.0 copy-done.5
  12.0 0.9 %shard_map.96 = (bf16[2048,128]{1,0:T(8,128)(2,1)S(1)}, bf16[96,288]{1,0:T(8,128)(2,1)S(1)}, bf16[48,288]{1,0:T(8,128)(2,1)S(1)}) custom-call(bf16[32,64,128]{2,1,0:T(8,128)(2,1)S(1)} %bitcast.11, bf16[3,3,3,32,32]{4,3,2,1,0:T(8,128)(2,1)S(1)} %copy-done.4, bf16[3,3,3,16,32]{4,3,2,1,0:T(8,128)(2,1)S(1)} %copy-done.5), custom_call_target="tpu_custom_call" | custom-call | bytes 4194304 | tf_op jit(solution)/shard_map/pallas_call | solution.py:199
  13.0 1.8 %collective-permute-done.5.pack_out = bf16[2048,128]{1,0:T(8,128)(2,1)S(1)} collective-permute-done((bf16[2048,128]{1,0:T(8,128)(2,1)S(1)}, bf16[2048,128]{1,0:T(8,128)(2,1)S(1)}, u32[]{:S(2)}, u32[]{:S(2)}) %collective-permute-start.5) | collective-permute-done | bytes 524320 | tf_op jit(solution)/shard_map/ppermute | solution.py:497
  14.7 0.0 collective-permute-done.4.pack_in
  14.7 2.6 %shard_map.97 = (bf16[6336,128]{1,0:T(8,128)(2,1)S(1)}, f32[288,128]{1,0:T(8,128)S(1)}) custom-call(bf16[2048,128]{1,0:T(8,128)(2,1)S(1)} %collective-permute-done.4.pack_in, bf16[2048,128]{1,0:T(8,128)(2,1)S(1)} %shard_map.93.refs_0_.pack_0, bf16[2048,128]{1,0:T(8,128)(2,1)S(1)} %collective-permute-done.5.pack_out, ...), custom_call_target="tpu_custom_call" | custom-call | flops 1000000000 | bytes 20971520 | tf_op jit(solution)/shard_map/pallas_call | solution.py:293
  17.3 0.2 collective-permute-done.3.pack_out
  17.6 0.0 collective-permute-done.2.pack_in
  17.6 0.8 %shard_map.98 = (bf16[256,128]{1,0:T(8,128)(2,1)S(1)}, f32[256,128]{1,0:T(8,128)S(1)}) custom-call(bf16[1024,128]{1,0:T(8,128)(2,1)S(1)} %collective-permute-done.2.pack_in, bf16[1024,128]{1,0:T(8,128)(2,1)S(1)} %shard_map.95.pack_0, bf16[1024,128]{1,0:T(8,128)(2,1)S(1)} %collective-permute-done.3.pack_out, bf16[6336,128]{1,0:T(8,128)(2,1)S(1)} %get-tuple-element.47.pres, ...), custom_call_target="tpu_custom_call" | custom-call | flops 1000000000 | bytes 5242880 | tf_op jit(solution)/shard_map/pallas_call | solution.py:307
  18.4 0.1 collective-permute-start.6
  18.4 1.0 %shard_map.100 = (bf16[1024,128]{1,0:T(8,128)(2,1)S(1)}, bf16[1024,128]{1,0:T(8,128)(2,1)S(1)}, bf16[1024,128]{1,0:T(8,128)(2,1)S(1)}) custom-call(bf16[6336,128]{1,0:T(8,128)(2,1)S(1)} %get-tuple-element.47.pres, bf16[48,288]{1,0:T(8,128)(2,1)S(1)} %get-tuple-element.51.w_one), custom_call_target="tpu_custom_call" | custom-call | flops 1000000000 | bytes 5242880 | tf_op jit(solution)/shard_map/pallas_call | solution.py:321
  19.5 0.2 collective-permute-done.6.more
  19.7 0.0 collective-permute-done.1.other
  19.7 0.1 shard_map.99
  19.8 17.6 %all_to_all.10.refs_0_ = bf16[16,80,128]{2,1,0:T(8,128)(2,1)S(1)} all-to-all(bf16[16,80,128]{2,1,0:T(8,128)(2,1)S(1)} %shard_map.99), channel_id=1, replica_groups=mesh['z'=4,'x'=2,'y'=2,'core'=2] {'x','y','z'}, dimensions={0} | all-to-all | bytes 655360 | tf_op jit(solution)/shard_map/all_to_all | solution.py:526
  37.4 1.0 %shard_map.101 = bf16[16,144,128]{2,1,0:T(8,128)(2,1)} custom-call(bf16[16,80,128]{2,1,0:T(8,128)(2,1)S(1)} %all_to_all.10.refs_0_), custom_call_target="tpu_custom_call" | custom-call | flops 163840 | bytes 983040 | tf_op jit(solution)/shard_map/pallas_call | solution.py:377
  38.4 3.6 %all-to-all-start.1 = ((bf16[16,144,128]{2,1,0:T(8,128)(2,1)}), bf16[16,144,128]{2,1,0:T(8,128)(2,1)S(1)}, u32[]{:S(2)}, u32[]{:S(2)}) async-start(bf16[16,144,128]{2,1,0:T(8,128)(2,1)} %shard_map.101), calls=%async_computation.1 | async-start | bytes 1179648 | tf_op jit(solution)/shard_map/all_to_all | solution.py:531
  42.0 1.9 %collective-permute-start.7 = (bf16[1024,128]{1,0:T(8,128)(2,1)S(1)}, bf16[1024,128]{1,0:T(8,128)(2,1)S(1)}, u32[]{:S(2)}, u32[]{:S(2)}) collective-permute-start(bf16[1024,128]{1,0:T(8,128)(2,1)S(1)} %get-tuple-element.59), channel_id=1, source_target_pairs={{0,1},{1,0},{2,3},{3,2},{4,5},{5,4},{6,7},{7,6},{8,9},{9,8},{10,11... | collective-permute-start | bytes 786440 | tf_op jit(solution)/shard_map/ppermute | solution.py:140
  43.9 3.3 %collective-permute-start.8 = (bf16[1024,128]{1,0:T(8,128)(2,1)S(1)}, bf16[1024,128]{1,0:T(8,128)(2,1)S(1)}, u32[]{:S(2)}, u32[]{:S(2)}) collective-permute-start(bf16[1024,128]{1,0:T(8,128)(2,1)S(1)} %get-tuple-element.60), channel_id=1, source_target_pairs={{1,2},{2,1},{5,6},{6,5},{9,10},{10,9},{13,14},{14,13},{17,18},{18,... | collective-permute-start | bytes 786440 | tf_op jit(solution)/shard_map/ppermute | solution.py:497
  47.2 0.0 collective-permute-done.7.first
  47.2 7.0 %collective-permute-done.8.second = bf16[1024,128]{1,0:T(8,128)(2,1)S(1)} collective-permute-done((bf16[1024,128]{1,0:T(8,128)(2,1)S(1)}, bf16[1024,128]{1,0:T(8,128)(2,1)S(1)}, u32[]{:S(2)}, u32[]{:S(2)}) %collective-permute-start.8) | collective-permute-done | bytes 262176 | tf_op jit(solution)/shard_map/ppermute | solution.py:497
  54.1 1.0 %shard_map.102 = bf16[16,64,128]{2,1,0:T(8,128)(2,1)} custom-call(bf16[1024,128]{1,0:T(8,128)(2,1)S(1)} %get-tuple-element.58.own, bf16[1024,128]{1,0:T(8,128)(2,1)S(1)} %collective-permute-done.7.first, bf16[1024,128]{1,0:T(8,128)(2,1)S(1)} %collective-permute-done.8.second), custom_call_target="tpu_custom_call" | custom-call | flops 262144 | bytes 1048576 | tf_op jit(solution)/shard_map/pallas_call | solution.py:351
  55.1 3.6 %all-to-all-done.1.refs_0_ = bf16[16,144,128]{2,1,0:T(8,128)(2,1)S(1)} async-done(((bf16[16,144,128]{2,1,0:T(8,128)(2,1)}), bf16[16,144,128]{2,1,0:T(8,128)(2,1)S(1)}, u32[]{:S(2)}, u32[]{:S(2)}) %all-to-all-start.1) | async-done | bytes 589856 | tf_op jit(solution)/shard_map/all_to_all | solution.py:531
  58.8 1.8 %collective-permute-start.9 = (bf16[16,144,128]{2,1,0:T(8,128)(2,1)S(1)}, bf16[16,144,128]{2,1,0:T(8,128)(2,1)S(1)}, u32[]{:S(2)}, u32[]{:S(2)}) collective-permute-start(bf16[16,144,128]{2,1,0:T(8,128)(2,1)S(1)} %all-to-all-done.1.refs_0_), channel_id=1, source_target_pairs={{0,1},{1,0},{2,3},{3,2},{4,5},{5,4},{6,7},{7,6},{8,9},{9,8},{10,11... | collective-permute-start | bytes 1769480 | tf_op jit(solution)/shard_map/ppermute | solution.py:140
  60.5 1.0 %shard_map.103.refs_2_ = f32[4096,128]{1,0:T(8,128)} custom-call(bf16[16,144,128]{2,1,0:T(8,128)(2,1)S(1)} %all-to-all-done.1.refs_0_), custom_call_target="tpu_custom_call" | custom-call | tf_op jit(solution)/shard_map/pallas_call | solution.py:466
  61.5 0.6 collective-permute-done.9.refs_1_
  62.2 1.4 %shard_map.104 = (f32[4096,128]{1,0:T(8,128)}, f32[432,32]{1,0:T(8,128)}, f32[864,32]{1,0:T(8,128)}) custom-call(bf16[16,144,128]{2,1,0:T(8,128)(2,1)S(1)} %all-to-all-done.1.refs_0_, bf16[16,144,128]{2,1,0:T(8,128)(2,1)S(1)} %collective-permute-done.9.refs_1_, f32[4096,128]{1,0:T(8,128)} %shard_map.103.refs_2_), custom_call_target="tpu_custom_call", output_to_operand_aliasing={{0}: (2, {})} | custom-call | tf_op jit(solution)/shard_map/pallas_call | solution.py:474
Async XLA Ops:
  0.6 2.0 %copy-start = (f32[1,524288]{1,0:T(1,128)S(1)}, f32[1,524288]{1,0:T(1,128)}, u32[]{:S(2)}) copy-start(f32[1,524288]{1,0:T(1,128)} %param.11) | copy-start | bytes 6291460
  0.7 1.2 %copy-start.1 = (bf16[1,1,32,64,128]{4,3,2,1,0:T(8,128)(2,1)S(1)}, bf16[1,1,32,64,128]{4,3,2,1,0:T(8,128)(2,1)}, u32[]{:S(2)}) copy-start(bf16[1,1,32,64,128]{4,3,2,1,0:T(8,128)(2,1)} %param.8) | copy-start | bytes 1572868
  1.8 5.8 %copy-start.3 = (bf16[1,1,16,64,128]{4,3,2,1,0:T(8,128)(2,1)S(1)}, bf16[1,1,16,64,128]{4,3,2,1,0:T(8,128)(2,1)}, u32[]{:S(2)}) copy-start(bf16[1,1,16,64,128]{4,3,2,1,0:T(8,128)(2,1)} %param.6) | copy-start | bytes 786436
  2.7 9.3 %copy-start.2 = (bf16[1,1,32,64,128]{4,3,2,1,0:T(8,128)(2,1)S(1)}, bf16[1,1,32,64,128]{4,3,2,1,0:T(8,128)(2,1)}, u32[]{:S(2)}) copy-start(bf16[1,1,32,64,128]{4,3,2,1,0:T(8,128)(2,1)} %param.7) | copy-start | bytes 1572868
  2.7 9.3 %copy-start.4 = (bf16[3,3,3,32,32]{4,3,2,1,0:T(8,128)(2,1)S(1)}, bf16[3,3,3,32,32]{4,3,2,1,0:T(8,128)(2,1)}, u32[]{:S(2)}) copy-start(bf16[3,3,3,32,32]{4,3,2,1,0:T(8,128)(2,1)} %two.1) | copy-start | bytes 165892
  2.7 9.3 %copy-start.5 = (bf16[3,3,3,16,32]{4,3,2,1,0:T(8,128)(2,1)S(1)}, bf16[3,3,3,16,32]{4,3,2,1,0:T(8,128)(2,1)}, u32[]{:S(2)}) copy-start(bf16[3,3,3,16,32]{4,3,2,1,0:T(8,128)(2,1)} %one.1) | copy-start | bytes 82948
  2.8 7.3 %collective-permute-start = (bf16[2048,128]{1,0:T(8,128)(2,1)S(1)}, bf16[2048,128]{1,0:T(8,128)(2,1)S(1)}, u32[]{:S(2)}, u32[]{:S(2)}) collective-permute-start(bf16[2048,128]{1,0:T(8,128)(2,1)S(1)} %dynamic-slice_convert_fusion), channel_id=1, source_target_pairs={{0,1},{1,0},{2,3},{3,2},{4,5},{5,4},{6,7},{7,6},{8,9},{9,8},{10,11... | collective-permute-start | bytes 1572872 | tf_op jit(solution)/shard_map/ppermute | solution.py:140
  3.0 11.8 %collective-permute-start.5 = (bf16[2048,128]{1,0:T(8,128)(2,1)S(1)}, bf16[2048,128]{1,0:T(8,128)(2,1)S(1)}, u32[]{:S(2)}, u32[]{:S(2)}) collective-permute-start(bf16[2048,128]{1,0:T(8,128)(2,1)S(1)} %shard_map.93.refs_0_.pack_0), channel_id=1, source_target_pairs={{1,2},{2,1},{5,6},{6,5},{9,10},{10,9},{13,14},{14,13},{17,18},{18,... | collective-permute-start | bytes 1572872 | tf_op jit(solution)/shard_map/ppermute | solution.py:497
  7.6 7.1 %collective-permute-start.4 = (bf16[2048,128]{1,0:T(8,128)(2,1)S(1)}, bf16[2048,128]{1,0:T(8,128)(2,1)S(1)}, u32[]{:S(2)}, u32[]{:S(2)}) collective-permute-start(bf16[2048,128]{1,0:T(8,128)(2,1)S(1)} %shard_map.93.refs_0_.pack_0), channel_id=1, source_target_pairs={{0,1},{1,0},{2,3},{3,2},{4,5},{5,4},{6,7},{7,6},{8,9},{9,8},{10,11... | collective-permute-start | bytes 1572872 | tf_op jit(solution)/shard_map/ppermute | solution.py:140
  8.2 9.4 %collective-permute-start.3 = (bf16[1024,128]{1,0:T(8,128)(2,1)S(1)}, bf16[1024,128]{1,0:T(8,128)(2,1)S(1)}, u32[]{:S(2)}, u32[]{:S(2)}) collective-permute-start(bf16[1024,128]{1,0:T(8,128)(2,1)S(1)} %shard_map.95.pack_0), channel_id=1, source_target_pairs={{1,2},{2,1},{5,6},{6,5},{9,10},{10,9},{13,14},{14,13},{17,18},{18,... | collective-permute-start | bytes 786440 | tf_op jit(solution)/shard_map/ppermute | solution.py:497
  10.1 7.5 %collective-permute-start.2 = (bf16[1024,128]{1,0:T(8,128)(2,1)S(1)}, bf16[1024,128]{1,0:T(8,128)(2,1)S(1)}, u32[]{:S(2)}, u32[]{:S(2)}) collective-permute-start(bf16[1024,128]{1,0:T(8,128)(2,1)S(1)} %shard_map.95.pack_0), channel_id=1, source_target_pairs={{0,1},{1,0},{2,3},{3,2},{4,5},{5,4},{6,7},{7,6},{8,9},{9,8},{10,11... | collective-permute-start | bytes 786440 | tf_op jit(solution)/shard_map/ppermute | solution.py:140
  10.3 9.4 %collective-permute-start.1 = (bf16[1024,128]{1,0:T(8,128)(2,1)S(1)}, bf16[1024,128]{1,0:T(8,128)(2,1)S(1)}, u32[]{:S(2)}, u32[]{:S(2)}) collective-permute-start(bf16[1024,128]{1,0:T(8,128)(2,1)S(1)} %get-tuple-element.42), channel_id=1, source_target_pairs={{0,4},{4,0},{1,5},{5,1},{2,6},{6,2},{3,7},{7,3},{8,12},{12,8},{9,1... | collective-permute-start | bytes 786440 | tf_op jit(solution)/shard_map/ppermute | solution.py:140
  18.4 1.3 %collective-permute-start.6 = (bf16[256,128]{1,0:T(8,128)(2,1)S(1)}, bf16[256,128]{1,0:T(8,128)(2,1)S(1)}, u32[]{:S(2)}, u32[]{:S(2)}) collective-permute-start(bf16[256,128]{1,0:T(8,128)(2,1)S(1)} %get-tuple-element.50), channel_id=1, source_target_pairs={{0,1},{1,0},{2,3},{3,2},{4,5},{5,4},{6,7},{7,6},{8,9},{9,8},{10,11... | collective-permute-start | bytes 196616 | tf_op jit(solution)/shard_map/ppermute | solution.py:140
  38.4 20.4 %all-to-all-start.1 = ((bf16[16,144,128]{2,1,0:T(8,128)(2,1)}), bf16[16,144,128]{2,1,0:T(8,128)(2,1)S(1)}, u32[]{:S(2)}, u32[]{:S(2)}) async-start(bf16[16,144,128]{2,1,0:T(8,128)(2,1)} %shard_map.101), calls=%async_computation.1 | async-start | bytes 1179648 | tf_op jit(solution)/shard_map/all_to_all | solution.py:531
  42.0 5.2 %collective-permute-start.7 = (bf16[1024,128]{1,0:T(8,128)(2,1)S(1)}, bf16[1024,128]{1,0:T(8,128)(2,1)S(1)}, u32[]{:S(2)}, u32[]{:S(2)}) collective-permute-start(bf16[1024,128]{1,0:T(8,128)(2,1)S(1)} %get-tuple-element.59), channel_id=1, source_target_pairs={{0,1},{1,0},{2,3},{3,2},{4,5},{5,4},{6,7},{7,6},{8,9},{9,8},{10,11... | collective-permute-start | bytes 786440 | tf_op jit(solution)/shard_map/ppermute | solution.py:140
  43.9 10.3 %collective-permute-start.8 = (bf16[1024,128]{1,0:T(8,128)(2,1)S(1)}, bf16[1024,128]{1,0:T(8,128)(2,1)S(1)}, u32[]{:S(2)}, u32[]{:S(2)}) collective-permute-start(bf16[1024,128]{1,0:T(8,128)(2,1)S(1)} %get-tuple-element.60), channel_id=1, source_target_pairs={{1,2},{2,1},{5,6},{6,5},{9,10},{10,9},{13,14},{14,13},{17,18},{18,... | collective-permute-start | bytes 786440 | tf_op jit(solution)/shard_map/ppermute | solution.py:497
  58.8 3.4 %collective-permute-start.9 = (bf16[16,144,128]{2,1,0:T(8,128)(2,1)S(1)}, bf16[16,144,128]{2,1,0:T(8,128)(2,1)S(1)}, u32[]{:S(2)}, u32[]{:S(2)}) collective-permute-start(bf16[16,144,128]{2,1,0:T(8,128)(2,1)S(1)} %all-to-all-done.1.refs_0_), channel_id=1, source_target_pairs={{0,1},{1,0},{2,3},{3,2},{4,5},{5,4},{6,7},{7,6},{8,9},{9,8},{10,11... | collective-permute-start | bytes 1769480 | tf_op jit(solution)/shard_map/ppermute | solution.py:140

commit v24 on v20

--- a/solution.py
+++ b/solution.py
@@ -9,6 +9,7 @@
 
 SPACE = ("y", "core")
 SAME = ("x", "z", "y")
+GATHER = ("z", "x", "y")
 EVERY = ("z", "x", "y", "core")
 GROUP = 8
 LANES = 128
@@ -387,14 +388,14 @@
     )(parts)
 
 
-def place(source, height, padded, which, bucket, buffer, sems):
+def place(source, height, padded, order, which, bucket, buffer, sems):
     copies, count = (source.shape[0], sems.shape[0])
     step = 2 * copies // count
     sent = []
     for n in range(count):
         for m in range(n * step, (n + 1) * step):
             half, q = (m // copies, m % copies)
-            value = source[q, half * padded : (half + 1) * padded, :].astype(F32)
+            value = source[order[q], half * padded : (half + 1) * padded, :].astype(F32)
             buffer[m * height : (m + 1) * height, :] = value[0:height]
         rows = pl.ds(n * step * height, step * height)
         at = (which * count + n) * step * height
@@ -404,13 +405,13 @@
     return sent
 
 
-def start_kernel(height, padded, mine, bucket, buffer, sems):
-    for copy in place(mine, height, padded, lax.axis_index("core"), bucket, buffer, sems):
+def start_kernel(height, padded, order, mine, bucket, buffer, sems):
+    for copy in place(mine, height, padded, order, lax.axis_index("core"), bucket, buffer, sems):
         copy.wait()
 
 
 def finish_kernel(
-    sizes, height, padded, mine, other, partial,
+    sizes, height, padded, order, mine, other, partial,
     bucket, out_one, out_two,
     raw, one, two, out_sems, buffer, sems,
 ):
@@ -418,12 +419,12 @@
     copies, rows, _ = mine.shape
     extra = rows - 2 * padded
     me = lax.axis_index("core")
-    sent = place(other, height, padded, 1 - me, bucket, buffer, sems)
+    sent = place(other, height, padded, order, 1 - me, bucket, buffer, sems)
 
     for q in range(copies):
         for source, which in ((mine, me), (other, 1 - me)):
             at = pl.multiple_of((which * copies + q) * extra, 8)
-            raw[pl.ds(at, extra), :] = source[q, 2 * padded : rows, :].astype(F32)
+            raw[pl.ds(at, extra), :] = source[order[q], 2 * padded : rows, :].astype(F32)
     block = 3 * c1
     first = -(-9 * c2 // LANES) * block
     for i in range(3):
@@ -454,6 +455,8 @@
     copies, rows, _ = mine.shape
     height = length // LANES // (4 * copies)
     padded = ceil_to(height, 16)
+    nx, nz, ny = [lax.axis_size(axis) for axis in SAME]
+    order = [(z * nx + x) * ny + y for x in range(nx) for z in range(nz) for y in range(ny)]
     spec = pl.BlockSpec(memory_space=pltpu.VMEM)
     remote = pl.BlockSpec(memory_space=pltpu.HBM)
     whole = jax.ShapeDtypeStruct((length // LANES, LANES), F32)
@@ -464,7 +467,7 @@
     ]
     params = pltpu.CompilerParams(vmem_limit_bytes=24 * 2**20)
     partial = pl.pallas_call(
-        lambda *refs: start_kernel(height, padded, *refs),
+        lambda *refs: start_kernel(height, padded, order, *refs),
         out_shape=whole,
         in_specs=[spec],
         out_specs=remote,
@@ -472,7 +475,7 @@
         compiler_params=params,
     )(mine)
     return pl.pallas_call(
-        lambda *refs: finish_kernel(sizes, height, padded, *refs),
+        lambda *refs: finish_kernel(sizes, height, padded, order, *refs),
         out_shape=(
             whole,
             jax.ShapeDtypeStruct((27 * c0, c1), F32),
@@ -528,7 +531,7 @@
     shares = share(parts, rows // devices, 1.0 / math.sqrt(cells))
 
     shares, inner, outer = lax.optimization_barrier((shares, inner, outer))
-    mine = lax.all_to_all(shares, SAME, 0, 0)
+    mine = lax.all_to_all(shares, GATHER, 0, 0)
     inner, outer = (swapped(inner), crossed(outer))
     grad_input = merge(own, inner, outer, volume_in.shape[2:])
     mine, grad_input = lax.optimization_barrier((mine, grad_input))

time: 62.7 us -> 62.3 us (level)
  waiting for transfers between devices: 11.8 us -> 9.7 us
  starting transfers between devices: 20.5 us -> 22.3 us
    ppermute x7, starting transfers between devices: 6.4 us -> 8.15 us  [swapped(): return lax.ppermute(value, axis, [(0, 1), (1, 0)])]
    all_to_all x1, waiting for transfers between devices: 2.27 us -> 0.81 us  [per_device(): mine = lax.all_to_all(shares, GATHER, 0, 0)]
    ppermute x3, waiting for transfers between devices: 8.75 us -> 8.08 us  [crossed(): return lax.ppermute(value, SPACE, pairs + [(m, n) for n, m in pairs])]
where the time goes in v24:
time: 62.3 us; the launch traced here: 61.7 us
  starting transfers between devices  22.3 us (36%)
  blocking collectives  16.4 us (26%)
  Pallas kernels  11.1 us (18%)
  waiting for transfers between devices  9.7 us (16%)
  local copies, waits for them, and re-layouts  1.35 us (2%)
  between operations  0.85 us (1%)
    all_to_all x1, blocking collectives, per_device(): parts = lax.all_to_all(parts, SAME, 0, 0)  16.4 us
    ppermute x3, starting transfers between devices, crossed(): return lax.ppermute(value, SPACE, pairs + [(m, n) for n, m in pairs])  9.81 us
    ppermute x7, starting transfers between devices, swapped(): return lax.ppermute(value, axis, [(0, 1), (1, 0)])  8.15 us
    ppermute x3, waiting for transfers between devices, crossed(): return lax.ppermute(value, SPACE, pairs + [(m, n) for n, m in pairs])  8.08 us
    all_to_all x1, starting transfers between devices, per_device(): mine = lax.all_to_all(shares, GATHER, 0, 0)  4.29 us
    pallas_call x1, Pallas kernels, first_part(): vmem_call(first_kernel, (jax.ShapeDtypeStruct(((length + 2) * 3 * c1, wid...  2.57 us
    pallas_call x1, Pallas kernels, finish(): pl.pallas_call(lambda *refs: finish_kernel(sizes, height, padded, order,...  1.37 us
    pallas_call x2, Pallas kernels, pack(): pl.pallas_call(pack_kernel, out_shape=jax.ShapeDtypeStruct((length * chan...  1.25 us
  transfers between devices with their start and end apart: 11, of which 6 were waited for; matrix products, arithmetic and copies ran while one was open for 0% of the time, Pallas kernels for 13%

profile of v24, /device:TPU:1, one launch (start us, length us, event | category | flops | bytes accessed | tf_op | source)
XLA Modules:
  0.0 61.7 jit_solution(14109781401901496942)
XLA Ops:
  0.6 0.0 copy-start
  0.7 0.0 copy-start.1
  0.7 1.2 %copy-done.1 = bf16[1,1,32,64,128]{4,3,2,1,0:T(8,128)(2,1)S(1)} copy-done((bf16[1,1,32,64,128]{4,3,2,1,0:T(8,128)(2,1)S(1)}, bf16[1,1,32,64,128]{4,3,2,1,0:T(8,128)(2,1)}, u32[]{:S(2)}) %copy-start.1) | copy-done | bytes 524312
  1.8 0.0 copy-start.3
  1.8 0.8 %shard_map.93.refs_0_.pack_0 = bf16[2048,128]{1,0:T(8,128)(2,1)S(1)} custom-call(bf16[32,64,128]{2,1,0:T(8,128)(2,1)S(1)} %bitcast.10), custom_call_target="tpu_custom_call" | custom-call | bytes 67108864 | tf_op jit(solution)/shard_map/pallas_call | solution.py:60
  2.6 0.0 copy-done
  2.6 0.1 dynamic-slice_convert_fusion
  2.7 0.0 copy-start.2
  2.7 0.0 copy-start.4
  2.7 0.0 copy-start.5
  2.8 0.1 constant_dynamic-slice_fusion.own
  2.8 0.1 collective-permute-start
  3.0 4.6 %collective-permute-start.5 = (bf16[2048,128]{1,0:T(8,128)(2,1)S(1)}, bf16[2048,128]{1,0:T(8,128)(2,1)S(1)}, u32[]{:S(2)}, u32[]{:S(2)}) collective-permute-start(bf16[2048,128]{1,0:T(8,128)(2,1)S(1)} %shard_map.93.refs_0_.pack_0), channel_id=1, source_target_pairs={{1,2},{2,1},{5,6},{6,5},{9,10},{10,9},{13,14},{14,13},{17,18},{18,... | collective-permute-start | bytes 1572872 | tf_op jit(solution)/shard_map/ppermute | solution.py:500
  7.6 0.1 collective-permute-start.4
  7.7 0.0 copy-done.3
  7.7 0.5 shard_map.95.pack_0
  8.2 1.9 %collective-permute-start.3 = (bf16[1024,128]{1,0:T(8,128)(2,1)S(1)}, bf16[1024,128]{1,0:T(8,128)(2,1)S(1)}, u32[]{:S(2)}, u32[]{:S(2)}) collective-permute-start(bf16[1024,128]{1,0:T(8,128)(2,1)S(1)} %shard_map.95.pack_0), channel_id=1, source_target_pairs={{1,2},{2,1},{5,6},{6,5},{9,10},{10,9},{13,14},{14,13},{17,18},{18,... | collective-permute-start | bytes 786440 | tf_op jit(solution)/shard_map/ppermute | solution.py:500
  10.1 0.1 collective-permute-start.2
  10.2 0.0 collective-permute-done.other
  10.2 0.1 shard_map.94
  10.3 1.7 %collective-permute-start.1 = (bf16[1024,128]{1,0:T(8,128)(2,1)S(1)}, bf16[1024,128]{1,0:T(8,128)(2,1)S(1)}, u32[]{:S(2)}, u32[]{:S(2)}) collective-permute-start(bf16[1024,128]{1,0:T(8,128)(2,1)S(1)} %get-tuple-element.42), channel_id=1, source_target_pairs={{0,4},{4,0},{1,5},{5,1},{2,6},{6,2},{3,7},{7,3},{8,12},{12,8},{9,1... | collective-permute-start | bytes 786440 | tf_op jit(solution)/shard_map/ppermute | solution.py:141
  12.0 0.0 copy-done.2
  12.0 0.0 copy-done.4
  12.0 0.0 copy-done.5
  12.0 0.9 %shard_map.96 = (bf16[2048,128]{1,0:T(8,128)(2,1)S(1)}, bf16[96,288]{1,0:T(8,128)(2,1)S(1)}, bf16[48,288]{1,0:T(8,128)(2,1)S(1)}) custom-call(bf16[32,64,128]{2,1,0:T(8,128)(2,1)S(1)} %bitcast.11, bf16[3,3,3,32,32]{4,3,2,1,0:T(8,128)(2,1)S(1)} %copy-done.4, bf16[3,3,3,16,32]{4,3,2,1,0:T(8,128)(2,1)S(1)} %copy-done.5), custom_call_target="tpu_custom_call" | custom-call | bytes 4194304 | tf_op jit(solution)/shard_map/pallas_call | solution.py:200
  13.0 1.8 %collective-permute-done.5.pack_out = bf16[2048,128]{1,0:T(8,128)(2,1)S(1)} collective-permute-done((bf16[2048,128]{1,0:T(8,128)(2,1)S(1)}, bf16[2048,128]{1,0:T(8,128)(2,1)S(1)}, u32[]{:S(2)}, u32[]{:S(2)}) %collective-permute-start.5) | collective-permute-done | bytes 524320 | tf_op jit(solution)/shard_map/ppermute | solution.py:500
  14.7 0.0 collective-permute-done.4.pack_in
  14.7 2.6 %shard_map.97 = (bf16[6336,128]{1,0:T(8,128)(2,1)S(1)}, f32[288,128]{1,0:T(8,128)S(1)}) custom-call(bf16[2048,128]{1,0:T(8,128)(2,1)S(1)} %collective-permute-done.4.pack_in, bf16[2048,128]{1,0:T(8,128)(2,1)S(1)} %shard_map.93.refs_0_.pack_0, bf16[2048,128]{1,0:T(8,128)(2,1)S(1)} %collective-permute-done.5.pack_out, ...), custom_call_target="tpu_custom_call" | custom-call | flops 1000000000 | bytes 20971520 | tf_op jit(solution)/shard_map/pallas_call | solution.py:294
  17.3 0.2 collective-permute-done.3.pack_out
  17.6 0.0 collective-permute-done.2.pack_in
  17.6 0.8 %shard_map.98 = (bf16[256,128]{1,0:T(8,128)(2,1)S(1)}, f32[256,128]{1,0:T(8,128)S(1)}) custom-call(bf16[1024,128]{1,0:T(8,128)(2,1)S(1)} %collective-permute-done.2.pack_in, bf16[1024,128]{1,0:T(8,128)(2,1)S(1)} %shard_map.95.pack_0, bf16[1024,128]{1,0:T(8,128)(2,1)S(1)} %collective-permute-done.3.pack_out, bf16[6336,128]{1,0:T(8,128)(2,1)S(1)} %get-tuple-element.47.pres, ...), custom_call_target="tpu_custom_call" | custom-call | flops 1000000000 | bytes 5242880 | tf_op jit(solution)/shard_map/pallas_call | solution.py:308
  18.4 0.1 collective-permute-start.6
  18.4 1.0 %shard_map.100 = (bf16[1024,128]{1,0:T(8,128)(2,1)S(1)}, bf16[1024,128]{1,0:T(8,128)(2,1)S(1)}, bf16[1024,128]{1,0:T(8,128)(2,1)S(1)}) custom-call(bf16[6336,128]{1,0:T(8,128)(2,1)S(1)} %get-tuple-element.47.pres, bf16[48,288]{1,0:T(8,128)(2,1)S(1)} %get-tuple-element.51.w_one), custom_call_target="tpu_custom_call" | custom-call | flops 1000000000 | bytes 5242880 | tf_op jit(solution)/shard_map/pallas_call | solution.py:322
  19.5 0.2 collective-permute-done.6.more
  19.7 0.0 collective-permute-done.1.other
  19.7 0.1 shard_map.99
  19.8 16.4 %all_to_all.10.refs_0_ = bf16[16,80,128]{2,1,0:T(8,128)(2,1)S(1)} all-to-all(bf16[16,80,128]{2,1,0:T(8,128)(2,1)S(1)} %shard_map.99), channel_id=1, replica_groups=mesh['z'=4,'x'=2,'y'=2,'core'=2] {'x','z','y'}, dimensions={0} | all-to-all | bytes 655360 | tf_op jit(solution)/shard_map/all_to_all | solution.py:529
  36.1 1.0 %shard_map.101 = bf16[16,144,128]{2,1,0:T(8,128)(2,1)} custom-call(bf16[16,80,128]{2,1,0:T(8,128)(2,1)S(1)} %all_to_all.10.refs_0_), custom_call_target="tpu_custom_call" | custom-call | flops 163840 | bytes 983040 | tf_op jit(solution)/shard_map/pallas_call | solution.py:378
  37.1 4.3 %all-to-all-start.1 = ((bf16[16,144,128]{2,1,0:T(8,128)(2,1)}), bf16[16,144,128]{2,1,0:T(8,128)(2,1)S(1)}, u32[]{:S(2)}, u32[]{:S(2)}) async-start(bf16[16,144,128]{2,1,0:T(8,128)(2,1)} %shard_map.101), calls=%async_computation.1 | async-start | bytes 1179648 | tf_op jit(solution)/shard_map/all_to_all | solution.py:534
  41.4 1.8 %collective-permute-start.7 = (bf16[1024,128]{1,0:T(8,128)(2,1)S(1)}, bf16[1024,128]{1,0:T(8,128)(2,1)S(1)}, u32[]{:S(2)}, u32[]{:S(2)}) collective-permute-start(bf16[1024,128]{1,0:T(8,128)(2,1)S(1)} %get-tuple-element.59), channel_id=1, source_target_pairs={{0,1},{1,0},{2,3},{3,2},{4,5},{5,4},{6,7},{7,6},{8,9},{9,8},{10,11... | collective-permute-start | bytes 786440 | tf_op jit(solution)/shard_map/ppermute | solution.py:141
  43.2 3.3 %collective-permute-start.8 = (bf16[1024,128]{1,0:T(8,128)(2,1)S(1)}, bf16[1024,128]{1,0:T(8,128)(2,1)S(1)}, u32[]{:S(2)}, u32[]{:S(2)}) collective-permute-start(bf16[1024,128]{1,0:T(8,128)(2,1)S(1)} %get-tuple-element.60), channel_id=1, source_target_pairs={{1,2},{2,1},{5,6},{6,5},{9,10},{10,9},{13,14},{14,13},{17,18},{18,... | collective-permute-start | bytes 786440 | tf_op jit(solution)/shard_map/ppermute | solution.py:500
  46.5 0.0 collective-permute-done.7.first
  46.5 6.1 %collective-permute-done.8.second = bf16[1024,128]{1,0:T(8,128)(2,1)S(1)} collective-permute-done((bf16[1024,128]{1,0:T(8,128)(2,1)S(1)}, bf16[1024,128]{1,0:T(8,128)(2,1)S(1)}, u32[]{:S(2)}, u32[]{:S(2)}) %collective-permute-start.8) | collective-permute-done | bytes 262176 | tf_op jit(solution)/shard_map/ppermute | solution.py:500
  52.6 1.0 %shard_map.102 = bf16[16,64,128]{2,1,0:T(8,128)(2,1)} custom-call(bf16[1024,128]{1,0:T(8,128)(2,1)S(1)} %get-tuple-element.58.own, bf16[1024,128]{1,0:T(8,128)(2,1)S(1)} %collective-permute-done.7.first, bf16[1024,128]{1,0:T(8,128)(2,1)S(1)} %collective-permute-done.8.second), custom_call_target="tpu_custom_call" | custom-call | flops 262144 | bytes 1048576 | tf_op jit(solution)/shard_map/pallas_call | solution.py:352
  53.6 0.8 %all-to-all-done.1.refs_0_ = bf16[16,144,128]{2,1,0:T(8,128)(2,1)S(1)} async-done(((bf16[16,144,128]{2,1,0:T(8,128)(2,1)}), bf16[16,144,128]{2,1,0:T(8,128)(2,1)S(1)}, u32[]{:S(2)}, u32[]{:S(2)}) %all-to-all-start.1) | async-done | bytes 589856 | tf_op jit(solution)/shard_map/all_to_all | solution.py:534
  54.4 4.3 %collective-permute-start.9 = (bf16[16,144,128]{2,1,0:T(8,128)(2,1)S(1)}, bf16[16,144,128]{2,1,0:T(8,128)(2,1)S(1)}, u32[]{:S(2)}, u32[]{:S(2)}) collective-permute-start(bf16[16,144,128]{2,1,0:T(8,128)(2,1)S(1)} %all-to-all-done.1.refs_0_), channel_id=1, source_target_pairs={{0,1},{1,0},{2,3},{3,2},{4,5},{5,4},{6,7},{7,6},{8,9},{9,8},{10,11... | collective-permute-start | bytes 1769480 | tf_op jit(solution)/shard_map/ppermute | solution.py:141
  58.7 1.0 %shard_map.103.refs_2_ = f32[4096,128]{1,0:T(8,128)} custom-call(bf16[16,144,128]{2,1,0:T(8,128)(2,1)S(1)} %all-to-all-done.1.refs_0_), custom_call_target="tpu_custom_call" | custom-call | tf_op jit(solution)/shard_map/pallas_call | solution.py:469
  59.7 0.6 collective-permute-done.9.refs_1_
  60.3 1.4 %shard_map.104 = (f32[4096,128]{1,0:T(8,128)}, f32[432,32]{1,0:T(8,128)}, f32[864,32]{1,0:T(8,128)}) custom-call(bf16[16,144,128]{2,1,0:T(8,128)(2,1)S(1)} %all-to-all-done.1.refs_0_, bf16[16,144,128]{2,1,0:T(8,128)(2,1)S(1)} %collective-permute-done.9.refs_1_, f32[4096,128]{1,0:T(8,128)} %shard_map.103.refs_2_), custom_call_target="tpu_custom_call", output_to_operand_aliasing={{0}: (2, {})} | custom-call | tf_op jit(solution)/shard_map/pallas_call | solution.py:477
Async XLA Ops:
  0.6 2.0 %copy-start = (f32[1,524288]{1,0:T(1,128)S(1)}, f32[1,524288]{1,0:T(1,128)}, u32[]{:S(2)}) copy-start(f32[1,524288]{1,0:T(1,128)} %param.11) | copy-start | bytes 6291460
  0.7 1.2 %copy-start.1 = (bf16[1,1,32,64,128]{4,3,2,1,0:T(8,128)(2,1)S(1)}, bf16[1,1,32,64,128]{4,3,2,1,0:T(8,128)(2,1)}, u32[]{:S(2)}) copy-start(bf16[1,1,32,64,128]{4,3,2,1,0:T(8,128)(2,1)} %param.8) | copy-start | bytes 1572868
  1.8 5.8 %copy-start.3 = (bf16[1,1,16,64,128]{4,3,2,1,0:T(8,128)(2,1)S(1)}, bf16[1,1,16,64,128]{4,3,2,1,0:T(8,128)(2,1)}, u32[]{:S(2)}) copy-start(bf16[1,1,16,64,128]{4,3,2,1,0:T(8,128)(2,1)} %param.6) | copy-start | bytes 786436
  2.7 9.3 %copy-start.2 = (bf16[1,1,32,64,128]{4,3,2,1,0:T(8,128)(2,1)S(1)}, bf16[1,1,32,64,128]{4,3,2,1,0:T(8,128)(2,1)}, u32[]{:S(2)}) copy-start(bf16[1,1,32,64,128]{4,3,2,1,0:T(8,128)(2,1)} %param.7) | copy-start | bytes 1572868
  2.7 9.3 %copy-start.4 = (bf16[3,3,3,32,32]{4,3,2,1,0:T(8,128)(2,1)S(1)}, bf16[3,3,3,32,32]{4,3,2,1,0:T(8,128)(2,1)}, u32[]{:S(2)}) copy-start(bf16[3,3,3,32,32]{4,3,2,1,0:T(8,128)(2,1)} %two.1) | copy-start | bytes 165892
  2.7 9.3 %copy-start.5 = (bf16[3,3,3,16,32]{4,3,2,1,0:T(8,128)(2,1)S(1)}, bf16[3,3,3,16,32]{4,3,2,1,0:T(8,128)(2,1)}, u32[]{:S(2)}) copy-start(bf16[3,3,3,16,32]{4,3,2,1,0:T(8,128)(2,1)} %one.1) | copy-start | bytes 82948
  2.8 7.3 %collective-permute-start = (bf16[2048,128]{1,0:T(8,128)(2,1)S(1)}, bf16[2048,128]{1,0:T(8,128)(2,1)S(1)}, u32[]{:S(2)}, u32[]{:S(2)}) collective-permute-start(bf16[2048,128]{1,0:T(8,128)(2,1)S(1)} %dynamic-slice_convert_fusion), channel_id=1, source_target_pairs={{0,1},{1,0},{2,3},{3,2},{4,5},{5,4},{6,7},{7,6},{8,9},{9,8},{10,11... | collective-permute-start | bytes 1572872 | tf_op jit(solution)/shard_map/ppermute | solution.py:141
  3.0 11.8 %collective-permute-start.5 = (bf16[2048,128]{1,0:T(8,128)(2,1)S(1)}, bf16[2048,128]{1,0:T(8,128)(2,1)S(1)}, u32[]{:S(2)}, u32[]{:S(2)}) collective-permute-start(bf16[2048,128]{1,0:T(8,128)(2,1)S(1)} %shard_map.93.refs_0_.pack_0), channel_id=1, source_target_pairs={{1,2},{2,1},{5,6},{6,5},{9,10},{10,9},{13,14},{14,13},{17,18},{18,... | collective-permute-start | bytes 1572872 | tf_op jit(solution)/shard_map/ppermute | solution.py:500
  7.6 7.1 %collective-permute-start.4 = (bf16[2048,128]{1,0:T(8,128)(2,1)S(1)}, bf16[2048,128]{1,0:T(8,128)(2,1)S(1)}, u32[]{:S(2)}, u32[]{:S(2)}) collective-permute-start(bf16[2048,128]{1,0:T(8,128)(2,1)S(1)} %shard_map.93.refs_0_.pack_0), channel_id=1, source_target_pairs={{0,1},{1,0},{2,3},{3,2},{4,5},{5,4},{6,7},{7,6},{8,9},{9,8},{10,11... | collective-permute-start | bytes 1572872 | tf_op jit(solution)/shard_map/ppermute | solution.py:141
  8.2 9.4 %collective-permute-start.3 = (bf16[1024,128]{1,0:T(8,128)(2,1)S(1)}, bf16[1024,128]{1,0:T(8,128)(2,1)S(1)}, u32[]{:S(2)}, u32[]{:S(2)}) collective-permute-start(bf16[1024,128]{1,0:T(8,128)(2,1)S(1)} %shard_map.95.pack_0), channel_id=1, source_target_pairs={{1,2},{2,1},{5,6},{6,5},{9,10},{10,9},{13,14},{14,13},{17,18},{18,... | collective-permute-start | bytes 786440 | tf_op jit(solution)/shard_map/ppermute | solution.py:500
  10.1 7.5 %collective-permute-start.2 = (bf16[1024,128]{1,0:T(8,128)(2,1)S(1)}, bf16[1024,128]{1,0:T(8,128)(2,1)S(1)}, u32[]{:S(2)}, u32[]{:S(2)}) collective-permute-start(bf16[1024,128]{1,0:T(8,128)(2,1)S(1)} %shard_map.95.pack_0), channel_id=1, source_target_pairs={{0,1},{1,0},{2,3},{3,2},{4,5},{5,4},{6,7},{7,6},{8,9},{9,8},{10,11... | collective-permute-start | bytes 786440 | tf_op jit(solution)/shard_map/ppermute | solution.py:141
  10.3 9.4 %collective-permute-start.1 = (bf16[1024,128]{1,0:T(8,128)(2,1)S(1)}, bf16[1024,128]{1,0:T(8,128)(2,1)S(1)}, u32[]{:S(2)}, u32[]{:S(2)}) collective-permute-start(bf16[1024,128]{1,0:T(8,128)(2,1)S(1)} %get-tuple-element.42), channel_id=1, source_target_pairs={{0,4},{4,0},{1,5},{5,1},{2,6},{6,2},{3,7},{7,3},{8,12},{12,8},{9,1... | collective-permute-start | bytes 786440 | tf_op jit(solution)/shard_map/ppermute | solution.py:141
  18.4 1.3 %collective-permute-start.6 = (bf16[256,128]{1,0:T(8,128)(2,1)S(1)}, bf16[256,128]{1,0:T(8,128)(2,1)S(1)}, u32[]{:S(2)}, u32[]{:S(2)}) collective-permute-start(bf16[256,128]{1,0:T(8,128)(2,1)S(1)} %get-tuple-element.50), channel_id=1, source_target_pairs={{0,1},{1,0},{2,3},{3,2},{4,5},{5,4},{6,7},{7,6},{8,9},{9,8},{10,11... | collective-permute-start | bytes 196616 | tf_op jit(solution)/shard_map/ppermute | solution.py:141
  37.1 17.2 %all-to-all-start.1 = ((bf16[16,144,128]{2,1,0:T(8,128)(2,1)}), bf16[16,144,128]{2,1,0:T(8,128)(2,1)S(1)}, u32[]{:S(2)}, u32[]{:S(2)}) async-start(bf16[16,144,128]{2,1,0:T(8,128)(2,1)} %shard_map.101), calls=%async_computation.1 | async-start | bytes 1179648 | tf_op jit(solution)/shard_map/all_to_all | solution.py:534
  41.4 5.1 %collective-permute-start.7 = (bf16[1024,128]{1,0:T(8,128)(2,1)S(1)}, bf16[1024,128]{1,0:T(8,128)(2,1)S(1)}, u32[]{:S(2)}, u32[]{:S(2)}) collective-permute-start(bf16[1024,128]{1,0:T(8,128)(2,1)S(1)} %get-tuple-element.59), channel_id=1, source_target_pairs={{0,1},{1,0},{2,3},{3,2},{4,5},{5,4},{6,7},{7,6},{8,9},{9,8},{10,11... | collective-permute-start | bytes 786440 | tf_op jit(solution)/shard_map/ppermute | solution.py:141
  43.2 9.4 %collective-permute-start.8 = (bf16[1024,128]{1,0:T(8,128)(2,1)S(1)}, bf16[1024,128]{1,0:T(8,128)(2,1)S(1)}, u32[]{:S(2)}, u32[]{:S(2)}) collective-permute-start(bf16[1024,128]{1,0:T(8,128)(2,1)S(1)} %get-tuple-element.60), channel_id=1, source_target_pairs={{1,2},{2,1},{5,6},{6,5},{9,10},{10,9},{13,14},{14,13},{17,18},{18,... | collective-permute-start | bytes 786440 | tf_op jit(solution)/shard_map/ppermute | solution.py:500
  54.4 5.9 %collective-permute-start.9 = (bf16[16,144,128]{2,1,0:T(8,128)(2,1)S(1)}, bf16[16,144,128]{2,1,0:T(8,128)(2,1)S(1)}, u32[]{:S(2)}, u32[]{:S(2)}) collective-permute-start(bf16[16,144,128]{2,1,0:T(8,128)(2,1)S(1)} %all-to-all-done.1.refs_0_), channel_id=1, source_target_pairs={{0,1},{1,0},{2,3},{3,2},{4,5},{5,4},{6,7},{7,6},{8,9},{9,8},{10,11... | collective-permute-start | bytes 1769480 | tf_op jit(solution)/shard_map/ppermute | solution.py:141
